TPU v7x, 32 devices: a whole 2x2x4 slice. The times are simulated.
32 devices in a mesh: doc: 16 (over z, x, core), feat: 2 (over y).
Axes of the slice: x: 2, y: 2, z: 4, core: 2. Of those that a mesh axis runs over, the one named last changes fastest.
Arguments:
- col_ids: int32 [8192, 32], P('doc', 'feat'), may hold values from 0 to 4095
- col_vals: bfloat16 [8192, 32], P('doc', 'feat'), may hold values from 0.019897461 to 0.19921875
- left_vec: float32 [8192, 256], P('doc'), may hold values from -6 to 6
- right_vec: float32 [8192, 256], P(('feat', 'doc')), may hold values from -6 to 6
- search_dir: float32 [8192, 256], P(('feat', 'doc')), may hold values from -6 to 6
- solution: float32 [8192, 256], P(('feat', 'doc')), may hold values from -6 to 6
- alpha_prev: float32 [256], replicated, may hold values from 1 to 3
- phibar: float32 [256], replicated, may hold values from 0.5 to 2
- rhobar: float32 [256], replicated, may hold values from 0.5 to 3
Outputs:
- left_next: float32 [8192, 256], P('doc')
- right_next: float32 [8192, 256], P(('feat', 'doc'))
- search_next: float32 [8192, 256], P(('feat', 'doc'))
- solution_next: float32 [8192, 256], P(('feat', 'doc'))
- alpha_next: float32 [256], replicated
- phibar_next: float32 [256], replicated
- rhobar_next: float32 [256], replicated
Inputs may be any that keep to these rules, and one draw needn't show every extreme that they name: `col_ids`: entries j of a row with the same j // 16 name columns of one feature block.
All inputs are finite; a program needn't handle non-finite values.
Results may differ from a plain program's by a relative error of at most 0.0003.
Values sent between devices are 32-bit elements; how exact they have to be, the bound alone decides.
No kernel may reach another device: no remote copies, remote signals or barrier semaphores. Data moves between devices by JAX's collectives and lax.ppermute only.
A program may use at most 64 MiB of HBM per device.

v0:
```python
import jax
import jax.numpy as jnp
from jax import lax
from jax.sharding import PartitionSpec as P

epsilon = 1e-06


def forward(col_ids, col_vals, table):
    nrows, count = col_ids.shape
    step_rows = min(512, nrows)
    nblocks = nrows // step_rows
    ids_blocks = col_ids.reshape(nblocks, step_rows, count)
    vals_blocks = col_vals.reshape(nblocks, step_rows, count)

    def forward_one_block(pair):
        index_rows, value_rows = pair
        picked = table[index_rows]
        return jnp.sum(value_rows.astype(jnp.float32)[:, :, None] * picked, axis=1)

    return lax.map(forward_one_block, (ids_blocks, vals_blocks)).reshape(nrows, table.shape[1])


def backward(col_ids, col_vals, rows_in, width):
    nrows, count = col_ids.shape
    step_rows = min(512, nrows)
    nblocks = nrows // step_rows
    ids_blocks = col_ids.reshape(nblocks, step_rows, count)
    vals_blocks = col_vals.reshape(nblocks, step_rows, count)
    rows_blocks = rows_in.reshape(nblocks, step_rows, rows_in.shape[1])

    def backward_one_block(carry, triple):
        index_rows, value_rows, left_rows = triple
        terms = value_rows.astype(jnp.float32)[:, :, None] * left_rows[:, None, :]
        terms = terms.reshape(step_rows * count, left_rows.shape[1])
        added = jax.ops.segment_sum(terms, index_rows.reshape(-1), num_segments=width)
        return (carry + added, None)

    start = jnp.zeros((width, rows_in.shape[1]), jnp.float32)
    result, unused = lax.scan(backward_one_block, start, (ids_blocks, vals_blocks, rows_blocks))
    return result


def on_device(
    col_ids, col_vals, left_vec, right_vec, search_dir, solution, alpha_prev, phibar, rhobar
):
    n_feat = lax.axis_size("feat")
    n_doc = lax.axis_size("doc")
    docs_total = left_vec.shape[0] * n_doc
    feat_total = right_vec.shape[0] * n_doc * n_feat
    table = lax.all_gather(right_vec, "doc", axis=0, tiled=True)
    partial_value = forward(col_ids, col_vals, table)
    total = lax.psum(partial_value, "feat")
    left_raw = total - alpha_prev[None, :] * left_vec
    row_part = jnp.sum(left_raw * left_raw, axis=0) / n_feat
    beta_norm = jnp.sqrt(lax.psum(row_part, ("doc", "feat")) / docs_total + epsilon)
    sent_rows = left_raw / beta_norm[None, :]
    feature_part = lax.psum_scatter(
        backward(col_ids, col_vals, sent_rows, table.shape[0]),
        "doc",
        scatter_dimension=0,
        tiled=True,
    )
    right_raw = feature_part - beta_norm[None, :] * right_vec
    squares = lax.psum(jnp.sum(right_raw * right_raw, axis=0), ("doc", "feat"))
    alpha_next = jnp.sqrt(squares / feat_total + epsilon)
    right_next = right_raw / alpha_next[None, :]
    rho_val = jnp.sqrt(rhobar * rhobar + beta_norm * beta_norm)
    cosine = rhobar / rho_val
    sine_val = beta_norm / rho_val
    theta_val = sine_val * alpha_next
    rhobar_next = -cosine * alpha_next
    phi_val = cosine * phibar
    phibar_next = sine_val * phibar
    solution_next = solution + (phi_val / rho_val)[None, :] * search_dir
    search_next = right_next - (theta_val / rho_val)[None, :] * search_dir
    return (sent_rows, right_next, search_next, solution_next, alpha_next, phibar_next, rhobar_next)


def solution(mesh):
    return jax.shard_map(
        on_device,
        mesh=mesh,
        in_specs=(
            P("doc", "feat"),
            P("doc", "feat"),
            P("doc", None),
            P(("feat", "doc"), None),
            P(("feat", "doc"), None),
            P(("feat", "doc"), None),
            P(),
            P(),
            P(),
        ),
        out_specs=(
            P("doc", None),
            P(("feat", "doc"), None),
            P(("feat", "doc"), None),
            P(("feat", "doc"), None),
            P(),
            P(),
            P(),
        ),
        check_vma=False,
    )
```

profile of v0, /device:TPU:0, one launch (start us, length us, event | category | flops | bytes accessed | tf_op | source)
XLA Modules:
  0.0 346.0 jit_solution(13976187407563011125)
XLA Ops:
  7.2 0.0 all-gather.2.cloned.1.call-start
  7.2 0.7 all-gather.2.cloned.1.call-update
  7.9 0.0 all-reduce.2.cloned.1.call-start
  7.9 0.8 compare_select_fusion
  8.7 0.1 copy.18
  8.8 0.1 reshape.50
  9.0 0.8 copy.17
  9.8 53.6 %all-gather.2.cloned.1.call-done = f32[4096,256]{1,0:T(8,128)} async-done(((f32[256,256]{1,0:T(8,128)}), f32[4096,256]{1,0:T(8,128)}) %all-gather.2.cloned.1.call-update) | async-done | bytes 4194320 | tf_op jit(solution)/shard_map/all_gather | solution.py:51
  63.5 33.6 %gather_fusion = f32[8192,256]{1,0:T(8,128)} fusion(f32[4096,256]{1,0:T(8,128)} %all-gather.2.cloned.1.call-done, s32[8192]{0:T(1024)S(1)} %broadcast_clamp_fusion), kind=kCustom, calls=%fused_computation | custom fusion | bytes 16809984 | tf_op jit(solution)/shard_map/while/body/eval_jaxpr/gather | solution.py:18
  97.0 0.0 copy-start.5
  97.0 0.0 copy-start.2
  97.0 0.0 copy-start.8
  97.0 5.9 %multiply_reduce_fusion = f32[512,256]{1,0:T(8,128)} fusion(f32[512,16]{1,0:T(8,128)S(1)} %copy.17, f32[8192,256]{1,0:T(8,128)} %gather_fusion), kind=kLoop, calls=%fused_computation.3 | loop fusion | flops 4063232 | bytes 8945664 | tf_op jit(solution)/shard_map/while/body/eval_jaxpr/reduce_sum | solution.py:19
  102.9 0.0 all-reduce.2.cloned.1.call-update
  102.9 0.0 reduce-scatter.2.cloned.1.call-start
  103.0 0.1 mul.98
  103.1 0.0 copy-done.5
  103.1 0.1 copy.19
  103.2 0.1 reshape.58
  103.4 26.8 %all-reduce.2.cloned.1.call-done = f32[512,256]{1,0:T(8,128)} async-done(((f32[512,256]{1,0:T(8,128)}), f32[512,256]{1,0:T(8,128)}) %all-reduce.2.cloned.1.call-update) | async-done | bytes 524304 | tf_op jit(solution)/shard_map/psum | solution.py:53
  130.2 0.0 copy-done.2
  130.2 0.0 copy-done.8
  130.2 1.2 multiply_reduce_fusion.1
  131.3 39.3 %psum.22 = f32[256]{0:T(256)S(1)} all-reduce(f32[256]{0:T(256)S(1)} %broadcast_multiply_fusion), channel_id=1, replica_groups=mesh['doc'=16,'feat'=2] {'doc','feat'}, use_global_device_ids=true, to_apply=%region_3.4 | all-reduce | flops 256 | bytes 2048 | tf_op jit(solution)/shard_map/psum | solution.py:56
  170.7 1.1 broadcast_divide_fusion
  171.8 0.0 copy-start.1
  171.8 0.0 copy-start
  171.8 0.0 copy-start.7
  171.8 0.0 copy-start.9
  171.9 0.0 copy-start.3
  171.9 0.0 copy-start.4
  171.9 4.0 %bitcast_multiply_fusion = f32[8192,256]{1,0:T(8,128)} fusion(f32[512,256]{1,0:T(8,128)S(1)} %broadcast_divide_fusion, f32[8192]{0:T(1024)S(1)} %mul.98), kind=kLoop, calls=%fused_computation.2 | loop fusion | flops 2097152 | bytes 8945664 | tf_op jit(solution)/shard_map/while/body/eval_jaxpr/mul | solution.py:34
  175.9 46.8 %scatter_custom_fusion = f32[4096,256]{1,0:T(8,128)} fusion(s32[8192]{0:T(1024)S(1)} %reshape.58, f32[8192,256]{1,0:T(8,128)} %bitcast_multiply_fusion, f32[]{:T(128)} %constant.29.clone.1), kind=kCustom, calls=%fused_computation.4 | custom fusion | flops 2097152 | bytes 4194816 | tf_op jit(solution)/shard_map/while/body/eval_jaxpr/scatter-add | solution.py:36
  222.7 0.0 reduce-scatter.2.cloned.1.call-update
  222.7 0.0 copy-done.1
  222.7 73.6 %reduce-scatter.2.cloned.1.call-done = f32[256,256]{1,0:T(8,128)} async-done(((f32[4096,256]{1,0:T(8,128)}), f32[256,256]{1,0:T(8,128)}) %reduce-scatter.2.cloned.1.call-update) | async-done | bytes 262160 | tf_op jit(solution)/shard_map/reduce_scatter | solution.py:58
  296.3 0.0 copy-done
  296.3 1.0 multiply_reduce_fusion.2
  297.3 39.6 %psum.23 = f32[256]{0:T(256)S(1)} all-reduce(f32[256]{0:T(256)S(1)} %multiply_reduce_fusion.2), channel_id=1, replica_groups=mesh['doc'=16,'feat'=2] {'doc','feat'}, use_global_device_ids=true, to_apply=%region_7.8 | all-reduce | flops 256 | bytes 2048 | tf_op jit(solution)/shard_map/psum | solution.py:65
  336.9 0.0 copy-done.7
  336.9 0.0 copy-done.9
  336.9 0.6 fusion.3
  337.5 0.0 copy-start.6
  337.5 0.0 copy-done.3
  337.5 0.0 copy-done.4
  337.6 1.9 multiply_subtract_fusion.1
  339.4 0.0 copy-done.6
  (4 shorter events, 0.0 us)
Async XLA Ops:
  7.2 56.3 %all-gather.2.cloned.1.call-start = ((), (), s32[]{:S(2)}) async-start(), calls=%async_computation.1 | async-start | bytes 4456448 | tf_op jit(solution)/shard_map/all_gather | solution.py:51
  7.9 122.3 %all-reduce.2.cloned.1.call-start = ((), (), s32[]{:S(2)}) async-start(), calls=%async_computation.2 | async-start | bytes 1048576 | tf_op jit(solution)/shard_map/psum | solution.py:53
  97.0 6.1 %copy-start.5 = (s32[512,16]{0,1:T(8,128)S(1)}, s32[512,16]{0,1:T(8,128)}, u32[]{:S(2)}) copy-start(s32[512,16]{0,1:T(8,128)} %param.9) | copy-start | bytes 98308
  97.0 33.2 %copy-start.2 = (f32[512,256]{1,0:T(8,128)S(1)}, f32[512,256]{1,0:T(8,128)}, u32[]{:S(2)}) copy-start(f32[512,256]{1,0:T(8,128)} %param.11) | copy-start | bytes 1572868
  97.0 33.2 %copy-start.8 = (f32[256]{0:T(256)S(1)}, f32[256]{0:T(256)}, u32[]{:S(2)}) copy-start(f32[256]{0:T(256)} %param.15) | copy-start | bytes 3076
  102.9 193.3 %reduce-scatter.2.cloned.1.call-start = ((), (), s32[]{:S(2)}) async-start(), calls=%async_computation.3 | async-start | bytes 4456448 | tf_op jit(solution)/shard_map/reduce_scatter | solution.py:58
  171.8 50.9 %copy-start.1 = (f32[512,256]{1,0:T(8,128)}, f32[512,256]{1,0:T(8,128)S(1)}, u32[]{:S(2)}) copy-start(f32[512,256]{1,0:T(8,128)S(1)} %broadcast_divide_fusion) | copy-start | bytes 1572868
  171.8 124.4 %copy-start = (f32[256,256]{1,0:T(8,128)S(1)}, f32[256,256]{1,0:T(8,128)}, u32[]{:S(2)}) copy-start(f32[256,256]{1,0:T(8,128)} %param.12) | copy-start | bytes 786436
  171.8 165.1 %copy-start.7 = (f32[256]{0:T(256)S(1)}, f32[256]{0:T(256)}, u32[]{:S(2)}) copy-start(f32[256]{0:T(256)} %param.17) | copy-start | bytes 3076
  171.8 165.1 %copy-start.9 = (f32[256]{0:T(256)S(1)}, f32[256]{0:T(256)}, u32[]{:S(2)}) copy-start(f32[256]{0:T(256)} %param.16) | copy-start | bytes 3076
  171.9 165.7 %copy-start.3 = (f32[256,256]{1,0:T(8,128)S(1)}, f32[256,256]{1,0:T(8,128)}, u32[]{:S(2)}) copy-start(f32[256,256]{1,0:T(8,128)} %param.13) | copy-start | bytes 786436
  171.9 165.7 %copy-start.4 = (f32[256,256]{1,0:T(8,128)S(1)}, f32[256,256]{1,0:T(8,128)}, u32[]{:S(2)}) copy-start(f32[256,256]{1,0:T(8,128)} %param.14) | copy-start | bytes 786436
  337.5 1.9 copy-start.6
Sparse Core Ops, SparseCore 0:
  10.2 53.2 all-gather.1
  103.0 27.0 all-reduce.1
  222.8 73.4 reduce-scatter.1
where the time goes:
time: 347 us; the launch traced here: 346 us
  waiting for transfers between devices  155 us (45%)
  blocking collectives  79 us (23%)
  other arithmetic  63.2 us (18%)
  local copies, waits for them, and re-layouts  35.1 us (10%)
  between operations  13.9 us (4%)
    reduce_scatter x1, waiting for transfers between devices, on_device(): lax.psum_scatter(backward(col_ids, col_vals, sent_rows, table.shape[0]),...  73.6 us
    all_gather x1, waiting for transfers between devices, on_device(): table = lax.all_gather(right_vec, 'doc', axis=0, tiled=True)  53.6 us
    scatter-add x1, other arithmetic, backward_one_block(): jax.ops.segment_sum(terms, index_rows.reshape(-1), num_segments=width)  46.8 us
    psum x1, blocking collectives, on_device(): squares = lax.psum(jnp.sum(right_raw * right_raw, axis=0), ('doc', 'feat'))  39.6 us
    psum x1, blocking collectives, on_device(): lax.psum(row_part, ('doc', 'feat')) / docs_total + epsilon  39.3 us
    gather x1, local copies, waits for them, and re-layouts, forward_one_block(): picked = table[index_rows]  33.6 us
    psum x1, waiting for transfers between devices, on_device(): total = lax.psum(partial_value, 'feat')  26.8 us
  transfers between devices with their start and end apart: 3, of which 3 were waited for; matrix products, arithmetic and copies ran while one was open for 1% of the time, Pallas kernels for 0%

commit v1 on v0

v1 whole, which is shorter than its diff:
```python
import functools

import jax
import jax.numpy as jnp
from jax import lax
from jax.experimental import pallas as pl
from jax.experimental.pallas import tpu as pltpu
from jax.sharding import PartitionSpec as P

epsilon = 1e-06
AXES = ("doc", "feat")
MIB = 1024 * 1024


Y_BIT, CORE_BIT, X_BIT, Z_SHIFT = 1, 2, 4, 3
NT = (((1,), (1,)), ((), ()))


def coords():
    d = lax.axis_index("doc")
    y = lax.axis_index("feat")
    return d, d >> 2, y


def full(shape):
    return pl.BlockSpec(shape, lambda *_: (0,) * len(shape))


def params(mib):
    return pltpu.CompilerParams(vmem_limit_bytes=mib * MIB)


def cost(flops, nbytes):
    return pl.CostEstimate(flops=int(flops), bytes_accessed=int(nbytes), transcendentals=0)


def f32(*shape):
    return jax.ShapeDtypeStruct(shape, jnp.float32)


def bf16(*shape):
    return jax.ShapeDtypeStruct(shape, jnp.bfloat16)


def right_kernel(right_ref, m0, m1, m2, m3, turned):
    _, z, _ = coords()
    cols = turned.shape[1]
    turned[...] = right_ref[...].T.reshape(turned.shape)
    for k, out in enumerate((m0, m1, m2, m3)):
        out[...] = turned[z ^ k]


def right_quarters(right):
    rows, cols = right.shape
    q = cols // 4
    return pl.pallas_call(
        right_kernel,
        out_shape=[f32(q, rows)] * 4,
        scratch_shapes=[pltpu.VMEM((4, q, rows), jnp.float32)],
        compiler_params=params(16),
        cost_estimate=cost(0, rows * cols * 8),
        name="right_quarters",
    )(right)


def left_kernel(left_ref, u0, u1, turned):
    _, z, y = coords()
    turned[...] = left_ref[...].T.reshape(turned.shape)
    for k1, out in enumerate((u0, u1)):
        out[...] = turned[2 * ((z >> 1) ^ k1) + y]


def left_quarters(left):
    rows, cols = left.shape
    q = cols // 4
    return pl.pallas_call(
        left_kernel,
        out_shape=[f32(q, rows)] * 2,
        scratch_shapes=[pltpu.VMEM((4, q, rows), jnp.float32)],
        compiler_params=params(16),
        cost_estimate=cost(0, rows * cols * 8),
        name="left_quarters",
    )(left)


def build_kernel(e00, e01, e10, e11, hi_ref, lo_ref):
    d, z, y = coords()
    half = pl.program_id(0)
    step = pl.program_id(1)
    rows = e00.shape[0] // 2
    iota = lax.broadcasted_iota(jnp.int32, (256, 256), 0).astype(jnp.float32).astype(jnp.bfloat16)
    lane_doc = lax.broadcasted_iota(jnp.int32, (8, 256), 1) >> 4
    one = jnp.ones((256, 256), jnp.bfloat16)
    zero = jnp.zeros((256, 256), jnp.bfloat16)

    def spread(row):
        wide = jnp.broadcast_to(row, (16, 256)).astype(jnp.bfloat16)
        return jnp.broadcast_to(wide[None], (16, 16, 256)).reshape(256, 256)

    for k0, (near, far) in enumerate(((e00, e10), (e01, e11))):
        y_rel = ((z & 1) ^ k0) ^ y
        at = pl.multiple_of(step * 8, 8)
        ids = jnp.where(half == 0, near[pl.ds(at, 8), :], far[pl.ds(at, 8), :])
        vals = jnp.where(half == 0, near[pl.ds(rows + at, 8), :], far[pl.ds(rows + at, 8), :])
        ids = ids.astype(jnp.int32)
        rel = (ids >> 8) ^ d
        block = ((rel & 1) << 3) | ((rel & 2) << 1) | (rel >> 2)
        code = (block * 16 + lane_doc).astype(jnp.float32)
        inner = (ids & 255).astype(jnp.float32)
        for t in range(8):
            pick = jnp.where(iota == spread(code[t : t + 1]), one, zero)
            weigh = jnp.where(iota == spread(inner[t : t + 1]), spread(vals[t : t + 1]), zero)
            dense = lax.dot_general(pick, weigh, NT, preferred_element_type=jnp.float32)
            high = dense.astype(jnp.bfloat16)
            low = (dense - high.astype(jnp.float32)).astype(jnp.bfloat16)
            high = high.reshape(16, 16, 256)
            low = low.reshape(16, 16, 256)
            for cc in range(2):
                to = pl.ds(cc * 16 + y_rel * 8, 8)
                hi_ref[to, 16 * t : 16 * t + 16, :] = high[8 * cc : 8 * cc + 8]
                lo_ref[to, 16 * t : 16 * t + 16, :] = low[8 * cc : 8 * cc + 8]


def build(entries):
    docs = entries[0].shape[0] // 2 * 16
    steps = docs // 128
    return pl.pallas_call(
        build_kernel,
        grid=(2, steps),
        in_specs=[full(entries[0].shape)] * 4,
        out_specs=[pl.BlockSpec((32, 128, 256), lambda a, s: (0, a * steps + s, 0))] * 2,
        out_shape=[bf16(32, 2 * docs, 256)] * 2,
        compiler_params=params(32),
        cost_estimate=cost(2 * 2 * docs * 2 * 16 * 256 * 256, 2 * docs * 8192 * 4),
        name="dense_rows",
    )(*entries)


def split_rows(value):
    high = value.astype(jnp.bfloat16)
    low = (value - high.astype(jnp.float32)).astype(jnp.bfloat16)
    return jnp.concatenate([high, low], axis=0)


def add_product(hi_ref, lo_ref, vec, total):
    both = split_rows(vec)
    total[...] += lax.dot_general(
        hi_ref[0], both, NT, preferred_element_type=jnp.float32
    ) + lax.dot_general(lo_ref[0], both, NT, preferred_element_type=jnp.float32)


def forward_kernel(per, count, first, hi_ref, lo_ref, *refs):
    vecs = refs[:count]
    if first:
        (total,) = refs[count:]
    else:
        before, total = refs[count:]
    step = pl.program_id(0)

    @pl.when(step == 0)
    def _():
        if first:
            total[...] = jnp.zeros_like(total)
        else:
            total[...] = before[...]

    for n in range(count):

        @pl.when(step // per == n)
        def _(n=n):
            add_product(hi_ref, lo_ref, vecs[n][step - n * per], total)


def a_spec(docs, block_of):
    return pl.BlockSpec((1, docs, 256), lambda s: (block_of(s), 0, 0))


def forward_part(hi, lo, vecs, before, block_of):
    docs = hi.shape[1]
    q = vecs[0].shape[1]
    per, count = vecs[0].shape[0], len(vecs)
    extra = [] if before is None else [before]
    return pl.pallas_call(
        functools.partial(forward_kernel, per, count, before is None),
        grid=(per * count,),
        in_specs=[a_spec(docs, block_of)] * 2
        + [full(v.shape) for v in vecs]
        + [full((docs, 2 * q))] * len(extra),
        out_specs=full((docs, 2 * q)),
        out_shape=f32(docs, 2 * q),
        compiler_params=params(32),
        cost_estimate=cost(4 * docs * 256 * 256 * per * count, 4 * docs * 256 * per * count),
        name="forward_part",
    )(hi, lo, *vecs, *extra)


def square_row(value, z, cols):
    squares = value * value
    ones = jnp.ones((8, value.shape[1]), jnp.float32)
    sums = lax.dot_general(
        ones,
        jnp.concatenate([squares] * 4, axis=0),
        NT,
        preferred_element_type=jnp.float32,
        precision=lax.Precision.HIGHEST,
    )
    lane = lax.broadcasted_iota(jnp.int32, (8, cols), 1)
    return jnp.where(lane // (cols // 4) == z, sums, 0.0)


def row_to_column(row):
    return jnp.broadcast_to(row, (128, row.shape[1])).T


def last_forward_kernel(per, count, hi_ref, lo_ref, *refs):
    vecs = refs[:count]
    before, u0, u1, alpha, l0, l1, both, sums, total, columns = refs[count:]
    step = pl.program_id(0)

    @pl.when(step == 0)
    def _():
        total[...] = before[...]
        columns[...] = row_to_column(alpha[...])

    for n in range(count):

        @pl.when(step // per == n)
        def _(n=n):
            add_product(hi_ref, lo_ref, vecs[n][step - n * per], total)

    @pl.when(step == per * count - 1)
    def _():
        _, z, _ = coords()
        q, docs = u0.shape
        turned = total[...].T
        product = turned[:q] + turned[q:]
        scale = columns[pl.ds(pl.multiple_of(z * q, q), q), :][:, 0:1]
        l0[...] = product[:, :docs] - scale * u0[...]
        l1[...] = product[:, docs:] - scale * u1[...]
        left = jnp.concatenate([l0[...], l1[...]], axis=1)
        both[...] = split_rows(left)
        sums[...] = square_row(left, z, sums.shape[1])


def last_forward(hi, lo, vecs, before, u0, u1, alpha, block_of):
    docs = hi.shape[1]
    q = vecs[0].shape[1]
    per, count = vecs[0].shape[0], len(vecs)
    return pl.pallas_call(
        functools.partial(last_forward_kernel, per, count),
        grid=(per * count,),
        in_specs=[a_spec(docs, block_of)] * 2
        + [full(v.shape) for v in vecs]
        + [full((docs, 2 * q)), full(u0.shape), full(u1.shape), full(alpha.shape)],
        out_specs=[full(u0.shape), full(u1.shape), full((2 * q, docs)), full((8, 4 * q))],
        out_shape=[f32(*u0.shape), f32(*u1.shape), bf16(2 * q, docs), f32(8, 4 * q)],
        scratch_shapes=[pltpu.VMEM((docs, 2 * q), jnp.float32), pltpu.VMEM((4 * q, 128), jnp.float32)],
        compiler_params=params(32),
        cost_estimate=cost(4 * docs * 256 * 256 * per * count, 4 * docs * 256 * per * count),
        name="last_forward",
    )(hi, lo, *vecs, before, u0, u1, alpha)


def backward_kernel(hi_ref, lo_ref, both_ref, out_ref):
    q = out_ref.shape[1]
    both = both_ref[...]
    got = jnp.dot(both, hi_ref[0], preferred_element_type=jnp.float32) + jnp.dot(
        both, lo_ref[0], preferred_element_type=jnp.float32
    )
    out_ref[0] = got[:q] + got[q:]


def backward_part(hi, lo, both, blocks, block_of):
    docs = hi.shape[1]
    q = both.shape[0] // 2
    return pl.pallas_call(
        backward_kernel,
        grid=(blocks,),
        in_specs=[a_spec(docs, block_of)] * 2 + [full(both.shape)],
        out_specs=pl.BlockSpec((1, q, 256), lambda s: (s, 0, 0)),
        out_shape=f32(blocks, q, 256),
        compiler_params=params(32),
        cost_estimate=cost(4 * docs * 256 * 256 * blocks, 4 * docs * 256 * blocks),
        name="backward_part",
    )(hi, lo, both)


def right_norm_kernel(docs_total, own, peer, r1, r2, r3, v0, v1, v2, v3, beta_sums, g0, g1, g2, g3, sums, columns):
    _, z, _ = coords()
    q = g0.shape[0]
    beta_row = jnp.sqrt(beta_sums[0:1, :] / docs_total + epsilon)
    columns[...] = row_to_column(beta_row)
    beta = columns[pl.ds(pl.multiple_of(z * q, q), q), :][:, 0:1]
    raws = []
    for k, (v, g) in enumerate(zip((v0, v1, v2, v3), (g0, g1, g2, g3))):
        total = ((own[k] + peer[k]) + r1[k]) + (r2[k] + r3[k])
        g[...] = total
        raws.append(total / beta - beta * v[...])
    sums[...] = square_row(jnp.concatenate(raws, axis=1), z, sums.shape[1])


def right_norm(docs_total, own, peer, received, quarters, beta_sums):
    q, rows = quarters[0].shape
    return pl.pallas_call(
        functools.partial(right_norm_kernel, docs_total),
        out_shape=[f32(q, rows)] * 4 + [f32(8, 4 * q)],
        scratch_shapes=[pltpu.VMEM((4 * q, 128), jnp.float32)],
        compiler_params=params(32),
        cost_estimate=cost(rows * q * 64, rows * q * 100),
        name="right_norm",
    )(own, peer, *received, *quarters, beta_sums)


def finish_kernel(docs_total, feat_total, g0, g1, g2, g3, a0, a1, a2, a3, beta_sums, right, search, phibar, rhobar,
                  right_out, search_out, alpha_out, phibar_out, rhobar_out, turned):
    _, z, _ = coords()
    for k, g in enumerate((g0, g1, g2, g3)):
        turned[z ^ k] = g[...]
    got = turned[...].reshape(-1, turned.shape[2]).T
    squares = (a0[0:1, :] + a1[0:1, :]) + (a2[0:1, :] + a3[0:1, :])
    alpha = jnp.sqrt(squares / feat_total + epsilon)
    beta = jnp.sqrt(beta_sums[0:1, :] / docs_total + epsilon)
    rho = jnp.sqrt(rhobar[...] * rhobar[...] + beta * beta)
    cosine = rhobar[...] / rho
    sine = beta / rho
    theta = sine * alpha
    rhobar_out[...] = -cosine * alpha
    phibar_out[...] = sine * phibar[...]
    alpha_out[...] = alpha
    following = (got / beta - beta * right[...]) / alpha
    right_out[...] = following
    search_out[...] = following - (theta / rho) * search[...]


def finish(docs_total, feat_total, pieces, alphas, beta_sums, right, search, phibar, rhobar):
    q, rows = pieces[0].shape
    return pl.pallas_call(
        functools.partial(finish_kernel, docs_total, feat_total),
        out_shape=[f32(*right.shape)] * 2 + [f32(1, 4 * q)] * 3,
        scratch_shapes=[pltpu.VMEM((4, q, rows), jnp.float32)],
        compiler_params=params(32),
        cost_estimate=cost(rows * q * 64, rows * q * 80),
        name="finish",
    )(*pieces, *alphas, beta_sums, right, search, phibar, rhobar)


def left_out_kernel(docs_total, p00, p01, p10, p11, beta_sums, search, solution, phibar, rhobar, left_out, solution_out, turned):
    _, z, y = coords()
    for k1, pair in enumerate(((p00, p01), (p10, p11))):
        for k0, piece in enumerate(pair):
            turned[2 * ((z >> 1) ^ k1) + (y ^ k0)] = piece[...]
    beta = jnp.sqrt(beta_sums[0:1, :] / docs_total + epsilon)
    left_out[...] = turned[...].reshape(-1, turned.shape[2]).T / beta
    rho = jnp.sqrt(rhobar[...] * rhobar[...] + beta * beta)
    phi = rhobar[...] / rho * phibar[...]
    solution_out[...] = solution[...] + (phi / rho) * search[...]


def left_out(docs_total, pieces, beta_sums, search, solution, phibar, rhobar):
    q, docs = pieces[0].shape
    return pl.pallas_call(
        functools.partial(left_out_kernel, docs_total),
        out_shape=[f32(docs, 4 * q), f32(*solution.shape)],
        scratch_shapes=[pltpu.VMEM((4, q, docs), jnp.float32)],
        compiler_params=params(32),
        cost_estimate=cost(docs * q * 16, docs * q * 60),
        name="left_out",
    )(*pieces, beta_sums, search, solution, phibar, rhobar)


def move(value, perm):
    return lax.ppermute(value, AXES, perm)


def swap(value, mask):
    return move(value, [(i, i ^ mask) for i in range(32)])


def doc_rounds():
    rounds = {}
    for k1 in range(2):
        for k0 in range(2):
            perm = []
            for i in range(32):
                z1, z0, y = i >> 4, (i >> 3) & 1, i & 1
                to = ((z1 ^ k1) << 4) | ((y ^ k0) << 3) | (i & 6) | z0
                perm.append((i, to))
            rounds[k1, k0] = perm
    return rounds


def small_sum(value):
    got = [value] + [swap(value, mask) for mask in range(1, 8)]
    while len(got) > 1:
        got = [a + b for a, b in zip(got[::2], got[1::2])]
    return got[0]


def along_z(value):
    return [value] + [swap(value, k << Z_SHIFT) for k in (1, 2, 3)]


def by_columns(
    col_ids, col_vals, left_vec, right_vec, search_dir, solution_vec, alpha_prev, phibar, rhobar
):
    docs_total = left_vec.shape[0] * 16
    feat_total = right_vec.shape[0] * 32
    alpha_row, phibar_row, rhobar_row = (v.reshape(1, -1) for v in (alpha_prev, phibar, rhobar))
    rounds = doc_rounds()

    entries = jnp.concatenate(
        [col_ids.astype(jnp.float32).reshape(-1, 256), col_vals.astype(jnp.float32).reshape(-1, 256)], axis=0
    )
    moved = [move(entries, rounds[k1, k0]) for k1 in range(2) for k0 in range(2)]

    mine = right_quarters(right_vec)
    quarters = [mine[0]] + [swap(mine[k], k << Z_SHIFT) for k in (1, 2, 3)]
    own = jnp.stack(quarters)

    turned = left_quarters(left_vec)
    u0, u1 = move(turned[0], rounds[0, 0]), move(turned[1], rounds[1, 0])

    plane = [swap(own, Y_BIT * (g >> 1) | X_BIT * (g & 1)) for g in (1, 2, 3)]
    own_peer = swap(own, CORE_BIT)
    plane_peer = [swap(p, CORE_BIT) for p in plane]

    hi, lo = build(moved)
    total = forward_part(hi, lo, [own, own_peer], None, lambda s: s + (s // 4) * 12)
    total = forward_part(hi, lo, plane, total, lambda s: s + 4)
    l0, l1, both, beta_part = last_forward(
        hi, lo, plane_peer, total, u0, u1, alpha_row, lambda s: s + 20
    )

    far = backward_part(hi, lo, both, 12, lambda s: s + 20)
    far_peer = swap(far, CORE_BIT)
    near = backward_part(hi, lo, both, 12, lambda s: s + 4)
    near_other = backward_part(hi, lo, both, 4, lambda s: s + 16)
    near_peer = swap(near_other, CORE_BIT)
    received = [
        swap(near[4 * g - 4 : 4 * g] + far_peer[4 * g - 4 : 4 * g], Y_BIT * (g >> 1) | X_BIT * (g & 1))
        for g in (1, 2, 3)
    ]
    near_own = backward_part(hi, lo, both, 4, lambda s: s)

    beta_all = along_z(small_sum(beta_part))
    beta_sums = (beta_all[0] + beta_all[1]) + (beta_all[2] + beta_all[3])
    pieces = [move(l, rounds_back) for l, rounds_back in (
        (l0, back(rounds[0, 0])), (l0, back(rounds[0, 1])), (l1, back(rounds[1, 0])), (l1, back(rounds[1, 1])))]
    left_next, solution_next = left_out(
        docs_total, pieces, beta_sums, search_dir, solution_vec, phibar_row, rhobar_row
    )

    *sent, alpha_part = right_norm(docs_total, near_own, near_peer, received, quarters, beta_sums)
    got = [sent[0]] + [swap(sent[k], k << Z_SHIFT) for k in (1, 2, 3)]
    alphas = along_z(small_sum(alpha_part))
    right_next, search_next, alpha_next, phibar_next, rhobar_next = finish(
        docs_total, feat_total, got, alphas, beta_sums, right_vec, search_dir, phibar_row, rhobar_row
    )
    return (
        left_next,
        right_next,
        search_next,
        solution_next,
        alpha_next.reshape(-1),
        phibar_next.reshape(-1),
        rhobar_next.reshape(-1),
    )


def back(perm):
    return [(b, a) for a, b in perm]


def forward(col_ids, col_vals, table):
    picked = table[col_ids]
    return jnp.sum(col_vals.astype(jnp.float32)[:, :, None] * picked, axis=1)


def backward(col_ids, col_vals, rows_in, width):
    terms = col_vals.astype(jnp.float32)[:, :, None] * rows_in[:, None, :]
    return jax.ops.segment_sum(
        terms.reshape(-1, rows_in.shape[1]), col_ids.reshape(-1), num_segments=width
    )


def by_blocks(
    col_ids, col_vals, left_vec, right_vec, search_dir, solution_vec, alpha_prev, phibar, rhobar
):
    n_feat = lax.axis_size("feat")
    n_doc = lax.axis_size("doc")
    docs_total = left_vec.shape[0] * n_doc
    feat_total = right_vec.shape[0] * n_doc * n_feat
    table = lax.all_gather(right_vec, "doc", axis=0, tiled=True)
    total = lax.psum(forward(col_ids, col_vals, table), "feat")
    left_raw = total - alpha_prev[None, :] * left_vec
    row_part = jnp.sum(left_raw * left_raw, axis=0)
    beta_norm = jnp.sqrt(lax.psum(row_part, "doc") / docs_total + epsilon)
    left_next = left_raw / beta_norm[None, :]
    feature_part = lax.psum_scatter(
        backward(col_ids, col_vals, left_next, table.shape[0]), "doc", scatter_dimension=0, tiled=True
    )
    right_raw = feature_part - beta_norm[None, :] * right_vec
    squares = lax.psum(jnp.sum(right_raw * right_raw, axis=0), AXES)
    alpha_next = jnp.sqrt(squares / feat_total + epsilon)
    right_next = right_raw / alpha_next[None, :]
    rho_val = jnp.sqrt(rhobar * rhobar + beta_norm * beta_norm)
    cosine = rhobar / rho_val
    sine_val = beta_norm / rho_val
    theta_val = sine_val * alpha_next
    phi_val = cosine * phibar
    solution_next = solution_vec + (phi_val / rho_val)[None, :] * search_dir
    search_next = right_next - (theta_val / rho_val)[None, :] * search_dir
    return (
        left_next,
        right_next,
        search_next,
        solution_next,
        alpha_next,
        sine_val * phibar,
        -cosine * alpha_next,
    )


def solution(mesh):
    small = mesh.shape["doc"] == 16 and mesh.shape["feat"] == 2
    rows = P(("feat", "doc"), None)
    return jax.shard_map(
        by_columns if small else by_blocks,
        mesh=mesh,
        in_specs=(P("doc", "feat"), P("doc", "feat"), P("doc", None), rows, rows, rows, P(), P(), P()),
        out_specs=(P("doc", None), rows, rows, rows, P(), P(), P()),
        check_vma=False,
    )
```

time: 347 us -> 163 us (0.47)
  waiting for transfers between devices: 155 us -> 15.8 us
  blocking collectives: 79 us -> 0 us
  Pallas kernels: 0 us -> 64.9 us
  starting transfers between devices: 0.12 us -> 64.6 us
  other arithmetic: 63.2 us -> 0.91 us
  local copies, waits for them, and re-layouts: 35.1 us -> 14.8 us
  between operations: 13.9 us -> 0.98 us
    psum x2 -> x0, blocking collectives: 79 us -> none  [the longest x1 39.6 us: on_device(): squares = lax.psum(jnp.sum(right_raw * right_raw, axis=0), ('doc', 'feat'))]
    reduce_scatter x1 -> x0, waiting for transfers between devices: 73.6 us -> none  [on_device(): lax.psum_scatter(backward(col_ids, col_vals, sent_rows, table.shape[0]),...]
    pallas_call x0 -> x13, Pallas kernels: none -> 64.9 us  [the longest x4 23.7 us: backward_part(): pl.pallas_call(backward_kernel, grid=(blocks,), in_specs=[a_spec(docs, bl...]
    ppermute x0 -> x48, starting transfers between devices: none -> 64.6 us  [move(): return lax.ppermute(value, AXES, perm)]
    all_gather x1 -> x0, waiting for transfers between devices: 53.6 us -> none  [on_device(): table = lax.all_gather(right_vec, 'doc', axis=0, tiled=True)]
    scatter-add x1 -> x0, other arithmetic: 46.8 us -> none  [backward_one_block(): jax.ops.segment_sum(terms, index_rows.reshape(-1), num_segments=width)]
    gather x1 -> x0, local copies, waits for them, and re-layouts: 33.6 us -> none  [forward_one_block(): picked = table[index_rows]]
    psum x1 -> x0, waiting for transfers between devices: 26.8 us -> none  [on_device(): total = lax.psum(partial_value, 'feat')]
  transfers between devices with their start and end apart: 3 -> 48, of which waited for: 3 -> 4; matrix products, arithmetic and copies ran while one was open for 1% -> 1% of each run, Pallas kernels for 0% -> 27%
where the time goes in v1:
time: 163 us; the launch traced here: 162 us
  Pallas kernels  64.9 us (40%)
  starting transfers between devices  64.6 us (40%)
  waiting for transfers between devices  15.8 us (10%)
  local copies, waits for them, and re-layouts  14.8 us (9%)
    ppermute x48, starting transfers between devices, move(): return lax.ppermute(value, AXES, perm)  64.6 us
    pallas_call x4, Pallas kernels, backward_part(): pl.pallas_call(backward_kernel, grid=(blocks,), in_specs=[a_spec(docs, bl...  23.7 us
    pallas_call x2, Pallas kernels, forward_part(): pl.pallas_call(functools.partial(forward_kernel, per, count, before is No...  16.2 us
    ppermute x48, waiting for transfers between devices, move(): return lax.ppermute(value, AXES, perm)  15.8 us
    unnamed x21, local copies, waits for them, and re-layouts  13.5 us
    pallas_call x1, Pallas kernels, last_forward(): pl.pallas_call(functools.partial(last_forward_kernel, per, count), grid=(...  10.9 us
    pallas_call x1, Pallas kernels, build(): pl.pallas_call(build_kernel, grid=(2, steps), in_specs=[full(entries[0].s...  10.6 us
  transfers between devices with their start and end apart: 48, of which 4 were waited for; matrix products, arithmetic and copies ran while one was open for 1% of the time, Pallas kernels for 27%

profile of v1, /device:TPU:0, one launch (start us, length us, event | category | flops | bytes accessed | tf_op | source)
XLA Modules:
  0.0 162.0 jit_solution(14643825149207308619)
XLA Ops:
  0.6 0.9 copy-done.2
  1.7 3.1 %collective-permute-start.4 = (f32[64,256]{1,0:T(8,128)S(1)}, f32[64,256]{1,0:T(8,128)S(1)}, u32[]{:S(2)}, u32[]{:S(2)}) collective-permute-start(f32[64,256]{1,0:T(8,128)S(1)} %get-tuple-element.34), channel_id=1, source_target_pairs={{0,8},{1,9},{2,10},{3,11},{4,12},{5,13},{6,14},{7,15},{8,0},{9,1},... | collective-permute-start | bytes 196616 | tf_op jit(solution)/shard_map/ppermute | solution.py:372
  4.8 2.6 %collective-permute-start.5 = (f32[64,256]{1,0:T(8,128)S(1)}, f32[64,256]{1,0:T(8,128)S(1)}, u32[]{:S(2)}, u32[]{:S(2)}) collective-permute-start(f32[64,256]{1,0:T(8,128)S(1)} %get-tuple-element.35), channel_id=1, source_target_pairs={{0,16},{1,17},{2,18},{3,19},{4,20},{5,21},{6,22},{7,23},{8,24},{9,... | collective-permute-start | bytes 196616 | tf_op jit(solution)/shard_map/ppermute | solution.py:372
  7.4 0.8 convert_element_type.4
  8.5 0.8 copy.19
  10.1 4.5 %collective-permute-start.1 = (f32[64,256]{1,0:T(8,128)S(1)}, f32[64,256]{1,0:T(8,128)S(1)}, u32[]{:S(2)}, u32[]{:S(2)}) collective-permute-start(f32[64,256]{1,0:T(8,128)S(1)} %constant_dynamic-update-slice_fusion), channel_id=1, source_target_pairs={{0,8},{1,0},{2,10},{3,2},{4,12},{5,4},{6,14},{7,6},{8,9},{9,1},{10... | collective-permute-start | bytes 196616 | tf_op jit(solution)/shard_map/ppermute | solution.py:372
  14.6 1.0 copy-done.5
  15.9 1.8 %collective-permute-start.2 = (f32[64,256]{1,0:T(8,128)S(1)}, f32[64,256]{1,0:T(8,128)S(1)}, u32[]{:S(2)}, u32[]{:S(2)}) collective-permute-start(f32[64,256]{1,0:T(8,128)S(1)} %constant_dynamic-update-slice_fusion), channel_id=1, source_target_pairs={{0,16},{1,24},{2,18},{3,26},{4,20},{5,28},{6,22},{7,30},{8,17},{9,... | collective-permute-start | bytes 196616 | tf_op jit(solution)/shard_map/ppermute | solution.py:372
  17.7 0.8 collective-permute-start.3
  19.2 5.4 %collective-permute-start.11 = (f32[4,64,256]{2,1,0:T(8,128)S(1)}, f32[4,64,256]{2,1,0:T(8,128)S(1)}, u32[]{:S(2)}, u32[]{:S(2)}) collective-permute-start(f32[4,64,256]{2,1,0:T(8,128)S(1)} %pad_maximum_fusion.refs_0_), channel_id=1, source_target_pairs={{0,5},{1,4},{2,7},{3,6},{4,1},{5,0},{6,3},{7,2},{8,13},{9,12},{10,... | collective-permute-start | bytes 786440 | tf_op jit(solution)/shard_map/ppermute | solution.py:372
  25.3 10.6 %dense_rows.1 = (bf16[32,1024,256]{2,1,0:T(8,128)(2,1)S(1)}, bf16[32,1024,256]{2,1,0:T(8,128)(2,1)}) custom-call(f32[64,256]{1,0:T(8,128)S(1)} %collective-permute-done.e00, f32[64,256]{1,0:T(8,128)S(1)} %collective-permute-done.1.e01, f32[64,256]{1,0:T(8,128)S(1)} %collective-permute-done.2.e10, f32[64,256]{1,0:T(8,128)S(1)} %collective-permute-done.3.e11), custom_call_target="tpu_custom_call" | custom-call | flops 4294967296 | bytes 33554432 | tf_op jit(solution)/shard_map/dense_rows/pallas_call | solution.py:127
  35.9 5.8 %copy-done = bf16[32,1024,256]{2,1,0:T(8,128)(2,1)} copy-done((bf16[32,1024,256]{2,1,0:T(8,128)(2,1)}, bf16[32,1024,256]{2,1,0:T(8,128)(2,1)S(1)}, u32[]{:S(2)}) %copy-start) | copy-done | bytes 16777240
  41.6 2.9 %collective-permute-start.15 = (f32[64,512]{1,0:T(8,128)S(1)}, f32[64,512]{1,0:T(8,128)S(1)}, u32[]{:S(2)}, u32[]{:S(2)}) collective-permute-start(f32[64,512]{1,0:T(8,128)S(1)} %get-tuple-element.38), channel_id=1, source_target_pairs={{0,16},{1,24},{2,18},{3,26},{4,20},{5,28},{6,22},{7,30},{8,17},{9,... | collective-permute-start | bytes 393224 | tf_op jit(solution)/shard_map/ppermute | solution.py:372
  45.1 5.8 %copy-done.1 = bf16[32,1024,256]{2,1,0:T(8,128)(2,1)S(1)} copy-done((bf16[32,1024,256]{2,1,0:T(8,128)(2,1)S(1)}, bf16[32,1024,256]{2,1,0:T(8,128)(2,1)}, u32[]{:S(2)}) %copy-start.1) | copy-done | bytes 16777240
  50.8 6.6 %forward_part.2.refs_3_ = f32[1024,128]{1,0:T(8,128)S(1)} custom-call(bf16[32,1024,256]{2,1,0:T(8,128)(2,1)S(1)} %copy-done.1, bf16[32,1024,256]{2,1,0:T(8,128)(2,1)} %get-tuple-element.32.lo_ref, f32[4,64,256]{2,1,0:T(8,128)S(1)} %pad_maximum_fusion.refs_0_, f32[4,64,256]{2,1,0:T(8,128)S(1)} %collective-permute-done.13.refs_1_), custom_call_target="tpu_custom_call" | custom-call | flops 2147483648 | bytes 8388608 | tf_op jit(solution)/shard_map/forward_part/pallas_call | solution.py:183
  57.5 9.6 %forward_part.3.refs_3_ = f32[1024,128]{1,0:T(8,128)S(1)} custom-call(bf16[32,1024,256]{2,1,0:T(8,128)(2,1)S(1)} %copy-done.1, bf16[32,1024,256]{2,1,0:T(8,128)(2,1)} %get-tuple-element.32.lo_ref, f32[4,64,256]{2,1,0:T(8,128)S(1)} %collective-permute-done.7.refs_0_, f32[4,64,256]{2,1,0:T(8,128)S(1)} %collective-permute-done.9.refs_1_, ...), custom_call_target="tpu_custom_call" | custom-call | flops 3221225472 | bytes 12582912 | tf_op jit(solution)/shard_map/forward_part/pallas_call | solution.py:183
  67.2 10.9 %last_forward.1 = (f32[64,512]{1,0:T(8,128)S(1)}, f32[64,512]{1,0:T(8,128)S(1)}, bf16[128,1024]{1,0:T(8,128)(2,1)S(1)}, f32[8,256]{1,0:T(8,128)S(1)}) custom-call(bf16[32,1024,256]{2,1,0:T(8,128)(2,1)S(1)} %copy-done.1, bf16[32,1024,256]{2,1,0:T(8,128)(2,1)} %get-tuple-element.32.lo_ref, f32[4,64,256]{2,1,0:T(8,128)S(1)} %collective-permute-done.8.refs_0_, ...), custom_call_target="tpu_custom_call" | custom-call | flops 3221225472 | bytes 12582912 | tf_op jit(solution)/shard_map/last_forward/pallas_call | solution.py:249
  78.0 8.7 %backward_part.7 = f32[12,64,256]{2,1,0:T(8,128)S(1)} custom-call(bf16[32,1024,256]{2,1,0:T(8,128)(2,1)S(1)} %copy-done.1, bf16[32,1024,256]{2,1,0:T(8,128)(2,1)} %get-tuple-element.32.lo_ref, bf16[128,1024]{1,0:T(8,128)(2,1)S(1)} %get-tuple-element.43.both_ref), custom_call_target="tpu_custom_call" | custom-call | flops 3221225472 | bytes 12582912 | tf_op jit(solution)/shard_map/backward_part/pallas_call | solution.py:276
  87.3 1.9 %collective-permute-start.20 = (f32[8,256]{1,0:T(8,128)S(1)}, f32[8,256]{1,0:T(8,128)S(1)}, u32[]{:S(2)}, u32[]{:S(2)}) collective-permute-start(f32[8,256]{1,0:T(8,128)S(1)} %get-tuple-element.41), channel_id=1, source_target_pairs={{0,1},{1,0},{2,3},{3,2},{4,5},{5,4},{6,7},{7,6},{8,9},{9,8},{10,11... | collective-permute-start | bytes 24584 | tf_op jit(solution)/shard_map/ppermute | solution.py:372
  89.4 8.7 %backward_part.6 = f32[12,64,256]{2,1,0:T(8,128)S(1)} custom-call(bf16[32,1024,256]{2,1,0:T(8,128)(2,1)S(1)} %copy-done.1, bf16[32,1024,256]{2,1,0:T(8,128)(2,1)} %get-tuple-element.32.lo_ref, bf16[128,1024]{1,0:T(8,128)(2,1)S(1)} %get-tuple-element.43.both_ref), custom_call_target="tpu_custom_call" | custom-call | flops 3221225472 | bytes 12582912 | tf_op jit(solution)/shard_map/backward_part/pallas_call | solution.py:276
  98.2 1.5 collective-permute-start.23
  99.6 1.9 %collective-permute-start.24 = (f32[8,256]{1,0:T(8,128)S(1)}, f32[8,256]{1,0:T(8,128)S(1)}, u32[]{:S(2)}, u32[]{:S(2)}) collective-permute-start(f32[8,256]{1,0:T(8,128)S(1)} %get-tuple-element.41), channel_id=1, source_target_pairs={{0,5},{1,4},{2,7},{3,6},{4,1},{5,0},{6,3},{7,2},{8,13},{9,12},{10,... | collective-permute-start | bytes 24584 | tf_op jit(solution)/shard_map/ppermute | solution.py:372
  102.1 0.8 collective-permute-start.26
  102.9 3.1 %backward_part.5 = f32[4,64,256]{2,1,0:T(8,128)S(1)} custom-call(bf16[32,1024,256]{2,1,0:T(8,128)(2,1)S(1)} %copy-done.1, bf16[32,1024,256]{2,1,0:T(8,128)(2,1)} %get-tuple-element.32.lo_ref, bf16[128,1024]{1,0:T(8,128)(2,1)S(1)} %get-tuple-element.43.both_ref), custom_call_target="tpu_custom_call" | custom-call | flops 1073741824 | bytes 4194304 | tf_op jit(solution)/shard_map/backward_part/pallas_call | solution.py:276
  106.4 1.7 %collective-permute-start.27 = (f32[8,256]{1,0:T(8,128)S(1)}, f32[8,256]{1,0:T(8,128)S(1)}, u32[]{:S(2)}, u32[]{:S(2)}) collective-permute-start(f32[8,256]{1,0:T(8,128)S(1)} %add_add_fusion.2), channel_id=1, source_target_pairs={{0,8},{1,9},{2,10},{3,11},{4,12},{5,13},{6,14},{7,15},{8,0},{9,1},... | collective-permute-start | bytes 24584 | tf_op jit(solution)/shard_map/ppermute | solution.py:372
  108.2 1.0 collective-permute-start.28
  109.1 1.7 %collective-permute-start.29 = (f32[8,256]{1,0:T(8,128)S(1)}, f32[8,256]{1,0:T(8,128)S(1)}, u32[]{:S(2)}, u32[]{:S(2)}) collective-permute-start(f32[8,256]{1,0:T(8,128)S(1)} %add_add_fusion.2), channel_id=1, source_target_pairs={{0,24},{1,25},{2,26},{3,27},{4,28},{5,29},{6,30},{7,31},{8,16},{9,... | collective-permute-start | bytes 24584 | tf_op jit(solution)/shard_map/ppermute | solution.py:372
  111.0 1.3 collective-permute-start.32
  112.3 1.9 %collective-permute-start.33 = (f32[4,64,256]{2,1,0:T(8,128)S(1)}, f32[4,64,256]{2,1,0:T(8,128)S(1)}, u32[]{:S(2)}, u32[]{:S(2)}) collective-permute-start(f32[4,64,256]{2,1,0:T(8,128)S(1)} %get-tuple-element.56), channel_id=1, source_target_pairs={{0,1},{1,0},{2,3},{3,2},{4,5},{5,4},{6,7},{7,6},{8,9},{9,8},{10,11... | collective-permute-start | bytes 786440 | tf_op jit(solution)/shard_map/ppermute | solution.py:372
  114.6 3.1 %backward_part.4.own = f32[4,64,256]{2,1,0:T(8,128)S(1)} custom-call(bf16[32,1024,256]{2,1,0:T(8,128)(2,1)S(1)} %copy-done.1, bf16[32,1024,256]{2,1,0:T(8,128)(2,1)} %get-tuple-element.32.lo_ref, bf16[128,1024]{1,0:T(8,128)(2,1)S(1)} %get-tuple-element.43.both_ref), custom_call_target="tpu_custom_call" | custom-call | flops 1073741824 | bytes 4194304 | tf_op jit(solution)/shard_map/backward_part/pallas_call | solution.py:276
  117.8 0.7 collective-permute-start.16
  118.5 3.8 %collective-permute-start.17 = (f32[64,512]{1,0:T(8,128)S(1)}, f32[64,512]{1,0:T(8,128)S(1)}, u32[]{:S(2)}, u32[]{:S(2)}) collective-permute-start(f32[64,512]{1,0:T(8,128)S(1)} %get-tuple-element.39), channel_id=1, source_target_pairs={{8,0},{0,1},{10,2},{2,3},{12,4},{4,5},{14,6},{6,7},{9,8},{1,9},{11... | collective-permute-start | bytes 393224 | tf_op jit(solution)/shard_map/ppermute | solution.py:372
  122.3 6.3 %collective-permute-done.33.r2 = f32[4,64,256]{2,1,0:T(8,128)S(1)} collective-permute-done((f32[4,64,256]{2,1,0:T(8,128)S(1)}, f32[4,64,256]{2,1,0:T(8,128)S(1)}, u32[]{:S(2)}, u32[]{:S(2)}) %collective-permute-start.33) | collective-permute-done | bytes 262176 | tf_op jit(solution)/shard_map/ppermute | solution.py:372
  128.6 1.1 right_norm.1
  129.8 2.5 %collective-permute-start.38 = (f32[8,256]{1,0:T(8,128)S(1)}, f32[8,256]{1,0:T(8,128)S(1)}, u32[]{:S(2)}, u32[]{:S(2)}) collective-permute-start(f32[8,256]{1,0:T(8,128)S(1)} %get-tuple-element.48), channel_id=1, source_target_pairs={{0,1},{1,0},{2,3},{3,2},{4,5},{5,4},{6,7},{7,6},{8,9},{9,8},{10,11... | collective-permute-start | bytes 24584 | tf_op jit(solution)/shard_map/ppermute | solution.py:372
  132.4 3.4 %collective-permute-start.42 = (f32[8,256]{1,0:T(8,128)S(1)}, f32[8,256]{1,0:T(8,128)S(1)}, u32[]{:S(2)}, u32[]{:S(2)}) collective-permute-start(f32[8,256]{1,0:T(8,128)S(1)} %get-tuple-element.48), channel_id=1, source_target_pairs={{0,5},{1,4},{2,7},{3,6},{4,1},{5,0},{6,3},{7,2},{8,13},{9,12},{10,... | collective-permute-start | bytes 24584 | tf_op jit(solution)/shard_map/ppermute | solution.py:372
  135.9 1.2 collective-permute-start.44
  137.1 3.5 %collective-permute-start.19 = (f32[64,512]{1,0:T(8,128)S(1)}, f32[64,512]{1,0:T(8,128)S(1)}, u32[]{:S(2)}, u32[]{:S(2)}) collective-permute-start(f32[64,512]{1,0:T(8,128)S(1)} %get-tuple-element.40), channel_id=1, source_target_pairs={{24,0},{16,1},{26,2},{18,3},{28,4},{20,5},{30,6},{22,7},{25,8},{17... | collective-permute-start | bytes 393224 | tf_op jit(solution)/shard_map/ppermute | solution.py:372
  140.6 2.8 %collective-permute-start.36 = (f32[64,256]{1,0:T(8,128)S(1)}, f32[64,256]{1,0:T(8,128)S(1)}, u32[]{:S(2)}, u32[]{:S(2)}) collective-permute-start(f32[64,256]{1,0:T(8,128)S(1)} %get-tuple-element.46), channel_id=1, source_target_pairs={{0,16},{1,17},{2,18},{3,19},{4,20},{5,21},{6,22},{7,23},{8,24},{9,... | collective-permute-start | bytes 196616 | tf_op jit(solution)/shard_map/ppermute | solution.py:372
  143.5 1.5 collective-permute-start.37
  145.0 6.0 %collective-permute-done.18.p10 = f32[64,512]{1,0:T(8,128)S(1)} collective-permute-done((f32[64,512]{1,0:T(8,128)S(1)}, f32[64,512]{1,0:T(8,128)S(1)}, u32[]{:S(2)}, u32[]{:S(2)}) %collective-permute-start.18) | collective-permute-done | bytes 131104 | tf_op jit(solution)/shard_map/ppermute | solution.py:372
  151.0 1.3 collective-permute-start.45
  152.4 2.5 %collective-permute-start.46 = (f32[8,256]{1,0:T(8,128)S(1)}, f32[8,256]{1,0:T(8,128)S(1)}, u32[]{:S(2)}, u32[]{:S(2)}) collective-permute-start(f32[8,256]{1,0:T(8,128)S(1)} %add_add_fusion.a0), channel_id=1, source_target_pairs={{0,16},{1,17},{2,18},{3,19},{4,20},{5,21},{6,22},{7,23},{8,24},{9,... | collective-permute-start | bytes 24584 | tf_op jit(solution)/shard_map/ppermute | solution.py:372
  154.9 0.7 collective-permute-done.45.a1
  155.5 1.7 %collective-permute-start.47 = (f32[8,256]{1,0:T(8,128)S(1)}, f32[8,256]{1,0:T(8,128)S(1)}, u32[]{:S(2)}, u32[]{:S(2)}) collective-permute-start(f32[8,256]{1,0:T(8,128)S(1)} %add_add_fusion.a0), channel_id=1, source_target_pairs={{0,24},{1,25},{2,26},{3,27},{4,28},{5,29},{6,30},{7,31},{8,16},{9,... | collective-permute-start | bytes 24584 | tf_op jit(solution)/shard_map/ppermute | solution.py:372
  157.2 1.1 left_out.1
  158.3 2.7 %collective-permute-done.47.a3 = f32[8,256]{1,0:T(8,128)S(1)} collective-permute-done((f32[8,256]{1,0:T(8,128)S(1)}, f32[8,256]{1,0:T(8,128)S(1)}, u32[]{:S(2)}, u32[]{:S(2)}) %collective-permute-start.47) | collective-permute-done | bytes 8224 | tf_op jit(solution)/shard_map/ppermute | solution.py:372
  161.0 1.0 finish.1
  (93 shorter events, 6.0 us)
Async XLA Ops:
  1.7 14.2 %collective-permute-start.4 = (f32[64,256]{1,0:T(8,128)S(1)}, f32[64,256]{1,0:T(8,128)S(1)}, u32[]{:S(2)}, u32[]{:S(2)}) collective-permute-start(f32[64,256]{1,0:T(8,128)S(1)} %get-tuple-element.34), channel_id=1, source_target_pairs={{0,8},{1,9},{2,10},{3,11},{4,12},{5,13},{6,14},{7,15},{8,0},{9,1},... | collective-permute-start | bytes 196616 | tf_op jit(solution)/shard_map/ppermute | solution.py:372
  4.8 12.8 %collective-permute-start.5 = (f32[64,256]{1,0:T(8,128)S(1)}, f32[64,256]{1,0:T(8,128)S(1)}, u32[]{:S(2)}, u32[]{:S(2)}) collective-permute-start(f32[64,256]{1,0:T(8,128)S(1)} %get-tuple-element.35), channel_id=1, source_target_pairs={{0,16},{1,17},{2,18},{3,19},{4,20},{5,21},{6,22},{7,23},{8,24},{9,... | collective-permute-start | bytes 196616 | tf_op jit(solution)/shard_map/ppermute | solution.py:372
  7.4 11.0 %collective-permute-start.6 = (f32[64,256]{1,0:T(8,128)S(1)}, f32[64,256]{1,0:T(8,128)S(1)}, u32[]{:S(2)}, u32[]{:S(2)}) collective-permute-start(f32[64,256]{1,0:T(8,128)S(1)} %get-tuple-element.36), channel_id=1, source_target_pairs={{0,24},{1,25},{2,26},{3,27},{4,28},{5,29},{6,30},{7,31},{8,16},{9,... | collective-permute-start | bytes 196616 | tf_op jit(solution)/shard_map/ppermute | solution.py:372
  9.5 9.7 %collective-permute-start = (f32[64,256]{1,0:T(8,128)S(1)}, f32[64,256]{1,0:T(8,128)S(1)}, u32[]{:S(2)}, u32[]{:S(2)}) collective-permute-start(f32[64,256]{1,0:T(8,128)S(1)} %constant_dynamic-update-slice_fusion), channel_id=1, source_target_pairs={{0,0},{1,8},{2,2},{3,10},{4,4},{5,12},{6,6},{7,14},{8,1},{9,9},{10... | collective-permute-start | bytes 196616 | tf_op jit(solution)/shard_map/ppermute | solution.py:372
  10.1 9.1 %collective-permute-start.1 = (f32[64,256]{1,0:T(8,128)S(1)}, f32[64,256]{1,0:T(8,128)S(1)}, u32[]{:S(2)}, u32[]{:S(2)}) collective-permute-start(f32[64,256]{1,0:T(8,128)S(1)} %constant_dynamic-update-slice_fusion), channel_id=1, source_target_pairs={{0,8},{1,0},{2,10},{3,2},{4,12},{5,4},{6,14},{7,6},{8,9},{9,1},{10... | collective-permute-start | bytes 196616 | tf_op jit(solution)/shard_map/ppermute | solution.py:372
  15.9 8.8 %collective-permute-start.2 = (f32[64,256]{1,0:T(8,128)S(1)}, f32[64,256]{1,0:T(8,128)S(1)}, u32[]{:S(2)}, u32[]{:S(2)}) collective-permute-start(f32[64,256]{1,0:T(8,128)S(1)} %constant_dynamic-update-slice_fusion), channel_id=1, source_target_pairs={{0,16},{1,24},{2,18},{3,26},{4,20},{5,28},{6,22},{7,30},{8,17},{9,... | collective-permute-start | bytes 196616 | tf_op jit(solution)/shard_map/ppermute | solution.py:372
  17.7 7.5 %collective-permute-start.3 = (f32[64,256]{1,0:T(8,128)S(1)}, f32[64,256]{1,0:T(8,128)S(1)}, u32[]{:S(2)}, u32[]{:S(2)}) collective-permute-start(f32[64,256]{1,0:T(8,128)S(1)} %constant_dynamic-update-slice_fusion), channel_id=1, source_target_pairs={{0,24},{1,16},{2,26},{3,18},{4,28},{5,20},{6,30},{7,22},{8,25},{9,... | collective-permute-start | bytes 196616 | tf_op jit(solution)/shard_map/ppermute | solution.py:372
  18.4 48.7 %collective-permute-start.14 = (f32[64,512]{1,0:T(8,128)S(1)}, f32[64,512]{1,0:T(8,128)S(1)}, u32[]{:S(2)}, u32[]{:S(2)}) collective-permute-start(f32[64,512]{1,0:T(8,128)S(1)} %get-tuple-element.37), channel_id=1, source_target_pairs={{0,0},{1,8},{2,2},{3,10},{4,4},{5,12},{6,6},{7,14},{8,1},{9,9},{10... | collective-permute-start | bytes 393224 | tf_op jit(solution)/shard_map/ppermute | solution.py:372
  19.1 22.5 %collective-permute-start.13 = (f32[4,64,256]{2,1,0:T(8,128)S(1)}, f32[4,64,256]{2,1,0:T(8,128)S(1)}, u32[]{:S(2)}, u32[]{:S(2)}) collective-permute-start(f32[4,64,256]{2,1,0:T(8,128)S(1)} %pad_maximum_fusion.refs_0_), channel_id=1, source_target_pairs={{0,2},{1,3},{2,0},{3,1},{4,6},{5,7},{6,4},{7,5},{8,10},{9,11},{10,... | collective-permute-start | bytes 786440 | tf_op jit(solution)/shard_map/ppermute | solution.py:372
  19.2 25.3 %collective-permute-start.11 = (f32[4,64,256]{2,1,0:T(8,128)S(1)}, f32[4,64,256]{2,1,0:T(8,128)S(1)}, u32[]{:S(2)}, u32[]{:S(2)}) collective-permute-start(f32[4,64,256]{2,1,0:T(8,128)S(1)} %pad_maximum_fusion.refs_0_), channel_id=1, source_target_pairs={{0,5},{1,4},{2,7},{3,6},{4,1},{5,0},{6,3},{7,2},{8,13},{9,12},{10,... | collective-permute-start | bytes 786440 | tf_op jit(solution)/shard_map/ppermute | solution.py:372
  24.7 20.3 %collective-permute-start.7 = (f32[4,64,256]{2,1,0:T(8,128)S(1)}, f32[4,64,256]{2,1,0:T(8,128)S(1)}, u32[]{:S(2)}, u32[]{:S(2)}) collective-permute-start(f32[4,64,256]{2,1,0:T(8,128)S(1)} %pad_maximum_fusion.refs_0_), channel_id=1, source_target_pairs={{0,4},{1,5},{2,6},{3,7},{4,0},{5,1},{6,2},{7,3},{8,12},{9,13},{10,... | collective-permute-start | bytes 786440 | tf_op jit(solution)/shard_map/ppermute | solution.py:372
  25.2 19.3 %collective-permute-start.9 = (f32[4,64,256]{2,1,0:T(8,128)S(1)}, f32[4,64,256]{2,1,0:T(8,128)S(1)}, u32[]{:S(2)}, u32[]{:S(2)}) collective-permute-start(f32[4,64,256]{2,1,0:T(8,128)S(1)} %pad_maximum_fusion.refs_0_), channel_id=1, source_target_pairs={{0,1},{1,0},{2,3},{3,2},{4,5},{5,4},{6,7},{7,6},{8,9},{9,8},{10,11... | collective-permute-start | bytes 786440 | tf_op jit(solution)/shard_map/ppermute | solution.py:372
  41.6 25.5 %collective-permute-start.15 = (f32[64,512]{1,0:T(8,128)S(1)}, f32[64,512]{1,0:T(8,128)S(1)}, u32[]{:S(2)}, u32[]{:S(2)}) collective-permute-start(f32[64,512]{1,0:T(8,128)S(1)} %get-tuple-element.38), channel_id=1, source_target_pairs={{0,16},{1,24},{2,18},{3,26},{4,20},{5,28},{6,22},{7,30},{8,17},{9,... | collective-permute-start | bytes 393224 | tf_op jit(solution)/shard_map/ppermute | solution.py:372
  44.5 22.7 %collective-permute-start.10 = (f32[4,64,256]{2,1,0:T(8,128)S(1)}, f32[4,64,256]{2,1,0:T(8,128)S(1)}, u32[]{:S(2)}, u32[]{:S(2)}) collective-permute-start(f32[4,64,256]{2,1,0:T(8,128)S(1)} %collective-permute-done.9.refs_1_), channel_id=1, source_target_pairs={{0,2},{1,3},{2,0},{3,1},{4,6},{5,7},{6,4},{7,5},{8,10},{9,11},{10,... | collective-permute-start | bytes 786440 | tf_op jit(solution)/shard_map/ppermute | solution.py:372
  44.5 22.7 %collective-permute-start.12 = (f32[4,64,256]{2,1,0:T(8,128)S(1)}, f32[4,64,256]{2,1,0:T(8,128)S(1)}, u32[]{:S(2)}, u32[]{:S(2)}) collective-permute-start(f32[4,64,256]{2,1,0:T(8,128)S(1)} %collective-permute-done.11.refs_2_), channel_id=1, source_target_pairs={{0,2},{1,3},{2,0},{3,1},{4,6},{5,7},{6,4},{7,5},{8,10},{9,11},{10,... | collective-permute-start | bytes 786440 | tf_op jit(solution)/shard_map/ppermute | solution.py:372
  45.0 22.2 %collective-permute-start.8 = (f32[4,64,256]{2,1,0:T(8,128)S(1)}, f32[4,64,256]{2,1,0:T(8,128)S(1)}, u32[]{:S(2)}, u32[]{:S(2)}) collective-permute-start(f32[4,64,256]{2,1,0:T(8,128)S(1)} %collective-permute-done.7.refs_0_), channel_id=1, source_target_pairs={{0,2},{1,3},{2,0},{3,1},{4,6},{5,7},{6,4},{7,5},{8,10},{9,11},{10,... | collective-permute-start | bytes 786440 | tf_op jit(solution)/shard_map/ppermute | solution.py:372
  86.8 24.1 %collective-permute-start.31 = (f32[12,64,256]{2,1,0:T(8,128)S(1)}, f32[12,64,256]{2,1,0:T(8,128)S(1)}, u32[]{:S(2)}, u32[]{:S(2)}) collective-permute-start(f32[12,64,256]{2,1,0:T(8,128)S(1)} %backward_part.7), channel_id=1, source_target_pairs={{0,2},{1,3},{2,0},{3,1},{4,6},{5,7},{6,4},{7,5},{8,10},{9,11},{10,... | collective-permute-start | bytes 2359304 | tf_op jit(solution)/shard_map/ppermute | solution.py:372
  87.3 12.3 %collective-permute-start.20 = (f32[8,256]{1,0:T(8,128)S(1)}, f32[8,256]{1,0:T(8,128)S(1)}, u32[]{:S(2)}, u32[]{:S(2)}) collective-permute-start(f32[8,256]{1,0:T(8,128)S(1)} %get-tuple-element.41), channel_id=1, source_target_pairs={{0,1},{1,0},{2,3},{3,2},{4,5},{5,4},{6,7},{7,6},{8,9},{9,8},{10,11... | collective-permute-start | bytes 24584 | tf_op jit(solution)/shard_map/ppermute | solution.py:372
  89.2 12.4 %collective-permute-start.21 = (f32[8,256]{1,0:T(8,128)S(1)}, f32[8,256]{1,0:T(8,128)S(1)}, u32[]{:S(2)}, u32[]{:S(2)}) collective-permute-start(f32[8,256]{1,0:T(8,128)S(1)} %get-tuple-element.41), channel_id=1, source_target_pairs={{0,2},{1,3},{2,0},{3,1},{4,6},{5,7},{6,4},{7,5},{8,10},{9,11},{10,... | collective-permute-start | bytes 24584 | tf_op jit(solution)/shard_map/ppermute | solution.py:372
  89.2 13.0 %collective-permute-start.22 = (f32[8,256]{1,0:T(8,128)S(1)}, f32[8,256]{1,0:T(8,128)S(1)}, u32[]{:S(2)}, u32[]{:S(2)}) collective-permute-start(f32[8,256]{1,0:T(8,128)S(1)} %get-tuple-element.41), channel_id=1, source_target_pairs={{0,3},{1,2},{2,1},{3,0},{4,7},{5,6},{6,5},{7,4},{8,11},{9,10},{10,... | collective-permute-start | bytes 24584 | tf_op jit(solution)/shard_map/ppermute | solution.py:372
  98.2 7.9 %collective-permute-start.23 = (f32[8,256]{1,0:T(8,128)S(1)}, f32[8,256]{1,0:T(8,128)S(1)}, u32[]{:S(2)}, u32[]{:S(2)}) collective-permute-start(f32[8,256]{1,0:T(8,128)S(1)} %get-tuple-element.41), channel_id=1, source_target_pairs={{0,4},{1,5},{2,6},{3,7},{4,0},{5,1},{6,2},{7,3},{8,12},{9,13},{10,... | collective-permute-start | bytes 24584 | tf_op jit(solution)/shard_map/ppermute | solution.py:372
  99.6 6.7 %collective-permute-start.24 = (f32[8,256]{1,0:T(8,128)S(1)}, f32[8,256]{1,0:T(8,128)S(1)}, u32[]{:S(2)}, u32[]{:S(2)}) collective-permute-start(f32[8,256]{1,0:T(8,128)S(1)} %get-tuple-element.41), channel_id=1, source_target_pairs={{0,5},{1,4},{2,7},{3,6},{4,1},{5,0},{6,3},{7,2},{8,13},{9,12},{10,... | collective-permute-start | bytes 24584 | tf_op jit(solution)/shard_map/ppermute | solution.py:372
  101.6 4.8 %collective-permute-start.25 = (f32[8,256]{1,0:T(8,128)S(1)}, f32[8,256]{1,0:T(8,128)S(1)}, u32[]{:S(2)}, u32[]{:S(2)}) collective-permute-start(f32[8,256]{1,0:T(8,128)S(1)} %get-tuple-element.41), channel_id=1, source_target_pairs={{0,6},{1,7},{2,4},{3,5},{4,2},{5,3},{6,0},{7,1},{8,14},{9,15},{10,... | collective-permute-start | bytes 24584 | tf_op jit(solution)/shard_map/ppermute | solution.py:372
  102.1 4.3 %collective-permute-start.26 = (f32[8,256]{1,0:T(8,128)S(1)}, f32[8,256]{1,0:T(8,128)S(1)}, u32[]{:S(2)}, u32[]{:S(2)}) collective-permute-start(f32[8,256]{1,0:T(8,128)S(1)} %get-tuple-element.41), channel_id=1, source_target_pairs={{0,7},{1,6},{2,5},{3,4},{4,3},{5,2},{6,1},{7,0},{8,15},{9,14},{10,... | collective-permute-start | bytes 24584 | tf_op jit(solution)/shard_map/ppermute | solution.py:372
  106.1 12.4 %collective-permute-start.30 = (f32[4,64,256]{2,1,0:T(8,128)S(1)}, f32[4,64,256]{2,1,0:T(8,128)S(1)}, u32[]{:S(2)}, u32[]{:S(2)}) collective-permute-start(f32[4,64,256]{2,1,0:T(8,128)S(1)} %backward_part.5), channel_id=1, source_target_pairs={{0,2},{1,3},{2,0},{3,1},{4,6},{5,7},{6,4},{7,5},{8,10},{9,11},{10,... | collective-permute-start | bytes 786440 | tf_op jit(solution)/shard_map/ppermute | solution.py:372
  106.4 5.9 %collective-permute-start.27 = (f32[8,256]{1,0:T(8,128)S(1)}, f32[8,256]{1,0:T(8,128)S(1)}, u32[]{:S(2)}, u32[]{:S(2)}) collective-permute-start(f32[8,256]{1,0:T(8,128)S(1)} %add_add_fusion.2), channel_id=1, source_target_pairs={{0,8},{1,9},{2,10},{3,11},{4,12},{5,13},{6,14},{7,15},{8,0},{9,1},... | collective-permute-start | bytes 24584 | tf_op jit(solution)/shard_map/ppermute | solution.py:372
  108.2 6.0 %collective-permute-start.28 = (f32[8,256]{1,0:T(8,128)S(1)}, f32[8,256]{1,0:T(8,128)S(1)}, u32[]{:S(2)}, u32[]{:S(2)}) collective-permute-start(f32[8,256]{1,0:T(8,128)S(1)} %add_add_fusion.2), channel_id=1, source_target_pairs={{0,16},{1,17},{2,18},{3,19},{4,20},{5,21},{6,22},{7,23},{8,24},{9,... | collective-permute-start | bytes 24584 | tf_op jit(solution)/shard_map/ppermute | solution.py:372
  109.1 8.6 %collective-permute-start.29 = (f32[8,256]{1,0:T(8,128)S(1)}, f32[8,256]{1,0:T(8,128)S(1)}, u32[]{:S(2)}, u32[]{:S(2)}) collective-permute-start(f32[8,256]{1,0:T(8,128)S(1)} %add_add_fusion.2), channel_id=1, source_target_pairs={{0,24},{1,25},{2,26},{3,27},{4,28},{5,29},{6,30},{7,31},{8,16},{9,... | collective-permute-start | bytes 24584 | tf_op jit(solution)/shard_map/ppermute | solution.py:372
  111.0 11.3 %collective-permute-start.32 = (f32[4,64,256]{2,1,0:T(8,128)S(1)}, f32[4,64,256]{2,1,0:T(8,128)S(1)}, u32[]{:S(2)}, u32[]{:S(2)}) collective-permute-start(f32[4,64,256]{2,1,0:T(8,128)S(1)} %get-tuple-element.57), channel_id=1, source_target_pairs={{0,4},{1,5},{2,6},{3,7},{4,0},{5,1},{6,2},{7,3},{8,12},{9,13},{10,... | collective-permute-start | bytes 786440 | tf_op jit(solution)/shard_map/ppermute | solution.py:372
  112.3 16.4 %collective-permute-start.33 = (f32[4,64,256]{2,1,0:T(8,128)S(1)}, f32[4,64,256]{2,1,0:T(8,128)S(1)}, u32[]{:S(2)}, u32[]{:S(2)}) collective-permute-start(f32[4,64,256]{2,1,0:T(8,128)S(1)} %get-tuple-element.56), channel_id=1, source_target_pairs={{0,1},{1,0},{2,3},{3,2},{4,5},{5,4},{6,7},{7,6},{8,9},{9,8},{10,11... | collective-permute-start | bytes 786440 | tf_op jit(solution)/shard_map/ppermute | solution.py:372
  114.2 14.4 %collective-permute-start.34 = (f32[4,64,256]{2,1,0:T(8,128)S(1)}, f32[4,64,256]{2,1,0:T(8,128)S(1)}, u32[]{:S(2)}, u32[]{:S(2)}) collective-permute-start(f32[4,64,256]{2,1,0:T(8,128)S(1)} %get-tuple-element.55), channel_id=1, source_target_pairs={{0,5},{1,4},{2,7},{3,6},{4,1},{5,0},{6,3},{7,2},{8,13},{9,12},{10,... | collective-permute-start | bytes 786440 | tf_op jit(solution)/shard_map/ppermute | solution.py:372
  117.8 14.7 %collective-permute-start.16 = (f32[64,512]{1,0:T(8,128)S(1)}, f32[64,512]{1,0:T(8,128)S(1)}, u32[]{:S(2)}, u32[]{:S(2)}) collective-permute-start(f32[64,512]{1,0:T(8,128)S(1)} %get-tuple-element.39), channel_id=1, source_target_pairs={{0,0},{8,1},{2,2},{10,3},{4,4},{12,5},{6,6},{14,7},{1,8},{9,9},{3,... | collective-permute-start | bytes 393224 | tf_op jit(solution)/shard_map/ppermute | solution.py:372
  118.5 14.0 %collective-permute-start.17 = (f32[64,512]{1,0:T(8,128)S(1)}, f32[64,512]{1,0:T(8,128)S(1)}, u32[]{:S(2)}, u32[]{:S(2)}) collective-permute-start(f32[64,512]{1,0:T(8,128)S(1)} %get-tuple-element.39), channel_id=1, source_target_pairs={{8,0},{0,1},{10,2},{2,3},{12,4},{4,5},{14,6},{6,7},{9,8},{1,9},{11... | collective-permute-start | bytes 393224 | tf_op jit(solution)/shard_map/ppermute | solution.py:372
  129.8 6.1 %collective-permute-start.38 = (f32[8,256]{1,0:T(8,128)S(1)}, f32[8,256]{1,0:T(8,128)S(1)}, u32[]{:S(2)}, u32[]{:S(2)}) collective-permute-start(f32[8,256]{1,0:T(8,128)S(1)} %get-tuple-element.48), channel_id=1, source_target_pairs={{0,1},{1,0},{2,3},{3,2},{4,5},{5,4},{6,7},{7,6},{8,9},{9,8},{10,11... | collective-permute-start | bytes 24584 | tf_op jit(solution)/shard_map/ppermute | solution.py:372
  132.3 3.6 %collective-permute-start.39 = (f32[8,256]{1,0:T(8,128)S(1)}, f32[8,256]{1,0:T(8,128)S(1)}, u32[]{:S(2)}, u32[]{:S(2)}) collective-permute-start(f32[8,256]{1,0:T(8,128)S(1)} %get-tuple-element.48), channel_id=1, source_target_pairs={{0,2},{1,3},{2,0},{3,1},{4,6},{5,7},{6,4},{7,5},{8,10},{9,11},{10,... | collective-permute-start | bytes 24584 | tf_op jit(solution)/shard_map/ppermute | solution.py:372
  132.3 4.8 %collective-permute-start.40 = (f32[8,256]{1,0:T(8,128)S(1)}, f32[8,256]{1,0:T(8,128)S(1)}, u32[]{:S(2)}, u32[]{:S(2)}) collective-permute-start(f32[8,256]{1,0:T(8,128)S(1)} %get-tuple-element.48), channel_id=1, source_target_pairs={{0,3},{1,2},{2,1},{3,0},{4,7},{5,6},{6,5},{7,4},{8,11},{9,10},{10,... | collective-permute-start | bytes 24584 | tf_op jit(solution)/shard_map/ppermute | solution.py:372
  132.4 4.7 %collective-permute-start.41 = (f32[8,256]{1,0:T(8,128)S(1)}, f32[8,256]{1,0:T(8,128)S(1)}, u32[]{:S(2)}, u32[]{:S(2)}) collective-permute-start(f32[8,256]{1,0:T(8,128)S(1)} %get-tuple-element.48), channel_id=1, source_target_pairs={{0,4},{1,5},{2,6},{3,7},{4,0},{5,1},{6,2},{7,3},{8,12},{9,13},{10,... | collective-permute-start | bytes 24584 | tf_op jit(solution)/shard_map/ppermute | solution.py:372
  132.4 8.2 %collective-permute-start.42 = (f32[8,256]{1,0:T(8,128)S(1)}, f32[8,256]{1,0:T(8,128)S(1)}, u32[]{:S(2)}, u32[]{:S(2)}) collective-permute-start(f32[8,256]{1,0:T(8,128)S(1)} %get-tuple-element.48), channel_id=1, source_target_pairs={{0,5},{1,4},{2,7},{3,6},{4,1},{5,0},{6,3},{7,2},{8,13},{9,12},{10,... | collective-permute-start | bytes 24584 | tf_op jit(solution)/shard_map/ppermute | solution.py:372
  135.9 4.7 %collective-permute-start.43 = (f32[8,256]{1,0:T(8,128)S(1)}, f32[8,256]{1,0:T(8,128)S(1)}, u32[]{:S(2)}, u32[]{:S(2)}) collective-permute-start(f32[8,256]{1,0:T(8,128)S(1)} %get-tuple-element.48), channel_id=1, source_target_pairs={{0,6},{1,7},{2,4},{3,5},{4,2},{5,3},{6,0},{7,1},{8,14},{9,15},{10,... | collective-permute-start | bytes 24584 | tf_op jit(solution)/shard_map/ppermute | solution.py:372
  135.9 7.6 %collective-permute-start.44 = (f32[8,256]{1,0:T(8,128)S(1)}, f32[8,256]{1,0:T(8,128)S(1)}, u32[]{:S(2)}, u32[]{:S(2)}) collective-permute-start(f32[8,256]{1,0:T(8,128)S(1)} %get-tuple-element.48), channel_id=1, source_target_pairs={{0,7},{1,6},{2,5},{3,4},{4,3},{5,2},{6,1},{7,0},{8,15},{9,14},{10,... | collective-permute-start | bytes 24584 | tf_op jit(solution)/shard_map/ppermute | solution.py:372
  137.1 13.9 %collective-permute-start.18 = (f32[64,512]{1,0:T(8,128)S(1)}, f32[64,512]{1,0:T(8,128)S(1)}, u32[]{:S(2)}, u32[]{:S(2)}) collective-permute-start(f32[64,512]{1,0:T(8,128)S(1)} %get-tuple-element.40), channel_id=1, source_target_pairs={{16,0},{24,1},{18,2},{26,3},{20,4},{28,5},{22,6},{30,7},{17,8},{25... | collective-permute-start | bytes 393224 | tf_op jit(solution)/shard_map/ppermute | solution.py:372
  137.1 15.2 %collective-permute-start.19 = (f32[64,512]{1,0:T(8,128)S(1)}, f32[64,512]{1,0:T(8,128)S(1)}, u32[]{:S(2)}, u32[]{:S(2)}) collective-permute-start(f32[64,512]{1,0:T(8,128)S(1)} %get-tuple-element.40), channel_id=1, source_target_pairs={{24,0},{16,1},{26,2},{18,3},{28,4},{20,5},{30,6},{22,7},{25,8},{17... | collective-permute-start | bytes 393224 | tf_op jit(solution)/shard_map/ppermute | solution.py:372
  140.6 20.4 %collective-permute-start.35 = (f32[64,256]{1,0:T(8,128)S(1)}, f32[64,256]{1,0:T(8,128)S(1)}, u32[]{:S(2)}, u32[]{:S(2)}) collective-permute-start(f32[64,256]{1,0:T(8,128)S(1)} %get-tuple-element.45), channel_id=1, source_target_pairs={{0,8},{1,9},{2,10},{3,11},{4,12},{5,13},{6,14},{7,15},{8,0},{9,1},... | collective-permute-start | bytes 196616 | tf_op jit(solution)/shard_map/ppermute | solution.py:372
  140.6 20.4 %collective-permute-start.36 = (f32[64,256]{1,0:T(8,128)S(1)}, f32[64,256]{1,0:T(8,128)S(1)}, u32[]{:S(2)}, u32[]{:S(2)}) collective-permute-start(f32[64,256]{1,0:T(8,128)S(1)} %get-tuple-element.46), channel_id=1, source_target_pairs={{0,16},{1,17},{2,18},{3,19},{4,20},{5,21},{6,22},{7,23},{8,24},{9,... | collective-permute-start | bytes 196616 | tf_op jit(solution)/shard_map/ppermute | solution.py:372
  143.5 17.5 %collective-permute-start.37 = (f32[64,256]{1,0:T(8,128)S(1)}, f32[64,256]{1,0:T(8,128)S(1)}, u32[]{:S(2)}, u32[]{:S(2)}) collective-permute-start(f32[64,256]{1,0:T(8,128)S(1)} %get-tuple-element.47), channel_id=1, source_target_pairs={{0,24},{1,25},{2,26},{3,27},{4,28},{5,29},{6,30},{7,31},{8,16},{9,... | collective-permute-start | bytes 196616 | tf_op jit(solution)/shard_map/ppermute | solution.py:372
  151.0 4.5 %collective-permute-start.45 = (f32[8,256]{1,0:T(8,128)S(1)}, f32[8,256]{1,0:T(8,128)S(1)}, u32[]{:S(2)}, u32[]{:S(2)}) collective-permute-start(f32[8,256]{1,0:T(8,128)S(1)} %add_add_fusion.a0), channel_id=1, source_target_pairs={{0,8},{1,9},{2,10},{3,11},{4,12},{5,13},{6,14},{7,15},{8,0},{9,1},... | collective-permute-start | bytes 24584 | tf_op jit(solution)/shard_map/ppermute | solution.py:372
  152.4 6.0 %collective-permute-start.46 = (f32[8,256]{1,0:T(8,128)S(1)}, f32[8,256]{1,0:T(8,128)S(1)}, u32[]{:S(2)}, u32[]{:S(2)}) collective-permute-start(f32[8,256]{1,0:T(8,128)S(1)} %add_add_fusion.a0), channel_id=1, source_target_pairs={{0,16},{1,17},{2,18},{3,19},{4,20},{5,21},{6,22},{7,23},{8,24},{9,... | collective-permute-start | bytes 24584 | tf_op jit(solution)/shard_map/ppermute | solution.py:372
  155.5 5.4 %collective-permute-start.47 = (f32[8,256]{1,0:T(8,128)S(1)}, f32[8,256]{1,0:T(8,128)S(1)}, u32[]{:S(2)}, u32[]{:S(2)}) collective-permute-start(f32[8,256]{1,0:T(8,128)S(1)} %add_add_fusion.a0), channel_id=1, source_target_pairs={{0,24},{1,25},{2,26},{3,27},{4,28},{5,29},{6,30},{7,31},{8,16},{9,... | collective-permute-start | bytes 24584 | tf_op jit(solution)/shard_map/ppermute | solution.py:372
  (10 other events, 242.2 us)

commit v2 on v0

v2 whole, which is shorter than its diff:
```python
import functools

import jax
import jax.numpy as jnp
from jax import lax
from jax.experimental import pallas as pl
from jax.experimental.pallas import tpu as pltpu
from jax.sharding import PartitionSpec as P

epsilon = 1e-06
AXES = ("doc", "feat")
MIB = 1024 * 1024


Y_BIT, CORE_BIT, X_BIT, Z_SHIFT = 1, 2, 4, 3
NT = (((1,), (1,)), ((), ()))


def coords():
    d = lax.axis_index("doc")
    y = lax.axis_index("feat")
    return d, d >> 2, y


def full(shape):
    return pl.BlockSpec(shape, lambda *_: (0,) * len(shape))


def params(mib):
    return pltpu.CompilerParams(vmem_limit_bytes=mib * MIB)


def cost(flops, nbytes):
    return pl.CostEstimate(flops=int(flops), bytes_accessed=int(nbytes), transcendentals=0)


def f32(*shape):
    return jax.ShapeDtypeStruct(shape, jnp.float32)


def bf16(*shape):
    return jax.ShapeDtypeStruct(shape, jnp.bfloat16)


def quarters_kernel(right_ref, left_ref, m0, m1, m2, m3, u0, u1, u2, u3, turned):
    _, z, y = coords()
    rows = right_ref.shape[0]
    half = left_ref.shape[0] // 2
    turned[...] = right_ref[...].T.reshape(turned.shape)
    for k, out in enumerate((m0, m1, m2, m3)):
        out[...] = turned[z ^ k]
    turned[...] = left_ref[pl.ds(pl.multiple_of(y * half, half), half), :].T.reshape(turned.shape)
    for k, out in enumerate((u0, u1, u2, u3)):
        out[...] = turned[z ^ k]


def quarters_of(right, left):
    rows, cols = right.shape
    q = cols // 4
    got = pl.pallas_call(
        quarters_kernel,
        out_shape=[f32(q, rows)] * 4 + [f32(q, left.shape[0] // 2)] * 4,
        scratch_shapes=[pltpu.VMEM((4, q, rows), jnp.float32)],
        compiler_params=params(8),
        cost_estimate=cost(0, rows * cols * 16),
        name="quarters",
    )(right, left)
    return got[:4], got[4:]


def halves_kernel(ids_ref, vals_ref, keep, send):
    _, _, y = coords()
    n = keep.shape[0] // 2
    for out, part in ((keep, y), (send, 1 - y)):
        at = pl.multiple_of(part * n, n)
        out[0:n, :] = ids_ref[pl.ds(at, n), :]
        out[n:, :] = vals_ref[pl.ds(at, n), :]


def halves_of(ids, vals):
    shape = f32(*ids.shape)
    return pl.pallas_call(
        halves_kernel,
        out_shape=[shape, shape],
        compiler_params=params(8),
        cost_estimate=cost(0, ids.size * 16),
        name="entry_halves",
    )(ids, vals)


def build_kernel(e0, e1, e2, e3, hi_ref, lo_ref):
    d, _, _ = coords()
    n = e0.shape[0] // 4
    steps = n // 8
    iota = lax.broadcasted_iota(jnp.int32, (256, 256), 0).astype(jnp.float32).astype(jnp.bfloat16)
    lane_doc = lax.broadcasted_iota(jnp.int32, (8, 256), 1) >> 4
    one = jnp.ones((256, 256), jnp.bfloat16)
    zero = jnp.zeros((256, 256), jnp.bfloat16)

    def spread(row):
        wide = jnp.broadcast_to(row, (16, 256)).astype(jnp.bfloat16)
        return jnp.broadcast_to(wide[None], (16, 16, 256)).reshape(256, 256)

    for k, entries in enumerate((e0, e1, e2, e3)):

        @pl.loop(0, steps)
        def _(step, k=k, entries=entries):
            for yy in range(2):
                at = pl.multiple_of(step * 8, 8)
                ids = entries[pl.ds(2 * n * yy + at, 8), :].astype(jnp.int32)
                vals = entries[pl.ds(2 * n * yy + n + at, 8), :]
                rel = (ids >> 8) ^ d
                block = ((rel & 1) << 3) | ((rel & 2) << 1) | (rel >> 2)
                code = (block * 16 + lane_doc).astype(jnp.float32)
                inner = (ids & 255).astype(jnp.float32)
                for t in range(8):
                    pick = jnp.where(iota == spread(code[t : t + 1]), one, zero)
                    weigh = jnp.where(iota == spread(inner[t : t + 1]), spread(vals[t : t + 1]), zero)
                    dense = lax.dot_general(pick, weigh, NT, preferred_element_type=jnp.float32)
                    high = dense.astype(jnp.bfloat16)
                    low = (dense - high.astype(jnp.float32)).astype(jnp.bfloat16)
                    high = high.reshape(16, 16, 256)
                    low = low.reshape(16, 16, 256)
                    docs = pl.ds(pl.multiple_of(k * 16 * n + step * 128 + 16 * t, 16), 16)
                    for cc in range(2):
                        to = slice(cc * 16 + yy * 8, cc * 16 + yy * 8 + 8)
                        hi_ref[to, docs, :] = high[8 * cc : 8 * cc + 8]
                        lo_ref[to, docs, :] = low[8 * cc : 8 * cc + 8]


def whole():
    return pl.BlockSpec(memory_space=pltpu.VMEM)


def build(entries):
    docs = 4 * (entries[0].shape[0] // 4 * 16)
    return pl.pallas_call(
        build_kernel,
        in_specs=[whole()] * 4,
        out_specs=[whole()] * 2,
        out_shape=[pltpu.VMEM((32, docs, 256), jnp.bfloat16)] * 2,
        compiler_params=params(12),
        cost_estimate=cost(2 * docs * 2 * 16 * 256 * 256, docs * 8192 * 4),
        name="dense_rows",
    )(*entries)


def split_rows(value):
    high = value.astype(jnp.bfloat16)
    low = (value - high.astype(jnp.float32)).astype(jnp.bfloat16)
    return jnp.concatenate([high, low], axis=0)


def add_products(hi_ref, lo_ref, first, vecs, total):
    for pair in range(0, 4, 2):
        lhs, rhs = [], []
        for k in (pair, pair + 1):
            both = split_rows(vecs[k])
            lhs += [hi_ref[first + k], lo_ref[first + k]]
            rhs += [both, both]
        total[...] += lax.dot_general(
            jnp.concatenate(lhs, axis=1), jnp.concatenate(rhs, axis=1), NT, preferred_element_type=jnp.float32
        )


def forward_kernel(blocks, has_before, hi_ref, lo_ref, *refs):
    count = len(blocks)
    vecs, total = refs[:count], refs[-1]
    total[...] = refs[count][...] if has_before else jnp.zeros_like(total)
    for n in range(count):
        add_products(hi_ref, lo_ref, blocks[n], vecs[n], total)


def forward_part(hi, lo, vecs, before, blocks):
    docs = hi.shape[1]
    q = vecs[0].shape[1]
    extra = [] if before is None else [before]
    n = 4 * len(blocks)
    return pl.pallas_call(
        functools.partial(forward_kernel, blocks, before is not None),
        in_specs=[whole()] * (2 + len(vecs) + len(extra)),
        out_specs=whole(),
        out_shape=f32(docs, 2 * q),
        compiler_params=params(12),
        cost_estimate=cost(8 * docs * 256 * 256 * n, 4 * docs * 256 * n),
        name="forward_part",
    )(hi, lo, *vecs, *extra)


def square_row(value, z, cols):
    squares = value * value
    ones = jnp.ones((8, value.shape[1]), jnp.float32)
    sums = lax.dot_general(
        ones,
        jnp.concatenate([squares] * 4, axis=0),
        NT,
        preferred_element_type=jnp.float32,
        precision=lax.Precision.HIGHEST,
    )
    lane = lax.broadcasted_iota(jnp.int32, (8, cols), 1)
    return jnp.where(lane // (cols // 4) == z, sums, 0.0)


def row_to_column(row):
    return jnp.broadcast_to(row, (128, row.shape[1])).T


def last_forward_kernel(blocks, hi_ref, lo_ref, *refs):
    count = len(blocks)
    vecs = refs[:count]
    before, u0, u1, u2, u3, alpha, l0, l1, l2, l3, both, sums, total, columns = refs[count:]
    _, z, _ = coords()
    q, docs = u0.shape
    total[...] = before[...]
    columns[...] = row_to_column(alpha[...])
    for n in range(count):
        add_products(hi_ref, lo_ref, blocks[n], vecs[n], total)
    turned = total[...].T
    product = turned[:q] + turned[q:]
    scale = columns[pl.ds(pl.multiple_of(z * q, q), q), :][:, 0:1]
    for k, (u, out) in enumerate(((u0, l0), (u1, l1), (u2, l2), (u3, l3))):
        out[...] = product[:, k * docs : (k + 1) * docs] - scale * u[...]
    left = jnp.concatenate([l0[...], l1[...], l2[...], l3[...]], axis=1)
    both[...] = split_rows(left)
    sums[...] = square_row(left, z, sums.shape[1])


def last_forward(hi, lo, vecs, before, lefts, alpha, blocks):
    docs = hi.shape[1]
    q = vecs[0].shape[1]
    n = 4 * len(blocks)
    got = pl.pallas_call(
        functools.partial(last_forward_kernel, blocks),
        in_specs=[whole()] * (2 + len(vecs) + 6),
        out_specs=[whole()] * 6,
        out_shape=[f32(*u.shape) for u in lefts] + [bf16(2 * q, docs), f32(8, 4 * q)],
        scratch_shapes=[pltpu.VMEM((docs, 2 * q), jnp.float32), pltpu.VMEM((4 * q, 128), jnp.float32)],
        compiler_params=params(12),
        cost_estimate=cost(8 * docs * 256 * 256 * n, 4 * docs * 256 * n),
        name="last_forward",
    )(hi, lo, *vecs, before, *lefts, alpha)
    return got[:4], got[4], got[5]


def backward_kernel(first, blocks, has_tail, hi_ref, lo_ref, both_ref, *refs):
    out_ref = refs[-1]
    both = both_ref[...]
    q = both.shape[0] // 2
    twice = jnp.concatenate([both, both], axis=1)
    for b in range(blocks):
        got = jnp.dot(
            twice,
            jnp.concatenate([hi_ref[first + b], lo_ref[first + b]], axis=0),
            preferred_element_type=jnp.float32,
        )
        out_ref[b * q : (b + 1) * q, :] = got[:q] + got[q:]
    if has_tail:
        out_ref[blocks * q :, :] = refs[0][...]


def backward_part(hi, lo, both, first, blocks, tail=None):
    docs = hi.shape[1]
    q = both.shape[0] // 2
    extra = [] if tail is None else [tail]
    rows = blocks * q + (0 if tail is None else tail.shape[0])
    return pl.pallas_call(
        functools.partial(backward_kernel, first, blocks, tail is not None),
        in_specs=[whole()] * (3 + len(extra)),
        out_specs=whole(),
        out_shape=f32(rows, 256),
        compiler_params=params(12),
        cost_estimate=cost(8 * docs * 256 * 256 * blocks, 4 * docs * 256 * blocks),
        name="backward_part",
    )(hi, lo, both, *extra)


def plane_kernel(near, far, beta, s1, s2, s3, beta_core):
    n = near.shape[0] // 3
    beta_core[...] = beta[...] + far[3 * n :, :]
    for g, out in enumerate((s1, s2, s3)):
        rows = slice(g * n, (g + 1) * n)
        out[0:n, :] = near[rows, :] + far[rows, :]
        out[n:, :] = beta_core[...]


def plane_sums(near, far, beta):
    rows = near.shape[0] // 3
    return pl.pallas_call(
        plane_kernel,
        out_shape=[f32(rows + 8, 256)] * 3 + [f32(8, 256)],
        compiler_params=params(8),
        cost_estimate=cost(near.size, near.size * 12),
        name="plane_sums",
    )(near, far, beta)


def right_norm_kernel(docs_total, own, peer, r1, r2, r3, beta_core, v0, v1, v2, v3, g0, g1, g2, g3, sums, columns):
    _, z, _ = coords()
    q = v0.shape[0]
    tail = slice(4 * q, 4 * q + 8)
    beta_sums = (beta_core[...] + r1[tail, :]) + (r2[tail, :] + r3[tail, :])
    columns[...] = row_to_column(jnp.sqrt(beta_sums[0:1, :] / docs_total + epsilon))
    beta = columns[pl.ds(pl.multiple_of(z * q, q), q), :][:, 0:1]
    raws = []
    for k, (v, g) in enumerate(zip((v0, v1, v2, v3), (g0, g1, g2, g3))):
        rows = slice(k * q, (k + 1) * q)
        total = ((own[rows, :] + peer[rows, :]) + r1[rows, :]) + (r2[rows, :] + r3[rows, :])
        g[0:q, :] = total
        g[q:, :] = beta_sums
        raws.append(total / beta - beta * v[...])
    sums[...] = square_row(jnp.concatenate(raws, axis=1), z, sums.shape[1])


def right_norm(docs_total, own, peer, received, beta_core, quarters):
    q, rows = quarters[0].shape
    got = pl.pallas_call(
        functools.partial(right_norm_kernel, docs_total),
        out_shape=[f32(q + 8, rows)] * 4 + [f32(8, 4 * q)],
        scratch_shapes=[pltpu.VMEM((4 * q, 128), jnp.float32)],
        compiler_params=params(12),
        cost_estimate=cost(rows * q * 64, rows * q * 100),
        name="right_norm",
    )(own, peer, *received, beta_core, *quarters)
    return got[:4], got[4]


def beta_of(pieces, q, docs_total):
    squares = [g[q : q + 1, :] for g in pieces]
    return jnp.sqrt(((squares[0] + squares[1]) + (squares[2] + squares[3])) / docs_total + epsilon)


def finish_kernel(docs_total, feat_total, g0, g1, g2, g3, a0, a1, a2, a3, right, search, phibar, rhobar,
                  right_out, search_out, alpha_out, phibar_out, rhobar_out, turned):
    _, z, _ = coords()
    q = turned.shape[1]
    for k, g in enumerate((g0, g1, g2, g3)):
        turned[z ^ k] = g[0:q, :]
    got = turned[...].reshape(-1, turned.shape[2]).T
    squares = (a0[0:1, :] + a1[0:1, :]) + (a2[0:1, :] + a3[0:1, :])
    alpha = jnp.sqrt(squares / feat_total + epsilon)
    beta = beta_of((g0, g1, g2, g3), q, docs_total)
    rho = jnp.sqrt(rhobar[...] * rhobar[...] + beta * beta)
    cosine = rhobar[...] / rho
    sine = beta / rho
    theta = sine * alpha
    rhobar_out[...] = -cosine * alpha
    phibar_out[...] = sine * phibar[...]
    alpha_out[...] = alpha
    following = (got / beta - beta * right[...]) / alpha
    right_out[...] = following
    search_out[...] = following - (theta / rho) * search[...]


def finish(docs_total, feat_total, pieces, alphas, right, search, phibar, rhobar):
    rows, cols = right.shape
    return pl.pallas_call(
        functools.partial(finish_kernel, docs_total, feat_total),
        out_shape=[f32(rows, cols)] * 2 + [f32(1, cols)] * 3,
        scratch_shapes=[pltpu.VMEM((4, cols // 4, rows), jnp.float32)],
        compiler_params=params(12),
        cost_estimate=cost(rows * cols * 16, rows * cols * 20),
        name="finish",
    )(*pieces, *alphas, right, search, phibar, rhobar)


def left_out_kernel(docs_total, own, other, g0, g1, g2, g3, search, solution, phibar, rhobar, left_out, solution_out, turned):
    _, z, y = coords()
    q, half = turned.shape[1:]
    beta = beta_of((g0, g1, g2, g3), q, docs_total)
    for part, ref in ((y, own), (1 - y, other)):
        for k in range(4):
            turned[z ^ k] = ref[k]
        left_out[pl.ds(pl.multiple_of(part * half, half), half), :] = turned[...].reshape(-1, half).T / beta
    rho = jnp.sqrt(rhobar[...] * rhobar[...] + beta * beta)
    phi = rhobar[...] / rho * phibar[...]
    solution_out[...] = solution[...] + (phi / rho) * search[...]


def left_out(docs_total, own, other, pieces, search, solution, phibar, rhobar):
    _, q, half = own.shape
    return pl.pallas_call(
        functools.partial(left_out_kernel, docs_total),
        out_shape=[f32(2 * half, 4 * q), f32(*solution.shape)],
        scratch_shapes=[pltpu.VMEM((4, q, half), jnp.float32)],
        compiler_params=params(12),
        cost_estimate=cost(half * q * 32, half * q * 120),
        name="left_out",
    )(own, other, *pieces, search, solution, phibar, rhobar)


def swap(value, mask):
    return lax.ppermute(value, AXES, [(i, i ^ mask) for i in range(32)])


def along_z(values):
    return [values[0]] + [swap(values[k], k << Z_SHIFT) for k in (1, 2, 3)]


def plane_mask(g):
    return Y_BIT * (g >> 1) | X_BIT * (g & 1)


def by_columns(
    col_ids, col_vals, left_vec, right_vec, search_dir, solution_vec, alpha_prev, phibar, rhobar
):
    docs_total = left_vec.shape[0] * 16
    feat_total = right_vec.shape[0] * 32
    alpha_row, phibar_row, rhobar_row = (v.reshape(1, -1) for v in (alpha_prev, phibar, rhobar))

    mine, lefts = quarters_of(right_vec, left_vec)
    quarters = along_z(mine)
    keep, send = halves_of(
        col_ids.astype(jnp.float32).reshape(-1, 256), col_vals.astype(jnp.float32).reshape(-1, 256)
    )
    entries = along_z([jnp.concatenate([keep, swap(send, Y_BIT)], axis=0)] * 4)
    own = jnp.stack(quarters)
    plane = [swap(own, plane_mask(g)) for g in (1, 2, 3)]
    own_peer = swap(own, CORE_BIT)
    lefts = along_z(lefts)

    hi, lo = build(entries)
    total = forward_part(hi, lo, [own, own_peer], None, (0, 16))
    plane_peer = [swap(p, CORE_BIT) for p in plane]
    total = forward_part(hi, lo, plane, total, (4, 8, 12))
    raws, both, beta_part = last_forward(hi, lo, plane_peer, total, lefts, alpha_row, (20, 24, 28))

    far_peer = swap(backward_part(hi, lo, both, 20, 12, beta_part), CORE_BIT)
    near = backward_part(hi, lo, both, 4, 12)
    *sent, beta_core = plane_sums(near, far_peer, beta_part)
    received = [swap(s, plane_mask(g)) for g, s in zip((1, 2, 3), sent)]
    near_peer = swap(backward_part(hi, lo, both, 16, 4), CORE_BIT)
    near_own = backward_part(hi, lo, both, 0, 4)

    near_own, *raws = lax.optimization_barrier((near_own, *raws))
    left_own = jnp.stack(along_z(raws))
    left_other = swap(left_own, Y_BIT)

    sent, alpha_part = right_norm(docs_total, near_own, near_peer, received, beta_core, quarters)
    got = along_z(sent)
    for mask in (CORE_BIT, X_BIT, Y_BIT):
        alpha_part = alpha_part + swap(alpha_part, mask)
    alphas = along_z([alpha_part] * 4)
    left_next, solution_next = left_out(
        docs_total, left_own, left_other, got, search_dir, solution_vec, phibar_row, rhobar_row
    )
    right_next, search_next, alpha_next, phibar_next, rhobar_next = finish(
        docs_total, feat_total, got, alphas, right_vec, search_dir, phibar_row, rhobar_row
    )
    return (
        left_next,
        right_next,
        search_next,
        solution_next,
        alpha_next.reshape(-1),
        phibar_next.reshape(-1),
        rhobar_next.reshape(-1),
    )


def forward(col_ids, col_vals, table):
    picked = table[col_ids]
    return jnp.sum(col_vals.astype(jnp.float32)[:, :, None] * picked, axis=1)


def backward(col_ids, col_vals, rows_in, width):
    terms = col_vals.astype(jnp.float32)[:, :, None] * rows_in[:, None, :]
    return jax.ops.segment_sum(
        terms.reshape(-1, rows_in.shape[1]), col_ids.reshape(-1), num_segments=width
    )


def by_blocks(
    col_ids, col_vals, left_vec, right_vec, search_dir, solution_vec, alpha_prev, phibar, rhobar
):
    n_feat = lax.axis_size("feat")
    n_doc = lax.axis_size("doc")
    docs_total = left_vec.shape[0] * n_doc
    feat_total = right_vec.shape[0] * n_doc * n_feat
    table = lax.all_gather(right_vec, "doc", axis=0, tiled=True)
    total = lax.psum(forward(col_ids, col_vals, table), "feat")
    left_raw = total - alpha_prev[None, :] * left_vec
    row_part = jnp.sum(left_raw * left_raw, axis=0)
    beta_norm = jnp.sqrt(lax.psum(row_part, "doc") / docs_total + epsilon)
    left_next = left_raw / beta_norm[None, :]
    feature_part = lax.psum_scatter(
        backward(col_ids, col_vals, left_next, table.shape[0]), "doc", scatter_dimension=0, tiled=True
    )
    right_raw = feature_part - beta_norm[None, :] * right_vec
    squares = lax.psum(jnp.sum(right_raw * right_raw, axis=0), AXES)
    alpha_next = jnp.sqrt(squares / feat_total + epsilon)
    right_next = right_raw / alpha_next[None, :]
    rho_val = jnp.sqrt(rhobar * rhobar + beta_norm * beta_norm)
    cosine = rhobar / rho_val
    sine_val = beta_norm / rho_val
    theta_val = sine_val * alpha_next
    phi_val = cosine * phibar
    solution_next = solution_vec + (phi_val / rho_val)[None, :] * search_dir
    search_next = right_next - (theta_val / rho_val)[None, :] * search_dir
    return (
        left_next,
        right_next,
        search_next,
        solution_next,
        alpha_next,
        sine_val * phibar,
        -cosine * alpha_next,
    )


def solution(mesh):
    small = mesh.shape["doc"] == 16 and mesh.shape["feat"] == 2
    rows = P(("feat", "doc"), None)
    return jax.shard_map(
        by_columns if small else by_blocks,
        mesh=mesh,
        in_specs=(P("doc", "feat"), P("doc", "feat"), P("doc", None), rows, rows, rows, P(), P(), P()),
        out_specs=(P("doc", None), rows, rows, rows, P(), P(), P()),
        check_vma=False,
    )
```

time: 347 us -> 103 us (0.30)
  waiting for transfers between devices: 155 us -> 23.9 us
  blocking collectives: 79 us -> 0 us
  other arithmetic: 63.2 us -> 0.81 us
  starting transfers between devices: 0.12 us -> 44.5 us
  local copies, waits for them, and re-layouts: 35.1 us -> 3.28 us
  Pallas kernels: 0 us -> 29.2 us
  between operations: 13.9 us -> 0.93 us
    psum x2 -> x0, blocking collectives: 79 us -> none  [the longest x1 39.6 us: on_device(): squares = lax.psum(jnp.sum(right_raw * right_raw, axis=0), ('doc', 'feat'))]
    reduce_scatter x1 -> x0, waiting for transfers between devices: 73.6 us -> none  [on_device(): lax.psum_scatter(backward(col_ids, col_vals, sent_rows, table.shape[0]),...]
    all_gather x1 -> x0, waiting for transfers between devices: 53.6 us -> none  [on_device(): table = lax.all_gather(right_vec, 'doc', axis=0, tiled=True)]
    scatter-add x1 -> x0, other arithmetic: 46.8 us -> none  [backward_one_block(): jax.ops.segment_sum(terms, index_rows.reshape(-1), num_segments=width)]
    ppermute x0 -> x35, starting transfers between devices: none -> 44.5 us  [swap(): return lax.ppermute(value, AXES, [(i, i ^ mask) for i in range(32)])]
    gather x1 -> x0, local copies, waits for them, and re-layouts: 33.6 us -> none  [forward_one_block(): picked = table[index_rows]]
    pallas_call x0 -> x14, Pallas kernels: none -> 29.2 us  [the longest x1 9.17 us: build(): pl.pallas_call(build_kernel, in_specs=[whole()] * 4, out_specs=[whole()]...]
    psum x1 -> x0, waiting for transfers between devices: 26.8 us -> none  [on_device(): total = lax.psum(partial_value, 'feat')]
  transfers between devices with their start and end apart: 3 -> 35, of which waited for: 3 -> 9; matrix products, arithmetic and copies ran while one was open for 1% -> 0% of each run, Pallas kernels for 0% -> 21%
where the time goes in v2:
time: 103 us
  starting transfers between devices  44.5 us (43%)
  Pallas kernels  29.2 us (28%)
  waiting for transfers between devices  23.9 us (23%)
  local copies, waits for them, and re-layouts  3.28 us (3%)
    ppermute x35, starting transfers between devices, swap(): return lax.ppermute(value, AXES, [(i, i ^ mask) for i in range(32)])  44.5 us
    ppermute x35, waiting for transfers between devices, swap(): return lax.ppermute(value, AXES, [(i, i ^ mask) for i in range(32)])  23.9 us
    pallas_call x1, Pallas kernels, build(): pl.pallas_call(build_kernel, in_specs=[whole()] * 4, out_specs=[whole()]...  9.17 us
    pallas_call x1, Pallas kernels, last_forward(): pl.pallas_call(functools.partial(last_forward_kernel, blocks), in_specs=[...  5.81 us
    pallas_call x2, Pallas kernels, forward_part(): pl.pallas_call(functools.partial(forward_kernel, blocks, before is not No...  5.72 us
    pallas_call x4, Pallas kernels, backward_part(): pl.pallas_call(functools.partial(backward_kernel, first, blocks, tail is...  5.03 us
  transfers between devices with their start and end apart: 35, of which 9 were waited for; matrix products, arithmetic and copies ran while one was open for 0% of the time, Pallas kernels for 21%

profile of v2, /device:TPU:0, one launch (start us, length us, event | category | flops | bytes accessed | tf_op | source)
XLA Modules:
  0.0 102.6 jit_solution(12886147874430432319)
XLA Ops:
  0.6 0.8 convert_element_type.4
  1.7 0.8 copy.19
  2.7 3.0 %collective-permute-start = (f32[32,256]{1,0:T(8,128)S(1)}, f32[32,256]{1,0:T(8,128)S(1)}, u32[]{:S(2)}, u32[]{:S(2)}) collective-permute-start(f32[32,256]{1,0:T(8,128)S(1)} %get-tuple-element.47), channel_id=1, source_target_pairs={{0,1},{1,0},{2,3},{3,2},{4,5},{5,4},{6,7},{7,6},{8,9},{9,8},{10,11... | collective-permute-start | bytes 98312 | tf_op jit(solution)/shard_map/ppermute | solution.py:392
  5.7 0.9 copy-done
  6.7 1.0 %copy-done.3 = f32[512,256]{1,0:T(8,128)S(1)} copy-done((f32[512,256]{1,0:T(8,128)S(1)}, f32[512,256]{1,0:T(8,128)}, u32[]{:S(2)}) %copy-start.3) | copy-done | bytes 524312
  7.9 1.7 %collective-permute-start.4 = (f32[64,256]{1,0:T(8,128)S(1)}, f32[64,256]{1,0:T(8,128)S(1)}, u32[]{:S(2)}, u32[]{:S(2)}) collective-permute-start(f32[64,256]{1,0:T(8,128)S(1)} %get-tuple-element.51), channel_id=1, source_target_pairs={{0,8},{1,9},{2,10},{3,11},{4,12},{5,13},{6,14},{7,15},{8,0},{9,1},... | collective-permute-start | bytes 196616 | tf_op jit(solution)/shard_map/ppermute | solution.py:392
  9.6 2.6 %collective-permute-start.5 = (f32[64,256]{1,0:T(8,128)S(1)}, f32[64,256]{1,0:T(8,128)S(1)}, u32[]{:S(2)}, u32[]{:S(2)}) collective-permute-start(f32[64,256]{1,0:T(8,128)S(1)} %get-tuple-element.52), channel_id=1, source_target_pairs={{0,16},{1,17},{2,18},{3,19},{4,20},{5,21},{6,22},{7,23},{8,24},{9,... | collective-permute-start | bytes 196616 | tf_op jit(solution)/shard_map/ppermute | solution.py:392
  12.4 0.7 collective-permute-start.14
  13.1 3.5 %collective-permute-start.15 = (f32[64,256]{1,0:T(8,128)S(1)}, f32[64,256]{1,0:T(8,128)S(1)}, u32[]{:S(2)}, u32[]{:S(2)}) collective-permute-start(f32[64,256]{1,0:T(8,128)S(1)} %get-tuple-element.56), channel_id=1, source_target_pairs={{0,16},{1,17},{2,18},{3,19},{4,20},{5,21},{6,22},{7,23},{8,24},{9,... | collective-permute-start | bytes 196616 | tf_op jit(solution)/shard_map/ppermute | solution.py:392
  16.8 1.3 %collective-permute-start.2 = (f32[64,256]{1,0:T(8,128)S(1)}, f32[64,256]{1,0:T(8,128)S(1)}, u32[]{:S(2)}, u32[]{:S(2)}) collective-permute-start(f32[64,256]{1,0:T(8,128)S(1)} %constant_dynamic-update-slice_fusion.e0), channel_id=1, source_target_pairs={{0,16},{1,17},{2,18},{3,19},{4,20},{5,21},{6,22},{7,23},{8,24},{9,... | collective-permute-start | bytes 196616 | tf_op jit(solution)/shard_map/ppermute | solution.py:392
  18.5 5.1 %collective-permute-start.1 = (f32[64,256]{1,0:T(8,128)S(1)}, f32[64,256]{1,0:T(8,128)S(1)}, u32[]{:S(2)}, u32[]{:S(2)}) collective-permute-start(f32[64,256]{1,0:T(8,128)S(1)} %constant_dynamic-update-slice_fusion.e0), channel_id=1, source_target_pairs={{0,8},{1,9},{2,10},{3,11},{4,12},{5,13},{6,14},{7,15},{8,0},{9,1},... | collective-permute-start | bytes 196616 | tf_op jit(solution)/shard_map/ppermute | solution.py:392
  23.7 2.9 %collective-permute-done.2.e2 = f32[64,256]{1,0:T(8,128)S(1)} collective-permute-done((f32[64,256]{1,0:T(8,128)S(1)}, f32[64,256]{1,0:T(8,128)S(1)}, u32[]{:S(2)}, u32[]{:S(2)}) %collective-permute-start.2) | collective-permute-done | bytes 65568 | tf_op jit(solution)/shard_map/ppermute | solution.py:392
  26.5 1.4 %collective-permute-start.11 = (f32[4,64,256]{2,1,0:T(8,128)S(1)}, f32[4,64,256]{2,1,0:T(8,128)S(1)}, u32[]{:S(2)}, u32[]{:S(2)}) collective-permute-start(f32[4,64,256]{2,1,0:T(8,128)S(1)} %pad_maximum_fusion.refs_0_), channel_id=1, source_target_pairs={{0,5},{1,4},{2,7},{3,6},{4,1},{5,0},{6,3},{7,2},{8,13},{9,12},{10,... | collective-permute-start | bytes 786440 | tf_op jit(solution)/shard_map/ppermute | solution.py:392
  28.0 1.5 %collective-permute-start.9 = (f32[4,64,256]{2,1,0:T(8,128)S(1)}, f32[4,64,256]{2,1,0:T(8,128)S(1)}, u32[]{:S(2)}, u32[]{:S(2)}) collective-permute-start(f32[4,64,256]{2,1,0:T(8,128)S(1)} %pad_maximum_fusion.refs_0_), channel_id=1, source_target_pairs={{0,1},{1,0},{2,3},{3,2},{4,5},{5,4},{6,7},{7,6},{8,9},{9,8},{10,11... | collective-permute-start | bytes 786440 | tf_op jit(solution)/shard_map/ppermute | solution.py:392
  29.5 9.2 %dense_rows.1 = (bf16[32,1024,256]{2,1,0:T(8,128)(2,1)S(1)}, bf16[32,1024,256]{2,1,0:T(8,128)(2,1)S(1)}) custom-call(f32[64,256]{1,0:T(8,128)S(1)} %constant_dynamic-update-slice_fusion.e0, f32[64,256]{1,0:T(8,128)S(1)} %collective-permute-done.1.e1, f32[64,256]{1,0:T(8,128)S(1)} %collective-permute-done.2.e2, f32[64,256]{1,0:T(8,128)S(1)} %collective-permute-done.3.e3), custom_call_target="tpu_custom_call" | custom-call | flops 4294967296 | bytes 33554432 | tf_op jit(solution)/shard_map/dense_rows/pallas_call | solution.py:137
  38.7 0.6 collective-permute-start.7
  39.3 2.3 %forward_part.2.refs_3_ = f32[1024,128]{1,0:T(8,128)S(1)} custom-call(bf16[32,1024,256]{2,1,0:T(8,128)(2,1)S(1)} %get-tuple-element.48.hi_ref, bf16[32,1024,256]{2,1,0:T(8,128)(2,1)S(1)} %get-tuple-element.49.lo_ref, f32[4,64,256]{2,1,0:T(8,128)S(1)} %pad_maximum_fusion.refs_0_, f32[4,64,256]{2,1,0:T(8,128)S(1)} %collective-permute-done.13.refs_1_), custom_call_target="tpu_custom_call" | custom-call | flops 4294967296 | bytes 8388608 | tf_op jit(solution)/shard_map/forward_part/pallas_call | solution.py:179
  41.6 2.5 %collective-permute-start.16 = (f32[64,256]{1,0:T(8,128)S(1)}, f32[64,256]{1,0:T(8,128)S(1)}, u32[]{:S(2)}, u32[]{:S(2)}) collective-permute-start(f32[64,256]{1,0:T(8,128)S(1)} %get-tuple-element.57), channel_id=1, source_target_pairs={{0,24},{1,25},{2,26},{3,27},{4,28},{5,29},{6,30},{7,31},{8,16},{9,... | collective-permute-start | bytes 196616 | tf_op jit(solution)/shard_map/ppermute | solution.py:392
  44.6 0.6 collective-permute-done.7.refs_0_
  45.3 3.4 %forward_part.3.refs_3_ = f32[1024,128]{1,0:T(8,128)S(1)} custom-call(bf16[32,1024,256]{2,1,0:T(8,128)(2,1)S(1)} %get-tuple-element.48.hi_ref, bf16[32,1024,256]{2,1,0:T(8,128)(2,1)S(1)} %get-tuple-element.49.lo_ref, f32[4,64,256]{2,1,0:T(8,128)S(1)} %collective-permute-done.7.refs_0_, f32[4,64,256]{2,1,0:T(8,128)S(1)} %collective-permute-done.9.refs_1_, ...), custom_call_target="tpu_custom_call" | custom-call | flops 6442450944 | bytes 12582912 | tf_op jit(solution)/shard_map/forward_part/pallas_call | solution.py:179
  48.7 5.8 %last_forward.1 = (f32[64,256]{1,0:T(8,128)S(1)}, f32[64,256]{1,0:T(8,128)S(1)}, f32[64,256]{1,0:T(8,128)S(1)}, f32[64,256]{1,0:T(8,128)S(1)}, bf16[128,1024]{1,0:T(8,128)(2,1)S(1)}, /*index=5*/f32[8,256]{1,0:T(8,128)S(1)}) custom-call(bf16[32,1024,256]{2,1,0:T(8,128)(2,1)S(1)} %get-tuple-element.48.hi_ref, ...), custom_call_target="tpu_custom_call" | custom-call | flops 6442450944 | bytes 12582912 | tf_op jit(solution)/shard_map/last_forward/pallas_call | solution.py:232
  54.5 0.7 backward_part.4.own
  55.3 1.5 %collective-permute-start.17 = (f32[64,256]{1,0:T(8,128)S(1)}, f32[64,256]{1,0:T(8,128)S(1)}, u32[]{:S(2)}, u32[]{:S(2)}) collective-permute-start(f32[64,256]{1,0:T(8,128)S(1)} %get-tuple-element.64), channel_id=1, source_target_pairs={{0,8},{1,9},{2,10},{3,11},{4,12},{5,13},{6,14},{7,15},{8,0},{9,1},... | collective-permute-start | bytes 196616 | tf_op jit(solution)/shard_map/ppermute | solution.py:392
  56.7 1.5 %collective-permute-start.18 = (f32[64,256]{1,0:T(8,128)S(1)}, f32[64,256]{1,0:T(8,128)S(1)}, u32[]{:S(2)}, u32[]{:S(2)}) collective-permute-start(f32[64,256]{1,0:T(8,128)S(1)} %get-tuple-element.65), channel_id=1, source_target_pairs={{0,16},{1,17},{2,18},{3,19},{4,20},{5,21},{6,22},{7,23},{8,24},{9,... | collective-permute-start | bytes 196616 | tf_op jit(solution)/shard_map/ppermute | solution.py:392
  58.2 1.5 %collective-permute-start.19 = (f32[64,256]{1,0:T(8,128)S(1)}, f32[64,256]{1,0:T(8,128)S(1)}, u32[]{:S(2)}, u32[]{:S(2)}) collective-permute-start(f32[64,256]{1,0:T(8,128)S(1)} %get-tuple-element.66), channel_id=1, source_target_pairs={{0,24},{1,25},{2,26},{3,27},{4,28},{5,29},{6,30},{7,31},{8,16},{9,... | collective-permute-start | bytes 196616 | tf_op jit(solution)/shard_map/ppermute | solution.py:392
  59.7 1.8 %backward_part.7 = f32[776,256]{1,0:T(8,128)S(1)} custom-call(bf16[32,1024,256]{2,1,0:T(8,128)(2,1)S(1)} %get-tuple-element.48.hi_ref, bf16[32,1024,256]{2,1,0:T(8,128)(2,1)S(1)} %get-tuple-element.49.lo_ref, bf16[128,1024]{1,0:T(8,128)(2,1)S(1)} %get-tuple-element.58.both_ref, f32[8,256]{1,0:T(8,128)S(1)} %get-tuple-element.68.refs_0_.beta), custom_call_target="tpu_custom_call" | custom-call | flops 6442450944 | bytes 12582912 | tf_op jit(solution)/shard_map/backward_part/pallas_call | solution.py:266
  61.6 1.8 %backward_part.6.near = f32[768,256]{1,0:T(8,128)S(1)} custom-call(bf16[32,1024,256]{2,1,0:T(8,128)(2,1)S(1)} %get-tuple-element.48.hi_ref, bf16[32,1024,256]{2,1,0:T(8,128)(2,1)S(1)} %get-tuple-element.49.lo_ref, bf16[128,1024]{1,0:T(8,128)(2,1)S(1)} %get-tuple-element.58.both_ref), custom_call_target="tpu_custom_call" | custom-call | flops 6442450944 | bytes 12582912 | tf_op jit(solution)/shard_map/backward_part/pallas_call | solution.py:266
  63.5 0.7 backward_part.5
  64.2 0.6 collective-permute-start.21
  64.8 1.0 %collective-permute-start.23 = (f32[264,256]{1,0:T(8,128)S(1)}, f32[264,256]{1,0:T(8,128)S(1)}, u32[]{:S(2)}, u32[]{:S(2)}) collective-permute-start(f32[264,256]{1,0:T(8,128)S(1)} %get-tuple-element.69), channel_id=1, source_target_pairs={{0,4},{1,5},{2,6},{3,7},{4,0},{5,1},{6,2},{7,3},{8,12},{9,13},{10,... | collective-permute-start | bytes 811016 | tf_op jit(solution)/shard_map/ppermute | solution.py:392
  65.9 0.5 collective-permute-start.24
  66.4 2.0 %collective-permute-start.25 = (f32[264,256]{1,0:T(8,128)S(1)}, f32[264,256]{1,0:T(8,128)S(1)}, u32[]{:S(2)}, u32[]{:S(2)}) collective-permute-start(f32[264,256]{1,0:T(8,128)S(1)} %get-tuple-element.71), channel_id=1, source_target_pairs={{0,5},{1,4},{2,7},{3,6},{4,1},{5,0},{6,3},{7,2},{8,13},{9,12},{10,... | collective-permute-start | bytes 811016 | tf_op jit(solution)/shard_map/ppermute | solution.py:392
  68.4 0.6 collective-permute-start.20
  69.0 5.2 %collective-permute-done.23.r1 = f32[264,256]{1,0:T(8,128)S(1)} collective-permute-done((f32[264,256]{1,0:T(8,128)S(1)}, f32[264,256]{1,0:T(8,128)S(1)}, u32[]{:S(2)}, u32[]{:S(2)}) %collective-permute-start.23) | collective-permute-done | bytes 270368 | tf_op jit(solution)/shard_map/ppermute | solution.py:392
  74.2 6.8 %collective-permute-done.24.r2 = f32[264,256]{1,0:T(8,128)S(1)} collective-permute-done((f32[264,256]{1,0:T(8,128)S(1)}, f32[264,256]{1,0:T(8,128)S(1)}, u32[]{:S(2)}, u32[]{:S(2)}) %collective-permute-start.24) | collective-permute-done | bytes 270368 | tf_op jit(solution)/shard_map/ppermute | solution.py:392
  81.0 1.1 %right_norm.1 = (f32[72,256]{1,0:T(8,128)S(1)}, f32[72,256]{1,0:T(8,128)S(1)}, f32[72,256]{1,0:T(8,128)S(1)}, f32[72,256]{1,0:T(8,128)S(1)}, f32[8,256]{1,0:T(8,128)S(1)}) custom-call(f32[256,256]{1,0:T(8,128)S(1)} %backward_part.4.own, f32[256,256]{1,0:T(8,128)S(1)} %collective-permute-done.21.peer, f32[264,256]{1,0:T(8,128)S(1)} %collective-permute-done.23.r1, ...), custom_call_target="tpu_custom_call" | custom-call | flops 1048576 | bytes 1638400 | tf_op jit(solution)/shard_map/right_norm/pallas_call | solution.py:316
  82.3 2.5 %collective-permute-start.27 = (f32[72,256]{1,0:T(8,128)S(1)}, f32[72,256]{1,0:T(8,128)S(1)}, u32[]{:S(2)}, u32[]{:S(2)}) collective-permute-start(f32[72,256]{1,0:T(8,128)S(1)} %get-tuple-element.75), channel_id=1, source_target_pairs={{0,16},{1,17},{2,18},{3,19},{4,20},{5,21},{6,22},{7,23},{8,24},{9,... | collective-permute-start | bytes 221192 | tf_op jit(solution)/shard_map/ppermute | solution.py:392
  84.8 1.8 %collective-permute-start.28 = (f32[72,256]{1,0:T(8,128)S(1)}, f32[72,256]{1,0:T(8,128)S(1)}, u32[]{:S(2)}, u32[]{:S(2)}) collective-permute-start(f32[72,256]{1,0:T(8,128)S(1)} %get-tuple-element.76), channel_id=1, source_target_pairs={{0,24},{1,25},{2,26},{3,27},{4,28},{5,29},{6,30},{7,31},{8,16},{9,... | collective-permute-start | bytes 221192 | tf_op jit(solution)/shard_map/ppermute | solution.py:392
  86.6 1.2 %collective-permute-done.29 = f32[8,256]{1,0:T(8,128)S(1)} collective-permute-done((f32[8,256]{1,0:T(8,128)S(1)}, f32[8,256]{1,0:T(8,128)S(1)}, u32[]{:S(2)}, u32[]{:S(2)}) %collective-permute-start.29) | collective-permute-done | bytes 8224 | tf_op jit(solution)/shard_map/ppermute | solution.py:392
  87.8 1.1 %collective-permute-start.30 = (f32[8,256]{1,0:T(8,128)S(1)}, f32[8,256]{1,0:T(8,128)S(1)}, u32[]{:S(2)}, u32[]{:S(2)}) collective-permute-start(f32[8,256]{1,0:T(8,128)S(1)} %add.9), channel_id=1, source_target_pairs={{0,4},{1,5},{2,6},{3,7},{4,0},{5,1},{6,2},{7,3},{8,12},{9,13},{10,... | collective-permute-start | bytes 24584 | tf_op jit(solution)/shard_map/ppermute | solution.py:392
  88.8 2.6 %collective-permute-done.30 = f32[8,256]{1,0:T(8,128)S(1)} collective-permute-done((f32[8,256]{1,0:T(8,128)S(1)}, f32[8,256]{1,0:T(8,128)S(1)}, u32[]{:S(2)}, u32[]{:S(2)}) %collective-permute-start.30) | collective-permute-done | bytes 8224 | tf_op jit(solution)/shard_map/ppermute | solution.py:392
  91.4 0.5 collective-permute-start.31
  91.9 3.1 %collective-permute-done.31 = f32[8,256]{1,0:T(8,128)S(1)} collective-permute-done((f32[8,256]{1,0:T(8,128)S(1)}, f32[8,256]{1,0:T(8,128)S(1)}, u32[]{:S(2)}, u32[]{:S(2)}) %collective-permute-start.31) | collective-permute-done | bytes 8224 | tf_op jit(solution)/shard_map/ppermute | solution.py:392
  95.1 2.0 %collective-permute-start.34 = (f32[8,256]{1,0:T(8,128)S(1)}, f32[8,256]{1,0:T(8,128)S(1)}, u32[]{:S(2)}, u32[]{:S(2)}) collective-permute-start(f32[8,256]{1,0:T(8,128)S(1)} %add.11.a0), channel_id=1, source_target_pairs={{0,24},{1,25},{2,26},{3,27},{4,28},{5,29},{6,30},{7,31},{8,16},{9,... | collective-permute-start | bytes 24584 | tf_op jit(solution)/shard_map/ppermute | solution.py:392
  97.1 2.4 %collective-permute-start.32 = (f32[8,256]{1,0:T(8,128)S(1)}, f32[8,256]{1,0:T(8,128)S(1)}, u32[]{:S(2)}, u32[]{:S(2)}) collective-permute-start(f32[8,256]{1,0:T(8,128)S(1)} %add.11.a0), channel_id=1, source_target_pairs={{0,8},{1,9},{2,10},{3,11},{4,12},{5,13},{6,14},{7,15},{8,0},{9,1},... | collective-permute-start | bytes 24584 | tf_op jit(solution)/shard_map/ppermute | solution.py:392
  99.5 1.1 %left_out.1 = (f32[512,256]{1,0:T(8,128)}, f32[256,256]{1,0:T(8,128)}) custom-call(f32[4,64,256]{2,1,0:T(8,128)S(1)} %pad_maximum_fusion.1.own, f32[4,64,256]{2,1,0:T(8,128)S(1)} %collective-permute-done.20.other, f32[72,256]{1,0:T(8,128)S(1)} %get-tuple-element.73.g0, f32[72,256]{1,0:T(8,128)S(1)} %collective-permute-done.26.g1, ...), custom_call_target="tpu_custom_call" | custom-call | flops 524288 | bytes 1966080 | tf_op jit(solution)/shard_map/left_out/pallas_call | solution.py:381
  100.6 1.1 %collective-permute-done.33.a2 = f32[8,256]{1,0:T(8,128)S(1)} collective-permute-done((f32[8,256]{1,0:T(8,128)S(1)}, f32[8,256]{1,0:T(8,128)S(1)}, u32[]{:S(2)}, u32[]{:S(2)}) %collective-permute-start.33) | collective-permute-done | bytes 8224 | tf_op jit(solution)/shard_map/ppermute | solution.py:392
  101.7 1.0 finish.1
  (64 shorter events, 2.4 us)
Async XLA Ops:
  2.7 10.4 %collective-permute-start = (f32[32,256]{1,0:T(8,128)S(1)}, f32[32,256]{1,0:T(8,128)S(1)}, u32[]{:S(2)}, u32[]{:S(2)}) collective-permute-start(f32[32,256]{1,0:T(8,128)S(1)} %get-tuple-element.47), channel_id=1, source_target_pairs={{0,1},{1,0},{2,3},{3,2},{4,5},{5,4},{6,7},{7,6},{8,9},{9,8},{10,11... | collective-permute-start | bytes 98312 | tf_op jit(solution)/shard_map/ppermute | solution.py:392
  5.7 0.9 copy-start
  6.7 1.0 %copy-start.3 = (f32[512,256]{1,0:T(8,128)S(1)}, f32[512,256]{1,0:T(8,128)}, u32[]{:S(2)}) copy-start(f32[512,256]{1,0:T(8,128)} %left_ref.1) | copy-start | bytes 1572868
  7.9 8.7 %collective-permute-start.4 = (f32[64,256]{1,0:T(8,128)S(1)}, f32[64,256]{1,0:T(8,128)S(1)}, u32[]{:S(2)}, u32[]{:S(2)}) collective-permute-start(f32[64,256]{1,0:T(8,128)S(1)} %get-tuple-element.51), channel_id=1, source_target_pairs={{0,8},{1,9},{2,10},{3,11},{4,12},{5,13},{6,14},{7,15},{8,0},{9,1},... | collective-permute-start | bytes 196616 | tf_op jit(solution)/shard_map/ppermute | solution.py:392
  9.6 7.2 %collective-permute-start.5 = (f32[64,256]{1,0:T(8,128)S(1)}, f32[64,256]{1,0:T(8,128)S(1)}, u32[]{:S(2)}, u32[]{:S(2)}) collective-permute-start(f32[64,256]{1,0:T(8,128)S(1)} %get-tuple-element.52), channel_id=1, source_target_pairs={{0,16},{1,17},{2,18},{3,19},{4,20},{5,21},{6,22},{7,23},{8,24},{9,... | collective-permute-start | bytes 196616 | tf_op jit(solution)/shard_map/ppermute | solution.py:392
  12.2 6.3 %collective-permute-start.6 = (f32[64,256]{1,0:T(8,128)S(1)}, f32[64,256]{1,0:T(8,128)S(1)}, u32[]{:S(2)}, u32[]{:S(2)}) collective-permute-start(f32[64,256]{1,0:T(8,128)S(1)} %get-tuple-element.53), channel_id=1, source_target_pairs={{0,24},{1,25},{2,26},{3,27},{4,28},{5,29},{6,30},{7,31},{8,16},{9,... | collective-permute-start | bytes 196616 | tf_op jit(solution)/shard_map/ppermute | solution.py:392
  12.4 29.2 %collective-permute-start.14 = (f32[64,256]{1,0:T(8,128)S(1)}, f32[64,256]{1,0:T(8,128)S(1)}, u32[]{:S(2)}, u32[]{:S(2)}) collective-permute-start(f32[64,256]{1,0:T(8,128)S(1)} %get-tuple-element.55), channel_id=1, source_target_pairs={{0,8},{1,9},{2,10},{3,11},{4,12},{5,13},{6,14},{7,15},{8,0},{9,1},... | collective-permute-start | bytes 196616 | tf_op jit(solution)/shard_map/ppermute | solution.py:392
  13.1 35.6 %collective-permute-start.15 = (f32[64,256]{1,0:T(8,128)S(1)}, f32[64,256]{1,0:T(8,128)S(1)}, u32[]{:S(2)}, u32[]{:S(2)}) collective-permute-start(f32[64,256]{1,0:T(8,128)S(1)} %get-tuple-element.56), channel_id=1, source_target_pairs={{0,16},{1,17},{2,18},{3,19},{4,20},{5,21},{6,22},{7,23},{8,24},{9,... | collective-permute-start | bytes 196616 | tf_op jit(solution)/shard_map/ppermute | solution.py:392
  16.6 7.0 %collective-permute-start.3 = (f32[64,256]{1,0:T(8,128)S(1)}, f32[64,256]{1,0:T(8,128)S(1)}, u32[]{:S(2)}, u32[]{:S(2)}) collective-permute-start(f32[64,256]{1,0:T(8,128)S(1)} %constant_dynamic-update-slice_fusion.e0), channel_id=1, source_target_pairs={{0,24},{1,25},{2,26},{3,27},{4,28},{5,29},{6,30},{7,31},{8,16},{9,... | collective-permute-start | bytes 196616 | tf_op jit(solution)/shard_map/ppermute | solution.py:392
  16.8 9.7 %collective-permute-start.2 = (f32[64,256]{1,0:T(8,128)S(1)}, f32[64,256]{1,0:T(8,128)S(1)}, u32[]{:S(2)}, u32[]{:S(2)}) collective-permute-start(f32[64,256]{1,0:T(8,128)S(1)} %constant_dynamic-update-slice_fusion.e0), channel_id=1, source_target_pairs={{0,16},{1,17},{2,18},{3,19},{4,20},{5,21},{6,22},{7,23},{8,24},{9,... | collective-permute-start | bytes 196616 | tf_op jit(solution)/shard_map/ppermute | solution.py:392
  18.5 9.5 %collective-permute-start.1 = (f32[64,256]{1,0:T(8,128)S(1)}, f32[64,256]{1,0:T(8,128)S(1)}, u32[]{:S(2)}, u32[]{:S(2)}) collective-permute-start(f32[64,256]{1,0:T(8,128)S(1)} %constant_dynamic-update-slice_fusion.e0), channel_id=1, source_target_pairs={{0,8},{1,9},{2,10},{3,11},{4,12},{5,13},{6,14},{7,15},{8,0},{9,1},... | collective-permute-start | bytes 196616 | tf_op jit(solution)/shard_map/ppermute | solution.py:392
  23.6 15.1 %collective-permute-start.13 = (f32[4,64,256]{2,1,0:T(8,128)S(1)}, f32[4,64,256]{2,1,0:T(8,128)S(1)}, u32[]{:S(2)}, u32[]{:S(2)}) collective-permute-start(f32[4,64,256]{2,1,0:T(8,128)S(1)} %pad_maximum_fusion.refs_0_), channel_id=1, source_target_pairs={{0,2},{1,3},{2,0},{3,1},{4,6},{5,7},{6,4},{7,5},{8,10},{9,11},{10,... | collective-permute-start | bytes 786440 | tf_op jit(solution)/shard_map/ppermute | solution.py:392
  26.5 17.6 %collective-permute-start.11 = (f32[4,64,256]{2,1,0:T(8,128)S(1)}, f32[4,64,256]{2,1,0:T(8,128)S(1)}, u32[]{:S(2)}, u32[]{:S(2)}) collective-permute-start(f32[4,64,256]{2,1,0:T(8,128)S(1)} %pad_maximum_fusion.refs_0_), channel_id=1, source_target_pairs={{0,5},{1,4},{2,7},{3,6},{4,1},{5,0},{6,3},{7,2},{8,13},{9,12},{10,... | collective-permute-start | bytes 786440 | tf_op jit(solution)/shard_map/ppermute | solution.py:392
  28.0 16.2 %collective-permute-start.9 = (f32[4,64,256]{2,1,0:T(8,128)S(1)}, f32[4,64,256]{2,1,0:T(8,128)S(1)}, u32[]{:S(2)}, u32[]{:S(2)}) collective-permute-start(f32[4,64,256]{2,1,0:T(8,128)S(1)} %pad_maximum_fusion.refs_0_), channel_id=1, source_target_pairs={{0,1},{1,0},{2,3},{3,2},{4,5},{5,4},{6,7},{7,6},{8,9},{9,8},{10,11... | collective-permute-start | bytes 786440 | tf_op jit(solution)/shard_map/ppermute | solution.py:392
  38.7 6.6 %collective-permute-start.7 = (f32[4,64,256]{2,1,0:T(8,128)S(1)}, f32[4,64,256]{2,1,0:T(8,128)S(1)}, u32[]{:S(2)}, u32[]{:S(2)}) collective-permute-start(f32[4,64,256]{2,1,0:T(8,128)S(1)} %pad_maximum_fusion.refs_0_), channel_id=1, source_target_pairs={{0,4},{1,5},{2,6},{3,7},{4,0},{5,1},{6,2},{7,3},{8,12},{9,13},{10,... | collective-permute-start | bytes 786440 | tf_op jit(solution)/shard_map/ppermute | solution.py:392
  41.6 7.1 %copy-start.7 = (f32[256]{0:T(256)S(1)}, f32[256]{0:T(256)}, u32[]{:S(2)}) copy-start(f32[256]{0:T(256)} %param.15) | copy-start | bytes 3076
  41.6 7.1 %collective-permute-start.16 = (f32[64,256]{1,0:T(8,128)S(1)}, f32[64,256]{1,0:T(8,128)S(1)}, u32[]{:S(2)}, u32[]{:S(2)}) collective-permute-start(f32[64,256]{1,0:T(8,128)S(1)} %get-tuple-element.57), channel_id=1, source_target_pairs={{0,24},{1,25},{2,26},{3,27},{4,28},{5,29},{6,30},{7,31},{8,16},{9,... | collective-permute-start | bytes 196616 | tf_op jit(solution)/shard_map/ppermute | solution.py:392
  44.1 4.6 %collective-permute-start.12 = (f32[4,64,256]{2,1,0:T(8,128)S(1)}, f32[4,64,256]{2,1,0:T(8,128)S(1)}, u32[]{:S(2)}, u32[]{:S(2)}) collective-permute-start(f32[4,64,256]{2,1,0:T(8,128)S(1)} %collective-permute-done.11.refs_2_), channel_id=1, source_target_pairs={{0,2},{1,3},{2,0},{3,1},{4,6},{5,7},{6,4},{7,5},{8,10},{9,11},{10,... | collective-permute-start | bytes 786440 | tf_op jit(solution)/shard_map/ppermute | solution.py:392
  44.1 4.6 %collective-permute-start.10 = (f32[4,64,256]{2,1,0:T(8,128)S(1)}, f32[4,64,256]{2,1,0:T(8,128)S(1)}, u32[]{:S(2)}, u32[]{:S(2)}) collective-permute-start(f32[4,64,256]{2,1,0:T(8,128)S(1)} %collective-permute-done.9.refs_1_), channel_id=1, source_target_pairs={{0,2},{1,3},{2,0},{3,1},{4,6},{5,7},{6,4},{7,5},{8,10},{9,11},{10,... | collective-permute-start | bytes 786440 | tf_op jit(solution)/shard_map/ppermute | solution.py:392
  45.3 3.5 %collective-permute-start.8 = (f32[4,64,256]{2,1,0:T(8,128)S(1)}, f32[4,64,256]{2,1,0:T(8,128)S(1)}, u32[]{:S(2)}, u32[]{:S(2)}) collective-permute-start(f32[4,64,256]{2,1,0:T(8,128)S(1)} %collective-permute-done.7.refs_0_), channel_id=1, source_target_pairs={{0,2},{1,3},{2,0},{3,1},{4,6},{5,7},{6,4},{7,5},{8,10},{9,11},{10,... | collective-permute-start | bytes 786440 | tf_op jit(solution)/shard_map/ppermute | solution.py:392
  55.3 10.6 %collective-permute-start.17 = (f32[64,256]{1,0:T(8,128)S(1)}, f32[64,256]{1,0:T(8,128)S(1)}, u32[]{:S(2)}, u32[]{:S(2)}) collective-permute-start(f32[64,256]{1,0:T(8,128)S(1)} %get-tuple-element.64), channel_id=1, source_target_pairs={{0,8},{1,9},{2,10},{3,11},{4,12},{5,13},{6,14},{7,15},{8,0},{9,1},... | collective-permute-start | bytes 196616 | tf_op jit(solution)/shard_map/ppermute | solution.py:392
  56.7 9.6 %collective-permute-start.18 = (f32[64,256]{1,0:T(8,128)S(1)}, f32[64,256]{1,0:T(8,128)S(1)}, u32[]{:S(2)}, u32[]{:S(2)}) collective-permute-start(f32[64,256]{1,0:T(8,128)S(1)} %get-tuple-element.65), channel_id=1, source_target_pairs={{0,16},{1,17},{2,18},{3,19},{4,20},{5,21},{6,22},{7,23},{8,24},{9,... | collective-permute-start | bytes 196616 | tf_op jit(solution)/shard_map/ppermute | solution.py:392
  58.2 10.2 %collective-permute-start.19 = (f32[64,256]{1,0:T(8,128)S(1)}, f32[64,256]{1,0:T(8,128)S(1)}, u32[]{:S(2)}, u32[]{:S(2)}) collective-permute-start(f32[64,256]{1,0:T(8,128)S(1)} %get-tuple-element.66), channel_id=1, source_target_pairs={{0,24},{1,25},{2,26},{3,27},{4,28},{5,29},{6,30},{7,31},{8,16},{9,... | collective-permute-start | bytes 196616 | tf_op jit(solution)/shard_map/ppermute | solution.py:392
  61.5 3.2 %collective-permute-start.22 = (f32[776,256]{1,0:T(8,128)S(1)}, f32[776,256]{1,0:T(8,128)S(1)}, u32[]{:S(2)}, u32[]{:S(2)}) collective-permute-start(f32[776,256]{1,0:T(8,128)S(1)} %backward_part.7), channel_id=1, source_target_pairs={{0,2},{1,3},{2,0},{3,1},{4,6},{5,7},{6,4},{7,5},{8,10},{9,11},{10,... | collective-permute-start | bytes 2383880 | tf_op jit(solution)/shard_map/ppermute | solution.py:392
  63.4 36.1 %copy-start.2 = (f32[256,256]{1,0:T(8,128)S(1)}, f32[256,256]{1,0:T(8,128)}, u32[]{:S(2)}) copy-start(f32[256,256]{1,0:T(8,128)} %search.3) | copy-start | bytes 786436
  63.4 36.1 %copy-start.4 = (f32[256,256]{1,0:T(8,128)S(1)}, f32[256,256]{1,0:T(8,128)}, u32[]{:S(2)}) copy-start(f32[256,256]{1,0:T(8,128)} %solution.1) | copy-start | bytes 786436
  63.4 36.1 %copy-start.5 = (f32[256]{0:T(256)S(1)}, f32[256]{0:T(256)}, u32[]{:S(2)}) copy-start(f32[256]{0:T(256)} %param.16) | copy-start | bytes 3076
  63.4 36.1 %copy-start.6 = (f32[256]{0:T(256)S(1)}, f32[256]{0:T(256)}, u32[]{:S(2)}) copy-start(f32[256]{0:T(256)} %param.17) | copy-start | bytes 3076
  63.5 38.2 %copy-start.1 = (f32[256,256]{1,0:T(8,128)S(1)}, f32[256,256]{1,0:T(8,128)}, u32[]{:S(2)}) copy-start(f32[256,256]{1,0:T(8,128)} %right.1) | copy-start | bytes 786436
  64.2 4.8 %collective-permute-start.21 = (f32[256,256]{1,0:T(8,128)S(1)}, f32[256,256]{1,0:T(8,128)S(1)}, u32[]{:S(2)}, u32[]{:S(2)}) collective-permute-start(f32[256,256]{1,0:T(8,128)S(1)} %backward_part.5), channel_id=1, source_target_pairs={{0,2},{1,3},{2,0},{3,1},{4,6},{5,7},{6,4},{7,5},{8,10},{9,11},{10,... | collective-permute-start | bytes 786440 | tf_op jit(solution)/shard_map/ppermute | solution.py:392
  64.8 9.4 %collective-permute-start.23 = (f32[264,256]{1,0:T(8,128)S(1)}, f32[264,256]{1,0:T(8,128)S(1)}, u32[]{:S(2)}, u32[]{:S(2)}) collective-permute-start(f32[264,256]{1,0:T(8,128)S(1)} %get-tuple-element.69), channel_id=1, source_target_pairs={{0,4},{1,5},{2,6},{3,7},{4,0},{5,1},{6,2},{7,3},{8,12},{9,13},{10,... | collective-permute-start | bytes 811016 | tf_op jit(solution)/shard_map/ppermute | solution.py:392
  65.9 15.2 %collective-permute-start.24 = (f32[264,256]{1,0:T(8,128)S(1)}, f32[264,256]{1,0:T(8,128)S(1)}, u32[]{:S(2)}, u32[]{:S(2)}) collective-permute-start(f32[264,256]{1,0:T(8,128)S(1)} %get-tuple-element.70), channel_id=1, source_target_pairs={{0,1},{1,0},{2,3},{3,2},{4,5},{5,4},{6,7},{7,6},{8,9},{9,8},{10,11... | collective-permute-start | bytes 811016 | tf_op jit(solution)/shard_map/ppermute | solution.py:392
  66.4 14.7 %collective-permute-start.25 = (f32[264,256]{1,0:T(8,128)S(1)}, f32[264,256]{1,0:T(8,128)S(1)}, u32[]{:S(2)}, u32[]{:S(2)}) collective-permute-start(f32[264,256]{1,0:T(8,128)S(1)} %get-tuple-element.71), channel_id=1, source_target_pairs={{0,5},{1,4},{2,7},{3,6},{4,1},{5,0},{6,3},{7,2},{8,13},{9,12},{10,... | collective-permute-start | bytes 811016 | tf_op jit(solution)/shard_map/ppermute | solution.py:392
  68.4 28.7 %collective-permute-start.20 = (f32[4,64,256]{2,1,0:T(8,128)S(1)}, f32[4,64,256]{2,1,0:T(8,128)S(1)}, u32[]{:S(2)}, u32[]{:S(2)}) collective-permute-start(f32[4,64,256]{2,1,0:T(8,128)S(1)} %pad_maximum_fusion.1.own), channel_id=1, source_target_pairs={{0,1},{1,0},{2,3},{3,2},{4,5},{5,4},{6,7},{7,6},{8,9},{9,8},{10,11... | collective-permute-start | bytes 786440 | tf_op jit(solution)/shard_map/ppermute | solution.py:392
  82.2 14.9 %collective-permute-start.26 = (f32[72,256]{1,0:T(8,128)S(1)}, f32[72,256]{1,0:T(8,128)S(1)}, u32[]{:S(2)}, u32[]{:S(2)}) collective-permute-start(f32[72,256]{1,0:T(8,128)S(1)} %get-tuple-element.74), channel_id=1, source_target_pairs={{0,8},{1,9},{2,10},{3,11},{4,12},{5,13},{6,14},{7,15},{8,0},{9,1},... | collective-permute-start | bytes 221192 | tf_op jit(solution)/shard_map/ppermute | solution.py:392
  82.3 17.2 %collective-permute-start.27 = (f32[72,256]{1,0:T(8,128)S(1)}, f32[72,256]{1,0:T(8,128)S(1)}, u32[]{:S(2)}, u32[]{:S(2)}) collective-permute-start(f32[72,256]{1,0:T(8,128)S(1)} %get-tuple-element.75), channel_id=1, source_target_pairs={{0,16},{1,17},{2,18},{3,19},{4,20},{5,21},{6,22},{7,23},{8,24},{9,... | collective-permute-start | bytes 221192 | tf_op jit(solution)/shard_map/ppermute | solution.py:392
  84.8 14.7 %collective-permute-start.28 = (f32[72,256]{1,0:T(8,128)S(1)}, f32[72,256]{1,0:T(8,128)S(1)}, u32[]{:S(2)}, u32[]{:S(2)}) collective-permute-start(f32[72,256]{1,0:T(8,128)S(1)} %get-tuple-element.76), channel_id=1, source_target_pairs={{0,24},{1,25},{2,26},{3,27},{4,28},{5,29},{6,30},{7,31},{8,16},{9,... | collective-permute-start | bytes 221192 | tf_op jit(solution)/shard_map/ppermute | solution.py:392
  86.6 1.2 %collective-permute-start.29 = (f32[8,256]{1,0:T(8,128)S(1)}, f32[8,256]{1,0:T(8,128)S(1)}, u32[]{:S(2)}, u32[]{:S(2)}) collective-permute-start(f32[8,256]{1,0:T(8,128)S(1)} %get-tuple-element.78), channel_id=1, source_target_pairs={{0,2},{1,3},{2,0},{3,1},{4,6},{5,7},{6,4},{7,5},{8,10},{9,11},{10,... | collective-permute-start | bytes 24584 | tf_op jit(solution)/shard_map/ppermute | solution.py:392
  87.8 3.7 %collective-permute-start.30 = (f32[8,256]{1,0:T(8,128)S(1)}, f32[8,256]{1,0:T(8,128)S(1)}, u32[]{:S(2)}, u32[]{:S(2)}) collective-permute-start(f32[8,256]{1,0:T(8,128)S(1)} %add.9), channel_id=1, source_target_pairs={{0,4},{1,5},{2,6},{3,7},{4,0},{5,1},{6,2},{7,3},{8,12},{9,13},{10,... | collective-permute-start | bytes 24584 | tf_op jit(solution)/shard_map/ppermute | solution.py:392
  91.4 3.7 %collective-permute-start.31 = (f32[8,256]{1,0:T(8,128)S(1)}, f32[8,256]{1,0:T(8,128)S(1)}, u32[]{:S(2)}, u32[]{:S(2)}) collective-permute-start(f32[8,256]{1,0:T(8,128)S(1)} %add.10), channel_id=1, source_target_pairs={{0,1},{1,0},{2,3},{3,2},{4,5},{5,4},{6,7},{7,6},{8,9},{9,8},{10,11... | collective-permute-start | bytes 24584 | tf_op jit(solution)/shard_map/ppermute | solution.py:392
  95.1 5.5 %collective-permute-start.34 = (f32[8,256]{1,0:T(8,128)S(1)}, f32[8,256]{1,0:T(8,128)S(1)}, u32[]{:S(2)}, u32[]{:S(2)}) collective-permute-start(f32[8,256]{1,0:T(8,128)S(1)} %add.11.a0), channel_id=1, source_target_pairs={{0,24},{1,25},{2,26},{3,27},{4,28},{5,29},{6,30},{7,31},{8,16},{9,... | collective-permute-start | bytes 24584 | tf_op jit(solution)/shard_map/ppermute | solution.py:392
  97.1 4.6 %collective-permute-start.33 = (f32[8,256]{1,0:T(8,128)S(1)}, f32[8,256]{1,0:T(8,128)S(1)}, u32[]{:S(2)}, u32[]{:S(2)}) collective-permute-start(f32[8,256]{1,0:T(8,128)S(1)} %add.11.a0), channel_id=1, source_target_pairs={{0,16},{1,17},{2,18},{3,19},{4,20},{5,21},{6,22},{7,23},{8,24},{9,... | collective-permute-start | bytes 24584 | tf_op jit(solution)/shard_map/ppermute | solution.py:392
  97.1 4.5 %collective-permute-start.32 = (f32[8,256]{1,0:T(8,128)S(1)}, f32[8,256]{1,0:T(8,128)S(1)}, u32[]{:S(2)}, u32[]{:S(2)}) collective-permute-start(f32[8,256]{1,0:T(8,128)S(1)} %add.11.a0), channel_id=1, source_target_pairs={{0,8},{1,9},{2,10},{3,11},{4,12},{5,13},{6,14},{7,15},{8,0},{9,1},... | collective-permute-start | bytes 24584 | tf_op jit(solution)/shard_map/ppermute | solution.py:392

commit v3 on v2

v3 whole, which is shorter than its diff:
```python
import functools

import jax
import jax.numpy as jnp
from jax import lax
from jax.experimental import pallas as pl
from jax.experimental.pallas import tpu as pltpu
from jax.sharding import PartitionSpec as P

epsilon = 1e-06
AXES = ("doc", "feat")
MIB = 1024 * 1024


Y_BIT, CORE_BIT, X_BIT, Z_SHIFT = 1, 2, 4, 3
NT = (((1,), (1,)), ((), ()))


def coords():
    d = lax.axis_index("doc")
    y = lax.axis_index("feat")
    return d, d >> 2, y


def params(mib):
    return pltpu.CompilerParams(vmem_limit_bytes=mib * MIB)


def cost(flops, nbytes):
    return pl.CostEstimate(flops=int(flops), bytes_accessed=int(nbytes), transcendentals=0)


def f32(*shape):
    return jax.ShapeDtypeStruct(shape, jnp.float32)


def bf16(*shape):
    return jax.ShapeDtypeStruct(shape, jnp.bfloat16)


def quarters_kernel(ref, m0, m1, m2, m3, turned):
    _, z, _ = coords()
    turned[...] = ref[...].T.reshape(turned.shape)
    for k, out in enumerate((m0, m1, m2, m3)):
        out[...] = turned[z ^ k]


def quarters_of(value, name):
    rows, cols = value.shape
    q = cols // 4
    return pl.pallas_call(
        quarters_kernel,
        out_shape=[f32(q, rows)] * 4,
        scratch_shapes=[pltpu.VMEM((4, q, rows), jnp.float32)],
        compiler_params=params(8),
        cost_estimate=cost(0, rows * cols * 8),
        name=name,
    )(value)


def build_kernel(e0, e1, e2, e3, hi_ref, lo_ref):
    d, _, _ = coords()
    n = e0.shape[0] // 2
    iota = lax.broadcasted_iota(jnp.int32, (256, 256), 0).astype(jnp.float32).astype(jnp.bfloat16)
    lane_doc = lax.broadcasted_iota(jnp.int32, (8, 256), 1) >> 4
    one = jnp.ones((256, 256), jnp.bfloat16)
    zero = jnp.zeros((256, 256), jnp.bfloat16)

    def spread(row):
        wide = jnp.broadcast_to(row, (16, 256)).astype(jnp.bfloat16)
        return jnp.broadcast_to(wide[None], (16, 16, 256)).reshape(256, 256)

    for k, entries in enumerate((e0, e1, e2, e3)):

        @pl.loop(0, n // 8)
        def _(step, k=k, entries=entries):
            at = pl.multiple_of(step * 8, 8)
            ids = entries[pl.ds(at, 8), :].astype(jnp.int32)
            vals = entries[pl.ds(n + at, 8), :]
            rel = (ids >> 8) ^ d
            block = ((rel & 1) << 3) | ((rel & 2) << 1) | (rel >> 2)
            code = (block * 16 + lane_doc).astype(jnp.float32)
            inner = (ids & 255).astype(jnp.float32)
            for t in range(8):
                pick = jnp.where(iota == spread(code[t : t + 1]), one, zero)
                weigh = jnp.where(iota == spread(inner[t : t + 1]), spread(vals[t : t + 1]), zero)
                dense = lax.dot_general(pick, weigh, NT, preferred_element_type=jnp.float32)
                high = dense.astype(jnp.bfloat16)
                low = (dense - high.astype(jnp.float32)).astype(jnp.bfloat16)
                docs = pl.ds(pl.multiple_of(k * 16 * n + step * 128 + 16 * t, 16), 16)
                hi_ref[:, docs, :] = high.reshape(16, 16, 256)
                lo_ref[:, docs, :] = low.reshape(16, 16, 256)


def whole():
    return pl.BlockSpec(memory_space=pltpu.VMEM)


def build(entries):
    docs = 4 * (entries[0].shape[0] // 2 * 16)
    return pl.pallas_call(
        build_kernel,
        in_specs=[whole()] * 4,
        out_specs=[whole()] * 2,
        out_shape=[pltpu.VMEM((16, docs, 256), jnp.bfloat16)] * 2,
        compiler_params=params(12),
        cost_estimate=cost(2 * docs * 16 * 256 * 256, docs * 4096 * 4),
        name="dense_rows",
    )(*entries)


def split_rows(value):
    high = value.astype(jnp.bfloat16)
    low = (value - high.astype(jnp.float32)).astype(jnp.bfloat16)
    return jnp.concatenate([high, low], axis=0)


def block_product(hi_ref, lo_ref, docs, first, vecs):
    lhs, rhs = [], []
    for k in range(2):
        both = split_rows(vecs[k])
        lhs += [hi_ref[first + k, docs, :], lo_ref[first + k, docs, :]]
        rhs += [both, both]
    return lax.dot_general(
        jnp.concatenate(lhs, axis=1), jnp.concatenate(rhs, axis=1), NT, preferred_element_type=jnp.float32
    )


def add_products(hi_ref, lo_ref, docs, vecs, blocks, total):
    for vec, first in zip(vecs, blocks):
        for pair in (0, 2):
            total[...] += block_product(hi_ref, lo_ref, docs, first + pair, vec[pair : pair + 2])


def forward_kernel(blocks, hi_ref, lo_ref, v0, v1, total):
    total[...] = jnp.zeros_like(total)
    for half in range(2):
        n = total.shape[0] // 2
        docs = slice(half * n, (half + 1) * n)
        add_products(hi_ref, lo_ref, docs, (v0, v1), blocks, total.at[docs])


def forward_part(hi, lo, vecs, blocks):
    docs = hi.shape[1]
    q = vecs[0].shape[1]
    n = 4 * len(blocks)
    return pl.pallas_call(
        functools.partial(forward_kernel, blocks),
        in_specs=[whole()] * 4,
        out_specs=whole(),
        out_shape=f32(docs, 2 * q),
        compiler_params=params(12),
        cost_estimate=cost(8 * docs * 256 * 256 * n, 4 * docs * 256 * n),
        name="forward_part",
    )(hi, lo, *vecs)


def forward_half_kernel(half, blocks, hi_ref, lo_ref, v0, v1, before, out, total):
    n = total.shape[0]
    docs = slice(half * n, (half + 1) * n)
    total[...] = before[docs, :]
    add_products(hi_ref, lo_ref, docs, (v0, v1), blocks, total)
    turned = total[...].T
    q = out.shape[0]
    out[...] = turned[:q] + turned[q:]


def forward_half(hi, lo, vecs, before, blocks, half):
    docs = hi.shape[1] // 2
    q = vecs[0].shape[1]
    n = 4 * len(blocks)
    return pl.pallas_call(
        functools.partial(forward_half_kernel, half, blocks),
        in_specs=[whole()] * 5,
        out_specs=whole(),
        out_shape=f32(q, docs),
        scratch_shapes=[pltpu.VMEM((docs, 2 * q), jnp.float32)],
        compiler_params=params(12),
        cost_estimate=cost(8 * docs * 256 * 256 * n, 4 * docs * 256 * n),
        name="forward_half",
    )(hi, lo, *vecs, before)


def square_row(value, z, cols):
    q, n = value.shape
    sums = value[:, 0:128] * value[:, 0:128]
    for at in range(128, n, 128):
        sums = sums + value[:, at : at + 128] * value[:, at : at + 128]
    row = jnp.sum(jnp.concatenate([sums] * (128 // q), axis=0).T, axis=0, keepdims=True)
    row = jnp.broadcast_to(jnp.concatenate([row] * (cols // 128), axis=1), (8, cols))
    lane = lax.broadcasted_iota(jnp.int32, (8, cols), 1)
    return jnp.where(lane // q == z, row, 0.0)


def row_to_column(row):
    return jnp.broadcast_to(row, (128, row.shape[1])).T


def left_raw_kernel(has_before, mine, other, u0, u1, alpha, *refs):
    l0, l1, both, sums, columns = refs[-5:]
    _, z, _ = coords()
    q, docs = u0.shape
    columns[...] = row_to_column(alpha[...])
    scale = columns[pl.ds(pl.multiple_of(z * q, q), q), :][:, 0:1]
    for k, (u, out) in enumerate(((u0, l0), (u1, l1))):
        at = slice(k * docs, (k + 1) * docs)
        out[...] = (mine[:, at] + other[:, at]) - scale * u[...]
    left = jnp.concatenate([l0[...], l1[...]], axis=1)
    both[...] = split_rows(left)
    squares = square_row(left, z, sums.shape[1])
    sums[...] = refs[0][...] + squares if has_before else squares


def left_raw(mine, other, lefts, alpha, before=None):
    q, docs = lefts[0].shape
    extra = [] if before is None else [before]
    return pl.pallas_call(
        functools.partial(left_raw_kernel, before is not None),
        out_shape=[f32(q, docs)] * 2 + [bf16(2 * q, 2 * docs), f32(8, 4 * q)],
        scratch_shapes=[pltpu.VMEM((4 * q, 128), jnp.float32)],
        compiler_params=params(8),
        cost_estimate=cost(8 * q * docs, 40 * q * docs),
        name="left_raw",
    )(mine, other, *lefts, alpha, *extra)


def backward_kernel(half, first, blocks, parts, hi_ref, lo_ref, both_ref, *refs):
    out_ref = refs[-1]
    both = both_ref[...]
    q, n = both.shape[0] // 2, both.shape[1]
    docs = slice(half * n, (half + 1) * n)
    twice = jnp.concatenate([both, both], axis=1)
    for b in range(blocks):
        got = jnp.dot(
            twice,
            jnp.concatenate([hi_ref[first + b, docs, :], lo_ref[first + b, docs, :]], axis=0),
            preferred_element_type=jnp.float32,
        )
        got = got[:q] + got[q:]
        if "before" in parts:
            got = got + refs[0][(first + b) * q : (first + b + 1) * q, :]
        out_ref[b * q : (b + 1) * q, :] = got
    if "tail" in parts:
        out_ref[blocks * q :, :] = refs[-2][...]


def backward_part(hi, lo, both, half, first, blocks, before=None, tail=None):
    q, docs = both.shape[0] // 2, both.shape[1]
    extra = {"before": before, "tail": tail}
    extra = {name: value for name, value in extra.items() if value is not None}
    rows = blocks * q + (0 if tail is None else tail.shape[0])
    return pl.pallas_call(
        functools.partial(backward_kernel, half, first, blocks, tuple(extra)),
        in_specs=[whole()] * (3 + len(extra)),
        out_specs=whole(),
        out_shape=f32(rows, 256),
        compiler_params=params(12),
        cost_estimate=cost(8 * docs * 256 * 256 * blocks, 4 * docs * 256 * blocks),
        name="backward_part",
    )(hi, lo, both, *extra.values())


def far_sum_kernel(near, far, beta, send, keep, beta_core):
    n = keep.shape[0]
    beta_core[...] = beta[...] + far[2 * n :, :]
    send[0:n, :] = near[n:, :] + far[n : 2 * n, :]
    send[n:, :] = beta_core[...]
    keep[...] = near[0:n, :] + far[0:n, :]


def far_sums(near, far, beta):
    rows = near.shape[0] // 2
    return pl.pallas_call(
        far_sum_kernel,
        out_shape=[f32(rows + 8, 256), f32(rows, 256), f32(8, 256)],
        compiler_params=params(8),
        cost_estimate=cost(near.size, near.size * 12),
        name="far_sums",
    )(near, far, beta)


def right_norm_kernel(docs_total, keep, got, beta_core, v0, v1, v2, v3, g0, g1, g2, g3, sums, columns):
    _, z, _ = coords()
    q = v0.shape[0]
    beta_sums = beta_core[...] + got[4 * q :, :]
    columns[...] = row_to_column(jnp.sqrt(beta_sums[0:1, :] / docs_total + epsilon))
    beta = columns[pl.ds(pl.multiple_of(z * q, q), q), :][:, 0:1]
    raws = []
    for k, (v, g) in enumerate(zip((v0, v1, v2, v3), (g0, g1, g2, g3))):
        rows = slice(k * q, (k + 1) * q)
        total = keep[rows, :] + got[rows, :]
        g[0:q, :] = total
        g[q:, :] = beta_sums
        raws.append(total / beta - beta * v[...])
    sums[...] = square_row(jnp.concatenate(raws, axis=1), z, sums.shape[1])


def right_norm(docs_total, keep, got, beta_core, quarters):
    q, rows = quarters[0].shape
    out = pl.pallas_call(
        functools.partial(right_norm_kernel, docs_total),
        out_shape=[f32(q + 8, rows)] * 4 + [f32(8, 4 * q)],
        scratch_shapes=[pltpu.VMEM((4 * q, 128), jnp.float32)],
        compiler_params=params(8),
        cost_estimate=cost(rows * q * 64, rows * q * 100),
        name="right_norm",
    )(keep, got, beta_core, *quarters)
    return out[:4], out[4]


def beta_of(pieces, q, docs_total):
    squares = [g[q : q + 1, :] for g in pieces]
    return jnp.sqrt(((squares[0] + squares[1]) + (squares[2] + squares[3])) / docs_total + epsilon)


def finish_kernel(docs_total, feat_total, g0, g1, g2, g3, a0, a1, a2, a3, right, search, phibar, rhobar,
                  right_out, search_out, alpha_out, phibar_out, rhobar_out, turned):
    _, z, _ = coords()
    q = turned.shape[1]
    for k, g in enumerate((g0, g1, g2, g3)):
        turned[z ^ k] = g[0:q, :]
    got = turned[...].reshape(-1, turned.shape[2]).T
    squares = (a0[0:1, :] + a1[0:1, :]) + (a2[0:1, :] + a3[0:1, :])
    alpha = jnp.sqrt(squares / feat_total + epsilon)
    beta = beta_of((g0, g1, g2, g3), q, docs_total)
    rho = jnp.sqrt(rhobar[...] * rhobar[...] + beta * beta)
    cosine = rhobar[...] / rho
    sine = beta / rho
    theta = sine * alpha
    rhobar_out[...] = -cosine * alpha
    phibar_out[...] = sine * phibar[...]
    alpha_out[...] = alpha
    following = (got / beta - beta * right[...]) / alpha
    right_out[...] = following
    search_out[...] = following - (theta / rho) * search[...]


def finish(docs_total, feat_total, pieces, alphas, right, search, phibar, rhobar):
    rows, cols = right.shape
    return pl.pallas_call(
        functools.partial(finish_kernel, docs_total, feat_total),
        out_shape=[f32(rows, cols)] * 2 + [f32(1, cols)] * 3,
        scratch_shapes=[pltpu.VMEM((4, cols // 4, rows), jnp.float32)],
        compiler_params=params(8),
        cost_estimate=cost(rows * cols * 16, rows * cols * 20),
        name="finish",
    )(*pieces, *alphas, right, search, phibar, rhobar)


def left_out_kernel(docs_total, l0, l1, l2, l3, g0, g1, g2, g3, search, solution, phibar, rhobar, left_out, solution_out, turned):
    _, z, _ = coords()
    q, docs = turned.shape[1:]
    beta = beta_of((g0, g1, g2, g3), q, docs_total)
    for k, piece in enumerate((l0, l1, l2, l3)):
        turned[z ^ k] = piece[...]
    left_out[...] = turned[...].reshape(-1, docs).T / beta
    rho = jnp.sqrt(rhobar[...] * rhobar[...] + beta * beta)
    phi = rhobar[...] / rho * phibar[...]
    solution_out[...] = solution[...] + (phi / rho) * search[...]


def left_out(docs_total, lefts, pieces, search, solution, phibar, rhobar):
    q, docs = lefts[0].shape
    return pl.pallas_call(
        functools.partial(left_out_kernel, docs_total),
        out_shape=[f32(docs, 4 * q), f32(*solution.shape)],
        scratch_shapes=[pltpu.VMEM((4, q, docs), jnp.float32)],
        compiler_params=params(8),
        cost_estimate=cost(docs * q * 16, docs * q * 60),
        name="left_out",
    )(*lefts, *pieces, search, solution, phibar, rhobar)


def swap(value, mask):
    return lax.ppermute(value, AXES, [(i, i ^ mask) for i in range(32)])


def along_z(values):
    return [values[0]] + [swap(values[k], k << Z_SHIFT) for k in (1, 2, 3)]


def after(value, *earlier):
    return lax.optimization_barrier((value, *earlier))[0]


def by_columns(
    col_ids, col_vals, left_vec, right_vec, search_dir, solution_vec, alpha_prev, phibar, rhobar
):
    docs_total = left_vec.shape[0] * 16
    feat_total = right_vec.shape[0] * 32
    alpha_row, phibar_row, rhobar_row = (v.reshape(1, -1) for v in (alpha_prev, phibar, rhobar))

    mine = quarters_of(right_vec, "right_quarters")
    quarters = along_z(mine)
    ids, vals = col_ids.astype(jnp.float32), col_vals.astype(jnp.float32)
    entries = along_z([jnp.concatenate([ids.reshape(-1, 256), vals.reshape(-1, 256)], axis=0)] * 4)
    own = jnp.stack(quarters)
    own_x = swap(own, X_BIT)
    own_peer = swap(own, CORE_BIT)
    lefts = along_z(quarters_of(after(left_vec, own), "left_quarters"))

    hi, lo = build(entries)
    total = forward_part(hi, lo, [own, own_peer], (0, 8))
    vecs = [own_x, swap(own_x, CORE_BIT)]
    product = [forward_half(hi, lo, vecs, total, (4, 12), half) for half in range(2)]
    other = [swap(p, Y_BIT) for p in product]

    l0, l1, both0, beta0 = left_raw(product[0], other[0], lefts[:2], alpha_row)
    partial = backward_part(hi, lo, both0, 0, 0, 16)
    l2, l3, both1, beta1 = left_raw(product[1], other[1], lefts[2:], alpha_row, beta0)
    far = swap(backward_part(hi, lo, both1, 1, 8, 8, partial, beta1), CORE_BIT)
    near = backward_part(hi, lo, both1, 1, 0, 8, partial)
    send, keep, beta_core = far_sums(near, far, beta1)
    got = swap(send, X_BIT)
    left_pieces = along_z([l0, after(l1, partial), after(l2, keep), after(l3, keep)])

    sent, alpha_part = right_norm(docs_total, keep, got, beta_core, quarters)
    pieces = along_z(sent)
    for mask in (CORE_BIT, X_BIT, Y_BIT):
        alpha_part = alpha_part + swap(alpha_part, mask)
    alphas = along_z([alpha_part] * 4)
    left_next, solution_next = left_out(
        docs_total, left_pieces, pieces, search_dir, solution_vec, phibar_row, rhobar_row
    )
    right_next, search_next, alpha_next, phibar_next, rhobar_next = finish(
        docs_total, feat_total, pieces, alphas, right_vec, search_dir, phibar_row, rhobar_row
    )
    return (
        left_next,
        right_next,
        search_next,
        solution_next,
        alpha_next.reshape(-1),
        phibar_next.reshape(-1),
        rhobar_next.reshape(-1),
    )


def forward(col_ids, col_vals, table):
    picked = table[col_ids]
    return jnp.sum(col_vals.astype(jnp.float32)[:, :, None] * picked, axis=1)


def backward(col_ids, col_vals, rows_in, width):
    terms = col_vals.astype(jnp.float32)[:, :, None] * rows_in[:, None, :]
    return jax.ops.segment_sum(
        terms.reshape(-1, rows_in.shape[1]), col_ids.reshape(-1), num_segments=width
    )


def by_blocks(
    col_ids, col_vals, left_vec, right_vec, search_dir, solution_vec, alpha_prev, phibar, rhobar
):
    n_feat = lax.axis_size("feat")
    n_doc = lax.axis_size("doc")
    docs_total = left_vec.shape[0] * n_doc
    feat_total = right_vec.shape[0] * n_doc * n_feat
    table = lax.all_gather(right_vec, "doc", axis=0, tiled=True)
    total = lax.psum(forward(col_ids, col_vals, table), "feat")
    left_raw = total - alpha_prev[None, :] * left_vec
    row_part = jnp.sum(left_raw * left_raw, axis=0)
    beta_norm = jnp.sqrt(lax.psum(row_part, "doc") / docs_total + epsilon)
    left_next = left_raw / beta_norm[None, :]
    feature_part = lax.psum_scatter(
        backward(col_ids, col_vals, left_next, table.shape[0]), "doc", scatter_dimension=0, tiled=True
    )
    right_raw = feature_part - beta_norm[None, :] * right_vec
    squares = lax.psum(jnp.sum(right_raw * right_raw, axis=0), AXES)
    alpha_next = jnp.sqrt(squares / feat_total + epsilon)
    right_next = right_raw / alpha_next[None, :]
    rho_val = jnp.sqrt(rhobar * rhobar + beta_norm * beta_norm)
    cosine = rhobar / rho_val
    sine_val = beta_norm / rho_val
    theta_val = sine_val * alpha_next
    phi_val = cosine * phibar
    solution_next = solution_vec + (phi_val / rho_val)[None, :] * search_dir
    search_next = right_next - (theta_val / rho_val)[None, :] * search_dir
    return (
        left_next,
        right_next,
        search_next,
        solution_next,
        alpha_next,
        sine_val * phibar,
        -cosine * alpha_next,
    )


def solution(mesh):
    small = mesh.shape["doc"] == 16 and mesh.shape["feat"] == 2
    rows = P(("feat", "doc"), None)
    return jax.shard_map(
        by_columns if small else by_blocks,
        mesh=mesh,
        in_specs=(P("doc", "feat"), P("doc", "feat"), P("doc", None), rows, rows, rows, P(), P(), P()),
        out_specs=(P("doc", None), rows, rows, rows, P(), P(), P()),
        check_vma=False,
    )
```

time: 103 us -> 104 us (level)
  waiting for transfers between devices: 23.9 us -> 39.9 us
  starting transfers between devices: 44.5 us -> 31.5 us
  Pallas kernels: 29.2 us -> 27.2 us
    ppermute x35 -> x28, waiting for transfers between devices: 23.9 us -> 39.9 us  [swap(): return lax.ppermute(value, AXES, [(i, i ^ mask) for i in range(32)])]
    ppermute x35 -> x28, starting transfers between devices: 44.5 us -> 31.5 us  [swap(): return lax.ppermute(value, AXES, [(i, i ^ mask) for i in range(32)])]
    pallas_call x10 -> x11, Pallas kernels: 16.9 us -> 15.2 us  [the longest x3 4.86 us: backward_part(): pl.pallas_call(functools.partial(backward_kernel, half, first, blocks, tu...]
  transfers between devices with their start and end apart: 35 -> 28, of which waited for: 9 -> 12; matrix products, arithmetic and copies ran while one was open for 0% -> 2% of each run, Pallas kernels for 21% -> 23%
where the time goes in v3:
time: 104 us
  waiting for transfers between devices  39.9 us (38%)
  starting transfers between devices  31.5 us (30%)
  Pallas kernels  27.2 us (26%)
  local copies, waits for them, and re-layouts  3.28 us (3%)
    ppermute x28, waiting for transfers between devices, swap(): return lax.ppermute(value, AXES, [(i, i ^ mask) for i in range(32)])  39.9 us
    ppermute x28, starting transfers between devices, swap(): return lax.ppermute(value, AXES, [(i, i ^ mask) for i in range(32)])  31.5 us
    pallas_call x1, Pallas kernels, build(): pl.pallas_call(build_kernel, in_specs=[whole()] * 4, out_specs=[whole()]...  9.64 us
    pallas_call x3, Pallas kernels, backward_part(): pl.pallas_call(functools.partial(backward_kernel, half, first, blocks, tu...  4.86 us
    pallas_call x2, Pallas kernels, forward_half(): pl.pallas_call(functools.partial(forward_half_kernel, half, blocks), in_s...  4.77 us
    pallas_call x1, Pallas kernels, forward_part(): pl.pallas_call(functools.partial(forward_kernel, blocks), in_specs=[whole...  4.47 us
  transfers between devices with their start and end apart: 28, of which 12 were waited for; matrix products, arithmetic and copies ran while one was open for 2% of the time, Pallas kernels for 23%

profile of v3, /device:TPU:0, one launch (start us, length us, event | category | flops | bytes accessed | tf_op | source)
XLA Modules:
  0.0 103.7 jit_solution(10997367257843807762)
XLA Ops:
  0.6 0.9 copy-done
  1.7 3.1 %collective-permute-start.3 = (f32[64,256]{1,0:T(8,128)S(1)}, f32[64,256]{1,0:T(8,128)S(1)}, u32[]{:S(2)}, u32[]{:S(2)}) collective-permute-start(f32[64,256]{1,0:T(8,128)S(1)} %get-tuple-element.47), channel_id=1, source_target_pairs={{0,8},{1,9},{2,10},{3,11},{4,12},{5,13},{6,14},{7,15},{8,0},{9,1},... | collective-permute-start | bytes 196616 | tf_op jit(solution)/shard_map/ppermute | solution.py:375
  4.8 2.6 %collective-permute-start.4 = (f32[64,256]{1,0:T(8,128)S(1)}, f32[64,256]{1,0:T(8,128)S(1)}, u32[]{:S(2)}, u32[]{:S(2)}) collective-permute-start(f32[64,256]{1,0:T(8,128)S(1)} %get-tuple-element.48), channel_id=1, source_target_pairs={{0,16},{1,17},{2,18},{3,19},{4,20},{5,21},{6,22},{7,23},{8,24},{9,... | collective-permute-start | bytes 196616 | tf_op jit(solution)/shard_map/ppermute | solution.py:375
  7.4 0.8 convert_element_type.4
  8.5 0.8 copy.19
  9.5 3.9 %collective-permute-start.2 = (f32[64,256]{1,0:T(8,128)S(1)}, f32[64,256]{1,0:T(8,128)S(1)}, u32[]{:S(2)}, u32[]{:S(2)}) collective-permute-start(f32[64,256]{1,0:T(8,128)S(1)} %constant_dynamic-update-slice_fusion.e0), channel_id=1, source_target_pairs={{0,24},{1,25},{2,26},{3,27},{4,28},{5,29},{6,30},{7,31},{8,16},{9,... | collective-permute-start | bytes 196616 | tf_op jit(solution)/shard_map/ppermute | solution.py:375
  13.4 0.6 collective-permute-start
  14.1 1.7 %collective-permute-start.6 = (f32[4,64,256]{2,1,0:T(8,128)S(1)}, f32[4,64,256]{2,1,0:T(8,128)S(1)}, u32[]{:S(2)}, u32[]{:S(2)}) collective-permute-start(f32[4,64,256]{2,1,0:T(8,128)S(1)} %pad_maximum_fusion.v0), channel_id=1, source_target_pairs={{0,4},{1,5},{2,6},{3,7},{4,0},{5,1},{6,2},{7,3},{8,12},{9,13},{10,... | collective-permute-start | bytes 786440 | tf_op jit(solution)/shard_map/ppermute | solution.py:375
  15.8 1.0 %copy-done.3 = f32[512,256]{1,0:T(8,128)S(1)} copy-done((f32[512,256]{1,0:T(8,128)S(1)}, f32[512,256]{1,0:T(8,128)}, u32[]{:S(2)}) %copy-start.3) | copy-done | bytes 524312
  16.9 0.3 left_quarters.1
  17.1 3.6 %collective-permute-start.10 = (f32[64,512]{1,0:T(8,128)S(1)}, f32[64,512]{1,0:T(8,128)S(1)}, u32[]{:S(2)}, u32[]{:S(2)}) collective-permute-start(f32[64,512]{1,0:T(8,128)S(1)} %get-tuple-element.52), channel_id=1, source_target_pairs={{0,8},{1,9},{2,10},{3,11},{4,12},{5,13},{6,14},{7,15},{8,0},{9,1},... | collective-permute-start | bytes 393224 | tf_op jit(solution)/shard_map/ppermute | solution.py:375
  20.7 0.6 collective-permute-start.13
  21.4 1.8 %collective-permute-start.14 = (f32[64,512]{1,0:T(8,128)S(1)}, f32[64,512]{1,0:T(8,128)S(1)}, u32[]{:S(2)}, u32[]{:S(2)}) collective-permute-start(f32[64,512]{1,0:T(8,128)S(1)} %get-tuple-element.58), channel_id=1, source_target_pairs={{0,24},{1,25},{2,26},{3,27},{4,28},{5,29},{6,30},{7,31},{8,16},{9,... | collective-permute-start | bytes 393224 | tf_op jit(solution)/shard_map/ppermute | solution.py:375
  23.2 9.6 %dense_rows.1 = (bf16[16,2048,256]{2,1,0:T(8,128)(2,1)S(1)}, bf16[16,2048,256]{2,1,0:T(8,128)(2,1)S(1)}) custom-call(f32[64,256]{1,0:T(8,128)S(1)} %constant_dynamic-update-slice_fusion.e0, f32[64,256]{1,0:T(8,128)S(1)} %collective-permute-done.e1, f32[64,256]{1,0:T(8,128)S(1)} %collective-permute-done.1.e2, f32[64,256]{1,0:T(8,128)S(1)} %collective-permute-done.2.e3), custom_call_target="tpu_custom_call" | custom-call | flops 4294967296 | bytes 33554432 | tf_op jit(solution)/shard_map/dense_rows/pallas_call | solution.py:101
  32.9 4.5 %forward_part.1.before = f32[2048,128]{1,0:T(8,128)S(1)} custom-call(bf16[16,2048,256]{2,1,0:T(8,128)(2,1)S(1)} %get-tuple-element.44.hi_ref, bf16[16,2048,256]{2,1,0:T(8,128)(2,1)S(1)} %get-tuple-element.45.lo_ref, f32[4,64,256]{2,1,0:T(8,128)S(1)} %pad_maximum_fusion.v0, f32[4,64,256]{2,1,0:T(8,128)S(1)} %collective-permute-done.8.v1), custom_call_target="tpu_custom_call" | custom-call | flops 8589934592 | bytes 16777216 | tf_op jit(solution)/shard_map/forward_part/pallas_call | solution.py:147
  37.4 2.4 %forward_half.2.mine = f32[64,1024]{1,0:T(8,128)S(1)} custom-call(bf16[16,2048,256]{2,1,0:T(8,128)(2,1)S(1)} %get-tuple-element.44.hi_ref, bf16[16,2048,256]{2,1,0:T(8,128)(2,1)S(1)} %get-tuple-element.45.lo_ref, f32[4,64,256]{2,1,0:T(8,128)S(1)} %collective-permute-done.6.v0, f32[4,64,256]{2,1,0:T(8,128)S(1)} %collective-permute-done.7.v1, ...), custom_call_target="tpu_custom_call" | custom-call | flops 4294967296 | bytes 8388608 | tf_op jit(solution)/shard_map/forward_half/pallas_call | solution.py:172
  39.8 1.6 %collective-permute-start.9 = (f32[64,1024]{1,0:T(8,128)S(1)}, f32[64,1024]{1,0:T(8,128)S(1)}, u32[]{:S(2)}, u32[]{:S(2)}) collective-permute-start(f32[64,1024]{1,0:T(8,128)S(1)} %forward_half.2.mine), channel_id=1, source_target_pairs={{0,1},{1,0},{2,3},{3,2},{4,5},{5,4},{6,7},{7,6},{8,9},{9,8},{10,11... | collective-permute-start | bytes 786440 | tf_op jit(solution)/shard_map/ppermute | solution.py:375
  41.4 2.4 %forward_half.3.mine = f32[64,1024]{1,0:T(8,128)S(1)} custom-call(bf16[16,2048,256]{2,1,0:T(8,128)(2,1)S(1)} %get-tuple-element.44.hi_ref, bf16[16,2048,256]{2,1,0:T(8,128)(2,1)S(1)} %get-tuple-element.45.lo_ref, f32[4,64,256]{2,1,0:T(8,128)S(1)} %collective-permute-done.6.v0, f32[4,64,256]{2,1,0:T(8,128)S(1)} %collective-permute-done.7.v1, ...), custom_call_target="tpu_custom_call" | custom-call | flops 4294967296 | bytes 8388608 | tf_op jit(solution)/shard_map/forward_half/pallas_call | solution.py:172
  43.8 0.6 collective-permute-start.12
  44.4 4.6 %collective-permute-done.9.other = f32[64,1024]{1,0:T(8,128)S(1)} collective-permute-done((f32[64,1024]{1,0:T(8,128)S(1)}, f32[64,1024]{1,0:T(8,128)S(1)}, u32[]{:S(2)}, u32[]{:S(2)}) %collective-permute-start.9) | collective-permute-done | bytes 262176 | tf_op jit(solution)/shard_map/ppermute | solution.py:375
  49.0 0.3 left_raw.2
  49.3 2.3 %backward_part.3.refs_0_ = f32[1024,256]{1,0:T(8,128)S(1)} custom-call(bf16[16,2048,256]{2,1,0:T(8,128)(2,1)S(1)} %get-tuple-element.44.hi_ref, bf16[16,2048,256]{2,1,0:T(8,128)(2,1)S(1)} %get-tuple-element.45.lo_ref, bf16[128,1024]{1,0:T(8,128)(2,1)S(1)} %get-tuple-element.55.both_ref), custom_call_target="tpu_custom_call" | custom-call | flops 8589934592 | bytes 16777216 | tf_op jit(solution)/shard_map/backward_part/pallas_call | solution.py:252
  51.7 2.5 %collective-permute-done.12.other = f32[64,1024]{1,0:T(8,128)S(1)} collective-permute-done((f32[64,1024]{1,0:T(8,128)S(1)}, f32[64,1024]{1,0:T(8,128)S(1)}, u32[]{:S(2)}, u32[]{:S(2)}) %collective-permute-start.12) | collective-permute-done | bytes 262176 | tf_op jit(solution)/shard_map/ppermute | solution.py:375
  54.2 0.3 left_raw.3
  54.5 1.3 %backward_part.5 = f32[520,256]{1,0:T(8,128)S(1)} custom-call(bf16[16,2048,256]{2,1,0:T(8,128)(2,1)S(1)} %get-tuple-element.44.hi_ref, bf16[16,2048,256]{2,1,0:T(8,128)(2,1)S(1)} %get-tuple-element.45.lo_ref, bf16[128,1024]{1,0:T(8,128)(2,1)S(1)} %get-tuple-element.61.both_ref, f32[1024,256]{1,0:T(8,128)S(1)} %backward_part.3.refs_0_, ...), custom_call_target="tpu_custom_call" | custom-call | flops 4294967296 | bytes 8388608 | tf_op jit(solution)/shard_map/backward_part/pallas_call | solution.py:252
  56.0 1.3 %backward_part.4.near = f32[512,256]{1,0:T(8,128)S(1)} custom-call(bf16[16,2048,256]{2,1,0:T(8,128)(2,1)S(1)} %get-tuple-element.44.hi_ref, bf16[16,2048,256]{2,1,0:T(8,128)(2,1)S(1)} %get-tuple-element.45.lo_ref, bf16[128,1024]{1,0:T(8,128)(2,1)S(1)} %get-tuple-element.61.both_ref, f32[1024,256]{1,0:T(8,128)S(1)} %backward_part.3.refs_0_), custom_call_target="tpu_custom_call" | custom-call | flops 4294967296 | bytes 8388608 | tf_op jit(solution)/shard_map/backward_part/pallas_call | solution.py:252
  57.2 0.6 collective-permute-done.15.far
  57.9 0.6 collective-permute-start.18
  58.5 8.0 %collective-permute-done.18.got = f32[264,256]{1,0:T(8,128)S(1)} collective-permute-done((f32[264,256]{1,0:T(8,128)S(1)}, f32[264,256]{1,0:T(8,128)S(1)}, u32[]{:S(2)}, u32[]{:S(2)}) %collective-permute-start.18) | collective-permute-done | bytes 270368 | tf_op jit(solution)/shard_map/ppermute | solution.py:375
  66.5 0.3 right_norm.1
  66.8 1.1 %collective-permute-start.19 = (f32[72,256]{1,0:T(8,128)S(1)}, f32[72,256]{1,0:T(8,128)S(1)}, u32[]{:S(2)}, u32[]{:S(2)}) collective-permute-start(f32[72,256]{1,0:T(8,128)S(1)} %get-tuple-element.70), channel_id=1, source_target_pairs={{0,8},{1,9},{2,10},{3,11},{4,12},{5,13},{6,14},{7,15},{8,0},{9,1},... | collective-permute-start | bytes 221192 | tf_op jit(solution)/shard_map/ppermute | solution.py:375
  68.0 1.0 collective-permute-start.11
  68.9 1.0 collective-permute-start.16
  70.0 2.4 %collective-permute-start.17 = (f32[64,512]{1,0:T(8,128)S(1)}, f32[64,512]{1,0:T(8,128)S(1)}, u32[]{:S(2)}, u32[]{:S(2)}) collective-permute-start(f32[64,512]{1,0:T(8,128)S(1)} %get-tuple-element.66), channel_id=1, source_target_pairs={{0,24},{1,25},{2,26},{3,27},{4,28},{5,29},{6,30},{7,31},{8,16},{9,... | collective-permute-start | bytes 393224 | tf_op jit(solution)/shard_map/ppermute | solution.py:375
  72.4 1.2 %collective-permute-done.22 = f32[8,256]{1,0:T(8,128)S(1)} collective-permute-done((f32[8,256]{1,0:T(8,128)S(1)}, f32[8,256]{1,0:T(8,128)S(1)}, u32[]{:S(2)}, u32[]{:S(2)}) %collective-permute-start.22) | collective-permute-done | bytes 8224 | tf_op jit(solution)/shard_map/ppermute | solution.py:375
  73.5 0.5 collective-permute-start.23
  74.0 3.1 %collective-permute-done.23 = f32[8,256]{1,0:T(8,128)S(1)} collective-permute-done((f32[8,256]{1,0:T(8,128)S(1)}, f32[8,256]{1,0:T(8,128)S(1)}, u32[]{:S(2)}, u32[]{:S(2)}) %collective-permute-start.23) | collective-permute-done | bytes 8224 | tf_op jit(solution)/shard_map/ppermute | solution.py:375
  77.2 1.5 %collective-permute-start.24 = (f32[8,256]{1,0:T(8,128)S(1)}, f32[8,256]{1,0:T(8,128)S(1)}, u32[]{:S(2)}, u32[]{:S(2)}) collective-permute-start(f32[8,256]{1,0:T(8,128)S(1)} %add.10), channel_id=1, source_target_pairs={{0,1},{1,0},{2,3},{3,2},{4,5},{5,4},{6,7},{7,6},{8,9},{9,8},{10,11... | collective-permute-start | bytes 24584 | tf_op jit(solution)/shard_map/ppermute | solution.py:375
  78.7 2.1 %collective-permute-done.24 = f32[8,256]{1,0:T(8,128)S(1)} collective-permute-done((f32[8,256]{1,0:T(8,128)S(1)}, f32[8,256]{1,0:T(8,128)S(1)}, u32[]{:S(2)}, u32[]{:S(2)}) %collective-permute-start.24) | collective-permute-done | bytes 8224 | tf_op jit(solution)/shard_map/ppermute | solution.py:375
  80.8 1.4 %collective-permute-start.27 = (f32[8,256]{1,0:T(8,128)S(1)}, f32[8,256]{1,0:T(8,128)S(1)}, u32[]{:S(2)}, u32[]{:S(2)}) collective-permute-start(f32[8,256]{1,0:T(8,128)S(1)} %add.11.a0), channel_id=1, source_target_pairs={{0,24},{1,25},{2,26},{3,27},{4,28},{5,29},{6,30},{7,31},{8,16},{9,... | collective-permute-start | bytes 24584 | tf_op jit(solution)/shard_map/ppermute | solution.py:375
  82.3 4.0 %collective-permute-done.27.a3 = f32[8,256]{1,0:T(8,128)S(1)} collective-permute-done((f32[8,256]{1,0:T(8,128)S(1)}, f32[8,256]{1,0:T(8,128)S(1)}, u32[]{:S(2)}, u32[]{:S(2)}) %collective-permute-start.27) | collective-permute-done | bytes 8224 | tf_op jit(solution)/shard_map/ppermute | solution.py:375
  86.3 4.5 %collective-permute-done.26.a2 = f32[8,256]{1,0:T(8,128)S(1)} collective-permute-done((f32[8,256]{1,0:T(8,128)S(1)}, f32[8,256]{1,0:T(8,128)S(1)}, u32[]{:S(2)}, u32[]{:S(2)}) %collective-permute-start.26) | collective-permute-done | bytes 8224 | tf_op jit(solution)/shard_map/ppermute | solution.py:375
  90.9 4.4 %collective-permute-done.25.a1 = f32[8,256]{1,0:T(8,128)S(1)} collective-permute-done((f32[8,256]{1,0:T(8,128)S(1)}, f32[8,256]{1,0:T(8,128)S(1)}, u32[]{:S(2)}, u32[]{:S(2)}) %collective-permute-start.25) | collective-permute-done | bytes 8224 | tf_op jit(solution)/shard_map/ppermute | solution.py:375
  95.3 1.6 %collective-permute-start.21 = (f32[72,256]{1,0:T(8,128)S(1)}, f32[72,256]{1,0:T(8,128)S(1)}, u32[]{:S(2)}, u32[]{:S(2)}) collective-permute-start(f32[72,256]{1,0:T(8,128)S(1)} %get-tuple-element.72), channel_id=1, source_target_pairs={{0,24},{1,25},{2,26},{3,27},{4,28},{5,29},{6,30},{7,31},{8,16},{9,... | collective-permute-start | bytes 221192 | tf_op jit(solution)/shard_map/ppermute | solution.py:375
  96.9 3.7 %collective-permute-done.20.g2 = f32[72,256]{1,0:T(8,128)S(1)} collective-permute-done((f32[72,256]{1,0:T(8,128)S(1)}, f32[72,256]{1,0:T(8,128)S(1)}, u32[]{:S(2)}, u32[]{:S(2)}) %collective-permute-start.20) | collective-permute-done | bytes 73760 | tf_op jit(solution)/shard_map/ppermute | solution.py:375
  100.5 1.0 collective-permute-done.21.g3
  101.6 1.0 finish.1
  102.6 1.1 %left_out.1 = (f32[512,256]{1,0:T(8,128)}, f32[256,256]{1,0:T(8,128)}) custom-call(f32[64,512]{1,0:T(8,128)S(1)} %get-tuple-element.53.l0, f32[64,512]{1,0:T(8,128)S(1)} %collective-permute-done.11.l1, f32[64,512]{1,0:T(8,128)S(1)} %collective-permute-done.16.l2, f32[64,512]{1,0:T(8,128)S(1)} %collective-permute-done.17.l3, ...), custom_call_target="tpu_custom_call" | custom-call | flops 524288 | bytes 1966080 | tf_op jit(solution)/shard_map/left_out/pallas_call | solution.py:364
  (50 shorter events, 1.0 us)
Async XLA Ops:
  0.6 1.0 copy-start
  1.7 11.6 %collective-permute-start.3 = (f32[64,256]{1,0:T(8,128)S(1)}, f32[64,256]{1,0:T(8,128)S(1)}, u32[]{:S(2)}, u32[]{:S(2)}) collective-permute-start(f32[64,256]{1,0:T(8,128)S(1)} %get-tuple-element.47), channel_id=1, source_target_pairs={{0,8},{1,9},{2,10},{3,11},{4,12},{5,13},{6,14},{7,15},{8,0},{9,1},... | collective-permute-start | bytes 196616 | tf_op jit(solution)/shard_map/ppermute | solution.py:375
  4.8 9.2 %collective-permute-start.4 = (f32[64,256]{1,0:T(8,128)S(1)}, f32[64,256]{1,0:T(8,128)S(1)}, u32[]{:S(2)}, u32[]{:S(2)}) collective-permute-start(f32[64,256]{1,0:T(8,128)S(1)} %get-tuple-element.48), channel_id=1, source_target_pairs={{0,16},{1,17},{2,18},{3,19},{4,20},{5,21},{6,22},{7,23},{8,24},{9,... | collective-permute-start | bytes 196616 | tf_op jit(solution)/shard_map/ppermute | solution.py:375
  7.4 6.6 %collective-permute-start.5 = (f32[64,256]{1,0:T(8,128)S(1)}, f32[64,256]{1,0:T(8,128)S(1)}, u32[]{:S(2)}, u32[]{:S(2)}) collective-permute-start(f32[64,256]{1,0:T(8,128)S(1)} %get-tuple-element.49), channel_id=1, source_target_pairs={{0,24},{1,25},{2,26},{3,27},{4,28},{5,29},{6,30},{7,31},{8,16},{9,... | collective-permute-start | bytes 196616 | tf_op jit(solution)/shard_map/ppermute | solution.py:375
  9.5 7.6 %collective-permute-start.2 = (f32[64,256]{1,0:T(8,128)S(1)}, f32[64,256]{1,0:T(8,128)S(1)}, u32[]{:S(2)}, u32[]{:S(2)}) collective-permute-start(f32[64,256]{1,0:T(8,128)S(1)} %constant_dynamic-update-slice_fusion.e0), channel_id=1, source_target_pairs={{0,24},{1,25},{2,26},{3,27},{4,28},{5,29},{6,30},{7,31},{8,16},{9,... | collective-permute-start | bytes 196616 | tf_op jit(solution)/shard_map/ppermute | solution.py:375
  13.4 7.4 %collective-permute-start.1 = (f32[64,256]{1,0:T(8,128)S(1)}, f32[64,256]{1,0:T(8,128)S(1)}, u32[]{:S(2)}, u32[]{:S(2)}) collective-permute-start(f32[64,256]{1,0:T(8,128)S(1)} %constant_dynamic-update-slice_fusion.e0), channel_id=1, source_target_pairs={{0,16},{1,17},{2,18},{3,19},{4,20},{5,21},{6,22},{7,23},{8,24},{9,... | collective-permute-start | bytes 196616 | tf_op jit(solution)/shard_map/ppermute | solution.py:375
  13.4 8.0 %collective-permute-start = (f32[64,256]{1,0:T(8,128)S(1)}, f32[64,256]{1,0:T(8,128)S(1)}, u32[]{:S(2)}, u32[]{:S(2)}) collective-permute-start(f32[64,256]{1,0:T(8,128)S(1)} %constant_dynamic-update-slice_fusion.e0), channel_id=1, source_target_pairs={{0,8},{1,9},{2,10},{3,11},{4,12},{5,13},{6,14},{7,15},{8,0},{9,1},... | collective-permute-start | bytes 196616 | tf_op jit(solution)/shard_map/ppermute | solution.py:375
  14.0 18.9 %collective-permute-start.8 = (f32[4,64,256]{2,1,0:T(8,128)S(1)}, f32[4,64,256]{2,1,0:T(8,128)S(1)}, u32[]{:S(2)}, u32[]{:S(2)}) collective-permute-start(f32[4,64,256]{2,1,0:T(8,128)S(1)} %pad_maximum_fusion.v0), channel_id=1, source_target_pairs={{0,2},{1,3},{2,0},{3,1},{4,6},{5,7},{6,4},{7,5},{8,10},{9,11},{10,... | collective-permute-start | bytes 786440 | tf_op jit(solution)/shard_map/ppermute | solution.py:375
  14.1 18.7 %collective-permute-start.6 = (f32[4,64,256]{2,1,0:T(8,128)S(1)}, f32[4,64,256]{2,1,0:T(8,128)S(1)}, u32[]{:S(2)}, u32[]{:S(2)}) collective-permute-start(f32[4,64,256]{2,1,0:T(8,128)S(1)} %pad_maximum_fusion.v0), channel_id=1, source_target_pairs={{0,4},{1,5},{2,6},{3,7},{4,0},{5,1},{6,2},{7,3},{8,12},{9,13},{10,... | collective-permute-start | bytes 786440 | tf_op jit(solution)/shard_map/ppermute | solution.py:375
  15.8 1.0 %copy-start.3 = (f32[512,256]{1,0:T(8,128)S(1)}, f32[512,256]{1,0:T(8,128)}, u32[]{:S(2)}) copy-start(f32[512,256]{1,0:T(8,128)} %ref.2) | copy-start | bytes 1572868
  17.1 27.3 %collective-permute-start.10 = (f32[64,512]{1,0:T(8,128)S(1)}, f32[64,512]{1,0:T(8,128)S(1)}, u32[]{:S(2)}, u32[]{:S(2)}) collective-permute-start(f32[64,512]{1,0:T(8,128)S(1)} %get-tuple-element.52), channel_id=1, source_target_pairs={{0,8},{1,9},{2,10},{3,11},{4,12},{5,13},{6,14},{7,15},{8,0},{9,1},... | collective-permute-start | bytes 393224 | tf_op jit(solution)/shard_map/ppermute | solution.py:375
  20.7 30.9 %collective-permute-start.13 = (f32[64,512]{1,0:T(8,128)S(1)}, f32[64,512]{1,0:T(8,128)S(1)}, u32[]{:S(2)}, u32[]{:S(2)}) collective-permute-start(f32[64,512]{1,0:T(8,128)S(1)} %get-tuple-element.57), channel_id=1, source_target_pairs={{0,16},{1,17},{2,18},{3,19},{4,20},{5,21},{6,22},{7,23},{8,24},{9,... | collective-permute-start | bytes 393224 | tf_op jit(solution)/shard_map/ppermute | solution.py:375
  21.4 30.3 %collective-permute-start.14 = (f32[64,512]{1,0:T(8,128)S(1)}, f32[64,512]{1,0:T(8,128)S(1)}, u32[]{:S(2)}, u32[]{:S(2)}) collective-permute-start(f32[64,512]{1,0:T(8,128)S(1)} %get-tuple-element.58), channel_id=1, source_target_pairs={{0,24},{1,25},{2,26},{3,27},{4,28},{5,29},{6,30},{7,31},{8,16},{9,... | collective-permute-start | bytes 393224 | tf_op jit(solution)/shard_map/ppermute | solution.py:375
  32.9 4.6 %collective-permute-start.7 = (f32[4,64,256]{2,1,0:T(8,128)S(1)}, f32[4,64,256]{2,1,0:T(8,128)S(1)}, u32[]{:S(2)}, u32[]{:S(2)}) collective-permute-start(f32[4,64,256]{2,1,0:T(8,128)S(1)} %collective-permute-done.6.v0), channel_id=1, source_target_pairs={{0,2},{1,3},{2,0},{3,1},{4,6},{5,7},{6,4},{7,5},{8,10},{9,11},{10,... | collective-permute-start | bytes 786440 | tf_op jit(solution)/shard_map/ppermute | solution.py:375
  39.8 9.2 %copy-start.5 = (f32[256]{0:T(256)S(1)}, f32[256]{0:T(256)}, u32[]{:S(2)}) copy-start(f32[256]{0:T(256)} %param.15) | copy-start | bytes 3076
  39.8 9.2 %collective-permute-start.9 = (f32[64,1024]{1,0:T(8,128)S(1)}, f32[64,1024]{1,0:T(8,128)S(1)}, u32[]{:S(2)}, u32[]{:S(2)}) collective-permute-start(f32[64,1024]{1,0:T(8,128)S(1)} %forward_half.2.mine), channel_id=1, source_target_pairs={{0,1},{1,0},{2,3},{3,2},{4,5},{5,4},{6,7},{7,6},{8,9},{9,8},{10,11... | collective-permute-start | bytes 786440 | tf_op jit(solution)/shard_map/ppermute | solution.py:375
  43.8 10.4 %collective-permute-start.12 = (f32[64,1024]{1,0:T(8,128)S(1)}, f32[64,1024]{1,0:T(8,128)S(1)}, u32[]{:S(2)}, u32[]{:S(2)}) collective-permute-start(f32[64,1024]{1,0:T(8,128)S(1)} %forward_half.3.mine), channel_id=1, source_target_pairs={{0,1},{1,0},{2,3},{3,2},{4,5},{5,4},{6,7},{7,6},{8,9},{9,8},{10,11... | collective-permute-start | bytes 786440 | tf_op jit(solution)/shard_map/ppermute | solution.py:375
  55.8 45.7 %copy-start.1 = (f32[256,256]{1,0:T(8,128)S(1)}, f32[256,256]{1,0:T(8,128)}, u32[]{:S(2)}) copy-start(f32[256,256]{1,0:T(8,128)} %right.1) | copy-start | bytes 786436
  55.8 45.7 %copy-start.2 = (f32[256,256]{1,0:T(8,128)S(1)}, f32[256,256]{1,0:T(8,128)}, u32[]{:S(2)}) copy-start(f32[256,256]{1,0:T(8,128)} %search.3) | copy-start | bytes 786436
  55.8 45.7 %copy-start.6 = (f32[256]{0:T(256)S(1)}, f32[256]{0:T(256)}, u32[]{:S(2)}) copy-start(f32[256]{0:T(256)} %param.16) | copy-start | bytes 3076
  55.9 45.7 %copy-start.7 = (f32[256]{0:T(256)S(1)}, f32[256]{0:T(256)}, u32[]{:S(2)}) copy-start(f32[256]{0:T(256)} %param.17) | copy-start | bytes 3076
  55.9 46.7 %copy-start.4 = (f32[256,256]{1,0:T(8,128)S(1)}, f32[256,256]{1,0:T(8,128)}, u32[]{:S(2)}) copy-start(f32[256,256]{1,0:T(8,128)} %solution.1) | copy-start | bytes 786436
  55.9 2.0 %collective-permute-start.15 = (f32[520,256]{1,0:T(8,128)S(1)}, f32[520,256]{1,0:T(8,128)S(1)}, u32[]{:S(2)}, u32[]{:S(2)}) collective-permute-start(f32[520,256]{1,0:T(8,128)S(1)} %backward_part.5), channel_id=1, source_target_pairs={{0,2},{1,3},{2,0},{3,1},{4,6},{5,7},{6,4},{7,5},{8,10},{9,11},{10,... | collective-permute-start | bytes 1597448 | tf_op jit(solution)/shard_map/ppermute | solution.py:375
  57.9 8.6 %collective-permute-start.18 = (f32[264,256]{1,0:T(8,128)S(1)}, f32[264,256]{1,0:T(8,128)S(1)}, u32[]{:S(2)}, u32[]{:S(2)}) collective-permute-start(f32[264,256]{1,0:T(8,128)S(1)} %get-tuple-element.67), channel_id=1, source_target_pairs={{0,4},{1,5},{2,6},{3,7},{4,0},{5,1},{6,2},{7,3},{8,12},{9,13},{10,... | collective-permute-start | bytes 811016 | tf_op jit(solution)/shard_map/ppermute | solution.py:375
  66.8 28.5 %collective-permute-start.19 = (f32[72,256]{1,0:T(8,128)S(1)}, f32[72,256]{1,0:T(8,128)S(1)}, u32[]{:S(2)}, u32[]{:S(2)}) collective-permute-start(f32[72,256]{1,0:T(8,128)S(1)} %get-tuple-element.70), channel_id=1, source_target_pairs={{0,8},{1,9},{2,10},{3,11},{4,12},{5,13},{6,14},{7,15},{8,0},{9,1},... | collective-permute-start | bytes 221192 | tf_op jit(solution)/shard_map/ppermute | solution.py:375
  68.0 34.6 %collective-permute-start.11 = (f32[64,512]{1,0:T(8,128)S(1)}, f32[64,512]{1,0:T(8,128)S(1)}, u32[]{:S(2)}, u32[]{:S(2)}) collective-permute-start(f32[64,512]{1,0:T(8,128)S(1)} %get-tuple-element.56), channel_id=1, source_target_pairs={{0,8},{1,9},{2,10},{3,11},{4,12},{5,13},{6,14},{7,15},{8,0},{9,1},... | collective-permute-start | bytes 393224 | tf_op jit(solution)/shard_map/ppermute | solution.py:375
  68.9 33.6 %collective-permute-start.16 = (f32[64,512]{1,0:T(8,128)S(1)}, f32[64,512]{1,0:T(8,128)S(1)}, u32[]{:S(2)}, u32[]{:S(2)}) collective-permute-start(f32[64,512]{1,0:T(8,128)S(1)} %get-tuple-element.64), channel_id=1, source_target_pairs={{0,16},{1,17},{2,18},{3,19},{4,20},{5,21},{6,22},{7,23},{8,24},{9,... | collective-permute-start | bytes 393224 | tf_op jit(solution)/shard_map/ppermute | solution.py:375
  70.0 32.6 %collective-permute-start.17 = (f32[64,512]{1,0:T(8,128)S(1)}, f32[64,512]{1,0:T(8,128)S(1)}, u32[]{:S(2)}, u32[]{:S(2)}) collective-permute-start(f32[64,512]{1,0:T(8,128)S(1)} %get-tuple-element.66), channel_id=1, source_target_pairs={{0,24},{1,25},{2,26},{3,27},{4,28},{5,29},{6,30},{7,31},{8,16},{9,... | collective-permute-start | bytes 393224 | tf_op jit(solution)/shard_map/ppermute | solution.py:375
  72.4 1.2 %collective-permute-start.22 = (f32[8,256]{1,0:T(8,128)S(1)}, f32[8,256]{1,0:T(8,128)S(1)}, u32[]{:S(2)}, u32[]{:S(2)}) collective-permute-start(f32[8,256]{1,0:T(8,128)S(1)} %get-tuple-element.74), channel_id=1, source_target_pairs={{0,2},{1,3},{2,0},{3,1},{4,6},{5,7},{6,4},{7,5},{8,10},{9,11},{10,... | collective-permute-start | bytes 24584 | tf_op jit(solution)/shard_map/ppermute | solution.py:375
  73.5 3.7 %collective-permute-start.23 = (f32[8,256]{1,0:T(8,128)S(1)}, f32[8,256]{1,0:T(8,128)S(1)}, u32[]{:S(2)}, u32[]{:S(2)}) collective-permute-start(f32[8,256]{1,0:T(8,128)S(1)} %add.9), channel_id=1, source_target_pairs={{0,4},{1,5},{2,6},{3,7},{4,0},{5,1},{6,2},{7,3},{8,12},{9,13},{10,... | collective-permute-start | bytes 24584 | tf_op jit(solution)/shard_map/ppermute | solution.py:375
  77.2 3.7 %collective-permute-start.24 = (f32[8,256]{1,0:T(8,128)S(1)}, f32[8,256]{1,0:T(8,128)S(1)}, u32[]{:S(2)}, u32[]{:S(2)}) collective-permute-start(f32[8,256]{1,0:T(8,128)S(1)} %add.10), channel_id=1, source_target_pairs={{0,1},{1,0},{2,3},{3,2},{4,5},{5,4},{6,7},{7,6},{8,9},{9,8},{10,11... | collective-permute-start | bytes 24584 | tf_op jit(solution)/shard_map/ppermute | solution.py:375
  80.8 5.4 %collective-permute-start.27 = (f32[8,256]{1,0:T(8,128)S(1)}, f32[8,256]{1,0:T(8,128)S(1)}, u32[]{:S(2)}, u32[]{:S(2)}) collective-permute-start(f32[8,256]{1,0:T(8,128)S(1)} %add.11.a0), channel_id=1, source_target_pairs={{0,24},{1,25},{2,26},{3,27},{4,28},{5,29},{6,30},{7,31},{8,16},{9,... | collective-permute-start | bytes 24584 | tf_op jit(solution)/shard_map/ppermute | solution.py:375
  86.3 4.5 %collective-permute-start.26 = (f32[8,256]{1,0:T(8,128)S(1)}, f32[8,256]{1,0:T(8,128)S(1)}, u32[]{:S(2)}, u32[]{:S(2)}) collective-permute-start(f32[8,256]{1,0:T(8,128)S(1)} %add.11.a0), channel_id=1, source_target_pairs={{0,16},{1,17},{2,18},{3,19},{4,20},{5,21},{6,22},{7,23},{8,24},{9,... | collective-permute-start | bytes 24584 | tf_op jit(solution)/shard_map/ppermute | solution.py:375
  90.8 4.4 %collective-permute-start.25 = (f32[8,256]{1,0:T(8,128)S(1)}, f32[8,256]{1,0:T(8,128)S(1)}, u32[]{:S(2)}, u32[]{:S(2)}) collective-permute-start(f32[8,256]{1,0:T(8,128)S(1)} %add.11.a0), channel_id=1, source_target_pairs={{0,8},{1,9},{2,10},{3,11},{4,12},{5,13},{6,14},{7,15},{8,0},{9,1},... | collective-permute-start | bytes 24584 | tf_op jit(solution)/shard_map/ppermute | solution.py:375
  95.3 5.3 %collective-permute-start.20 = (f32[72,256]{1,0:T(8,128)S(1)}, f32[72,256]{1,0:T(8,128)S(1)}, u32[]{:S(2)}, u32[]{:S(2)}) collective-permute-start(f32[72,256]{1,0:T(8,128)S(1)} %get-tuple-element.71), channel_id=1, source_target_pairs={{0,16},{1,17},{2,18},{3,19},{4,20},{5,21},{6,22},{7,23},{8,24},{9,... | collective-permute-start | bytes 221192 | tf_op jit(solution)/shard_map/ppermute | solution.py:375
  95.3 6.3 %collective-permute-start.21 = (f32[72,256]{1,0:T(8,128)S(1)}, f32[72,256]{1,0:T(8,128)S(1)}, u32[]{:S(2)}, u32[]{:S(2)}) collective-permute-start(f32[72,256]{1,0:T(8,128)S(1)} %get-tuple-element.72), channel_id=1, source_target_pairs={{0,24},{1,25},{2,26},{3,27},{4,28},{5,29},{6,30},{7,31},{8,16},{9,... | collective-permute-start | bytes 221192 | tf_op jit(solution)/shard_map/ppermute | solution.py:375

commit v4 on v3

--- a/solution.py
+++ b/solution.py
@@ -13,6 +13,7 @@
 
 
 Y_BIT, CORE_BIT, X_BIT, Z_SHIFT = 1, 2, 4, 3
+PLANES = [list(range(first, first + 8)) for first in range(0, 32, 8)]
 NT = (((1,), (1,)), ((), ()))
 
 
@@ -38,24 +39,43 @@
     return jax.ShapeDtypeStruct(shape, jnp.bfloat16)
 
 
-def quarters_kernel(ref, m0, m1, m2, m3, turned):
-    _, z, _ = coords()
-    turned[...] = ref[...].T.reshape(turned.shape)
-    for k, out in enumerate((m0, m1, m2, m3)):
-        out[...] = turned[z ^ k]
-
-
-def quarters_of(value, name):
-    rows, cols = value.shape
+def quarters_kernel(right_ref, left_ref, m0, m1, m2, m3, turned):
+    _, z, y = coords()
+    q, rows = turned.shape[1:]
+    for part in range(2):
+        value = left_ref[pl.ds(pl.multiple_of(y * rows, rows), rows), :] if part else right_ref[...]
+        turned[...] = value.T.reshape(turned.shape)
+        for k, out in enumerate((m0, m1, m2, m3)):
+            out[part * q : (part + 1) * q, :] = turned[z ^ k]
+
+
+def quarters_of(right, left):
+    rows, cols = right.shape
     q = cols // 4
     return pl.pallas_call(
         quarters_kernel,
-        out_shape=[f32(q, rows)] * 4,
+        out_shape=[f32(2 * q, rows)] * 4,
         scratch_shapes=[pltpu.VMEM((4, q, rows), jnp.float32)],
         compiler_params=params(8),
-        cost_estimate=cost(0, rows * cols * 8),
-        name=name,
-    )(value)
+        cost_estimate=cost(0, rows * cols * 16),
+        name="quarters",
+    )(right, left)
+
+
+def stack_kernel(m0, m1, m2, m3, out):
+    for k, m in enumerate((m0, m1, m2, m3)):
+        out[k] = m[0 : out.shape[1], :]
+
+
+def stack_right(messages):
+    q, rows = messages[0].shape[0] // 2, messages[0].shape[1]
+    return pl.pallas_call(
+        stack_kernel,
+        out_shape=f32(4, q, rows),
+        compiler_params=params(8),
+        cost_estimate=cost(0, 32 * q * rows),
+        name="stack_right",
+    )(*messages)
 
 
 def build_kernel(e0, e1, e2, e3, hi_ref, lo_ref):
@@ -87,7 +107,9 @@
                 dense = lax.dot_general(pick, weigh, NT, preferred_element_type=jnp.float32)
                 high = dense.astype(jnp.bfloat16)
                 low = (dense - high.astype(jnp.float32)).astype(jnp.bfloat16)
-                docs = pl.ds(pl.multiple_of(k * 16 * n + step * 128 + 16 * t, 16), 16)
+                half = 8 * n
+                to = (step * 128 // half) * 4 * half + k * half + step * 128 % half + 16 * t
+                docs = pl.ds(pl.multiple_of(to, 16), 16)
                 hi_ref[:, docs, :] = high.reshape(16, 16, 256)
                 lo_ref[:, docs, :] = low.reshape(16, 16, 256)
 
@@ -155,7 +177,8 @@
     )(hi, lo, *vecs)
 
 
-def forward_half_kernel(half, blocks, hi_ref, lo_ref, v0, v1, before, out, total):
+def forward_half_kernel(half, blocks, hi_ref, lo_ref, v0, v1, before, m0, m1, m2, m3, alpha, out, total, columns):
+    _, z, y = coords()
     n = total.shape[0]
     docs = slice(half * n, (half + 1) * n)
     total[...] = before[docs, :]
@@ -164,21 +187,29 @@
     q = out.shape[0]
     out[...] = turned[:q] + turned[q:]
 
-
-def forward_half(hi, lo, vecs, before, blocks, half):
+    @pl.when(y == half)
+    def _():
+        columns[...] = row_to_column(alpha[...])
+        scale = columns[pl.ds(pl.multiple_of(z * q, q), q), :][:, 0:1]
+        for k, m in enumerate((m0, m1, m2, m3)):
+            at = slice(k * m.shape[1], (k + 1) * m.shape[1])
+            out[:, at] = out[:, at] - scale * m[q:, :]
+
+
+def forward_half(hi, lo, vecs, before, messages, alpha, blocks, half):
     docs = hi.shape[1] // 2
     q = vecs[0].shape[1]
     n = 4 * len(blocks)
     return pl.pallas_call(
         functools.partial(forward_half_kernel, half, blocks),
-        in_specs=[whole()] * 5,
+        in_specs=[whole()] * 10,
         out_specs=whole(),
         out_shape=f32(q, docs),
-        scratch_shapes=[pltpu.VMEM((docs, 2 * q), jnp.float32)],
+        scratch_shapes=[pltpu.VMEM((docs, 2 * q), jnp.float32), pltpu.VMEM((4 * q, 128), jnp.float32)],
         compiler_params=params(12),
         cost_estimate=cost(8 * docs * 256 * 256 * n, 4 * docs * 256 * n),
         name="forward_half",
-    )(hi, lo, *vecs, before)
+    )(hi, lo, *vecs, before, *messages, alpha)
 
 
 def square_row(value, z, cols):
@@ -196,32 +227,46 @@
     return jnp.broadcast_to(row, (128, row.shape[1])).T
 
 
-def left_raw_kernel(has_before, mine, other, u0, u1, alpha, *refs):
-    l0, l1, both, sums, columns = refs[-5:]
+def left_half_kernel(mine, other, raw, both, sums):
     _, z, _ = coords()
-    q, docs = u0.shape
-    columns[...] = row_to_column(alpha[...])
-    scale = columns[pl.ds(pl.multiple_of(z * q, q), q), :][:, 0:1]
-    for k, (u, out) in enumerate(((u0, l0), (u1, l1))):
-        at = slice(k * docs, (k + 1) * docs)
-        out[...] = (mine[:, at] + other[:, at]) - scale * u[...]
-    left = jnp.concatenate([l0[...], l1[...]], axis=1)
+    left = mine[...] + other[...]
+    raw[...] = left
     both[...] = split_rows(left)
-    squares = square_row(left, z, sums.shape[1])
-    sums[...] = refs[0][...] + squares if has_before else squares
-
-
-def left_raw(mine, other, lefts, alpha, before=None):
-    q, docs = lefts[0].shape
-    extra = [] if before is None else [before]
-    return pl.pallas_call(
-        functools.partial(left_raw_kernel, before is not None),
-        out_shape=[f32(q, docs)] * 2 + [bf16(2 * q, 2 * docs), f32(8, 4 * q)],
-        scratch_shapes=[pltpu.VMEM((4 * q, 128), jnp.float32)],
-        compiler_params=params(8),
-        cost_estimate=cost(8 * q * docs, 40 * q * docs),
-        name="left_raw",
-    )(mine, other, *lefts, alpha, *extra)
+    sums[...] = square_row(left, z, sums.shape[1])
+
+
+def left_half(mine, other):
+    q, docs = mine.shape
+    return pl.pallas_call(
+        left_half_kernel,
+        out_shape=[f32(q, docs), bf16(2 * q, docs), f32(8, 4 * q)],
+        compiler_params=params(8),
+        cost_estimate=cost(8 * q * docs, 16 * q * docs),
+        name="left_half",
+    )(mine, other)
+
+
+def left_rest_kernel(mine, other, raw, squares, both, sums, l0, l1, l2, l3):
+    _, z, _ = coords()
+    left = mine[...] + other[...]
+    both[...] = split_rows(left)
+    sums[...] = squares[...] + square_row(left, z, sums.shape[1])
+    n = left.shape[1] // 4
+    for k, out in enumerate((l0, l1, l2, l3)):
+        out[:, :n] = raw[:, k * n : (k + 1) * n]
+        out[:, n:] = left[:, k * n : (k + 1) * n]
+
+
+def left_rest(mine, other, raw, squares):
+    q, docs = mine.shape
+    both, sums, *lefts = pl.pallas_call(
+        left_rest_kernel,
+        out_shape=[bf16(2 * q, docs), f32(8, 4 * q)] + [f32(q, docs // 2)] * 4,
+        compiler_params=params(8),
+        cost_estimate=cost(8 * q * docs, 24 * q * docs),
+        name="left_rest",
+    )(mine, other, raw, squares)
+    return both, sums, lefts
 
 
 def backward_kernel(half, first, blocks, parts, hi_ref, lo_ref, both_ref, *refs):
@@ -260,52 +305,52 @@
     )(hi, lo, both, *extra.values())
 
 
-def far_sum_kernel(near, far, beta, send, keep, beta_core):
-    n = keep.shape[0]
-    beta_core[...] = beta[...] + far[2 * n :, :]
-    send[0:n, :] = near[n:, :] + far[n : 2 * n, :]
+def far_sum_kernel(near, far, beta, send, beta_core):
+    n = near.shape[0]
+    beta_core[...] = beta[...] + far[n:, :]
+    send[0:n, :] = near[...] + far[0:n, :]
     send[n:, :] = beta_core[...]
-    keep[...] = near[0:n, :] + far[0:n, :]
 
 
 def far_sums(near, far, beta):
-    rows = near.shape[0] // 2
+    rows = near.shape[0]
     return pl.pallas_call(
         far_sum_kernel,
-        out_shape=[f32(rows + 8, 256), f32(rows, 256), f32(8, 256)],
+        out_shape=[f32(rows + 8, 256), f32(8, 256)],
         compiler_params=params(8),
         cost_estimate=cost(near.size, near.size * 12),
         name="far_sums",
     )(near, far, beta)
 
 
-def right_norm_kernel(docs_total, keep, got, beta_core, v0, v1, v2, v3, g0, g1, g2, g3, sums, columns):
+def right_norm_kernel(docs_total, keep, peer, got, beta_core, v0, v1, v2, v3, g0, g1, g2, g3, columns):
     _, z, _ = coords()
-    q = v0.shape[0]
+    q = g0.shape[0] - 16
     beta_sums = beta_core[...] + got[4 * q :, :]
     columns[...] = row_to_column(jnp.sqrt(beta_sums[0:1, :] / docs_total + epsilon))
     beta = columns[pl.ds(pl.multiple_of(z * q, q), q), :][:, 0:1]
     raws = []
     for k, (v, g) in enumerate(zip((v0, v1, v2, v3), (g0, g1, g2, g3))):
         rows = slice(k * q, (k + 1) * q)
-        total = keep[rows, :] + got[rows, :]
+        total = (keep[rows, :] + peer[rows, :]) + got[rows, :]
         g[0:q, :] = total
-        g[q:, :] = beta_sums
-        raws.append(total / beta - beta * v[...])
-    sums[...] = square_row(jnp.concatenate(raws, axis=1), z, sums.shape[1])
-
-
-def right_norm(docs_total, keep, got, beta_core, quarters):
-    q, rows = quarters[0].shape
-    out = pl.pallas_call(
+        g[q : q + 8, :] = beta_sums
+        raws.append(total / beta - beta * v[0:q, :])
+    squares = square_row(jnp.concatenate(raws, axis=1), z, 4 * q)
+    for g in (g0, g1, g2, g3):
+        g[q + 8 :, :] = squares
+
+
+def right_norm(docs_total, keep, peer, got, beta_core, messages):
+    q, rows = keep.shape[0] // 4, keep.shape[1]
+    return pl.pallas_call(
         functools.partial(right_norm_kernel, docs_total),
-        out_shape=[f32(q + 8, rows)] * 4 + [f32(8, 4 * q)],
+        out_shape=[f32(q + 16, rows)] * 4,
         scratch_shapes=[pltpu.VMEM((4 * q, 128), jnp.float32)],
         compiler_params=params(8),
         cost_estimate=cost(rows * q * 64, rows * q * 100),
         name="right_norm",
-    )(keep, got, beta_core, *quarters)
-    return out[:4], out[4]
+    )(keep, peer, got, beta_core, *messages)
 
 
 def beta_of(pieces, q, docs_total):
@@ -313,15 +358,34 @@
     return jnp.sqrt(((squares[0] + squares[1]) + (squares[2] + squares[3])) / docs_total + epsilon)
 
 
-def finish_kernel(docs_total, feat_total, g0, g1, g2, g3, a0, a1, a2, a3, right, search, phibar, rhobar,
+def alpha_rows_kernel(g0, g1, g2, g3, out):
+    rows = [g[g.shape[0] - 8 :, :] for g in (g0, g1, g2, g3)]
+    total = (rows[0] + rows[1]) + (rows[2] + rows[3])
+    for i in range(8):
+        out[8 * i : 8 * i + 8, :] = total
+
+
+def alpha_rows(pieces):
+    return pl.pallas_call(
+        alpha_rows_kernel,
+        out_shape=f32(64, pieces[0].shape[1]),
+        compiler_params=params(8),
+        cost_estimate=cost(0, 100000),
+        name="alpha_rows",
+    )(*pieces)
+
+
+def finish_kernel(docs_total, feat_total, g0, g1, g2, g3, squares, right, search, phibar, rhobar,
                   right_out, search_out, alpha_out, phibar_out, rhobar_out, turned):
     _, z, _ = coords()
     q = turned.shape[1]
     for k, g in enumerate((g0, g1, g2, g3)):
         turned[z ^ k] = g[0:q, :]
     got = turned[...].reshape(-1, turned.shape[2]).T
-    squares = (a0[0:1, :] + a1[0:1, :]) + (a2[0:1, :] + a3[0:1, :])
-    alpha = jnp.sqrt(squares / feat_total + epsilon)
+    parts = [squares[8 * i : 8 * i + 1, :] for i in range(8)]
+    while len(parts) > 1:
+        parts = [a + b for a, b in zip(parts[::2], parts[1::2])]
+    alpha = jnp.sqrt(parts[0] / feat_total + epsilon)
     beta = beta_of((g0, g1, g2, g3), q, docs_total)
     rho = jnp.sqrt(rhobar[...] * rhobar[...] + beta * beta)
     cosine = rhobar[...] / rho
@@ -335,7 +399,7 @@
     search_out[...] = following - (theta / rho) * search[...]
 
 
-def finish(docs_total, feat_total, pieces, alphas, right, search, phibar, rhobar):
+def finish(docs_total, feat_total, pieces, squares, right, search, phibar, rhobar):
     rows, cols = right.shape
     return pl.pallas_call(
         functools.partial(finish_kernel, docs_total, feat_total),
@@ -344,7 +408,7 @@
         compiler_params=params(8),
         cost_estimate=cost(rows * cols * 16, rows * cols * 20),
         name="finish",
-    )(*pieces, *alphas, right, search, phibar, rhobar)
+    )(*pieces, squares, right, search, phibar, rhobar)
 
 
 def left_out_kernel(docs_total, l0, l1, l2, l3, g0, g1, g2, g3, search, solution, phibar, rhobar, left_out, solution_out, turned):
@@ -390,40 +454,38 @@
     feat_total = right_vec.shape[0] * 32
     alpha_row, phibar_row, rhobar_row = (v.reshape(1, -1) for v in (alpha_prev, phibar, rhobar))
 
-    mine = quarters_of(right_vec, "right_quarters")
-    quarters = along_z(mine)
     ids, vals = col_ids.astype(jnp.float32), col_vals.astype(jnp.float32)
-    entries = along_z([jnp.concatenate([ids.reshape(-1, 256), vals.reshape(-1, 256)], axis=0)] * 4)
-    own = jnp.stack(quarters)
+    stored = jnp.concatenate([ids.reshape(-1, 256), vals.reshape(-1, 256)], axis=0)
+    entries = along_z([stored] * 4)
+    messages = along_z(quarters_of(after(right_vec, stored), left_vec))
+    own = stack_right(messages)
     own_x = swap(own, X_BIT)
     own_peer = swap(own, CORE_BIT)
-    lefts = along_z(quarters_of(after(left_vec, own), "left_quarters"))
 
     hi, lo = build(entries)
     total = forward_part(hi, lo, [own, own_peer], (0, 8))
     vecs = [own_x, swap(own_x, CORE_BIT)]
-    product = [forward_half(hi, lo, vecs, total, (4, 12), half) for half in range(2)]
+    product = [forward_half(hi, lo, vecs, total, messages, alpha_row, (4, 12), half) for half in range(2)]
     other = [swap(p, Y_BIT) for p in product]
 
-    l0, l1, both0, beta0 = left_raw(product[0], other[0], lefts[:2], alpha_row)
+    raw, both0, beta0 = left_half(product[0], other[0])
     partial = backward_part(hi, lo, both0, 0, 0, 16)
-    l2, l3, both1, beta1 = left_raw(product[1], other[1], lefts[2:], alpha_row, beta0)
-    far = swap(backward_part(hi, lo, both1, 1, 8, 8, partial, beta1), CORE_BIT)
-    near = backward_part(hi, lo, both1, 1, 0, 8, partial)
-    send, keep, beta_core = far_sums(near, far, beta1)
+    both1, beta1, lefts = left_rest(product[1], other[1], raw, beta0)
+    far = swap(backward_part(hi, lo, both1, 1, 12, 4, partial, beta1), CORE_BIT)
+    near = backward_part(hi, lo, both1, 1, 4, 4, partial)
+    send, beta_core = far_sums(near, far, beta1)
     got = swap(send, X_BIT)
-    left_pieces = along_z([l0, after(l1, partial), after(l2, keep), after(l3, keep)])
-
-    sent, alpha_part = right_norm(docs_total, keep, got, beta_core, quarters)
-    pieces = along_z(sent)
-    for mask in (CORE_BIT, X_BIT, Y_BIT):
-        alpha_part = alpha_part + swap(alpha_part, mask)
-    alphas = along_z([alpha_part] * 4)
+    peer = swap(backward_part(hi, lo, both1, 1, 8, 4, partial), CORE_BIT)
+    keep = backward_part(hi, lo, both1, 1, 0, 4, partial)
+    left_pieces = along_z([after(l, send) for l in lefts])
+
+    pieces = along_z(right_norm(docs_total, keep, peer, got, beta_core, messages))
+    squares = lax.all_to_all(alpha_rows(pieces), AXES, 0, 0, axis_index_groups=PLANES, tiled=True)
     left_next, solution_next = left_out(
         docs_total, left_pieces, pieces, search_dir, solution_vec, phibar_row, rhobar_row
     )
     right_next, search_next, alpha_next, phibar_next, rhobar_next = finish(
-        docs_total, feat_total, pieces, alphas, right_vec, search_dir, phibar_row, rhobar_row
+        docs_total, feat_total, pieces, squares, right_vec, search_dir, phibar_row, rhobar_row
     )
     return (
         left_next,

time: 104 us -> 95.5 us (0.918)
  the two profiles are of different devices: /device:TPU:0 before, /device:TPU:9 now
where the time goes in v4:
time: 95.5 us; the launch traced here: 95.1 us
  starting transfers between devices  33.7 us (35%)
  waiting for transfers between devices  28.5 us (30%)
  Pallas kernels  27.9 us (29%)
  local copies, waits for them, and re-layouts  3.28 us (3%)
    ppermute x20, waiting for transfers between devices, swap(): return lax.ppermute(value, AXES, [(i, i ^ mask) for i in range(32)])  25.3 us
    ppermute x20, starting transfers between devices, swap(): return lax.ppermute(value, AXES, [(i, i ^ mask) for i in range(32)])  21.6 us
    all_to_all x1, starting transfers between devices, by_columns(): lax.all_to_all(alpha_rows(pieces), AXES, 0, 0, axis_index_groups=PLANES,...  12.2 us
    pallas_call x1, Pallas kernels, build(): pl.pallas_call(build_kernel, in_specs=[whole()] * 4, out_specs=[whole()]...  9.49 us
    pallas_call x5, Pallas kernels, backward_part(): pl.pallas_call(functools.partial(backward_kernel, half, first, blocks, tu...  5.23 us
    pallas_call x2, Pallas kernels, forward_half(): pl.pallas_call(functools.partial(forward_half_kernel, half, blocks), in_s...  5.09 us
    pallas_call x1, Pallas kernels, forward_part(): pl.pallas_call(functools.partial(forward_kernel, blocks), in_specs=[whole...  4.47 us
    all_to_all x1, waiting for transfers between devices, by_columns(): lax.all_to_all(alpha_rows(pieces), AXES, 0, 0, axis_index_groups=PLANES,...  3.2 us
  transfers between devices with their start and end apart: 21, of which 9 were waited for; matrix products, arithmetic and copies ran while one was open for 0% of the time, Pallas kernels for 24%

profile of v4, /device:TPU:9, one launch (start us, length us, event | category | flops | bytes accessed | tf_op | source)
XLA Modules:
  0.0 95.1 jit_solution(15588681430055459797)
XLA Ops:
  0.6 0.8 convert_element_type.4
  1.7 0.8 copy.19
  2.7 0.9 copy-done
  3.6 1.0 %copy-done.3 = f32[512,256]{1,0:T(8,128)S(1)} copy-done((f32[512,256]{1,0:T(8,128)S(1)}, f32[512,256]{1,0:T(8,128)}, u32[]{:S(2)}) %copy-start.3) | copy-done | bytes 524312
  4.7 0.3 quarters.1
  5.0 2.4 %collective-permute-start.4 = (f32[128,256]{1,0:T(8,128)S(1)}, f32[128,256]{1,0:T(8,128)S(1)}, u32[]{:S(2)}, u32[]{:S(2)}) collective-permute-start(f32[128,256]{1,0:T(8,128)S(1)} %get-tuple-element.45), channel_id=1, source_target_pairs={{0,16},{1,17},{2,18},{3,19},{4,20},{5,21},{6,22},{7,23},{8,24},{9,... | collective-permute-start | bytes 393224 | tf_op jit(solution)/shard_map/ppermute | solution.py:439
  7.5 0.2 collective-permute-start.5
  7.7 1.1 %collective-permute-start = (f32[64,256]{1,0:T(8,128)S(1)}, f32[64,256]{1,0:T(8,128)S(1)}, u32[]{:S(2)}, u32[]{:S(2)}) collective-permute-start(f32[64,256]{1,0:T(8,128)S(1)} %constant_dynamic-update-slice_fusion.e0), channel_id=1, source_target_pairs={{0,8},{1,9},{2,10},{3,11},{4,12},{5,13},{6,14},{7,15},{8,0},{9,1},... | collective-permute-start | bytes 196616 | tf_op jit(solution)/shard_map/ppermute | solution.py:439
  8.8 2.1 %collective-permute-start.1 = (f32[64,256]{1,0:T(8,128)S(1)}, f32[64,256]{1,0:T(8,128)S(1)}, u32[]{:S(2)}, u32[]{:S(2)}) collective-permute-start(f32[64,256]{1,0:T(8,128)S(1)} %constant_dynamic-update-slice_fusion.e0), channel_id=1, source_target_pairs={{0,16},{1,17},{2,18},{3,19},{4,20},{5,21},{6,22},{7,23},{8,24},{9,... | collective-permute-start | bytes 196616 | tf_op jit(solution)/shard_map/ppermute | solution.py:439
  10.9 0.3 collective-permute-start.2
  11.1 2.0 %collective-permute-done.4.m2.v2 = f32[128,256]{1,0:T(8,128)S(1)} collective-permute-done((f32[128,256]{1,0:T(8,128)S(1)}, f32[128,256]{1,0:T(8,128)S(1)}, u32[]{:S(2)}, u32[]{:S(2)}) %collective-permute-start.4) | collective-permute-done | bytes 131104 | tf_op jit(solution)/shard_map/ppermute | solution.py:439
  13.2 8.1 %collective-permute-done.5.m3.v3 = f32[128,256]{1,0:T(8,128)S(1)} collective-permute-done((f32[128,256]{1,0:T(8,128)S(1)}, f32[128,256]{1,0:T(8,128)S(1)}, u32[]{:S(2)}, u32[]{:S(2)}) %collective-permute-start.5) | collective-permute-done | bytes 131104 | tf_op jit(solution)/shard_map/ppermute | solution.py:439
  21.3 1.3 %collective-permute-start.6 = (f32[4,64,256]{2,1,0:T(8,128)S(1)}, f32[4,64,256]{2,1,0:T(8,128)S(1)}, u32[]{:S(2)}, u32[]{:S(2)}) collective-permute-start(f32[4,64,256]{2,1,0:T(8,128)S(1)} %stack_right.1.v0), channel_id=1, source_target_pairs={{0,4},{1,5},{2,6},{3,7},{4,0},{5,1},{6,2},{7,3},{8,12},{9,13},{10,... | collective-permute-start | bytes 786440 | tf_op jit(solution)/shard_map/ppermute | solution.py:439
  22.6 3.8 %collective-permute-start.8 = (f32[4,64,256]{2,1,0:T(8,128)S(1)}, f32[4,64,256]{2,1,0:T(8,128)S(1)}, u32[]{:S(2)}, u32[]{:S(2)}) collective-permute-start(f32[4,64,256]{2,1,0:T(8,128)S(1)} %stack_right.1.v0), channel_id=1, source_target_pairs={{0,2},{1,3},{2,0},{3,1},{4,6},{5,7},{6,4},{7,5},{8,10},{9,11},{10,... | collective-permute-start | bytes 786440 | tf_op jit(solution)/shard_map/ppermute | solution.py:439
  26.4 9.5 %dense_rows.1 = (bf16[16,2048,256]{2,1,0:T(8,128)(2,1)S(1)}, bf16[16,2048,256]{2,1,0:T(8,128)(2,1)S(1)}) custom-call(f32[64,256]{1,0:T(8,128)S(1)} %constant_dynamic-update-slice_fusion.e0, f32[64,256]{1,0:T(8,128)S(1)} %collective-permute-done.e1, f32[64,256]{1,0:T(8,128)S(1)} %collective-permute-done.1.e2, f32[64,256]{1,0:T(8,128)S(1)} %collective-permute-done.2.e3), custom_call_target="tpu_custom_call" | custom-call | flops 4294967296 | bytes 33554432 | tf_op jit(solution)/shard_map/dense_rows/pallas_call | solution.py:123
  36.0 4.5 %forward_part.1.before = f32[2048,128]{1,0:T(8,128)S(1)} custom-call(bf16[16,2048,256]{2,1,0:T(8,128)(2,1)S(1)} %get-tuple-element.40.hi_ref, bf16[16,2048,256]{2,1,0:T(8,128)(2,1)S(1)} %get-tuple-element.41.lo_ref, f32[4,64,256]{2,1,0:T(8,128)S(1)} %stack_right.1.v0, f32[4,64,256]{2,1,0:T(8,128)S(1)} %collective-permute-done.8.v1), custom_call_target="tpu_custom_call" | custom-call | flops 8589934592 | bytes 16777216 | tf_op jit(solution)/shard_map/forward_part/pallas_call | solution.py:169
  40.5 2.5 %forward_half.3.mine = f32[64,1024]{1,0:T(8,128)S(1)} custom-call(bf16[16,2048,256]{2,1,0:T(8,128)(2,1)S(1)} %get-tuple-element.40.hi_ref, bf16[16,2048,256]{2,1,0:T(8,128)(2,1)S(1)} %get-tuple-element.41.lo_ref, f32[4,64,256]{2,1,0:T(8,128)S(1)} %collective-permute-done.6.v0, f32[4,64,256]{2,1,0:T(8,128)S(1)} %collective-permute-done.7.v1, ...), custom_call_target="tpu_custom_call" | custom-call | flops 4294967296 | bytes 8388608 | tf_op jit(solution)/shard_map/forward_half/pallas_call | solution.py:203
  43.0 1.1 %collective-permute-start.10 = (f32[64,1024]{1,0:T(8,128)S(1)}, f32[64,1024]{1,0:T(8,128)S(1)}, u32[]{:S(2)}, u32[]{:S(2)}) collective-permute-start(f32[64,1024]{1,0:T(8,128)S(1)} %forward_half.3.mine), channel_id=1, source_target_pairs={{0,1},{1,0},{2,3},{3,2},{4,5},{5,4},{6,7},{7,6},{8,9},{9,8},{10,11... | collective-permute-start | bytes 786440 | tf_op jit(solution)/shard_map/ppermute | solution.py:439
  44.1 2.6 %forward_half.2.mine = f32[64,1024]{1,0:T(8,128)S(1)} custom-call(bf16[16,2048,256]{2,1,0:T(8,128)(2,1)S(1)} %get-tuple-element.40.hi_ref, bf16[16,2048,256]{2,1,0:T(8,128)(2,1)S(1)} %get-tuple-element.41.lo_ref, f32[4,64,256]{2,1,0:T(8,128)S(1)} %collective-permute-done.6.v0, f32[4,64,256]{2,1,0:T(8,128)S(1)} %collective-permute-done.7.v1, ...), custom_call_target="tpu_custom_call" | custom-call | flops 4294967296 | bytes 8388608 | tf_op jit(solution)/shard_map/forward_half/pallas_call | solution.py:203
  46.7 0.6 collective-permute-start.9
  47.3 3.2 %collective-permute-done.10.other = f32[64,1024]{1,0:T(8,128)S(1)} collective-permute-done((f32[64,1024]{1,0:T(8,128)S(1)}, f32[64,1024]{1,0:T(8,128)S(1)}, u32[]{:S(2)}, u32[]{:S(2)}) %collective-permute-start.10) | collective-permute-done | bytes 262176 | tf_op jit(solution)/shard_map/ppermute | solution.py:439
  50.5 0.1 left_half.1
  50.6 2.3 %backward_part.5.refs_0_ = f32[1024,256]{1,0:T(8,128)S(1)} custom-call(bf16[16,2048,256]{2,1,0:T(8,128)(2,1)S(1)} %get-tuple-element.40.hi_ref, bf16[16,2048,256]{2,1,0:T(8,128)(2,1)S(1)} %get-tuple-element.41.lo_ref, bf16[128,1024]{1,0:T(8,128)(2,1)S(1)} %get-tuple-element.51.both_ref), custom_call_target="tpu_custom_call" | custom-call | flops 8589934592 | bytes 16777216 | tf_op jit(solution)/shard_map/backward_part/pallas_call | solution.py:297
  53.0 3.1 %collective-permute-done.9.other = f32[64,1024]{1,0:T(8,128)S(1)} collective-permute-done((f32[64,1024]{1,0:T(8,128)S(1)}, f32[64,1024]{1,0:T(8,128)S(1)}, u32[]{:S(2)}, u32[]{:S(2)}) %collective-permute-start.9) | collective-permute-done | bytes 262176 | tf_op jit(solution)/shard_map/ppermute | solution.py:439
  56.1 0.2 left_rest.1
  56.3 0.7 backward_part.7
  57.0 1.4 %collective-permute-start.11 = (f32[264,256]{1,0:T(8,128)S(1)}, f32[264,256]{1,0:T(8,128)S(1)}, u32[]{:S(2)}, u32[]{:S(2)}) collective-permute-start(f32[264,256]{1,0:T(8,128)S(1)} %backward_part.7), channel_id=1, source_target_pairs={{0,2},{1,3},{2,0},{3,1},{4,6},{5,7},{6,4},{7,5},{8,10},{9,11},{10,... | collective-permute-start | bytes 811016 | tf_op jit(solution)/shard_map/ppermute | solution.py:439
  58.4 0.7 backward_part.6.near
  59.1 0.4 collective-permute-done.11.far
  59.6 1.0 %collective-permute-start.16 = (f32[264,256]{1,0:T(8,128)S(1)}, f32[264,256]{1,0:T(8,128)S(1)}, u32[]{:S(2)}, u32[]{:S(2)}) collective-permute-start(f32[264,256]{1,0:T(8,128)S(1)} %get-tuple-element.53), channel_id=1, source_target_pairs={{0,4},{1,5},{2,6},{3,7},{4,0},{5,1},{6,2},{7,3},{8,12},{9,13},{10,... | collective-permute-start | bytes 811016 | tf_op jit(solution)/shard_map/ppermute | solution.py:439
  60.6 0.7 backward_part.9
  61.4 0.7 collective-permute-start.15
  62.1 0.7 backward_part.8.keep
  62.9 0.4 collective-permute-done.15.peer
  63.3 4.1 %collective-permute-done.16.got = f32[264,256]{1,0:T(8,128)S(1)} collective-permute-done((f32[264,256]{1,0:T(8,128)S(1)}, f32[264,256]{1,0:T(8,128)S(1)}, u32[]{:S(2)}, u32[]{:S(2)}) %collective-permute-start.16) | collective-permute-done | bytes 270368 | tf_op jit(solution)/shard_map/ppermute | solution.py:439
  67.4 0.3 right_norm.1
  67.7 0.3 collective-permute-start.17
  68.0 2.1 %collective-permute-start.18 = (f32[80,256]{1,0:T(8,128)S(1)}, f32[80,256]{1,0:T(8,128)S(1)}, u32[]{:S(2)}, u32[]{:S(2)}) collective-permute-start(f32[80,256]{1,0:T(8,128)S(1)} %get-tuple-element.64), channel_id=1, source_target_pairs={{0,16},{1,17},{2,18},{3,19},{4,20},{5,21},{6,22},{7,23},{8,24},{9,... | collective-permute-start | bytes 245768 | tf_op jit(solution)/shard_map/ppermute | solution.py:439
  70.0 0.4 collective-permute-start.19
  70.4 1.1 %collective-permute-start.12 = (f32[64,512]{1,0:T(8,128)S(1)}, f32[64,512]{1,0:T(8,128)S(1)}, u32[]{:S(2)}, u32[]{:S(2)}) collective-permute-start(f32[64,512]{1,0:T(8,128)S(1)} %get-tuple-element.56), channel_id=1, source_target_pairs={{0,8},{1,9},{2,10},{3,11},{4,12},{5,13},{6,14},{7,15},{8,0},{9,1},... | collective-permute-start | bytes 393224 | tf_op jit(solution)/shard_map/ppermute | solution.py:439
  71.5 1.2 %collective-permute-start.13 = (f32[64,512]{1,0:T(8,128)S(1)}, f32[64,512]{1,0:T(8,128)S(1)}, u32[]{:S(2)}, u32[]{:S(2)}) collective-permute-start(f32[64,512]{1,0:T(8,128)S(1)} %get-tuple-element.58), channel_id=1, source_target_pairs={{0,16},{1,17},{2,18},{3,19},{4,20},{5,21},{6,22},{7,23},{8,24},{9,... | collective-permute-start | bytes 393224 | tf_op jit(solution)/shard_map/ppermute | solution.py:439
  72.7 0.4 collective-permute-start.14
  73.1 3.9 %collective-permute-done.19.g3 = f32[80,256]{1,0:T(8,128)S(1)} collective-permute-done((f32[80,256]{1,0:T(8,128)S(1)}, f32[80,256]{1,0:T(8,128)S(1)}, u32[]{:S(2)}, u32[]{:S(2)}) %collective-permute-start.19) | collective-permute-done | bytes 81952 | tf_op jit(solution)/shard_map/ppermute | solution.py:439
  77.0 0.6 alpha_rows.1
  77.6 12.2 %all-to-all-start = ((f32[8,8,256]{2,1,0:T(8,128)}), f32[8,8,256]{2,1,0:T(8,128)S(1)}, u32[]{:S(2)}, u32[]{:S(2)}) async-start(f32[8,8,256]{2,1,0:T(8,128)} %bitcast.3), calls=%async_computation | async-start | bytes 131072 | tf_op jit(solution)/shard_map/all_to_all | solution.py:483
  89.8 1.1 %left_out.1 = (f32[512,256]{1,0:T(8,128)}, f32[256,256]{1,0:T(8,128)}) custom-call(f32[64,512]{1,0:T(8,128)S(1)} %get-tuple-element.54.l0, f32[64,512]{1,0:T(8,128)S(1)} %collective-permute-done.12.l1, f32[64,512]{1,0:T(8,128)S(1)} %collective-permute-done.13.l2, f32[64,512]{1,0:T(8,128)S(1)} %collective-permute-done.14.l3, ...), custom_call_target="tpu_custom_call" | custom-call | flops 524288 | bytes 1966080 | tf_op jit(solution)/shard_map/left_out/pallas_call | solution.py:428
  90.9 3.2 %all-to-all-done = f32[8,8,256]{2,1,0:T(8,128)S(1)} async-done(((f32[8,8,256]{2,1,0:T(8,128)}), f32[8,8,256]{2,1,0:T(8,128)S(1)}, u32[]{:S(2)}, u32[]{:S(2)}) %all-to-all-start) | async-done | bytes 65568 | tf_op jit(solution)/shard_map/all_to_all | solution.py:483
  94.1 1.0 %finish.1 = (f32[256,256]{1,0:T(8,128)}, f32[256,256]{1,0:T(8,128)}, f32[1,256]{1,0:T(1,128)}, f32[1,256]{1,0:T(1,128)}, f32[1,256]{1,0:T(1,128)}) custom-call(f32[80,256]{1,0:T(8,128)S(1)} %get-tuple-element.62.g0, f32[80,256]{1,0:T(8,128)S(1)} %collective-permute-done.17.g1, f32[80,256]{1,0:T(8,128)S(1)} %collective-permute-done.18.g2, ...), custom_call_target="tpu_custom_call" | custom-call | flops 1048576 | bytes 1310720 | tf_op jit(solution)/shard_map/finish/pallas_call | solution.py:404
  (35 shorter events, 0.7 us)
Async XLA Ops:
  2.7 1.0 %copy-start = (f32[256,256]{1,0:T(8,128)S(1)}, f32[256,256]{1,0:T(8,128)}, u32[]{:S(2)}) copy-start(f32[256,256]{1,0:T(8,128)} %right.1) | copy-start | bytes 786436
  3.6 1.0 %copy-start.3 = (f32[512,256]{1,0:T(8,128)S(1)}, f32[512,256]{1,0:T(8,128)}, u32[]{:S(2)}) copy-start(f32[512,256]{1,0:T(8,128)} %left_ref.1) | copy-start | bytes 1572868
  4.9 5.9 %collective-permute-start.3 = (f32[128,256]{1,0:T(8,128)S(1)}, f32[128,256]{1,0:T(8,128)S(1)}, u32[]{:S(2)}, u32[]{:S(2)}) collective-permute-start(f32[128,256]{1,0:T(8,128)S(1)} %get-tuple-element.44), channel_id=1, source_target_pairs={{0,8},{1,9},{2,10},{3,11},{4,12},{5,13},{6,14},{7,15},{8,0},{9,1},... | collective-permute-start | bytes 393224 | tf_op jit(solution)/shard_map/ppermute | solution.py:439
  5.0 8.2 %collective-permute-start.4 = (f32[128,256]{1,0:T(8,128)S(1)}, f32[128,256]{1,0:T(8,128)S(1)}, u32[]{:S(2)}, u32[]{:S(2)}) collective-permute-start(f32[128,256]{1,0:T(8,128)S(1)} %get-tuple-element.45), channel_id=1, source_target_pairs={{0,16},{1,17},{2,18},{3,19},{4,20},{5,21},{6,22},{7,23},{8,24},{9,... | collective-permute-start | bytes 393224 | tf_op jit(solution)/shard_map/ppermute | solution.py:439
  7.5 13.8 %collective-permute-start.5 = (f32[128,256]{1,0:T(8,128)S(1)}, f32[128,256]{1,0:T(8,128)S(1)}, u32[]{:S(2)}, u32[]{:S(2)}) collective-permute-start(f32[128,256]{1,0:T(8,128)S(1)} %get-tuple-element.46), channel_id=1, source_target_pairs={{0,24},{1,25},{2,26},{3,27},{4,28},{5,29},{6,30},{7,31},{8,16},{9,... | collective-permute-start | bytes 393224 | tf_op jit(solution)/shard_map/ppermute | solution.py:439
  7.7 18.7 %collective-permute-start = (f32[64,256]{1,0:T(8,128)S(1)}, f32[64,256]{1,0:T(8,128)S(1)}, u32[]{:S(2)}, u32[]{:S(2)}) collective-permute-start(f32[64,256]{1,0:T(8,128)S(1)} %constant_dynamic-update-slice_fusion.e0), channel_id=1, source_target_pairs={{0,8},{1,9},{2,10},{3,11},{4,12},{5,13},{6,14},{7,15},{8,0},{9,1},... | collective-permute-start | bytes 196616 | tf_op jit(solution)/shard_map/ppermute | solution.py:439
  8.8 17.6 %collective-permute-start.1 = (f32[64,256]{1,0:T(8,128)S(1)}, f32[64,256]{1,0:T(8,128)S(1)}, u32[]{:S(2)}, u32[]{:S(2)}) collective-permute-start(f32[64,256]{1,0:T(8,128)S(1)} %constant_dynamic-update-slice_fusion.e0), channel_id=1, source_target_pairs={{0,16},{1,17},{2,18},{3,19},{4,20},{5,21},{6,22},{7,23},{8,24},{9,... | collective-permute-start | bytes 196616 | tf_op jit(solution)/shard_map/ppermute | solution.py:439
  10.9 15.5 %collective-permute-start.2 = (f32[64,256]{1,0:T(8,128)S(1)}, f32[64,256]{1,0:T(8,128)S(1)}, u32[]{:S(2)}, u32[]{:S(2)}) collective-permute-start(f32[64,256]{1,0:T(8,128)S(1)} %constant_dynamic-update-slice_fusion.e0), channel_id=1, source_target_pairs={{0,24},{1,25},{2,26},{3,27},{4,28},{5,29},{6,30},{7,31},{8,16},{9,... | collective-permute-start | bytes 196616 | tf_op jit(solution)/shard_map/ppermute | solution.py:439
  21.3 14.6 %collective-permute-start.6 = (f32[4,64,256]{2,1,0:T(8,128)S(1)}, f32[4,64,256]{2,1,0:T(8,128)S(1)}, u32[]{:S(2)}, u32[]{:S(2)}) collective-permute-start(f32[4,64,256]{2,1,0:T(8,128)S(1)} %stack_right.1.v0), channel_id=1, source_target_pairs={{0,4},{1,5},{2,6},{3,7},{4,0},{5,1},{6,2},{7,3},{8,12},{9,13},{10,... | collective-permute-start | bytes 786440 | tf_op jit(solution)/shard_map/ppermute | solution.py:439
  22.6 13.4 %collective-permute-start.8 = (f32[4,64,256]{2,1,0:T(8,128)S(1)}, f32[4,64,256]{2,1,0:T(8,128)S(1)}, u32[]{:S(2)}, u32[]{:S(2)}) collective-permute-start(f32[4,64,256]{2,1,0:T(8,128)S(1)} %stack_right.1.v0), channel_id=1, source_target_pairs={{0,2},{1,3},{2,0},{3,1},{4,6},{5,7},{6,4},{7,5},{8,10},{9,11},{10,... | collective-permute-start | bytes 786440 | tf_op jit(solution)/shard_map/ppermute | solution.py:439
  35.9 4.6 %collective-permute-start.7 = (f32[4,64,256]{2,1,0:T(8,128)S(1)}, f32[4,64,256]{2,1,0:T(8,128)S(1)}, u32[]{:S(2)}, u32[]{:S(2)}) collective-permute-start(f32[4,64,256]{2,1,0:T(8,128)S(1)} %collective-permute-done.6.v0), channel_id=1, source_target_pairs={{0,2},{1,3},{2,0},{3,1},{4,6},{5,7},{6,4},{7,5},{8,10},{9,11},{10,... | collective-permute-start | bytes 786440 | tf_op jit(solution)/shard_map/ppermute | solution.py:439
  36.0 4.5 %copy-start.5 = (f32[256]{0:T(256)S(1)}, f32[256]{0:T(256)}, u32[]{:S(2)}) copy-start(f32[256]{0:T(256)} %param.15) | copy-start | bytes 3076
  43.0 7.5 %collective-permute-start.10 = (f32[64,1024]{1,0:T(8,128)S(1)}, f32[64,1024]{1,0:T(8,128)S(1)}, u32[]{:S(2)}, u32[]{:S(2)}) collective-permute-start(f32[64,1024]{1,0:T(8,128)S(1)} %forward_half.3.mine), channel_id=1, source_target_pairs={{0,1},{1,0},{2,3},{3,2},{4,5},{5,4},{6,7},{7,6},{8,9},{9,8},{10,11... | collective-permute-start | bytes 786440 | tf_op jit(solution)/shard_map/ppermute | solution.py:439
  46.7 9.4 %collective-permute-start.9 = (f32[64,1024]{1,0:T(8,128)S(1)}, f32[64,1024]{1,0:T(8,128)S(1)}, u32[]{:S(2)}, u32[]{:S(2)}) collective-permute-start(f32[64,1024]{1,0:T(8,128)S(1)} %forward_half.2.mine), channel_id=1, source_target_pairs={{0,1},{1,0},{2,3},{3,2},{4,5},{5,4},{6,7},{7,6},{8,9},{9,8},{10,11... | collective-permute-start | bytes 786440 | tf_op jit(solution)/shard_map/ppermute | solution.py:439
  57.0 2.6 %collective-permute-start.11 = (f32[264,256]{1,0:T(8,128)S(1)}, f32[264,256]{1,0:T(8,128)S(1)}, u32[]{:S(2)}, u32[]{:S(2)}) collective-permute-start(f32[264,256]{1,0:T(8,128)S(1)} %backward_part.7), channel_id=1, source_target_pairs={{0,2},{1,3},{2,0},{3,1},{4,6},{5,7},{6,4},{7,5},{8,10},{9,11},{10,... | collective-permute-start | bytes 811016 | tf_op jit(solution)/shard_map/ppermute | solution.py:439
  59.6 7.8 %collective-permute-start.16 = (f32[264,256]{1,0:T(8,128)S(1)}, f32[264,256]{1,0:T(8,128)S(1)}, u32[]{:S(2)}, u32[]{:S(2)}) collective-permute-start(f32[264,256]{1,0:T(8,128)S(1)} %get-tuple-element.53), channel_id=1, source_target_pairs={{0,4},{1,5},{2,6},{3,7},{4,0},{5,1},{6,2},{7,3},{8,12},{9,13},{10,... | collective-permute-start | bytes 811016 | tf_op jit(solution)/shard_map/ppermute | solution.py:439
  61.4 28.4 %copy-start.2 = (f32[256,256]{1,0:T(8,128)S(1)}, f32[256,256]{1,0:T(8,128)}, u32[]{:S(2)}) copy-start(f32[256,256]{1,0:T(8,128)} %search.3) | copy-start | bytes 786436
  61.4 28.4 %copy-start.4 = (f32[256,256]{1,0:T(8,128)S(1)}, f32[256,256]{1,0:T(8,128)}, u32[]{:S(2)}) copy-start(f32[256,256]{1,0:T(8,128)} %solution.1) | copy-start | bytes 786436
  61.4 28.4 %copy-start.6 = (f32[256]{0:T(256)S(1)}, f32[256]{0:T(256)}, u32[]{:S(2)}) copy-start(f32[256]{0:T(256)} %param.16) | copy-start | bytes 3076
  61.4 28.4 %copy-start.7 = (f32[256]{0:T(256)S(1)}, f32[256]{0:T(256)}, u32[]{:S(2)}) copy-start(f32[256]{0:T(256)} %param.17) | copy-start | bytes 3076
  61.4 32.7 %copy-start.1 = (f32[256,256]{1,0:T(8,128)S(1)}, f32[256,256]{1,0:T(8,128)}, u32[]{:S(2)}) copy-start(f32[256,256]{1,0:T(8,128)} %right.1) | copy-start | bytes 786436
  61.4 1.9 %collective-permute-start.15 = (f32[256,256]{1,0:T(8,128)S(1)}, f32[256,256]{1,0:T(8,128)S(1)}, u32[]{:S(2)}, u32[]{:S(2)}) collective-permute-start(f32[256,256]{1,0:T(8,128)S(1)} %backward_part.9), channel_id=1, source_target_pairs={{0,2},{1,3},{2,0},{3,1},{4,6},{5,7},{6,4},{7,5},{8,10},{9,11},{10,... | collective-permute-start | bytes 786440 | tf_op jit(solution)/shard_map/ppermute | solution.py:439
  67.7 5.0 %collective-permute-start.17 = (f32[80,256]{1,0:T(8,128)S(1)}, f32[80,256]{1,0:T(8,128)S(1)}, u32[]{:S(2)}, u32[]{:S(2)}) collective-permute-start(f32[80,256]{1,0:T(8,128)S(1)} %get-tuple-element.63), channel_id=1, source_target_pairs={{0,8},{1,9},{2,10},{3,11},{4,12},{5,13},{6,14},{7,15},{8,0},{9,1},... | collective-permute-start | bytes 245768 | tf_op jit(solution)/shard_map/ppermute | solution.py:439
  68.0 5.1 %collective-permute-start.18 = (f32[80,256]{1,0:T(8,128)S(1)}, f32[80,256]{1,0:T(8,128)S(1)}, u32[]{:S(2)}, u32[]{:S(2)}) collective-permute-start(f32[80,256]{1,0:T(8,128)S(1)} %get-tuple-element.64), channel_id=1, source_target_pairs={{0,16},{1,17},{2,18},{3,19},{4,20},{5,21},{6,22},{7,23},{8,24},{9,... | collective-permute-start | bytes 245768 | tf_op jit(solution)/shard_map/ppermute | solution.py:439
  70.0 6.9 %collective-permute-start.19 = (f32[80,256]{1,0:T(8,128)S(1)}, f32[80,256]{1,0:T(8,128)S(1)}, u32[]{:S(2)}, u32[]{:S(2)}) collective-permute-start(f32[80,256]{1,0:T(8,128)S(1)} %get-tuple-element.65), channel_id=1, source_target_pairs={{0,24},{1,25},{2,26},{3,27},{4,28},{5,29},{6,30},{7,31},{8,16},{9,... | collective-permute-start | bytes 245768 | tf_op jit(solution)/shard_map/ppermute | solution.py:439
  70.4 19.4 %collective-permute-start.12 = (f32[64,512]{1,0:T(8,128)S(1)}, f32[64,512]{1,0:T(8,128)S(1)}, u32[]{:S(2)}, u32[]{:S(2)}) collective-permute-start(f32[64,512]{1,0:T(8,128)S(1)} %get-tuple-element.56), channel_id=1, source_target_pairs={{0,8},{1,9},{2,10},{3,11},{4,12},{5,13},{6,14},{7,15},{8,0},{9,1},... | collective-permute-start | bytes 393224 | tf_op jit(solution)/shard_map/ppermute | solution.py:439
  71.5 18.3 %collective-permute-start.13 = (f32[64,512]{1,0:T(8,128)S(1)}, f32[64,512]{1,0:T(8,128)S(1)}, u32[]{:S(2)}, u32[]{:S(2)}) collective-permute-start(f32[64,512]{1,0:T(8,128)S(1)} %get-tuple-element.58), channel_id=1, source_target_pairs={{0,16},{1,17},{2,18},{3,19},{4,20},{5,21},{6,22},{7,23},{8,24},{9,... | collective-permute-start | bytes 393224 | tf_op jit(solution)/shard_map/ppermute | solution.py:439
  72.7 17.1 %collective-permute-start.14 = (f32[64,512]{1,0:T(8,128)S(1)}, f32[64,512]{1,0:T(8,128)S(1)}, u32[]{:S(2)}, u32[]{:S(2)}) collective-permute-start(f32[64,512]{1,0:T(8,128)S(1)} %get-tuple-element.60), channel_id=1, source_target_pairs={{0,24},{1,25},{2,26},{3,27},{4,28},{5,29},{6,30},{7,31},{8,16},{9,... | collective-permute-start | bytes 393224 | tf_op jit(solution)/shard_map/ppermute | solution.py:439
  77.6 16.5 %all-to-all-start = ((f32[8,8,256]{2,1,0:T(8,128)}), f32[8,8,256]{2,1,0:T(8,128)S(1)}, u32[]{:S(2)}, u32[]{:S(2)}) async-start(f32[8,8,256]{2,1,0:T(8,128)} %bitcast.3), calls=%async_computation | async-start | bytes 131072 | tf_op jit(solution)/shard_map/all_to_all | solution.py:483

commit v5 on v4

--- a/solution.py
+++ b/solution.py
@@ -39,7 +39,7 @@
     return jax.ShapeDtypeStruct(shape, jnp.bfloat16)
 
 
-def quarters_kernel(right_ref, left_ref, m0, m1, m2, m3, turned):
+def quarters_kernel(right_ref, left_ref, token, m0, m1, m2, m3, turned):
     _, z, y = coords()
     q, rows = turned.shape[1:]
     for part in range(2):
@@ -49,7 +49,7 @@
             out[part * q : (part + 1) * q, :] = turned[z ^ k]
 
 
-def quarters_of(right, left):
+def quarters_of(right, left, token):
     rows, cols = right.shape
     q = cols // 4
     return pl.pallas_call(
@@ -59,26 +59,28 @@
         compiler_params=params(8),
         cost_estimate=cost(0, rows * cols * 16),
         name="quarters",
-    )(right, left)
-
-
-def stack_kernel(m0, m1, m2, m3, out):
+    )(right, left, token)
+
+
+def stack_kernel(m0, m1, m2, m3, *refs):
+    out = refs[-1]
     for k, m in enumerate((m0, m1, m2, m3)):
         out[k] = m[0 : out.shape[1], :]
 
 
-def stack_right(messages):
-    q, rows = messages[0].shape[0] // 2, messages[0].shape[1]
+def stack(messages, q, name, *tokens):
+    rows = messages[0].shape[1]
     return pl.pallas_call(
         stack_kernel,
         out_shape=f32(4, q, rows),
         compiler_params=params(8),
         cost_estimate=cost(0, 32 * q * rows),
-        name="stack_right",
-    )(*messages)
-
-
-def build_kernel(e0, e1, e2, e3, hi_ref, lo_ref):
+        name=name,
+    )(*messages, *tokens)
+
+
+def build_kernel(e0, e1, e2, e3, hi_ref, lo_ref, token):
+    token[...] = jnp.zeros_like(token)
     d, _, _ = coords()
     n = e0.shape[0] // 2
     iota = lax.broadcasted_iota(jnp.int32, (256, 256), 0).astype(jnp.float32).astype(jnp.bfloat16)
@@ -123,8 +125,8 @@
     return pl.pallas_call(
         build_kernel,
         in_specs=[whole()] * 4,
-        out_specs=[whole()] * 2,
-        out_shape=[pltpu.VMEM((16, docs, 256), jnp.bfloat16)] * 2,
+        out_specs=[whole()] * 3,
+        out_shape=[pltpu.VMEM((16, docs, 256), jnp.bfloat16)] * 2 + [f32(8, 128)],
         compiler_params=params(12),
         cost_estimate=cost(2 * docs * 16 * 256 * 256, docs * 4096 * 4),
         name="dense_rows",
@@ -247,21 +249,21 @@
 
 
 def left_rest_kernel(mine, other, raw, squares, both, sums, l0, l1, l2, l3):
-    _, z, _ = coords()
+    _, z, y = coords()
     left = mine[...] + other[...]
     both[...] = split_rows(left)
     sums[...] = squares[...] + square_row(left, z, sums.shape[1])
     n = left.shape[1] // 4
     for k, out in enumerate((l0, l1, l2, l3)):
-        out[:, :n] = raw[:, k * n : (k + 1) * n]
-        out[:, n:] = left[:, k * n : (k + 1) * n]
+        at = slice(k * n, (k + 1) * n)
+        out[...] = jnp.where(y == 0, raw[:, at], left[:, at])
 
 
 def left_rest(mine, other, raw, squares):
     q, docs = mine.shape
     both, sums, *lefts = pl.pallas_call(
         left_rest_kernel,
-        out_shape=[bf16(2 * q, docs), f32(8, 4 * q)] + [f32(q, docs // 2)] * 4,
+        out_shape=[bf16(2 * q, docs), f32(8, 4 * q)] + [f32(q, docs // 4)] * 4,
         compiler_params=params(8),
         cost_estimate=cost(8 * q * docs, 24 * q * docs),
         name="left_rest",
@@ -323,7 +325,7 @@
     )(near, far, beta)
 
 
-def right_norm_kernel(docs_total, keep, peer, got, beta_core, v0, v1, v2, v3, g0, g1, g2, g3, columns):
+def right_norm_kernel(docs_total, keep, peer, got, beta_core, v0, v1, v2, v3, token, g0, g1, g2, g3, columns):
     _, z, _ = coords()
     q = g0.shape[0] - 16
     beta_sums = beta_core[...] + got[4 * q :, :]
@@ -341,7 +343,7 @@
         g[q + 8 :, :] = squares
 
 
-def right_norm(docs_total, keep, peer, got, beta_core, messages):
+def right_norm(docs_total, keep, peer, got, beta_core, messages, token):
     q, rows = keep.shape[0] // 4, keep.shape[1]
     return pl.pallas_call(
         functools.partial(right_norm_kernel, docs_total),
@@ -350,7 +352,7 @@
         compiler_params=params(8),
         cost_estimate=cost(rows * q * 64, rows * q * 100),
         name="right_norm",
-    )(keep, peer, got, beta_core, *messages)
+    )(keep, peer, got, beta_core, *messages, token)
 
 
 def beta_of(pieces, q, docs_total):
@@ -411,28 +413,29 @@
     )(*pieces, squares, right, search, phibar, rhobar)
 
 
-def left_out_kernel(docs_total, l0, l1, l2, l3, g0, g1, g2, g3, search, solution, phibar, rhobar, left_out, solution_out, turned):
-    _, z, _ = coords()
-    q, docs = turned.shape[1:]
+def left_out_kernel(docs_total, own, other, g0, g1, g2, g3, search, solution, phibar, rhobar, left_out, solution_out, turned):
+    _, z, y = coords()
+    q, half = turned.shape[1:]
     beta = beta_of((g0, g1, g2, g3), q, docs_total)
-    for k, piece in enumerate((l0, l1, l2, l3)):
-        turned[z ^ k] = piece[...]
-    left_out[...] = turned[...].reshape(-1, docs).T / beta
+    for part, ref in ((y, own), (1 - y, other)):
+        for k in range(4):
+            turned[z ^ k] = ref[k]
+        left_out[pl.ds(pl.multiple_of(part * half, half), half), :] = turned[...].reshape(-1, half).T / beta
     rho = jnp.sqrt(rhobar[...] * rhobar[...] + beta * beta)
     phi = rhobar[...] / rho * phibar[...]
     solution_out[...] = solution[...] + (phi / rho) * search[...]
 
 
-def left_out(docs_total, lefts, pieces, search, solution, phibar, rhobar):
-    q, docs = lefts[0].shape
+def left_out(docs_total, own, other, pieces, search, solution, phibar, rhobar):
+    _, q, half = own.shape
     return pl.pallas_call(
         functools.partial(left_out_kernel, docs_total),
-        out_shape=[f32(docs, 4 * q), f32(*solution.shape)],
-        scratch_shapes=[pltpu.VMEM((4, q, docs), jnp.float32)],
-        compiler_params=params(8),
-        cost_estimate=cost(docs * q * 16, docs * q * 60),
+        out_shape=[f32(2 * half, 4 * q), f32(*solution.shape)],
+        scratch_shapes=[pltpu.VMEM((4, q, half), jnp.float32)],
+        compiler_params=params(8),
+        cost_estimate=cost(half * q * 32, half * q * 120),
         name="left_out",
-    )(*lefts, *pieces, search, solution, phibar, rhobar)
+    )(own, other, *pieces, search, solution, phibar, rhobar)
 
 
 def swap(value, mask):
@@ -457,12 +460,13 @@
     ids, vals = col_ids.astype(jnp.float32), col_vals.astype(jnp.float32)
     stored = jnp.concatenate([ids.reshape(-1, 256), vals.reshape(-1, 256)], axis=0)
     entries = along_z([stored] * 4)
-    messages = along_z(quarters_of(after(right_vec, stored), left_vec))
-    own = stack_right(messages)
+    messages = along_z(quarters_of(right_vec, left_vec, entries[1]))
+    q = messages[0].shape[0] // 2
+
+    hi, lo, token = build(entries)
+    own = stack(messages, q, "stack_right", token)
     own_x = swap(own, X_BIT)
     own_peer = swap(own, CORE_BIT)
-
-    hi, lo = build(entries)
     total = forward_part(hi, lo, [own, own_peer], (0, 8))
     vecs = [own_x, swap(own_x, CORE_BIT)]
     product = [forward_half(hi, lo, vecs, total, messages, alpha_row, (4, 12), half) for half in range(2)]
@@ -477,12 +481,13 @@
     got = swap(send, X_BIT)
     peer = swap(backward_part(hi, lo, both1, 1, 8, 4, partial), CORE_BIT)
     keep = backward_part(hi, lo, both1, 1, 0, 4, partial)
-    left_pieces = along_z([after(l, send) for l in lefts])
-
-    pieces = along_z(right_norm(docs_total, keep, peer, got, beta_core, messages))
+    left_own = stack(along_z([after(l, keep) for l in lefts]), q, "stack_left")
+
+    pieces = along_z(right_norm(docs_total, keep, peer, got, beta_core, messages, left_own))
+    left_other = swap(after(left_own, pieces[0]), Y_BIT)
     squares = lax.all_to_all(alpha_rows(pieces), AXES, 0, 0, axis_index_groups=PLANES, tiled=True)
     left_next, solution_next = left_out(
-        docs_total, left_pieces, pieces, search_dir, solution_vec, phibar_row, rhobar_row
+        docs_total, left_own, left_other, pieces, search_dir, solution_vec, phibar_row, rhobar_row
     )
     right_next, search_next, alpha_next, phibar_next, rhobar_next = finish(
         docs_total, feat_total, pieces, squares, right_vec, search_dir, phibar_row, rhobar_row

time: 95.5 us -> 90.6 us (0.949)
  the two profiles are of different devices: /device:TPU:9 before, /device:TPU:0 now
where the time goes in v5:
time: 90.6 us; the launch traced here: 90.3 us
  Pallas kernels  27.2 us (30%)
  starting transfers between devices  26.4 us (29%)
  waiting for transfers between devices  24.5 us (27%)
  blocking collectives  7.13 us (8%)
  local copies, waits for them, and re-layouts  3.28 us (4%)
  between operations  0.92 us (1%)
    ppermute x21, starting transfers between devices, swap(): return lax.ppermute(value, AXES, [(i, i ^ mask) for i in range(32)])  26.4 us
    ppermute x21, waiting for transfers between devices, swap(): return lax.ppermute(value, AXES, [(i, i ^ mask) for i in range(32)])  24.5 us
    pallas_call x1, Pallas kernels, build(): pl.pallas_call(build_kernel, in_specs=[whole()] * 4, out_specs=[whole()]...  9.45 us
    all_to_all x1, blocking collectives, by_columns(): lax.all_to_all(alpha_rows(pieces), AXES, 0, 0, axis_index_groups=PLANES,...  7.13 us
    pallas_call x5, Pallas kernels, backward_part(): pl.pallas_call(functools.partial(backward_kernel, half, first, blocks, tu...  5.24 us
    pallas_call x2, Pallas kernels, forward_half(): pl.pallas_call(functools.partial(forward_half_kernel, half, blocks), in_s...  5.09 us
    pallas_call x1, Pallas kernels, forward_part(): pl.pallas_call(functools.partial(forward_kernel, blocks), in_specs=[whole...  4.46 us
    unnamed x17, local copies, waits for them, and re-layouts  2.03 us
  transfers between devices with their start and end apart: 21, of which 8 were waited for; matrix products, arithmetic and copies ran while one was open for 0% of the time, Pallas kernels for 25%

profile of v5, /device:TPU:0, one launch (start us, length us, event | category | flops | bytes accessed | tf_op | source)
XLA Modules:
  0.0 90.3 jit_solution(6016476161766932545)
XLA Ops:
  0.6 0.8 convert_element_type.4
  1.4 0.1 copy.18
  1.5 0.1 reshape.43
  1.7 0.8 copy.19
  2.5 0.1 reshape.53
  2.7 3.1 %collective-permute-start = (f32[64,256]{1,0:T(8,128)S(1)}, f32[64,256]{1,0:T(8,128)S(1)}, u32[]{:S(2)}, u32[]{:S(2)}) collective-permute-start(f32[64,256]{1,0:T(8,128)S(1)} %constant_dynamic-update-slice_fusion.e0), channel_id=1, source_target_pairs={{0,8},{1,9},{2,10},{3,11},{4,12},{5,13},{6,14},{7,15},{8,0},{9,1},... | collective-permute-start | bytes 196616 | tf_op jit(solution)/shard_map/ppermute | solution.py:442
  5.8 2.5 %collective-permute-start.2 = (f32[64,256]{1,0:T(8,128)S(1)}, f32[64,256]{1,0:T(8,128)S(1)}, u32[]{:S(2)}, u32[]{:S(2)}) collective-permute-start(f32[64,256]{1,0:T(8,128)S(1)} %constant_dynamic-update-slice_fusion.e0), channel_id=1, source_target_pairs={{0,24},{1,25},{2,26},{3,27},{4,28},{5,29},{6,30},{7,31},{8,16},{9,... | collective-permute-start | bytes 196616 | tf_op jit(solution)/shard_map/ppermute | solution.py:442
  8.2 0.1 collective-permute-start.1
  8.4 0.9 %copy-done = f32[256,256]{1,0:T(8,128)S(1)} copy-done((f32[256,256]{1,0:T(8,128)S(1)}, f32[256,256]{1,0:T(8,128)}, u32[]{:S(2)}) %copy-start) | copy-done | bytes 262168
  9.3 1.0 %copy-done.3 = f32[512,256]{1,0:T(8,128)S(1)} copy-done((f32[512,256]{1,0:T(8,128)S(1)}, f32[512,256]{1,0:T(8,128)}, u32[]{:S(2)}) %copy-start.3) | copy-done | bytes 524312
  10.3 0.2 quarters.1
  10.6 1.9 %collective-permute-start.3 = (f32[128,256]{1,0:T(8,128)S(1)}, f32[128,256]{1,0:T(8,128)S(1)}, u32[]{:S(2)}, u32[]{:S(2)}) collective-permute-start(f32[128,256]{1,0:T(8,128)S(1)} %get-tuple-element.44), channel_id=1, source_target_pairs={{0,8},{1,9},{2,10},{3,11},{4,12},{5,13},{6,14},{7,15},{8,0},{9,1},... | collective-permute-start | bytes 393224 | tf_op jit(solution)/shard_map/ppermute | solution.py:442
  12.5 2.5 %collective-permute-start.4 = (f32[128,256]{1,0:T(8,128)S(1)}, f32[128,256]{1,0:T(8,128)S(1)}, u32[]{:S(2)}, u32[]{:S(2)}) collective-permute-start(f32[128,256]{1,0:T(8,128)S(1)} %get-tuple-element.45), channel_id=1, source_target_pairs={{0,16},{1,17},{2,18},{3,19},{4,20},{5,21},{6,22},{7,23},{8,24},{9,... | collective-permute-start | bytes 393224 | tf_op jit(solution)/shard_map/ppermute | solution.py:442
  14.9 0.5 collective-permute-start.5
  15.5 9.4 %dense_rows.1 = (bf16[16,2048,256]{2,1,0:T(8,128)(2,1)S(1)}, bf16[16,2048,256]{2,1,0:T(8,128)(2,1)S(1)}, f32[8,128]{1,0:T(8,128)S(1)}) custom-call(f32[64,256]{1,0:T(8,128)S(1)} %constant_dynamic-update-slice_fusion.e0, f32[64,256]{1,0:T(8,128)S(1)} %collective-permute-done.e1.token, f32[64,256]{1,0:T(8,128)S(1)} %collective-permute-done.1.e2, ...), custom_call_target="tpu_custom_call" | custom-call | flops 4294967296 | bytes 33554432 | tf_op jit(solution)/shard_map/dense_rows/pallas_call | solution.py:125
  25.0 1.6 %collective-permute-start.6 = (f32[4,64,256]{2,1,0:T(8,128)S(1)}, f32[4,64,256]{2,1,0:T(8,128)S(1)}, u32[]{:S(2)}, u32[]{:S(2)}) collective-permute-start(f32[4,64,256]{2,1,0:T(8,128)S(1)} %stack_right.1.v0), channel_id=1, source_target_pairs={{0,4},{1,5},{2,6},{3,7},{4,0},{5,1},{6,2},{7,3},{8,12},{9,13},{10,... | collective-permute-start | bytes 786440 | tf_op jit(solution)/shard_map/ppermute | solution.py:442
  26.5 5.9 %collective-permute-done.6.v0 = f32[4,64,256]{2,1,0:T(8,128)S(1)} collective-permute-done((f32[4,64,256]{2,1,0:T(8,128)S(1)}, f32[4,64,256]{2,1,0:T(8,128)S(1)}, u32[]{:S(2)}, u32[]{:S(2)}) %collective-permute-start.6) | collective-permute-done | bytes 262176 | tf_op jit(solution)/shard_map/ppermute | solution.py:442
  32.5 4.5 %forward_part.1.before = f32[2048,128]{1,0:T(8,128)S(1)} custom-call(bf16[16,2048,256]{2,1,0:T(8,128)(2,1)S(1)} %get-tuple-element.41.hi_ref, bf16[16,2048,256]{2,1,0:T(8,128)(2,1)S(1)} %get-tuple-element.42.lo_ref, f32[4,64,256]{2,1,0:T(8,128)S(1)} %stack_right.1.v0, f32[4,64,256]{2,1,0:T(8,128)S(1)} %collective-permute-done.8.v1), custom_call_target="tpu_custom_call" | custom-call | flops 8589934592 | bytes 16777216 | tf_op jit(solution)/shard_map/forward_part/pallas_call | solution.py:171
  37.0 2.5 %forward_half.3.mine = f32[64,1024]{1,0:T(8,128)S(1)} custom-call(bf16[16,2048,256]{2,1,0:T(8,128)(2,1)S(1)} %get-tuple-element.41.hi_ref, bf16[16,2048,256]{2,1,0:T(8,128)(2,1)S(1)} %get-tuple-element.42.lo_ref, f32[4,64,256]{2,1,0:T(8,128)S(1)} %collective-permute-done.6.v0, f32[4,64,256]{2,1,0:T(8,128)S(1)} %collective-permute-done.7.v1, ...), custom_call_target="tpu_custom_call" | custom-call | flops 4294967296 | bytes 8388608 | tf_op jit(solution)/shard_map/forward_half/pallas_call | solution.py:205
  39.5 1.5 %collective-permute-start.10 = (f32[64,1024]{1,0:T(8,128)S(1)}, f32[64,1024]{1,0:T(8,128)S(1)}, u32[]{:S(2)}, u32[]{:S(2)}) collective-permute-start(f32[64,1024]{1,0:T(8,128)S(1)} %forward_half.3.mine), channel_id=1, source_target_pairs={{0,1},{1,0},{2,3},{3,2},{4,5},{5,4},{6,7},{7,6},{8,9},{9,8},{10,11... | collective-permute-start | bytes 786440 | tf_op jit(solution)/shard_map/ppermute | solution.py:442
  41.0 2.6 %forward_half.2.mine = f32[64,1024]{1,0:T(8,128)S(1)} custom-call(bf16[16,2048,256]{2,1,0:T(8,128)(2,1)S(1)} %get-tuple-element.41.hi_ref, bf16[16,2048,256]{2,1,0:T(8,128)(2,1)S(1)} %get-tuple-element.42.lo_ref, f32[4,64,256]{2,1,0:T(8,128)S(1)} %collective-permute-done.6.v0, f32[4,64,256]{2,1,0:T(8,128)S(1)} %collective-permute-done.7.v1, ...), custom_call_target="tpu_custom_call" | custom-call | flops 4294967296 | bytes 8388608 | tf_op jit(solution)/shard_map/forward_half/pallas_call | solution.py:205
  43.6 0.8 collective-permute-start.9
  44.4 4.3 %collective-permute-done.10.other = f32[64,1024]{1,0:T(8,128)S(1)} collective-permute-done((f32[64,1024]{1,0:T(8,128)S(1)}, f32[64,1024]{1,0:T(8,128)S(1)}, u32[]{:S(2)}, u32[]{:S(2)}) %collective-permute-start.10) | collective-permute-done | bytes 262176 | tf_op jit(solution)/shard_map/ppermute | solution.py:442
  48.7 0.1 left_half.1
  48.8 2.3 %backward_part.5.refs_0_ = f32[1024,256]{1,0:T(8,128)S(1)} custom-call(bf16[16,2048,256]{2,1,0:T(8,128)(2,1)S(1)} %get-tuple-element.41.hi_ref, bf16[16,2048,256]{2,1,0:T(8,128)(2,1)S(1)} %get-tuple-element.42.lo_ref, bf16[128,1024]{1,0:T(8,128)(2,1)S(1)} %get-tuple-element.52.both_ref), custom_call_target="tpu_custom_call" | custom-call | flops 8589934592 | bytes 16777216 | tf_op jit(solution)/shard_map/backward_part/pallas_call | solution.py:299
  51.2 2.7 %collective-permute-done.9.other = f32[64,1024]{1,0:T(8,128)S(1)} collective-permute-done((f32[64,1024]{1,0:T(8,128)S(1)}, f32[64,1024]{1,0:T(8,128)S(1)}, u32[]{:S(2)}, u32[]{:S(2)}) %collective-permute-start.9) | collective-permute-done | bytes 262176 | tf_op jit(solution)/shard_map/ppermute | solution.py:442
  53.9 0.2 left_rest.1
  54.1 0.7 backward_part.9
  54.9 0.7 backward_part.8.near
  55.6 0.8 collective-permute-done.15.far
  56.5 1.6 %collective-permute-start.16 = (f32[264,256]{1,0:T(8,128)S(1)}, f32[264,256]{1,0:T(8,128)S(1)}, u32[]{:S(2)}, u32[]{:S(2)}) collective-permute-start(f32[264,256]{1,0:T(8,128)S(1)} %get-tuple-element.61), channel_id=1, source_target_pairs={{0,4},{1,5},{2,6},{3,7},{4,0},{5,1},{6,2},{7,3},{8,12},{9,13},{10,... | collective-permute-start | bytes 811016 | tf_op jit(solution)/shard_map/ppermute | solution.py:442
  58.1 0.7 backward_part.7
  58.9 0.7 backward_part.6.keep
  59.6 1.2 %collective-permute-start.11 = (f32[64,256]{1,0:T(8,128)S(1)}, f32[64,256]{1,0:T(8,128)S(1)}, u32[]{:S(2)}, u32[]{:S(2)}) collective-permute-start(f32[64,256]{1,0:T(8,128)S(1)} %get-tuple-element.55), channel_id=1, source_target_pairs={{0,8},{1,9},{2,10},{3,11},{4,12},{5,13},{6,14},{7,15},{8,0},{9,1},... | collective-permute-start | bytes 196616 | tf_op jit(solution)/shard_map/ppermute | solution.py:442
  60.8 1.7 %collective-permute-start.12 = (f32[64,256]{1,0:T(8,128)S(1)}, f32[64,256]{1,0:T(8,128)S(1)}, u32[]{:S(2)}, u32[]{:S(2)}) collective-permute-start(f32[64,256]{1,0:T(8,128)S(1)} %get-tuple-element.57), channel_id=1, source_target_pairs={{0,16},{1,17},{2,18},{3,19},{4,20},{5,21},{6,22},{7,23},{8,24},{9,... | collective-permute-start | bytes 196616 | tf_op jit(solution)/shard_map/ppermute | solution.py:442
  62.5 1.6 %collective-permute-start.13 = (f32[64,256]{1,0:T(8,128)S(1)}, f32[64,256]{1,0:T(8,128)S(1)}, u32[]{:S(2)}, u32[]{:S(2)}) collective-permute-start(f32[64,256]{1,0:T(8,128)S(1)} %get-tuple-element.59), channel_id=1, source_target_pairs={{0,24},{1,25},{2,26},{3,27},{4,28},{5,29},{6,30},{7,31},{8,16},{9,... | collective-permute-start | bytes 196616 | tf_op jit(solution)/shard_map/ppermute | solution.py:442
  64.1 0.1 collective-permute-done.11.m1
  64.2 5.0 %collective-permute-done.12.m2 = f32[64,256]{1,0:T(8,128)S(1)} collective-permute-done((f32[64,256]{1,0:T(8,128)S(1)}, f32[64,256]{1,0:T(8,128)S(1)}, u32[]{:S(2)}, u32[]{:S(2)}) %collective-permute-start.12) | collective-permute-done | bytes 65568 | tf_op jit(solution)/shard_map/ppermute | solution.py:442
  69.3 0.3 right_norm.1
  69.6 1.5 %collective-permute-start.17 = (f32[4,64,256]{2,1,0:T(8,128)S(1)}, f32[4,64,256]{2,1,0:T(8,128)S(1)}, u32[]{:S(2)}, u32[]{:S(2)}) collective-permute-start(f32[4,64,256]{2,1,0:T(8,128)S(1)} %stack_left.1.token.own), channel_id=1, source_target_pairs={{0,1},{1,0},{2,3},{3,2},{4,5},{5,4},{6,7},{7,6},{8,9},{9,8},{10,11... | collective-permute-start | bytes 786440 | tf_op jit(solution)/shard_map/ppermute | solution.py:442
  71.1 1.5 %collective-permute-start.18 = (f32[80,256]{1,0:T(8,128)S(1)}, f32[80,256]{1,0:T(8,128)S(1)}, u32[]{:S(2)}, u32[]{:S(2)}) collective-permute-start(f32[80,256]{1,0:T(8,128)S(1)} %get-tuple-element.65), channel_id=1, source_target_pairs={{0,8},{1,9},{2,10},{3,11},{4,12},{5,13},{6,14},{7,15},{8,0},{9,1},... | collective-permute-start | bytes 245768 | tf_op jit(solution)/shard_map/ppermute | solution.py:442
  72.5 1.1 %collective-permute-start.19 = (f32[80,256]{1,0:T(8,128)S(1)}, f32[80,256]{1,0:T(8,128)S(1)}, u32[]{:S(2)}, u32[]{:S(2)}) collective-permute-start(f32[80,256]{1,0:T(8,128)S(1)} %get-tuple-element.66), channel_id=1, source_target_pairs={{0,16},{1,17},{2,18},{3,19},{4,20},{5,21},{6,22},{7,23},{8,24},{9,... | collective-permute-start | bytes 245768 | tf_op jit(solution)/shard_map/ppermute | solution.py:442
  73.6 1.9 %collective-permute-start.20 = (f32[80,256]{1,0:T(8,128)S(1)}, f32[80,256]{1,0:T(8,128)S(1)}, u32[]{:S(2)}, u32[]{:S(2)}) collective-permute-start(f32[80,256]{1,0:T(8,128)S(1)} %get-tuple-element.67), channel_id=1, source_target_pairs={{0,24},{1,25},{2,26},{3,27},{4,28},{5,29},{6,30},{7,31},{8,16},{9,... | collective-permute-start | bytes 245768 | tf_op jit(solution)/shard_map/ppermute | solution.py:442
  75.4 0.1 collective-permute-done.18.g1
  75.5 5.5 %collective-permute-done.19.g2 = f32[80,256]{1,0:T(8,128)S(1)} collective-permute-done((f32[80,256]{1,0:T(8,128)S(1)}, f32[80,256]{1,0:T(8,128)S(1)}, u32[]{:S(2)}, u32[]{:S(2)}) %collective-permute-start.19) | collective-permute-done | bytes 81952 | tf_op jit(solution)/shard_map/ppermute | solution.py:442
  81.1 7.1 %all_to_all.11 = f32[8,8,256]{2,1,0:T(8,128)S(1)} all-to-all(f32[8,8,256]{2,1,0:T(8,128)S(1)} %bitcast.9), channel_id=1, replica_groups={{0,1,2,3,4,5,6,7},{8,9,10,11,12,13,14,15},{16,17,18,19,20,21,22,23},{24..., dimensions={0} | all-to-all | bytes 131072 | tf_op jit(solution)/shard_map/all_to_all | solution.py:488
  88.2 1.0 %finish.1 = (f32[256,256]{1,0:T(8,128)}, f32[256,256]{1,0:T(8,128)}, f32[1,256]{1,0:T(1,128)}, f32[1,256]{1,0:T(1,128)}, f32[1,256]{1,0:T(1,128)}) custom-call(f32[80,256]{1,0:T(8,128)S(1)} %get-tuple-element.63.g0, f32[80,256]{1,0:T(8,128)S(1)} %collective-permute-done.18.g1, f32[80,256]{1,0:T(8,128)S(1)} %collective-permute-done.19.g2, ...), custom_call_target="tpu_custom_call" | custom-call | flops 1048576 | bytes 1310720 | tf_op jit(solution)/shard_map/finish/pallas_call | solution.py:406
  89.2 1.1 %left_out.1 = (f32[512,256]{1,0:T(8,128)}, f32[256,256]{1,0:T(8,128)}) custom-call(f32[4,64,256]{2,1,0:T(8,128)S(1)} %stack_left.1.token.own, f32[4,64,256]{2,1,0:T(8,128)S(1)} %collective-permute-done.17.other, f32[80,256]{1,0:T(8,128)S(1)} %get-tuple-element.63.g0, f32[80,256]{1,0:T(8,128)S(1)} %collective-permute-done.18.g1, ...), custom_call_target="tpu_custom_call" | custom-call | flops 524288 | bytes 1966080 | tf_op jit(solution)/shard_map/left_out/pallas_call | solution.py:431
  (37 shorter events, 0.3 us)
Async XLA Ops:
  2.7 5.7 %collective-permute-start = (f32[64,256]{1,0:T(8,128)S(1)}, f32[64,256]{1,0:T(8,128)S(1)}, u32[]{:S(2)}, u32[]{:S(2)}) collective-permute-start(f32[64,256]{1,0:T(8,128)S(1)} %constant_dynamic-update-slice_fusion.e0), channel_id=1, source_target_pairs={{0,8},{1,9},{2,10},{3,11},{4,12},{5,13},{6,14},{7,15},{8,0},{9,1},... | collective-permute-start | bytes 196616 | tf_op jit(solution)/shard_map/ppermute | solution.py:442
  5.8 9.7 %collective-permute-start.2 = (f32[64,256]{1,0:T(8,128)S(1)}, f32[64,256]{1,0:T(8,128)S(1)}, u32[]{:S(2)}, u32[]{:S(2)}) collective-permute-start(f32[64,256]{1,0:T(8,128)S(1)} %constant_dynamic-update-slice_fusion.e0), channel_id=1, source_target_pairs={{0,24},{1,25},{2,26},{3,27},{4,28},{5,29},{6,30},{7,31},{8,16},{9,... | collective-permute-start | bytes 196616 | tf_op jit(solution)/shard_map/ppermute | solution.py:442
  8.2 7.2 %collective-permute-start.1 = (f32[64,256]{1,0:T(8,128)S(1)}, f32[64,256]{1,0:T(8,128)S(1)}, u32[]{:S(2)}, u32[]{:S(2)}) collective-permute-start(f32[64,256]{1,0:T(8,128)S(1)} %constant_dynamic-update-slice_fusion.e0), channel_id=1, source_target_pairs={{0,16},{1,17},{2,18},{3,19},{4,20},{5,21},{6,22},{7,23},{8,24},{9,... | collective-permute-start | bytes 196616 | tf_op jit(solution)/shard_map/ppermute | solution.py:442
  8.4 1.0 %copy-start = (f32[256,256]{1,0:T(8,128)S(1)}, f32[256,256]{1,0:T(8,128)}, u32[]{:S(2)}) copy-start(f32[256,256]{1,0:T(8,128)} %right.1) | copy-start | bytes 786436
  9.3 1.0 %copy-start.3 = (f32[512,256]{1,0:T(8,128)S(1)}, f32[512,256]{1,0:T(8,128)}, u32[]{:S(2)}) copy-start(f32[512,256]{1,0:T(8,128)} %left_ref.1) | copy-start | bytes 1572868
  10.6 14.3 %collective-permute-start.3 = (f32[128,256]{1,0:T(8,128)S(1)}, f32[128,256]{1,0:T(8,128)S(1)}, u32[]{:S(2)}, u32[]{:S(2)}) collective-permute-start(f32[128,256]{1,0:T(8,128)S(1)} %get-tuple-element.44), channel_id=1, source_target_pairs={{0,8},{1,9},{2,10},{3,11},{4,12},{5,13},{6,14},{7,15},{8,0},{9,1},... | collective-permute-start | bytes 393224 | tf_op jit(solution)/shard_map/ppermute | solution.py:442
  12.5 12.4 %collective-permute-start.4 = (f32[128,256]{1,0:T(8,128)S(1)}, f32[128,256]{1,0:T(8,128)S(1)}, u32[]{:S(2)}, u32[]{:S(2)}) collective-permute-start(f32[128,256]{1,0:T(8,128)S(1)} %get-tuple-element.45), channel_id=1, source_target_pairs={{0,16},{1,17},{2,18},{3,19},{4,20},{5,21},{6,22},{7,23},{8,24},{9,... | collective-permute-start | bytes 393224 | tf_op jit(solution)/shard_map/ppermute | solution.py:442
  14.9 10.0 %collective-permute-start.5 = (f32[128,256]{1,0:T(8,128)S(1)}, f32[128,256]{1,0:T(8,128)S(1)}, u32[]{:S(2)}, u32[]{:S(2)}) collective-permute-start(f32[128,256]{1,0:T(8,128)S(1)} %get-tuple-element.46), channel_id=1, source_target_pairs={{0,24},{1,25},{2,26},{3,27},{4,28},{5,29},{6,30},{7,31},{8,16},{9,... | collective-permute-start | bytes 393224 | tf_op jit(solution)/shard_map/ppermute | solution.py:442
  25.0 7.5 %collective-permute-start.6 = (f32[4,64,256]{2,1,0:T(8,128)S(1)}, f32[4,64,256]{2,1,0:T(8,128)S(1)}, u32[]{:S(2)}, u32[]{:S(2)}) collective-permute-start(f32[4,64,256]{2,1,0:T(8,128)S(1)} %stack_right.1.v0), channel_id=1, source_target_pairs={{0,4},{1,5},{2,6},{3,7},{4,0},{5,1},{6,2},{7,3},{8,12},{9,13},{10,... | collective-permute-start | bytes 786440 | tf_op jit(solution)/shard_map/ppermute | solution.py:442
  26.5 5.9 %collective-permute-start.8 = (f32[4,64,256]{2,1,0:T(8,128)S(1)}, f32[4,64,256]{2,1,0:T(8,128)S(1)}, u32[]{:S(2)}, u32[]{:S(2)}) collective-permute-start(f32[4,64,256]{2,1,0:T(8,128)S(1)} %stack_right.1.v0), channel_id=1, source_target_pairs={{0,2},{1,3},{2,0},{3,1},{4,6},{5,7},{6,4},{7,5},{8,10},{9,11},{10,... | collective-permute-start | bytes 786440 | tf_op jit(solution)/shard_map/ppermute | solution.py:442
  32.5 4.5 %collective-permute-start.7 = (f32[4,64,256]{2,1,0:T(8,128)S(1)}, f32[4,64,256]{2,1,0:T(8,128)S(1)}, u32[]{:S(2)}, u32[]{:S(2)}) collective-permute-start(f32[4,64,256]{2,1,0:T(8,128)S(1)} %collective-permute-done.6.v0), channel_id=1, source_target_pairs={{0,2},{1,3},{2,0},{3,1},{4,6},{5,7},{6,4},{7,5},{8,10},{9,11},{10,... | collective-permute-start | bytes 786440 | tf_op jit(solution)/shard_map/ppermute | solution.py:442
  32.5 4.5 %copy-start.5 = (f32[256]{0:T(256)S(1)}, f32[256]{0:T(256)}, u32[]{:S(2)}) copy-start(f32[256]{0:T(256)} %param.15) | copy-start | bytes 3076
  39.5 9.2 %collective-permute-start.10 = (f32[64,1024]{1,0:T(8,128)S(1)}, f32[64,1024]{1,0:T(8,128)S(1)}, u32[]{:S(2)}, u32[]{:S(2)}) collective-permute-start(f32[64,1024]{1,0:T(8,128)S(1)} %forward_half.3.mine), channel_id=1, source_target_pairs={{0,1},{1,0},{2,3},{3,2},{4,5},{5,4},{6,7},{7,6},{8,9},{9,8},{10,11... | collective-permute-start | bytes 786440 | tf_op jit(solution)/shard_map/ppermute | solution.py:442
  43.6 10.3 %collective-permute-start.9 = (f32[64,1024]{1,0:T(8,128)S(1)}, f32[64,1024]{1,0:T(8,128)S(1)}, u32[]{:S(2)}, u32[]{:S(2)}) collective-permute-start(f32[64,1024]{1,0:T(8,128)S(1)} %forward_half.2.mine), channel_id=1, source_target_pairs={{0,1},{1,0},{2,3},{3,2},{4,5},{5,4},{6,7},{7,6},{8,9},{9,8},{10,11... | collective-permute-start | bytes 786440 | tf_op jit(solution)/shard_map/ppermute | solution.py:442
  54.8 1.6 %collective-permute-start.15 = (f32[264,256]{1,0:T(8,128)S(1)}, f32[264,256]{1,0:T(8,128)S(1)}, u32[]{:S(2)}, u32[]{:S(2)}) collective-permute-start(f32[264,256]{1,0:T(8,128)S(1)} %backward_part.9), channel_id=1, source_target_pairs={{0,2},{1,3},{2,0},{3,1},{4,6},{5,7},{6,4},{7,5},{8,10},{9,11},{10,... | collective-permute-start | bytes 811016 | tf_op jit(solution)/shard_map/ppermute | solution.py:442
  56.5 12.8 %collective-permute-start.16 = (f32[264,256]{1,0:T(8,128)S(1)}, f32[264,256]{1,0:T(8,128)S(1)}, u32[]{:S(2)}, u32[]{:S(2)}) collective-permute-start(f32[264,256]{1,0:T(8,128)S(1)} %get-tuple-element.61), channel_id=1, source_target_pairs={{0,4},{1,5},{2,6},{3,7},{4,0},{5,1},{6,2},{7,3},{8,12},{9,13},{10,... | collective-permute-start | bytes 811016 | tf_op jit(solution)/shard_map/ppermute | solution.py:442
  58.8 29.4 %copy-start.1 = (f32[256,256]{1,0:T(8,128)S(1)}, f32[256,256]{1,0:T(8,128)}, u32[]{:S(2)}) copy-start(f32[256,256]{1,0:T(8,128)} %right.1) | copy-start | bytes 786436
  58.8 29.4 %copy-start.2 = (f32[256,256]{1,0:T(8,128)S(1)}, f32[256,256]{1,0:T(8,128)}, u32[]{:S(2)}) copy-start(f32[256,256]{1,0:T(8,128)} %search.3) | copy-start | bytes 786436
  58.8 29.4 %copy-start.6 = (f32[256]{0:T(256)S(1)}, f32[256]{0:T(256)}, u32[]{:S(2)}) copy-start(f32[256]{0:T(256)} %param.16) | copy-start | bytes 3076
  58.8 29.4 %copy-start.7 = (f32[256]{0:T(256)S(1)}, f32[256]{0:T(256)}, u32[]{:S(2)}) copy-start(f32[256]{0:T(256)} %param.17) | copy-start | bytes 3076
  58.8 30.4 %copy-start.4 = (f32[256,256]{1,0:T(8,128)S(1)}, f32[256,256]{1,0:T(8,128)}, u32[]{:S(2)}) copy-start(f32[256,256]{1,0:T(8,128)} %solution.1) | copy-start | bytes 786436
  58.8 10.4 %collective-permute-start.14 = (f32[256,256]{1,0:T(8,128)S(1)}, f32[256,256]{1,0:T(8,128)S(1)}, u32[]{:S(2)}, u32[]{:S(2)}) collective-permute-start(f32[256,256]{1,0:T(8,128)S(1)} %backward_part.7), channel_id=1, source_target_pairs={{0,2},{1,3},{2,0},{3,1},{4,6},{5,7},{6,4},{7,5},{8,10},{9,11},{10,... | collective-permute-start | bytes 786440 | tf_op jit(solution)/shard_map/ppermute | solution.py:442
  59.6 4.6 %collective-permute-start.11 = (f32[64,256]{1,0:T(8,128)S(1)}, f32[64,256]{1,0:T(8,128)S(1)}, u32[]{:S(2)}, u32[]{:S(2)}) collective-permute-start(f32[64,256]{1,0:T(8,128)S(1)} %get-tuple-element.55), channel_id=1, source_target_pairs={{0,8},{1,9},{2,10},{3,11},{4,12},{5,13},{6,14},{7,15},{8,0},{9,1},... | collective-permute-start | bytes 196616 | tf_op jit(solution)/shard_map/ppermute | solution.py:442
  60.8 8.4 %collective-permute-start.12 = (f32[64,256]{1,0:T(8,128)S(1)}, f32[64,256]{1,0:T(8,128)S(1)}, u32[]{:S(2)}, u32[]{:S(2)}) collective-permute-start(f32[64,256]{1,0:T(8,128)S(1)} %get-tuple-element.57), channel_id=1, source_target_pairs={{0,16},{1,17},{2,18},{3,19},{4,20},{5,21},{6,22},{7,23},{8,24},{9,... | collective-permute-start | bytes 196616 | tf_op jit(solution)/shard_map/ppermute | solution.py:442
  62.5 6.8 %collective-permute-start.13 = (f32[64,256]{1,0:T(8,128)S(1)}, f32[64,256]{1,0:T(8,128)S(1)}, u32[]{:S(2)}, u32[]{:S(2)}) collective-permute-start(f32[64,256]{1,0:T(8,128)S(1)} %get-tuple-element.59), channel_id=1, source_target_pairs={{0,24},{1,25},{2,26},{3,27},{4,28},{5,29},{6,30},{7,31},{8,16},{9,... | collective-permute-start | bytes 196616 | tf_op jit(solution)/shard_map/ppermute | solution.py:442
  69.6 19.6 %collective-permute-start.17 = (f32[4,64,256]{2,1,0:T(8,128)S(1)}, f32[4,64,256]{2,1,0:T(8,128)S(1)}, u32[]{:S(2)}, u32[]{:S(2)}) collective-permute-start(f32[4,64,256]{2,1,0:T(8,128)S(1)} %stack_left.1.token.own), channel_id=1, source_target_pairs={{0,1},{1,0},{2,3},{3,2},{4,5},{5,4},{6,7},{7,6},{8,9},{9,8},{10,11... | collective-permute-start | bytes 786440 | tf_op jit(solution)/shard_map/ppermute | solution.py:442
  71.1 4.5 %collective-permute-start.18 = (f32[80,256]{1,0:T(8,128)S(1)}, f32[80,256]{1,0:T(8,128)S(1)}, u32[]{:S(2)}, u32[]{:S(2)}) collective-permute-start(f32[80,256]{1,0:T(8,128)S(1)} %get-tuple-element.65), channel_id=1, source_target_pairs={{0,8},{1,9},{2,10},{3,11},{4,12},{5,13},{6,14},{7,15},{8,0},{9,1},... | collective-permute-start | bytes 245768 | tf_op jit(solution)/shard_map/ppermute | solution.py:442
  72.5 8.5 %collective-permute-start.19 = (f32[80,256]{1,0:T(8,128)S(1)}, f32[80,256]{1,0:T(8,128)S(1)}, u32[]{:S(2)}, u32[]{:S(2)}) collective-permute-start(f32[80,256]{1,0:T(8,128)S(1)} %get-tuple-element.66), channel_id=1, source_target_pairs={{0,16},{1,17},{2,18},{3,19},{4,20},{5,21},{6,22},{7,23},{8,24},{9,... | collective-permute-start | bytes 245768 | tf_op jit(solution)/shard_map/ppermute | solution.py:442
  73.6 7.5 %collective-permute-start.20 = (f32[80,256]{1,0:T(8,128)S(1)}, f32[80,256]{1,0:T(8,128)S(1)}, u32[]{:S(2)}, u32[]{:S(2)}) collective-permute-start(f32[80,256]{1,0:T(8,128)S(1)} %get-tuple-element.67), channel_id=1, source_target_pairs={{0,24},{1,25},{2,26},{3,27},{4,28},{5,29},{6,30},{7,31},{8,16},{9,... | collective-permute-start | bytes 245768 | tf_op jit(solution)/shard_map/ppermute | solution.py:442

commit v6 on v5

v6 whole, which is shorter than its diff:
```python
import functools

import jax
import jax.numpy as jnp
from jax import lax
from jax.experimental import pallas as pl
from jax.experimental.pallas import tpu as pltpu
from jax.sharding import PartitionSpec as P

epsilon = 1e-06
AXES = ("doc", "feat")
MIB = 1024 * 1024


Y_BIT, CORE_BIT, X_BIT, Z_SHIFT = 1, 2, 4, 3
NT = (((1,), (1,)), ((), ()))


def coords():
    d = lax.axis_index("doc")
    y = lax.axis_index("feat")
    return d, d >> 2, y


def params(mib):
    return pltpu.CompilerParams(vmem_limit_bytes=mib * MIB)


def cost(flops, nbytes):
    return pl.CostEstimate(flops=int(flops), bytes_accessed=int(nbytes), transcendentals=0)


def f32(*shape):
    return jax.ShapeDtypeStruct(shape, jnp.float32)


def bf16(*shape):
    return jax.ShapeDtypeStruct(shape, jnp.bfloat16)


def prepare_kernel(ids_hbm, vals_hbm, right_hbm, left_hbm, stored, m0, m1, m2, m3,
                   ids, vals, wide, right, left, turned, arrived):
    _, z, y = coords()
    q, rows = turned.shape[1:]
    copies = [
        pltpu.make_async_copy(src, dst, arrived.at[i])
        for i, (src, dst) in enumerate((
            (ids_hbm, ids),
            (vals_hbm, vals),
            (right_hbm, right),
            (left_hbm.at[pl.ds(pl.multiple_of(y * rows, rows), rows), :], left),
        ))
    ]
    for copy in copies:
        copy.start()
    lines, count = stored.shape[0] // 2, ids.shape[0]
    for part, ref in enumerate((ids, vals)):
        copies[part].wait()
        wide[...] = ref[...].astype(jnp.float32).T
        for r in range(256 // count):
            stored[part * lines : (part + 1) * lines, r * count : (r + 1) * count] = wide[
                pl.ds(r, lines, stride=256 // count), :
            ]
    for part, ref in enumerate((right, left)):
        copies[2 + part].wait()
        turned[...] = ref[...].T.reshape(turned.shape)
        for k, out in enumerate((m0, m1, m2, m3)):
            out[part * q : (part + 1) * q, :] = turned[z ^ k]


def prepare(ids, vals, right, left):
    rows, cols = right.shape
    q = cols // 4
    got = pl.pallas_call(
        prepare_kernel,
        in_specs=[pl.BlockSpec(memory_space=pltpu.HBM)] * 4,
        out_specs=[whole()] * 5,
        out_shape=[pltpu.VMEM((ids.size // 128, 256), jnp.float32)] + [pltpu.VMEM((2 * q, rows), jnp.float32)] * 4,
        scratch_shapes=[
            pltpu.VMEM(ids.shape, jnp.int32),
            pltpu.VMEM(vals.shape, jnp.bfloat16),
            pltpu.VMEM(ids.shape[::-1], jnp.float32),
            pltpu.VMEM(right.shape, jnp.float32),
            pltpu.VMEM(right.shape, jnp.float32),
            pltpu.VMEM((4, q, rows), jnp.float32),
            pltpu.SemaphoreType.DMA((4,)),
        ],
        compiler_params=params(60),
        cost_estimate=cost(0, rows * cols * 16),
        name="prepare",
    )(ids, vals, right, left)
    return got[0], got[1:]


def stack_kernel(m0, m1, m2, m3, *refs):
    out = refs[-1]
    for k, m in enumerate((m0, m1, m2, m3)):
        out[k] = m[0 : out.shape[1], :]


def stack(messages, q, name, *tokens):
    rows = messages[0].shape[1]
    return pl.pallas_call(
        stack_kernel,
        out_shape=f32(4, q, rows),
        compiler_params=params(8),
        cost_estimate=cost(0, 32 * q * rows),
        name=name,
    )(*messages, *tokens)


def build_kernel(rel, e0, e1, e2, e3, *refs):
    hi_ref, lo_ref, token = refs[-3:]
    token[...] = jnp.zeros_like(token)
    d, _, y = coords()
    n = e0.shape[0] // 2
    iota = lax.broadcasted_iota(jnp.int32, (256, 256), 0).astype(jnp.float32).astype(jnp.bfloat16)
    lane_doc = lax.broadcasted_iota(jnp.int32, (8, 256), 1) >> 4
    one = jnp.ones((256, 256), jnp.bfloat16)
    zero = jnp.zeros((256, 256), jnp.bfloat16)

    def spread(row):
        wide = jnp.broadcast_to(row, (16, 256)).astype(jnp.bfloat16)
        return jnp.broadcast_to(wide[None], (16, 16, 256)).reshape(256, 256)

    for k, entries in enumerate((e0, e1, e2, e3)):

        @pl.loop(0, n // 16)
        def _(step, k=k, entries=entries):
            at = pl.multiple_of((y ^ rel) * (n // 2) + step * 8, 8)
            ids = entries[pl.ds(at, 8), :].astype(jnp.int32)
            vals = entries[pl.ds(n + at, 8), :]
            owner = (ids >> 8) ^ d
            block = ((owner & 1) << 3) | ((owner & 2) << 1) | (owner >> 2)
            code = (block * 16 + lane_doc).astype(jnp.float32)
            inner = (ids & 255).astype(jnp.float32)
            for t in range(8):
                pick = jnp.where(iota == spread(code[t : t + 1]), one, zero)
                weigh = jnp.where(iota == spread(inner[t : t + 1]), spread(vals[t : t + 1]), zero)
                dense = lax.dot_general(pick, weigh, NT, preferred_element_type=jnp.float32)
                high = dense.astype(jnp.bfloat16)
                low = (dense - high.astype(jnp.float32)).astype(jnp.bfloat16)
                docs = pl.ds(pl.multiple_of(k * 8 * n + step * 128 + 16 * t, 16), 16)
                hi_ref[:, docs, :] = high.reshape(16, 16, 256)
                lo_ref[:, docs, :] = low.reshape(16, 16, 256)


def whole():
    return pl.BlockSpec(memory_space=pltpu.VMEM)


def build(entries, rel, *tokens):
    docs = 4 * (entries[0].shape[0] // 4 * 16)
    *rows, token = pl.pallas_call(
        functools.partial(build_kernel, rel),
        in_specs=[whole()] * (4 + len(tokens)),
        out_specs=[whole()] * 3,
        out_shape=[pltpu.VMEM((16, docs, 256), jnp.bfloat16)] * 2 + [f32(8, 128)],
        compiler_params=params(8),
        cost_estimate=cost(2 * docs * 16 * 256 * 256, docs * 4096 * 4),
        name="dense_rows",
    )(*entries, *tokens)
    return rows, token


def split_rows(value):
    high = value.astype(jnp.bfloat16)
    low = (value - high.astype(jnp.float32)).astype(jnp.bfloat16)
    return jnp.concatenate([high, low], axis=0)


def add_products(hi_ref, lo_ref, vecs, blocks, total):
    for vec, first in zip(vecs, blocks):
        for pair in (0, 2):
            lhs, rhs = [], []
            for k in (pair, pair + 1):
                both = split_rows(vec[k])
                lhs += [hi_ref[first + k], lo_ref[first + k]]
                rhs += [both, both]
            total[...] += lax.dot_general(
                jnp.concatenate(lhs, axis=1), jnp.concatenate(rhs, axis=1), NT, preferred_element_type=jnp.float32
            )


def forward_kernel(blocks, hi_ref, lo_ref, *refs):
    count = len(blocks)
    total = refs[-1]
    total[...] = refs[count][...] if len(refs) > count + 1 else jnp.zeros_like(total)
    add_products(hi_ref, lo_ref, refs[:count], blocks, total)


def forward_part(rows, vecs, blocks, before=None):
    docs, q = rows[0].shape[1], vecs[0].shape[1]
    n = 4 * len(blocks)
    extra = [] if before is None else [before]
    return pl.pallas_call(
        functools.partial(forward_kernel, blocks),
        in_specs=[whole()] * (2 + len(vecs) + len(extra)),
        out_specs=whole(),
        out_shape=f32(docs, 2 * q),
        compiler_params=params(8),
        cost_estimate=cost(8 * docs * 256 * 256 * n, 4 * docs * 256 * n),
        name="forward_part",
    )(*rows, *vecs, *extra)


def product_kernel(blocks, hi_ref, lo_ref, vec, before, *refs):
    out, total, columns = refs[-3:]
    total[...] = before[...]
    add_products(hi_ref, lo_ref, (vec,), blocks, total)
    turned = total[...].T
    q = out.shape[0]
    product = turned[:q] + turned[q:]
    if len(refs) == 3:
        out[...] = product
        return
    _, z, _ = coords()
    *messages, alpha = refs[:5]
    columns[...] = row_to_column(alpha[...])
    scale = columns[pl.ds(pl.multiple_of(z * q, q), q), :][:, 0:1]
    for k, m in enumerate(messages):
        at = slice(k * m.shape[1], (k + 1) * m.shape[1])
        out[:, at] = product[:, at] - scale * m[q:, :]


def product_half(rows, vec, before, blocks, *left):
    docs, q = rows[0].shape[1], vec.shape[1]
    return pl.pallas_call(
        functools.partial(product_kernel, blocks),
        in_specs=[whole()] * (4 + len(left)),
        out_specs=whole(),
        out_shape=f32(q, docs),
        scratch_shapes=[pltpu.VMEM((docs, 2 * q), jnp.float32), pltpu.VMEM((4 * q, 128), jnp.float32)],
        compiler_params=params(8),
        cost_estimate=cost(8 * docs * 256 * 256 * 4, 16 * docs * 256),
        name="product_half",
    )(*rows, vec, before, *left)


def square_sums(value):
    q, n = value.shape
    sums = value[:, 0:128] * value[:, 0:128]
    for at in range(128, n, 128):
        sums = sums + value[:, at : at + 128] * value[:, at : at + 128]
    return jnp.sum(jnp.concatenate([sums] * (128 // q), axis=0).T, axis=0, keepdims=True)


def square_row(value, z, cols):
    row = square_sums(value)
    row = jnp.broadcast_to(jnp.concatenate([row] * (cols // 128), axis=1), (8, cols))
    lane = lax.broadcasted_iota(jnp.int32, (8, cols), 1)
    return jnp.where(lane // value.shape[0] == z, row, 0.0)


def row_to_column(row):
    return jnp.broadcast_to(row, (128, row.shape[1])).T


def left_half_kernel(mine, other, *refs):
    _, z, _ = coords()
    left = mine[...] + other[...]
    both, sums = refs[-2:]
    both[...] = split_rows(left)
    squares = square_row(left, z, sums.shape[1])
    sums[...] = refs[0][...] + squares if len(refs) == 3 else squares
    if len(refs) > 3:
        n = left.shape[1] // 4
        for k, out in enumerate(refs[:4]):
            out[...] = left[:, k * n : (k + 1) * n]


def left_half(mine, other, squares=None):
    q, docs = mine.shape
    extra = [] if squares is None else [squares]
    pieces = [f32(q, docs // 4)] * 4 if squares is None else []
    return pl.pallas_call(
        left_half_kernel,
        out_shape=pieces + [bf16(2 * q, docs), f32(8, 4 * q)],
        compiler_params=params(8),
        cost_estimate=cost(8 * q * docs, 16 * q * docs),
        name="left_half",
    )(mine, other, *extra)


def backward_kernel(first, blocks, parts, hi_ref, lo_ref, both_ref, *refs):
    out_ref = refs[-1]
    both = both_ref[...]
    q = both.shape[0] // 2
    twice = jnp.concatenate([both, both], axis=1)
    for b in range(blocks):
        got = jnp.dot(
            twice,
            jnp.concatenate([hi_ref[first + b], lo_ref[first + b]], axis=0),
            preferred_element_type=jnp.float32,
        )
        got = got[:q] + got[q:]
        if "before" in parts:
            got = got + refs[0][(first + b) * q : (first + b + 1) * q, :]
        out_ref[b * q : (b + 1) * q, :] = got
    if "tail" in parts:
        out_ref[blocks * q :, :] = refs[parts.index("tail")][...]


def backward_part(rows, both, first, blocks, before=None, tail=None, tokens=()):
    q, docs = both.shape[0] // 2, both.shape[1]
    extra = {"before": before, "tail": tail, **{str(i): token for i, token in enumerate(tokens)}}
    extra = {name: value for name, value in extra.items() if value is not None}
    height = blocks * q + (0 if tail is None else tail.shape[0])
    return pl.pallas_call(
        functools.partial(backward_kernel, first, blocks, tuple(extra)),
        in_specs=[whole()] * (3 + len(extra)),
        out_specs=whole(),
        out_shape=f32(height, 256),
        compiler_params=params(8),
        cost_estimate=cost(8 * docs * 256 * 256 * blocks, 4 * docs * 256 * blocks),
        name="backward_part",
    )(*rows, both, *extra.values())


def far_sum_kernel(near, far, beta, send, beta_core):
    n = near.shape[0]
    beta_core[...] = beta[...] + far[n:, :]
    send[0:n, :] = near[...] + far[0:n, :]
    send[n:, :] = beta_core[...]


def far_sums(near, far, beta):
    rows = near.shape[0]
    return pl.pallas_call(
        far_sum_kernel,
        out_shape=[f32(rows + 8, 256), f32(8, 256)],
        compiler_params=params(8),
        cost_estimate=cost(near.size, near.size * 12),
        name="far_sums",
    )(near, far, beta)


def right_norm_kernel(docs_total, keep, peer, got, beta_core, v0, v1, v2, v3, token, g0, g1, g2, g3, sums, columns):
    _, z, _ = coords()
    q = g0.shape[0] - 8
    beta_sums = beta_core[...] + got[4 * q :, :]
    columns[...] = row_to_column(jnp.sqrt(beta_sums[0:1, :] / docs_total + epsilon))
    beta = columns[pl.ds(pl.multiple_of(z * q, q), q), :][:, 0:1]
    raws = []
    for k, (v, g) in enumerate(zip((v0, v1, v2, v3), (g0, g1, g2, g3))):
        rows = slice(k * q, (k + 1) * q)
        total = (keep[rows, :] + peer[rows, :]) + got[rows, :]
        g[0:q, :] = total
        g[q:, :] = beta_sums
        raws.append(total / beta - beta * v[0:q, :])
    sums[...] = jnp.broadcast_to(square_sums(jnp.concatenate(raws, axis=1))[None], sums.shape)


def right_norm(docs_total, keep, peer, got, beta_core, messages, token):
    q, rows = keep.shape[0] // 4, keep.shape[1]
    *pieces, sums = pl.pallas_call(
        functools.partial(right_norm_kernel, docs_total),
        out_shape=[f32(q + 8, rows)] * 4 + [f32(32, 1, 128)],
        scratch_shapes=[pltpu.VMEM((4 * q, 128), jnp.float32)],
        compiler_params=params(8),
        cost_estimate=cost(rows * q * 64, rows * q * 100),
        name="right_norm",
    )(keep, peer, got, beta_core, *messages, token)
    return pieces, sums


def beta_of(pieces, q, docs_total):
    squares = [g[q : q + 1, :] for g in pieces]
    return jnp.sqrt(((squares[0] + squares[1]) + (squares[2] + squares[3])) / docs_total + epsilon)


def finish_kernel(docs_total, feat_total, g0, g1, g2, g3, squares, right, search, phibar, rhobar,
                  right_out, search_out, alpha_out, phibar_out, rhobar_out, turned):
    _, z, _ = coords()
    q = turned.shape[1]
    for k, g in enumerate((g0, g1, g2, g3)):
        turned[z ^ k] = g[0:q, :]
    got = turned[...].reshape(-1, turned.shape[2]).T
    parts = [squares[i] for i in range(32)]
    while len(parts) > 4:
        parts = [a + b for a, b in zip(parts[::2], parts[1::2])]
    low = lax.broadcasted_iota(jnp.int32, parts[0].shape, 1) < q
    parts = [jnp.where(low, parts[0], parts[1]), jnp.where(low, parts[2], parts[3])]
    alpha = jnp.sqrt(jnp.concatenate(parts, axis=1) / feat_total + epsilon)
    beta = beta_of((g0, g1, g2, g3), q, docs_total)
    rho = jnp.sqrt(rhobar[...] * rhobar[...] + beta * beta)
    cosine = rhobar[...] / rho
    sine = beta / rho
    theta = sine * alpha
    rhobar_out[...] = -cosine * alpha
    phibar_out[...] = sine * phibar[...]
    alpha_out[...] = alpha
    following = (got / beta - beta * right[...]) / alpha
    right_out[...] = following
    search_out[...] = following - (theta / rho) * search[...]


def finish(docs_total, feat_total, pieces, squares, right, search, phibar, rhobar):
    rows, cols = right.shape
    return pl.pallas_call(
        functools.partial(finish_kernel, docs_total, feat_total),
        out_shape=[f32(rows, cols)] * 2 + [f32(1, cols)] * 3,
        scratch_shapes=[pltpu.VMEM((4, cols // 4, rows), jnp.float32)],
        compiler_params=params(8),
        cost_estimate=cost(rows * cols * 16, rows * cols * 20),
        name="finish",
    )(*pieces, squares, right, search, phibar, rhobar)


def left_out_kernel(docs_total, own, other, g0, g1, g2, g3, search, solution, phibar, rhobar, left_out, solution_out, turned):
    _, z, y = coords()
    q, half = turned.shape[1:]
    beta = beta_of((g0, g1, g2, g3), q, docs_total)
    for part, ref in ((y, own), (1 - y, other)):
        for k in range(4):
            turned[z ^ k] = ref[k]
        left_out[pl.ds(pl.multiple_of(part * half, half), half), :] = turned[...].reshape(-1, half).T / beta
    rho = jnp.sqrt(rhobar[...] * rhobar[...] + beta * beta)
    phi = rhobar[...] / rho * phibar[...]
    solution_out[...] = solution[...] + (phi / rho) * search[...]


def left_out(docs_total, own, other, pieces, search, solution, phibar, rhobar):
    _, q, half = own.shape
    return pl.pallas_call(
        functools.partial(left_out_kernel, docs_total),
        out_shape=[f32(2 * half, 4 * q), f32(*solution.shape)],
        scratch_shapes=[pltpu.VMEM((4, q, half), jnp.float32)],
        compiler_params=params(8),
        cost_estimate=cost(half * q * 32, half * q * 120),
        name="left_out",
    )(own, other, *pieces, search, solution, phibar, rhobar)


def swap(value, mask):
    return lax.ppermute(value, AXES, [(i, i ^ mask) for i in range(32)])


def along_z(values):
    return [values[0]] + [swap(values[k], k << Z_SHIFT) for k in (1, 2, 3)]


def after(value, *earlier):
    return lax.optimization_barrier((value, *earlier))[0]


def by_columns(
    col_ids, col_vals, left_vec, right_vec, search_dir, solution_vec, alpha_prev, phibar, rhobar
):
    docs_total = left_vec.shape[0] * 16
    feat_total = right_vec.shape[0] * 32
    alpha_row, phibar_row, rhobar_row = (v.reshape(1, -1) for v in (alpha_prev, phibar, rhobar))

    stored, messages = prepare(col_ids.T, col_vals.T, right_vec, left_vec)
    entries = along_z([stored] * 4)
    messages = along_z([messages[0]] + [after(m, entries[1]) for m in messages[1:]])
    q = messages[0].shape[0] // 2

    rows1, token1 = build(entries, 1)
    rows0, token0 = build(entries, 0, token1)
    own = stack(messages, q, "stack_right", token0)
    own_x = swap(own, X_BIT)
    own_peer = swap(own, CORE_BIT)
    total1 = forward_part(rows1, [own, own_peer], (0, 8))
    total0 = forward_part(rows0, [own, own_peer], (0, 8))
    x_peer = swap(after(own_x, total0, total1), CORE_BIT)
    total1 = forward_part(rows1, [own_x], (4,), total1)
    total0 = forward_part(rows0, [own_x], (4,), total0)
    product1 = product_half(rows1, x_peer, total1, (12,))
    product0 = product_half(rows0, x_peer, total0, (12,), *messages, alpha_row)

    *lefts, both0, beta0 = left_half(product0, swap(product1, Y_BIT))
    partial = backward_part(rows0, both0, 0, 16)
    lefts = along_z(lefts)
    both1, beta1 = left_half(product1, swap(product0, Y_BIT), beta0)
    far = swap(backward_part(rows1, both1, 12, 4, partial, beta1, lefts[1:3]), CORE_BIT)
    left_own = stack(lefts, q, "stack_left")
    near = backward_part(rows1, both1, 4, 4, partial)
    send, beta_core = far_sums(near, far, beta1)
    got = swap(send, X_BIT)
    peer = swap(backward_part(rows1, both1, 8, 4, partial, None, [left_own]), CORE_BIT)
    keep = backward_part(rows1, both1, 0, 4, partial)
    left_other = swap(left_own, Y_BIT)

    sent, sums = right_norm(docs_total, keep, peer, got, beta_core, messages, left_other)
    pieces = along_z(sent)
    squares = lax.all_to_all(sums, AXES, 0, 0, tiled=True)
    left_next, solution_next = left_out(
        docs_total, left_own, left_other, pieces, search_dir, solution_vec, phibar_row, rhobar_row
    )
    right_next, search_next, alpha_next, phibar_next, rhobar_next = finish(
        docs_total, feat_total, pieces, squares, right_vec, search_dir, phibar_row, rhobar_row
    )
    return (
        left_next,
        right_next,
        search_next,
        solution_next,
        alpha_next.reshape(-1),
        phibar_next.reshape(-1),
        rhobar_next.reshape(-1),
    )


def forward(col_ids, col_vals, table):
    picked = table[col_ids]
    return jnp.sum(col_vals.astype(jnp.float32)[:, :, None] * picked, axis=1)


def backward(col_ids, col_vals, rows_in, width):
    terms = col_vals.astype(jnp.float32)[:, :, None] * rows_in[:, None, :]
    return jax.ops.segment_sum(
        terms.reshape(-1, rows_in.shape[1]), col_ids.reshape(-1), num_segments=width
    )


def by_blocks(
    col_ids, col_vals, left_vec, right_vec, search_dir, solution_vec, alpha_prev, phibar, rhobar
):
    n_feat = lax.axis_size("feat")
    n_doc = lax.axis_size("doc")
    docs_total = left_vec.shape[0] * n_doc
    feat_total = right_vec.shape[0] * n_doc * n_feat
    table = lax.all_gather(right_vec, "doc", axis=0, tiled=True)
    total = lax.psum(forward(col_ids, col_vals, table), "feat")
    left_raw = total - alpha_prev[None, :] * left_vec
    row_part = jnp.sum(left_raw * left_raw, axis=0)
    beta_norm = jnp.sqrt(lax.psum(row_part, "doc") / docs_total + epsilon)
    left_next = left_raw / beta_norm[None, :]
    feature_part = lax.psum_scatter(
        backward(col_ids, col_vals, left_next, table.shape[0]), "doc", scatter_dimension=0, tiled=True
    )
    right_raw = feature_part - beta_norm[None, :] * right_vec
    squares = lax.psum(jnp.sum(right_raw * right_raw, axis=0), AXES)
    alpha_next = jnp.sqrt(squares / feat_total + epsilon)
    right_next = right_raw / alpha_next[None, :]
    rho_val = jnp.sqrt(rhobar * rhobar + beta_norm * beta_norm)
    cosine = rhobar / rho_val
    sine_val = beta_norm / rho_val
    theta_val = sine_val * alpha_next
    phi_val = cosine * phibar
    solution_next = solution_vec + (phi_val / rho_val)[None, :] * search_dir
    search_next = right_next - (theta_val / rho_val)[None, :] * search_dir
    return (
        left_next,
        right_next,
        search_next,
        solution_next,
        alpha_next,
        sine_val * phibar,
        -cosine * alpha_next,
    )


def solution(mesh):
    small = mesh.shape["doc"] == 16 and mesh.shape["feat"] == 2
    rows = P(("feat", "doc"), None)
    return jax.shard_map(
        by_columns if small else by_blocks,
        mesh=mesh,
        in_specs=(P("doc", "feat"), P("doc", "feat"), P("doc", None), rows, rows, rows, P(), P(), P()),
        out_specs=(P("doc", None), rows, rows, rows, P(), P(), P()),
        check_vma=False,
    )
```

time: 90.6 us -> 90.6 us (level)
  starting transfers between devices: 26.4 us -> 35.8 us
  blocking collectives: 7.13 us -> 0 us
  local copies, waits for them, and re-layouts: 3.28 us -> 0.04 us
  Pallas kernels: 27.2 us -> 29.6 us
    all_to_all x1 -> x0, blocking collectives: 7.13 us -> none  [by_columns(): lax.all_to_all(alpha_rows(pieces), AXES, 0, 0, axis_index_groups=PLANES,...]
    ppermute x21, starting transfers between devices: 26.4 us -> 32.7 us  [swap(): return lax.ppermute(value, AXES, [(i, i ^ mask) for i in range(32)])]
    ppermute x21, waiting for transfers between devices: 24.5 us -> 19.2 us  [swap(): return lax.ppermute(value, AXES, [(i, i ^ mask) for i in range(32)])]
    all_to_all x0 -> x1, waiting for transfers between devices: none -> 4.9 us  [by_columns(): squares = lax.all_to_all(sums, AXES, 0, 0, tiled=True)]
    all_to_all x0 -> x1, starting transfers between devices: none -> 3.04 us  [by_columns(): squares = lax.all_to_all(sums, AXES, 0, 0, tiled=True)]
    pallas_call x1 -> x4, Pallas kernels: 4.46 us -> 7.12 us  [forward_part(): pl.pallas_call(functools.partial(forward_kernel, blocks), in_specs=[whole...]
    unnamed x17 -> x12, local copies, waits for them, and re-layouts: 2.03 us -> 0.04 us
    reshape x3 -> x0, local copies, waits for them, and re-layouts: 1.12 us -> none  [the longest x2 0.97 us: by_columns(): vals.reshape(-1, 256)]
  transfers between devices with their start and end apart: 21 -> 22, of which waited for: 8 -> 10; matrix products, arithmetic and copies ran while one was open for 0% -> 0% of each run, Pallas kernels for 25% -> 27%
where the time goes in v6:
time: 90.6 us; the launch traced here: 90.4 us
  starting transfers between devices  35.8 us (40%)
  Pallas kernels  29.6 us (33%)
  waiting for transfers between devices  24.1 us (27%)
  between operations  0.93 us (1%)
    ppermute x21, starting transfers between devices, swap(): return lax.ppermute(value, AXES, [(i, i ^ mask) for i in range(32)])  32.7 us
    ppermute x21, waiting for transfers between devices, swap(): return lax.ppermute(value, AXES, [(i, i ^ mask) for i in range(32)])  19.2 us
    pallas_call x2, Pallas kernels, build(): pl.pallas_call(functools.partial(build_kernel, rel), in_specs=[whole()] *...  9.65 us
    pallas_call x4, Pallas kernels, forward_part(): pl.pallas_call(functools.partial(forward_kernel, blocks), in_specs=[whole...  7.12 us
    pallas_call x5, Pallas kernels, backward_part(): pl.pallas_call(functools.partial(backward_kernel, first, blocks, tuple(ex...  5.18 us
    all_to_all x1, waiting for transfers between devices, by_columns(): squares = lax.all_to_all(sums, AXES, 0, 0, tiled=True)  4.9 us
    all_to_all x1, starting transfers between devices, by_columns(): squares = lax.all_to_all(sums, AXES, 0, 0, tiled=True)  3.04 us
    pallas_call x2, Pallas kernels, product_half(): pl.pallas_call(functools.partial(product_kernel, blocks), in_specs=[whole...  2.64 us
  transfers between devices with their start and end apart: 22, of which 10 were waited for; matrix products, arithmetic and copies ran while one was open for 0% of the time, Pallas kernels for 27%

profile of v6, /device:TPU:0, one launch (start us, length us, event | category | flops | bytes accessed | tf_op | source)
XLA Modules:
  0.0 90.4 jit_solution(11008824802782823788)
XLA Ops:
  0.6 1.6 %prepare.1 = (f32[64,256]{1,0:T(8,128)S(1)}, f32[128,256]{1,0:T(8,128)S(1)}, f32[128,256]{1,0:T(8,128)S(1)}, f32[128,256]{1,0:T(8,128)S(1)}, f32[128,256]{1,0:T(8,128)S(1)}) custom-call(s32[16,512]{1,0:T(8,128)} %bitcast.13, bf16[16,512]{1,0:T(8,128)(2,1)} %bitcast.14, f32[256,256]{1,0:T(8,128)} %right.1, f32[512,256]{1,0:T(8,128)} %left_hbm.1), custom_call_target="tpu_custom_call" | custom-call | bytes 1048576 | tf_op jit(solution)/shard_map/prepare/pallas_call | solution.py:74
  2.3 3.1 %collective-permute-start = (f32[64,256]{1,0:T(8,128)S(1)}, f32[64,256]{1,0:T(8,128)S(1)}, u32[]{:S(2)}, u32[]{:S(2)}) collective-permute-start(f32[64,256]{1,0:T(8,128)S(1)} %get-tuple-element.44.e0), channel_id=1, source_target_pairs={{0,8},{1,9},{2,10},{3,11},{4,12},{5,13},{6,14},{7,15},{8,0},{9,1},... | collective-permute-start | bytes 196616 | tf_op jit(solution)/shard_map/ppermute | solution.py:436
  5.4 2.4 %collective-permute-start.2 = (f32[64,256]{1,0:T(8,128)S(1)}, f32[64,256]{1,0:T(8,128)S(1)}, u32[]{:S(2)}, u32[]{:S(2)}) collective-permute-start(f32[64,256]{1,0:T(8,128)S(1)} %get-tuple-element.44.e0), channel_id=1, source_target_pairs={{0,24},{1,25},{2,26},{3,27},{4,28},{5,29},{6,30},{7,31},{8,16},{9,... | collective-permute-start | bytes 196616 | tf_op jit(solution)/shard_map/ppermute | solution.py:436
  7.8 0.1 collective-permute-start.1
  8.0 1.8 %collective-permute-start.3 = (f32[128,256]{1,0:T(8,128)S(1)}, f32[128,256]{1,0:T(8,128)S(1)}, u32[]{:S(2)}, u32[]{:S(2)}) collective-permute-start(f32[128,256]{1,0:T(8,128)S(1)} %get-tuple-element.50), channel_id=1, source_target_pairs={{0,8},{1,9},{2,10},{3,11},{4,12},{5,13},{6,14},{7,15},{8,0},{9,1},... | collective-permute-start | bytes 393224 | tf_op jit(solution)/shard_map/ppermute | solution.py:436
  9.8 2.5 %collective-permute-start.4 = (f32[128,256]{1,0:T(8,128)S(1)}, f32[128,256]{1,0:T(8,128)S(1)}, u32[]{:S(2)}, u32[]{:S(2)}) collective-permute-start(f32[128,256]{1,0:T(8,128)S(1)} %get-tuple-element.52), channel_id=1, source_target_pairs={{0,16},{1,17},{2,18},{3,19},{4,20},{5,21},{6,22},{7,23},{8,24},{9,... | collective-permute-start | bytes 393224 | tf_op jit(solution)/shard_map/ppermute | solution.py:436
  12.2 0.5 collective-permute-start.5
  12.8 1.9 %collective-permute-done.1.e2 = f32[64,256]{1,0:T(8,128)S(1)} collective-permute-done((f32[64,256]{1,0:T(8,128)S(1)}, f32[64,256]{1,0:T(8,128)S(1)}, u32[]{:S(2)}, u32[]{:S(2)}) %collective-permute-start.1) | collective-permute-done | bytes 65568 | tf_op jit(solution)/shard_map/ppermute | solution.py:436
  14.7 4.7 %dense_rows.2 = (bf16[16,1024,256]{2,1,0:T(8,128)(2,1)S(1)}, bf16[16,1024,256]{2,1,0:T(8,128)(2,1)S(1)}, f32[8,128]{1,0:T(8,128)S(1)}) custom-call(f32[64,256]{1,0:T(8,128)S(1)} %get-tuple-element.44.e0, f32[64,256]{1,0:T(8,128)S(1)} %collective-permute-done.e1, f32[64,256]{1,0:T(8,128)S(1)} %collective-permute-done.1.e2, ...), custom_call_target="tpu_custom_call" | custom-call | flops 2147483648 | bytes 16777216 | tf_op jit(solution)/shard_map/dense_rows/pallas_call | solution.py:154
  19.4 4.9 %dense_rows.3 = (bf16[16,1024,256]{2,1,0:T(8,128)(2,1)S(1)}, bf16[16,1024,256]{2,1,0:T(8,128)(2,1)S(1)}, f32[8,128]{1,0:T(8,128)S(1)}) custom-call(f32[64,256]{1,0:T(8,128)S(1)} %get-tuple-element.44.e0, f32[64,256]{1,0:T(8,128)S(1)} %collective-permute-done.e1, f32[64,256]{1,0:T(8,128)S(1)} %collective-permute-done.1.e2, ...), custom_call_target="tpu_custom_call" | custom-call | flops 2147483648 | bytes 16777216 | tf_op jit(solution)/shard_map/dense_rows/pallas_call | solution.py:154
  24.5 1.6 %collective-permute-start.6 = (f32[4,64,256]{2,1,0:T(8,128)S(1)}, f32[4,64,256]{2,1,0:T(8,128)S(1)}, u32[]{:S(2)}, u32[]{:S(2)}) collective-permute-start(f32[4,64,256]{2,1,0:T(8,128)S(1)} %stack_right.1.refs_0_), channel_id=1, source_target_pairs={{0,4},{1,5},{2,6},{3,7},{4,0},{5,1},{6,2},{7,3},{8,12},{9,13},{10,... | collective-permute-start | bytes 786440 | tf_op jit(solution)/shard_map/ppermute | solution.py:436
  26.1 2.3 %forward_part.5.refs_1_ = f32[1024,128]{1,0:T(8,128)S(1)} custom-call(bf16[16,1024,256]{2,1,0:T(8,128)(2,1)S(1)} %get-tuple-element.56.hi_ref, bf16[16,1024,256]{2,1,0:T(8,128)(2,1)S(1)} %get-tuple-element.57.lo_ref, f32[4,64,256]{2,1,0:T(8,128)S(1)} %stack_right.1.refs_0_, f32[4,64,256]{2,1,0:T(8,128)S(1)} %collective-permute-done.7.refs_1_), custom_call_target="tpu_custom_call" | custom-call | flops 4294967296 | bytes 8388608 | tf_op jit(solution)/shard_map/forward_part/pallas_call | solution.py:196
  28.4 2.3 %forward_part.4.refs_1_ = f32[1024,128]{1,0:T(8,128)S(1)} custom-call(bf16[16,1024,256]{2,1,0:T(8,128)(2,1)S(1)} %get-tuple-element.46.hi_ref, bf16[16,1024,256]{2,1,0:T(8,128)(2,1)S(1)} %get-tuple-element.47.lo_ref, f32[4,64,256]{2,1,0:T(8,128)S(1)} %stack_right.1.refs_0_, f32[4,64,256]{2,1,0:T(8,128)S(1)} %collective-permute-done.7.refs_1_), custom_call_target="tpu_custom_call" | custom-call | flops 4294967296 | bytes 8388608 | tf_op jit(solution)/shard_map/forward_part/pallas_call | solution.py:196
  30.7 2.5 %collective-permute-done.6.refs_0_ = f32[4,64,256]{2,1,0:T(8,128)S(1)} collective-permute-done((f32[4,64,256]{2,1,0:T(8,128)S(1)}, f32[4,64,256]{2,1,0:T(8,128)S(1)}, u32[]{:S(2)}, u32[]{:S(2)}) %collective-permute-start.6) | collective-permute-done | bytes 262176 | tf_op jit(solution)/shard_map/ppermute | solution.py:436
  33.2 1.2 %forward_part.7.before = f32[1024,128]{1,0:T(8,128)S(1)} custom-call(bf16[16,1024,256]{2,1,0:T(8,128)(2,1)S(1)} %get-tuple-element.56.hi_ref, bf16[16,1024,256]{2,1,0:T(8,128)(2,1)S(1)} %get-tuple-element.57.lo_ref, f32[4,64,256]{2,1,0:T(8,128)S(1)} %collective-permute-done.6.refs_0_, f32[1024,128]{1,0:T(8,128)S(1)} %forward_part.5.refs_1_), custom_call_target="tpu_custom_call" | custom-call | flops 2147483648 | bytes 4194304 | tf_op jit(solution)/shard_map/forward_part/pallas_call | solution.py:196
  34.5 0.3 collective-permute-done.8.vec
  34.8 1.3 %product_half.3.mine = f32[64,1024]{1,0:T(8,128)S(1)} custom-call(bf16[16,1024,256]{2,1,0:T(8,128)(2,1)S(1)} %get-tuple-element.56.hi_ref, bf16[16,1024,256]{2,1,0:T(8,128)(2,1)S(1)} %get-tuple-element.57.lo_ref, f32[4,64,256]{2,1,0:T(8,128)S(1)} %collective-permute-done.8.vec, f32[1024,128]{1,0:T(8,128)S(1)} %forward_part.7.before), custom_call_target="tpu_custom_call" | custom-call | flops 2147483648 | bytes 4194304 | tf_op jit(solution)/shard_map/product_half/pallas_call | solution.py:228
  36.1 1.6 %collective-permute-start.9 = (f32[64,1024]{1,0:T(8,128)S(1)}, f32[64,1024]{1,0:T(8,128)S(1)}, u32[]{:S(2)}, u32[]{:S(2)}) collective-permute-start(f32[64,1024]{1,0:T(8,128)S(1)} %product_half.3.mine), channel_id=1, source_target_pairs={{0,1},{1,0},{2,3},{3,2},{4,5},{5,4},{6,7},{7,6},{8,9},{9,8},{10,11... | collective-permute-start | bytes 786440 | tf_op jit(solution)/shard_map/ppermute | solution.py:436
  37.7 1.2 %forward_part.6.before = f32[1024,128]{1,0:T(8,128)S(1)} custom-call(bf16[16,1024,256]{2,1,0:T(8,128)(2,1)S(1)} %get-tuple-element.46.hi_ref, bf16[16,1024,256]{2,1,0:T(8,128)(2,1)S(1)} %get-tuple-element.47.lo_ref, f32[4,64,256]{2,1,0:T(8,128)S(1)} %collective-permute-done.6.refs_0_, f32[1024,128]{1,0:T(8,128)S(1)} %forward_part.4.refs_1_), custom_call_target="tpu_custom_call" | custom-call | flops 2147483648 | bytes 4194304 | tf_op jit(solution)/shard_map/forward_part/pallas_call | solution.py:196
  38.9 1.3 %product_half.2.mine = f32[64,1024]{1,0:T(8,128)S(1)} custom-call(bf16[16,1024,256]{2,1,0:T(8,128)(2,1)S(1)} %get-tuple-element.46.hi_ref, bf16[16,1024,256]{2,1,0:T(8,128)(2,1)S(1)} %get-tuple-element.47.lo_ref, f32[4,64,256]{2,1,0:T(8,128)S(1)} %collective-permute-done.8.vec, f32[1024,128]{1,0:T(8,128)S(1)} %forward_part.6.before, ...), custom_call_target="tpu_custom_call" | custom-call | flops 2147483648 | bytes 4194304 | tf_op jit(solution)/shard_map/product_half/pallas_call | solution.py:228
  40.3 0.6 collective-permute-start.14
  40.8 4.5 %collective-permute-done.9.other = f32[64,1024]{1,0:T(8,128)S(1)} collective-permute-done((f32[64,1024]{1,0:T(8,128)S(1)}, f32[64,1024]{1,0:T(8,128)S(1)}, u32[]{:S(2)}, u32[]{:S(2)}) %collective-permute-start.9) | collective-permute-done | bytes 262176 | tf_op jit(solution)/shard_map/ppermute | solution.py:436
  45.3 0.1 left_half.2
  45.5 1.8 %collective-permute-start.10 = (f32[64,256]{1,0:T(8,128)S(1)}, f32[64,256]{1,0:T(8,128)S(1)}, u32[]{:S(2)}, u32[]{:S(2)}) collective-permute-start(f32[64,256]{1,0:T(8,128)S(1)} %get-tuple-element.60), channel_id=1, source_target_pairs={{0,8},{1,9},{2,10},{3,11},{4,12},{5,13},{6,14},{7,15},{8,0},{9,1},... | collective-permute-start | bytes 196616 | tf_op jit(solution)/shard_map/ppermute | solution.py:436
  47.2 7.2 %collective-permute-start.11 = (f32[64,256]{1,0:T(8,128)S(1)}, f32[64,256]{1,0:T(8,128)S(1)}, u32[]{:S(2)}, u32[]{:S(2)}) collective-permute-start(f32[64,256]{1,0:T(8,128)S(1)} %get-tuple-element.61), channel_id=1, source_target_pairs={{0,16},{1,17},{2,18},{3,19},{4,20},{5,21},{6,22},{7,23},{8,24},{9,... | collective-permute-start | bytes 196616 | tf_op jit(solution)/shard_map/ppermute | solution.py:436
  54.4 2.3 %backward_part.5.refs_0_ = f32[1024,256]{1,0:T(8,128)S(1)} custom-call(bf16[16,1024,256]{2,1,0:T(8,128)(2,1)S(1)} %get-tuple-element.46.hi_ref, bf16[16,1024,256]{2,1,0:T(8,128)(2,1)S(1)} %get-tuple-element.47.lo_ref, bf16[128,1024]{1,0:T(8,128)(2,1)S(1)} %get-tuple-element.65.both_ref), custom_call_target="tpu_custom_call" | custom-call | flops 8589934592 | bytes 16777216 | tf_op jit(solution)/shard_map/backward_part/pallas_call | solution.py:309
  56.8 0.2 left_half.3
  57.0 0.4 collective-permute-done.11.m2.refs_3_
  57.4 0.7 backward_part.9
  58.1 0.1 collective-permute-start.16
  58.2 1.8 %collective-permute-start.12 = (f32[64,256]{1,0:T(8,128)S(1)}, f32[64,256]{1,0:T(8,128)S(1)}, u32[]{:S(2)}, u32[]{:S(2)}) collective-permute-start(f32[64,256]{1,0:T(8,128)S(1)} %get-tuple-element.62), channel_id=1, source_target_pairs={{0,24},{1,25},{2,26},{3,27},{4,28},{5,29},{6,30},{7,31},{8,16},{9,... | collective-permute-start | bytes 196616 | tf_op jit(solution)/shard_map/ppermute | solution.py:436
  60.0 0.7 backward_part.8.near
  60.7 3.9 %collective-permute-done.12.m3 = f32[64,256]{1,0:T(8,128)S(1)} collective-permute-done((f32[64,256]{1,0:T(8,128)S(1)}, f32[64,256]{1,0:T(8,128)S(1)}, u32[]{:S(2)}, u32[]{:S(2)}) %collective-permute-start.12) | collective-permute-done | bytes 65568 | tf_op jit(solution)/shard_map/ppermute | solution.py:436
  64.6 1.6 %collective-permute-start.13 = (f32[4,64,256]{2,1,0:T(8,128)S(1)}, f32[4,64,256]{2,1,0:T(8,128)S(1)}, u32[]{:S(2)}, u32[]{:S(2)}) collective-permute-start(f32[4,64,256]{2,1,0:T(8,128)S(1)} %stack_left.1.refs_1_.own), channel_id=1, source_target_pairs={{0,1},{1,0},{2,3},{3,2},{4,5},{5,4},{6,7},{7,6},{8,9},{9,8},{10,11... | collective-permute-start | bytes 786440 | tf_op jit(solution)/shard_map/ppermute | solution.py:436
  66.2 1.6 %collective-permute-start.17 = (f32[264,256]{1,0:T(8,128)S(1)}, f32[264,256]{1,0:T(8,128)S(1)}, u32[]{:S(2)}, u32[]{:S(2)}) collective-permute-start(f32[264,256]{1,0:T(8,128)S(1)} %get-tuple-element.67), channel_id=1, source_target_pairs={{0,4},{1,5},{2,6},{3,7},{4,0},{5,1},{6,2},{7,3},{8,12},{9,13},{10,... | collective-permute-start | bytes 811016 | tf_op jit(solution)/shard_map/ppermute | solution.py:436
  67.8 0.7 backward_part.7
  68.5 0.1 collective-permute-start.15
  68.6 0.7 backward_part.6.keep
  69.3 3.1 %collective-permute-done.13.token.other = f32[4,64,256]{2,1,0:T(8,128)S(1)} collective-permute-done((f32[4,64,256]{2,1,0:T(8,128)S(1)}, f32[4,64,256]{2,1,0:T(8,128)S(1)}, u32[]{:S(2)}, u32[]{:S(2)}) %collective-permute-start.13) | collective-permute-done | bytes 262176 | tf_op jit(solution)/shard_map/ppermute | solution.py:436
  72.4 1.5 %collective-permute-done.17.got = f32[264,256]{1,0:T(8,128)S(1)} collective-permute-done((f32[264,256]{1,0:T(8,128)S(1)}, f32[264,256]{1,0:T(8,128)S(1)}, u32[]{:S(2)}, u32[]{:S(2)}) %collective-permute-start.17) | collective-permute-done | bytes 270368 | tf_op jit(solution)/shard_map/ppermute | solution.py:436
  73.9 0.9 %right_norm.1 = (f32[72,256]{1,0:T(8,128)S(1)}, f32[72,256]{1,0:T(8,128)S(1)}, f32[72,256]{1,0:T(8,128)S(1)}, f32[72,256]{1,0:T(8,128)S(1)}, f32[32,1,128]{2,1,0:T(1,128)}) custom-call(f32[256,256]{1,0:T(8,128)S(1)} %backward_part.6.keep, f32[256,256]{1,0:T(8,128)S(1)} %collective-permute-done.15.peer, f32[264,256]{1,0:T(8,128)S(1)} %collective-permute-done.17.got, ...), custom_call_target="tpu_custom_call" | custom-call | flops 1048576 | bytes 1638400 | tf_op jit(solution)/shard_map/right_norm/pallas_call | solution.py:356
  74.9 2.3 %collective-permute-start.19 = (f32[72,256]{1,0:T(8,128)S(1)}, f32[72,256]{1,0:T(8,128)S(1)}, u32[]{:S(2)}, u32[]{:S(2)}) collective-permute-start(f32[72,256]{1,0:T(8,128)S(1)} %get-tuple-element.71), channel_id=1, source_target_pairs={{0,16},{1,17},{2,18},{3,19},{4,20},{5,21},{6,22},{7,23},{8,24},{9,... | collective-permute-start | bytes 221192 | tf_op jit(solution)/shard_map/ppermute | solution.py:436
  77.2 2.1 %collective-permute-start.20 = (f32[72,256]{1,0:T(8,128)S(1)}, f32[72,256]{1,0:T(8,128)S(1)}, u32[]{:S(2)}, u32[]{:S(2)}) collective-permute-start(f32[72,256]{1,0:T(8,128)S(1)} %get-tuple-element.72), channel_id=1, source_target_pairs={{0,24},{1,25},{2,26},{3,27},{4,28},{5,29},{6,30},{7,31},{8,16},{9,... | collective-permute-start | bytes 221192 | tf_op jit(solution)/shard_map/ppermute | solution.py:436
  79.3 3.0 %all-to-all-start = ((f32[32,1,128]{2,1,0:T(1,128)}), f32[32,1,128]{2,1,0:T(1,128)S(1)}, u32[]{:S(2)}, u32[]{:S(2)}) async-start(f32[32,1,128]{2,1,0:T(1,128)} %get-tuple-element.74), calls=%async_computation | async-start | bytes 32768 | tf_op jit(solution)/shard_map/all_to_all | solution.py:487
  82.3 1.1 %collective-permute-done.20.g3 = f32[72,256]{1,0:T(8,128)S(1)} collective-permute-done((f32[72,256]{1,0:T(8,128)S(1)}, f32[72,256]{1,0:T(8,128)S(1)}, u32[]{:S(2)}, u32[]{:S(2)}) %collective-permute-start.20) | collective-permute-done | bytes 73760 | tf_op jit(solution)/shard_map/ppermute | solution.py:436
  83.5 1.1 %left_out.1 = (f32[512,256]{1,0:T(8,128)}, f32[256,256]{1,0:T(8,128)}) custom-call(f32[4,64,256]{2,1,0:T(8,128)S(1)} %stack_left.1.refs_1_.own, f32[4,64,256]{2,1,0:T(8,128)S(1)} %collective-permute-done.13.token.other, f32[72,256]{1,0:T(8,128)S(1)} %get-tuple-element.69.g0, f32[72,256]{1,0:T(8,128)S(1)} %collective-permute-done.18.g1, ...), custom_call_target="tpu_custom_call" | custom-call | flops 524288 | bytes 1966080 | tf_op jit(solution)/shard_map/left_out/pallas_call | solution.py:425
  84.5 4.9 %all-to-all-done.squares = f32[32,1,128]{2,1,0:T(1,128)S(1)} async-done(((f32[32,1,128]{2,1,0:T(1,128)}), f32[32,1,128]{2,1,0:T(1,128)S(1)}, u32[]{:S(2)}, u32[]{:S(2)}) %all-to-all-start) | async-done | bytes 16416 | tf_op jit(solution)/shard_map/all_to_all | solution.py:487
  89.4 1.0 %finish.1 = (f32[256,256]{1,0:T(8,128)}, f32[256,256]{1,0:T(8,128)}, f32[1,256]{1,0:T(1,128)}, f32[1,256]{1,0:T(1,128)}, f32[1,256]{1,0:T(1,128)}) custom-call(f32[72,256]{1,0:T(8,128)S(1)} %get-tuple-element.69.g0, f32[72,256]{1,0:T(8,128)S(1)} %collective-permute-done.18.g1, f32[72,256]{1,0:T(8,128)S(1)} %collective-permute-done.19.g2, ...), custom_call_target="tpu_custom_call" | custom-call | flops 1048576 | bytes 1310720 | tf_op jit(solution)/shard_map/finish/pallas_call | solution.py:400
  (30 shorter events, 0.2 us)
Async XLA Ops:
  2.3 5.7 %collective-permute-start = (f32[64,256]{1,0:T(8,128)S(1)}, f32[64,256]{1,0:T(8,128)S(1)}, u32[]{:S(2)}, u32[]{:S(2)}) collective-permute-start(f32[64,256]{1,0:T(8,128)S(1)} %get-tuple-element.44.e0), channel_id=1, source_target_pairs={{0,8},{1,9},{2,10},{3,11},{4,12},{5,13},{6,14},{7,15},{8,0},{9,1},... | collective-permute-start | bytes 196616 | tf_op jit(solution)/shard_map/ppermute | solution.py:436
  5.4 7.4 %collective-permute-start.2 = (f32[64,256]{1,0:T(8,128)S(1)}, f32[64,256]{1,0:T(8,128)S(1)}, u32[]{:S(2)}, u32[]{:S(2)}) collective-permute-start(f32[64,256]{1,0:T(8,128)S(1)} %get-tuple-element.44.e0), channel_id=1, source_target_pairs={{0,24},{1,25},{2,26},{3,27},{4,28},{5,29},{6,30},{7,31},{8,16},{9,... | collective-permute-start | bytes 196616 | tf_op jit(solution)/shard_map/ppermute | solution.py:436
  7.8 6.9 %collective-permute-start.1 = (f32[64,256]{1,0:T(8,128)S(1)}, f32[64,256]{1,0:T(8,128)S(1)}, u32[]{:S(2)}, u32[]{:S(2)}) collective-permute-start(f32[64,256]{1,0:T(8,128)S(1)} %get-tuple-element.44.e0), channel_id=1, source_target_pairs={{0,16},{1,17},{2,18},{3,19},{4,20},{5,21},{6,22},{7,23},{8,24},{9,... | collective-permute-start | bytes 196616 | tf_op jit(solution)/shard_map/ppermute | solution.py:436
  8.0 16.4 %collective-permute-start.3 = (f32[128,256]{1,0:T(8,128)S(1)}, f32[128,256]{1,0:T(8,128)S(1)}, u32[]{:S(2)}, u32[]{:S(2)}) collective-permute-start(f32[128,256]{1,0:T(8,128)S(1)} %get-tuple-element.50), channel_id=1, source_target_pairs={{0,8},{1,9},{2,10},{3,11},{4,12},{5,13},{6,14},{7,15},{8,0},{9,1},... | collective-permute-start | bytes 393224 | tf_op jit(solution)/shard_map/ppermute | solution.py:436
  9.8 14.6 %collective-permute-start.4 = (f32[128,256]{1,0:T(8,128)S(1)}, f32[128,256]{1,0:T(8,128)S(1)}, u32[]{:S(2)}, u32[]{:S(2)}) collective-permute-start(f32[128,256]{1,0:T(8,128)S(1)} %get-tuple-element.52), channel_id=1, source_target_pairs={{0,16},{1,17},{2,18},{3,19},{4,20},{5,21},{6,22},{7,23},{8,24},{9,... | collective-permute-start | bytes 393224 | tf_op jit(solution)/shard_map/ppermute | solution.py:436
  12.2 12.1 %collective-permute-start.5 = (f32[128,256]{1,0:T(8,128)S(1)}, f32[128,256]{1,0:T(8,128)S(1)}, u32[]{:S(2)}, u32[]{:S(2)}) collective-permute-start(f32[128,256]{1,0:T(8,128)S(1)} %get-tuple-element.54), channel_id=1, source_target_pairs={{0,24},{1,25},{2,26},{3,27},{4,28},{5,29},{6,30},{7,31},{8,16},{9,... | collective-permute-start | bytes 393224 | tf_op jit(solution)/shard_map/ppermute | solution.py:436
  24.4 1.7 %collective-permute-start.7 = (f32[4,64,256]{2,1,0:T(8,128)S(1)}, f32[4,64,256]{2,1,0:T(8,128)S(1)}, u32[]{:S(2)}, u32[]{:S(2)}) collective-permute-start(f32[4,64,256]{2,1,0:T(8,128)S(1)} %stack_right.1.refs_0_), channel_id=1, source_target_pairs={{0,2},{1,3},{2,0},{3,1},{4,6},{5,7},{6,4},{7,5},{8,10},{9,11},{10,... | collective-permute-start | bytes 786440 | tf_op jit(solution)/shard_map/ppermute | solution.py:436
  24.5 8.7 %collective-permute-start.6 = (f32[4,64,256]{2,1,0:T(8,128)S(1)}, f32[4,64,256]{2,1,0:T(8,128)S(1)}, u32[]{:S(2)}, u32[]{:S(2)}) collective-permute-start(f32[4,64,256]{2,1,0:T(8,128)S(1)} %stack_right.1.refs_0_), channel_id=1, source_target_pairs={{0,4},{1,5},{2,6},{3,7},{4,0},{5,1},{6,2},{7,3},{8,12},{9,13},{10,... | collective-permute-start | bytes 786440 | tf_op jit(solution)/shard_map/ppermute | solution.py:436
  33.2 1.5 %collective-permute-start.8 = (f32[4,64,256]{2,1,0:T(8,128)S(1)}, f32[4,64,256]{2,1,0:T(8,128)S(1)}, u32[]{:S(2)}, u32[]{:S(2)}) collective-permute-start(f32[4,64,256]{2,1,0:T(8,128)S(1)} %collective-permute-done.6.refs_0_), channel_id=1, source_target_pairs={{0,2},{1,3},{2,0},{3,1},{4,6},{5,7},{6,4},{7,5},{8,10},{9,11},{10,... | collective-permute-start | bytes 786440 | tf_op jit(solution)/shard_map/ppermute | solution.py:436
  36.1 2.8 %copy-start.5 = (f32[256]{0:T(256)S(1)}, f32[256]{0:T(256)}, u32[]{:S(2)}) copy-start(f32[256]{0:T(256)} %param.15) | copy-start | bytes 3076
  36.1 9.2 %collective-permute-start.9 = (f32[64,1024]{1,0:T(8,128)S(1)}, f32[64,1024]{1,0:T(8,128)S(1)}, u32[]{:S(2)}, u32[]{:S(2)}) collective-permute-start(f32[64,1024]{1,0:T(8,128)S(1)} %product_half.3.mine), channel_id=1, source_target_pairs={{0,1},{1,0},{2,3},{3,2},{4,5},{5,4},{6,7},{7,6},{8,9},{9,8},{10,11... | collective-permute-start | bytes 786440 | tf_op jit(solution)/shard_map/ppermute | solution.py:436
  40.3 16.5 %collective-permute-start.14 = (f32[64,1024]{1,0:T(8,128)S(1)}, f32[64,1024]{1,0:T(8,128)S(1)}, u32[]{:S(2)}, u32[]{:S(2)}) collective-permute-start(f32[64,1024]{1,0:T(8,128)S(1)} %product_half.2.mine), channel_id=1, source_target_pairs={{0,1},{1,0},{2,3},{3,2},{4,5},{5,4},{6,7},{7,6},{8,9},{9,8},{10,11... | collective-permute-start | bytes 786440 | tf_op jit(solution)/shard_map/ppermute | solution.py:436
  45.5 11.5 %collective-permute-start.10 = (f32[64,256]{1,0:T(8,128)S(1)}, f32[64,256]{1,0:T(8,128)S(1)}, u32[]{:S(2)}, u32[]{:S(2)}) collective-permute-start(f32[64,256]{1,0:T(8,128)S(1)} %get-tuple-element.60), channel_id=1, source_target_pairs={{0,8},{1,9},{2,10},{3,11},{4,12},{5,13},{6,14},{7,15},{8,0},{9,1},... | collective-permute-start | bytes 196616 | tf_op jit(solution)/shard_map/ppermute | solution.py:436
  47.2 10.1 %collective-permute-start.11 = (f32[64,256]{1,0:T(8,128)S(1)}, f32[64,256]{1,0:T(8,128)S(1)}, u32[]{:S(2)}, u32[]{:S(2)}) collective-permute-start(f32[64,256]{1,0:T(8,128)S(1)} %get-tuple-element.61), channel_id=1, source_target_pairs={{0,16},{1,17},{2,18},{3,19},{4,20},{5,21},{6,22},{7,23},{8,24},{9,... | collective-permute-start | bytes 196616 | tf_op jit(solution)/shard_map/ppermute | solution.py:436
  58.1 8.0 %collective-permute-start.16 = (f32[264,256]{1,0:T(8,128)S(1)}, f32[264,256]{1,0:T(8,128)S(1)}, u32[]{:S(2)}, u32[]{:S(2)}) collective-permute-start(f32[264,256]{1,0:T(8,128)S(1)} %backward_part.9), channel_id=1, source_target_pairs={{0,2},{1,3},{2,0},{3,1},{4,6},{5,7},{6,4},{7,5},{8,10},{9,11},{10,... | collective-permute-start | bytes 811016 | tf_op jit(solution)/shard_map/ppermute | solution.py:436
  58.2 6.4 %collective-permute-start.12 = (f32[64,256]{1,0:T(8,128)S(1)}, f32[64,256]{1,0:T(8,128)S(1)}, u32[]{:S(2)}, u32[]{:S(2)}) collective-permute-start(f32[64,256]{1,0:T(8,128)S(1)} %get-tuple-element.62), channel_id=1, source_target_pairs={{0,24},{1,25},{2,26},{3,27},{4,28},{5,29},{6,30},{7,31},{8,16},{9,... | collective-permute-start | bytes 196616 | tf_op jit(solution)/shard_map/ppermute | solution.py:436
  64.6 7.9 %collective-permute-start.13 = (f32[4,64,256]{2,1,0:T(8,128)S(1)}, f32[4,64,256]{2,1,0:T(8,128)S(1)}, u32[]{:S(2)}, u32[]{:S(2)}) collective-permute-start(f32[4,64,256]{2,1,0:T(8,128)S(1)} %stack_left.1.refs_1_.own), channel_id=1, source_target_pairs={{0,1},{1,0},{2,3},{3,2},{4,5},{5,4},{6,7},{7,6},{8,9},{9,8},{10,11... | collective-permute-start | bytes 786440 | tf_op jit(solution)/shard_map/ppermute | solution.py:436
  66.2 7.8 %collective-permute-start.17 = (f32[264,256]{1,0:T(8,128)S(1)}, f32[264,256]{1,0:T(8,128)S(1)}, u32[]{:S(2)}, u32[]{:S(2)}) collective-permute-start(f32[264,256]{1,0:T(8,128)S(1)} %get-tuple-element.67), channel_id=1, source_target_pairs={{0,4},{1,5},{2,6},{3,7},{4,0},{5,1},{6,2},{7,3},{8,12},{9,13},{10,... | collective-permute-start | bytes 811016 | tf_op jit(solution)/shard_map/ppermute | solution.py:436
  68.5 15.0 %copy-start.1 = (f32[256,256]{1,0:T(8,128)S(1)}, f32[256,256]{1,0:T(8,128)}, u32[]{:S(2)}) copy-start(f32[256,256]{1,0:T(8,128)} %search.3) | copy-start | bytes 786436
  68.5 15.0 %copy-start.2 = (f32[256,256]{1,0:T(8,128)S(1)}, f32[256,256]{1,0:T(8,128)}, u32[]{:S(2)}) copy-start(f32[256,256]{1,0:T(8,128)} %solution.1) | copy-start | bytes 786436
  68.5 14.9 %copy-start.3 = (f32[256]{0:T(256)S(1)}, f32[256]{0:T(256)}, u32[]{:S(2)}) copy-start(f32[256]{0:T(256)} %param.16) | copy-start | bytes 3076
  68.5 14.9 %copy-start.4 = (f32[256]{0:T(256)S(1)}, f32[256]{0:T(256)}, u32[]{:S(2)}) copy-start(f32[256]{0:T(256)} %param.17) | copy-start | bytes 3076
  68.5 20.9 %copy-start = (f32[256,256]{1,0:T(8,128)S(1)}, f32[256,256]{1,0:T(8,128)}, u32[]{:S(2)}) copy-start(f32[256,256]{1,0:T(8,128)} %right.1) | copy-start | bytes 786436
  68.5 3.9 %collective-permute-start.15 = (f32[256,256]{1,0:T(8,128)S(1)}, f32[256,256]{1,0:T(8,128)S(1)}, u32[]{:S(2)}, u32[]{:S(2)}) collective-permute-start(f32[256,256]{1,0:T(8,128)S(1)} %backward_part.7), channel_id=1, source_target_pairs={{0,2},{1,3},{2,0},{3,1},{4,6},{5,7},{6,4},{7,5},{8,10},{9,11},{10,... | collective-permute-start | bytes 786440 | tf_op jit(solution)/shard_map/ppermute | solution.py:436
  74.9 7.4 %collective-permute-start.18 = (f32[72,256]{1,0:T(8,128)S(1)}, f32[72,256]{1,0:T(8,128)S(1)}, u32[]{:S(2)}, u32[]{:S(2)}) collective-permute-start(f32[72,256]{1,0:T(8,128)S(1)} %get-tuple-element.70), channel_id=1, source_target_pairs={{0,8},{1,9},{2,10},{3,11},{4,12},{5,13},{6,14},{7,15},{8,0},{9,1},... | collective-permute-start | bytes 221192 | tf_op jit(solution)/shard_map/ppermute | solution.py:436
  74.9 7.4 %collective-permute-start.19 = (f32[72,256]{1,0:T(8,128)S(1)}, f32[72,256]{1,0:T(8,128)S(1)}, u32[]{:S(2)}, u32[]{:S(2)}) collective-permute-start(f32[72,256]{1,0:T(8,128)S(1)} %get-tuple-element.71), channel_id=1, source_target_pairs={{0,16},{1,17},{2,18},{3,19},{4,20},{5,21},{6,22},{7,23},{8,24},{9,... | collective-permute-start | bytes 221192 | tf_op jit(solution)/shard_map/ppermute | solution.py:436
  77.2 6.3 %collective-permute-start.20 = (f32[72,256]{1,0:T(8,128)S(1)}, f32[72,256]{1,0:T(8,128)S(1)}, u32[]{:S(2)}, u32[]{:S(2)}) collective-permute-start(f32[72,256]{1,0:T(8,128)S(1)} %get-tuple-element.72), channel_id=1, source_target_pairs={{0,24},{1,25},{2,26},{3,27},{4,28},{5,29},{6,30},{7,31},{8,16},{9,... | collective-permute-start | bytes 221192 | tf_op jit(solution)/shard_map/ppermute | solution.py:436
  79.3 10.2 %all-to-all-start = ((f32[32,1,128]{2,1,0:T(1,128)}), f32[32,1,128]{2,1,0:T(1,128)S(1)}, u32[]{:S(2)}, u32[]{:S(2)}) async-start(f32[32,1,128]{2,1,0:T(1,128)} %get-tuple-element.74), calls=%async_computation | async-start | bytes 32768 | tf_op jit(solution)/shard_map/all_to_all | solution.py:487

commit v7 on v6

--- a/solution.py
+++ b/solution.py
@@ -348,7 +348,9 @@
         g[0:q, :] = total
         g[q:, :] = beta_sums
         raws.append(total / beta - beta * v[0:q, :])
-    sums[...] = jnp.broadcast_to(square_sums(jnp.concatenate(raws, axis=1))[None], sums.shape)
+    line = square_sums(jnp.concatenate(raws, axis=1))
+    for i in range(sums.shape[0]):
+        sums[i] = line
 
 
 def right_norm(docs_total, keep, peer, got, beta_core, messages, token):
@@ -453,12 +455,12 @@
 
     stored, messages = prepare(col_ids.T, col_vals.T, right_vec, left_vec)
     entries = along_z([stored] * 4)
-    messages = along_z([messages[0]] + [after(m, entries[1]) for m in messages[1:]])
+    messages = along_z([messages[0]] + [after(m, *entries[1:]) for m in messages[1:]])
     q = messages[0].shape[0] // 2
 
     rows1, token1 = build(entries, 1)
-    rows0, token0 = build(entries, 0, token1)
-    own = stack(messages, q, "stack_right", token0)
+    rows0, _ = build(entries, 0, token1)
+    own = stack(messages, q, "stack_right", token1)
     own_x = swap(own, X_BIT)
     own_peer = swap(own, CORE_BIT)
     total1 = forward_part(rows1, [own, own_peer], (0, 8))
@@ -474,17 +476,17 @@
     lefts = along_z(lefts)
     both1, beta1 = left_half(product1, swap(product0, Y_BIT), beta0)
     far = swap(backward_part(rows1, both1, 12, 4, partial, beta1, lefts[1:3]), CORE_BIT)
-    left_own = stack(lefts, q, "stack_left")
     near = backward_part(rows1, both1, 4, 4, partial)
     send, beta_core = far_sums(near, far, beta1)
     got = swap(send, X_BIT)
-    peer = swap(backward_part(rows1, both1, 8, 4, partial, None, [left_own]), CORE_BIT)
+    peer = backward_part(rows1, both1, 8, 4, partial)
+    left_own = stack(lefts, q, "stack_left", peer)
+    left_other = swap(left_own, Y_BIT)
     keep = backward_part(rows1, both1, 0, 4, partial)
-    left_other = swap(left_own, Y_BIT)
-
-    sent, sums = right_norm(docs_total, keep, peer, got, beta_core, messages, left_other)
+
+    sent, sums = right_norm(docs_total, keep, swap(peer, CORE_BIT), got, beta_core, messages, left_own)
     pieces = along_z(sent)
-    squares = lax.all_to_all(sums, AXES, 0, 0, tiled=True)
+    squares = lax.all_to_all(after(sums, left_other), AXES, 0, 0, tiled=True)
     left_next, solution_next = left_out(
         docs_total, left_own, left_other, pieces, search_dir, solution_vec, phibar_row, rhobar_row
     )

time: 90.6 us -> 90.2 us (level)
  starting transfers between devices: 35.8 us -> 30.9 us
  waiting for transfers between devices: 24.1 us -> 28.2 us
    ppermute x21, starting transfers between devices: 32.7 us -> 26.8 us  [swap(): return lax.ppermute(value, AXES, [(i, i ^ mask) for i in range(32)])]
    ppermute x21, waiting for transfers between devices: 19.2 us -> 22.4 us  [swap(): return lax.ppermute(value, AXES, [(i, i ^ mask) for i in range(32)])]
    all_to_all x1, starting transfers between devices: 3.04 us -> 4.05 us  [by_columns(): squares = lax.all_to_all(after(sums, left_other), AXES, 0, 0, tiled=True)]
    all_to_all x1, waiting for transfers between devices: 4.9 us -> 5.86 us  [by_columns(): squares = lax.all_to_all(after(sums, left_other), AXES, 0, 0, tiled=True)]
  transfers between devices with their start and end apart: 22 -> 22, of which waited for: 10 -> 11; matrix products, arithmetic and copies ran while one was open for 0% -> 0% of each run, Pallas kernels for 27% -> 28%
where the time goes in v7:
time: 90.2 us; the launch traced here: 90 us
  starting transfers between devices  30.9 us (34%)
  Pallas kernels  29.9 us (33%)
  waiting for transfers between devices  28.2 us (31%)
  between operations  0.92 us (1%)
    ppermute x21, starting transfers between devices, swap(): return lax.ppermute(value, AXES, [(i, i ^ mask) for i in range(32)])  26.8 us
    ppermute x21, waiting for transfers between devices, swap(): return lax.ppermute(value, AXES, [(i, i ^ mask) for i in range(32)])  22.4 us
    pallas_call x2, Pallas kernels, build(): pl.pallas_call(functools.partial(build_kernel, rel), in_specs=[whole()] *...  9.91 us
    pallas_call x4, Pallas kernels, forward_part(): pl.pallas_call(functools.partial(forward_kernel, blocks), in_specs=[whole...  7.12 us
    all_to_all x1, waiting for transfers between devices, by_columns(): squares = lax.all_to_all(after(sums, left_other), AXES, 0, 0, tiled=True)  5.86 us
    pallas_call x5, Pallas kernels, backward_part(): pl.pallas_call(functools.partial(backward_kernel, first, blocks, tuple(ex...  5.23 us
    all_to_all x1, starting transfers between devices, by_columns(): squares = lax.all_to_all(after(sums, left_other), AXES, 0, 0, tiled=True)  4.05 us
    pallas_call x2, Pallas kernels, product_half(): pl.pallas_call(functools.partial(product_kernel, blocks), in_specs=[whole...  2.64 us
  transfers between devices with their start and end apart: 22, of which 11 were waited for; matrix products, arithmetic and copies ran while one was open for 0% of the time, Pallas kernels for 28%

profile of v7, /device:TPU:0, one launch (start us, length us, event | category | flops | bytes accessed | tf_op | source)
XLA Modules:
  0.0 90.0 jit_solution(2915466664730745947)
XLA Ops:
  0.6 1.6 %prepare.1 = (f32[64,256]{1,0:T(8,128)S(1)}, f32[128,256]{1,0:T(8,128)S(1)}, f32[128,256]{1,0:T(8,128)S(1)}, f32[128,256]{1,0:T(8,128)S(1)}, f32[128,256]{1,0:T(8,128)S(1)}) custom-call(s32[16,512]{1,0:T(8,128)} %bitcast.13, bf16[16,512]{1,0:T(8,128)(2,1)} %bitcast.14, f32[256,256]{1,0:T(8,128)} %right.1, f32[512,256]{1,0:T(8,128)} %left_hbm.1), custom_call_target="tpu_custom_call" | custom-call | bytes 1048576 | tf_op jit(solution)/shard_map/prepare/pallas_call | solution.py:74
  2.3 3.1 %collective-permute-start = (f32[64,256]{1,0:T(8,128)S(1)}, f32[64,256]{1,0:T(8,128)S(1)}, u32[]{:S(2)}, u32[]{:S(2)}) collective-permute-start(f32[64,256]{1,0:T(8,128)S(1)} %get-tuple-element.44.e0), channel_id=1, source_target_pairs={{0,8},{1,9},{2,10},{3,11},{4,12},{5,13},{6,14},{7,15},{8,0},{9,1},... | collective-permute-start | bytes 196616 | tf_op jit(solution)/shard_map/ppermute | solution.py:438
  5.4 2.6 %collective-permute-start.1 = (f32[64,256]{1,0:T(8,128)S(1)}, f32[64,256]{1,0:T(8,128)S(1)}, u32[]{:S(2)}, u32[]{:S(2)}) collective-permute-start(f32[64,256]{1,0:T(8,128)S(1)} %get-tuple-element.44.e0), channel_id=1, source_target_pairs={{0,16},{1,17},{2,18},{3,19},{4,20},{5,21},{6,22},{7,23},{8,24},{9,... | collective-permute-start | bytes 196616 | tf_op jit(solution)/shard_map/ppermute | solution.py:438
  8.0 4.7 %collective-permute-done.1.e2 = f32[64,256]{1,0:T(8,128)S(1)} collective-permute-done((f32[64,256]{1,0:T(8,128)S(1)}, f32[64,256]{1,0:T(8,128)S(1)}, u32[]{:S(2)}, u32[]{:S(2)}) %collective-permute-start.1) | collective-permute-done | bytes 65568 | tf_op jit(solution)/shard_map/ppermute | solution.py:438
  12.6 1.4 %collective-permute-done.2.e3 = f32[64,256]{1,0:T(8,128)S(1)} collective-permute-done((f32[64,256]{1,0:T(8,128)S(1)}, f32[64,256]{1,0:T(8,128)S(1)}, u32[]{:S(2)}, u32[]{:S(2)}) %collective-permute-start.2) | collective-permute-done | bytes 65568 | tf_op jit(solution)/shard_map/ppermute | solution.py:438
  14.1 2.3 %collective-permute-start.4 = (f32[128,256]{1,0:T(8,128)S(1)}, f32[128,256]{1,0:T(8,128)S(1)}, u32[]{:S(2)}, u32[]{:S(2)}) collective-permute-start(f32[128,256]{1,0:T(8,128)S(1)} %get-tuple-element.52), channel_id=1, source_target_pairs={{0,16},{1,17},{2,18},{3,19},{4,20},{5,21},{6,22},{7,23},{8,24},{9,... | collective-permute-start | bytes 393224 | tf_op jit(solution)/shard_map/ppermute | solution.py:438
  16.4 2.1 %collective-permute-start.5 = (f32[128,256]{1,0:T(8,128)S(1)}, f32[128,256]{1,0:T(8,128)S(1)}, u32[]{:S(2)}, u32[]{:S(2)}) collective-permute-start(f32[128,256]{1,0:T(8,128)S(1)} %get-tuple-element.54), channel_id=1, source_target_pairs={{0,24},{1,25},{2,26},{3,27},{4,28},{5,29},{6,30},{7,31},{8,16},{9,... | collective-permute-start | bytes 393224 | tf_op jit(solution)/shard_map/ppermute | solution.py:438
  18.4 4.8 %dense_rows.2 = (bf16[16,1024,256]{2,1,0:T(8,128)(2,1)S(1)}, bf16[16,1024,256]{2,1,0:T(8,128)(2,1)S(1)}, f32[8,128]{1,0:T(8,128)S(1)}) custom-call(f32[64,256]{1,0:T(8,128)S(1)} %get-tuple-element.44.e0, f32[64,256]{1,0:T(8,128)S(1)} %collective-permute-done.e1, f32[64,256]{1,0:T(8,128)S(1)} %collective-permute-done.1.e2, ...), custom_call_target="tpu_custom_call" | custom-call | flops 2147483648 | bytes 16777216 | tf_op jit(solution)/shard_map/dense_rows/pallas_call | solution.py:154
  23.2 2.9 %collective-permute-done.4.m2.refs_2_.v2 = f32[128,256]{1,0:T(8,128)S(1)} collective-permute-done((f32[128,256]{1,0:T(8,128)S(1)}, f32[128,256]{1,0:T(8,128)S(1)}, u32[]{:S(2)}, u32[]{:S(2)}) %collective-permute-start.4) | collective-permute-done | bytes 131104 | tf_op jit(solution)/shard_map/ppermute | solution.py:438
  26.1 0.1 collective-permute-start.7
  26.2 5.2 %dense_rows.3 = (bf16[16,1024,256]{2,1,0:T(8,128)(2,1)S(1)}, bf16[16,1024,256]{2,1,0:T(8,128)(2,1)S(1)}, f32[8,128]{1,0:T(8,128)}) custom-call(f32[64,256]{1,0:T(8,128)S(1)} %get-tuple-element.44.e0, f32[64,256]{1,0:T(8,128)S(1)} %collective-permute-done.e1, f32[64,256]{1,0:T(8,128)S(1)} %collective-permute-done.1.e2, ...), custom_call_target="tpu_custom_call" | custom-call | flops 2147483648 | bytes 16777216 | tf_op jit(solution)/shard_map/dense_rows/pallas_call | solution.py:154
  31.4 1.5 %collective-permute-start.6 = (f32[4,64,256]{2,1,0:T(8,128)S(1)}, f32[4,64,256]{2,1,0:T(8,128)S(1)}, u32[]{:S(2)}, u32[]{:S(2)}) collective-permute-start(f32[4,64,256]{2,1,0:T(8,128)S(1)} %stack_right.1.refs_0_), channel_id=1, source_target_pairs={{0,4},{1,5},{2,6},{3,7},{4,0},{5,1},{6,2},{7,3},{8,12},{9,13},{10,... | collective-permute-start | bytes 786440 | tf_op jit(solution)/shard_map/ppermute | solution.py:438
  32.9 2.3 %forward_part.4.refs_1_ = f32[1024,128]{1,0:T(8,128)S(1)} custom-call(bf16[16,1024,256]{2,1,0:T(8,128)(2,1)S(1)} %get-tuple-element.46.hi_ref, bf16[16,1024,256]{2,1,0:T(8,128)(2,1)S(1)} %get-tuple-element.47.lo_ref, f32[4,64,256]{2,1,0:T(8,128)S(1)} %stack_right.1.refs_0_, f32[4,64,256]{2,1,0:T(8,128)S(1)} %collective-permute-done.7.refs_1_), custom_call_target="tpu_custom_call" | custom-call | flops 4294967296 | bytes 8388608 | tf_op jit(solution)/shard_map/forward_part/pallas_call | solution.py:196
  35.2 2.3 %forward_part.5.refs_1_ = f32[1024,128]{1,0:T(8,128)S(1)} custom-call(bf16[16,1024,256]{2,1,0:T(8,128)(2,1)S(1)} %get-tuple-element.55.hi_ref, bf16[16,1024,256]{2,1,0:T(8,128)(2,1)S(1)} %get-tuple-element.56.lo_ref, f32[4,64,256]{2,1,0:T(8,128)S(1)} %stack_right.1.refs_0_, f32[4,64,256]{2,1,0:T(8,128)S(1)} %collective-permute-done.7.refs_1_), custom_call_target="tpu_custom_call" | custom-call | flops 4294967296 | bytes 8388608 | tf_op jit(solution)/shard_map/forward_part/pallas_call | solution.py:196
  37.5 2.5 %collective-permute-done.6.refs_0_ = f32[4,64,256]{2,1,0:T(8,128)S(1)} collective-permute-done((f32[4,64,256]{2,1,0:T(8,128)S(1)}, f32[4,64,256]{2,1,0:T(8,128)S(1)}, u32[]{:S(2)}, u32[]{:S(2)}) %collective-permute-start.6) | collective-permute-done | bytes 262176 | tf_op jit(solution)/shard_map/ppermute | solution.py:438
  40.1 1.2 %forward_part.7.before = f32[1024,128]{1,0:T(8,128)S(1)} custom-call(bf16[16,1024,256]{2,1,0:T(8,128)(2,1)S(1)} %get-tuple-element.55.hi_ref, bf16[16,1024,256]{2,1,0:T(8,128)(2,1)S(1)} %get-tuple-element.56.lo_ref, f32[4,64,256]{2,1,0:T(8,128)S(1)} %collective-permute-done.6.refs_0_, f32[1024,128]{1,0:T(8,128)S(1)} %forward_part.5.refs_1_), custom_call_target="tpu_custom_call" | custom-call | flops 2147483648 | bytes 4194304 | tf_op jit(solution)/shard_map/forward_part/pallas_call | solution.py:196
  41.3 0.3 collective-permute-done.8.vec
  41.6 1.3 %product_half.3.mine = f32[64,1024]{1,0:T(8,128)S(1)} custom-call(bf16[16,1024,256]{2,1,0:T(8,128)(2,1)S(1)} %get-tuple-element.55.hi_ref, bf16[16,1024,256]{2,1,0:T(8,128)(2,1)S(1)} %get-tuple-element.56.lo_ref, f32[4,64,256]{2,1,0:T(8,128)S(1)} %collective-permute-done.8.vec, f32[1024,128]{1,0:T(8,128)S(1)} %forward_part.7.before), custom_call_target="tpu_custom_call" | custom-call | flops 2147483648 | bytes 4194304 | tf_op jit(solution)/shard_map/product_half/pallas_call | solution.py:228
  42.9 1.6 %collective-permute-start.9 = (f32[64,1024]{1,0:T(8,128)S(1)}, f32[64,1024]{1,0:T(8,128)S(1)}, u32[]{:S(2)}, u32[]{:S(2)}) collective-permute-start(f32[64,1024]{1,0:T(8,128)S(1)} %product_half.3.mine), channel_id=1, source_target_pairs={{0,1},{1,0},{2,3},{3,2},{4,5},{5,4},{6,7},{7,6},{8,9},{9,8},{10,11... | collective-permute-start | bytes 786440 | tf_op jit(solution)/shard_map/ppermute | solution.py:438
  44.6 1.2 %forward_part.6.before = f32[1024,128]{1,0:T(8,128)S(1)} custom-call(bf16[16,1024,256]{2,1,0:T(8,128)(2,1)S(1)} %get-tuple-element.46.hi_ref, bf16[16,1024,256]{2,1,0:T(8,128)(2,1)S(1)} %get-tuple-element.47.lo_ref, f32[4,64,256]{2,1,0:T(8,128)S(1)} %collective-permute-done.6.refs_0_, f32[1024,128]{1,0:T(8,128)S(1)} %forward_part.4.refs_1_), custom_call_target="tpu_custom_call" | custom-call | flops 2147483648 | bytes 4194304 | tf_op jit(solution)/shard_map/forward_part/pallas_call | solution.py:196
  45.8 1.3 %product_half.2.mine = f32[64,1024]{1,0:T(8,128)S(1)} custom-call(bf16[16,1024,256]{2,1,0:T(8,128)(2,1)S(1)} %get-tuple-element.46.hi_ref, bf16[16,1024,256]{2,1,0:T(8,128)(2,1)S(1)} %get-tuple-element.47.lo_ref, f32[4,64,256]{2,1,0:T(8,128)S(1)} %collective-permute-done.8.vec, f32[1024,128]{1,0:T(8,128)S(1)} %forward_part.6.before, ...), custom_call_target="tpu_custom_call" | custom-call | flops 2147483648 | bytes 4194304 | tf_op jit(solution)/shard_map/product_half/pallas_call | solution.py:228
  47.1 0.5 collective-permute-start.13
  47.7 4.5 %collective-permute-done.9.other = f32[64,1024]{1,0:T(8,128)S(1)} collective-permute-done((f32[64,1024]{1,0:T(8,128)S(1)}, f32[64,1024]{1,0:T(8,128)S(1)}, u32[]{:S(2)}, u32[]{:S(2)}) %collective-permute-start.9) | collective-permute-done | bytes 262176 | tf_op jit(solution)/shard_map/ppermute | solution.py:438
  52.1 0.1 left_half.2
  52.3 2.0 %collective-permute-start.10 = (f32[64,256]{1,0:T(8,128)S(1)}, f32[64,256]{1,0:T(8,128)S(1)}, u32[]{:S(2)}, u32[]{:S(2)}) collective-permute-start(f32[64,256]{1,0:T(8,128)S(1)} %get-tuple-element.59), channel_id=1, source_target_pairs={{0,8},{1,9},{2,10},{3,11},{4,12},{5,13},{6,14},{7,15},{8,0},{9,1},... | collective-permute-start | bytes 196616 | tf_op jit(solution)/shard_map/ppermute | solution.py:438
  54.3 1.2 %collective-permute-start.11 = (f32[64,256]{1,0:T(8,128)S(1)}, f32[64,256]{1,0:T(8,128)S(1)}, u32[]{:S(2)}, u32[]{:S(2)}) collective-permute-start(f32[64,256]{1,0:T(8,128)S(1)} %get-tuple-element.60), channel_id=1, source_target_pairs={{0,16},{1,17},{2,18},{3,19},{4,20},{5,21},{6,22},{7,23},{8,24},{9,... | collective-permute-start | bytes 196616 | tf_op jit(solution)/shard_map/ppermute | solution.py:438
  55.5 2.3 %backward_part.5.refs_0_ = f32[1024,256]{1,0:T(8,128)S(1)} custom-call(bf16[16,1024,256]{2,1,0:T(8,128)(2,1)S(1)} %get-tuple-element.46.hi_ref, bf16[16,1024,256]{2,1,0:T(8,128)(2,1)S(1)} %get-tuple-element.47.lo_ref, bf16[128,1024]{1,0:T(8,128)(2,1)S(1)} %get-tuple-element.64.both_ref), custom_call_target="tpu_custom_call" | custom-call | flops 8589934592 | bytes 16777216 | tf_op jit(solution)/shard_map/backward_part/pallas_call | solution.py:309
  57.8 0.2 left_half.3
  58.0 2.2 %collective-permute-done.11.m2.refs_3_ = f32[64,256]{1,0:T(8,128)S(1)} collective-permute-done((f32[64,256]{1,0:T(8,128)S(1)}, f32[64,256]{1,0:T(8,128)S(1)}, u32[]{:S(2)}, u32[]{:S(2)}) %collective-permute-start.11) | collective-permute-done | bytes 65568 | tf_op jit(solution)/shard_map/ppermute | solution.py:438
  60.2 0.7 backward_part.9
  60.9 0.1 collective-permute-start.16
  61.0 2.1 %collective-permute-start.12 = (f32[64,256]{1,0:T(8,128)S(1)}, f32[64,256]{1,0:T(8,128)S(1)}, u32[]{:S(2)}, u32[]{:S(2)}) collective-permute-start(f32[64,256]{1,0:T(8,128)S(1)} %get-tuple-element.61), channel_id=1, source_target_pairs={{0,24},{1,25},{2,26},{3,27},{4,28},{5,29},{6,30},{7,31},{8,16},{9,... | collective-permute-start | bytes 196616 | tf_op jit(solution)/shard_map/ppermute | solution.py:438
  63.1 0.7 backward_part.8.near
  63.9 1.5 %collective-permute-start.17 = (f32[264,256]{1,0:T(8,128)S(1)}, f32[264,256]{1,0:T(8,128)S(1)}, u32[]{:S(2)}, u32[]{:S(2)}) collective-permute-start(f32[264,256]{1,0:T(8,128)S(1)} %get-tuple-element.66), channel_id=1, source_target_pairs={{0,4},{1,5},{2,6},{3,7},{4,0},{5,1},{6,2},{7,3},{8,12},{9,13},{10,... | collective-permute-start | bytes 811016 | tf_op jit(solution)/shard_map/ppermute | solution.py:438
  65.4 0.7 backward_part.6.refs_0_
  66.2 0.1 collective-permute-start.15
  66.2 1.1 %collective-permute-done.12.m3 = f32[64,256]{1,0:T(8,128)S(1)} collective-permute-done((f32[64,256]{1,0:T(8,128)S(1)}, f32[64,256]{1,0:T(8,128)S(1)}, u32[]{:S(2)}, u32[]{:S(2)}) %collective-permute-start.12) | collective-permute-done | bytes 65568 | tf_op jit(solution)/shard_map/ppermute | solution.py:438
  67.4 1.6 %collective-permute-start.14 = (f32[4,64,256]{2,1,0:T(8,128)S(1)}, f32[4,64,256]{2,1,0:T(8,128)S(1)}, u32[]{:S(2)}, u32[]{:S(2)}) collective-permute-start(f32[4,64,256]{2,1,0:T(8,128)S(1)} %stack_left.1.token.own), channel_id=1, source_target_pairs={{0,1},{1,0},{2,3},{3,2},{4,5},{5,4},{6,7},{7,6},{8,9},{9,8},{10,11... | collective-permute-start | bytes 786440 | tf_op jit(solution)/shard_map/ppermute | solution.py:438
  69.0 0.7 backward_part.7.keep
  69.7 2.8 %collective-permute-done.17.got = f32[264,256]{1,0:T(8,128)S(1)} collective-permute-done((f32[264,256]{1,0:T(8,128)S(1)}, f32[264,256]{1,0:T(8,128)S(1)}, u32[]{:S(2)}, u32[]{:S(2)}) %collective-permute-start.17) | collective-permute-done | bytes 270368 | tf_op jit(solution)/shard_map/ppermute | solution.py:438
  72.5 0.9 %right_norm.1 = (f32[72,256]{1,0:T(8,128)S(1)}, f32[72,256]{1,0:T(8,128)S(1)}, f32[72,256]{1,0:T(8,128)S(1)}, f32[72,256]{1,0:T(8,128)S(1)}, f32[32,1,128]{2,1,0:T(1,128)}) custom-call(f32[256,256]{1,0:T(8,128)S(1)} %backward_part.7.keep, f32[256,256]{1,0:T(8,128)S(1)} %collective-permute-done.15.peer, f32[264,256]{1,0:T(8,128)S(1)} %collective-permute-done.17.got, ...), custom_call_target="tpu_custom_call" | custom-call | flops 1048576 | bytes 1638400 | tf_op jit(solution)/shard_map/right_norm/pallas_call | solution.py:358
  73.4 2.3 %collective-permute-start.19 = (f32[72,256]{1,0:T(8,128)S(1)}, f32[72,256]{1,0:T(8,128)S(1)}, u32[]{:S(2)}, u32[]{:S(2)}) collective-permute-start(f32[72,256]{1,0:T(8,128)S(1)} %get-tuple-element.70), channel_id=1, source_target_pairs={{0,16},{1,17},{2,18},{3,19},{4,20},{5,21},{6,22},{7,23},{8,24},{9,... | collective-permute-start | bytes 221192 | tf_op jit(solution)/shard_map/ppermute | solution.py:438
  75.8 2.0 %collective-permute-start.20 = (f32[72,256]{1,0:T(8,128)S(1)}, f32[72,256]{1,0:T(8,128)S(1)}, u32[]{:S(2)}, u32[]{:S(2)}) collective-permute-start(f32[72,256]{1,0:T(8,128)S(1)} %get-tuple-element.71), channel_id=1, source_target_pairs={{0,24},{1,25},{2,26},{3,27},{4,28},{5,29},{6,30},{7,31},{8,16},{9,... | collective-permute-start | bytes 221192 | tf_op jit(solution)/shard_map/ppermute | solution.py:438
  77.8 4.0 %all-to-all-start = ((f32[32,1,128]{2,1,0:T(1,128)}), f32[32,1,128]{2,1,0:T(1,128)S(1)}, u32[]{:S(2)}, u32[]{:S(2)}) async-start(f32[32,1,128]{2,1,0:T(1,128)} %get-tuple-element.74), calls=%async_computation | async-start | bytes 32768 | tf_op jit(solution)/shard_map/all_to_all | solution.py:489
  81.9 0.1 collective-permute-done.20.g3
  82.1 1.1 %left_out.1 = (f32[512,256]{1,0:T(8,128)}, f32[256,256]{1,0:T(8,128)}) custom-call(f32[4,64,256]{2,1,0:T(8,128)S(1)} %stack_left.1.token.own, f32[4,64,256]{2,1,0:T(8,128)S(1)} %collective-permute-done.14.other, f32[72,256]{1,0:T(8,128)S(1)} %get-tuple-element.68.g0, f32[72,256]{1,0:T(8,128)S(1)} %collective-permute-done.18.g1, ...), custom_call_target="tpu_custom_call" | custom-call | flops 524288 | bytes 1966080 | tf_op jit(solution)/shard_map/left_out/pallas_call | solution.py:427
  83.1 5.9 %all-to-all-done.squares = f32[32,1,128]{2,1,0:T(1,128)S(1)} async-done(((f32[32,1,128]{2,1,0:T(1,128)}), f32[32,1,128]{2,1,0:T(1,128)S(1)}, u32[]{:S(2)}, u32[]{:S(2)}) %all-to-all-start) | async-done | bytes 16416 | tf_op jit(solution)/shard_map/all_to_all | solution.py:489
  89.0 1.0 %finish.1 = (f32[256,256]{1,0:T(8,128)}, f32[256,256]{1,0:T(8,128)}, f32[1,256]{1,0:T(1,128)}, f32[1,256]{1,0:T(1,128)}, f32[1,256]{1,0:T(1,128)}) custom-call(f32[72,256]{1,0:T(8,128)S(1)} %get-tuple-element.68.g0, f32[72,256]{1,0:T(8,128)S(1)} %collective-permute-done.18.g1, f32[72,256]{1,0:T(8,128)S(1)} %collective-permute-done.19.g2, ...), custom_call_target="tpu_custom_call" | custom-call | flops 1048576 | bytes 1310720 | tf_op jit(solution)/shard_map/finish/pallas_call | solution.py:402
  (30 shorter events, 0.1 us)
Async XLA Ops:
  2.3 5.7 %collective-permute-start = (f32[64,256]{1,0:T(8,128)S(1)}, f32[64,256]{1,0:T(8,128)S(1)}, u32[]{:S(2)}, u32[]{:S(2)}) collective-permute-start(f32[64,256]{1,0:T(8,128)S(1)} %get-tuple-element.44.e0), channel_id=1, source_target_pairs={{0,8},{1,9},{2,10},{3,11},{4,12},{5,13},{6,14},{7,15},{8,0},{9,1},... | collective-permute-start | bytes 196616 | tf_op jit(solution)/shard_map/ppermute | solution.py:438
  5.4 7.3 %collective-permute-start.1 = (f32[64,256]{1,0:T(8,128)S(1)}, f32[64,256]{1,0:T(8,128)S(1)}, u32[]{:S(2)}, u32[]{:S(2)}) collective-permute-start(f32[64,256]{1,0:T(8,128)S(1)} %get-tuple-element.44.e0), channel_id=1, source_target_pairs={{0,16},{1,17},{2,18},{3,19},{4,20},{5,21},{6,22},{7,23},{8,24},{9,... | collective-permute-start | bytes 196616 | tf_op jit(solution)/shard_map/ppermute | solution.py:438
  8.0 6.1 %collective-permute-start.2 = (f32[64,256]{1,0:T(8,128)S(1)}, f32[64,256]{1,0:T(8,128)S(1)}, u32[]{:S(2)}, u32[]{:S(2)}) collective-permute-start(f32[64,256]{1,0:T(8,128)S(1)} %get-tuple-element.44.e0), channel_id=1, source_target_pairs={{0,24},{1,25},{2,26},{3,27},{4,28},{5,29},{6,30},{7,31},{8,16},{9,... | collective-permute-start | bytes 196616 | tf_op jit(solution)/shard_map/ppermute | solution.py:438
  14.1 9.2 %collective-permute-start.3 = (f32[128,256]{1,0:T(8,128)S(1)}, f32[128,256]{1,0:T(8,128)S(1)}, u32[]{:S(2)}, u32[]{:S(2)}) collective-permute-start(f32[128,256]{1,0:T(8,128)S(1)} %get-tuple-element.50), channel_id=1, source_target_pairs={{0,8},{1,9},{2,10},{3,11},{4,12},{5,13},{6,14},{7,15},{8,0},{9,1},... | collective-permute-start | bytes 393224 | tf_op jit(solution)/shard_map/ppermute | solution.py:438
  14.1 12.0 %collective-permute-start.4 = (f32[128,256]{1,0:T(8,128)S(1)}, f32[128,256]{1,0:T(8,128)S(1)}, u32[]{:S(2)}, u32[]{:S(2)}) collective-permute-start(f32[128,256]{1,0:T(8,128)S(1)} %get-tuple-element.52), channel_id=1, source_target_pairs={{0,16},{1,17},{2,18},{3,19},{4,20},{5,21},{6,22},{7,23},{8,24},{9,... | collective-permute-start | bytes 393224 | tf_op jit(solution)/shard_map/ppermute | solution.py:438
  16.4 9.7 %collective-permute-start.5 = (f32[128,256]{1,0:T(8,128)S(1)}, f32[128,256]{1,0:T(8,128)S(1)}, u32[]{:S(2)}, u32[]{:S(2)}) collective-permute-start(f32[128,256]{1,0:T(8,128)S(1)} %get-tuple-element.54), channel_id=1, source_target_pairs={{0,24},{1,25},{2,26},{3,27},{4,28},{5,29},{6,30},{7,31},{8,16},{9,... | collective-permute-start | bytes 393224 | tf_op jit(solution)/shard_map/ppermute | solution.py:438
  26.1 6.8 %collective-permute-start.7 = (f32[4,64,256]{2,1,0:T(8,128)S(1)}, f32[4,64,256]{2,1,0:T(8,128)S(1)}, u32[]{:S(2)}, u32[]{:S(2)}) collective-permute-start(f32[4,64,256]{2,1,0:T(8,128)S(1)} %stack_right.1.refs_0_), channel_id=1, source_target_pairs={{0,2},{1,3},{2,0},{3,1},{4,6},{5,7},{6,4},{7,5},{8,10},{9,11},{10,... | collective-permute-start | bytes 786440 | tf_op jit(solution)/shard_map/ppermute | solution.py:438
  31.4 8.7 %collective-permute-start.6 = (f32[4,64,256]{2,1,0:T(8,128)S(1)}, f32[4,64,256]{2,1,0:T(8,128)S(1)}, u32[]{:S(2)}, u32[]{:S(2)}) collective-permute-start(f32[4,64,256]{2,1,0:T(8,128)S(1)} %stack_right.1.refs_0_), channel_id=1, source_target_pairs={{0,4},{1,5},{2,6},{3,7},{4,0},{5,1},{6,2},{7,3},{8,12},{9,13},{10,... | collective-permute-start | bytes 786440 | tf_op jit(solution)/shard_map/ppermute | solution.py:438
  40.1 1.5 %collective-permute-start.8 = (f32[4,64,256]{2,1,0:T(8,128)S(1)}, f32[4,64,256]{2,1,0:T(8,128)S(1)}, u32[]{:S(2)}, u32[]{:S(2)}) collective-permute-start(f32[4,64,256]{2,1,0:T(8,128)S(1)} %collective-permute-done.6.refs_0_), channel_id=1, source_target_pairs={{0,2},{1,3},{2,0},{3,1},{4,6},{5,7},{6,4},{7,5},{8,10},{9,11},{10,... | collective-permute-start | bytes 786440 | tf_op jit(solution)/shard_map/ppermute | solution.py:438
  42.9 2.9 %copy-start.5 = (f32[256]{0:T(256)S(1)}, f32[256]{0:T(256)}, u32[]{:S(2)}) copy-start(f32[256]{0:T(256)} %param.15) | copy-start | bytes 3076
  42.9 9.2 %collective-permute-start.9 = (f32[64,1024]{1,0:T(8,128)S(1)}, f32[64,1024]{1,0:T(8,128)S(1)}, u32[]{:S(2)}, u32[]{:S(2)}) collective-permute-start(f32[64,1024]{1,0:T(8,128)S(1)} %product_half.3.mine), channel_id=1, source_target_pairs={{0,1},{1,0},{2,3},{3,2},{4,5},{5,4},{6,7},{7,6},{8,9},{9,8},{10,11... | collective-permute-start | bytes 786440 | tf_op jit(solution)/shard_map/ppermute | solution.py:438
  47.1 10.7 %collective-permute-start.13 = (f32[64,1024]{1,0:T(8,128)S(1)}, f32[64,1024]{1,0:T(8,128)S(1)}, u32[]{:S(2)}, u32[]{:S(2)}) collective-permute-start(f32[64,1024]{1,0:T(8,128)S(1)} %product_half.2.mine), channel_id=1, source_target_pairs={{0,1},{1,0},{2,3},{3,2},{4,5},{5,4},{6,7},{7,6},{8,9},{9,8},{10,11... | collective-permute-start | bytes 786440 | tf_op jit(solution)/shard_map/ppermute | solution.py:438
  52.3 5.7 %collective-permute-start.10 = (f32[64,256]{1,0:T(8,128)S(1)}, f32[64,256]{1,0:T(8,128)S(1)}, u32[]{:S(2)}, u32[]{:S(2)}) collective-permute-start(f32[64,256]{1,0:T(8,128)S(1)} %get-tuple-element.59), channel_id=1, source_target_pairs={{0,8},{1,9},{2,10},{3,11},{4,12},{5,13},{6,14},{7,15},{8,0},{9,1},... | collective-permute-start | bytes 196616 | tf_op jit(solution)/shard_map/ppermute | solution.py:438
  54.3 5.9 %collective-permute-start.11 = (f32[64,256]{1,0:T(8,128)S(1)}, f32[64,256]{1,0:T(8,128)S(1)}, u32[]{:S(2)}, u32[]{:S(2)}) collective-permute-start(f32[64,256]{1,0:T(8,128)S(1)} %get-tuple-element.60), channel_id=1, source_target_pairs={{0,16},{1,17},{2,18},{3,19},{4,20},{5,21},{6,22},{7,23},{8,24},{9,... | collective-permute-start | bytes 196616 | tf_op jit(solution)/shard_map/ppermute | solution.py:438
  60.9 2.9 %collective-permute-start.16 = (f32[264,256]{1,0:T(8,128)S(1)}, f32[264,256]{1,0:T(8,128)S(1)}, u32[]{:S(2)}, u32[]{:S(2)}) collective-permute-start(f32[264,256]{1,0:T(8,128)S(1)} %backward_part.9), channel_id=1, source_target_pairs={{0,2},{1,3},{2,0},{3,1},{4,6},{5,7},{6,4},{7,5},{8,10},{9,11},{10,... | collective-permute-start | bytes 811016 | tf_op jit(solution)/shard_map/ppermute | solution.py:438
  61.0 6.3 %collective-permute-start.12 = (f32[64,256]{1,0:T(8,128)S(1)}, f32[64,256]{1,0:T(8,128)S(1)}, u32[]{:S(2)}, u32[]{:S(2)}) collective-permute-start(f32[64,256]{1,0:T(8,128)S(1)} %get-tuple-element.61), channel_id=1, source_target_pairs={{0,24},{1,25},{2,26},{3,27},{4,28},{5,29},{6,30},{7,31},{8,16},{9,... | collective-permute-start | bytes 196616 | tf_op jit(solution)/shard_map/ppermute | solution.py:438
  63.9 8.6 %collective-permute-start.17 = (f32[264,256]{1,0:T(8,128)S(1)}, f32[264,256]{1,0:T(8,128)S(1)}, u32[]{:S(2)}, u32[]{:S(2)}) collective-permute-start(f32[264,256]{1,0:T(8,128)S(1)} %get-tuple-element.66), channel_id=1, source_target_pairs={{0,4},{1,5},{2,6},{3,7},{4,0},{5,1},{6,2},{7,3},{8,12},{9,13},{10,... | collective-permute-start | bytes 811016 | tf_op jit(solution)/shard_map/ppermute | solution.py:438
  66.2 3.6 %collective-permute-start.15 = (f32[256,256]{1,0:T(8,128)S(1)}, f32[256,256]{1,0:T(8,128)S(1)}, u32[]{:S(2)}, u32[]{:S(2)}) collective-permute-start(f32[256,256]{1,0:T(8,128)S(1)} %backward_part.6.refs_0_), channel_id=1, source_target_pairs={{0,2},{1,3},{2,0},{3,1},{4,6},{5,7},{6,4},{7,5},{8,10},{9,11},{10,... | collective-permute-start | bytes 786440 | tf_op jit(solution)/shard_map/ppermute | solution.py:438
  67.3 14.7 %copy-start.1 = (f32[256,256]{1,0:T(8,128)S(1)}, f32[256,256]{1,0:T(8,128)}, u32[]{:S(2)}) copy-start(f32[256,256]{1,0:T(8,128)} %search.3) | copy-start | bytes 786436
  67.3 14.7 %copy-start.2 = (f32[256,256]{1,0:T(8,128)S(1)}, f32[256,256]{1,0:T(8,128)}, u32[]{:S(2)}) copy-start(f32[256,256]{1,0:T(8,128)} %solution.1) | copy-start | bytes 786436
  67.3 14.7 %copy-start.3 = (f32[256]{0:T(256)S(1)}, f32[256]{0:T(256)}, u32[]{:S(2)}) copy-start(f32[256]{0:T(256)} %param.16) | copy-start | bytes 3076
  67.4 14.7 %copy-start.4 = (f32[256]{0:T(256)S(1)}, f32[256]{0:T(256)}, u32[]{:S(2)}) copy-start(f32[256]{0:T(256)} %param.17) | copy-start | bytes 3076
  67.4 21.6 %copy-start = (f32[256,256]{1,0:T(8,128)S(1)}, f32[256,256]{1,0:T(8,128)}, u32[]{:S(2)}) copy-start(f32[256,256]{1,0:T(8,128)} %right.1) | copy-start | bytes 786436
  67.4 10.5 %collective-permute-start.14 = (f32[4,64,256]{2,1,0:T(8,128)S(1)}, f32[4,64,256]{2,1,0:T(8,128)S(1)}, u32[]{:S(2)}, u32[]{:S(2)}) collective-permute-start(f32[4,64,256]{2,1,0:T(8,128)S(1)} %stack_left.1.token.own), channel_id=1, source_target_pairs={{0,1},{1,0},{2,3},{3,2},{4,5},{5,4},{6,7},{7,6},{8,9},{9,8},{10,11... | collective-permute-start | bytes 786440 | tf_op jit(solution)/shard_map/ppermute | solution.py:438
  73.4 8.4 %collective-permute-start.18 = (f32[72,256]{1,0:T(8,128)S(1)}, f32[72,256]{1,0:T(8,128)S(1)}, u32[]{:S(2)}, u32[]{:S(2)}) collective-permute-start(f32[72,256]{1,0:T(8,128)S(1)} %get-tuple-element.69), channel_id=1, source_target_pairs={{0,8},{1,9},{2,10},{3,11},{4,12},{5,13},{6,14},{7,15},{8,0},{9,1},... | collective-permute-start | bytes 221192 | tf_op jit(solution)/shard_map/ppermute | solution.py:438
  73.4 8.5 %collective-permute-start.19 = (f32[72,256]{1,0:T(8,128)S(1)}, f32[72,256]{1,0:T(8,128)S(1)}, u32[]{:S(2)}, u32[]{:S(2)}) collective-permute-start(f32[72,256]{1,0:T(8,128)S(1)} %get-tuple-element.70), channel_id=1, source_target_pairs={{0,16},{1,17},{2,18},{3,19},{4,20},{5,21},{6,22},{7,23},{8,24},{9,... | collective-permute-start | bytes 221192 | tf_op jit(solution)/shard_map/ppermute | solution.py:438
  75.8 6.3 %collective-permute-start.20 = (f32[72,256]{1,0:T(8,128)S(1)}, f32[72,256]{1,0:T(8,128)S(1)}, u32[]{:S(2)}, u32[]{:S(2)}) collective-permute-start(f32[72,256]{1,0:T(8,128)S(1)} %get-tuple-element.71), channel_id=1, source_target_pairs={{0,24},{1,25},{2,26},{3,27},{4,28},{5,29},{6,30},{7,31},{8,16},{9,... | collective-permute-start | bytes 221192 | tf_op jit(solution)/shard_map/ppermute | solution.py:438
  77.8 11.2 %all-to-all-start = ((f32[32,1,128]{2,1,0:T(1,128)}), f32[32,1,128]{2,1,0:T(1,128)S(1)}, u32[]{:S(2)}, u32[]{:S(2)}) async-start(f32[32,1,128]{2,1,0:T(1,128)} %get-tuple-element.74), calls=%async_computation | async-start | bytes 32768 | tf_op jit(solution)/shard_map/all_to_all | solution.py:489

commit v8 on v7

--- a/solution.py
+++ b/solution.py
@@ -10,9 +10,11 @@
 epsilon = 1e-06
 AXES = ("doc", "feat")
 MIB = 1024 * 1024
-
-
-Y_BIT, CORE_BIT, X_BIT, Z_SHIFT = 1, 2, 4, 3
+SCALE = 64
+
+
+Y_BIT, CORE_BIT, X_BIT = 1, 2, 4
+Z_LINES = [[z * 8 + i for z in range(4)] for i in range(8)]
 NT = (((1,), (1,)), ((), ()))
 
 
@@ -27,7 +29,7 @@
 
 
 def cost(flops, nbytes):
-    return pl.CostEstimate(flops=int(flops), bytes_accessed=int(nbytes), transcendentals=0)
+    return pl.CostEstimate(flops=int(flops) // SCALE, bytes_accessed=int(nbytes) // SCALE, transcendentals=0)
 
 
 def f32(*shape):
@@ -38,10 +40,9 @@
     return jax.ShapeDtypeStruct(shape, jnp.bfloat16)
 
 
-def prepare_kernel(ids_hbm, vals_hbm, right_hbm, left_hbm, stored, m0, m1, m2, m3,
-                   ids, vals, wide, right, left, turned, arrived):
-    _, z, y = coords()
-    q, rows = turned.shape[1:]
+def entries_kernel(ids_hbm, vals_hbm, right_hbm, left_hbm, stored, right, left, ids, vals, wide, arrived):
+    _, _, y = coords()
+    rows = left.shape[0]
     copies = [
         pltpu.make_async_copy(src, dst, arrived.at[i])
         for i, (src, dst) in enumerate((
@@ -53,7 +54,8 @@
     ]
     for copy in copies:
         copy.start()
-    lines, count = stored.shape[0] // 2, ids.shape[0]
+    count = ids.shape[0]
+    lines = ids.shape[1] * count // 256
     for part, ref in enumerate((ids, vals)):
         copies[part].wait()
         wide[...] = ref[...].astype(jnp.float32).T
@@ -61,59 +63,70 @@
             stored[part * lines : (part + 1) * lines, r * count : (r + 1) * count] = wide[
                 pl.ds(r, lines, stride=256 // count), :
             ]
-    for part, ref in enumerate((right, left)):
-        copies[2 + part].wait()
-        turned[...] = ref[...].T.reshape(turned.shape)
-        for k, out in enumerate((m0, m1, m2, m3)):
-            out[part * q : (part + 1) * q, :] = turned[z ^ k]
-
-
-def prepare(ids, vals, right, left):
-    rows, cols = right.shape
-    q = cols // 4
-    got = pl.pallas_call(
-        prepare_kernel,
+    for z in range(1, 4):
+        stored[z * 2 * lines : (z + 1) * 2 * lines, :] = stored[0 : 2 * lines, :]
+    copies[2].wait()
+    copies[3].wait()
+
+
+def entries_of(ids, vals, right, left):
+    return pl.pallas_call(
+        entries_kernel,
         in_specs=[pl.BlockSpec(memory_space=pltpu.HBM)] * 4,
-        out_specs=[whole()] * 5,
-        out_shape=[pltpu.VMEM((ids.size // 128, 256), jnp.float32)] + [pltpu.VMEM((2 * q, rows), jnp.float32)] * 4,
+        out_specs=[whole()] * 3,
+        out_shape=[
+            pltpu.VMEM((4 * ids.size // 128, 256), jnp.float32),
+            pltpu.VMEM(right.shape, jnp.float32),
+            pltpu.VMEM(right.shape, jnp.float32),
+        ],
         scratch_shapes=[
             pltpu.VMEM(ids.shape, jnp.int32),
             pltpu.VMEM(vals.shape, jnp.bfloat16),
             pltpu.VMEM(ids.shape[::-1], jnp.float32),
-            pltpu.VMEM(right.shape, jnp.float32),
-            pltpu.VMEM(right.shape, jnp.float32),
-            pltpu.VMEM((4, q, rows), jnp.float32),
             pltpu.SemaphoreType.DMA((4,)),
         ],
         compiler_params=params(60),
-        cost_estimate=cost(0, rows * cols * 16),
-        name="prepare",
+        cost_estimate=cost(0, right.size * 16),
+        name="entries",
     )(ids, vals, right, left)
-    return got[0], got[1:]
-
-
-def stack_kernel(m0, m1, m2, m3, *refs):
-    out = refs[-1]
-    for k, m in enumerate((m0, m1, m2, m3)):
-        out[k] = m[0 : out.shape[1], :]
-
-
-def stack(messages, q, name, *tokens):
-    rows = messages[0].shape[1]
-    return pl.pallas_call(
-        stack_kernel,
-        out_shape=f32(4, q, rows),
-        compiler_params=params(8),
-        cost_estimate=cost(0, 32 * q * rows),
+
+
+def turn_kernel(ref, token, out):
+    out[...] = ref[...].T
+
+
+def turn(value, token, name):
+    return pl.pallas_call(
+        turn_kernel,
+        out_shape=f32(*value.shape[::-1]),
+        compiler_params=params(8),
+        cost_estimate=cost(0, value.size * 8),
         name=name,
-    )(*messages, *tokens)
-
-
-def build_kernel(rel, e0, e1, e2, e3, *refs):
+    )(value, token)
+
+
+def relative_kernel(ref, token, out):
+    _, z, _ = coords()
+    q = out.shape[1]
+    for k in range(4):
+        out[k] = ref[pl.ds(pl.multiple_of((z ^ k) * q, q), q), :]
+
+
+def relative(value, token, name):
+    return pl.pallas_call(
+        relative_kernel,
+        out_shape=f32(4, value.shape[0] // 4, value.shape[1]),
+        compiler_params=params(8),
+        cost_estimate=cost(0, value.size * 8),
+        name=name,
+    )(value, token)
+
+
+def build_kernel(rel, entries, *refs):
     hi_ref, lo_ref, token = refs[-3:]
     token[...] = jnp.zeros_like(token)
-    d, _, y = coords()
-    n = e0.shape[0] // 2
+    d, z, y = coords()
+    n = entries.shape[0] // 8
     iota = lax.broadcasted_iota(jnp.int32, (256, 256), 0).astype(jnp.float32).astype(jnp.bfloat16)
     lane_doc = lax.broadcasted_iota(jnp.int32, (8, 256), 1) >> 4
     one = jnp.ones((256, 256), jnp.bfloat16)
@@ -123,11 +136,11 @@
         wide = jnp.broadcast_to(row, (16, 256)).astype(jnp.bfloat16)
         return jnp.broadcast_to(wide[None], (16, 16, 256)).reshape(256, 256)
 
-    for k, entries in enumerate((e0, e1, e2, e3)):
+    for k in range(4):
 
         @pl.loop(0, n // 16)
-        def _(step, k=k, entries=entries):
-            at = pl.multiple_of((y ^ rel) * (n // 2) + step * 8, 8)
+        def _(step, k=k):
+            at = pl.multiple_of((z ^ k) * 2 * n + (y ^ rel) * (n // 2) + step * 8, 8)
             ids = entries[pl.ds(at, 8), :].astype(jnp.int32)
             vals = entries[pl.ds(n + at, 8), :]
             owner = (ids >> 8) ^ d
@@ -150,16 +163,16 @@
 
 
 def build(entries, rel, *tokens):
-    docs = 4 * (entries[0].shape[0] // 4 * 16)
+    docs = entries.shape[0] // 4 * 16
     *rows, token = pl.pallas_call(
         functools.partial(build_kernel, rel),
-        in_specs=[whole()] * (4 + len(tokens)),
+        in_specs=[whole()] * (1 + len(tokens)),
         out_specs=[whole()] * 3,
         out_shape=[pltpu.VMEM((16, docs, 256), jnp.bfloat16)] * 2 + [f32(8, 128)],
         compiler_params=params(8),
         cost_estimate=cost(2 * docs * 16 * 256 * 256, docs * 4096 * 4),
         name="dense_rows",
-    )(*entries, *tokens)
+    )(entries, *tokens)
     return rows, token
 
 
@@ -215,12 +228,13 @@
         out[...] = product
         return
     _, z, _ = coords()
-    *messages, alpha = refs[:5]
+    left, alpha = refs[:2]
     columns[...] = row_to_column(alpha[...])
     scale = columns[pl.ds(pl.multiple_of(z * q, q), q), :][:, 0:1]
-    for k, m in enumerate(messages):
-        at = slice(k * m.shape[1], (k + 1) * m.shape[1])
-        out[:, at] = product[:, at] - scale * m[q:, :]
+    n = left.shape[1]
+    for k in range(4):
+        at = slice(k * n, (k + 1) * n)
+        out[:, at] = product[:, at] - scale * left[pl.ds(pl.multiple_of((z ^ k) * q, q), q), :]
 
 
 def product_half(rows, vec, before, blocks, *left):
@@ -256,25 +270,25 @@
     return jnp.broadcast_to(row, (128, row.shape[1])).T
 
 
-def left_half_kernel(mine, other, *refs):
+def left_half_kernel(pieces, mine, other, *refs):
     _, z, _ = coords()
     left = mine[...] + other[...]
     both, sums = refs[-2:]
     both[...] = split_rows(left)
     squares = square_row(left, z, sums.shape[1])
-    sums[...] = refs[0][...] + squares if len(refs) == 3 else squares
-    if len(refs) > 3:
-        n = left.shape[1] // 4
-        for k, out in enumerate(refs[:4]):
-            out[...] = left[:, k * n : (k + 1) * n]
+    sums[...] = squares if pieces else refs[0][...] + squares
+    if pieces:
+        q, n = left.shape[0], left.shape[1] // 4
+        for k in range(4):
+            refs[0][pl.ds(pl.multiple_of((z ^ k) * q, q), q), :] = left[:, k * n : (k + 1) * n]
 
 
 def left_half(mine, other, squares=None):
     q, docs = mine.shape
     extra = [] if squares is None else [squares]
-    pieces = [f32(q, docs // 4)] * 4 if squares is None else []
-    return pl.pallas_call(
-        left_half_kernel,
+    pieces = [f32(4 * q, docs // 4)] if squares is None else []
+    return pl.pallas_call(
+        functools.partial(left_half_kernel, bool(pieces)),
         out_shape=pieces + [bf16(2 * q, docs), f32(8, 4 * q)],
         compiler_params=params(8),
         cost_estimate=cost(8 * q * docs, 16 * q * docs),
@@ -335,56 +349,53 @@
     )(near, far, beta)
 
 
-def right_norm_kernel(docs_total, keep, peer, got, beta_core, v0, v1, v2, v3, token, g0, g1, g2, g3, sums, columns):
+def right_norm_kernel(docs_total, keep, peer, got, beta_core, right, out, sums, columns):
     _, z, _ = coords()
-    q = g0.shape[0] - 8
+    q = right.shape[1]
     beta_sums = beta_core[...] + got[4 * q :, :]
     columns[...] = row_to_column(jnp.sqrt(beta_sums[0:1, :] / docs_total + epsilon))
     beta = columns[pl.ds(pl.multiple_of(z * q, q), q), :][:, 0:1]
     raws = []
-    for k, (v, g) in enumerate(zip((v0, v1, v2, v3), (g0, g1, g2, g3))):
+    for k in range(4):
         rows = slice(k * q, (k + 1) * q)
         total = (keep[rows, :] + peer[rows, :]) + got[rows, :]
-        g[0:q, :] = total
-        g[q:, :] = beta_sums
-        raws.append(total / beta - beta * v[0:q, :])
+        at = (z ^ k) * (q + 8)
+        out[pl.ds(pl.multiple_of(at, 8), q), :] = total
+        out[pl.ds(pl.multiple_of(at + q, 8), 8), :] = beta_sums
+        raws.append(total / beta - beta * right[k])
     line = square_sums(jnp.concatenate(raws, axis=1))
     for i in range(sums.shape[0]):
         sums[i] = line
 
 
-def right_norm(docs_total, keep, peer, got, beta_core, messages, token):
+def right_norm(docs_total, keep, peer, got, beta_core, right):
     q, rows = keep.shape[0] // 4, keep.shape[1]
-    *pieces, sums = pl.pallas_call(
+    return pl.pallas_call(
         functools.partial(right_norm_kernel, docs_total),
-        out_shape=[f32(q + 8, rows)] * 4 + [f32(32, 1, 128)],
+        out_shape=[f32(4 * (q + 8), rows), f32(32, 1, 128)],
         scratch_shapes=[pltpu.VMEM((4 * q, 128), jnp.float32)],
         compiler_params=params(8),
         cost_estimate=cost(rows * q * 64, rows * q * 100),
         name="right_norm",
-    )(keep, peer, got, beta_core, *messages, token)
-    return pieces, sums
+    )(keep, peer, got, beta_core, right)
 
 
 def beta_of(pieces, q, docs_total):
-    squares = [g[q : q + 1, :] for g in pieces]
+    squares = [pieces[k * (q + 8) + q : k * (q + 8) + q + 1, :] for k in range(4)]
     return jnp.sqrt(((squares[0] + squares[1]) + (squares[2] + squares[3])) / docs_total + epsilon)
 
 
-def finish_kernel(docs_total, feat_total, g0, g1, g2, g3, squares, right, search, phibar, rhobar,
-                  right_out, search_out, alpha_out, phibar_out, rhobar_out, turned):
-    _, z, _ = coords()
-    q = turned.shape[1]
-    for k, g in enumerate((g0, g1, g2, g3)):
-        turned[z ^ k] = g[0:q, :]
-    got = turned[...].reshape(-1, turned.shape[2]).T
+def finish_kernel(docs_total, feat_total, pieces, squares, right, search, phibar, rhobar,
+                  right_out, search_out, alpha_out, phibar_out, rhobar_out):
+    q = right.shape[1] // 4
+    got = jnp.concatenate([pieces[k * (q + 8) : k * (q + 8) + q, :] for k in range(4)], axis=0).T
     parts = [squares[i] for i in range(32)]
     while len(parts) > 4:
         parts = [a + b for a, b in zip(parts[::2], parts[1::2])]
     low = lax.broadcasted_iota(jnp.int32, parts[0].shape, 1) < q
     parts = [jnp.where(low, parts[0], parts[1]), jnp.where(low, parts[2], parts[3])]
     alpha = jnp.sqrt(jnp.concatenate(parts, axis=1) / feat_total + epsilon)
-    beta = beta_of((g0, g1, g2, g3), q, docs_total)
+    beta = beta_of(pieces, q, docs_total)
     rho = jnp.sqrt(rhobar[...] * rhobar[...] + beta * beta)
     cosine = rhobar[...] / rho
     sine = beta / rho
@@ -402,44 +413,40 @@
     return pl.pallas_call(
         functools.partial(finish_kernel, docs_total, feat_total),
         out_shape=[f32(rows, cols)] * 2 + [f32(1, cols)] * 3,
-        scratch_shapes=[pltpu.VMEM((4, cols // 4, rows), jnp.float32)],
         compiler_params=params(8),
         cost_estimate=cost(rows * cols * 16, rows * cols * 20),
         name="finish",
-    )(*pieces, squares, right, search, phibar, rhobar)
-
-
-def left_out_kernel(docs_total, own, other, g0, g1, g2, g3, search, solution, phibar, rhobar, left_out, solution_out, turned):
-    _, z, y = coords()
-    q, half = turned.shape[1:]
-    beta = beta_of((g0, g1, g2, g3), q, docs_total)
+    )(pieces, squares, right, search, phibar, rhobar)
+
+
+def left_out_kernel(docs_total, own, other, pieces, search, solution, phibar, rhobar, left_out, solution_out):
+    _, _, y = coords()
+    cols, half = own.shape
+    beta = beta_of(pieces, cols // 4, docs_total)
     for part, ref in ((y, own), (1 - y, other)):
-        for k in range(4):
-            turned[z ^ k] = ref[k]
-        left_out[pl.ds(pl.multiple_of(part * half, half), half), :] = turned[...].reshape(-1, half).T / beta
+        left_out[pl.ds(pl.multiple_of(part * half, half), half), :] = ref[...].T / beta
     rho = jnp.sqrt(rhobar[...] * rhobar[...] + beta * beta)
     phi = rhobar[...] / rho * phibar[...]
     solution_out[...] = solution[...] + (phi / rho) * search[...]
 
 
 def left_out(docs_total, own, other, pieces, search, solution, phibar, rhobar):
-    _, q, half = own.shape
+    cols, half = own.shape
     return pl.pallas_call(
         functools.partial(left_out_kernel, docs_total),
-        out_shape=[f32(2 * half, 4 * q), f32(*solution.shape)],
-        scratch_shapes=[pltpu.VMEM((4, q, half), jnp.float32)],
-        compiler_params=params(8),
-        cost_estimate=cost(half * q * 32, half * q * 120),
+        out_shape=[f32(2 * half, cols), f32(*solution.shape)],
+        compiler_params=params(8),
+        cost_estimate=cost(half * cols * 8, half * cols * 30),
         name="left_out",
-    )(own, other, *pieces, search, solution, phibar, rhobar)
+    )(own, other, pieces, search, solution, phibar, rhobar)
 
 
 def swap(value, mask):
     return lax.ppermute(value, AXES, [(i, i ^ mask) for i in range(32)])
 
 
-def along_z(values):
-    return [values[0]] + [swap(values[k], k << Z_SHIFT) for k in (1, 2, 3)]
+def along_z(value):
+    return lax.all_to_all(value, AXES, 0, 0, axis_index_groups=Z_LINES, tiled=True)
 
 
 def after(value, *earlier):
@@ -453,38 +460,38 @@
     feat_total = right_vec.shape[0] * 32
     alpha_row, phibar_row, rhobar_row = (v.reshape(1, -1) for v in (alpha_prev, phibar, rhobar))
 
-    stored, messages = prepare(col_ids.T, col_vals.T, right_vec, left_vec)
-    entries = along_z([stored] * 4)
-    messages = along_z([messages[0]] + [after(m, *entries[1:]) for m in messages[1:]])
-    q = messages[0].shape[0] // 2
+    stored, right_here, left_here = entries_of(col_ids.T, col_vals.T, right_vec, left_vec)
+    entries = along_z(stored)
+    right_turned = turn(right_here, stored, "turn_right")
+    right_line = along_z(right_turned)
+    left_line = along_z(turn(left_here, right_turned, "turn_left"))
 
     rows1, token1 = build(entries, 1)
-    rows0, _ = build(entries, 0, token1)
-    own = stack(messages, q, "stack_right", token1)
+    own = relative(right_line, token1, "relative_right")
     own_x = swap(own, X_BIT)
     own_peer = swap(own, CORE_BIT)
+    rows0, _ = build(entries, 0, own)
     total1 = forward_part(rows1, [own, own_peer], (0, 8))
     total0 = forward_part(rows0, [own, own_peer], (0, 8))
-    x_peer = swap(after(own_x, total0, total1), CORE_BIT)
+    x_peer = swap(own_x, CORE_BIT)
     total1 = forward_part(rows1, [own_x], (4,), total1)
     total0 = forward_part(rows0, [own_x], (4,), total0)
     product1 = product_half(rows1, x_peer, total1, (12,))
-    product0 = product_half(rows0, x_peer, total0, (12,), *messages, alpha_row)
-
-    *lefts, both0, beta0 = left_half(product0, swap(product1, Y_BIT))
+    product0 = product_half(rows0, x_peer, total0, (12,), left_line, alpha_row)
+
+    lefts, both0, beta0 = left_half(product0, swap(product1, Y_BIT))
     partial = backward_part(rows0, both0, 0, 16)
-    lefts = along_z(lefts)
+    left_own = along_z(lefts)
     both1, beta1 = left_half(product1, swap(product0, Y_BIT), beta0)
-    far = swap(backward_part(rows1, both1, 12, 4, partial, beta1, lefts[1:3]), CORE_BIT)
+    far = swap(backward_part(rows1, both1, 12, 4, partial, beta1), CORE_BIT)
     near = backward_part(rows1, both1, 4, 4, partial)
     send, beta_core = far_sums(near, far, beta1)
     got = swap(send, X_BIT)
     peer = backward_part(rows1, both1, 8, 4, partial)
-    left_own = stack(lefts, q, "stack_left", peer)
-    left_other = swap(left_own, Y_BIT)
+    left_other = swap(after(left_own, peer), Y_BIT)
     keep = backward_part(rows1, both1, 0, 4, partial)
 
-    sent, sums = right_norm(docs_total, keep, swap(peer, CORE_BIT), got, beta_core, messages, left_own)
+    sent, sums = right_norm(docs_total, keep, swap(peer, CORE_BIT), got, beta_core, own)
     pieces = along_z(sent)
     squares = lax.all_to_all(after(sums, left_other), AXES, 0, 0, tiled=True)
     left_next, solution_next = left_out(

time: 90.2 us -> 134 us (1.49)
  local copies, waits for them, and re-layouts: 0.04 us -> 36.8 us
  Pallas kernels: 29.9 us -> 34.4 us
  starting transfers between devices: 30.9 us -> 32.7 us
    unnamed x12 -> x44, local copies, waits for them, and re-layouts: 0.04 us -> 36.8 us
    all_to_all x0 -> x5, starting transfers between devices: none -> 24.7 us  [along_z(): lax.all_to_all(value, AXES, 0, 0, axis_index_groups=Z_LINES, tiled=True)]
    ppermute x21 -> x9, starting transfers between devices: 26.8 us -> 5.44 us  [swap(): return lax.ppermute(value, AXES, [(i, i ^ mask) for i in range(32)])]
    ppermute x21 -> x9, waiting for transfers between devices: 22.4 us -> 13.2 us  [swap(): return lax.ppermute(value, AXES, [(i, i ^ mask) for i in range(32)])]
    all_to_all x0 -> x5, waiting for transfers between devices: none -> 8.91 us  [along_z(): lax.all_to_all(value, AXES, 0, 0, axis_index_groups=Z_LINES, tiled=True)]
    pallas_call x5 -> x6, Pallas kernels: 1.97 us -> 6.6 us  [the longest x2 3.6 us: turn(): pl.pallas_call(turn_kernel, out_shape=f32(*value.shape[::-1]), compiler_p...]
    all_to_all x1, starting transfers between devices: 4.05 us -> 2.55 us  [by_columns(): squares = lax.all_to_all(after(sums, left_other), AXES, 0, 0, tiled=True)]
  transfers between devices with their start and end apart: 22 -> 15, of which waited for: 11 -> 7; matrix products, arithmetic and copies ran while one was open for 0% -> 0% of each run, Pallas kernels for 28% -> 23%
where the time goes in v8:
time: 134 us; the launch traced here: 133 us
  local copies, waits for them, and re-layouts  36.8 us (27%)
  Pallas kernels  34.4 us (26%)
  starting transfers between devices  32.7 us (24%)
  waiting for transfers between devices  28.1 us (21%)
    unnamed x44, local copies, waits for them, and re-layouts  36.8 us
    all_to_all x5, starting transfers between devices, along_z(): lax.all_to_all(value, AXES, 0, 0, axis_index_groups=Z_LINES, tiled=True)  24.7 us
    ppermute x9, waiting for transfers between devices, swap(): return lax.ppermute(value, AXES, [(i, i ^ mask) for i in range(32)])  13.2 us
    pallas_call x2, Pallas kernels, build(): pl.pallas_call(functools.partial(build_kernel, rel), in_specs=[whole()] *...  9.92 us
    all_to_all x5, waiting for transfers between devices, along_z(): lax.all_to_all(value, AXES, 0, 0, axis_index_groups=Z_LINES, tiled=True)  8.91 us
    pallas_call x4, Pallas kernels, forward_part(): pl.pallas_call(functools.partial(forward_kernel, blocks), in_specs=[whole...  7.12 us
    all_to_all x1, waiting for transfers between devices, by_columns(): squares = lax.all_to_all(after(sums, left_other), AXES, 0, 0, tiled=True)  6.03 us
    ppermute x9, starting transfers between devices, swap(): return lax.ppermute(value, AXES, [(i, i ^ mask) for i in range(32)])  5.44 us
  transfers between devices with their start and end apart: 15, of which 7 were waited for; matrix products, arithmetic and copies ran while one was open for 0% of the time, Pallas kernels for 23%

profile of v8, /device:TPU:0, one launch (start us, length us, event | category | flops | bytes accessed | tf_op | source)
XLA Modules:
  0.0 133.1 jit_solution(18320112211458937891)
XLA Ops:
  0.6 2.0 %entries.1 = (f32[256,256]{1,0:T(8,128)}, f32[256,256]{1,0:T(8,128)S(1)}, f32[256,256]{1,0:T(8,128)S(1)}) custom-call(s32[16,512]{1,0:T(8,128)} %bitcast.35, bf16[16,512]{1,0:T(8,128)(2,1)} %bitcast.36, f32[256,256]{1,0:T(8,128)} %right.1, f32[512,256]{1,0:T(8,128)} %left_hbm.1), custom_call_target="tpu_custom_call" | custom-call | bytes 16384 | tf_op jit(solution)/shard_map/entries/pallas_call | solution.py:73
  2.7 6.3 %all-to-all-start = ((f32[4,64,256]{2,1,0:T(8,128)}), f32[4,64,256]{2,1,0:T(8,128)S(1)}, u32[]{:S(2)}, u32[]{:S(2)}) async-start(f32[4,64,256]{2,1,0:T(8,128)} %bitcast.2), calls=%async_computation | async-start | bytes 524288 | tf_op jit(solution)/shard_map/all_to_all | solution.py:449
  9.0 1.8 %turn_right.1.token = f32[256,256]{1,0:T(8,128)} custom-call(f32[256,256]{1,0:T(8,128)S(1)} %get-tuple-element.34.ref, f32[256,256]{1,0:T(8,128)} %get-tuple-element.33.token), custom_call_target="tpu_custom_call" | custom-call | bytes 8192 | tf_op jit(solution)/shard_map/turn_right/pallas_call | solution.py:99
  10.8 7.1 %all-to-all-done = f32[4,64,256]{2,1,0:T(8,128)S(1)} async-done(((f32[4,64,256]{2,1,0:T(8,128)}), f32[4,64,256]{2,1,0:T(8,128)S(1)}, u32[]{:S(2)}, u32[]{:S(2)}) %all-to-all-start) | async-done | bytes 262176 | tf_op jit(solution)/shard_map/all_to_all | solution.py:449
  17.9 3.4 %all-to-all-start.1 = ((f32[4,64,256]{2,1,0:T(8,128)}), f32[4,64,256]{2,1,0:T(8,128)S(1)}, u32[]{:S(2)}, u32[]{:S(2)}) async-start(f32[4,64,256]{2,1,0:T(8,128)} %bitcast.4), calls=%async_computation.1 | async-start | bytes 524288 | tf_op jit(solution)/shard_map/all_to_all | solution.py:449
  21.3 4.8 %dense_rows.2 = (bf16[16,1024,256]{2,1,0:T(8,128)(2,1)S(1)}, bf16[16,1024,256]{2,1,0:T(8,128)(2,1)S(1)}, f32[8,128]{1,0:T(8,128)S(1)}) custom-call(f32[256,256]{1,0:T(8,128)S(1)} %bitcast.24), custom_call_target="tpu_custom_call" | custom-call | flops 33554432 | bytes 262144 | tf_op jit(solution)/shard_map/dense_rows/pallas_call | solution.py:167
  26.1 3.3 %copy-done = bf16[16,1024,256]{2,1,0:T(8,128)(2,1)} copy-done((bf16[16,1024,256]{2,1,0:T(8,128)(2,1)}, bf16[16,1024,256]{2,1,0:T(8,128)(2,1)S(1)}, u32[]{:S(2)}) %copy-start) | copy-done | bytes 8388632
  29.4 3.3 %copy-done.4 = bf16[16,1024,256]{2,1,0:T(8,128)(2,1)} copy-done((bf16[16,1024,256]{2,1,0:T(8,128)(2,1)}, bf16[16,1024,256]{2,1,0:T(8,128)(2,1)S(1)}, u32[]{:S(2)}) %copy-start.4) | copy-done | bytes 8388632
  32.7 1.5 %collective-permute-start = (f32[4,64,256]{2,1,0:T(8,128)S(1)}, f32[4,64,256]{2,1,0:T(8,128)S(1)}, u32[]{:S(2)}, u32[]{:S(2)}) collective-permute-start(f32[4,64,256]{2,1,0:T(8,128)S(1)} %relative_right.1.refs_0_.right), channel_id=1, source_target_pairs={{0,4},{1,5},{2,6},{3,7},{4,0},{5,1},{6,2},{7,3},{8,12},{9,13},{10,... | collective-permute-start | bytes 786440 | tf_op jit(solution)/shard_map/ppermute | solution.py:445
  34.2 1.8 %turn_left.1 = f32[256,256]{1,0:T(8,128)} custom-call(f32[256,256]{1,0:T(8,128)S(1)} %get-tuple-element.38.ref, f32[256,256]{1,0:T(8,128)} %turn_right.1.token), custom_call_target="tpu_custom_call" | custom-call | bytes 8192 | tf_op jit(solution)/shard_map/turn_left/pallas_call | solution.py:99
  36.0 5.1 %all-to-all-start.2 = ((f32[4,64,256]{2,1,0:T(8,128)}), f32[4,64,256]{2,1,0:T(8,128)S(1)}, u32[]{:S(2)}, u32[]{:S(2)}) async-start(f32[4,64,256]{2,1,0:T(8,128)} %bitcast.6), calls=%async_computation.2 | async-start | bytes 524288 | tf_op jit(solution)/shard_map/all_to_all | solution.py:449
  41.6 5.2 %dense_rows.3 = (bf16[16,1024,256]{2,1,0:T(8,128)(2,1)S(1)}, bf16[16,1024,256]{2,1,0:T(8,128)(2,1)S(1)}, f32[8,128]{1,0:T(8,128)}) custom-call(f32[256,256]{1,0:T(8,128)S(1)} %bitcast.25, f32[4,64,256]{2,1,0:T(8,128)S(1)} %relative_right.1.refs_0_.right), custom_call_target="tpu_custom_call" | custom-call | flops 33554432 | bytes 262144 | tf_op jit(solution)/shard_map/dense_rows/pallas_call | solution.py:167
  46.8 9.1 %copy-done.1 = bf16[16,1024,256]{2,1,0:T(8,128)(2,1)S(1)} copy-done((bf16[16,1024,256]{2,1,0:T(8,128)(2,1)S(1)}, bf16[16,1024,256]{2,1,0:T(8,128)(2,1)}, u32[]{:S(2)}) %copy-start.1) | copy-done | bytes 8388632
  56.0 3.4 %copy-done.5 = bf16[16,1024,256]{2,1,0:T(8,128)(2,1)S(1)} copy-done((bf16[16,1024,256]{2,1,0:T(8,128)(2,1)S(1)}, bf16[16,1024,256]{2,1,0:T(8,128)(2,1)}, u32[]{:S(2)}) %copy-start.5) | copy-done | bytes 8388632
  59.3 2.3 %forward_part.6.refs_1_ = f32[1024,128]{1,0:T(8,128)S(1)} custom-call(bf16[16,1024,256]{2,1,0:T(8,128)(2,1)S(1)} %copy-done.1, bf16[16,1024,256]{2,1,0:T(8,128)(2,1)S(1)} %copy-done.5, f32[4,64,256]{2,1,0:T(8,128)S(1)} %relative_right.1.refs_0_.right, f32[4,64,256]{2,1,0:T(8,128)S(1)} %collective-permute-done.2.refs_1_), custom_call_target="tpu_custom_call" | custom-call | flops 67108864 | bytes 131072 | tf_op jit(solution)/shard_map/forward_part/pallas_call | solution.py:209
  61.7 1.2 forward_part.7.before
  62.9 1.3 product_half.3.mine
  64.2 1.6 %collective-permute-start.3 = (f32[64,1024]{1,0:T(8,128)S(1)}, f32[64,1024]{1,0:T(8,128)S(1)}, u32[]{:S(2)}, u32[]{:S(2)}) collective-permute-start(f32[64,1024]{1,0:T(8,128)S(1)} %product_half.3.mine), channel_id=1, source_target_pairs={{0,1},{1,0},{2,3},{3,2},{4,5},{5,4},{6,7},{7,6},{8,9},{9,8},{10,11... | collective-permute-start | bytes 786440 | tf_op jit(solution)/shard_map/ppermute | solution.py:445
  65.8 2.3 %forward_part.4.refs_1_ = f32[1024,128]{1,0:T(8,128)S(1)} custom-call(bf16[16,1024,256]{2,1,0:T(8,128)(2,1)S(1)} %get-tuple-element.36.hi_ref, bf16[16,1024,256]{2,1,0:T(8,128)(2,1)S(1)} %get-tuple-element.37.lo_ref, f32[4,64,256]{2,1,0:T(8,128)S(1)} %relative_right.1.refs_0_.right, f32[4,64,256]{2,1,0:T(8,128)S(1)} %collective-permute-done.2.refs_1_), custom_call_target="tpu_custom_call" | custom-call | flops 67108864 | bytes 131072 | tf_op jit(solution)/shard_map/forward_part/pallas_call | solution.py:209
  68.1 1.2 forward_part.5.before
  69.4 3.4 %copy-done.8 = bf16[16,1024,256]{2,1,0:T(8,128)(2,1)S(1)} copy-done((bf16[16,1024,256]{2,1,0:T(8,128)(2,1)S(1)}, bf16[16,1024,256]{2,1,0:T(8,128)(2,1)}, u32[]{:S(2)}) %copy-start.8) | copy-done | bytes 8388632
  72.8 3.4 %copy-done.11 = bf16[16,1024,256]{2,1,0:T(8,128)(2,1)S(1)} copy-done((bf16[16,1024,256]{2,1,0:T(8,128)(2,1)S(1)}, bf16[16,1024,256]{2,1,0:T(8,128)(2,1)}, u32[]{:S(2)}) %copy-start.11) | copy-done | bytes 8388632
  76.2 1.3 product_half.2.mine
  77.5 0.6 collective-permute-start.4
  78.1 0.8 left_half.2
  78.9 0.7 copy-done.9
  79.7 2.3 %backward_part.5.refs_0_ = f32[1024,256]{1,0:T(8,128)S(1)} custom-call(bf16[16,1024,256]{2,1,0:T(8,128)(2,1)S(1)} %copy-done.9, bf16[16,1024,256]{2,1,0:T(8,128)(2,1)S(1)} %copy-done.11, bf16[128,1024]{1,0:T(8,128)(2,1)S(1)} %get-tuple-element.44.both_ref), custom_call_target="tpu_custom_call" | custom-call | flops 134217728 | bytes 262144 | tf_op jit(solution)/shard_map/backward_part/pallas_call | solution.py:323
  82.0 3.6 %collective-permute-done.4.other = f32[64,1024]{1,0:T(8,128)S(1)} collective-permute-done((f32[64,1024]{1,0:T(8,128)S(1)}, f32[64,1024]{1,0:T(8,128)S(1)}, u32[]{:S(2)}, u32[]{:S(2)}) %collective-permute-start.4) | collective-permute-done | bytes 262176 | tf_op jit(solution)/shard_map/ppermute | solution.py:445
  85.8 0.7 backward_part.9
  86.6 5.1 %all-to-all-start.3 = ((f32[4,64,256]{2,1,0:T(8,128)}), f32[4,64,256]{2,1,0:T(8,128)S(1)}, u32[]{:S(2)}, u32[]{:S(2)}) async-start(f32[4,64,256]{2,1,0:T(8,128)} %bitcast.9), calls=%async_computation.3 | async-start | bytes 524288 | tf_op jit(solution)/shard_map/all_to_all | solution.py:449
  91.7 3.4 %copy-done.2 = bf16[16,1024,256]{2,1,0:T(8,128)(2,1)S(1)} copy-done((bf16[16,1024,256]{2,1,0:T(8,128)(2,1)S(1)}, bf16[16,1024,256]{2,1,0:T(8,128)(2,1)}, u32[]{:S(2)}) %copy-start.2) | copy-done | bytes 8388632
  95.1 3.4 %copy-done.6 = bf16[16,1024,256]{2,1,0:T(8,128)(2,1)S(1)} copy-done((bf16[16,1024,256]{2,1,0:T(8,128)(2,1)S(1)}, bf16[16,1024,256]{2,1,0:T(8,128)(2,1)}, u32[]{:S(2)}) %copy-start.6) | copy-done | bytes 8388632
  98.5 0.7 backward_part.8.near
  99.2 0.6 collective-permute-start.8
  99.8 3.4 %copy-done.3 = bf16[16,1024,256]{2,1,0:T(8,128)(2,1)S(1)} copy-done((bf16[16,1024,256]{2,1,0:T(8,128)(2,1)S(1)}, bf16[16,1024,256]{2,1,0:T(8,128)(2,1)}, u32[]{:S(2)}) %copy-start.3) | copy-done | bytes 8388632
  103.2 0.7 backward_part.6
  104.1 0.7 backward_part.7.keep
  104.8 0.8 collective-permute-done.6.peer
  105.6 2.3 %collective-permute-done.8.got = f32[264,256]{1,0:T(8,128)S(1)} collective-permute-done((f32[264,256]{1,0:T(8,128)S(1)}, f32[264,256]{1,0:T(8,128)S(1)}, u32[]{:S(2)}, u32[]{:S(2)}) %collective-permute-start.8) | collective-permute-done | bytes 270368 | tf_op jit(solution)/shard_map/ppermute | solution.py:445
  107.9 0.9 right_norm.1
  108.8 4.8 %all-to-all-start.4 = ((f32[4,72,256]{2,1,0:T(8,128)}), f32[4,72,256]{2,1,0:T(8,128)S(1)}, u32[]{:S(2)}, u32[]{:S(2)}) async-start(f32[4,72,256]{2,1,0:T(8,128)} %bitcast.11), calls=%async_computation.4 | async-start | bytes 589824 | tf_op jit(solution)/shard_map/all_to_all | solution.py:449
  113.7 0.5 collective-permute-start.5
  114.2 6.5 %collective-permute-done.5.other = f32[256,256]{1,0:T(8,128)S(1)} collective-permute-done((f32[256,256]{1,0:T(8,128)S(1)}, f32[256,256]{1,0:T(8,128)S(1)}, u32[]{:S(2)}, u32[]{:S(2)}) %collective-permute-start.5) | collective-permute-done | bytes 262176 | tf_op jit(solution)/shard_map/ppermute | solution.py:445
  120.7 1.8 %all-to-all-done.4 = f32[4,72,256]{2,1,0:T(8,128)S(1)} async-done(((f32[4,72,256]{2,1,0:T(8,128)}), f32[4,72,256]{2,1,0:T(8,128)S(1)}, u32[]{:S(2)}, u32[]{:S(2)}) %all-to-all-start.4) | async-done | bytes 294944 | tf_op jit(solution)/shard_map/all_to_all | solution.py:449
  122.5 2.5 %all-to-all-start.5 = ((f32[32,1,128]{2,1,0:T(1,128)}), f32[32,1,128]{2,1,0:T(1,128)S(1)}, u32[]{:S(2)}, u32[]{:S(2)}) async-start(f32[32,1,128]{2,1,0:T(1,128)} %get-tuple-element.52), calls=%async_computation.5 | async-start | bytes 32768 | tf_op jit(solution)/shard_map/all_to_all | solution.py:496
  125.1 1.1 left_out.1
  126.1 6.0 %all-to-all-done.5.squares = f32[32,1,128]{2,1,0:T(1,128)S(1)} async-done(((f32[32,1,128]{2,1,0:T(1,128)}), f32[32,1,128]{2,1,0:T(1,128)S(1)}, u32[]{:S(2)}, u32[]{:S(2)}) %all-to-all-start.5) | async-done | bytes 16416 | tf_op jit(solution)/shard_map/all_to_all | solution.py:496
  132.1 0.9 finish.1
  (51 shorter events, 0.9 us)
Async XLA Ops:
  2.7 15.2 %all-to-all-start = ((f32[4,64,256]{2,1,0:T(8,128)}), f32[4,64,256]{2,1,0:T(8,128)S(1)}, u32[]{:S(2)}, u32[]{:S(2)}) async-start(f32[4,64,256]{2,1,0:T(8,128)} %bitcast.2), calls=%async_computation | async-start | bytes 524288 | tf_op jit(solution)/shard_map/all_to_all | solution.py:449
  17.9 14.8 %all-to-all-start.1 = ((f32[4,64,256]{2,1,0:T(8,128)}), f32[4,64,256]{2,1,0:T(8,128)S(1)}, u32[]{:S(2)}, u32[]{:S(2)}) async-start(f32[4,64,256]{2,1,0:T(8,128)} %bitcast.4), calls=%async_computation.1 | async-start | bytes 524288 | tf_op jit(solution)/shard_map/all_to_all | solution.py:449
  26.1 3.3 %copy-start = (bf16[16,1024,256]{2,1,0:T(8,128)(2,1)}, bf16[16,1024,256]{2,1,0:T(8,128)(2,1)S(1)}, u32[]{:S(2)}) copy-start(bf16[16,1024,256]{2,1,0:T(8,128)(2,1)S(1)} %get-tuple-element.39.hi_ref) | copy-start | bytes 25165828
  29.4 3.3 %copy-start.4 = (bf16[16,1024,256]{2,1,0:T(8,128)(2,1)}, bf16[16,1024,256]{2,1,0:T(8,128)(2,1)S(1)}, u32[]{:S(2)}) copy-start(bf16[16,1024,256]{2,1,0:T(8,128)(2,1)S(1)} %get-tuple-element.40.lo_ref) | copy-start | bytes 25165828
  32.7 8.4 %collective-permute-start = (f32[4,64,256]{2,1,0:T(8,128)S(1)}, f32[4,64,256]{2,1,0:T(8,128)S(1)}, u32[]{:S(2)}, u32[]{:S(2)}) collective-permute-start(f32[4,64,256]{2,1,0:T(8,128)S(1)} %relative_right.1.refs_0_.right), channel_id=1, source_target_pairs={{0,4},{1,5},{2,6},{3,7},{4,0},{5,1},{6,2},{7,3},{8,12},{9,13},{10,... | collective-permute-start | bytes 786440 | tf_op jit(solution)/shard_map/ppermute | solution.py:445
  36.0 33.4 %all-to-all-start.2 = ((f32[4,64,256]{2,1,0:T(8,128)}), f32[4,64,256]{2,1,0:T(8,128)S(1)}, u32[]{:S(2)}, u32[]{:S(2)}) async-start(f32[4,64,256]{2,1,0:T(8,128)} %bitcast.6), calls=%async_computation.2 | async-start | bytes 524288 | tf_op jit(solution)/shard_map/all_to_all | solution.py:449
  41.1 5.7 %collective-permute-start.2 = (f32[4,64,256]{2,1,0:T(8,128)S(1)}, f32[4,64,256]{2,1,0:T(8,128)S(1)}, u32[]{:S(2)}, u32[]{:S(2)}) collective-permute-start(f32[4,64,256]{2,1,0:T(8,128)S(1)} %relative_right.1.refs_0_.right), channel_id=1, source_target_pairs={{0,2},{1,3},{2,0},{3,1},{4,6},{5,7},{6,4},{7,5},{8,10},{9,11},{10,... | collective-permute-start | bytes 786440 | tf_op jit(solution)/shard_map/ppermute | solution.py:445
  41.1 21.8 %collective-permute-start.1 = (f32[4,64,256]{2,1,0:T(8,128)S(1)}, f32[4,64,256]{2,1,0:T(8,128)S(1)}, u32[]{:S(2)}, u32[]{:S(2)}) collective-permute-start(f32[4,64,256]{2,1,0:T(8,128)S(1)} %collective-permute-done.refs_0_), channel_id=1, source_target_pairs={{0,2},{1,3},{2,0},{3,1},{4,6},{5,7},{6,4},{7,5},{8,10},{9,11},{10,... | collective-permute-start | bytes 786440 | tf_op jit(solution)/shard_map/ppermute | solution.py:445
  46.8 21.3 %copy-start.7 = (bf16[16,1024,256]{2,1,0:T(8,128)(2,1)}, bf16[16,1024,256]{2,1,0:T(8,128)(2,1)S(1)}, u32[]{:S(2)}) copy-start(bf16[16,1024,256]{2,1,0:T(8,128)(2,1)S(1)} %get-tuple-element.36.hi_ref) | copy-start | bytes 25165828
  46.8 21.3 %copy-start.10 = (bf16[16,1024,256]{2,1,0:T(8,128)(2,1)}, bf16[16,1024,256]{2,1,0:T(8,128)(2,1)S(1)}, u32[]{:S(2)}) copy-start(bf16[16,1024,256]{2,1,0:T(8,128)(2,1)S(1)} %get-tuple-element.37.lo_ref) | copy-start | bytes 25165828
  46.8 9.1 %copy-start.1 = (bf16[16,1024,256]{2,1,0:T(8,128)(2,1)S(1)}, bf16[16,1024,256]{2,1,0:T(8,128)(2,1)}, u32[]{:S(2)}) copy-start(bf16[16,1024,256]{2,1,0:T(8,128)(2,1)} %copy-done) | copy-start | bytes 25165828
  55.9 3.4 %copy-start.5 = (bf16[16,1024,256]{2,1,0:T(8,128)(2,1)S(1)}, bf16[16,1024,256]{2,1,0:T(8,128)(2,1)}, u32[]{:S(2)}) copy-start(bf16[16,1024,256]{2,1,0:T(8,128)(2,1)} %copy-done.4) | copy-start | bytes 25165828
  64.2 13.9 %collective-permute-start.3 = (f32[64,1024]{1,0:T(8,128)S(1)}, f32[64,1024]{1,0:T(8,128)S(1)}, u32[]{:S(2)}, u32[]{:S(2)}) collective-permute-start(f32[64,1024]{1,0:T(8,128)S(1)} %product_half.3.mine), channel_id=1, source_target_pairs={{0,1},{1,0},{2,3},{3,2},{4,5},{5,4},{6,7},{7,6},{8,9},{9,8},{10,11... | collective-permute-start | bytes 786440 | tf_op jit(solution)/shard_map/ppermute | solution.py:445
  68.1 1.3 copy-start.17
  69.4 3.4 %copy-start.8 = (bf16[16,1024,256]{2,1,0:T(8,128)(2,1)S(1)}, bf16[16,1024,256]{2,1,0:T(8,128)(2,1)}, u32[]{:S(2)}) copy-start(bf16[16,1024,256]{2,1,0:T(8,128)(2,1)} %copy-done.7) | copy-start | bytes 25165828
  72.8 3.4 %copy-start.11 = (bf16[16,1024,256]{2,1,0:T(8,128)(2,1)S(1)}, bf16[16,1024,256]{2,1,0:T(8,128)(2,1)}, u32[]{:S(2)}) copy-start(bf16[16,1024,256]{2,1,0:T(8,128)(2,1)} %copy-done.10) | copy-start | bytes 25165828
  76.2 3.5 %copy-start.9 = (bf16[16,1024,256]{2,1,0:T(8,128)(2,1)S(1)}, bf16[16,1024,256]{2,1,0:T(8,128)(2,1)}, u32[]{:S(2)}) copy-start(bf16[16,1024,256]{2,1,0:T(8,128)(2,1)} %copy-done.7) | copy-start | bytes 25165828
  76.2 9.6 %slice-start = ((s8[8388608]{0:T(1024)(128)(4,1)}), s8[4194304]{0:T(1024)(128)(4,1)S(1)}, s32[]{:S(2)}) async-start(s8[8388608]{0:T(1024)(128)(4,1)} %bitcast.18), calls=%async_computation.6 | async-start | bytes 8388608
  76.2 9.6 %slice-start.2 = ((s8[8388608]{0:T(1024)(128)(4,1)}), s8[4194304]{0:T(1024)(128)(4,1)S(1)}, s32[]{:S(2)}) async-start(s8[8388608]{0:T(1024)(128)(4,1)} %bitcast.20), calls=%async_computation.8 | async-start | bytes 8388608
  77.5 8.1 %collective-permute-start.4 = (f32[64,1024]{1,0:T(8,128)S(1)}, f32[64,1024]{1,0:T(8,128)S(1)}, u32[]{:S(2)}, u32[]{:S(2)}) collective-permute-start(f32[64,1024]{1,0:T(8,128)S(1)} %product_half.2.mine), channel_id=1, source_target_pairs={{0,1},{1,0},{2,3},{3,2},{4,5},{5,4},{6,7},{7,6},{8,9},{9,8},{10,11... | collective-permute-start | bytes 786440 | tf_op jit(solution)/shard_map/ppermute | solution.py:445
  79.7 6.1 %slice-start.1 = ((s8[8388608]{0:T(1024)(128)(4,1)}), s8[4194304]{0:T(1024)(128)(4,1)S(1)}, s32[]{:S(2)}) async-start(s8[8388608]{0:T(1024)(128)(4,1)} %bitcast.18), calls=%async_computation.7 | async-start | bytes 8388608
  79.7 6.1 %slice-start.3 = ((s8[8388608]{0:T(1024)(128)(4,1)}), s8[4194304]{0:T(1024)(128)(4,1)S(1)}, s32[]{:S(2)}) async-start(s8[8388608]{0:T(1024)(128)(4,1)} %bitcast.20), calls=%async_computation.9 | async-start | bytes 8388608
  86.5 12.7 %collective-permute-start.7 = (f32[264,256]{1,0:T(8,128)S(1)}, f32[264,256]{1,0:T(8,128)S(1)}, u32[]{:S(2)}, u32[]{:S(2)}) collective-permute-start(f32[264,256]{1,0:T(8,128)S(1)} %backward_part.9), channel_id=1, source_target_pairs={{0,2},{1,3},{2,0},{3,1},{4,6},{5,7},{6,4},{7,5},{8,10},{9,11},{10,... | collective-permute-start | bytes 811016 | tf_op jit(solution)/shard_map/ppermute | solution.py:445
  86.6 22.2 %all-to-all-start.3 = ((f32[4,64,256]{2,1,0:T(8,128)}), f32[4,64,256]{2,1,0:T(8,128)S(1)}, u32[]{:S(2)}, u32[]{:S(2)}) async-start(f32[4,64,256]{2,1,0:T(8,128)} %bitcast.9), calls=%async_computation.3 | async-start | bytes 524288 | tf_op jit(solution)/shard_map/all_to_all | solution.py:449
  91.7 3.4 %copy-start.2 = (bf16[16,1024,256]{2,1,0:T(8,128)(2,1)S(1)}, bf16[16,1024,256]{2,1,0:T(8,128)(2,1)}, u32[]{:S(2)}) copy-start(bf16[16,1024,256]{2,1,0:T(8,128)(2,1)} %copy-done) | copy-start | bytes 25165828
  95.1 3.4 %copy-start.6 = (bf16[16,1024,256]{2,1,0:T(8,128)(2,1)S(1)}, bf16[16,1024,256]{2,1,0:T(8,128)(2,1)}, u32[]{:S(2)}) copy-start(bf16[16,1024,256]{2,1,0:T(8,128)(2,1)} %copy-done.4) | copy-start | bytes 25165828
  99.2 8.7 %collective-permute-start.8 = (f32[264,256]{1,0:T(8,128)S(1)}, f32[264,256]{1,0:T(8,128)S(1)}, u32[]{:S(2)}, u32[]{:S(2)}) collective-permute-start(f32[264,256]{1,0:T(8,128)S(1)} %get-tuple-element.47), channel_id=1, source_target_pairs={{0,4},{1,5},{2,6},{3,7},{4,0},{5,1},{6,2},{7,3},{8,12},{9,13},{10,... | collective-permute-start | bytes 811016 | tf_op jit(solution)/shard_map/ppermute | solution.py:445
  99.8 3.4 %copy-start.3 = (bf16[16,1024,256]{2,1,0:T(8,128)(2,1)S(1)}, bf16[16,1024,256]{2,1,0:T(8,128)(2,1)}, u32[]{:S(2)}) copy-start(bf16[16,1024,256]{2,1,0:T(8,128)(2,1)} %copy-done) | copy-start | bytes 25165828
  103.9 21.1 %copy-start.13 = (f32[256,256]{1,0:T(8,128)S(1)}, f32[256,256]{1,0:T(8,128)}, u32[]{:S(2)}) copy-start(f32[256,256]{1,0:T(8,128)} %search.3) | copy-start | bytes 786436
  104.0 21.1 %copy-start.14 = (f32[256,256]{1,0:T(8,128)S(1)}, f32[256,256]{1,0:T(8,128)}, u32[]{:S(2)}) copy-start(f32[256,256]{1,0:T(8,128)} %solution.1) | copy-start | bytes 786436
  104.0 21.1 %copy-start.15 = (f32[256]{0:T(256)S(1)}, f32[256]{0:T(256)}, u32[]{:S(2)}) copy-start(f32[256]{0:T(256)} %param.16) | copy-start | bytes 3076
  104.0 21.1 %copy-start.16 = (f32[256]{0:T(256)S(1)}, f32[256]{0:T(256)}, u32[]{:S(2)}) copy-start(f32[256]{0:T(256)} %param.17) | copy-start | bytes 3076
  104.0 28.2 %copy-start.12 = (f32[256,256]{1,0:T(8,128)S(1)}, f32[256,256]{1,0:T(8,128)}, u32[]{:S(2)}) copy-start(f32[256,256]{1,0:T(8,128)} %right.1) | copy-start | bytes 786436
  104.0 1.6 %collective-permute-start.6 = (f32[256,256]{1,0:T(8,128)S(1)}, f32[256,256]{1,0:T(8,128)S(1)}, u32[]{:S(2)}, u32[]{:S(2)}) collective-permute-start(f32[256,256]{1,0:T(8,128)S(1)} %backward_part.6), channel_id=1, source_target_pairs={{0,2},{1,3},{2,0},{3,1},{4,6},{5,7},{6,4},{7,5},{8,10},{9,11},{10,... | collective-permute-start | bytes 786440 | tf_op jit(solution)/shard_map/ppermute | solution.py:445
  108.8 13.6 %all-to-all-start.4 = ((f32[4,72,256]{2,1,0:T(8,128)}), f32[4,72,256]{2,1,0:T(8,128)S(1)}, u32[]{:S(2)}, u32[]{:S(2)}) async-start(f32[4,72,256]{2,1,0:T(8,128)} %bitcast.11), calls=%async_computation.4 | async-start | bytes 589824 | tf_op jit(solution)/shard_map/all_to_all | solution.py:449
  113.7 7.0 %collective-permute-start.5 = (f32[256,256]{1,0:T(8,128)S(1)}, f32[256,256]{1,0:T(8,128)S(1)}, u32[]{:S(2)}, u32[]{:S(2)}) collective-permute-start(f32[256,256]{1,0:T(8,128)S(1)} %bitcast.28), channel_id=1, source_target_pairs={{0,1},{1,0},{2,3},{3,2},{4,5},{5,4},{6,7},{7,6},{8,9},{9,8},{10,11... | collective-permute-start | bytes 786440 | tf_op jit(solution)/shard_map/ppermute | solution.py:445
  122.5 9.7 %all-to-all-start.5 = ((f32[32,1,128]{2,1,0:T(1,128)}), f32[32,1,128]{2,1,0:T(1,128)S(1)}, u32[]{:S(2)}, u32[]{:S(2)}) async-start(f32[32,1,128]{2,1,0:T(1,128)} %get-tuple-element.52), calls=%async_computation.5 | async-start | bytes 32768 | tf_op jit(solution)/shard_map/all_to_all | solution.py:496

commit v9 on v7

--- a/solution.py
+++ b/solution.py
@@ -10,6 +10,7 @@
 epsilon = 1e-06
 AXES = ("doc", "feat")
 MIB = 1024 * 1024
+SCALE = 64
 
 
 Y_BIT, CORE_BIT, X_BIT, Z_SHIFT = 1, 2, 4, 3
@@ -27,7 +28,7 @@
 
 
 def cost(flops, nbytes):
-    return pl.CostEstimate(flops=int(flops), bytes_accessed=int(nbytes), transcendentals=0)
+    return pl.CostEstimate(flops=int(flops) // SCALE, bytes_accessed=int(nbytes) // SCALE, transcendentals=0)
 
 
 def f32(*shape):
@@ -38,8 +39,8 @@
     return jax.ShapeDtypeStruct(shape, jnp.bfloat16)
 
 
-def prepare_kernel(ids_hbm, vals_hbm, right_hbm, left_hbm, stored, m0, m1, m2, m3,
-                   ids, vals, wide, right, left, turned, arrived):
+def prepare_kernel(ids_hbm, vals_hbm, right_hbm, left_hbm, a0, a1, a2, a3, b0, b1, b2, b3,
+                   ids, vals, wide, lines, right, left, turned, arrived):
     _, z, y = coords()
     q, rows = turned.shape[1:]
     copies = [
@@ -53,33 +54,38 @@
     ]
     for copy in copies:
         copy.start()
-    lines, count = stored.shape[0] // 2, ids.shape[0]
+    count, n = ids.shape[0], lines.shape[0]
+    half = n // 2
+    groups = (b0, b1, b2, b3), (a0, a1, a2, a3)
     for part, ref in enumerate((ids, vals)):
         copies[part].wait()
         wide[...] = ref[...].astype(jnp.float32).T
         for r in range(256 // count):
-            stored[part * lines : (part + 1) * lines, r * count : (r + 1) * count] = wide[
-                pl.ds(r, lines, stride=256 // count), :
-            ]
-    for part, ref in enumerate((right, left)):
-        copies[2 + part].wait()
+            lines[:, r * count : (r + 1) * count] = wide[pl.ds(r, n, stride=256 // count), :]
+        for rel, outs in enumerate(groups):
+            value = lines[pl.ds(pl.multiple_of((y ^ rel) * half, half), half), :]
+            for out in outs:
+                out[part * half : (part + 1) * half, :] = value
+    for copy, ref, outs in zip(copies[2:], (right, left), groups[::-1]):
+        copy.wait()
         turned[...] = ref[...].T.reshape(turned.shape)
-        for k, out in enumerate((m0, m1, m2, m3)):
-            out[part * q : (part + 1) * q, :] = turned[z ^ k]
+        for k, out in enumerate(outs):
+            out[n:, :] = turned[z ^ k]
 
 
 def prepare(ids, vals, right, left):
     rows, cols = right.shape
-    q = cols // 4
+    n, q = ids.size // 256, cols // 4
     got = pl.pallas_call(
         prepare_kernel,
         in_specs=[pl.BlockSpec(memory_space=pltpu.HBM)] * 4,
-        out_specs=[whole()] * 5,
-        out_shape=[pltpu.VMEM((ids.size // 128, 256), jnp.float32)] + [pltpu.VMEM((2 * q, rows), jnp.float32)] * 4,
+        out_specs=[whole()] * 8,
+        out_shape=[pltpu.VMEM((n + q, rows), jnp.float32)] * 8,
         scratch_shapes=[
             pltpu.VMEM(ids.shape, jnp.int32),
             pltpu.VMEM(vals.shape, jnp.bfloat16),
             pltpu.VMEM(ids.shape[::-1], jnp.float32),
+            pltpu.VMEM((n, 256), jnp.float32),
             pltpu.VMEM(right.shape, jnp.float32),
             pltpu.VMEM(right.shape, jnp.float32),
             pltpu.VMEM((4, q, rows), jnp.float32),
@@ -89,13 +95,13 @@
         cost_estimate=cost(0, rows * cols * 16),
         name="prepare",
     )(ids, vals, right, left)
-    return got[0], got[1:]
+    return got[:4], got[4:]
 
 
 def stack_kernel(m0, m1, m2, m3, *refs):
     out = refs[-1]
     for k, m in enumerate((m0, m1, m2, m3)):
-        out[k] = m[0 : out.shape[1], :]
+        out[k] = m[m.shape[0] - out.shape[1] :, :]
 
 
 def stack(messages, q, name, *tokens):
@@ -109,11 +115,10 @@
     )(*messages, *tokens)
 
 
-def build_kernel(rel, e0, e1, e2, e3, *refs):
-    hi_ref, lo_ref, token = refs[-3:]
-    token[...] = jnp.zeros_like(token)
-    d, _, y = coords()
-    n = e0.shape[0] // 2
+def build_kernel(e0, e1, e2, e3, *refs):
+    hi_ref, lo_ref = refs[-2:]
+    d, _, _ = coords()
+    n = hi_ref.shape[1] // 64
     iota = lax.broadcasted_iota(jnp.int32, (256, 256), 0).astype(jnp.float32).astype(jnp.bfloat16)
     lane_doc = lax.broadcasted_iota(jnp.int32, (8, 256), 1) >> 4
     one = jnp.ones((256, 256), jnp.bfloat16)
@@ -125,9 +130,9 @@
 
     for k, entries in enumerate((e0, e1, e2, e3)):
 
-        @pl.loop(0, n // 16)
+        @pl.loop(0, n // 8)
         def _(step, k=k, entries=entries):
-            at = pl.multiple_of((y ^ rel) * (n // 2) + step * 8, 8)
+            at = pl.multiple_of(step * 8, 8)
             ids = entries[pl.ds(at, 8), :].astype(jnp.int32)
             vals = entries[pl.ds(n + at, 8), :]
             owner = (ids >> 8) ^ d
@@ -140,7 +145,7 @@
                 dense = lax.dot_general(pick, weigh, NT, preferred_element_type=jnp.float32)
                 high = dense.astype(jnp.bfloat16)
                 low = (dense - high.astype(jnp.float32)).astype(jnp.bfloat16)
-                docs = pl.ds(pl.multiple_of(k * 8 * n + step * 128 + 16 * t, 16), 16)
+                docs = pl.ds(pl.multiple_of(k * 16 * n + step * 128 + 16 * t, 16), 16)
                 hi_ref[:, docs, :] = high.reshape(16, 16, 256)
                 lo_ref[:, docs, :] = low.reshape(16, 16, 256)
 
@@ -149,18 +154,17 @@
     return pl.BlockSpec(memory_space=pltpu.VMEM)
 
 
-def build(entries, rel, *tokens):
-    docs = 4 * (entries[0].shape[0] // 4 * 16)
-    *rows, token = pl.pallas_call(
-        functools.partial(build_kernel, rel),
+def build(messages, lines, *tokens):
+    docs = 4 * lines // 2 * 16
+    return pl.pallas_call(
+        build_kernel,
         in_specs=[whole()] * (4 + len(tokens)),
-        out_specs=[whole()] * 3,
-        out_shape=[pltpu.VMEM((16, docs, 256), jnp.bfloat16)] * 2 + [f32(8, 128)],
+        out_specs=[whole()] * 2,
+        out_shape=[pltpu.VMEM((16, docs, 256), jnp.bfloat16)] * 2,
         compiler_params=params(8),
         cost_estimate=cost(2 * docs * 16 * 256 * 256, docs * 4096 * 4),
         name="dense_rows",
-    )(*entries, *tokens)
-    return rows, token
+    )(*messages, *tokens)
 
 
 def split_rows(value):
@@ -182,19 +186,19 @@
             )
 
 
-def forward_kernel(blocks, hi_ref, lo_ref, *refs):
+def forward_kernel(blocks, has_before, hi_ref, lo_ref, *refs):
     count = len(blocks)
     total = refs[-1]
-    total[...] = refs[count][...] if len(refs) > count + 1 else jnp.zeros_like(total)
+    total[...] = refs[count][...] if has_before else jnp.zeros_like(total)
     add_products(hi_ref, lo_ref, refs[:count], blocks, total)
 
 
-def forward_part(rows, vecs, blocks, before=None):
+def forward_part(rows, vecs, blocks, before=None, tokens=()):
     docs, q = rows[0].shape[1], vecs[0].shape[1]
     n = 4 * len(blocks)
-    extra = [] if before is None else [before]
-    return pl.pallas_call(
-        functools.partial(forward_kernel, blocks),
+    extra = [*tokens] if before is None else [before, *tokens]
+    return pl.pallas_call(
+        functools.partial(forward_kernel, blocks, before is not None),
         in_specs=[whole()] * (2 + len(vecs) + len(extra)),
         out_specs=whole(),
         out_shape=f32(docs, 2 * q),
@@ -220,7 +224,7 @@
     scale = columns[pl.ds(pl.multiple_of(z * q, q), q), :][:, 0:1]
     for k, m in enumerate(messages):
         at = slice(k * m.shape[1], (k + 1) * m.shape[1])
-        out[:, at] = product[:, at] - scale * m[q:, :]
+        out[:, at] = product[:, at] - scale * m[m.shape[0] - q :, :]
 
 
 def product_half(rows, vec, before, blocks, *left):
@@ -262,16 +266,16 @@
     both, sums = refs[-2:]
     both[...] = split_rows(left)
     squares = square_row(left, z, sums.shape[1])
-    sums[...] = refs[0][...] + squares if len(refs) == 3 else squares
-    if len(refs) > 3:
+    sums[...] = refs[0][...] + squares if len(refs) == 4 else squares
+    if len(refs) > 4:
         n = left.shape[1] // 4
         for k, out in enumerate(refs[:4]):
             out[...] = left[:, k * n : (k + 1) * n]
 
 
-def left_half(mine, other, squares=None):
+def left_half(mine, other, squares=None, token=None):
     q, docs = mine.shape
-    extra = [] if squares is None else [squares]
+    extra = [] if squares is None else [squares, token]
     pieces = [f32(q, docs // 4)] * 4 if squares is None else []
     return pl.pallas_call(
         left_half_kernel,
@@ -335,35 +339,33 @@
     )(near, far, beta)
 
 
-def right_norm_kernel(docs_total, keep, peer, got, beta_core, v0, v1, v2, v3, token, g0, g1, g2, g3, sums, columns):
+def right_norm_kernel(docs_total, keep, peer, got, beta_core, right, g0, g1, g2, g3, sums, columns):
     _, z, _ = coords()
-    q = g0.shape[0] - 8
+    q = right.shape[1]
     beta_sums = beta_core[...] + got[4 * q :, :]
     columns[...] = row_to_column(jnp.sqrt(beta_sums[0:1, :] / docs_total + epsilon))
     beta = columns[pl.ds(pl.multiple_of(z * q, q), q), :][:, 0:1]
     raws = []
-    for k, (v, g) in enumerate(zip((v0, v1, v2, v3), (g0, g1, g2, g3))):
+    for k, g in enumerate((g0, g1, g2, g3)):
         rows = slice(k * q, (k + 1) * q)
         total = (keep[rows, :] + peer[rows, :]) + got[rows, :]
         g[0:q, :] = total
         g[q:, :] = beta_sums
-        raws.append(total / beta - beta * v[0:q, :])
-    line = square_sums(jnp.concatenate(raws, axis=1))
-    for i in range(sums.shape[0]):
-        sums[i] = line
-
-
-def right_norm(docs_total, keep, peer, got, beta_core, messages, token):
+        raws.append(total / beta - beta * right[k])
+    sums[...] = jnp.broadcast_to(square_sums(jnp.concatenate(raws, axis=1)), sums.shape)
+
+
+def right_norm(docs_total, keep, peer, got, beta_core, right):
     q, rows = keep.shape[0] // 4, keep.shape[1]
     *pieces, sums = pl.pallas_call(
         functools.partial(right_norm_kernel, docs_total),
-        out_shape=[f32(q + 8, rows)] * 4 + [f32(32, 1, 128)],
+        out_shape=[f32(q + 8, rows)] * 4 + [f32(32, 128)],
         scratch_shapes=[pltpu.VMEM((4 * q, 128), jnp.float32)],
         compiler_params=params(8),
         cost_estimate=cost(rows * q * 64, rows * q * 100),
         name="right_norm",
-    )(keep, peer, got, beta_core, *messages, token)
-    return pieces, sums
+    )(keep, peer, got, beta_core, right)
+    return pieces, sums.reshape(32, 1, 128)
 
 
 def beta_of(pieces, q, docs_total):
@@ -453,38 +455,38 @@
     feat_total = right_vec.shape[0] * 32
     alpha_row, phibar_row, rhobar_row = (v.reshape(1, -1) for v in (alpha_prev, phibar, rhobar))
 
-    stored, messages = prepare(col_ids.T, col_vals.T, right_vec, left_vec)
-    entries = along_z([stored] * 4)
-    messages = along_z([messages[0]] + [after(m, *entries[1:]) for m in messages[1:]])
-    q = messages[0].shape[0] // 2
-
-    rows1, token1 = build(entries, 1)
-    rows0, _ = build(entries, 0, token1)
-    own = stack(messages, q, "stack_right", token1)
+    first, second = prepare(col_ids.T, col_vals.T, right_vec, left_vec)
+    first = along_z(first)
+    second = along_z(second)
+    q = right_vec.shape[1] // 4
+    lines = first[0].shape[0] - q
+
+    own = stack(first, q, "stack_right", second[1])
     own_x = swap(own, X_BIT)
     own_peer = swap(own, CORE_BIT)
-    total1 = forward_part(rows1, [own, own_peer], (0, 8))
+    rows1 = build(first, lines, own)
+    total1 = forward_part(rows1, [own, own_peer], (0, 8), None, second[2:3])
+    x_peer = swap(after(own_x, total1), CORE_BIT)
+    total1 = forward_part(rows1, [own_x], (4,), total1)
+    product1 = product_half(rows1, x_peer, total1, (12,))
+    rows0 = build(second, lines, product1)
     total0 = forward_part(rows0, [own, own_peer], (0, 8))
-    x_peer = swap(after(own_x, total0, total1), CORE_BIT)
-    total1 = forward_part(rows1, [own_x], (4,), total1)
     total0 = forward_part(rows0, [own_x], (4,), total0)
-    product1 = product_half(rows1, x_peer, total1, (12,))
-    product0 = product_half(rows0, x_peer, total0, (12,), *messages, alpha_row)
+    product0 = product_half(rows0, x_peer, total0, (12,), *second, alpha_row)
 
     *lefts, both0, beta0 = left_half(product0, swap(product1, Y_BIT))
     partial = backward_part(rows0, both0, 0, 16)
-    lefts = along_z(lefts)
-    both1, beta1 = left_half(product1, swap(product0, Y_BIT), beta0)
-    far = swap(backward_part(rows1, both1, 12, 4, partial, beta1, lefts[1:3]), CORE_BIT)
+    left_own = stack(along_z(lefts), q, "stack_left")
+    both1, beta1 = left_half(product1, swap(product0, Y_BIT), beta0, partial)
+    far = swap(backward_part(rows1, both1, 12, 4, partial, beta1, [left_own]), CORE_BIT)
     near = backward_part(rows1, both1, 4, 4, partial)
     send, beta_core = far_sums(near, far, beta1)
     got = swap(send, X_BIT)
     peer = backward_part(rows1, both1, 8, 4, partial)
-    left_own = stack(lefts, q, "stack_left", peer)
-    left_other = swap(left_own, Y_BIT)
+    left_other = swap(after(left_own, peer), Y_BIT)
     keep = backward_part(rows1, both1, 0, 4, partial)
 
-    sent, sums = right_norm(docs_total, keep, swap(peer, CORE_BIT), got, beta_core, messages, left_own)
+    sent, sums = right_norm(docs_total, keep, swap(peer, CORE_BIT), got, beta_core, own)
     pieces = along_z(sent)
     squares = lax.all_to_all(after(sums, left_other), AXES, 0, 0, tiled=True)
     left_next, solution_next = left_out(

time: 90.2 us -> 83.8 us (0.929)
  waiting for transfers between devices: 28.2 us -> 16.6 us
  blocking collectives: 0 us -> 8.88 us
  starting transfers between devices: 30.9 us -> 28 us
    all_to_all x0 -> x1, blocking collectives: none -> 8.88 us  [by_columns(): squares = lax.all_to_all(after(sums, left_other), AXES, 0, 0, tiled=True)]
    all_to_all x1 -> x0, waiting for transfers between devices: 5.86 us -> none  [by_columns(): squares = lax.all_to_all(after(sums, left_other), AXES, 0, 0, tiled=True)]
    ppermute x21, waiting for transfers between devices: 22.4 us -> 16.6 us  [swap(): return lax.ppermute(value, AXES, [(i, i ^ mask) for i in range(32)])]
    all_to_all x1 -> x0, starting transfers between devices: 4.05 us -> none  [by_columns(): squares = lax.all_to_all(after(sums, left_other), AXES, 0, 0, tiled=True)]
    ppermute x21, starting transfers between devices: 26.8 us -> 28 us  [swap(): return lax.ppermute(value, AXES, [(i, i ^ mask) for i in range(32)])]
  transfers between devices with their start and end apart: 22 -> 21, of which waited for: 11 -> 11; matrix products, arithmetic and copies ran while one was open for 0% -> 0% of each run, Pallas kernels for 28% -> 29%
where the time goes in v9:
time: 83.8 us; the launch traced here: 83.6 us
  Pallas kernels  29.1 us (35%)
  starting transfers between devices  28 us (33%)
  waiting for transfers between devices  16.6 us (20%)
  blocking collectives  8.88 us (11%)
  between operations  0.95 us (1%)
    ppermute x21, starting transfers between devices, swap(): return lax.ppermute(value, AXES, [(i, i ^ mask) for i in range(32)])  28 us
    ppermute x21, waiting for transfers between devices, swap(): return lax.ppermute(value, AXES, [(i, i ^ mask) for i in range(32)])  16.6 us
    pallas_call x2, Pallas kernels, build(): pl.pallas_call(build_kernel, in_specs=[whole()] * (4 + len(tokens)), out_...  9.66 us
    all_to_all x1, blocking collectives, by_columns(): squares = lax.all_to_all(after(sums, left_other), AXES, 0, 0, tiled=True)  8.88 us
    pallas_call x4, Pallas kernels, forward_part(): pl.pallas_call(functools.partial(forward_kernel, blocks, before is not No...  7.13 us
    pallas_call x5, Pallas kernels, backward_part(): pl.pallas_call(functools.partial(backward_kernel, first, blocks, tuple(ex...  5.23 us
    pallas_call x2, Pallas kernels, product_half(): pl.pallas_call(functools.partial(product_kernel, blocks), in_specs=[whole...  2.65 us
  transfers between devices with their start and end apart: 21, of which 11 were waited for; matrix products, arithmetic and copies ran while one was open for 0% of the time, Pallas kernels for 29%

profile of v9, /device:TPU:0, one launch (start us, length us, event | category | flops | bytes accessed | tf_op | source)
XLA Modules:
  0.0 83.6 jit_solution(13451407617518036540)
XLA Ops:
  0.6 1.7 %prepare.1 = (f32[96,256]{1,0:T(8,128)S(1)}, f32[96,256]{1,0:T(8,128)S(1)}, f32[96,256]{1,0:T(8,128)S(1)}, f32[96,256]{1,0:T(8,128)S(1)}, f32[96,256]{1,0:T(8,12...) custom-call(s32[16,512]{1,0:T(8,128)} %bitcast.15, bf16[16,512]{1,0:T(8,128)(2,1)} %bitcast.16, ...), custom_call_target="tpu_custom_call" | custom-call | bytes 16384 | tf_op jit(solution)/shard_map/prepare/pallas_call | solution.py:79
  2.3 3.1 %collective-permute-start = (f32[96,256]{1,0:T(8,128)S(1)}, f32[96,256]{1,0:T(8,128)S(1)}, u32[]{:S(2)}, u32[]{:S(2)}) collective-permute-start(f32[96,256]{1,0:T(8,128)S(1)} %get-tuple-element.45), channel_id=1, source_target_pairs={{0,8},{1,9},{2,10},{3,11},{4,12},{5,13},{6,14},{7,15},{8,0},{9,1},... | collective-permute-start | bytes 294920 | tf_op jit(solution)/shard_map/ppermute | solution.py:440
  5.4 0.1 collective-permute-start.3
  5.5 2.9 %collective-permute-start.4 = (f32[96,256]{1,0:T(8,128)S(1)}, f32[96,256]{1,0:T(8,128)S(1)}, u32[]{:S(2)}, u32[]{:S(2)}) collective-permute-start(f32[96,256]{1,0:T(8,128)S(1)} %get-tuple-element.50), channel_id=1, source_target_pairs={{0,16},{1,17},{2,18},{3,19},{4,20},{5,21},{6,22},{7,23},{8,24},{9,... | collective-permute-start | bytes 294920 | tf_op jit(solution)/shard_map/ppermute | solution.py:440
  8.4 1.4 %collective-permute-start.5 = (f32[96,256]{1,0:T(8,128)S(1)}, f32[96,256]{1,0:T(8,128)S(1)}, u32[]{:S(2)}, u32[]{:S(2)}) collective-permute-start(f32[96,256]{1,0:T(8,128)S(1)} %get-tuple-element.51), channel_id=1, source_target_pairs={{0,24},{1,25},{2,26},{3,27},{4,28},{5,29},{6,30},{7,31},{8,16},{9,... | collective-permute-start | bytes 294920 | tf_op jit(solution)/shard_map/ppermute | solution.py:440
  9.8 0.2 collective-permute-done.refs_0_.e1.refs_1_
  10.0 2.5 %collective-permute-done.3.m1.e1 = f32[96,256]{1,0:T(8,128)S(1)} collective-permute-done((f32[96,256]{1,0:T(8,128)S(1)}, f32[96,256]{1,0:T(8,128)S(1)}, u32[]{:S(2)}, u32[]{:S(2)}) %collective-permute-start.3) | collective-permute-done | bytes 98336 | tf_op jit(solution)/shard_map/ppermute | solution.py:440
  12.4 0.4 collective-permute-done.4.m2.e2
  12.8 4.1 %collective-permute-done.5.m3.e3 = f32[96,256]{1,0:T(8,128)S(1)} collective-permute-done((f32[96,256]{1,0:T(8,128)S(1)}, f32[96,256]{1,0:T(8,128)S(1)}, u32[]{:S(2)}, u32[]{:S(2)}) %collective-permute-start.5) | collective-permute-done | bytes 98336 | tf_op jit(solution)/shard_map/ppermute | solution.py:440
  16.9 0.1 collective-permute-start.7
  17.0 1.6 %collective-permute-start.6 = (f32[4,64,256]{2,1,0:T(8,128)S(1)}, f32[4,64,256]{2,1,0:T(8,128)S(1)}, u32[]{:S(2)}, u32[]{:S(2)}) collective-permute-start(f32[4,64,256]{2,1,0:T(8,128)S(1)} %stack_right.1.refs_0_.right), channel_id=1, source_target_pairs={{0,4},{1,5},{2,6},{3,7},{4,0},{5,1},{6,2},{7,3},{8,12},{9,13},{10,... | collective-permute-start | bytes 786440 | tf_op jit(solution)/shard_map/ppermute | solution.py:440
  18.5 2.9 %collective-permute-start.1 = (f32[96,256]{1,0:T(8,128)S(1)}, f32[96,256]{1,0:T(8,128)S(1)}, u32[]{:S(2)}, u32[]{:S(2)}) collective-permute-start(f32[96,256]{1,0:T(8,128)S(1)} %get-tuple-element.46), channel_id=1, source_target_pairs={{0,16},{1,17},{2,18},{3,19},{4,20},{5,21},{6,22},{7,23},{8,24},{9,... | collective-permute-start | bytes 294920 | tf_op jit(solution)/shard_map/ppermute | solution.py:440
  21.4 4.8 %dense_rows.2 = (bf16[16,1024,256]{2,1,0:T(8,128)(2,1)S(1)}, bf16[16,1024,256]{2,1,0:T(8,128)(2,1)S(1)}) custom-call(f32[96,256]{1,0:T(8,128)S(1)} %get-tuple-element.48.m0.e0, f32[96,256]{1,0:T(8,128)S(1)} %collective-permute-done.3.m1.e1, f32[96,256]{1,0:T(8,128)S(1)} %collective-permute-done.4.m2.e2, f32[96,256]{1,0:T(8,128)S(1)} %collective-permute-done.5.m3.e3, ...), custom_call_target="tpu_custom_call" | custom-call | flops 33554432 | bytes 262144 | tf_op jit(solution)/shard_map/dense_rows/pallas_call | solution.py:159
  26.2 0.5 collective-permute-done.1.refs_2_.e2
  26.6 2.3 %forward_part.4.refs_1_ = f32[1024,128]{1,0:T(8,128)S(1)} custom-call(bf16[16,1024,256]{2,1,0:T(8,128)(2,1)S(1)} %get-tuple-element.52.hi_ref, bf16[16,1024,256]{2,1,0:T(8,128)(2,1)S(1)} %get-tuple-element.53.lo_ref, f32[4,64,256]{2,1,0:T(8,128)S(1)} %stack_right.1.refs_0_.right, f32[4,64,256]{2,1,0:T(8,128)S(1)} %collective-permute-done.7.refs_1_, ...), custom_call_target="tpu_custom_call" | custom-call | flops 67108864 | bytes 131072 | tf_op jit(solution)/shard_map/forward_part/pallas_call | solution.py:200
  29.0 0.1 collective-permute-start.8
  29.1 2.6 %collective-permute-start.2 = (f32[96,256]{1,0:T(8,128)S(1)}, f32[96,256]{1,0:T(8,128)S(1)}, u32[]{:S(2)}, u32[]{:S(2)}) collective-permute-start(f32[96,256]{1,0:T(8,128)S(1)} %get-tuple-element.47), channel_id=1, source_target_pairs={{0,24},{1,25},{2,26},{3,27},{4,28},{5,29},{6,30},{7,31},{8,16},{9,... | collective-permute-start | bytes 294920 | tf_op jit(solution)/shard_map/ppermute | solution.py:440
  31.6 1.2 %forward_part.5.before = f32[1024,128]{1,0:T(8,128)S(1)} custom-call(bf16[16,1024,256]{2,1,0:T(8,128)(2,1)S(1)} %get-tuple-element.52.hi_ref, bf16[16,1024,256]{2,1,0:T(8,128)(2,1)S(1)} %get-tuple-element.53.lo_ref, f32[4,64,256]{2,1,0:T(8,128)S(1)} %collective-permute-done.6.refs_0_, f32[1024,128]{1,0:T(8,128)S(1)} %forward_part.4.refs_1_), custom_call_target="tpu_custom_call" | custom-call | flops 33554432 | bytes 65536 | tf_op jit(solution)/shard_map/forward_part/pallas_call | solution.py:200
  32.9 1.3 %product_half.2.refs_0_.mine = f32[64,1024]{1,0:T(8,128)S(1)} custom-call(bf16[16,1024,256]{2,1,0:T(8,128)(2,1)S(1)} %get-tuple-element.52.hi_ref, bf16[16,1024,256]{2,1,0:T(8,128)(2,1)S(1)} %get-tuple-element.53.lo_ref, f32[4,64,256]{2,1,0:T(8,128)S(1)} %collective-permute-done.8.vec, f32[1024,128]{1,0:T(8,128)S(1)} %forward_part.5.before), custom_call_target="tpu_custom_call" | custom-call | flops 33554432 | bytes 65536 | tf_op jit(solution)/shard_map/product_half/pallas_call | solution.py:232
  34.2 1.6 %collective-permute-start.9 = (f32[64,1024]{1,0:T(8,128)S(1)}, f32[64,1024]{1,0:T(8,128)S(1)}, u32[]{:S(2)}, u32[]{:S(2)}) collective-permute-start(f32[64,1024]{1,0:T(8,128)S(1)} %product_half.2.refs_0_.mine), channel_id=1, source_target_pairs={{0,1},{1,0},{2,3},{3,2},{4,5},{5,4},{6,7},{7,6},{8,9},{9,8},{10,11... | collective-permute-start | bytes 786440 | tf_op jit(solution)/shard_map/ppermute | solution.py:440
  35.8 0.3 collective-permute-done.2.e3.refs_3_
  36.1 4.9 %dense_rows.3 = (bf16[16,1024,256]{2,1,0:T(8,128)(2,1)S(1)}, bf16[16,1024,256]{2,1,0:T(8,128)(2,1)S(1)}) custom-call(f32[96,256]{1,0:T(8,128)S(1)} %get-tuple-element.44.e0.refs_0_, f32[96,256]{1,0:T(8,128)S(1)} %collective-permute-done.refs_0_.e1.refs_1_, f32[96,256]{1,0:T(8,128)S(1)} %collective-permute-done.1.refs_2_.e2, ...), custom_call_target="tpu_custom_call" | custom-call | flops 33554432 | bytes 262144 | tf_op jit(solution)/shard_map/dense_rows/pallas_call | solution.py:159
  41.0 2.3 %forward_part.6.refs_1_ = f32[1024,128]{1,0:T(8,128)S(1)} custom-call(bf16[16,1024,256]{2,1,0:T(8,128)(2,1)S(1)} %get-tuple-element.55.hi_ref, bf16[16,1024,256]{2,1,0:T(8,128)(2,1)S(1)} %get-tuple-element.56.lo_ref, f32[4,64,256]{2,1,0:T(8,128)S(1)} %stack_right.1.refs_0_.right, f32[4,64,256]{2,1,0:T(8,128)S(1)} %collective-permute-done.7.refs_1_), custom_call_target="tpu_custom_call" | custom-call | flops 67108864 | bytes 131072 | tf_op jit(solution)/shard_map/forward_part/pallas_call | solution.py:200
  43.3 1.2 %forward_part.7.before = f32[1024,128]{1,0:T(8,128)S(1)} custom-call(bf16[16,1024,256]{2,1,0:T(8,128)(2,1)S(1)} %get-tuple-element.55.hi_ref, bf16[16,1024,256]{2,1,0:T(8,128)(2,1)S(1)} %get-tuple-element.56.lo_ref, f32[4,64,256]{2,1,0:T(8,128)S(1)} %collective-permute-done.6.refs_0_, f32[1024,128]{1,0:T(8,128)S(1)} %forward_part.6.refs_1_), custom_call_target="tpu_custom_call" | custom-call | flops 33554432 | bytes 65536 | tf_op jit(solution)/shard_map/forward_part/pallas_call | solution.py:200
  44.6 1.3 %product_half.3.mine = f32[64,1024]{1,0:T(8,128)S(1)} custom-call(bf16[16,1024,256]{2,1,0:T(8,128)(2,1)S(1)} %get-tuple-element.55.hi_ref, bf16[16,1024,256]{2,1,0:T(8,128)(2,1)S(1)} %get-tuple-element.56.lo_ref, f32[4,64,256]{2,1,0:T(8,128)S(1)} %collective-permute-done.8.vec, f32[1024,128]{1,0:T(8,128)S(1)} %forward_part.7.before, ...), custom_call_target="tpu_custom_call" | custom-call | flops 33554432 | bytes 65536 | tf_op jit(solution)/shard_map/product_half/pallas_call | solution.py:232
  45.9 1.6 %collective-permute-start.13 = (f32[64,1024]{1,0:T(8,128)S(1)}, f32[64,1024]{1,0:T(8,128)S(1)}, u32[]{:S(2)}, u32[]{:S(2)}) collective-permute-start(f32[64,1024]{1,0:T(8,128)S(1)} %product_half.3.mine), channel_id=1, source_target_pairs={{0,1},{1,0},{2,3},{3,2},{4,5},{5,4},{6,7},{7,6},{8,9},{9,8},{10,11... | collective-permute-start | bytes 786440 | tf_op jit(solution)/shard_map/ppermute | solution.py:440
  47.5 0.1 left_half.2
  47.8 3.0 %collective-permute-start.11 = (f32[64,256]{1,0:T(8,128)S(1)}, f32[64,256]{1,0:T(8,128)S(1)}, u32[]{:S(2)}, u32[]{:S(2)}) collective-permute-start(f32[64,256]{1,0:T(8,128)S(1)} %get-tuple-element.59), channel_id=1, source_target_pairs={{0,16},{1,17},{2,18},{3,19},{4,20},{5,21},{6,22},{7,23},{8,24},{9,... | collective-permute-start | bytes 196616 | tf_op jit(solution)/shard_map/ppermute | solution.py:440
  50.8 1.3 %collective-permute-start.12 = (f32[64,256]{1,0:T(8,128)S(1)}, f32[64,256]{1,0:T(8,128)S(1)}, u32[]{:S(2)}, u32[]{:S(2)}) collective-permute-start(f32[64,256]{1,0:T(8,128)S(1)} %get-tuple-element.60), channel_id=1, source_target_pairs={{0,24},{1,25},{2,26},{3,27},{4,28},{5,29},{6,30},{7,31},{8,16},{9,... | collective-permute-start | bytes 196616 | tf_op jit(solution)/shard_map/ppermute | solution.py:440
  52.1 2.3 %backward_part.5.refs_1_.refs_0_ = f32[1024,256]{1,0:T(8,128)S(1)} custom-call(bf16[16,1024,256]{2,1,0:T(8,128)(2,1)S(1)} %get-tuple-element.55.hi_ref, bf16[16,1024,256]{2,1,0:T(8,128)(2,1)S(1)} %get-tuple-element.56.lo_ref, bf16[128,1024]{1,0:T(8,128)(2,1)S(1)} %get-tuple-element.62.both_ref), custom_call_target="tpu_custom_call" | custom-call | flops 134217728 | bytes 262144 | tf_op jit(solution)/shard_map/backward_part/pallas_call | solution.py:313
  54.5 0.2 left_half.3
  54.7 0.8 collective-permute-done.11.m2
  55.4 1.4 %collective-permute-done.12.m3 = f32[64,256]{1,0:T(8,128)S(1)} collective-permute-done((f32[64,256]{1,0:T(8,128)S(1)}, f32[64,256]{1,0:T(8,128)S(1)}, u32[]{:S(2)}, u32[]{:S(2)}) %collective-permute-start.12) | collective-permute-done | bytes 65568 | tf_op jit(solution)/shard_map/ppermute | solution.py:440
  56.9 0.7 backward_part.9
  57.7 0.7 backward_part.8.near
  58.4 0.8 collective-permute-done.16.far
  59.3 0.6 collective-permute-start.17
  59.9 0.7 backward_part.6
  60.8 0.6 collective-permute-start.14
  61.4 0.7 backward_part.7.keep
  62.1 0.2 collective-permute-done.15.peer
  62.3 5.6 %collective-permute-done.17.got = f32[264,256]{1,0:T(8,128)S(1)} collective-permute-done((f32[264,256]{1,0:T(8,128)S(1)}, f32[264,256]{1,0:T(8,128)S(1)}, u32[]{:S(2)}, u32[]{:S(2)}) %collective-permute-start.17) | collective-permute-done | bytes 270368 | tf_op jit(solution)/shard_map/ppermute | solution.py:440
  67.9 0.3 right_norm.1
  68.3 2.0 %collective-permute-start.19 = (f32[72,256]{1,0:T(8,128)S(1)}, f32[72,256]{1,0:T(8,128)S(1)}, u32[]{:S(2)}, u32[]{:S(2)}) collective-permute-start(f32[72,256]{1,0:T(8,128)S(1)} %get-tuple-element.70), channel_id=1, source_target_pairs={{0,16},{1,17},{2,18},{3,19},{4,20},{5,21},{6,22},{7,23},{8,24},{9,... | collective-permute-start | bytes 221192 | tf_op jit(solution)/shard_map/ppermute | solution.py:440
  70.3 2.4 %collective-permute-start.20 = (f32[72,256]{1,0:T(8,128)S(1)}, f32[72,256]{1,0:T(8,128)S(1)}, u32[]{:S(2)}, u32[]{:S(2)}) collective-permute-start(f32[72,256]{1,0:T(8,128)S(1)} %get-tuple-element.71), channel_id=1, source_target_pairs={{0,24},{1,25},{2,26},{3,27},{4,28},{5,29},{6,30},{7,31},{8,16},{9,... | collective-permute-start | bytes 221192 | tf_op jit(solution)/shard_map/ppermute | solution.py:440
  72.6 8.9 %all_to_all.5.squares = f32[32,1,128]{2,1,0:T(1,128)S(1)} all-to-all(f32[32,1,128]{2,1,0:T(1,128)S(1)} %bitcast.9), channel_id=1, replica_groups=mesh['doc'=16,'feat'=2] {'doc','feat'}, dimensions={0} | all-to-all | bytes 32768 | tf_op jit(solution)/shard_map/all_to_all | solution.py:491
  81.6 1.0 %finish.1 = (f32[256,256]{1,0:T(8,128)}, f32[256,256]{1,0:T(8,128)}, f32[1,256]{1,0:T(1,128)}, f32[1,256]{1,0:T(1,128)}, f32[1,256]{1,0:T(1,128)}) custom-call(f32[72,256]{1,0:T(8,128)S(1)} %get-tuple-element.68.g0, f32[72,256]{1,0:T(8,128)S(1)} %collective-permute-done.18.g1, f32[72,256]{1,0:T(8,128)S(1)} %collective-permute-done.19.g2, ...), custom_call_target="tpu_custom_call" | custom-call | flops 16384 | bytes 20480 | tf_op jit(solution)/shard_map/finish/pallas_call | solution.py:404
  82.5 1.1 %left_out.1 = (f32[512,256]{1,0:T(8,128)}, f32[256,256]{1,0:T(8,128)}) custom-call(f32[4,64,256]{2,1,0:T(8,128)S(1)} %stack_left.1.refs_2_.own, f32[4,64,256]{2,1,0:T(8,128)S(1)} %collective-permute-done.14.other, f32[72,256]{1,0:T(8,128)S(1)} %get-tuple-element.68.g0, f32[72,256]{1,0:T(8,128)S(1)} %collective-permute-done.18.g1, ...), custom_call_target="tpu_custom_call" | custom-call | flops 8192 | bytes 30720 | tf_op jit(solution)/shard_map/left_out/pallas_call | solution.py:429
  (29 shorter events, 0.4 us)
Async XLA Ops:
  2.3 7.7 %collective-permute-start = (f32[96,256]{1,0:T(8,128)S(1)}, f32[96,256]{1,0:T(8,128)S(1)}, u32[]{:S(2)}, u32[]{:S(2)}) collective-permute-start(f32[96,256]{1,0:T(8,128)S(1)} %get-tuple-element.45), channel_id=1, source_target_pairs={{0,8},{1,9},{2,10},{3,11},{4,12},{5,13},{6,14},{7,15},{8,0},{9,1},... | collective-permute-start | bytes 294920 | tf_op jit(solution)/shard_map/ppermute | solution.py:440
  5.4 7.0 %collective-permute-start.3 = (f32[96,256]{1,0:T(8,128)S(1)}, f32[96,256]{1,0:T(8,128)S(1)}, u32[]{:S(2)}, u32[]{:S(2)}) collective-permute-start(f32[96,256]{1,0:T(8,128)S(1)} %get-tuple-element.49), channel_id=1, source_target_pairs={{0,8},{1,9},{2,10},{3,11},{4,12},{5,13},{6,14},{7,15},{8,0},{9,1},... | collective-permute-start | bytes 294920 | tf_op jit(solution)/shard_map/ppermute | solution.py:440
  5.5 7.3 %collective-permute-start.4 = (f32[96,256]{1,0:T(8,128)S(1)}, f32[96,256]{1,0:T(8,128)S(1)}, u32[]{:S(2)}, u32[]{:S(2)}) collective-permute-start(f32[96,256]{1,0:T(8,128)S(1)} %get-tuple-element.50), channel_id=1, source_target_pairs={{0,16},{1,17},{2,18},{3,19},{4,20},{5,21},{6,22},{7,23},{8,24},{9,... | collective-permute-start | bytes 294920 | tf_op jit(solution)/shard_map/ppermute | solution.py:440
  8.4 8.4 %collective-permute-start.5 = (f32[96,256]{1,0:T(8,128)S(1)}, f32[96,256]{1,0:T(8,128)S(1)}, u32[]{:S(2)}, u32[]{:S(2)}) collective-permute-start(f32[96,256]{1,0:T(8,128)S(1)} %get-tuple-element.51), channel_id=1, source_target_pairs={{0,24},{1,25},{2,26},{3,27},{4,28},{5,29},{6,30},{7,31},{8,16},{9,... | collective-permute-start | bytes 294920 | tf_op jit(solution)/shard_map/ppermute | solution.py:440
  16.9 9.7 %collective-permute-start.7 = (f32[4,64,256]{2,1,0:T(8,128)S(1)}, f32[4,64,256]{2,1,0:T(8,128)S(1)}, u32[]{:S(2)}, u32[]{:S(2)}) collective-permute-start(f32[4,64,256]{2,1,0:T(8,128)S(1)} %stack_right.1.refs_0_.right), channel_id=1, source_target_pairs={{0,2},{1,3},{2,0},{3,1},{4,6},{5,7},{6,4},{7,5},{8,10},{9,11},{10,... | collective-permute-start | bytes 786440 | tf_op jit(solution)/shard_map/ppermute | solution.py:440
  17.0 12.0 %collective-permute-start.6 = (f32[4,64,256]{2,1,0:T(8,128)S(1)}, f32[4,64,256]{2,1,0:T(8,128)S(1)}, u32[]{:S(2)}, u32[]{:S(2)}) collective-permute-start(f32[4,64,256]{2,1,0:T(8,128)S(1)} %stack_right.1.refs_0_.right), channel_id=1, source_target_pairs={{0,4},{1,5},{2,6},{3,7},{4,0},{5,1},{6,2},{7,3},{8,12},{9,13},{10,... | collective-permute-start | bytes 786440 | tf_op jit(solution)/shard_map/ppermute | solution.py:440
  18.5 8.1 %collective-permute-start.1 = (f32[96,256]{1,0:T(8,128)S(1)}, f32[96,256]{1,0:T(8,128)S(1)}, u32[]{:S(2)}, u32[]{:S(2)}) collective-permute-start(f32[96,256]{1,0:T(8,128)S(1)} %get-tuple-element.46), channel_id=1, source_target_pairs={{0,16},{1,17},{2,18},{3,19},{4,20},{5,21},{6,22},{7,23},{8,24},{9,... | collective-permute-start | bytes 294920 | tf_op jit(solution)/shard_map/ppermute | solution.py:440
  29.0 3.9 %collective-permute-start.8 = (f32[4,64,256]{2,1,0:T(8,128)S(1)}, f32[4,64,256]{2,1,0:T(8,128)S(1)}, u32[]{:S(2)}, u32[]{:S(2)}) collective-permute-start(f32[4,64,256]{2,1,0:T(8,128)S(1)} %collective-permute-done.6.refs_0_), channel_id=1, source_target_pairs={{0,2},{1,3},{2,0},{3,1},{4,6},{5,7},{6,4},{7,5},{8,10},{9,11},{10,... | collective-permute-start | bytes 786440 | tf_op jit(solution)/shard_map/ppermute | solution.py:440
  29.1 7.0 %collective-permute-start.2 = (f32[96,256]{1,0:T(8,128)S(1)}, f32[96,256]{1,0:T(8,128)S(1)}, u32[]{:S(2)}, u32[]{:S(2)}) collective-permute-start(f32[96,256]{1,0:T(8,128)S(1)} %get-tuple-element.47), channel_id=1, source_target_pairs={{0,24},{1,25},{2,26},{3,27},{4,28},{5,29},{6,30},{7,31},{8,16},{9,... | collective-permute-start | bytes 294920 | tf_op jit(solution)/shard_map/ppermute | solution.py:440
  34.2 13.3 %collective-permute-start.9 = (f32[64,1024]{1,0:T(8,128)S(1)}, f32[64,1024]{1,0:T(8,128)S(1)}, u32[]{:S(2)}, u32[]{:S(2)}) collective-permute-start(f32[64,1024]{1,0:T(8,128)S(1)} %product_half.2.refs_0_.mine), channel_id=1, source_target_pairs={{0,1},{1,0},{2,3},{3,2},{4,5},{5,4},{6,7},{7,6},{8,9},{9,8},{10,11... | collective-permute-start | bytes 786440 | tf_op jit(solution)/shard_map/ppermute | solution.py:440
  43.3 1.3 %copy-start.5 = (f32[256]{0:T(256)S(1)}, f32[256]{0:T(256)}, u32[]{:S(2)}) copy-start(f32[256]{0:T(256)} %param.15) | copy-start | bytes 3076
  45.9 8.5 %collective-permute-start.13 = (f32[64,1024]{1,0:T(8,128)S(1)}, f32[64,1024]{1,0:T(8,128)S(1)}, u32[]{:S(2)}, u32[]{:S(2)}) collective-permute-start(f32[64,1024]{1,0:T(8,128)S(1)} %product_half.3.mine), channel_id=1, source_target_pairs={{0,1},{1,0},{2,3},{3,2},{4,5},{5,4},{6,7},{7,6},{8,9},{9,8},{10,11... | collective-permute-start | bytes 786440 | tf_op jit(solution)/shard_map/ppermute | solution.py:440
  47.7 7.0 %collective-permute-start.10 = (f32[64,256]{1,0:T(8,128)S(1)}, f32[64,256]{1,0:T(8,128)S(1)}, u32[]{:S(2)}, u32[]{:S(2)}) collective-permute-start(f32[64,256]{1,0:T(8,128)S(1)} %get-tuple-element.58), channel_id=1, source_target_pairs={{0,8},{1,9},{2,10},{3,11},{4,12},{5,13},{6,14},{7,15},{8,0},{9,1},... | collective-permute-start | bytes 196616 | tf_op jit(solution)/shard_map/ppermute | solution.py:440
  47.8 7.7 %collective-permute-start.11 = (f32[64,256]{1,0:T(8,128)S(1)}, f32[64,256]{1,0:T(8,128)S(1)}, u32[]{:S(2)}, u32[]{:S(2)}) collective-permute-start(f32[64,256]{1,0:T(8,128)S(1)} %get-tuple-element.59), channel_id=1, source_target_pairs={{0,16},{1,17},{2,18},{3,19},{4,20},{5,21},{6,22},{7,23},{8,24},{9,... | collective-permute-start | bytes 196616 | tf_op jit(solution)/shard_map/ppermute | solution.py:440
  50.8 6.1 %collective-permute-start.12 = (f32[64,256]{1,0:T(8,128)S(1)}, f32[64,256]{1,0:T(8,128)S(1)}, u32[]{:S(2)}, u32[]{:S(2)}) collective-permute-start(f32[64,256]{1,0:T(8,128)S(1)} %get-tuple-element.60), channel_id=1, source_target_pairs={{0,24},{1,25},{2,26},{3,27},{4,28},{5,29},{6,30},{7,31},{8,16},{9,... | collective-permute-start | bytes 196616 | tf_op jit(solution)/shard_map/ppermute | solution.py:440
  57.6 1.6 %collective-permute-start.16 = (f32[264,256]{1,0:T(8,128)S(1)}, f32[264,256]{1,0:T(8,128)S(1)}, u32[]{:S(2)}, u32[]{:S(2)}) collective-permute-start(f32[264,256]{1,0:T(8,128)S(1)} %backward_part.9), channel_id=1, source_target_pairs={{0,2},{1,3},{2,0},{3,1},{4,6},{5,7},{6,4},{7,5},{8,10},{9,11},{10,... | collective-permute-start | bytes 811016 | tf_op jit(solution)/shard_map/ppermute | solution.py:440
  59.3 8.6 %collective-permute-start.17 = (f32[264,256]{1,0:T(8,128)S(1)}, f32[264,256]{1,0:T(8,128)S(1)}, u32[]{:S(2)}, u32[]{:S(2)}) collective-permute-start(f32[264,256]{1,0:T(8,128)S(1)} %get-tuple-element.66), channel_id=1, source_target_pairs={{0,4},{1,5},{2,6},{3,7},{4,0},{5,1},{6,2},{7,3},{8,12},{9,13},{10,... | collective-permute-start | bytes 811016 | tf_op jit(solution)/shard_map/ppermute | solution.py:440
  60.6 20.9 %copy-start = (f32[256,256]{1,0:T(8,128)S(1)}, f32[256,256]{1,0:T(8,128)}, u32[]{:S(2)}) copy-start(f32[256,256]{1,0:T(8,128)} %right.1) | copy-start | bytes 786436
  60.7 20.9 %copy-start.1 = (f32[256,256]{1,0:T(8,128)S(1)}, f32[256,256]{1,0:T(8,128)}, u32[]{:S(2)}) copy-start(f32[256,256]{1,0:T(8,128)} %search.3) | copy-start | bytes 786436
  60.7 20.9 %copy-start.3 = (f32[256]{0:T(256)S(1)}, f32[256]{0:T(256)}, u32[]{:S(2)}) copy-start(f32[256]{0:T(256)} %param.16) | copy-start | bytes 3076
  60.7 20.9 %copy-start.4 = (f32[256]{0:T(256)S(1)}, f32[256]{0:T(256)}, u32[]{:S(2)}) copy-start(f32[256]{0:T(256)} %param.17) | copy-start | bytes 3076
  60.7 21.8 %copy-start.2 = (f32[256,256]{1,0:T(8,128)S(1)}, f32[256,256]{1,0:T(8,128)}, u32[]{:S(2)}) copy-start(f32[256,256]{1,0:T(8,128)} %solution.1) | copy-start | bytes 786436
  60.7 1.6 %collective-permute-start.15 = (f32[256,256]{1,0:T(8,128)S(1)}, f32[256,256]{1,0:T(8,128)S(1)}, u32[]{:S(2)}, u32[]{:S(2)}) collective-permute-start(f32[256,256]{1,0:T(8,128)S(1)} %backward_part.6), channel_id=1, source_target_pairs={{0,2},{1,3},{2,0},{3,1},{4,6},{5,7},{6,4},{7,5},{8,10},{9,11},{10,... | collective-permute-start | bytes 786440 | tf_op jit(solution)/shard_map/ppermute | solution.py:440
  60.8 11.9 %collective-permute-start.14 = (f32[4,64,256]{2,1,0:T(8,128)S(1)}, f32[4,64,256]{2,1,0:T(8,128)S(1)}, u32[]{:S(2)}, u32[]{:S(2)}) collective-permute-start(f32[4,64,256]{2,1,0:T(8,128)S(1)} %stack_left.1.refs_2_.own), channel_id=1, source_target_pairs={{0,1},{1,0},{2,3},{3,2},{4,5},{5,4},{6,7},{7,6},{8,9},{9,8},{10,11... | collective-permute-start | bytes 786440 | tf_op jit(solution)/shard_map/ppermute | solution.py:440
  68.2 13.3 %collective-permute-start.18 = (f32[72,256]{1,0:T(8,128)S(1)}, f32[72,256]{1,0:T(8,128)S(1)}, u32[]{:S(2)}, u32[]{:S(2)}) collective-permute-start(f32[72,256]{1,0:T(8,128)S(1)} %get-tuple-element.69), channel_id=1, source_target_pairs={{0,8},{1,9},{2,10},{3,11},{4,12},{5,13},{6,14},{7,15},{8,0},{9,1},... | collective-permute-start | bytes 221192 | tf_op jit(solution)/shard_map/ppermute | solution.py:440
  68.3 13.3 %collective-permute-start.19 = (f32[72,256]{1,0:T(8,128)S(1)}, f32[72,256]{1,0:T(8,128)S(1)}, u32[]{:S(2)}, u32[]{:S(2)}) collective-permute-start(f32[72,256]{1,0:T(8,128)S(1)} %get-tuple-element.70), channel_id=1, source_target_pairs={{0,16},{1,17},{2,18},{3,19},{4,20},{5,21},{6,22},{7,23},{8,24},{9,... | collective-permute-start | bytes 221192 | tf_op jit(solution)/shard_map/ppermute | solution.py:440
  70.3 11.3 %collective-permute-start.20 = (f32[72,256]{1,0:T(8,128)S(1)}, f32[72,256]{1,0:T(8,128)S(1)}, u32[]{:S(2)}, u32[]{:S(2)}) collective-permute-start(f32[72,256]{1,0:T(8,128)S(1)} %get-tuple-element.71), channel_id=1, source_target_pairs={{0,24},{1,25},{2,26},{3,27},{4,28},{5,29},{6,30},{7,31},{8,16},{9,... | collective-permute-start | bytes 221192 | tf_op jit(solution)/shard_map/ppermute | solution.py:440

commit v10 on v7

--- a/solution.py
+++ b/solution.py
@@ -26,8 +26,8 @@
     return pltpu.CompilerParams(vmem_limit_bytes=mib * MIB)
 
 
-def cost(flops, nbytes):
-    return pl.CostEstimate(flops=int(flops), bytes_accessed=int(nbytes), transcendentals=0)
+def cost(flops, nbytes, scale=64):
+    return pl.CostEstimate(flops=int(flops) // scale, bytes_accessed=int(nbytes) // scale, transcendentals=0)
 
 
 def f32(*shape):
@@ -157,7 +157,7 @@
         out_specs=[whole()] * 3,
         out_shape=[pltpu.VMEM((16, docs, 256), jnp.bfloat16)] * 2 + [f32(8, 128)],
         compiler_params=params(8),
-        cost_estimate=cost(2 * docs * 16 * 256 * 256, docs * 4096 * 4),
+        cost_estimate=cost(2 * docs * 16 * 256 * 256, docs * 4096 * 4, 1 if rel else 64),
         name="dense_rows",
     )(*entries, *tokens)
     return rows, token
@@ -262,16 +262,16 @@
     both, sums = refs[-2:]
     both[...] = split_rows(left)
     squares = square_row(left, z, sums.shape[1])
-    sums[...] = refs[0][...] + squares if len(refs) == 3 else squares
-    if len(refs) > 3:
+    sums[...] = refs[0][...] + squares if len(refs) == 4 else squares
+    if len(refs) > 4:
         n = left.shape[1] // 4
         for k, out in enumerate(refs[:4]):
             out[...] = left[:, k * n : (k + 1) * n]
 
 
-def left_half(mine, other, squares=None):
+def left_half(mine, other, squares=None, token=None):
     q, docs = mine.shape
-    extra = [] if squares is None else [squares]
+    extra = [] if squares is None else [squares, token]
     pieces = [f32(q, docs // 4)] * 4 if squares is None else []
     return pl.pallas_call(
         left_half_kernel,
@@ -335,103 +335,84 @@
     )(near, far, beta)
 
 
-def right_norm_kernel(docs_total, keep, peer, got, beta_core, v0, v1, v2, v3, token, g0, g1, g2, g3, sums, columns):
+def right_norm_kernel(docs_total, keep, peer, got, beta_core, right, g0, g1, g2, g3, sums, columns):
     _, z, _ = coords()
-    q = g0.shape[0] - 8
-    beta_sums = beta_core[...] + got[4 * q :, :]
-    columns[...] = row_to_column(jnp.sqrt(beta_sums[0:1, :] / docs_total + epsilon))
+    q = right.shape[1]
+    beta_sums = beta_core[0:1, :] + got[4 * q : 4 * q + 1, :]
+    columns[...] = row_to_column(jnp.sqrt(beta_sums / docs_total + epsilon))
     beta = columns[pl.ds(pl.multiple_of(z * q, q), q), :][:, 0:1]
     raws = []
-    for k, (v, g) in enumerate(zip((v0, v1, v2, v3), (g0, g1, g2, g3))):
+    for k, g in enumerate((g0, g1, g2, g3)):
         rows = slice(k * q, (k + 1) * q)
         total = (keep[rows, :] + peer[rows, :]) + got[rows, :]
-        g[0:q, :] = total
-        g[q:, :] = beta_sums
-        raws.append(total / beta - beta * v[0:q, :])
+        g[...] = total
+        raws.append(total / beta - beta * right[k])
     line = square_sums(jnp.concatenate(raws, axis=1))
-    for i in range(sums.shape[0]):
-        sums[i] = line
-
-
-def right_norm(docs_total, keep, peer, got, beta_core, messages, token):
+    folded = beta_sums[:, :128] + beta_sums[:, 128:]
+    folded = folded + jnp.concatenate([folded[:, q:], folded[:, :q]], axis=1)
+    low = lax.broadcasted_iota(jnp.int32, line.shape, 1) < q
+    sums[...] = jnp.broadcast_to(jnp.where(low, line, folded), sums.shape)
+
+
+def right_norm(docs_total, keep, peer, got, beta_core, right):
     q, rows = keep.shape[0] // 4, keep.shape[1]
     *pieces, sums = pl.pallas_call(
         functools.partial(right_norm_kernel, docs_total),
-        out_shape=[f32(q + 8, rows)] * 4 + [f32(32, 1, 128)],
+        out_shape=[f32(q, rows)] * 4 + [f32(32, 128)],
         scratch_shapes=[pltpu.VMEM((4 * q, 128), jnp.float32)],
         compiler_params=params(8),
         cost_estimate=cost(rows * q * 64, rows * q * 100),
         name="right_norm",
-    )(keep, peer, got, beta_core, *messages, token)
-    return pieces, sums
-
-
-def beta_of(pieces, q, docs_total):
-    squares = [g[q : q + 1, :] for g in pieces]
-    return jnp.sqrt(((squares[0] + squares[1]) + (squares[2] + squares[3])) / docs_total + epsilon)
-
-
-def finish_kernel(docs_total, feat_total, g0, g1, g2, g3, squares, right, search, phibar, rhobar,
-                  right_out, search_out, alpha_out, phibar_out, rhobar_out, turned):
-    _, z, _ = coords()
-    q = turned.shape[1]
-    for k, g in enumerate((g0, g1, g2, g3)):
-        turned[z ^ k] = g[0:q, :]
-    got = turned[...].reshape(-1, turned.shape[2]).T
+    )(keep, peer, got, beta_core, right)
+    return pieces, sums.reshape(32, 1, 128)
+
+
+def finish_kernel(docs_total, feat_total, g0, g1, g2, g3, squares, own, other, right, search, solution, phibar, rhobar,
+                  left_out, right_out, search_out, solution_out, alpha_out, phibar_out, rhobar_out, turned):
+    _, z, y = coords()
+    q, half = turned.shape[1:]
     parts = [squares[i] for i in range(32)]
+    high = [jnp.concatenate([parts[8 * i][:, q:], parts[8 * i][:, :q]], axis=1) if i % 2 == 0 else parts[8 * i] for i in range(4)]
     while len(parts) > 4:
         parts = [a + b for a, b in zip(parts[::2], parts[1::2])]
+    parts[1::2] = [jnp.concatenate([p[:, q:], p[:, :q]], axis=1) for p in parts[1::2]]
     low = lax.broadcasted_iota(jnp.int32, parts[0].shape, 1) < q
-    parts = [jnp.where(low, parts[0], parts[1]), jnp.where(low, parts[2], parts[3])]
-    alpha = jnp.sqrt(jnp.concatenate(parts, axis=1) / feat_total + epsilon)
-    beta = beta_of((g0, g1, g2, g3), q, docs_total)
-    rho = jnp.sqrt(rhobar[...] * rhobar[...] + beta * beta)
-    cosine = rhobar[...] / rho
-    sine = beta / rho
-    theta = sine * alpha
-    rhobar_out[...] = -cosine * alpha
-    phibar_out[...] = sine * phibar[...]
-    alpha_out[...] = alpha
-    following = (got / beta - beta * right[...]) / alpha
-    right_out[...] = following
-    search_out[...] = following - (theta / rho) * search[...]
-
-
-def finish(docs_total, feat_total, pieces, squares, right, search, phibar, rhobar):
-    rows, cols = right.shape
-    return pl.pallas_call(
-        functools.partial(finish_kernel, docs_total, feat_total),
-        out_shape=[f32(rows, cols)] * 2 + [f32(1, cols)] * 3,
-        scratch_shapes=[pltpu.VMEM((4, cols // 4, rows), jnp.float32)],
-        compiler_params=params(8),
-        cost_estimate=cost(rows * cols * 16, rows * cols * 20),
-        name="finish",
-    )(*pieces, squares, right, search, phibar, rhobar)
-
-
-def left_out_kernel(docs_total, own, other, g0, g1, g2, g3, search, solution, phibar, rhobar, left_out, solution_out, turned):
-    _, z, y = coords()
-    q, half = turned.shape[1:]
-    beta = beta_of((g0, g1, g2, g3), q, docs_total)
+    alpha_sums, beta_sums = (
+        jnp.concatenate([jnp.where(low, p[0], p[1]), jnp.where(low, p[2], p[3])], axis=1) for p in (parts, high)
+    )
+    alpha = jnp.sqrt(alpha_sums / feat_total + epsilon)
+    beta = jnp.sqrt(beta_sums / docs_total + epsilon)
     for part, ref in ((y, own), (1 - y, other)):
         for k in range(4):
             turned[z ^ k] = ref[k]
         left_out[pl.ds(pl.multiple_of(part * half, half), half), :] = turned[...].reshape(-1, half).T / beta
     rho = jnp.sqrt(rhobar[...] * rhobar[...] + beta * beta)
-    phi = rhobar[...] / rho * phibar[...]
+    cosine = rhobar[...] / rho
+    sine = beta / rho
+    theta = sine * alpha
+    phi = cosine * phibar[...]
+    rhobar_out[...] = -cosine * alpha
+    phibar_out[...] = sine * phibar[...]
+    alpha_out[...] = alpha
+    for k, g in enumerate((g0, g1, g2, g3)):
+        turned[z ^ k] = g[...]
+    got = turned[...].reshape(-1, half).T
+    following = (got / beta - beta * right[...]) / alpha
+    right_out[...] = following
+    search_out[...] = following - (theta / rho) * search[...]
     solution_out[...] = solution[...] + (phi / rho) * search[...]
 
 
-def left_out(docs_total, own, other, pieces, search, solution, phibar, rhobar):
-    _, q, half = own.shape
-    return pl.pallas_call(
-        functools.partial(left_out_kernel, docs_total),
-        out_shape=[f32(2 * half, 4 * q), f32(*solution.shape)],
-        scratch_shapes=[pltpu.VMEM((4, q, half), jnp.float32)],
-        compiler_params=params(8),
-        cost_estimate=cost(half * q * 32, half * q * 120),
-        name="left_out",
-    )(own, other, *pieces, search, solution, phibar, rhobar)
+def finish(docs_total, feat_total, pieces, squares, own, other, right, search, solution, phibar, rhobar):
+    rows, cols = right.shape
+    return pl.pallas_call(
+        functools.partial(finish_kernel, docs_total, feat_total),
+        out_shape=[f32(2 * rows, cols)] + [f32(rows, cols)] * 3 + [f32(1, cols)] * 3,
+        scratch_shapes=[pltpu.VMEM((4, cols // 4, rows), jnp.float32)],
+        compiler_params=params(12),
+        cost_estimate=cost(rows * cols * 16, rows * cols * 20),
+        name="finish",
+    )(*pieces, squares, own, other, right, search, solution, phibar, rhobar)
 
 
 def swap(value, mask):
@@ -455,43 +436,40 @@
 
     stored, messages = prepare(col_ids.T, col_vals.T, right_vec, left_vec)
     entries = along_z([stored] * 4)
-    messages = along_z([messages[0]] + [after(m, *entries[1:]) for m in messages[1:]])
-    q = messages[0].shape[0] // 2
+    messages = along_z([messages[0]] + [after(m, entries[1]) for m in messages[1:]])
+    q = right_vec.shape[1] // 4
 
     rows1, token1 = build(entries, 1)
-    rows0, _ = build(entries, 0, token1)
     own = stack(messages, q, "stack_right", token1)
     own_x = swap(own, X_BIT)
     own_peer = swap(own, CORE_BIT)
+    rows0, token0 = build(entries, 0, own)
     total1 = forward_part(rows1, [own, own_peer], (0, 8))
+    x_peer = swap(after(own_x, total1, token0), CORE_BIT)
+    total1 = forward_part(rows1, [own_x], (4,), total1)
+    product1 = product_half(rows1, x_peer, total1, (12,))
     total0 = forward_part(rows0, [own, own_peer], (0, 8))
-    x_peer = swap(after(own_x, total0, total1), CORE_BIT)
-    total1 = forward_part(rows1, [own_x], (4,), total1)
     total0 = forward_part(rows0, [own_x], (4,), total0)
-    product1 = product_half(rows1, x_peer, total1, (12,))
     product0 = product_half(rows0, x_peer, total0, (12,), *messages, alpha_row)
 
     *lefts, both0, beta0 = left_half(product0, swap(product1, Y_BIT))
     partial = backward_part(rows0, both0, 0, 16)
-    lefts = along_z(lefts)
-    both1, beta1 = left_half(product1, swap(product0, Y_BIT), beta0)
-    far = swap(backward_part(rows1, both1, 12, 4, partial, beta1, lefts[1:3]), CORE_BIT)
+    left_own = stack(along_z(lefts), q, "stack_left")
+    both1, beta1 = left_half(product1, swap(product0, Y_BIT), beta0, partial)
+    far = swap(backward_part(rows1, both1, 12, 4, partial, beta1, [left_own]), CORE_BIT)
     near = backward_part(rows1, both1, 4, 4, partial)
     send, beta_core = far_sums(near, far, beta1)
     got = swap(send, X_BIT)
     peer = backward_part(rows1, both1, 8, 4, partial)
-    left_own = stack(lefts, q, "stack_left", peer)
-    left_other = swap(left_own, Y_BIT)
+    left_other = swap(after(left_own, peer), Y_BIT)
     keep = backward_part(rows1, both1, 0, 4, partial)
 
-    sent, sums = right_norm(docs_total, keep, swap(peer, CORE_BIT), got, beta_core, messages, left_own)
+    sent, sums = right_norm(docs_total, keep, swap(peer, CORE_BIT), got, beta_core, own)
     pieces = along_z(sent)
     squares = lax.all_to_all(after(sums, left_other), AXES, 0, 0, tiled=True)
-    left_next, solution_next = left_out(
-        docs_total, left_own, left_other, pieces, search_dir, solution_vec, phibar_row, rhobar_row
-    )
-    right_next, search_next, alpha_next, phibar_next, rhobar_next = finish(
-        docs_total, feat_total, pieces, squares, right_vec, search_dir, phibar_row, rhobar_row
+    left_next, right_next, search_next, solution_next, alpha_next, phibar_next, rhobar_next = finish(
+        docs_total, feat_total, pieces, squares, left_own, left_other,
+        right_vec, search_dir, solution_vec, phibar_row, rhobar_row,
     )
     return (
         left_next,

time: 90.2 us -> 87 us (0.965)
  blocking collectives: 0 us -> 11.7 us
  waiting for transfers between devices: 28.2 us -> 18.1 us
  starting transfers between devices: 30.9 us -> 27.6 us
  Pallas kernels: 29.9 us -> 28.6 us
    all_to_all x0 -> x1, blocking collectives: none -> 11.7 us  [by_columns(): squares = lax.all_to_all(after(sums, left_other), AXES, 0, 0, tiled=True)]
    all_to_all x1 -> x0, waiting for transfers between devices: 5.86 us -> none  [by_columns(): squares = lax.all_to_all(after(sums, left_other), AXES, 0, 0, tiled=True)]
    ppermute x21, waiting for transfers between devices: 22.4 us -> 18.1 us  [swap(): return lax.ppermute(value, AXES, [(i, i ^ mask) for i in range(32)])]
    all_to_all x1 -> x0, starting transfers between devices: 4.05 us -> none  [by_columns(): squares = lax.all_to_all(after(sums, left_other), AXES, 0, 0, tiled=True)]
    pallas_call x1 -> x0, Pallas kernels: 1.09 us -> none  [left_out(): pl.pallas_call(functools.partial(left_out_kernel, docs_total), out_shape=...]
  transfers between devices with their start and end apart: 22 -> 21, of which waited for: 11 -> 7; matrix products, arithmetic and copies ran while one was open for 0% -> 0% of each run, Pallas kernels for 28% -> 27%
where the time goes in v10:
time: 87 us; the launch traced here: 86.9 us
  Pallas kernels  28.6 us (33%)
  starting transfers between devices  27.6 us (32%)
  waiting for transfers between devices  18.1 us (21%)
  blocking collectives  11.7 us (13%)
  between operations  0.93 us (1%)
    ppermute x21, starting transfers between devices, swap(): return lax.ppermute(value, AXES, [(i, i ^ mask) for i in range(32)])  27.6 us
    ppermute x21, waiting for transfers between devices, swap(): return lax.ppermute(value, AXES, [(i, i ^ mask) for i in range(32)])  18.1 us
    all_to_all x1, blocking collectives, by_columns(): squares = lax.all_to_all(after(sums, left_other), AXES, 0, 0, tiled=True)  11.7 us
    pallas_call x2, Pallas kernels, build(): pl.pallas_call(functools.partial(build_kernel, rel), in_specs=[whole()] *...  9.92 us
    pallas_call x4, Pallas kernels, forward_part(): pl.pallas_call(functools.partial(forward_kernel, blocks), in_specs=[whole...  7.12 us
    pallas_call x5, Pallas kernels, backward_part(): pl.pallas_call(functools.partial(backward_kernel, first, blocks, tuple(ex...  5.23 us
    pallas_call x2, Pallas kernels, product_half(): pl.pallas_call(functools.partial(product_kernel, blocks), in_specs=[whole...  2.64 us
  transfers between devices with their start and end apart: 21, of which 7 were waited for; matrix products, arithmetic and copies ran while one was open for 0% of the time, Pallas kernels for 27%

profile of v10, /device:TPU:0, one launch (start us, length us, event | category | flops | bytes accessed | tf_op | source)
XLA Modules:
  0.0 86.9 jit_solution(7045213527943681066)
XLA Ops:
  0.6 1.6 %prepare.1 = (f32[64,256]{1,0:T(8,128)S(1)}, f32[128,256]{1,0:T(8,128)S(1)}, f32[128,256]{1,0:T(8,128)S(1)}, f32[128,256]{1,0:T(8,128)S(1)}, f32[128,256]{1,0:T(8,128)S(1)}) custom-call(s32[16,512]{1,0:T(8,128)} %bitcast.13, bf16[16,512]{1,0:T(8,128)(2,1)} %bitcast.14, f32[256,256]{1,0:T(8,128)} %right.1, f32[512,256]{1,0:T(8,128)} %left_hbm.1), custom_call_target="tpu_custom_call" | custom-call | bytes 16384 | tf_op jit(solution)/shard_map/prepare/pallas_call | solution.py:74
  2.3 3.1 %collective-permute-start = (f32[64,256]{1,0:T(8,128)S(1)}, f32[64,256]{1,0:T(8,128)S(1)}, u32[]{:S(2)}, u32[]{:S(2)}) collective-permute-start(f32[64,256]{1,0:T(8,128)S(1)} %get-tuple-element.45.e0), channel_id=1, source_target_pairs={{0,8},{1,9},{2,10},{3,11},{4,12},{5,13},{6,14},{7,15},{8,0},{9,1},... | collective-permute-start | bytes 196616 | tf_op jit(solution)/shard_map/ppermute | solution.py:419
  5.4 2.6 %collective-permute-start.1 = (f32[64,256]{1,0:T(8,128)S(1)}, f32[64,256]{1,0:T(8,128)S(1)}, u32[]{:S(2)}, u32[]{:S(2)}) collective-permute-start(f32[64,256]{1,0:T(8,128)S(1)} %get-tuple-element.45.e0), channel_id=1, source_target_pairs={{0,16},{1,17},{2,18},{3,19},{4,20},{5,21},{6,22},{7,23},{8,24},{9,... | collective-permute-start | bytes 196616 | tf_op jit(solution)/shard_map/ppermute | solution.py:419
  8.0 1.7 %collective-permute-start.3 = (f32[128,256]{1,0:T(8,128)S(1)}, f32[128,256]{1,0:T(8,128)S(1)}, u32[]{:S(2)}, u32[]{:S(2)}) collective-permute-start(f32[128,256]{1,0:T(8,128)S(1)} %get-tuple-element.50), channel_id=1, source_target_pairs={{0,8},{1,9},{2,10},{3,11},{4,12},{5,13},{6,14},{7,15},{8,0},{9,1},... | collective-permute-start | bytes 393224 | tf_op jit(solution)/shard_map/ppermute | solution.py:419
  9.7 3.2 %collective-permute-start.4 = (f32[128,256]{1,0:T(8,128)S(1)}, f32[128,256]{1,0:T(8,128)S(1)}, u32[]{:S(2)}, u32[]{:S(2)}) collective-permute-start(f32[128,256]{1,0:T(8,128)S(1)} %get-tuple-element.52), channel_id=1, source_target_pairs={{0,16},{1,17},{2,18},{3,19},{4,20},{5,21},{6,22},{7,23},{8,24},{9,... | collective-permute-start | bytes 393224 | tf_op jit(solution)/shard_map/ppermute | solution.py:419
  12.9 2.1 %collective-permute-done.2.e3 = f32[64,256]{1,0:T(8,128)S(1)} collective-permute-done((f32[64,256]{1,0:T(8,128)S(1)}, f32[64,256]{1,0:T(8,128)S(1)}, u32[]{:S(2)}, u32[]{:S(2)}) %collective-permute-start.2) | collective-permute-done | bytes 65568 | tf_op jit(solution)/shard_map/ppermute | solution.py:419
  14.9 4.8 %dense_rows.2 = (bf16[16,1024,256]{2,1,0:T(8,128)(2,1)S(1)}, bf16[16,1024,256]{2,1,0:T(8,128)(2,1)S(1)}, f32[8,128]{1,0:T(8,128)S(1)}) custom-call(f32[64,256]{1,0:T(8,128)S(1)} %get-tuple-element.45.e0, f32[64,256]{1,0:T(8,128)S(1)} %collective-permute-done.e1, f32[64,256]{1,0:T(8,128)S(1)} %collective-permute-done.1.e2, ...), custom_call_target="tpu_custom_call" | custom-call | flops 2147483648 | bytes 16777216 | tf_op jit(solution)/shard_map/dense_rows/pallas_call | solution.py:154
  19.7 3.6 %collective-permute-done.4.m2.refs_2_ = f32[128,256]{1,0:T(8,128)S(1)} collective-permute-done((f32[128,256]{1,0:T(8,128)S(1)}, f32[128,256]{1,0:T(8,128)S(1)}, u32[]{:S(2)}, u32[]{:S(2)}) %collective-permute-start.4) | collective-permute-done | bytes 131104 | tf_op jit(solution)/shard_map/ppermute | solution.py:419
  23.3 0.1 collective-permute-start.7
  23.4 1.6 %collective-permute-start.6 = (f32[4,64,256]{2,1,0:T(8,128)S(1)}, f32[4,64,256]{2,1,0:T(8,128)S(1)}, u32[]{:S(2)}, u32[]{:S(2)}) collective-permute-start(f32[4,64,256]{2,1,0:T(8,128)S(1)} %stack_right.1.refs_0_.right), channel_id=1, source_target_pairs={{0,4},{1,5},{2,6},{3,7},{4,0},{5,1},{6,2},{7,3},{8,12},{9,13},{10,... | collective-permute-start | bytes 786440 | tf_op jit(solution)/shard_map/ppermute | solution.py:419
  24.9 2.3 %forward_part.4.refs_1_ = f32[1024,128]{1,0:T(8,128)S(1)} custom-call(bf16[16,1024,256]{2,1,0:T(8,128)(2,1)S(1)} %get-tuple-element.46.hi_ref, bf16[16,1024,256]{2,1,0:T(8,128)(2,1)S(1)} %get-tuple-element.47.lo_ref, f32[4,64,256]{2,1,0:T(8,128)S(1)} %stack_right.1.refs_0_.right, f32[4,64,256]{2,1,0:T(8,128)S(1)} %collective-permute-done.7.refs_1_), custom_call_target="tpu_custom_call" | custom-call | flops 67108864 | bytes 131072 | tf_op jit(solution)/shard_map/forward_part/pallas_call | solution.py:196
  27.3 4.8 %collective-permute-done.6.refs_0_ = f32[4,64,256]{2,1,0:T(8,128)S(1)} collective-permute-done((f32[4,64,256]{2,1,0:T(8,128)S(1)}, f32[4,64,256]{2,1,0:T(8,128)S(1)}, u32[]{:S(2)}, u32[]{:S(2)}) %collective-permute-start.6) | collective-permute-done | bytes 262176 | tf_op jit(solution)/shard_map/ppermute | solution.py:419
  32.1 1.2 %forward_part.5.before = f32[1024,128]{1,0:T(8,128)S(1)} custom-call(bf16[16,1024,256]{2,1,0:T(8,128)(2,1)S(1)} %get-tuple-element.46.hi_ref, bf16[16,1024,256]{2,1,0:T(8,128)(2,1)S(1)} %get-tuple-element.47.lo_ref, f32[4,64,256]{2,1,0:T(8,128)S(1)} %collective-permute-done.6.refs_0_, f32[1024,128]{1,0:T(8,128)S(1)} %forward_part.4.refs_1_), custom_call_target="tpu_custom_call" | custom-call | flops 33554432 | bytes 65536 | tf_op jit(solution)/shard_map/forward_part/pallas_call | solution.py:196
  33.3 0.3 collective-permute-done.8.vec
  33.6 1.3 %product_half.2.mine = f32[64,1024]{1,0:T(8,128)S(1)} custom-call(bf16[16,1024,256]{2,1,0:T(8,128)(2,1)S(1)} %get-tuple-element.46.hi_ref, bf16[16,1024,256]{2,1,0:T(8,128)(2,1)S(1)} %get-tuple-element.47.lo_ref, f32[4,64,256]{2,1,0:T(8,128)S(1)} %collective-permute-done.8.vec, f32[1024,128]{1,0:T(8,128)S(1)} %forward_part.5.before), custom_call_target="tpu_custom_call" | custom-call | flops 33554432 | bytes 65536 | tf_op jit(solution)/shard_map/product_half/pallas_call | solution.py:228
  34.9 1.6 %collective-permute-start.10 = (f32[64,1024]{1,0:T(8,128)S(1)}, f32[64,1024]{1,0:T(8,128)S(1)}, u32[]{:S(2)}, u32[]{:S(2)}) collective-permute-start(f32[64,1024]{1,0:T(8,128)S(1)} %product_half.2.mine), channel_id=1, source_target_pairs={{0,1},{1,0},{2,3},{3,2},{4,5},{5,4},{6,7},{7,6},{8,9},{9,8},{10,11... | collective-permute-start | bytes 786440 | tf_op jit(solution)/shard_map/ppermute | solution.py:419
  36.5 5.2 %dense_rows.3 = (bf16[16,1024,256]{2,1,0:T(8,128)(2,1)S(1)}, bf16[16,1024,256]{2,1,0:T(8,128)(2,1)S(1)}, f32[8,128]{1,0:T(8,128)}) custom-call(f32[64,256]{1,0:T(8,128)S(1)} %get-tuple-element.45.e0, f32[64,256]{1,0:T(8,128)S(1)} %collective-permute-done.e1, f32[64,256]{1,0:T(8,128)S(1)} %collective-permute-done.1.e2, ...), custom_call_target="tpu_custom_call" | custom-call | flops 33554432 | bytes 262144 | tf_op jit(solution)/shard_map/dense_rows/pallas_call | solution.py:154
  41.7 2.3 %forward_part.6.refs_1_ = f32[1024,128]{1,0:T(8,128)S(1)} custom-call(bf16[16,1024,256]{2,1,0:T(8,128)(2,1)S(1)} %get-tuple-element.57.hi_ref, bf16[16,1024,256]{2,1,0:T(8,128)(2,1)S(1)} %get-tuple-element.58.lo_ref, f32[4,64,256]{2,1,0:T(8,128)S(1)} %stack_right.1.refs_0_.right, f32[4,64,256]{2,1,0:T(8,128)S(1)} %collective-permute-done.7.refs_1_), custom_call_target="tpu_custom_call" | custom-call | flops 67108864 | bytes 131072 | tf_op jit(solution)/shard_map/forward_part/pallas_call | solution.py:196
  44.0 0.0 copy-start.3
  44.0 1.2 %forward_part.7.before = f32[1024,128]{1,0:T(8,128)S(1)} custom-call(bf16[16,1024,256]{2,1,0:T(8,128)(2,1)S(1)} %get-tuple-element.57.hi_ref, bf16[16,1024,256]{2,1,0:T(8,128)(2,1)S(1)} %get-tuple-element.58.lo_ref, f32[4,64,256]{2,1,0:T(8,128)S(1)} %collective-permute-done.6.refs_0_, f32[1024,128]{1,0:T(8,128)S(1)} %forward_part.6.refs_1_), custom_call_target="tpu_custom_call" | custom-call | flops 33554432 | bytes 65536 | tf_op jit(solution)/shard_map/forward_part/pallas_call | solution.py:196
  45.3 1.3 %product_half.3.mine = f32[64,1024]{1,0:T(8,128)S(1)} custom-call(bf16[16,1024,256]{2,1,0:T(8,128)(2,1)S(1)} %get-tuple-element.57.hi_ref, bf16[16,1024,256]{2,1,0:T(8,128)(2,1)S(1)} %get-tuple-element.58.lo_ref, f32[4,64,256]{2,1,0:T(8,128)S(1)} %collective-permute-done.8.vec, f32[1024,128]{1,0:T(8,128)S(1)} %forward_part.7.before, ...), custom_call_target="tpu_custom_call" | custom-call | flops 33554432 | bytes 65536 | tf_op jit(solution)/shard_map/product_half/pallas_call | solution.py:228
  46.6 0.6 collective-permute-start.9
  47.2 0.2 left_half.2
  47.3 2.7 %collective-permute-start.12 = (f32[64,256]{1,0:T(8,128)S(1)}, f32[64,256]{1,0:T(8,128)S(1)}, u32[]{:S(2)}, u32[]{:S(2)}) collective-permute-start(f32[64,256]{1,0:T(8,128)S(1)} %get-tuple-element.64), channel_id=1, source_target_pairs={{0,8},{1,9},{2,10},{3,11},{4,12},{5,13},{6,14},{7,15},{8,0},{9,1},... | collective-permute-start | bytes 196616 | tf_op jit(solution)/shard_map/ppermute | solution.py:419
  50.0 1.4 %collective-permute-start.13 = (f32[64,256]{1,0:T(8,128)S(1)}, f32[64,256]{1,0:T(8,128)S(1)}, u32[]{:S(2)}, u32[]{:S(2)}) collective-permute-start(f32[64,256]{1,0:T(8,128)S(1)} %get-tuple-element.65), channel_id=1, source_target_pairs={{0,16},{1,17},{2,18},{3,19},{4,20},{5,21},{6,22},{7,23},{8,24},{9,... | collective-permute-start | bytes 196616 | tf_op jit(solution)/shard_map/ppermute | solution.py:419
  51.4 1.4 %collective-permute-start.14 = (f32[64,256]{1,0:T(8,128)S(1)}, f32[64,256]{1,0:T(8,128)S(1)}, u32[]{:S(2)}, u32[]{:S(2)}) collective-permute-start(f32[64,256]{1,0:T(8,128)S(1)} %get-tuple-element.66), channel_id=1, source_target_pairs={{0,24},{1,25},{2,26},{3,27},{4,28},{5,29},{6,30},{7,31},{8,16},{9,... | collective-permute-start | bytes 196616 | tf_op jit(solution)/shard_map/ppermute | solution.py:419
  52.8 2.3 %backward_part.5.refs_1_.refs_0_ = f32[1024,256]{1,0:T(8,128)S(1)} custom-call(bf16[16,1024,256]{2,1,0:T(8,128)(2,1)S(1)} %get-tuple-element.57.hi_ref, bf16[16,1024,256]{2,1,0:T(8,128)(2,1)S(1)} %get-tuple-element.58.lo_ref, bf16[128,1024]{1,0:T(8,128)(2,1)S(1)} %get-tuple-element.60.both_ref), custom_call_target="tpu_custom_call" | custom-call | flops 134217728 | bytes 262144 | tf_op jit(solution)/shard_map/backward_part/pallas_call | solution.py:309
  55.2 0.2 left_half.3
  55.3 2.6 %collective-permute-done.13.m2 = f32[64,256]{1,0:T(8,128)S(1)} collective-permute-done((f32[64,256]{1,0:T(8,128)S(1)}, f32[64,256]{1,0:T(8,128)S(1)}, u32[]{:S(2)}, u32[]{:S(2)}) %collective-permute-start.13) | collective-permute-done | bytes 65568 | tf_op jit(solution)/shard_map/ppermute | solution.py:419
  58.0 0.7 backward_part.9
  58.7 0.1 collective-permute-start.15
  58.8 0.7 backward_part.8.near
  59.5 0.8 collective-permute-done.15.far
  60.4 1.5 %collective-permute-start.16 = (f32[264,256]{1,0:T(8,128)S(1)}, f32[264,256]{1,0:T(8,128)S(1)}, u32[]{:S(2)}, u32[]{:S(2)}) collective-permute-start(f32[264,256]{1,0:T(8,128)S(1)} %get-tuple-element.67), channel_id=1, source_target_pairs={{0,4},{1,5},{2,6},{3,7},{4,0},{5,1},{6,2},{7,3},{8,12},{9,13},{10,... | collective-permute-start | bytes 811016 | tf_op jit(solution)/shard_map/ppermute | solution.py:419
  61.9 0.7 backward_part.7
  62.7 0.0 copy-start
  62.7 0.0 copy-start.2
  62.7 0.0 copy-start.4
  62.7 0.1 collective-permute-start.11
  62.8 1.6 %collective-permute-start.20 = (f32[4,64,256]{2,1,0:T(8,128)S(1)}, f32[4,64,256]{2,1,0:T(8,128)S(1)}, u32[]{:S(2)}, u32[]{:S(2)}) collective-permute-start(f32[4,64,256]{2,1,0:T(8,128)S(1)} %stack_left.1.refs_2_.own), channel_id=1, source_target_pairs={{0,1},{1,0},{2,3},{3,2},{4,5},{5,4},{6,7},{7,6},{8,9},{9,8},{10,11... | collective-permute-start | bytes 786440 | tf_op jit(solution)/shard_map/ppermute | solution.py:419
  64.4 0.7 backward_part.6.keep
  65.1 3.8 %collective-permute-done.16.got = f32[264,256]{1,0:T(8,128)S(1)} collective-permute-done((f32[264,256]{1,0:T(8,128)S(1)}, f32[264,256]{1,0:T(8,128)S(1)}, u32[]{:S(2)}, u32[]{:S(2)}) %collective-permute-start.16) | collective-permute-done | bytes 270368 | tf_op jit(solution)/shard_map/ppermute | solution.py:419
  69.0 0.3 right_norm.1
  69.3 1.4 %collective-permute-start.17 = (f32[64,256]{1,0:T(8,128)S(1)}, f32[64,256]{1,0:T(8,128)S(1)}, u32[]{:S(2)}, u32[]{:S(2)}) collective-permute-start(f32[64,256]{1,0:T(8,128)S(1)} %get-tuple-element.70), channel_id=1, source_target_pairs={{0,8},{1,9},{2,10},{3,11},{4,12},{5,13},{6,14},{7,15},{8,0},{9,1},... | collective-permute-start | bytes 196616 | tf_op jit(solution)/shard_map/ppermute | solution.py:419
  70.6 1.7 %collective-permute-start.18 = (f32[64,256]{1,0:T(8,128)S(1)}, f32[64,256]{1,0:T(8,128)S(1)}, u32[]{:S(2)}, u32[]{:S(2)}) collective-permute-start(f32[64,256]{1,0:T(8,128)S(1)} %get-tuple-element.71), channel_id=1, source_target_pairs={{0,16},{1,17},{2,18},{3,19},{4,20},{5,21},{6,22},{7,23},{8,24},{9,... | collective-permute-start | bytes 196616 | tf_op jit(solution)/shard_map/ppermute | solution.py:419
  72.4 1.4 %collective-permute-start.19 = (f32[64,256]{1,0:T(8,128)S(1)}, f32[64,256]{1,0:T(8,128)S(1)}, u32[]{:S(2)}, u32[]{:S(2)}) collective-permute-start(f32[64,256]{1,0:T(8,128)S(1)} %get-tuple-element.72), channel_id=1, source_target_pairs={{0,24},{1,25},{2,26},{3,27},{4,28},{5,29},{6,30},{7,31},{8,16},{9,... | collective-permute-start | bytes 196616 | tf_op jit(solution)/shard_map/ppermute | solution.py:419
  73.7 11.7 %all_to_all.5.squares = f32[32,1,128]{2,1,0:T(1,128)S(1)} all-to-all(f32[32,1,128]{2,1,0:T(1,128)S(1)} %bitcast.9), channel_id=1, replica_groups=mesh['doc'=16,'feat'=2] {'doc','feat'}, dimensions={0} | all-to-all | bytes 32768 | tf_op jit(solution)/shard_map/all_to_all | solution.py:469
  85.5 1.3 %finish.1 = (f32[512,256]{1,0:T(8,128)}, f32[256,256]{1,0:T(8,128)}, f32[256,256]{1,0:T(8,128)}, f32[256,256]{1,0:T(8,128)}, f32[1,256]{1,0:T(1,128)}, /*index=5*/f32[1,256]{1,0:T(1,128)}, f32[1,256]{1,0:T(1,128)}) custom-call(f32[64,256]{1,0:T(8,128)S(1)} %get-tuple-element.69.g0, f32[64,256]{1,0:T(8,128)S(1)} %collective-permute-done.17.g1, ...), custom_call_target="tpu_custom_call" | custom-call | flops 16384 | bytes 20480 | tf_op jit(solution)/shard_map/finish/pallas_call | solution.py:408
  (28 shorter events, 0.1 us)
Async XLA Ops:
  2.3 5.7 %collective-permute-start = (f32[64,256]{1,0:T(8,128)S(1)}, f32[64,256]{1,0:T(8,128)S(1)}, u32[]{:S(2)}, u32[]{:S(2)}) collective-permute-start(f32[64,256]{1,0:T(8,128)S(1)} %get-tuple-element.45.e0), channel_id=1, source_target_pairs={{0,8},{1,9},{2,10},{3,11},{4,12},{5,13},{6,14},{7,15},{8,0},{9,1},... | collective-permute-start | bytes 196616 | tf_op jit(solution)/shard_map/ppermute | solution.py:419
  5.4 7.5 %collective-permute-start.1 = (f32[64,256]{1,0:T(8,128)S(1)}, f32[64,256]{1,0:T(8,128)S(1)}, u32[]{:S(2)}, u32[]{:S(2)}) collective-permute-start(f32[64,256]{1,0:T(8,128)S(1)} %get-tuple-element.45.e0), channel_id=1, source_target_pairs={{0,16},{1,17},{2,18},{3,19},{4,20},{5,21},{6,22},{7,23},{8,24},{9,... | collective-permute-start | bytes 196616 | tf_op jit(solution)/shard_map/ppermute | solution.py:419
  8.0 6.9 %collective-permute-start.2 = (f32[64,256]{1,0:T(8,128)S(1)}, f32[64,256]{1,0:T(8,128)S(1)}, u32[]{:S(2)}, u32[]{:S(2)}) collective-permute-start(f32[64,256]{1,0:T(8,128)S(1)} %get-tuple-element.45.e0), channel_id=1, source_target_pairs={{0,24},{1,25},{2,26},{3,27},{4,28},{5,29},{6,30},{7,31},{8,16},{9,... | collective-permute-start | bytes 196616 | tf_op jit(solution)/shard_map/ppermute | solution.py:419
  8.0 11.7 %collective-permute-start.3 = (f32[128,256]{1,0:T(8,128)S(1)}, f32[128,256]{1,0:T(8,128)S(1)}, u32[]{:S(2)}, u32[]{:S(2)}) collective-permute-start(f32[128,256]{1,0:T(8,128)S(1)} %get-tuple-element.50), channel_id=1, source_target_pairs={{0,8},{1,9},{2,10},{3,11},{4,12},{5,13},{6,14},{7,15},{8,0},{9,1},... | collective-permute-start | bytes 393224 | tf_op jit(solution)/shard_map/ppermute | solution.py:419
  9.7 13.6 %collective-permute-start.4 = (f32[128,256]{1,0:T(8,128)S(1)}, f32[128,256]{1,0:T(8,128)S(1)}, u32[]{:S(2)}, u32[]{:S(2)}) collective-permute-start(f32[128,256]{1,0:T(8,128)S(1)} %get-tuple-element.52), channel_id=1, source_target_pairs={{0,16},{1,17},{2,18},{3,19},{4,20},{5,21},{6,22},{7,23},{8,24},{9,... | collective-permute-start | bytes 393224 | tf_op jit(solution)/shard_map/ppermute | solution.py:419
  12.9 10.4 %collective-permute-start.5 = (f32[128,256]{1,0:T(8,128)S(1)}, f32[128,256]{1,0:T(8,128)S(1)}, u32[]{:S(2)}, u32[]{:S(2)}) collective-permute-start(f32[128,256]{1,0:T(8,128)S(1)} %get-tuple-element.54), channel_id=1, source_target_pairs={{0,24},{1,25},{2,26},{3,27},{4,28},{5,29},{6,30},{7,31},{8,16},{9,... | collective-permute-start | bytes 393224 | tf_op jit(solution)/shard_map/ppermute | solution.py:419
  23.3 1.6 %collective-permute-start.7 = (f32[4,64,256]{2,1,0:T(8,128)S(1)}, f32[4,64,256]{2,1,0:T(8,128)S(1)}, u32[]{:S(2)}, u32[]{:S(2)}) collective-permute-start(f32[4,64,256]{2,1,0:T(8,128)S(1)} %stack_right.1.refs_0_.right), channel_id=1, source_target_pairs={{0,2},{1,3},{2,0},{3,1},{4,6},{5,7},{6,4},{7,5},{8,10},{9,11},{10,... | collective-permute-start | bytes 786440 | tf_op jit(solution)/shard_map/ppermute | solution.py:419
  23.4 8.7 %collective-permute-start.6 = (f32[4,64,256]{2,1,0:T(8,128)S(1)}, f32[4,64,256]{2,1,0:T(8,128)S(1)}, u32[]{:S(2)}, u32[]{:S(2)}) collective-permute-start(f32[4,64,256]{2,1,0:T(8,128)S(1)} %stack_right.1.refs_0_.right), channel_id=1, source_target_pairs={{0,4},{1,5},{2,6},{3,7},{4,0},{5,1},{6,2},{7,3},{8,12},{9,13},{10,... | collective-permute-start | bytes 786440 | tf_op jit(solution)/shard_map/ppermute | solution.py:419
  32.1 1.5 %collective-permute-start.8 = (f32[4,64,256]{2,1,0:T(8,128)S(1)}, f32[4,64,256]{2,1,0:T(8,128)S(1)}, u32[]{:S(2)}, u32[]{:S(2)}) collective-permute-start(f32[4,64,256]{2,1,0:T(8,128)S(1)} %collective-permute-done.6.refs_0_), channel_id=1, source_target_pairs={{0,2},{1,3},{2,0},{3,1},{4,6},{5,7},{6,4},{7,5},{8,10},{9,11},{10,... | collective-permute-start | bytes 786440 | tf_op jit(solution)/shard_map/ppermute | solution.py:419
  34.9 12.2 %collective-permute-start.10 = (f32[64,1024]{1,0:T(8,128)S(1)}, f32[64,1024]{1,0:T(8,128)S(1)}, u32[]{:S(2)}, u32[]{:S(2)}) collective-permute-start(f32[64,1024]{1,0:T(8,128)S(1)} %product_half.2.mine), channel_id=1, source_target_pairs={{0,1},{1,0},{2,3},{3,2},{4,5},{5,4},{6,7},{7,6},{8,9},{9,8},{10,11... | collective-permute-start | bytes 786440 | tf_op jit(solution)/shard_map/ppermute | solution.py:419
  44.0 1.3 %copy-start.3 = (f32[256]{0:T(256)S(1)}, f32[256]{0:T(256)}, u32[]{:S(2)}) copy-start(f32[256]{0:T(256)} %param.15) | copy-start | bytes 3076
  46.6 8.5 %collective-permute-start.9 = (f32[64,1024]{1,0:T(8,128)S(1)}, f32[64,1024]{1,0:T(8,128)S(1)}, u32[]{:S(2)}, u32[]{:S(2)}) collective-permute-start(f32[64,1024]{1,0:T(8,128)S(1)} %product_half.3.mine), channel_id=1, source_target_pairs={{0,1},{1,0},{2,3},{3,2},{4,5},{5,4},{6,7},{7,6},{8,9},{9,8},{10,11... | collective-permute-start | bytes 786440 | tf_op jit(solution)/shard_map/ppermute | solution.py:419
  47.3 8.0 %collective-permute-start.12 = (f32[64,256]{1,0:T(8,128)S(1)}, f32[64,256]{1,0:T(8,128)S(1)}, u32[]{:S(2)}, u32[]{:S(2)}) collective-permute-start(f32[64,256]{1,0:T(8,128)S(1)} %get-tuple-element.64), channel_id=1, source_target_pairs={{0,8},{1,9},{2,10},{3,11},{4,12},{5,13},{6,14},{7,15},{8,0},{9,1},... | collective-permute-start | bytes 196616 | tf_op jit(solution)/shard_map/ppermute | solution.py:419
  50.0 8.0 %collective-permute-start.13 = (f32[64,256]{1,0:T(8,128)S(1)}, f32[64,256]{1,0:T(8,128)S(1)}, u32[]{:S(2)}, u32[]{:S(2)}) collective-permute-start(f32[64,256]{1,0:T(8,128)S(1)} %get-tuple-element.65), channel_id=1, source_target_pairs={{0,16},{1,17},{2,18},{3,19},{4,20},{5,21},{6,22},{7,23},{8,24},{9,... | collective-permute-start | bytes 196616 | tf_op jit(solution)/shard_map/ppermute | solution.py:419
  51.4 6.5 %collective-permute-start.14 = (f32[64,256]{1,0:T(8,128)S(1)}, f32[64,256]{1,0:T(8,128)S(1)}, u32[]{:S(2)}, u32[]{:S(2)}) collective-permute-start(f32[64,256]{1,0:T(8,128)S(1)} %get-tuple-element.66), channel_id=1, source_target_pairs={{0,24},{1,25},{2,26},{3,27},{4,28},{5,29},{6,30},{7,31},{8,16},{9,... | collective-permute-start | bytes 196616 | tf_op jit(solution)/shard_map/ppermute | solution.py:419
  58.7 1.6 %collective-permute-start.15 = (f32[264,256]{1,0:T(8,128)S(1)}, f32[264,256]{1,0:T(8,128)S(1)}, u32[]{:S(2)}, u32[]{:S(2)}) collective-permute-start(f32[264,256]{1,0:T(8,128)S(1)} %backward_part.9), channel_id=1, source_target_pairs={{0,2},{1,3},{2,0},{3,1},{4,6},{5,7},{6,4},{7,5},{8,10},{9,11},{10,... | collective-permute-start | bytes 811016 | tf_op jit(solution)/shard_map/ppermute | solution.py:419
  60.4 8.6 %collective-permute-start.16 = (f32[264,256]{1,0:T(8,128)S(1)}, f32[264,256]{1,0:T(8,128)S(1)}, u32[]{:S(2)}, u32[]{:S(2)}) collective-permute-start(f32[264,256]{1,0:T(8,128)S(1)} %get-tuple-element.67), channel_id=1, source_target_pairs={{0,4},{1,5},{2,6},{3,7},{4,0},{5,1},{6,2},{7,3},{8,12},{9,13},{10,... | collective-permute-start | bytes 811016 | tf_op jit(solution)/shard_map/ppermute | solution.py:419
  62.7 22.8 %copy-start = (f32[256,256]{1,0:T(8,128)S(1)}, f32[256,256]{1,0:T(8,128)}, u32[]{:S(2)}) copy-start(f32[256,256]{1,0:T(8,128)} %right.1) | copy-start | bytes 786436
  62.7 22.8 %copy-start.1 = (f32[256,256]{1,0:T(8,128)S(1)}, f32[256,256]{1,0:T(8,128)}, u32[]{:S(2)}) copy-start(f32[256,256]{1,0:T(8,128)} %search.1) | copy-start | bytes 786436
  62.7 22.8 %copy-start.2 = (f32[256,256]{1,0:T(8,128)S(1)}, f32[256,256]{1,0:T(8,128)}, u32[]{:S(2)}) copy-start(f32[256,256]{1,0:T(8,128)} %solution.1) | copy-start | bytes 786436
  62.7 22.8 %copy-start.4 = (f32[256]{0:T(256)S(1)}, f32[256]{0:T(256)}, u32[]{:S(2)}) copy-start(f32[256]{0:T(256)} %param.16) | copy-start | bytes 3076
  62.7 22.8 %copy-start.5 = (f32[256]{0:T(256)S(1)}, f32[256]{0:T(256)}, u32[]{:S(2)}) copy-start(f32[256]{0:T(256)} %param.17) | copy-start | bytes 3076
  62.7 2.4 %collective-permute-start.11 = (f32[256,256]{1,0:T(8,128)S(1)}, f32[256,256]{1,0:T(8,128)S(1)}, u32[]{:S(2)}, u32[]{:S(2)}) collective-permute-start(f32[256,256]{1,0:T(8,128)S(1)} %backward_part.7), channel_id=1, source_target_pairs={{0,2},{1,3},{2,0},{3,1},{4,6},{5,7},{6,4},{7,5},{8,10},{9,11},{10,... | collective-permute-start | bytes 786440 | tf_op jit(solution)/shard_map/ppermute | solution.py:419
  62.8 11.0 %collective-permute-start.20 = (f32[4,64,256]{2,1,0:T(8,128)S(1)}, f32[4,64,256]{2,1,0:T(8,128)S(1)}, u32[]{:S(2)}, u32[]{:S(2)}) collective-permute-start(f32[4,64,256]{2,1,0:T(8,128)S(1)} %stack_left.1.refs_2_.own), channel_id=1, source_target_pairs={{0,1},{1,0},{2,3},{3,2},{4,5},{5,4},{6,7},{7,6},{8,9},{9,8},{10,11... | collective-permute-start | bytes 786440 | tf_op jit(solution)/shard_map/ppermute | solution.py:419
  69.3 16.2 %collective-permute-start.17 = (f32[64,256]{1,0:T(8,128)S(1)}, f32[64,256]{1,0:T(8,128)S(1)}, u32[]{:S(2)}, u32[]{:S(2)}) collective-permute-start(f32[64,256]{1,0:T(8,128)S(1)} %get-tuple-element.70), channel_id=1, source_target_pairs={{0,8},{1,9},{2,10},{3,11},{4,12},{5,13},{6,14},{7,15},{8,0},{9,1},... | collective-permute-start | bytes 196616 | tf_op jit(solution)/shard_map/ppermute | solution.py:419
  70.6 14.8 %collective-permute-start.18 = (f32[64,256]{1,0:T(8,128)S(1)}, f32[64,256]{1,0:T(8,128)S(1)}, u32[]{:S(2)}, u32[]{:S(2)}) collective-permute-start(f32[64,256]{1,0:T(8,128)S(1)} %get-tuple-element.71), channel_id=1, source_target_pairs={{0,16},{1,17},{2,18},{3,19},{4,20},{5,21},{6,22},{7,23},{8,24},{9,... | collective-permute-start | bytes 196616 | tf_op jit(solution)/shard_map/ppermute | solution.py:419
  72.4 13.1 %collective-permute-start.19 = (f32[64,256]{1,0:T(8,128)S(1)}, f32[64,256]{1,0:T(8,128)S(1)}, u32[]{:S(2)}, u32[]{:S(2)}) collective-permute-start(f32[64,256]{1,0:T(8,128)S(1)} %get-tuple-element.72), channel_id=1, source_target_pairs={{0,24},{1,25},{2,26},{3,27},{4,28},{5,29},{6,30},{7,31},{8,16},{9,... | collective-permute-start | bytes 196616 | tf_op jit(solution)/shard_map/ppermute | solution.py:419

commit v11 on v10

--- a/solution.py
+++ b/solution.py
@@ -182,19 +182,19 @@
             )
 
 
-def forward_kernel(blocks, hi_ref, lo_ref, *refs):
+def forward_kernel(blocks, has_before, hi_ref, lo_ref, *refs):
     count = len(blocks)
     total = refs[-1]
-    total[...] = refs[count][...] if len(refs) > count + 1 else jnp.zeros_like(total)
+    total[...] = refs[count][...] if has_before else jnp.zeros_like(total)
     add_products(hi_ref, lo_ref, refs[:count], blocks, total)
 
 
-def forward_part(rows, vecs, blocks, before=None):
+def forward_part(rows, vecs, blocks, before=None, tokens=()):
     docs, q = rows[0].shape[1], vecs[0].shape[1]
     n = 4 * len(blocks)
-    extra = [] if before is None else [before]
-    return pl.pallas_call(
-        functools.partial(forward_kernel, blocks),
+    extra = [*tokens] if before is None else [before, *tokens]
+    return pl.pallas_call(
+        functools.partial(forward_kernel, blocks, before is not None),
         in_specs=[whole()] * (2 + len(vecs) + len(extra)),
         out_specs=whole(),
         out_shape=f32(docs, 2 * q),
@@ -444,8 +444,8 @@
     own_x = swap(own, X_BIT)
     own_peer = swap(own, CORE_BIT)
     rows0, token0 = build(entries, 0, own)
-    total1 = forward_part(rows1, [own, own_peer], (0, 8))
-    x_peer = swap(after(own_x, total1, token0), CORE_BIT)
+    total1 = forward_part(rows1, [own, own_peer], (0, 8), None, [token0])
+    x_peer = swap(after(own_x, total1), CORE_BIT)
     total1 = forward_part(rows1, [own_x], (4,), total1)
     product1 = product_half(rows1, x_peer, total1, (12,))
     total0 = forward_part(rows0, [own, own_peer], (0, 8))

time: 87 us -> 83 us (0.954)
  waiting for transfers between devices: 18.1 us -> 14.8 us
  blocking collectives: 11.7 us -> 10.7 us
    ppermute x21, waiting for transfers between devices: 18.1 us -> 14.8 us  [swap(): return lax.ppermute(value, AXES, [(i, i ^ mask) for i in range(32)])]
    all_to_all x1, blocking collectives: 11.7 us -> 10.7 us  [by_columns(): squares = lax.all_to_all(after(sums, left_other), AXES, 0, 0, tiled=True)]
  transfers between devices with their start and end apart: 21 -> 21, of which waited for: 7 -> 8; matrix products, arithmetic and copies ran while one was open for 0% -> 0% of each run, Pallas kernels for 27% -> 28%
where the time goes in v11:
time: 83 us; the launch traced here: 82.9 us
  Pallas kernels  28.3 us (34%)
  starting transfers between devices  28.1 us (34%)
  waiting for transfers between devices  14.8 us (18%)
  blocking collectives  10.7 us (13%)
  between operations  0.96 us (1%)
    ppermute x21, starting transfers between devices, swap(): return lax.ppermute(value, AXES, [(i, i ^ mask) for i in range(32)])  28.1 us
    ppermute x21, waiting for transfers between devices, swap(): return lax.ppermute(value, AXES, [(i, i ^ mask) for i in range(32)])  14.8 us
    all_to_all x1, blocking collectives, by_columns(): squares = lax.all_to_all(after(sums, left_other), AXES, 0, 0, tiled=True)  10.7 us
    pallas_call x2, Pallas kernels, build(): pl.pallas_call(functools.partial(build_kernel, rel), in_specs=[whole()] *...  9.64 us
    pallas_call x4, Pallas kernels, forward_part(): pl.pallas_call(functools.partial(forward_kernel, blocks, before is not No...  7.11 us
    pallas_call x5, Pallas kernels, backward_part(): pl.pallas_call(functools.partial(backward_kernel, first, blocks, tuple(ex...  5.23 us
    pallas_call x2, Pallas kernels, product_half(): pl.pallas_call(functools.partial(product_kernel, blocks), in_specs=[whole...  2.64 us
  transfers between devices with their start and end apart: 21, of which 8 were waited for; matrix products, arithmetic and copies ran while one was open for 0% of the time, Pallas kernels for 28%

profile of v11, /device:TPU:0, one launch (start us, length us, event | category | flops | bytes accessed | tf_op | source)
XLA Modules:
  0.0 82.9 jit_solution(17621543711786897609)
XLA Ops:
  0.6 1.6 %prepare.1 = (f32[64,256]{1,0:T(8,128)S(1)}, f32[128,256]{1,0:T(8,128)S(1)}, f32[128,256]{1,0:T(8,128)S(1)}, f32[128,256]{1,0:T(8,128)S(1)}, f32[128,256]{1,0:T(8,128)S(1)}) custom-call(s32[16,512]{1,0:T(8,128)} %bitcast.13, bf16[16,512]{1,0:T(8,128)(2,1)} %bitcast.14, f32[256,256]{1,0:T(8,128)} %right.1, f32[512,256]{1,0:T(8,128)} %left_hbm.1), custom_call_target="tpu_custom_call" | custom-call | bytes 16384 | tf_op jit(solution)/shard_map/prepare/pallas_call | solution.py:74
  2.3 3.1 %collective-permute-start = (f32[64,256]{1,0:T(8,128)S(1)}, f32[64,256]{1,0:T(8,128)S(1)}, u32[]{:S(2)}, u32[]{:S(2)}) collective-permute-start(f32[64,256]{1,0:T(8,128)S(1)} %get-tuple-element.46.e0), channel_id=1, source_target_pairs={{0,8},{1,9},{2,10},{3,11},{4,12},{5,13},{6,14},{7,15},{8,0},{9,1},... | collective-permute-start | bytes 196616 | tf_op jit(solution)/shard_map/ppermute | solution.py:419
  5.4 2.4 %collective-permute-start.2 = (f32[64,256]{1,0:T(8,128)S(1)}, f32[64,256]{1,0:T(8,128)S(1)}, u32[]{:S(2)}, u32[]{:S(2)}) collective-permute-start(f32[64,256]{1,0:T(8,128)S(1)} %get-tuple-element.46.e0), channel_id=1, source_target_pairs={{0,24},{1,25},{2,26},{3,27},{4,28},{5,29},{6,30},{7,31},{8,16},{9,... | collective-permute-start | bytes 196616 | tf_op jit(solution)/shard_map/ppermute | solution.py:419
  7.8 0.1 collective-permute-start.1
  8.0 1.8 %collective-permute-start.3 = (f32[128,256]{1,0:T(8,128)S(1)}, f32[128,256]{1,0:T(8,128)S(1)}, u32[]{:S(2)}, u32[]{:S(2)}) collective-permute-start(f32[128,256]{1,0:T(8,128)S(1)} %get-tuple-element.51), channel_id=1, source_target_pairs={{0,8},{1,9},{2,10},{3,11},{4,12},{5,13},{6,14},{7,15},{8,0},{9,1},... | collective-permute-start | bytes 393224 | tf_op jit(solution)/shard_map/ppermute | solution.py:419
  9.8 2.5 %collective-permute-start.4 = (f32[128,256]{1,0:T(8,128)S(1)}, f32[128,256]{1,0:T(8,128)S(1)}, u32[]{:S(2)}, u32[]{:S(2)}) collective-permute-start(f32[128,256]{1,0:T(8,128)S(1)} %get-tuple-element.53), channel_id=1, source_target_pairs={{0,16},{1,17},{2,18},{3,19},{4,20},{5,21},{6,22},{7,23},{8,24},{9,... | collective-permute-start | bytes 393224 | tf_op jit(solution)/shard_map/ppermute | solution.py:419
  12.2 0.5 collective-permute-start.5
  12.8 1.9 %collective-permute-done.1.e2 = f32[64,256]{1,0:T(8,128)S(1)} collective-permute-done((f32[64,256]{1,0:T(8,128)S(1)}, f32[64,256]{1,0:T(8,128)S(1)}, u32[]{:S(2)}, u32[]{:S(2)}) %collective-permute-start.1) | collective-permute-done | bytes 65568 | tf_op jit(solution)/shard_map/ppermute | solution.py:419
  14.7 4.7 %dense_rows.2 = (bf16[16,1024,256]{2,1,0:T(8,128)(2,1)S(1)}, bf16[16,1024,256]{2,1,0:T(8,128)(2,1)S(1)}, f32[8,128]{1,0:T(8,128)S(1)}) custom-call(f32[64,256]{1,0:T(8,128)S(1)} %get-tuple-element.46.e0, f32[64,256]{1,0:T(8,128)S(1)} %collective-permute-done.e1, f32[64,256]{1,0:T(8,128)S(1)} %collective-permute-done.1.e2, ...), custom_call_target="tpu_custom_call" | custom-call | flops 2147483648 | bytes 16777216 | tf_op jit(solution)/shard_map/dense_rows/pallas_call | solution.py:154
  19.5 3.4 %collective-permute-done.4.m2.refs_2_ = f32[128,256]{1,0:T(8,128)S(1)} collective-permute-done((f32[128,256]{1,0:T(8,128)S(1)}, f32[128,256]{1,0:T(8,128)S(1)}, u32[]{:S(2)}, u32[]{:S(2)}) %collective-permute-start.4) | collective-permute-done | bytes 131104 | tf_op jit(solution)/shard_map/ppermute | solution.py:419
  22.9 0.1 collective-permute-start.7
  23.0 1.6 %collective-permute-start.6 = (f32[4,64,256]{2,1,0:T(8,128)S(1)}, f32[4,64,256]{2,1,0:T(8,128)S(1)}, u32[]{:S(2)}, u32[]{:S(2)}) collective-permute-start(f32[4,64,256]{2,1,0:T(8,128)S(1)} %stack_right.1.refs_0_.right), channel_id=1, source_target_pairs={{0,4},{1,5},{2,6},{3,7},{4,0},{5,1},{6,2},{7,3},{8,12},{9,13},{10,... | collective-permute-start | bytes 786440 | tf_op jit(solution)/shard_map/ppermute | solution.py:419
  24.5 4.9 %dense_rows.3 = (bf16[16,1024,256]{2,1,0:T(8,128)(2,1)S(1)}, bf16[16,1024,256]{2,1,0:T(8,128)(2,1)S(1)}, f32[8,128]{1,0:T(8,128)S(1)}) custom-call(f32[64,256]{1,0:T(8,128)S(1)} %get-tuple-element.46.e0, f32[64,256]{1,0:T(8,128)S(1)} %collective-permute-done.e1, f32[64,256]{1,0:T(8,128)S(1)} %collective-permute-done.1.e2, ...), custom_call_target="tpu_custom_call" | custom-call | flops 33554432 | bytes 262144 | tf_op jit(solution)/shard_map/dense_rows/pallas_call | solution.py:154
  29.5 2.3 %forward_part.4.refs_1_ = f32[1024,128]{1,0:T(8,128)S(1)} custom-call(bf16[16,1024,256]{2,1,0:T(8,128)(2,1)S(1)} %get-tuple-element.47.hi_ref, bf16[16,1024,256]{2,1,0:T(8,128)(2,1)S(1)} %get-tuple-element.48.lo_ref, f32[4,64,256]{2,1,0:T(8,128)S(1)} %stack_right.1.refs_0_.right, f32[4,64,256]{2,1,0:T(8,128)S(1)} %collective-permute-done.7.refs_1_, ...), custom_call_target="tpu_custom_call" | custom-call | flops 67108864 | bytes 131072 | tf_op jit(solution)/shard_map/forward_part/pallas_call | solution.py:196
  31.8 0.3 collective-permute-start.8
  32.1 1.2 %forward_part.5.before = f32[1024,128]{1,0:T(8,128)S(1)} custom-call(bf16[16,1024,256]{2,1,0:T(8,128)(2,1)S(1)} %get-tuple-element.47.hi_ref, bf16[16,1024,256]{2,1,0:T(8,128)(2,1)S(1)} %get-tuple-element.48.lo_ref, f32[4,64,256]{2,1,0:T(8,128)S(1)} %collective-permute-done.6.refs_0_, f32[1024,128]{1,0:T(8,128)S(1)} %forward_part.4.refs_1_), custom_call_target="tpu_custom_call" | custom-call | flops 33554432 | bytes 65536 | tf_op jit(solution)/shard_map/forward_part/pallas_call | solution.py:196
  33.3 0.1 collective-permute-done.8.vec
  33.4 1.3 %product_half.2.mine = f32[64,1024]{1,0:T(8,128)S(1)} custom-call(bf16[16,1024,256]{2,1,0:T(8,128)(2,1)S(1)} %get-tuple-element.47.hi_ref, bf16[16,1024,256]{2,1,0:T(8,128)(2,1)S(1)} %get-tuple-element.48.lo_ref, f32[4,64,256]{2,1,0:T(8,128)S(1)} %collective-permute-done.8.vec, f32[1024,128]{1,0:T(8,128)S(1)} %forward_part.5.before), custom_call_target="tpu_custom_call" | custom-call | flops 33554432 | bytes 65536 | tf_op jit(solution)/shard_map/product_half/pallas_call | solution.py:228
  34.7 1.6 %collective-permute-start.10 = (f32[64,1024]{1,0:T(8,128)S(1)}, f32[64,1024]{1,0:T(8,128)S(1)}, u32[]{:S(2)}, u32[]{:S(2)}) collective-permute-start(f32[64,1024]{1,0:T(8,128)S(1)} %product_half.2.mine), channel_id=1, source_target_pairs={{0,1},{1,0},{2,3},{3,2},{4,5},{5,4},{6,7},{7,6},{8,9},{9,8},{10,11... | collective-permute-start | bytes 786440 | tf_op jit(solution)/shard_map/ppermute | solution.py:419
  36.3 2.3 %forward_part.6.refs_1_ = f32[1024,128]{1,0:T(8,128)S(1)} custom-call(bf16[16,1024,256]{2,1,0:T(8,128)(2,1)S(1)} %get-tuple-element.59.hi_ref, bf16[16,1024,256]{2,1,0:T(8,128)(2,1)S(1)} %get-tuple-element.60.lo_ref, f32[4,64,256]{2,1,0:T(8,128)S(1)} %stack_right.1.refs_0_.right, f32[4,64,256]{2,1,0:T(8,128)S(1)} %collective-permute-done.7.refs_1_), custom_call_target="tpu_custom_call" | custom-call | flops 67108864 | bytes 131072 | tf_op jit(solution)/shard_map/forward_part/pallas_call | solution.py:196
  38.7 1.2 %forward_part.7.before = f32[1024,128]{1,0:T(8,128)S(1)} custom-call(bf16[16,1024,256]{2,1,0:T(8,128)(2,1)S(1)} %get-tuple-element.59.hi_ref, bf16[16,1024,256]{2,1,0:T(8,128)(2,1)S(1)} %get-tuple-element.60.lo_ref, f32[4,64,256]{2,1,0:T(8,128)S(1)} %collective-permute-done.6.refs_0_, f32[1024,128]{1,0:T(8,128)S(1)} %forward_part.6.refs_1_), custom_call_target="tpu_custom_call" | custom-call | flops 33554432 | bytes 65536 | tf_op jit(solution)/shard_map/forward_part/pallas_call | solution.py:196
  39.9 1.3 %product_half.3.mine = f32[64,1024]{1,0:T(8,128)S(1)} custom-call(bf16[16,1024,256]{2,1,0:T(8,128)(2,1)S(1)} %get-tuple-element.59.hi_ref, bf16[16,1024,256]{2,1,0:T(8,128)(2,1)S(1)} %get-tuple-element.60.lo_ref, f32[4,64,256]{2,1,0:T(8,128)S(1)} %collective-permute-done.8.vec, f32[1024,128]{1,0:T(8,128)S(1)} %forward_part.7.before, ...), custom_call_target="tpu_custom_call" | custom-call | flops 33554432 | bytes 65536 | tf_op jit(solution)/shard_map/product_half/pallas_call | solution.py:228
  41.3 0.5 collective-permute-start.9
  41.8 1.4 %collective-permute-done.10.other = f32[64,1024]{1,0:T(8,128)S(1)} collective-permute-done((f32[64,1024]{1,0:T(8,128)S(1)}, f32[64,1024]{1,0:T(8,128)S(1)}, u32[]{:S(2)}, u32[]{:S(2)}) %collective-permute-start.10) | collective-permute-done | bytes 262176 | tf_op jit(solution)/shard_map/ppermute | solution.py:419
  43.2 0.2 left_half.2
  43.4 3.3 %collective-permute-start.12 = (f32[64,256]{1,0:T(8,128)S(1)}, f32[64,256]{1,0:T(8,128)S(1)}, u32[]{:S(2)}, u32[]{:S(2)}) collective-permute-start(f32[64,256]{1,0:T(8,128)S(1)} %get-tuple-element.66), channel_id=1, source_target_pairs={{0,8},{1,9},{2,10},{3,11},{4,12},{5,13},{6,14},{7,15},{8,0},{9,1},... | collective-permute-start | bytes 196616 | tf_op jit(solution)/shard_map/ppermute | solution.py:419
  46.7 2.3 %collective-permute-start.13 = (f32[64,256]{1,0:T(8,128)S(1)}, f32[64,256]{1,0:T(8,128)S(1)}, u32[]{:S(2)}, u32[]{:S(2)}) collective-permute-start(f32[64,256]{1,0:T(8,128)S(1)} %get-tuple-element.67), channel_id=1, source_target_pairs={{0,16},{1,17},{2,18},{3,19},{4,20},{5,21},{6,22},{7,23},{8,24},{9,... | collective-permute-start | bytes 196616 | tf_op jit(solution)/shard_map/ppermute | solution.py:419
  49.0 0.2 collective-permute-start.14
  49.1 2.3 %backward_part.5.refs_1_.refs_0_ = f32[1024,256]{1,0:T(8,128)S(1)} custom-call(bf16[16,1024,256]{2,1,0:T(8,128)(2,1)S(1)} %get-tuple-element.59.hi_ref, bf16[16,1024,256]{2,1,0:T(8,128)(2,1)S(1)} %get-tuple-element.60.lo_ref, bf16[128,1024]{1,0:T(8,128)(2,1)S(1)} %get-tuple-element.62.both_ref), custom_call_target="tpu_custom_call" | custom-call | flops 134217728 | bytes 262144 | tf_op jit(solution)/shard_map/backward_part/pallas_call | solution.py:309
  51.5 0.2 left_half.3
  51.7 1.9 %collective-permute-done.13.m2 = f32[64,256]{1,0:T(8,128)S(1)} collective-permute-done((f32[64,256]{1,0:T(8,128)S(1)}, f32[64,256]{1,0:T(8,128)S(1)}, u32[]{:S(2)}, u32[]{:S(2)}) %collective-permute-start.13) | collective-permute-done | bytes 65568 | tf_op jit(solution)/shard_map/ppermute | solution.py:419
  53.5 1.5 %collective-permute-done.14.m3 = f32[64,256]{1,0:T(8,128)S(1)} collective-permute-done((f32[64,256]{1,0:T(8,128)S(1)}, f32[64,256]{1,0:T(8,128)S(1)}, u32[]{:S(2)}, u32[]{:S(2)}) %collective-permute-start.14) | collective-permute-done | bytes 65568 | tf_op jit(solution)/shard_map/ppermute | solution.py:419
  55.1 0.7 backward_part.9
  55.8 0.1 collective-permute-start.15
  55.9 0.7 backward_part.8.near
  56.6 0.8 collective-permute-done.15.far
  57.5 1.4 %collective-permute-start.16 = (f32[264,256]{1,0:T(8,128)S(1)}, f32[264,256]{1,0:T(8,128)S(1)}, u32[]{:S(2)}, u32[]{:S(2)}) collective-permute-start(f32[264,256]{1,0:T(8,128)S(1)} %get-tuple-element.69), channel_id=1, source_target_pairs={{0,4},{1,5},{2,6},{3,7},{4,0},{5,1},{6,2},{7,3},{8,12},{9,13},{10,... | collective-permute-start | bytes 811016 | tf_op jit(solution)/shard_map/ppermute | solution.py:419
  58.9 0.7 backward_part.7
  59.6 0.1 collective-permute-start.11
  59.7 1.9 %collective-permute-start.20 = (f32[4,64,256]{2,1,0:T(8,128)S(1)}, f32[4,64,256]{2,1,0:T(8,128)S(1)}, u32[]{:S(2)}, u32[]{:S(2)}) collective-permute-start(f32[4,64,256]{2,1,0:T(8,128)S(1)} %stack_left.1.refs_2_.own), channel_id=1, source_target_pairs={{0,1},{1,0},{2,3},{3,2},{4,5},{5,4},{6,7},{7,6},{8,9},{9,8},{10,11... | collective-permute-start | bytes 786440 | tf_op jit(solution)/shard_map/ppermute | solution.py:419
  61.6 0.7 backward_part.6.keep
  62.3 3.7 %collective-permute-done.16.got = f32[264,256]{1,0:T(8,128)S(1)} collective-permute-done((f32[264,256]{1,0:T(8,128)S(1)}, f32[264,256]{1,0:T(8,128)S(1)}, u32[]{:S(2)}, u32[]{:S(2)}) %collective-permute-start.16) | collective-permute-done | bytes 270368 | tf_op jit(solution)/shard_map/ppermute | solution.py:419
  66.0 0.3 right_norm.1
  66.4 0.1 collective-permute-start.17
  66.4 2.1 %collective-permute-start.18 = (f32[64,256]{1,0:T(8,128)S(1)}, f32[64,256]{1,0:T(8,128)S(1)}, u32[]{:S(2)}, u32[]{:S(2)}) collective-permute-start(f32[64,256]{1,0:T(8,128)S(1)} %get-tuple-element.73), channel_id=1, source_target_pairs={{0,16},{1,17},{2,18},{3,19},{4,20},{5,21},{6,22},{7,23},{8,24},{9,... | collective-permute-start | bytes 196616 | tf_op jit(solution)/shard_map/ppermute | solution.py:419
  68.6 2.2 %collective-permute-start.19 = (f32[64,256]{1,0:T(8,128)S(1)}, f32[64,256]{1,0:T(8,128)S(1)}, u32[]{:S(2)}, u32[]{:S(2)}) collective-permute-start(f32[64,256]{1,0:T(8,128)S(1)} %get-tuple-element.74), channel_id=1, source_target_pairs={{0,24},{1,25},{2,26},{3,27},{4,28},{5,29},{6,30},{7,31},{8,16},{9,... | collective-permute-start | bytes 196616 | tf_op jit(solution)/shard_map/ppermute | solution.py:419
  70.8 10.7 %all_to_all.5.squares = f32[32,1,128]{2,1,0:T(1,128)S(1)} all-to-all(f32[32,1,128]{2,1,0:T(1,128)S(1)} %bitcast.9), channel_id=1, replica_groups=mesh['doc'=16,'feat'=2] {'doc','feat'}, dimensions={0} | all-to-all | bytes 32768 | tf_op jit(solution)/shard_map/all_to_all | solution.py:469
  81.5 1.3 %finish.1 = (f32[512,256]{1,0:T(8,128)}, f32[256,256]{1,0:T(8,128)}, f32[256,256]{1,0:T(8,128)}, f32[256,256]{1,0:T(8,128)}, f32[1,256]{1,0:T(1,128)}, /*index=5*/f32[1,256]{1,0:T(1,128)}, f32[1,256]{1,0:T(1,128)}) custom-call(f32[64,256]{1,0:T(8,128)S(1)} %get-tuple-element.71.g0, f32[64,256]{1,0:T(8,128)S(1)} %collective-permute-done.17.g1, ...), custom_call_target="tpu_custom_call" | custom-call | flops 16384 | bytes 20480 | tf_op jit(solution)/shard_map/finish/pallas_call | solution.py:408
  (28 shorter events, 0.1 us)
Async XLA Ops:
  2.3 5.7 %collective-permute-start = (f32[64,256]{1,0:T(8,128)S(1)}, f32[64,256]{1,0:T(8,128)S(1)}, u32[]{:S(2)}, u32[]{:S(2)}) collective-permute-start(f32[64,256]{1,0:T(8,128)S(1)} %get-tuple-element.46.e0), channel_id=1, source_target_pairs={{0,8},{1,9},{2,10},{3,11},{4,12},{5,13},{6,14},{7,15},{8,0},{9,1},... | collective-permute-start | bytes 196616 | tf_op jit(solution)/shard_map/ppermute | solution.py:419
  5.4 7.4 %collective-permute-start.2 = (f32[64,256]{1,0:T(8,128)S(1)}, f32[64,256]{1,0:T(8,128)S(1)}, u32[]{:S(2)}, u32[]{:S(2)}) collective-permute-start(f32[64,256]{1,0:T(8,128)S(1)} %get-tuple-element.46.e0), channel_id=1, source_target_pairs={{0,24},{1,25},{2,26},{3,27},{4,28},{5,29},{6,30},{7,31},{8,16},{9,... | collective-permute-start | bytes 196616 | tf_op jit(solution)/shard_map/ppermute | solution.py:419
  7.8 6.9 %collective-permute-start.1 = (f32[64,256]{1,0:T(8,128)S(1)}, f32[64,256]{1,0:T(8,128)S(1)}, u32[]{:S(2)}, u32[]{:S(2)}) collective-permute-start(f32[64,256]{1,0:T(8,128)S(1)} %get-tuple-element.46.e0), channel_id=1, source_target_pairs={{0,16},{1,17},{2,18},{3,19},{4,20},{5,21},{6,22},{7,23},{8,24},{9,... | collective-permute-start | bytes 196616 | tf_op jit(solution)/shard_map/ppermute | solution.py:419
  8.0 11.5 %collective-permute-start.3 = (f32[128,256]{1,0:T(8,128)S(1)}, f32[128,256]{1,0:T(8,128)S(1)}, u32[]{:S(2)}, u32[]{:S(2)}) collective-permute-start(f32[128,256]{1,0:T(8,128)S(1)} %get-tuple-element.51), channel_id=1, source_target_pairs={{0,8},{1,9},{2,10},{3,11},{4,12},{5,13},{6,14},{7,15},{8,0},{9,1},... | collective-permute-start | bytes 393224 | tf_op jit(solution)/shard_map/ppermute | solution.py:419
  9.8 13.1 %collective-permute-start.4 = (f32[128,256]{1,0:T(8,128)S(1)}, f32[128,256]{1,0:T(8,128)S(1)}, u32[]{:S(2)}, u32[]{:S(2)}) collective-permute-start(f32[128,256]{1,0:T(8,128)S(1)} %get-tuple-element.53), channel_id=1, source_target_pairs={{0,16},{1,17},{2,18},{3,19},{4,20},{5,21},{6,22},{7,23},{8,24},{9,... | collective-permute-start | bytes 393224 | tf_op jit(solution)/shard_map/ppermute | solution.py:419
  12.2 10.7 %collective-permute-start.5 = (f32[128,256]{1,0:T(8,128)S(1)}, f32[128,256]{1,0:T(8,128)S(1)}, u32[]{:S(2)}, u32[]{:S(2)}) collective-permute-start(f32[128,256]{1,0:T(8,128)S(1)} %get-tuple-element.55), channel_id=1, source_target_pairs={{0,24},{1,25},{2,26},{3,27},{4,28},{5,29},{6,30},{7,31},{8,16},{9,... | collective-permute-start | bytes 393224 | tf_op jit(solution)/shard_map/ppermute | solution.py:419
  22.9 6.6 %collective-permute-start.7 = (f32[4,64,256]{2,1,0:T(8,128)S(1)}, f32[4,64,256]{2,1,0:T(8,128)S(1)}, u32[]{:S(2)}, u32[]{:S(2)}) collective-permute-start(f32[4,64,256]{2,1,0:T(8,128)S(1)} %stack_right.1.refs_0_.right), channel_id=1, source_target_pairs={{0,2},{1,3},{2,0},{3,1},{4,6},{5,7},{6,4},{7,5},{8,10},{9,11},{10,... | collective-permute-start | bytes 786440 | tf_op jit(solution)/shard_map/ppermute | solution.py:419
  23.0 8.8 %collective-permute-start.6 = (f32[4,64,256]{2,1,0:T(8,128)S(1)}, f32[4,64,256]{2,1,0:T(8,128)S(1)}, u32[]{:S(2)}, u32[]{:S(2)}) collective-permute-start(f32[4,64,256]{2,1,0:T(8,128)S(1)} %stack_right.1.refs_0_.right), channel_id=1, source_target_pairs={{0,4},{1,5},{2,6},{3,7},{4,0},{5,1},{6,2},{7,3},{8,12},{9,13},{10,... | collective-permute-start | bytes 786440 | tf_op jit(solution)/shard_map/ppermute | solution.py:419
  31.8 1.6 %collective-permute-start.8 = (f32[4,64,256]{2,1,0:T(8,128)S(1)}, f32[4,64,256]{2,1,0:T(8,128)S(1)}, u32[]{:S(2)}, u32[]{:S(2)}) collective-permute-start(f32[4,64,256]{2,1,0:T(8,128)S(1)} %collective-permute-done.6.refs_0_), channel_id=1, source_target_pairs={{0,2},{1,3},{2,0},{3,1},{4,6},{5,7},{6,4},{7,5},{8,10},{9,11},{10,... | collective-permute-start | bytes 786440 | tf_op jit(solution)/shard_map/ppermute | solution.py:419
  34.7 8.5 %collective-permute-start.10 = (f32[64,1024]{1,0:T(8,128)S(1)}, f32[64,1024]{1,0:T(8,128)S(1)}, u32[]{:S(2)}, u32[]{:S(2)}) collective-permute-start(f32[64,1024]{1,0:T(8,128)S(1)} %product_half.2.mine), channel_id=1, source_target_pairs={{0,1},{1,0},{2,3},{3,2},{4,5},{5,4},{6,7},{7,6},{8,9},{9,8},{10,11... | collective-permute-start | bytes 786440 | tf_op jit(solution)/shard_map/ppermute | solution.py:419
  38.7 1.3 %copy-start.3 = (f32[256]{0:T(256)S(1)}, f32[256]{0:T(256)}, u32[]{:S(2)}) copy-start(f32[256]{0:T(256)} %param.15) | copy-start | bytes 3076
  41.3 10.2 %collective-permute-start.9 = (f32[64,1024]{1,0:T(8,128)S(1)}, f32[64,1024]{1,0:T(8,128)S(1)}, u32[]{:S(2)}, u32[]{:S(2)}) collective-permute-start(f32[64,1024]{1,0:T(8,128)S(1)} %product_half.3.mine), channel_id=1, source_target_pairs={{0,1},{1,0},{2,3},{3,2},{4,5},{5,4},{6,7},{7,6},{8,9},{9,8},{10,11... | collective-permute-start | bytes 786440 | tf_op jit(solution)/shard_map/ppermute | solution.py:419
  43.4 8.3 %collective-permute-start.12 = (f32[64,256]{1,0:T(8,128)S(1)}, f32[64,256]{1,0:T(8,128)S(1)}, u32[]{:S(2)}, u32[]{:S(2)}) collective-permute-start(f32[64,256]{1,0:T(8,128)S(1)} %get-tuple-element.66), channel_id=1, source_target_pairs={{0,8},{1,9},{2,10},{3,11},{4,12},{5,13},{6,14},{7,15},{8,0},{9,1},... | collective-permute-start | bytes 196616 | tf_op jit(solution)/shard_map/ppermute | solution.py:419
  46.7 6.8 %collective-permute-start.13 = (f32[64,256]{1,0:T(8,128)S(1)}, f32[64,256]{1,0:T(8,128)S(1)}, u32[]{:S(2)}, u32[]{:S(2)}) collective-permute-start(f32[64,256]{1,0:T(8,128)S(1)} %get-tuple-element.67), channel_id=1, source_target_pairs={{0,16},{1,17},{2,18},{3,19},{4,20},{5,21},{6,22},{7,23},{8,24},{9,... | collective-permute-start | bytes 196616 | tf_op jit(solution)/shard_map/ppermute | solution.py:419
  49.0 6.1 %collective-permute-start.14 = (f32[64,256]{1,0:T(8,128)S(1)}, f32[64,256]{1,0:T(8,128)S(1)}, u32[]{:S(2)}, u32[]{:S(2)}) collective-permute-start(f32[64,256]{1,0:T(8,128)S(1)} %get-tuple-element.68), channel_id=1, source_target_pairs={{0,24},{1,25},{2,26},{3,27},{4,28},{5,29},{6,30},{7,31},{8,16},{9,... | collective-permute-start | bytes 196616 | tf_op jit(solution)/shard_map/ppermute | solution.py:419
  55.8 1.6 %collective-permute-start.15 = (f32[264,256]{1,0:T(8,128)S(1)}, f32[264,256]{1,0:T(8,128)S(1)}, u32[]{:S(2)}, u32[]{:S(2)}) collective-permute-start(f32[264,256]{1,0:T(8,128)S(1)} %backward_part.9), channel_id=1, source_target_pairs={{0,2},{1,3},{2,0},{3,1},{4,6},{5,7},{6,4},{7,5},{8,10},{9,11},{10,... | collective-permute-start | bytes 811016 | tf_op jit(solution)/shard_map/ppermute | solution.py:419
  57.5 8.6 %collective-permute-start.16 = (f32[264,256]{1,0:T(8,128)S(1)}, f32[264,256]{1,0:T(8,128)S(1)}, u32[]{:S(2)}, u32[]{:S(2)}) collective-permute-start(f32[264,256]{1,0:T(8,128)S(1)} %get-tuple-element.69), channel_id=1, source_target_pairs={{0,4},{1,5},{2,6},{3,7},{4,0},{5,1},{6,2},{7,3},{8,12},{9,13},{10,... | collective-permute-start | bytes 811016 | tf_op jit(solution)/shard_map/ppermute | solution.py:419
  59.6 21.9 %copy-start = (f32[256,256]{1,0:T(8,128)S(1)}, f32[256,256]{1,0:T(8,128)}, u32[]{:S(2)}) copy-start(f32[256,256]{1,0:T(8,128)} %right.1) | copy-start | bytes 786436
  59.6 21.9 %copy-start.1 = (f32[256,256]{1,0:T(8,128)S(1)}, f32[256,256]{1,0:T(8,128)}, u32[]{:S(2)}) copy-start(f32[256,256]{1,0:T(8,128)} %search.1) | copy-start | bytes 786436
  59.6 21.9 %copy-start.2 = (f32[256,256]{1,0:T(8,128)S(1)}, f32[256,256]{1,0:T(8,128)}, u32[]{:S(2)}) copy-start(f32[256,256]{1,0:T(8,128)} %solution.1) | copy-start | bytes 786436
  59.6 21.9 %copy-start.4 = (f32[256]{0:T(256)S(1)}, f32[256]{0:T(256)}, u32[]{:S(2)}) copy-start(f32[256]{0:T(256)} %param.16) | copy-start | bytes 3076
  59.6 21.9 %copy-start.5 = (f32[256]{0:T(256)S(1)}, f32[256]{0:T(256)}, u32[]{:S(2)}) copy-start(f32[256]{0:T(256)} %param.17) | copy-start | bytes 3076
  59.6 2.7 %collective-permute-start.11 = (f32[256,256]{1,0:T(8,128)S(1)}, f32[256,256]{1,0:T(8,128)S(1)}, u32[]{:S(2)}, u32[]{:S(2)}) collective-permute-start(f32[256,256]{1,0:T(8,128)S(1)} %backward_part.7), channel_id=1, source_target_pairs={{0,2},{1,3},{2,0},{3,1},{4,6},{5,7},{6,4},{7,5},{8,10},{9,11},{10,... | collective-permute-start | bytes 786440 | tf_op jit(solution)/shard_map/ppermute | solution.py:419
  59.7 11.1 %collective-permute-start.20 = (f32[4,64,256]{2,1,0:T(8,128)S(1)}, f32[4,64,256]{2,1,0:T(8,128)S(1)}, u32[]{:S(2)}, u32[]{:S(2)}) collective-permute-start(f32[4,64,256]{2,1,0:T(8,128)S(1)} %stack_left.1.refs_2_.own), channel_id=1, source_target_pairs={{0,1},{1,0},{2,3},{3,2},{4,5},{5,4},{6,7},{7,6},{8,9},{9,8},{10,11... | collective-permute-start | bytes 786440 | tf_op jit(solution)/shard_map/ppermute | solution.py:419
  66.4 15.1 %collective-permute-start.17 = (f32[64,256]{1,0:T(8,128)S(1)}, f32[64,256]{1,0:T(8,128)S(1)}, u32[]{:S(2)}, u32[]{:S(2)}) collective-permute-start(f32[64,256]{1,0:T(8,128)S(1)} %get-tuple-element.72), channel_id=1, source_target_pairs={{0,8},{1,9},{2,10},{3,11},{4,12},{5,13},{6,14},{7,15},{8,0},{9,1},... | collective-permute-start | bytes 196616 | tf_op jit(solution)/shard_map/ppermute | solution.py:419
  66.4 15.0 %collective-permute-start.18 = (f32[64,256]{1,0:T(8,128)S(1)}, f32[64,256]{1,0:T(8,128)S(1)}, u32[]{:S(2)}, u32[]{:S(2)}) collective-permute-start(f32[64,256]{1,0:T(8,128)S(1)} %get-tuple-element.73), channel_id=1, source_target_pairs={{0,16},{1,17},{2,18},{3,19},{4,20},{5,21},{6,22},{7,23},{8,24},{9,... | collective-permute-start | bytes 196616 | tf_op jit(solution)/shard_map/ppermute | solution.py:419
  68.6 12.9 %collective-permute-start.19 = (f32[64,256]{1,0:T(8,128)S(1)}, f32[64,256]{1,0:T(8,128)S(1)}, u32[]{:S(2)}, u32[]{:S(2)}) collective-permute-start(f32[64,256]{1,0:T(8,128)S(1)} %get-tuple-element.74), channel_id=1, source_target_pairs={{0,24},{1,25},{2,26},{3,27},{4,28},{5,29},{6,30},{7,31},{8,16},{9,... | collective-permute-start | bytes 196616 | tf_op jit(solution)/shard_map/ppermute | solution.py:419

commit v12 on v11

--- a/solution.py
+++ b/solution.py
@@ -256,30 +256,46 @@
     return jnp.broadcast_to(row, (128, row.shape[1])).T
 
 
-def left_half_kernel(mine, other, *refs):
+def left_half_kernel(mine, other, raw, both, sums):
     _, z, _ = coords()
     left = mine[...] + other[...]
-    both, sums = refs[-2:]
+    raw[...] = left
     both[...] = split_rows(left)
-    squares = square_row(left, z, sums.shape[1])
-    sums[...] = refs[0][...] + squares if len(refs) == 4 else squares
-    if len(refs) > 4:
-        n = left.shape[1] // 4
-        for k, out in enumerate(refs[:4]):
-            out[...] = left[:, k * n : (k + 1) * n]
-
-
-def left_half(mine, other, squares=None, token=None):
+    sums[...] = square_row(left, z, sums.shape[1])
+
+
+def left_half(mine, other):
     q, docs = mine.shape
-    extra = [] if squares is None else [squares, token]
-    pieces = [f32(q, docs // 4)] * 4 if squares is None else []
     return pl.pallas_call(
         left_half_kernel,
-        out_shape=pieces + [bf16(2 * q, docs), f32(8, 4 * q)],
+        out_shape=[f32(q, docs), bf16(2 * q, docs), f32(8, 4 * q)],
         compiler_params=params(8),
         cost_estimate=cost(8 * q * docs, 16 * q * docs),
         name="left_half",
-    )(mine, other, *extra)
+    )(mine, other)
+
+
+def left_rest_kernel(mine, other, raw, squares, token, both, sums, l0, l1, l2, l3):
+    _, z, _ = coords()
+    left = mine[...] + other[...]
+    both[...] = split_rows(left)
+    sums[...] = squares[...] + square_row(left, z, sums.shape[1])
+    q, n = left.shape[0], left.shape[1] // 4
+    for k, out in enumerate((l0, l1, l2, l3)):
+        out[:q, :] = raw[:, k * n : (k + 1) * n]
+        out[q:, :] = left[:, k * n : (k + 1) * n]
+
+
+def left_rest(mine, other, raw, squares, token):
+    q, docs = mine.shape
+    both, sums, *pieces = pl.pallas_call(
+        left_rest_kernel,
+        out_shape=[bf16(2 * q, docs), f32(8, 4 * q)] + [f32(2 * q, docs // 4)] * 4,
+        compiler_params=params(8),
+        cost_estimate=cost(8 * q * docs, 24 * q * docs),
+        name="left_rest",
+    )(mine, other, raw, squares, token)
+    return both, sums, pieces
 
 
 def backward_kernel(first, blocks, parts, hi_ref, lo_ref, both_ref, *refs):
@@ -367,7 +383,7 @@
     return pieces, sums.reshape(32, 1, 128)
 
 
-def finish_kernel(docs_total, feat_total, g0, g1, g2, g3, squares, own, other, right, search, solution, phibar, rhobar,
+def finish_kernel(docs_total, feat_total, g0, g1, g2, g3, squares, l0, l1, l2, l3, right, search, solution, phibar, rhobar,
                   left_out, right_out, search_out, solution_out, alpha_out, phibar_out, rhobar_out, turned):
     _, z, y = coords()
     q, half = turned.shape[1:]
@@ -382,9 +398,9 @@
     )
     alpha = jnp.sqrt(alpha_sums / feat_total + epsilon)
     beta = jnp.sqrt(beta_sums / docs_total + epsilon)
-    for part, ref in ((y, own), (1 - y, other)):
-        for k in range(4):
-            turned[z ^ k] = ref[k]
+    for rel, part in enumerate((y, 1 - y)):
+        for k, piece in enumerate((l0, l1, l2, l3)):
+            turned[z ^ k] = piece[rel * q : (rel + 1) * q, :]
         left_out[pl.ds(pl.multiple_of(part * half, half), half), :] = turned[...].reshape(-1, half).T / beta
     rho = jnp.sqrt(rhobar[...] * rhobar[...] + beta * beta)
     cosine = rhobar[...] / rho
@@ -403,7 +419,7 @@
     solution_out[...] = solution[...] + (phi / rho) * search[...]
 
 
-def finish(docs_total, feat_total, pieces, squares, own, other, right, search, solution, phibar, rhobar):
+def finish(docs_total, feat_total, pieces, squares, lefts, right, search, solution, phibar, rhobar):
     rows, cols = right.shape
     return pl.pallas_call(
         functools.partial(finish_kernel, docs_total, feat_total),
@@ -412,7 +428,7 @@
         compiler_params=params(12),
         cost_estimate=cost(rows * cols * 16, rows * cols * 20),
         name="finish",
-    )(*pieces, squares, own, other, right, search, solution, phibar, rhobar)
+    )(*pieces, squares, *lefts, right, search, solution, phibar, rhobar)
 
 
 def swap(value, mask):
@@ -452,23 +468,22 @@
     total0 = forward_part(rows0, [own_x], (4,), total0)
     product0 = product_half(rows0, x_peer, total0, (12,), *messages, alpha_row)
 
-    *lefts, both0, beta0 = left_half(product0, swap(product1, Y_BIT))
+    raw, both0, beta0 = left_half(product0, swap(product1, Y_BIT))
     partial = backward_part(rows0, both0, 0, 16)
-    left_own = stack(along_z(lefts), q, "stack_left")
-    both1, beta1 = left_half(product1, swap(product0, Y_BIT), beta0, partial)
-    far = swap(backward_part(rows1, both1, 12, 4, partial, beta1, [left_own]), CORE_BIT)
+    both1, beta1, lefts = left_rest(product1, swap(product0, Y_BIT), raw, beta0, partial)
+    far = swap(backward_part(rows1, both1, 12, 4, partial, beta1), CORE_BIT)
     near = backward_part(rows1, both1, 4, 4, partial)
     send, beta_core = far_sums(near, far, beta1)
     got = swap(send, X_BIT)
+    lefts = along_z([lefts[0]] + [after(l, send) for l in lefts[1:]])
     peer = backward_part(rows1, both1, 8, 4, partial)
-    left_other = swap(after(left_own, peer), Y_BIT)
     keep = backward_part(rows1, both1, 0, 4, partial)
 
     sent, sums = right_norm(docs_total, keep, swap(peer, CORE_BIT), got, beta_core, own)
     pieces = along_z(sent)
-    squares = lax.all_to_all(after(sums, left_other), AXES, 0, 0, tiled=True)
+    squares = lax.all_to_all(after(sums, *lefts[1:]), AXES, 0, 0, tiled=True)
     left_next, right_next, search_next, solution_next, alpha_next, phibar_next, rhobar_next = finish(
-        docs_total, feat_total, pieces, squares, left_own, left_other,
+        docs_total, feat_total, pieces, squares, lefts,
         right_vec, search_dir, solution_vec, phibar_row, rhobar_row,
     )
     return (

time: 83 us -> 87.1 us (1.049)
  blocking collectives: 10.7 us -> 14.8 us
    all_to_all x1, blocking collectives: 10.7 us -> 14.8 us  [by_columns(): squares = lax.all_to_all(after(sums, *lefts[1:]), AXES, 0, 0, tiled=True)]
    ppermute x21 -> x20, starting transfers between devices: 28.1 us -> 27.4 us  [swap(): return lax.ppermute(value, AXES, [(i, i ^ mask) for i in range(32)])]
    ppermute x21 -> x20, waiting for transfers between devices: 14.8 us -> 15.5 us  [swap(): return lax.ppermute(value, AXES, [(i, i ^ mask) for i in range(32)])]
  transfers between devices with their start and end apart: 21 -> 20, of which waited for: 8 -> 7; matrix products, arithmetic and copies ran while one was open for 0% -> 0% of each run, Pallas kernels for 28% -> 27%
where the time goes in v12:
time: 87.1 us; the launch traced here: 87 us
  Pallas kernels  28.3 us (32%)
  starting transfers between devices  27.4 us (31%)
  waiting for transfers between devices  15.5 us (18%)
  blocking collectives  14.8 us (17%)
  between operations  0.91 us (1%)
    ppermute x20, starting transfers between devices, swap(): return lax.ppermute(value, AXES, [(i, i ^ mask) for i in range(32)])  27.4 us
    ppermute x20, waiting for transfers between devices, swap(): return lax.ppermute(value, AXES, [(i, i ^ mask) for i in range(32)])  15.5 us
    all_to_all x1, blocking collectives, by_columns(): squares = lax.all_to_all(after(sums, *lefts[1:]), AXES, 0, 0, tiled=True)  14.8 us
    pallas_call x2, Pallas kernels, build(): pl.pallas_call(functools.partial(build_kernel, rel), in_specs=[whole()] *...  9.64 us
    pallas_call x4, Pallas kernels, forward_part(): pl.pallas_call(functools.partial(forward_kernel, blocks, before is not No...  7.11 us
    pallas_call x5, Pallas kernels, backward_part(): pl.pallas_call(functools.partial(backward_kernel, first, blocks, tuple(ex...  5.24 us
    pallas_call x2, Pallas kernels, product_half(): pl.pallas_call(functools.partial(product_kernel, blocks), in_specs=[whole...  2.64 us
  transfers between devices with their start and end apart: 20, of which 7 were waited for; matrix products, arithmetic and copies ran while one was open for 0% of the time, Pallas kernels for 27%

profile of v12, /device:TPU:0, one launch (start us, length us, event | category | flops | bytes accessed | tf_op | source)
XLA Modules:
  0.0 87.0 jit_solution(12725598578652840280)
XLA Ops:
  0.6 1.6 %prepare.1 = (f32[64,256]{1,0:T(8,128)S(1)}, f32[128,256]{1,0:T(8,128)S(1)}, f32[128,256]{1,0:T(8,128)S(1)}, f32[128,256]{1,0:T(8,128)S(1)}, f32[128,256]{1,0:T(8,128)S(1)}) custom-call(s32[16,512]{1,0:T(8,128)} %bitcast.13, bf16[16,512]{1,0:T(8,128)(2,1)} %bitcast.14, f32[256,256]{1,0:T(8,128)} %right.1, f32[512,256]{1,0:T(8,128)} %left_hbm.1), custom_call_target="tpu_custom_call" | custom-call | bytes 16384 | tf_op jit(solution)/shard_map/prepare/pallas_call | solution.py:74
  2.3 3.1 %collective-permute-start = (f32[64,256]{1,0:T(8,128)S(1)}, f32[64,256]{1,0:T(8,128)S(1)}, u32[]{:S(2)}, u32[]{:S(2)}) collective-permute-start(f32[64,256]{1,0:T(8,128)S(1)} %get-tuple-element.49.e0), channel_id=1, source_target_pairs={{0,8},{1,9},{2,10},{3,11},{4,12},{5,13},{6,14},{7,15},{8,0},{9,1},... | collective-permute-start | bytes 196616 | tf_op jit(solution)/shard_map/ppermute | solution.py:435
  5.4 2.4 %collective-permute-start.2 = (f32[64,256]{1,0:T(8,128)S(1)}, f32[64,256]{1,0:T(8,128)S(1)}, u32[]{:S(2)}, u32[]{:S(2)}) collective-permute-start(f32[64,256]{1,0:T(8,128)S(1)} %get-tuple-element.49.e0), channel_id=1, source_target_pairs={{0,24},{1,25},{2,26},{3,27},{4,28},{5,29},{6,30},{7,31},{8,16},{9,... | collective-permute-start | bytes 196616 | tf_op jit(solution)/shard_map/ppermute | solution.py:435
  7.8 0.1 collective-permute-start.1
  8.0 1.8 %collective-permute-start.3 = (f32[128,256]{1,0:T(8,128)S(1)}, f32[128,256]{1,0:T(8,128)S(1)}, u32[]{:S(2)}, u32[]{:S(2)}) collective-permute-start(f32[128,256]{1,0:T(8,128)S(1)} %get-tuple-element.54), channel_id=1, source_target_pairs={{0,8},{1,9},{2,10},{3,11},{4,12},{5,13},{6,14},{7,15},{8,0},{9,1},... | collective-permute-start | bytes 393224 | tf_op jit(solution)/shard_map/ppermute | solution.py:435
  9.8 2.5 %collective-permute-start.4 = (f32[128,256]{1,0:T(8,128)S(1)}, f32[128,256]{1,0:T(8,128)S(1)}, u32[]{:S(2)}, u32[]{:S(2)}) collective-permute-start(f32[128,256]{1,0:T(8,128)S(1)} %get-tuple-element.56), channel_id=1, source_target_pairs={{0,16},{1,17},{2,18},{3,19},{4,20},{5,21},{6,22},{7,23},{8,24},{9,... | collective-permute-start | bytes 393224 | tf_op jit(solution)/shard_map/ppermute | solution.py:435
  12.2 0.5 collective-permute-start.5
  12.8 1.9 %collective-permute-done.1.e2 = f32[64,256]{1,0:T(8,128)S(1)} collective-permute-done((f32[64,256]{1,0:T(8,128)S(1)}, f32[64,256]{1,0:T(8,128)S(1)}, u32[]{:S(2)}, u32[]{:S(2)}) %collective-permute-start.1) | collective-permute-done | bytes 65568 | tf_op jit(solution)/shard_map/ppermute | solution.py:435
  14.7 4.7 %dense_rows.2 = (bf16[16,1024,256]{2,1,0:T(8,128)(2,1)S(1)}, bf16[16,1024,256]{2,1,0:T(8,128)(2,1)S(1)}, f32[8,128]{1,0:T(8,128)S(1)}) custom-call(f32[64,256]{1,0:T(8,128)S(1)} %get-tuple-element.49.e0, f32[64,256]{1,0:T(8,128)S(1)} %collective-permute-done.e1, f32[64,256]{1,0:T(8,128)S(1)} %collective-permute-done.1.e2, ...), custom_call_target="tpu_custom_call" | custom-call | flops 2147483648 | bytes 16777216 | tf_op jit(solution)/shard_map/dense_rows/pallas_call | solution.py:154
  19.5 3.4 %collective-permute-done.4.m2.refs_2_ = f32[128,256]{1,0:T(8,128)S(1)} collective-permute-done((f32[128,256]{1,0:T(8,128)S(1)}, f32[128,256]{1,0:T(8,128)S(1)}, u32[]{:S(2)}, u32[]{:S(2)}) %collective-permute-start.4) | collective-permute-done | bytes 131104 | tf_op jit(solution)/shard_map/ppermute | solution.py:435
  22.9 0.1 collective-permute-start.7
  23.0 1.6 %collective-permute-start.6 = (f32[4,64,256]{2,1,0:T(8,128)S(1)}, f32[4,64,256]{2,1,0:T(8,128)S(1)}, u32[]{:S(2)}, u32[]{:S(2)}) collective-permute-start(f32[4,64,256]{2,1,0:T(8,128)S(1)} %stack_right.1.refs_0_.right), channel_id=1, source_target_pairs={{0,4},{1,5},{2,6},{3,7},{4,0},{5,1},{6,2},{7,3},{8,12},{9,13},{10,... | collective-permute-start | bytes 786440 | tf_op jit(solution)/shard_map/ppermute | solution.py:435
  24.5 4.9 %dense_rows.3 = (bf16[16,1024,256]{2,1,0:T(8,128)(2,1)S(1)}, bf16[16,1024,256]{2,1,0:T(8,128)(2,1)S(1)}, f32[8,128]{1,0:T(8,128)S(1)}) custom-call(f32[64,256]{1,0:T(8,128)S(1)} %get-tuple-element.49.e0, f32[64,256]{1,0:T(8,128)S(1)} %collective-permute-done.e1, f32[64,256]{1,0:T(8,128)S(1)} %collective-permute-done.1.e2, ...), custom_call_target="tpu_custom_call" | custom-call | flops 33554432 | bytes 262144 | tf_op jit(solution)/shard_map/dense_rows/pallas_call | solution.py:154
  29.5 2.3 %forward_part.4.refs_1_ = f32[1024,128]{1,0:T(8,128)S(1)} custom-call(bf16[16,1024,256]{2,1,0:T(8,128)(2,1)S(1)} %get-tuple-element.50.hi_ref, bf16[16,1024,256]{2,1,0:T(8,128)(2,1)S(1)} %get-tuple-element.51.lo_ref, f32[4,64,256]{2,1,0:T(8,128)S(1)} %stack_right.1.refs_0_.right, f32[4,64,256]{2,1,0:T(8,128)S(1)} %collective-permute-done.7.refs_1_, ...), custom_call_target="tpu_custom_call" | custom-call | flops 67108864 | bytes 131072 | tf_op jit(solution)/shard_map/forward_part/pallas_call | solution.py:196
  31.8 0.3 collective-permute-start.8
  32.1 1.2 %forward_part.5.before = f32[1024,128]{1,0:T(8,128)S(1)} custom-call(bf16[16,1024,256]{2,1,0:T(8,128)(2,1)S(1)} %get-tuple-element.50.hi_ref, bf16[16,1024,256]{2,1,0:T(8,128)(2,1)S(1)} %get-tuple-element.51.lo_ref, f32[4,64,256]{2,1,0:T(8,128)S(1)} %collective-permute-done.6.refs_0_, f32[1024,128]{1,0:T(8,128)S(1)} %forward_part.4.refs_1_), custom_call_target="tpu_custom_call" | custom-call | flops 33554432 | bytes 65536 | tf_op jit(solution)/shard_map/forward_part/pallas_call | solution.py:196
  33.3 0.1 collective-permute-done.8.vec
  33.4 1.3 %product_half.2.mine = f32[64,1024]{1,0:T(8,128)S(1)} custom-call(bf16[16,1024,256]{2,1,0:T(8,128)(2,1)S(1)} %get-tuple-element.50.hi_ref, bf16[16,1024,256]{2,1,0:T(8,128)(2,1)S(1)} %get-tuple-element.51.lo_ref, f32[4,64,256]{2,1,0:T(8,128)S(1)} %collective-permute-done.8.vec, f32[1024,128]{1,0:T(8,128)S(1)} %forward_part.5.before), custom_call_target="tpu_custom_call" | custom-call | flops 33554432 | bytes 65536 | tf_op jit(solution)/shard_map/product_half/pallas_call | solution.py:228
  34.7 1.6 %collective-permute-start.10 = (f32[64,1024]{1,0:T(8,128)S(1)}, f32[64,1024]{1,0:T(8,128)S(1)}, u32[]{:S(2)}, u32[]{:S(2)}) collective-permute-start(f32[64,1024]{1,0:T(8,128)S(1)} %product_half.2.mine), channel_id=1, source_target_pairs={{0,1},{1,0},{2,3},{3,2},{4,5},{5,4},{6,7},{7,6},{8,9},{9,8},{10,11... | collective-permute-start | bytes 786440 | tf_op jit(solution)/shard_map/ppermute | solution.py:435
  36.3 2.3 %forward_part.6.refs_1_ = f32[1024,128]{1,0:T(8,128)S(1)} custom-call(bf16[16,1024,256]{2,1,0:T(8,128)(2,1)S(1)} %get-tuple-element.62.hi_ref, bf16[16,1024,256]{2,1,0:T(8,128)(2,1)S(1)} %get-tuple-element.63.lo_ref, f32[4,64,256]{2,1,0:T(8,128)S(1)} %stack_right.1.refs_0_.right, f32[4,64,256]{2,1,0:T(8,128)S(1)} %collective-permute-done.7.refs_1_), custom_call_target="tpu_custom_call" | custom-call | flops 67108864 | bytes 131072 | tf_op jit(solution)/shard_map/forward_part/pallas_call | solution.py:196
  38.7 0.0 copy-start.3
  38.7 1.2 %forward_part.7.before = f32[1024,128]{1,0:T(8,128)S(1)} custom-call(bf16[16,1024,256]{2,1,0:T(8,128)(2,1)S(1)} %get-tuple-element.62.hi_ref, bf16[16,1024,256]{2,1,0:T(8,128)(2,1)S(1)} %get-tuple-element.63.lo_ref, f32[4,64,256]{2,1,0:T(8,128)S(1)} %collective-permute-done.6.refs_0_, f32[1024,128]{1,0:T(8,128)S(1)} %forward_part.6.refs_1_), custom_call_target="tpu_custom_call" | custom-call | flops 33554432 | bytes 65536 | tf_op jit(solution)/shard_map/forward_part/pallas_call | solution.py:196
  39.9 1.3 %product_half.3.mine = f32[64,1024]{1,0:T(8,128)S(1)} custom-call(bf16[16,1024,256]{2,1,0:T(8,128)(2,1)S(1)} %get-tuple-element.62.hi_ref, bf16[16,1024,256]{2,1,0:T(8,128)(2,1)S(1)} %get-tuple-element.63.lo_ref, f32[4,64,256]{2,1,0:T(8,128)S(1)} %collective-permute-done.8.vec, f32[1024,128]{1,0:T(8,128)S(1)} %forward_part.7.before, ...), custom_call_target="tpu_custom_call" | custom-call | flops 33554432 | bytes 65536 | tf_op jit(solution)/shard_map/product_half/pallas_call | solution.py:228
  41.3 0.5 collective-permute-start.9
  41.8 1.4 %collective-permute-done.10.other = f32[64,1024]{1,0:T(8,128)S(1)} collective-permute-done((f32[64,1024]{1,0:T(8,128)S(1)}, f32[64,1024]{1,0:T(8,128)S(1)}, u32[]{:S(2)}, u32[]{:S(2)}) %collective-permute-start.10) | collective-permute-done | bytes 262176 | tf_op jit(solution)/shard_map/ppermute | solution.py:435
  43.2 0.2 left_half.1
  43.4 2.3 %backward_part.5.token.refs_0_ = f32[1024,256]{1,0:T(8,128)S(1)} custom-call(bf16[16,1024,256]{2,1,0:T(8,128)(2,1)S(1)} %get-tuple-element.62.hi_ref, bf16[16,1024,256]{2,1,0:T(8,128)(2,1)S(1)} %get-tuple-element.63.lo_ref, bf16[128,1024]{1,0:T(8,128)(2,1)S(1)} %get-tuple-element.66.both_ref), custom_call_target="tpu_custom_call" | custom-call | flops 134217728 | bytes 262144 | tf_op jit(solution)/shard_map/backward_part/pallas_call | solution.py:325
  45.7 3.7 %collective-permute-done.9.other = f32[64,1024]{1,0:T(8,128)S(1)} collective-permute-done((f32[64,1024]{1,0:T(8,128)S(1)}, f32[64,1024]{1,0:T(8,128)S(1)}, u32[]{:S(2)}, u32[]{:S(2)}) %collective-permute-start.9) | collective-permute-done | bytes 262176 | tf_op jit(solution)/shard_map/ppermute | solution.py:435
  49.5 0.2 left_rest.1
  49.7 0.7 backward_part.9
  50.4 0.1 collective-permute-start.12
  50.5 0.7 backward_part.8.near
  51.2 0.8 collective-permute-done.12.far
  52.0 1.4 %collective-permute-start.13 = (f32[264,256]{1,0:T(8,128)S(1)}, f32[264,256]{1,0:T(8,128)S(1)}, u32[]{:S(2)}, u32[]{:S(2)}) collective-permute-start(f32[264,256]{1,0:T(8,128)S(1)} %get-tuple-element.69), channel_id=1, source_target_pairs={{0,4},{1,5},{2,6},{3,7},{4,0},{5,1},{6,2},{7,3},{8,12},{9,13},{10,... | collective-permute-start | bytes 811016 | tf_op jit(solution)/shard_map/ppermute | solution.py:435
  53.4 0.7 backward_part.7
  54.1 0.1 collective-permute-start.11
  54.2 3.3 %collective-permute-start.17 = (f32[128,256]{1,0:T(8,128)S(1)}, f32[128,256]{1,0:T(8,128)S(1)}, u32[]{:S(2)}, u32[]{:S(2)}) collective-permute-start(f32[128,256]{1,0:T(8,128)S(1)} %get-tuple-element.77), channel_id=1, source_target_pairs={{0,8},{1,9},{2,10},{3,11},{4,12},{5,13},{6,14},{7,15},{8,0},{9,1},... | collective-permute-start | bytes 393224 | tf_op jit(solution)/shard_map/ppermute | solution.py:435
  57.5 0.0 copy-start.5
  57.5 2.3 %collective-permute-start.18 = (f32[128,256]{1,0:T(8,128)S(1)}, f32[128,256]{1,0:T(8,128)S(1)}, u32[]{:S(2)}, u32[]{:S(2)}) collective-permute-start(f32[128,256]{1,0:T(8,128)S(1)} %get-tuple-element.79), channel_id=1, source_target_pairs={{0,16},{1,17},{2,18},{3,19},{4,20},{5,21},{6,22},{7,23},{8,24},{9,... | collective-permute-start | bytes 393224 | tf_op jit(solution)/shard_map/ppermute | solution.py:435
  59.9 0.2 collective-permute-start.19
  60.1 0.7 backward_part.6.keep
  60.8 0.3 right_norm.1
  61.1 3.1 %collective-permute-start.14 = (f32[64,256]{1,0:T(8,128)S(1)}, f32[64,256]{1,0:T(8,128)S(1)}, u32[]{:S(2)}, u32[]{:S(2)}) collective-permute-start(f32[64,256]{1,0:T(8,128)S(1)} %get-tuple-element.72), channel_id=1, source_target_pairs={{0,8},{1,9},{2,10},{3,11},{4,12},{5,13},{6,14},{7,15},{8,0},{9,1},... | collective-permute-start | bytes 196616 | tf_op jit(solution)/shard_map/ppermute | solution.py:435
  64.2 2.3 %collective-permute-start.15 = (f32[64,256]{1,0:T(8,128)S(1)}, f32[64,256]{1,0:T(8,128)S(1)}, u32[]{:S(2)}, u32[]{:S(2)}) collective-permute-start(f32[64,256]{1,0:T(8,128)S(1)} %get-tuple-element.73), channel_id=1, source_target_pairs={{0,16},{1,17},{2,18},{3,19},{4,20},{5,21},{6,22},{7,23},{8,24},{9,... | collective-permute-start | bytes 196616 | tf_op jit(solution)/shard_map/ppermute | solution.py:435
  66.5 0.2 collective-permute-start.16
  66.7 4.0 %collective-permute-done.18.l2 = f32[128,256]{1,0:T(8,128)S(1)} collective-permute-done((f32[128,256]{1,0:T(8,128)S(1)}, f32[128,256]{1,0:T(8,128)S(1)}, u32[]{:S(2)}, u32[]{:S(2)}) %collective-permute-start.18) | collective-permute-done | bytes 131104 | tf_op jit(solution)/shard_map/ppermute | solution.py:435
  70.7 14.8 %all_to_all.5.squares = f32[32,1,128]{2,1,0:T(1,128)S(1)} all-to-all(f32[32,1,128]{2,1,0:T(1,128)S(1)} %bitcast.9), channel_id=1, replica_groups=mesh['doc'=16,'feat'=2] {'doc','feat'}, dimensions={0} | all-to-all | bytes 32768 | tf_op jit(solution)/shard_map/all_to_all | solution.py:484
  85.6 1.3 %finish.1 = (f32[512,256]{1,0:T(8,128)}, f32[256,256]{1,0:T(8,128)}, f32[256,256]{1,0:T(8,128)}, f32[256,256]{1,0:T(8,128)}, f32[1,256]{1,0:T(1,128)}, /*index=5*/f32[1,256]{1,0:T(1,128)}, f32[1,256]{1,0:T(1,128)}) custom-call(f32[64,256]{1,0:T(8,128)S(1)} %get-tuple-element.71.g0, f32[64,256]{1,0:T(8,128)S(1)} %collective-permute-done.14.g1, ...), custom_call_target="tpu_custom_call" | custom-call | flops 16384 | bytes 20480 | tf_op jit(solution)/shard_map/finish/pallas_call | solution.py:424
  (25 shorter events, 0.1 us)
Async XLA Ops:
  2.3 5.7 %collective-permute-start = (f32[64,256]{1,0:T(8,128)S(1)}, f32[64,256]{1,0:T(8,128)S(1)}, u32[]{:S(2)}, u32[]{:S(2)}) collective-permute-start(f32[64,256]{1,0:T(8,128)S(1)} %get-tuple-element.49.e0), channel_id=1, source_target_pairs={{0,8},{1,9},{2,10},{3,11},{4,12},{5,13},{6,14},{7,15},{8,0},{9,1},... | collective-permute-start | bytes 196616 | tf_op jit(solution)/shard_map/ppermute | solution.py:435
  5.4 7.4 %collective-permute-start.2 = (f32[64,256]{1,0:T(8,128)S(1)}, f32[64,256]{1,0:T(8,128)S(1)}, u32[]{:S(2)}, u32[]{:S(2)}) collective-permute-start(f32[64,256]{1,0:T(8,128)S(1)} %get-tuple-element.49.e0), channel_id=1, source_target_pairs={{0,24},{1,25},{2,26},{3,27},{4,28},{5,29},{6,30},{7,31},{8,16},{9,... | collective-permute-start | bytes 196616 | tf_op jit(solution)/shard_map/ppermute | solution.py:435
  7.8 6.9 %collective-permute-start.1 = (f32[64,256]{1,0:T(8,128)S(1)}, f32[64,256]{1,0:T(8,128)S(1)}, u32[]{:S(2)}, u32[]{:S(2)}) collective-permute-start(f32[64,256]{1,0:T(8,128)S(1)} %get-tuple-element.49.e0), channel_id=1, source_target_pairs={{0,16},{1,17},{2,18},{3,19},{4,20},{5,21},{6,22},{7,23},{8,24},{9,... | collective-permute-start | bytes 196616 | tf_op jit(solution)/shard_map/ppermute | solution.py:435
  8.0 11.5 %collective-permute-start.3 = (f32[128,256]{1,0:T(8,128)S(1)}, f32[128,256]{1,0:T(8,128)S(1)}, u32[]{:S(2)}, u32[]{:S(2)}) collective-permute-start(f32[128,256]{1,0:T(8,128)S(1)} %get-tuple-element.54), channel_id=1, source_target_pairs={{0,8},{1,9},{2,10},{3,11},{4,12},{5,13},{6,14},{7,15},{8,0},{9,1},... | collective-permute-start | bytes 393224 | tf_op jit(solution)/shard_map/ppermute | solution.py:435
  9.8 13.1 %collective-permute-start.4 = (f32[128,256]{1,0:T(8,128)S(1)}, f32[128,256]{1,0:T(8,128)S(1)}, u32[]{:S(2)}, u32[]{:S(2)}) collective-permute-start(f32[128,256]{1,0:T(8,128)S(1)} %get-tuple-element.56), channel_id=1, source_target_pairs={{0,16},{1,17},{2,18},{3,19},{4,20},{5,21},{6,22},{7,23},{8,24},{9,... | collective-permute-start | bytes 393224 | tf_op jit(solution)/shard_map/ppermute | solution.py:435
  12.2 10.7 %collective-permute-start.5 = (f32[128,256]{1,0:T(8,128)S(1)}, f32[128,256]{1,0:T(8,128)S(1)}, u32[]{:S(2)}, u32[]{:S(2)}) collective-permute-start(f32[128,256]{1,0:T(8,128)S(1)} %get-tuple-element.58), channel_id=1, source_target_pairs={{0,24},{1,25},{2,26},{3,27},{4,28},{5,29},{6,30},{7,31},{8,16},{9,... | collective-permute-start | bytes 393224 | tf_op jit(solution)/shard_map/ppermute | solution.py:435
  22.9 6.6 %collective-permute-start.7 = (f32[4,64,256]{2,1,0:T(8,128)S(1)}, f32[4,64,256]{2,1,0:T(8,128)S(1)}, u32[]{:S(2)}, u32[]{:S(2)}) collective-permute-start(f32[4,64,256]{2,1,0:T(8,128)S(1)} %stack_right.1.refs_0_.right), channel_id=1, source_target_pairs={{0,2},{1,3},{2,0},{3,1},{4,6},{5,7},{6,4},{7,5},{8,10},{9,11},{10,... | collective-permute-start | bytes 786440 | tf_op jit(solution)/shard_map/ppermute | solution.py:435
  23.0 8.8 %collective-permute-start.6 = (f32[4,64,256]{2,1,0:T(8,128)S(1)}, f32[4,64,256]{2,1,0:T(8,128)S(1)}, u32[]{:S(2)}, u32[]{:S(2)}) collective-permute-start(f32[4,64,256]{2,1,0:T(8,128)S(1)} %stack_right.1.refs_0_.right), channel_id=1, source_target_pairs={{0,4},{1,5},{2,6},{3,7},{4,0},{5,1},{6,2},{7,3},{8,12},{9,13},{10,... | collective-permute-start | bytes 786440 | tf_op jit(solution)/shard_map/ppermute | solution.py:435
  31.8 1.6 %collective-permute-start.8 = (f32[4,64,256]{2,1,0:T(8,128)S(1)}, f32[4,64,256]{2,1,0:T(8,128)S(1)}, u32[]{:S(2)}, u32[]{:S(2)}) collective-permute-start(f32[4,64,256]{2,1,0:T(8,128)S(1)} %collective-permute-done.6.refs_0_), channel_id=1, source_target_pairs={{0,2},{1,3},{2,0},{3,1},{4,6},{5,7},{6,4},{7,5},{8,10},{9,11},{10,... | collective-permute-start | bytes 786440 | tf_op jit(solution)/shard_map/ppermute | solution.py:435
  34.7 8.5 %collective-permute-start.10 = (f32[64,1024]{1,0:T(8,128)S(1)}, f32[64,1024]{1,0:T(8,128)S(1)}, u32[]{:S(2)}, u32[]{:S(2)}) collective-permute-start(f32[64,1024]{1,0:T(8,128)S(1)} %product_half.2.mine), channel_id=1, source_target_pairs={{0,1},{1,0},{2,3},{3,2},{4,5},{5,4},{6,7},{7,6},{8,9},{9,8},{10,11... | collective-permute-start | bytes 786440 | tf_op jit(solution)/shard_map/ppermute | solution.py:435
  38.7 1.3 %copy-start.3 = (f32[256]{0:T(256)S(1)}, f32[256]{0:T(256)}, u32[]{:S(2)}) copy-start(f32[256]{0:T(256)} %param.15) | copy-start | bytes 3076
  41.3 8.2 %collective-permute-start.9 = (f32[64,1024]{1,0:T(8,128)S(1)}, f32[64,1024]{1,0:T(8,128)S(1)}, u32[]{:S(2)}, u32[]{:S(2)}) collective-permute-start(f32[64,1024]{1,0:T(8,128)S(1)} %product_half.3.mine), channel_id=1, source_target_pairs={{0,1},{1,0},{2,3},{3,2},{4,5},{5,4},{6,7},{7,6},{8,9},{9,8},{10,11... | collective-permute-start | bytes 786440 | tf_op jit(solution)/shard_map/ppermute | solution.py:435
  50.4 1.6 %collective-permute-start.12 = (f32[264,256]{1,0:T(8,128)S(1)}, f32[264,256]{1,0:T(8,128)S(1)}, u32[]{:S(2)}, u32[]{:S(2)}) collective-permute-start(f32[264,256]{1,0:T(8,128)S(1)} %backward_part.9), channel_id=1, source_target_pairs={{0,2},{1,3},{2,0},{3,1},{4,6},{5,7},{6,4},{7,5},{8,10},{9,11},{10,... | collective-permute-start | bytes 811016 | tf_op jit(solution)/shard_map/ppermute | solution.py:435
  52.0 8.8 %collective-permute-start.13 = (f32[264,256]{1,0:T(8,128)S(1)}, f32[264,256]{1,0:T(8,128)S(1)}, u32[]{:S(2)}, u32[]{:S(2)}) collective-permute-start(f32[264,256]{1,0:T(8,128)S(1)} %get-tuple-element.69), channel_id=1, source_target_pairs={{0,4},{1,5},{2,6},{3,7},{4,0},{5,1},{6,2},{7,3},{8,12},{9,13},{10,... | collective-permute-start | bytes 811016 | tf_op jit(solution)/shard_map/ppermute | solution.py:435
  54.1 6.6 %collective-permute-start.11 = (f32[256,256]{1,0:T(8,128)S(1)}, f32[256,256]{1,0:T(8,128)S(1)}, u32[]{:S(2)}, u32[]{:S(2)}) collective-permute-start(f32[256,256]{1,0:T(8,128)S(1)} %backward_part.7), channel_id=1, source_target_pairs={{0,2},{1,3},{2,0},{3,1},{4,6},{5,7},{6,4},{7,5},{8,10},{9,11},{10,... | collective-permute-start | bytes 786440 | tf_op jit(solution)/shard_map/ppermute | solution.py:435
  54.2 12.3 %collective-permute-start.17 = (f32[128,256]{1,0:T(8,128)S(1)}, f32[128,256]{1,0:T(8,128)S(1)}, u32[]{:S(2)}, u32[]{:S(2)}) collective-permute-start(f32[128,256]{1,0:T(8,128)S(1)} %get-tuple-element.77), channel_id=1, source_target_pairs={{0,8},{1,9},{2,10},{3,11},{4,12},{5,13},{6,14},{7,15},{8,0},{9,1},... | collective-permute-start | bytes 393224 | tf_op jit(solution)/shard_map/ppermute | solution.py:435
  57.5 28.0 %copy-start = (f32[256,256]{1,0:T(8,128)S(1)}, f32[256,256]{1,0:T(8,128)}, u32[]{:S(2)}) copy-start(f32[256,256]{1,0:T(8,128)} %right.1) | copy-start | bytes 786436
  57.5 28.0 %copy-start.1 = (f32[256,256]{1,0:T(8,128)S(1)}, f32[256,256]{1,0:T(8,128)}, u32[]{:S(2)}) copy-start(f32[256,256]{1,0:T(8,128)} %search.1) | copy-start | bytes 786436
  57.5 28.1 %copy-start.2 = (f32[256,256]{1,0:T(8,128)S(1)}, f32[256,256]{1,0:T(8,128)}, u32[]{:S(2)}) copy-start(f32[256,256]{1,0:T(8,128)} %solution.1) | copy-start | bytes 786436
  57.5 28.1 %copy-start.4 = (f32[256]{0:T(256)S(1)}, f32[256]{0:T(256)}, u32[]{:S(2)}) copy-start(f32[256]{0:T(256)} %param.16) | copy-start | bytes 3076
  57.5 28.1 %copy-start.5 = (f32[256]{0:T(256)S(1)}, f32[256]{0:T(256)}, u32[]{:S(2)}) copy-start(f32[256]{0:T(256)} %param.17) | copy-start | bytes 3076
  57.5 13.1 %collective-permute-start.18 = (f32[128,256]{1,0:T(8,128)S(1)}, f32[128,256]{1,0:T(8,128)S(1)}, u32[]{:S(2)}, u32[]{:S(2)}) collective-permute-start(f32[128,256]{1,0:T(8,128)S(1)} %get-tuple-element.79), channel_id=1, source_target_pairs={{0,16},{1,17},{2,18},{3,19},{4,20},{5,21},{6,22},{7,23},{8,24},{9,... | collective-permute-start | bytes 393224 | tf_op jit(solution)/shard_map/ppermute | solution.py:435
  59.9 10.8 %collective-permute-start.19 = (f32[128,256]{1,0:T(8,128)S(1)}, f32[128,256]{1,0:T(8,128)S(1)}, u32[]{:S(2)}, u32[]{:S(2)}) collective-permute-start(f32[128,256]{1,0:T(8,128)S(1)} %get-tuple-element.81), channel_id=1, source_target_pairs={{0,24},{1,25},{2,26},{3,27},{4,28},{5,29},{6,30},{7,31},{8,16},{9,... | collective-permute-start | bytes 393224 | tf_op jit(solution)/shard_map/ppermute | solution.py:435
  61.1 24.4 %collective-permute-start.14 = (f32[64,256]{1,0:T(8,128)S(1)}, f32[64,256]{1,0:T(8,128)S(1)}, u32[]{:S(2)}, u32[]{:S(2)}) collective-permute-start(f32[64,256]{1,0:T(8,128)S(1)} %get-tuple-element.72), channel_id=1, source_target_pairs={{0,8},{1,9},{2,10},{3,11},{4,12},{5,13},{6,14},{7,15},{8,0},{9,1},... | collective-permute-start | bytes 196616 | tf_op jit(solution)/shard_map/ppermute | solution.py:435
  64.2 21.3 %collective-permute-start.15 = (f32[64,256]{1,0:T(8,128)S(1)}, f32[64,256]{1,0:T(8,128)S(1)}, u32[]{:S(2)}, u32[]{:S(2)}) collective-permute-start(f32[64,256]{1,0:T(8,128)S(1)} %get-tuple-element.73), channel_id=1, source_target_pairs={{0,16},{1,17},{2,18},{3,19},{4,20},{5,21},{6,22},{7,23},{8,24},{9,... | collective-permute-start | bytes 196616 | tf_op jit(solution)/shard_map/ppermute | solution.py:435
  66.5 19.0 %collective-permute-start.16 = (f32[64,256]{1,0:T(8,128)S(1)}, f32[64,256]{1,0:T(8,128)S(1)}, u32[]{:S(2)}, u32[]{:S(2)}) collective-permute-start(f32[64,256]{1,0:T(8,128)S(1)} %get-tuple-element.74), channel_id=1, source_target_pairs={{0,24},{1,25},{2,26},{3,27},{4,28},{5,29},{6,30},{7,31},{8,16},{9,... | collective-permute-start | bytes 196616 | tf_op jit(solution)/shard_map/ppermute | solution.py:435

commit v13 on v11

--- a/solution.py
+++ b/solution.py
@@ -420,7 +420,10 @@
 
 
 def along_z(values):
-    return [values[0]] + [swap(values[k], k << Z_SHIFT) for k in (1, 2, 3)]
+    got = {0: values[0]}
+    for k in (2, 3, 1):
+        got[k] = swap(values[k], k << Z_SHIFT)
+    return [got[k] for k in range(4)]
 
 
 def after(value, *earlier):
@@ -436,7 +439,7 @@
 
     stored, messages = prepare(col_ids.T, col_vals.T, right_vec, left_vec)
     entries = along_z([stored] * 4)
-    messages = along_z([messages[0]] + [after(m, entries[1]) for m in messages[1:]])
+    messages = along_z([messages[0]] + [after(messages[1], entries[2]), messages[2], messages[3]])
     q = right_vec.shape[1] // 4
 
     rows1, token1 = build(entries, 1)

time: 83 us -> 82.5 us (level)
  waiting for transfers between devices: 14.8 us -> 12.8 us
  blocking collectives: 10.7 us -> 11.6 us
    ppermute x21, waiting for transfers between devices: 14.8 us -> 12.8 us  [swap(): return lax.ppermute(value, AXES, [(i, i ^ mask) for i in range(32)])]
    all_to_all x1, blocking collectives: 10.7 us -> 11.6 us  [by_columns(): squares = lax.all_to_all(after(sums, left_other), AXES, 0, 0, tiled=True)]
where the time goes in v13:
time: 82.5 us; the launch traced here: 82.3 us
  starting transfers between devices  28.6 us (35%)
  Pallas kernels  28.3 us (34%)
  waiting for transfers between devices  12.8 us (16%)
  blocking collectives  11.6 us (14%)
  between operations  0.94 us (1%)
    ppermute x21, starting transfers between devices, swap(): return lax.ppermute(value, AXES, [(i, i ^ mask) for i in range(32)])  28.6 us
    ppermute x21, waiting for transfers between devices, swap(): return lax.ppermute(value, AXES, [(i, i ^ mask) for i in range(32)])  12.8 us
    all_to_all x1, blocking collectives, by_columns(): squares = lax.all_to_all(after(sums, left_other), AXES, 0, 0, tiled=True)  11.6 us
    pallas_call x2, Pallas kernels, build(): pl.pallas_call(functools.partial(build_kernel, rel), in_specs=[whole()] *...  9.67 us
    pallas_call x4, Pallas kernels, forward_part(): pl.pallas_call(functools.partial(forward_kernel, blocks, before is not No...  7.11 us
    pallas_call x5, Pallas kernels, backward_part(): pl.pallas_call(functools.partial(backward_kernel, first, blocks, tuple(ex...  5.23 us
    pallas_call x2, Pallas kernels, product_half(): pl.pallas_call(functools.partial(product_kernel, blocks), in_specs=[whole...  2.64 us
  transfers between devices with their start and end apart: 21, of which 8 were waited for; matrix products, arithmetic and copies ran while one was open for 0% of the time, Pallas kernels for 28%

profile of v13, /device:TPU:0, one launch (start us, length us, event | category | flops | bytes accessed | tf_op | source)
XLA Modules:
  0.0 82.3 jit_solution(18271571662721421425)
XLA Ops:
  0.6 1.6 %prepare.1 = (f32[64,256]{1,0:T(8,128)S(1)}, f32[128,256]{1,0:T(8,128)S(1)}, f32[128,256]{1,0:T(8,128)S(1)}, f32[128,256]{1,0:T(8,128)S(1)}, f32[128,256]{1,0:T(8,128)S(1)}) custom-call(s32[16,512]{1,0:T(8,128)} %bitcast.13, bf16[16,512]{1,0:T(8,128)(2,1)} %bitcast.14, f32[256,256]{1,0:T(8,128)} %right.1, f32[512,256]{1,0:T(8,128)} %left_hbm.1), custom_call_target="tpu_custom_call" | custom-call | bytes 16384 | tf_op jit(solution)/shard_map/prepare/pallas_call | solution.py:74
  2.3 4.1 %collective-permute-start.1 = (f32[64,256]{1,0:T(8,128)S(1)}, f32[64,256]{1,0:T(8,128)S(1)}, u32[]{:S(2)}, u32[]{:S(2)}) collective-permute-start(f32[64,256]{1,0:T(8,128)S(1)} %get-tuple-element.44.e0), channel_id=1, source_target_pairs={{0,16},{1,17},{2,18},{3,19},{4,20},{5,21},{6,22},{7,23},{8,24},{9,... | collective-permute-start | bytes 196616 | tf_op jit(solution)/shard_map/ppermute | solution.py:419
  6.4 1.4 %collective-permute-start.2 = (f32[64,256]{1,0:T(8,128)S(1)}, f32[64,256]{1,0:T(8,128)S(1)}, u32[]{:S(2)}, u32[]{:S(2)}) collective-permute-start(f32[64,256]{1,0:T(8,128)S(1)} %get-tuple-element.44.e0), channel_id=1, source_target_pairs={{0,24},{1,25},{2,26},{3,27},{4,28},{5,29},{6,30},{7,31},{8,16},{9,... | collective-permute-start | bytes 196616 | tf_op jit(solution)/shard_map/ppermute | solution.py:419
  7.7 0.2 collective-permute-start
  8.0 2.8 %collective-permute-start.4 = (f32[128,256]{1,0:T(8,128)S(1)}, f32[128,256]{1,0:T(8,128)S(1)}, u32[]{:S(2)}, u32[]{:S(2)}) collective-permute-start(f32[128,256]{1,0:T(8,128)S(1)} %get-tuple-element.50), channel_id=1, source_target_pairs={{0,16},{1,17},{2,18},{3,19},{4,20},{5,21},{6,22},{7,23},{8,24},{9,... | collective-permute-start | bytes 393224 | tf_op jit(solution)/shard_map/ppermute | solution.py:419
  10.8 1.4 %collective-permute-start.5 = (f32[128,256]{1,0:T(8,128)S(1)}, f32[128,256]{1,0:T(8,128)S(1)}, u32[]{:S(2)}, u32[]{:S(2)}) collective-permute-start(f32[128,256]{1,0:T(8,128)S(1)} %get-tuple-element.51), channel_id=1, source_target_pairs={{0,24},{1,25},{2,26},{3,27},{4,28},{5,29},{6,30},{7,31},{8,16},{9,... | collective-permute-start | bytes 393224 | tf_op jit(solution)/shard_map/ppermute | solution.py:419
  12.1 0.6 collective-permute-start.3
  12.7 0.5 collective-permute-done.2.e3
  13.3 4.7 %dense_rows.2 = (bf16[16,1024,256]{2,1,0:T(8,128)(2,1)S(1)}, bf16[16,1024,256]{2,1,0:T(8,128)(2,1)S(1)}, f32[8,128]{1,0:T(8,128)S(1)}) custom-call(f32[64,256]{1,0:T(8,128)S(1)} %get-tuple-element.44.e0, f32[64,256]{1,0:T(8,128)S(1)} %collective-permute-done.e1, f32[64,256]{1,0:T(8,128)S(1)} %collective-permute-done.1.e2, ...), custom_call_target="tpu_custom_call" | custom-call | flops 2147483648 | bytes 16777216 | tf_op jit(solution)/shard_map/dense_rows/pallas_call | solution.py:154
  18.0 3.6 %collective-permute-done.4.m2.refs_2_ = f32[128,256]{1,0:T(8,128)S(1)} collective-permute-done((f32[128,256]{1,0:T(8,128)S(1)}, f32[128,256]{1,0:T(8,128)S(1)}, u32[]{:S(2)}, u32[]{:S(2)}) %collective-permute-start.4) | collective-permute-done | bytes 131104 | tf_op jit(solution)/shard_map/ppermute | solution.py:419
  21.7 0.1 collective-permute-done.3.m1.refs_1_
  21.8 0.1 collective-permute-start.7
  21.9 1.8 %collective-permute-start.6 = (f32[4,64,256]{2,1,0:T(8,128)S(1)}, f32[4,64,256]{2,1,0:T(8,128)S(1)}, u32[]{:S(2)}, u32[]{:S(2)}) collective-permute-start(f32[4,64,256]{2,1,0:T(8,128)S(1)} %stack_right.1.refs_0_.right), channel_id=1, source_target_pairs={{0,4},{1,5},{2,6},{3,7},{4,0},{5,1},{6,2},{7,3},{8,12},{9,13},{10,... | collective-permute-start | bytes 786440 | tf_op jit(solution)/shard_map/ppermute | solution.py:419
  23.6 4.9 %dense_rows.3 = (bf16[16,1024,256]{2,1,0:T(8,128)(2,1)S(1)}, bf16[16,1024,256]{2,1,0:T(8,128)(2,1)S(1)}, f32[8,128]{1,0:T(8,128)S(1)}) custom-call(f32[64,256]{1,0:T(8,128)S(1)} %get-tuple-element.44.e0, f32[64,256]{1,0:T(8,128)S(1)} %collective-permute-done.e1, f32[64,256]{1,0:T(8,128)S(1)} %collective-permute-done.1.e2, ...), custom_call_target="tpu_custom_call" | custom-call | flops 33554432 | bytes 262144 | tf_op jit(solution)/shard_map/dense_rows/pallas_call | solution.py:154
  28.6 2.3 %forward_part.4.refs_1_ = f32[1024,128]{1,0:T(8,128)S(1)} custom-call(bf16[16,1024,256]{2,1,0:T(8,128)(2,1)S(1)} %get-tuple-element.45.hi_ref, bf16[16,1024,256]{2,1,0:T(8,128)(2,1)S(1)} %get-tuple-element.46.lo_ref, f32[4,64,256]{2,1,0:T(8,128)S(1)} %stack_right.1.refs_0_.right, f32[4,64,256]{2,1,0:T(8,128)S(1)} %collective-permute-done.7.refs_1_, ...), custom_call_target="tpu_custom_call" | custom-call | flops 67108864 | bytes 131072 | tf_op jit(solution)/shard_map/forward_part/pallas_call | solution.py:196
  30.9 0.2 collective-permute-start.8
  31.1 1.2 %forward_part.5.before = f32[1024,128]{1,0:T(8,128)S(1)} custom-call(bf16[16,1024,256]{2,1,0:T(8,128)(2,1)S(1)} %get-tuple-element.45.hi_ref, bf16[16,1024,256]{2,1,0:T(8,128)(2,1)S(1)} %get-tuple-element.46.lo_ref, f32[4,64,256]{2,1,0:T(8,128)S(1)} %collective-permute-done.6.refs_0_, f32[1024,128]{1,0:T(8,128)S(1)} %forward_part.4.refs_1_), custom_call_target="tpu_custom_call" | custom-call | flops 33554432 | bytes 65536 | tf_op jit(solution)/shard_map/forward_part/pallas_call | solution.py:196
  32.4 0.2 collective-permute-done.8.vec
  32.5 1.3 %product_half.2.mine = f32[64,1024]{1,0:T(8,128)S(1)} custom-call(bf16[16,1024,256]{2,1,0:T(8,128)(2,1)S(1)} %get-tuple-element.45.hi_ref, bf16[16,1024,256]{2,1,0:T(8,128)(2,1)S(1)} %get-tuple-element.46.lo_ref, f32[4,64,256]{2,1,0:T(8,128)S(1)} %collective-permute-done.8.vec, f32[1024,128]{1,0:T(8,128)S(1)} %forward_part.5.before), custom_call_target="tpu_custom_call" | custom-call | flops 33554432 | bytes 65536 | tf_op jit(solution)/shard_map/product_half/pallas_call | solution.py:228
  33.8 1.6 %collective-permute-start.10 = (f32[64,1024]{1,0:T(8,128)S(1)}, f32[64,1024]{1,0:T(8,128)S(1)}, u32[]{:S(2)}, u32[]{:S(2)}) collective-permute-start(f32[64,1024]{1,0:T(8,128)S(1)} %product_half.2.mine), channel_id=1, source_target_pairs={{0,1},{1,0},{2,3},{3,2},{4,5},{5,4},{6,7},{7,6},{8,9},{9,8},{10,11... | collective-permute-start | bytes 786440 | tf_op jit(solution)/shard_map/ppermute | solution.py:419
  35.4 2.3 %forward_part.6.refs_1_ = f32[1024,128]{1,0:T(8,128)S(1)} custom-call(bf16[16,1024,256]{2,1,0:T(8,128)(2,1)S(1)} %get-tuple-element.55.hi_ref, bf16[16,1024,256]{2,1,0:T(8,128)(2,1)S(1)} %get-tuple-element.56.lo_ref, f32[4,64,256]{2,1,0:T(8,128)S(1)} %stack_right.1.refs_0_.right, f32[4,64,256]{2,1,0:T(8,128)S(1)} %collective-permute-done.7.refs_1_), custom_call_target="tpu_custom_call" | custom-call | flops 67108864 | bytes 131072 | tf_op jit(solution)/shard_map/forward_part/pallas_call | solution.py:196
  37.7 1.2 %forward_part.7.before = f32[1024,128]{1,0:T(8,128)S(1)} custom-call(bf16[16,1024,256]{2,1,0:T(8,128)(2,1)S(1)} %get-tuple-element.55.hi_ref, bf16[16,1024,256]{2,1,0:T(8,128)(2,1)S(1)} %get-tuple-element.56.lo_ref, f32[4,64,256]{2,1,0:T(8,128)S(1)} %collective-permute-done.6.refs_0_, f32[1024,128]{1,0:T(8,128)S(1)} %forward_part.6.refs_1_), custom_call_target="tpu_custom_call" | custom-call | flops 33554432 | bytes 65536 | tf_op jit(solution)/shard_map/forward_part/pallas_call | solution.py:196
  39.0 1.3 %product_half.3.mine = f32[64,1024]{1,0:T(8,128)S(1)} custom-call(bf16[16,1024,256]{2,1,0:T(8,128)(2,1)S(1)} %get-tuple-element.55.hi_ref, bf16[16,1024,256]{2,1,0:T(8,128)(2,1)S(1)} %get-tuple-element.56.lo_ref, f32[4,64,256]{2,1,0:T(8,128)S(1)} %collective-permute-done.8.vec, f32[1024,128]{1,0:T(8,128)S(1)} %forward_part.7.before, ...), custom_call_target="tpu_custom_call" | custom-call | flops 33554432 | bytes 65536 | tf_op jit(solution)/shard_map/product_half/pallas_call | solution.py:228
  40.3 0.6 collective-permute-start.9
  40.9 1.4 %collective-permute-done.10.other = f32[64,1024]{1,0:T(8,128)S(1)} collective-permute-done((f32[64,1024]{1,0:T(8,128)S(1)}, f32[64,1024]{1,0:T(8,128)S(1)}, u32[]{:S(2)}, u32[]{:S(2)}) %collective-permute-start.10) | collective-permute-done | bytes 262176 | tf_op jit(solution)/shard_map/ppermute | solution.py:419
  42.3 0.2 left_half.2
  42.5 3.0 %collective-permute-start.12 = (f32[64,256]{1,0:T(8,128)S(1)}, f32[64,256]{1,0:T(8,128)S(1)}, u32[]{:S(2)}, u32[]{:S(2)}) collective-permute-start(f32[64,256]{1,0:T(8,128)S(1)} %get-tuple-element.62), channel_id=1, source_target_pairs={{0,8},{1,9},{2,10},{3,11},{4,12},{5,13},{6,14},{7,15},{8,0},{9,1},... | collective-permute-start | bytes 196616 | tf_op jit(solution)/shard_map/ppermute | solution.py:419
  45.5 1.8 %collective-permute-start.13 = (f32[64,256]{1,0:T(8,128)S(1)}, f32[64,256]{1,0:T(8,128)S(1)}, u32[]{:S(2)}, u32[]{:S(2)}) collective-permute-start(f32[64,256]{1,0:T(8,128)S(1)} %get-tuple-element.63), channel_id=1, source_target_pairs={{0,16},{1,17},{2,18},{3,19},{4,20},{5,21},{6,22},{7,23},{8,24},{9,... | collective-permute-start | bytes 196616 | tf_op jit(solution)/shard_map/ppermute | solution.py:419
  47.3 1.4 %collective-permute-start.14 = (f32[64,256]{1,0:T(8,128)S(1)}, f32[64,256]{1,0:T(8,128)S(1)}, u32[]{:S(2)}, u32[]{:S(2)}) collective-permute-start(f32[64,256]{1,0:T(8,128)S(1)} %get-tuple-element.64), channel_id=1, source_target_pairs={{0,24},{1,25},{2,26},{3,27},{4,28},{5,29},{6,30},{7,31},{8,16},{9,... | collective-permute-start | bytes 196616 | tf_op jit(solution)/shard_map/ppermute | solution.py:419
  48.7 2.3 %backward_part.5.refs_1_.refs_0_ = f32[1024,256]{1,0:T(8,128)S(1)} custom-call(bf16[16,1024,256]{2,1,0:T(8,128)(2,1)S(1)} %get-tuple-element.55.hi_ref, bf16[16,1024,256]{2,1,0:T(8,128)(2,1)S(1)} %get-tuple-element.56.lo_ref, bf16[128,1024]{1,0:T(8,128)(2,1)S(1)} %get-tuple-element.58.both_ref), custom_call_target="tpu_custom_call" | custom-call | flops 134217728 | bytes 262144 | tf_op jit(solution)/shard_map/backward_part/pallas_call | solution.py:309
  51.0 0.2 left_half.3
  51.2 2.3 %collective-permute-done.13.m2 = f32[64,256]{1,0:T(8,128)S(1)} collective-permute-done((f32[64,256]{1,0:T(8,128)S(1)}, f32[64,256]{1,0:T(8,128)S(1)}, u32[]{:S(2)}, u32[]{:S(2)}) %collective-permute-start.13) | collective-permute-done | bytes 65568 | tf_op jit(solution)/shard_map/ppermute | solution.py:419
  53.5 0.7 backward_part.9
  54.3 0.1 collective-permute-start.15
  54.3 0.7 backward_part.8.near
  55.1 0.8 collective-permute-done.15.far
  55.9 1.4 %collective-permute-start.16 = (f32[264,256]{1,0:T(8,128)S(1)}, f32[264,256]{1,0:T(8,128)S(1)}, u32[]{:S(2)}, u32[]{:S(2)}) collective-permute-start(f32[264,256]{1,0:T(8,128)S(1)} %get-tuple-element.65), channel_id=1, source_target_pairs={{0,4},{1,5},{2,6},{3,7},{4,0},{5,1},{6,2},{7,3},{8,12},{9,13},{10,... | collective-permute-start | bytes 811016 | tf_op jit(solution)/shard_map/ppermute | solution.py:419
  57.3 0.7 backward_part.7
  58.1 0.1 collective-permute-start.11
  58.1 1.8 %collective-permute-start.20 = (f32[4,64,256]{2,1,0:T(8,128)S(1)}, f32[4,64,256]{2,1,0:T(8,128)S(1)}, u32[]{:S(2)}, u32[]{:S(2)}) collective-permute-start(f32[4,64,256]{2,1,0:T(8,128)S(1)} %stack_left.1.refs_2_.own), channel_id=1, source_target_pairs={{0,1},{1,0},{2,3},{3,2},{4,5},{5,4},{6,7},{7,6},{8,9},{9,8},{10,11... | collective-permute-start | bytes 786440 | tf_op jit(solution)/shard_map/ppermute | solution.py:419
  60.0 0.7 backward_part.6.keep
  60.7 3.8 %collective-permute-done.16.got = f32[264,256]{1,0:T(8,128)S(1)} collective-permute-done((f32[264,256]{1,0:T(8,128)S(1)}, f32[264,256]{1,0:T(8,128)S(1)}, u32[]{:S(2)}, u32[]{:S(2)}) %collective-permute-start.16) | collective-permute-done | bytes 270368 | tf_op jit(solution)/shard_map/ppermute | solution.py:419
  64.5 0.3 right_norm.1
  64.8 1.4 %collective-permute-start.17 = (f32[64,256]{1,0:T(8,128)S(1)}, f32[64,256]{1,0:T(8,128)S(1)}, u32[]{:S(2)}, u32[]{:S(2)}) collective-permute-start(f32[64,256]{1,0:T(8,128)S(1)} %get-tuple-element.68), channel_id=1, source_target_pairs={{0,8},{1,9},{2,10},{3,11},{4,12},{5,13},{6,14},{7,15},{8,0},{9,1},... | collective-permute-start | bytes 196616 | tf_op jit(solution)/shard_map/ppermute | solution.py:419
  66.2 1.6 %collective-permute-start.18 = (f32[64,256]{1,0:T(8,128)S(1)}, f32[64,256]{1,0:T(8,128)S(1)}, u32[]{:S(2)}, u32[]{:S(2)}) collective-permute-start(f32[64,256]{1,0:T(8,128)S(1)} %get-tuple-element.69), channel_id=1, source_target_pairs={{0,16},{1,17},{2,18},{3,19},{4,20},{5,21},{6,22},{7,23},{8,24},{9,... | collective-permute-start | bytes 196616 | tf_op jit(solution)/shard_map/ppermute | solution.py:419
  67.8 1.4 %collective-permute-start.19 = (f32[64,256]{1,0:T(8,128)S(1)}, f32[64,256]{1,0:T(8,128)S(1)}, u32[]{:S(2)}, u32[]{:S(2)}) collective-permute-start(f32[64,256]{1,0:T(8,128)S(1)} %get-tuple-element.70), channel_id=1, source_target_pairs={{0,24},{1,25},{2,26},{3,27},{4,28},{5,29},{6,30},{7,31},{8,16},{9,... | collective-permute-start | bytes 196616 | tf_op jit(solution)/shard_map/ppermute | solution.py:419
  69.3 11.6 %all_to_all.5.squares = f32[32,1,128]{2,1,0:T(1,128)S(1)} all-to-all(f32[32,1,128]{2,1,0:T(1,128)S(1)} %bitcast.9), channel_id=1, replica_groups=mesh['doc'=16,'feat'=2] {'doc','feat'}, dimensions={0} | all-to-all | bytes 32768 | tf_op jit(solution)/shard_map/all_to_all | solution.py:472
  81.0 1.3 %finish.1 = (f32[512,256]{1,0:T(8,128)}, f32[256,256]{1,0:T(8,128)}, f32[256,256]{1,0:T(8,128)}, f32[256,256]{1,0:T(8,128)}, f32[1,256]{1,0:T(1,128)}, /*index=5*/f32[1,256]{1,0:T(1,128)}, f32[1,256]{1,0:T(1,128)}) custom-call(f32[64,256]{1,0:T(8,128)S(1)} %get-tuple-element.67.g0, f32[64,256]{1,0:T(8,128)S(1)} %collective-permute-done.17.g1, ...), custom_call_target="tpu_custom_call" | custom-call | flops 16384 | bytes 20480 | tf_op jit(solution)/shard_map/finish/pallas_call | solution.py:408
  (28 shorter events, 0.1 us)
Async XLA Ops:
  2.3 9.9 %collective-permute-start.1 = (f32[64,256]{1,0:T(8,128)S(1)}, f32[64,256]{1,0:T(8,128)S(1)}, u32[]{:S(2)}, u32[]{:S(2)}) collective-permute-start(f32[64,256]{1,0:T(8,128)S(1)} %get-tuple-element.44.e0), channel_id=1, source_target_pairs={{0,16},{1,17},{2,18},{3,19},{4,20},{5,21},{6,22},{7,23},{8,24},{9,... | collective-permute-start | bytes 196616 | tf_op jit(solution)/shard_map/ppermute | solution.py:419
  6.4 6.9 %collective-permute-start.2 = (f32[64,256]{1,0:T(8,128)S(1)}, f32[64,256]{1,0:T(8,128)S(1)}, u32[]{:S(2)}, u32[]{:S(2)}) collective-permute-start(f32[64,256]{1,0:T(8,128)S(1)} %get-tuple-element.44.e0), channel_id=1, source_target_pairs={{0,24},{1,25},{2,26},{3,27},{4,28},{5,29},{6,30},{7,31},{8,16},{9,... | collective-permute-start | bytes 196616 | tf_op jit(solution)/shard_map/ppermute | solution.py:419
  7.7 5.6 %collective-permute-start = (f32[64,256]{1,0:T(8,128)S(1)}, f32[64,256]{1,0:T(8,128)S(1)}, u32[]{:S(2)}, u32[]{:S(2)}) collective-permute-start(f32[64,256]{1,0:T(8,128)S(1)} %get-tuple-element.44.e0), channel_id=1, source_target_pairs={{0,8},{1,9},{2,10},{3,11},{4,12},{5,13},{6,14},{7,15},{8,0},{9,1},... | collective-permute-start | bytes 196616 | tf_op jit(solution)/shard_map/ppermute | solution.py:419
  8.0 13.7 %collective-permute-start.4 = (f32[128,256]{1,0:T(8,128)S(1)}, f32[128,256]{1,0:T(8,128)S(1)}, u32[]{:S(2)}, u32[]{:S(2)}) collective-permute-start(f32[128,256]{1,0:T(8,128)S(1)} %get-tuple-element.50), channel_id=1, source_target_pairs={{0,16},{1,17},{2,18},{3,19},{4,20},{5,21},{6,22},{7,23},{8,24},{9,... | collective-permute-start | bytes 393224 | tf_op jit(solution)/shard_map/ppermute | solution.py:419
  10.8 10.9 %collective-permute-start.5 = (f32[128,256]{1,0:T(8,128)S(1)}, f32[128,256]{1,0:T(8,128)S(1)}, u32[]{:S(2)}, u32[]{:S(2)}) collective-permute-start(f32[128,256]{1,0:T(8,128)S(1)} %get-tuple-element.51), channel_id=1, source_target_pairs={{0,24},{1,25},{2,26},{3,27},{4,28},{5,29},{6,30},{7,31},{8,16},{9,... | collective-permute-start | bytes 393224 | tf_op jit(solution)/shard_map/ppermute | solution.py:419
  12.1 9.6 %collective-permute-start.3 = (f32[128,256]{1,0:T(8,128)S(1)}, f32[128,256]{1,0:T(8,128)S(1)}, u32[]{:S(2)}, u32[]{:S(2)}) collective-permute-start(f32[128,256]{1,0:T(8,128)S(1)} %get-tuple-element.49), channel_id=1, source_target_pairs={{0,8},{1,9},{2,10},{3,11},{4,12},{5,13},{6,14},{7,15},{8,0},{9,1},... | collective-permute-start | bytes 393224 | tf_op jit(solution)/shard_map/ppermute | solution.py:419
  21.8 6.8 %collective-permute-start.7 = (f32[4,64,256]{2,1,0:T(8,128)S(1)}, f32[4,64,256]{2,1,0:T(8,128)S(1)}, u32[]{:S(2)}, u32[]{:S(2)}) collective-permute-start(f32[4,64,256]{2,1,0:T(8,128)S(1)} %stack_right.1.refs_0_.right), channel_id=1, source_target_pairs={{0,2},{1,3},{2,0},{3,1},{4,6},{5,7},{6,4},{7,5},{8,10},{9,11},{10,... | collective-permute-start | bytes 786440 | tf_op jit(solution)/shard_map/ppermute | solution.py:419
  21.9 9.0 %collective-permute-start.6 = (f32[4,64,256]{2,1,0:T(8,128)S(1)}, f32[4,64,256]{2,1,0:T(8,128)S(1)}, u32[]{:S(2)}, u32[]{:S(2)}) collective-permute-start(f32[4,64,256]{2,1,0:T(8,128)S(1)} %stack_right.1.refs_0_.right), channel_id=1, source_target_pairs={{0,4},{1,5},{2,6},{3,7},{4,0},{5,1},{6,2},{7,3},{8,12},{9,13},{10,... | collective-permute-start | bytes 786440 | tf_op jit(solution)/shard_map/ppermute | solution.py:419
  30.9 1.6 %collective-permute-start.8 = (f32[4,64,256]{2,1,0:T(8,128)S(1)}, f32[4,64,256]{2,1,0:T(8,128)S(1)}, u32[]{:S(2)}, u32[]{:S(2)}) collective-permute-start(f32[4,64,256]{2,1,0:T(8,128)S(1)} %collective-permute-done.6.refs_0_), channel_id=1, source_target_pairs={{0,2},{1,3},{2,0},{3,1},{4,6},{5,7},{6,4},{7,5},{8,10},{9,11},{10,... | collective-permute-start | bytes 786440 | tf_op jit(solution)/shard_map/ppermute | solution.py:419
  33.8 8.5 %collective-permute-start.10 = (f32[64,1024]{1,0:T(8,128)S(1)}, f32[64,1024]{1,0:T(8,128)S(1)}, u32[]{:S(2)}, u32[]{:S(2)}) collective-permute-start(f32[64,1024]{1,0:T(8,128)S(1)} %product_half.2.mine), channel_id=1, source_target_pairs={{0,1},{1,0},{2,3},{3,2},{4,5},{5,4},{6,7},{7,6},{8,9},{9,8},{10,11... | collective-permute-start | bytes 786440 | tf_op jit(solution)/shard_map/ppermute | solution.py:419
  37.7 1.3 %copy-start.3 = (f32[256]{0:T(256)S(1)}, f32[256]{0:T(256)}, u32[]{:S(2)}) copy-start(f32[256]{0:T(256)} %param.15) | copy-start | bytes 3076
  40.3 10.7 %collective-permute-start.9 = (f32[64,1024]{1,0:T(8,128)S(1)}, f32[64,1024]{1,0:T(8,128)S(1)}, u32[]{:S(2)}, u32[]{:S(2)}) collective-permute-start(f32[64,1024]{1,0:T(8,128)S(1)} %product_half.3.mine), channel_id=1, source_target_pairs={{0,1},{1,0},{2,3},{3,2},{4,5},{5,4},{6,7},{7,6},{8,9},{9,8},{10,11... | collective-permute-start | bytes 786440 | tf_op jit(solution)/shard_map/ppermute | solution.py:419
  42.5 8.7 %collective-permute-start.12 = (f32[64,256]{1,0:T(8,128)S(1)}, f32[64,256]{1,0:T(8,128)S(1)}, u32[]{:S(2)}, u32[]{:S(2)}) collective-permute-start(f32[64,256]{1,0:T(8,128)S(1)} %get-tuple-element.62), channel_id=1, source_target_pairs={{0,8},{1,9},{2,10},{3,11},{4,12},{5,13},{6,14},{7,15},{8,0},{9,1},... | collective-permute-start | bytes 196616 | tf_op jit(solution)/shard_map/ppermute | solution.py:419
  45.5 8.0 %collective-permute-start.13 = (f32[64,256]{1,0:T(8,128)S(1)}, f32[64,256]{1,0:T(8,128)S(1)}, u32[]{:S(2)}, u32[]{:S(2)}) collective-permute-start(f32[64,256]{1,0:T(8,128)S(1)} %get-tuple-element.63), channel_id=1, source_target_pairs={{0,16},{1,17},{2,18},{3,19},{4,20},{5,21},{6,22},{7,23},{8,24},{9,... | collective-permute-start | bytes 196616 | tf_op jit(solution)/shard_map/ppermute | solution.py:419
  47.3 6.2 %collective-permute-start.14 = (f32[64,256]{1,0:T(8,128)S(1)}, f32[64,256]{1,0:T(8,128)S(1)}, u32[]{:S(2)}, u32[]{:S(2)}) collective-permute-start(f32[64,256]{1,0:T(8,128)S(1)} %get-tuple-element.64), channel_id=1, source_target_pairs={{0,24},{1,25},{2,26},{3,27},{4,28},{5,29},{6,30},{7,31},{8,16},{9,... | collective-permute-start | bytes 196616 | tf_op jit(solution)/shard_map/ppermute | solution.py:419
  54.3 1.6 %collective-permute-start.15 = (f32[264,256]{1,0:T(8,128)S(1)}, f32[264,256]{1,0:T(8,128)S(1)}, u32[]{:S(2)}, u32[]{:S(2)}) collective-permute-start(f32[264,256]{1,0:T(8,128)S(1)} %backward_part.9), channel_id=1, source_target_pairs={{0,2},{1,3},{2,0},{3,1},{4,6},{5,7},{6,4},{7,5},{8,10},{9,11},{10,... | collective-permute-start | bytes 811016 | tf_op jit(solution)/shard_map/ppermute | solution.py:419
  55.9 8.6 %collective-permute-start.16 = (f32[264,256]{1,0:T(8,128)S(1)}, f32[264,256]{1,0:T(8,128)S(1)}, u32[]{:S(2)}, u32[]{:S(2)}) collective-permute-start(f32[264,256]{1,0:T(8,128)S(1)} %get-tuple-element.65), channel_id=1, source_target_pairs={{0,4},{1,5},{2,6},{3,7},{4,0},{5,1},{6,2},{7,3},{8,12},{9,13},{10,... | collective-permute-start | bytes 811016 | tf_op jit(solution)/shard_map/ppermute | solution.py:419
  58.0 22.9 %copy-start = (f32[256,256]{1,0:T(8,128)S(1)}, f32[256,256]{1,0:T(8,128)}, u32[]{:S(2)}) copy-start(f32[256,256]{1,0:T(8,128)} %right.1) | copy-start | bytes 786436
  58.0 22.9 %copy-start.1 = (f32[256,256]{1,0:T(8,128)S(1)}, f32[256,256]{1,0:T(8,128)}, u32[]{:S(2)}) copy-start(f32[256,256]{1,0:T(8,128)} %search.1) | copy-start | bytes 786436
  58.0 22.9 %copy-start.2 = (f32[256,256]{1,0:T(8,128)S(1)}, f32[256,256]{1,0:T(8,128)}, u32[]{:S(2)}) copy-start(f32[256,256]{1,0:T(8,128)} %solution.1) | copy-start | bytes 786436
  58.0 22.9 %copy-start.4 = (f32[256]{0:T(256)S(1)}, f32[256]{0:T(256)}, u32[]{:S(2)}) copy-start(f32[256]{0:T(256)} %param.16) | copy-start | bytes 3076
  58.1 22.9 %copy-start.5 = (f32[256]{0:T(256)S(1)}, f32[256]{0:T(256)}, u32[]{:S(2)}) copy-start(f32[256]{0:T(256)} %param.17) | copy-start | bytes 3076
  58.1 2.6 %collective-permute-start.11 = (f32[256,256]{1,0:T(8,128)S(1)}, f32[256,256]{1,0:T(8,128)S(1)}, u32[]{:S(2)}, u32[]{:S(2)}) collective-permute-start(f32[256,256]{1,0:T(8,128)S(1)} %backward_part.7), channel_id=1, source_target_pairs={{0,2},{1,3},{2,0},{3,1},{4,6},{5,7},{6,4},{7,5},{8,10},{9,11},{10,... | collective-permute-start | bytes 786440 | tf_op jit(solution)/shard_map/ppermute | solution.py:419
  58.1 11.1 %collective-permute-start.20 = (f32[4,64,256]{2,1,0:T(8,128)S(1)}, f32[4,64,256]{2,1,0:T(8,128)S(1)}, u32[]{:S(2)}, u32[]{:S(2)}) collective-permute-start(f32[4,64,256]{2,1,0:T(8,128)S(1)} %stack_left.1.refs_2_.own), channel_id=1, source_target_pairs={{0,1},{1,0},{2,3},{3,2},{4,5},{5,4},{6,7},{7,6},{8,9},{9,8},{10,11... | collective-permute-start | bytes 786440 | tf_op jit(solution)/shard_map/ppermute | solution.py:419
  64.8 16.1 %collective-permute-start.17 = (f32[64,256]{1,0:T(8,128)S(1)}, f32[64,256]{1,0:T(8,128)S(1)}, u32[]{:S(2)}, u32[]{:S(2)}) collective-permute-start(f32[64,256]{1,0:T(8,128)S(1)} %get-tuple-element.68), channel_id=1, source_target_pairs={{0,8},{1,9},{2,10},{3,11},{4,12},{5,13},{6,14},{7,15},{8,0},{9,1},... | collective-permute-start | bytes 196616 | tf_op jit(solution)/shard_map/ppermute | solution.py:419
  66.2 14.7 %collective-permute-start.18 = (f32[64,256]{1,0:T(8,128)S(1)}, f32[64,256]{1,0:T(8,128)S(1)}, u32[]{:S(2)}, u32[]{:S(2)}) collective-permute-start(f32[64,256]{1,0:T(8,128)S(1)} %get-tuple-element.69), channel_id=1, source_target_pairs={{0,16},{1,17},{2,18},{3,19},{4,20},{5,21},{6,22},{7,23},{8,24},{9,... | collective-permute-start | bytes 196616 | tf_op jit(solution)/shard_map/ppermute | solution.py:419
  67.8 13.1 %collective-permute-start.19 = (f32[64,256]{1,0:T(8,128)S(1)}, f32[64,256]{1,0:T(8,128)S(1)}, u32[]{:S(2)}, u32[]{:S(2)}) collective-permute-start(f32[64,256]{1,0:T(8,128)S(1)} %get-tuple-element.70), channel_id=1, source_target_pairs={{0,24},{1,25},{2,26},{3,27},{4,28},{5,29},{6,30},{7,31},{8,16},{9,... | collective-permute-start | bytes 196616 | tf_op jit(solution)/shard_map/ppermute | solution.py:419

commit v14 on v13

--- a/solution.py
+++ b/solution.py
@@ -172,13 +172,13 @@
 def add_products(hi_ref, lo_ref, vecs, blocks, total):
     for vec, first in zip(vecs, blocks):
         for pair in (0, 2):
-            lhs, rhs = [], []
+            rows, columns = [], []
             for k in (pair, pair + 1):
                 both = split_rows(vec[k])
-                lhs += [hi_ref[first + k], lo_ref[first + k]]
-                rhs += [both, both]
+                rows += [hi_ref[first + k], lo_ref[first + k]]
+                columns += [both, both]
             total[...] += lax.dot_general(
-                jnp.concatenate(lhs, axis=1), jnp.concatenate(rhs, axis=1), NT, preferred_element_type=jnp.float32
+                jnp.concatenate(columns, axis=1), jnp.concatenate(rows, axis=1), NT, preferred_element_type=jnp.float32
             )
 
 
@@ -197,7 +197,7 @@
         functools.partial(forward_kernel, blocks, before is not None),
         in_specs=[whole()] * (2 + len(vecs) + len(extra)),
         out_specs=whole(),
-        out_shape=f32(docs, 2 * q),
+        out_shape=f32(2 * q, docs),
         compiler_params=params(8),
         cost_estimate=cost(8 * docs * 256 * 256 * n, 4 * docs * 256 * n),
         name="forward_part",
@@ -208,9 +208,8 @@
     out, total, columns = refs[-3:]
     total[...] = before[...]
     add_products(hi_ref, lo_ref, (vec,), blocks, total)
-    turned = total[...].T
     q = out.shape[0]
-    product = turned[:q] + turned[q:]
+    product = total[:q, :] + total[q:, :]
     if len(refs) == 3:
         out[...] = product
         return
@@ -230,7 +229,7 @@
         in_specs=[whole()] * (4 + len(left)),
         out_specs=whole(),
         out_shape=f32(q, docs),
-        scratch_shapes=[pltpu.VMEM((docs, 2 * q), jnp.float32), pltpu.VMEM((4 * q, 128), jnp.float32)],
+        scratch_shapes=[pltpu.VMEM((2 * q, docs), jnp.float32), pltpu.VMEM((4 * q, 128), jnp.float32)],
         compiler_params=params(8),
         cost_estimate=cost(8 * docs * 256 * 256 * 4, 16 * docs * 256),
         name="product_half",

time: 82.5 us -> 82.7 us (level)
  Pallas kernels: 28.3 us -> 30 us
    pallas_call x4, Pallas kernels: 7.11 us -> 8.52 us  [forward_part(): pl.pallas_call(functools.partial(forward_kernel, blocks, before is not No...]
  transfers between devices with their start and end apart: 21 -> 21, of which waited for: 8 -> 7; matrix products, arithmetic and copies ran while one was open for 0% -> 0% of each run, Pallas kernels for 28% -> 30%
where the time goes in v14:
time: 82.7 us; the launch traced here: 82.5 us
  Pallas kernels  30 us (36%)
  starting transfers between devices  28 us (34%)
  waiting for transfers between devices  12.6 us (15%)
  blocking collectives  10.9 us (13%)
  between operations  0.96 us (1%)
    ppermute x21, starting transfers between devices, swap(): return lax.ppermute(value, AXES, [(i, i ^ mask) for i in range(32)])  28 us
    ppermute x21, waiting for transfers between devices, swap(): return lax.ppermute(value, AXES, [(i, i ^ mask) for i in range(32)])  12.6 us
    all_to_all x1, blocking collectives, by_columns(): squares = lax.all_to_all(after(sums, left_other), AXES, 0, 0, tiled=True)  10.9 us
    pallas_call x2, Pallas kernels, build(): pl.pallas_call(functools.partial(build_kernel, rel), in_specs=[whole()] *...  9.67 us
    pallas_call x4, Pallas kernels, forward_part(): pl.pallas_call(functools.partial(forward_kernel, blocks, before is not No...  8.52 us
    pallas_call x5, Pallas kernels, backward_part(): pl.pallas_call(functools.partial(backward_kernel, first, blocks, tuple(ex...  5.23 us
    pallas_call x2, Pallas kernels, product_half(): pl.pallas_call(functools.partial(product_kernel, blocks), in_specs=[whole...  2.94 us
  transfers between devices with their start and end apart: 21, of which 7 were waited for; matrix products, arithmetic and copies ran while one was open for 0% of the time, Pallas kernels for 30%

profile of v14, /device:TPU:0, one launch (start us, length us, event | category | flops | bytes accessed | tf_op | source)
XLA Modules:
  0.0 82.5 jit_solution(14821930905364589135)
XLA Ops:
  0.6 1.6 %prepare.1 = (f32[64,256]{1,0:T(8,128)S(1)}, f32[128,256]{1,0:T(8,128)S(1)}, f32[128,256]{1,0:T(8,128)S(1)}, f32[128,256]{1,0:T(8,128)S(1)}, f32[128,256]{1,0:T(8,128)S(1)}) custom-call(s32[16,512]{1,0:T(8,128)} %bitcast.13, bf16[16,512]{1,0:T(8,128)(2,1)} %bitcast.14, f32[256,256]{1,0:T(8,128)} %right.1, f32[512,256]{1,0:T(8,128)} %left_hbm.1), custom_call_target="tpu_custom_call" | custom-call | bytes 16384 | tf_op jit(solution)/shard_map/prepare/pallas_call | solution.py:74
  2.3 4.1 %collective-permute-start.1 = (f32[64,256]{1,0:T(8,128)S(1)}, f32[64,256]{1,0:T(8,128)S(1)}, u32[]{:S(2)}, u32[]{:S(2)}) collective-permute-start(f32[64,256]{1,0:T(8,128)S(1)} %get-tuple-element.44.e0), channel_id=1, source_target_pairs={{0,16},{1,17},{2,18},{3,19},{4,20},{5,21},{6,22},{7,23},{8,24},{9,... | collective-permute-start | bytes 196616 | tf_op jit(solution)/shard_map/ppermute | solution.py:418
  6.4 1.4 %collective-permute-start.2 = (f32[64,256]{1,0:T(8,128)S(1)}, f32[64,256]{1,0:T(8,128)S(1)}, u32[]{:S(2)}, u32[]{:S(2)}) collective-permute-start(f32[64,256]{1,0:T(8,128)S(1)} %get-tuple-element.44.e0), channel_id=1, source_target_pairs={{0,24},{1,25},{2,26},{3,27},{4,28},{5,29},{6,30},{7,31},{8,16},{9,... | collective-permute-start | bytes 196616 | tf_op jit(solution)/shard_map/ppermute | solution.py:418
  7.7 0.2 collective-permute-start
  8.0 2.8 %collective-permute-start.4 = (f32[128,256]{1,0:T(8,128)S(1)}, f32[128,256]{1,0:T(8,128)S(1)}, u32[]{:S(2)}, u32[]{:S(2)}) collective-permute-start(f32[128,256]{1,0:T(8,128)S(1)} %get-tuple-element.50), channel_id=1, source_target_pairs={{0,16},{1,17},{2,18},{3,19},{4,20},{5,21},{6,22},{7,23},{8,24},{9,... | collective-permute-start | bytes 393224 | tf_op jit(solution)/shard_map/ppermute | solution.py:418
  10.8 1.4 %collective-permute-start.5 = (f32[128,256]{1,0:T(8,128)S(1)}, f32[128,256]{1,0:T(8,128)S(1)}, u32[]{:S(2)}, u32[]{:S(2)}) collective-permute-start(f32[128,256]{1,0:T(8,128)S(1)} %get-tuple-element.51), channel_id=1, source_target_pairs={{0,24},{1,25},{2,26},{3,27},{4,28},{5,29},{6,30},{7,31},{8,16},{9,... | collective-permute-start | bytes 393224 | tf_op jit(solution)/shard_map/ppermute | solution.py:418
  12.1 0.6 collective-permute-start.3
  12.7 0.5 collective-permute-done.2.e3
  13.3 4.7 %dense_rows.2 = (bf16[16,1024,256]{2,1,0:T(8,128)(2,1)S(1)}, bf16[16,1024,256]{2,1,0:T(8,128)(2,1)S(1)}, f32[8,128]{1,0:T(8,128)S(1)}) custom-call(f32[64,256]{1,0:T(8,128)S(1)} %get-tuple-element.44.e0, f32[64,256]{1,0:T(8,128)S(1)} %collective-permute-done.e1, f32[64,256]{1,0:T(8,128)S(1)} %collective-permute-done.1.e2, ...), custom_call_target="tpu_custom_call" | custom-call | flops 2147483648 | bytes 16777216 | tf_op jit(solution)/shard_map/dense_rows/pallas_call | solution.py:154
  18.0 3.6 %collective-permute-done.4.m2.refs_2_ = f32[128,256]{1,0:T(8,128)S(1)} collective-permute-done((f32[128,256]{1,0:T(8,128)S(1)}, f32[128,256]{1,0:T(8,128)S(1)}, u32[]{:S(2)}, u32[]{:S(2)}) %collective-permute-start.4) | collective-permute-done | bytes 131104 | tf_op jit(solution)/shard_map/ppermute | solution.py:418
  21.7 0.1 collective-permute-done.3.m1.refs_1_
  21.8 0.1 collective-permute-start.7
  21.9 1.8 %collective-permute-start.6 = (f32[4,64,256]{2,1,0:T(8,128)S(1)}, f32[4,64,256]{2,1,0:T(8,128)S(1)}, u32[]{:S(2)}, u32[]{:S(2)}) collective-permute-start(f32[4,64,256]{2,1,0:T(8,128)S(1)} %stack_right.1.refs_0_.right), channel_id=1, source_target_pairs={{0,4},{1,5},{2,6},{3,7},{4,0},{5,1},{6,2},{7,3},{8,12},{9,13},{10,... | collective-permute-start | bytes 786440 | tf_op jit(solution)/shard_map/ppermute | solution.py:418
  23.6 4.9 %dense_rows.3 = (bf16[16,1024,256]{2,1,0:T(8,128)(2,1)S(1)}, bf16[16,1024,256]{2,1,0:T(8,128)(2,1)S(1)}, f32[8,128]{1,0:T(8,128)S(1)}) custom-call(f32[64,256]{1,0:T(8,128)S(1)} %get-tuple-element.44.e0, f32[64,256]{1,0:T(8,128)S(1)} %collective-permute-done.e1, f32[64,256]{1,0:T(8,128)S(1)} %collective-permute-done.1.e2, ...), custom_call_target="tpu_custom_call" | custom-call | flops 33554432 | bytes 262144 | tf_op jit(solution)/shard_map/dense_rows/pallas_call | solution.py:154
  28.6 2.8 %forward_part.4.refs_1_ = f32[128,1024]{1,0:T(8,128)S(1)} custom-call(bf16[16,1024,256]{2,1,0:T(8,128)(2,1)S(1)} %get-tuple-element.45.hi_ref, bf16[16,1024,256]{2,1,0:T(8,128)(2,1)S(1)} %get-tuple-element.46.lo_ref, f32[4,64,256]{2,1,0:T(8,128)S(1)} %stack_right.1.refs_0_.right, f32[4,64,256]{2,1,0:T(8,128)S(1)} %collective-permute-done.7.refs_1_, ...), custom_call_target="tpu_custom_call" | custom-call | flops 67108864 | bytes 131072 | tf_op jit(solution)/shard_map/forward_part/pallas_call | solution.py:196
  31.4 0.2 collective-permute-start.8
  31.6 1.5 %forward_part.5.before = f32[128,1024]{1,0:T(8,128)S(1)} custom-call(bf16[16,1024,256]{2,1,0:T(8,128)(2,1)S(1)} %get-tuple-element.45.hi_ref, bf16[16,1024,256]{2,1,0:T(8,128)(2,1)S(1)} %get-tuple-element.46.lo_ref, f32[4,64,256]{2,1,0:T(8,128)S(1)} %collective-permute-done.6.refs_0_, f32[128,1024]{1,0:T(8,128)S(1)} %forward_part.4.refs_1_), custom_call_target="tpu_custom_call" | custom-call | flops 33554432 | bytes 65536 | tf_op jit(solution)/shard_map/forward_part/pallas_call | solution.py:196
  33.1 1.5 %product_half.2.mine = f32[64,1024]{1,0:T(8,128)S(1)} custom-call(bf16[16,1024,256]{2,1,0:T(8,128)(2,1)S(1)} %get-tuple-element.45.hi_ref, bf16[16,1024,256]{2,1,0:T(8,128)(2,1)S(1)} %get-tuple-element.46.lo_ref, f32[4,64,256]{2,1,0:T(8,128)S(1)} %collective-permute-done.8.vec, f32[128,1024]{1,0:T(8,128)S(1)} %forward_part.5.before), custom_call_target="tpu_custom_call" | custom-call | flops 33554432 | bytes 65536 | tf_op jit(solution)/shard_map/product_half/pallas_call | solution.py:227
  34.5 1.6 %collective-permute-start.10 = (f32[64,1024]{1,0:T(8,128)S(1)}, f32[64,1024]{1,0:T(8,128)S(1)}, u32[]{:S(2)}, u32[]{:S(2)}) collective-permute-start(f32[64,1024]{1,0:T(8,128)S(1)} %product_half.2.mine), channel_id=1, source_target_pairs={{0,1},{1,0},{2,3},{3,2},{4,5},{5,4},{6,7},{7,6},{8,9},{9,8},{10,11... | collective-permute-start | bytes 786440 | tf_op jit(solution)/shard_map/ppermute | solution.py:418
  36.1 2.8 %forward_part.6.refs_1_ = f32[128,1024]{1,0:T(8,128)S(1)} custom-call(bf16[16,1024,256]{2,1,0:T(8,128)(2,1)S(1)} %get-tuple-element.55.hi_ref, bf16[16,1024,256]{2,1,0:T(8,128)(2,1)S(1)} %get-tuple-element.56.lo_ref, f32[4,64,256]{2,1,0:T(8,128)S(1)} %stack_right.1.refs_0_.right, f32[4,64,256]{2,1,0:T(8,128)S(1)} %collective-permute-done.7.refs_1_), custom_call_target="tpu_custom_call" | custom-call | flops 67108864 | bytes 131072 | tf_op jit(solution)/shard_map/forward_part/pallas_call | solution.py:196
  38.9 0.0 copy-start.3
  38.9 1.5 %forward_part.7.before = f32[128,1024]{1,0:T(8,128)S(1)} custom-call(bf16[16,1024,256]{2,1,0:T(8,128)(2,1)S(1)} %get-tuple-element.55.hi_ref, bf16[16,1024,256]{2,1,0:T(8,128)(2,1)S(1)} %get-tuple-element.56.lo_ref, f32[4,64,256]{2,1,0:T(8,128)S(1)} %collective-permute-done.6.refs_0_, f32[128,1024]{1,0:T(8,128)S(1)} %forward_part.6.refs_1_), custom_call_target="tpu_custom_call" | custom-call | flops 33554432 | bytes 65536 | tf_op jit(solution)/shard_map/forward_part/pallas_call | solution.py:196
  40.4 1.5 %product_half.3.mine = f32[64,1024]{1,0:T(8,128)S(1)} custom-call(bf16[16,1024,256]{2,1,0:T(8,128)(2,1)S(1)} %get-tuple-element.55.hi_ref, bf16[16,1024,256]{2,1,0:T(8,128)(2,1)S(1)} %get-tuple-element.56.lo_ref, f32[4,64,256]{2,1,0:T(8,128)S(1)} %collective-permute-done.8.vec, f32[128,1024]{1,0:T(8,128)S(1)} %forward_part.7.before, ...), custom_call_target="tpu_custom_call" | custom-call | flops 33554432 | bytes 65536 | tf_op jit(solution)/shard_map/product_half/pallas_call | solution.py:227
  41.9 0.6 collective-permute-start.9
  42.5 0.7 collective-permute-done.10.other
  43.2 0.2 left_half.2
  43.3 3.0 %collective-permute-start.12 = (f32[64,256]{1,0:T(8,128)S(1)}, f32[64,256]{1,0:T(8,128)S(1)}, u32[]{:S(2)}, u32[]{:S(2)}) collective-permute-start(f32[64,256]{1,0:T(8,128)S(1)} %get-tuple-element.62), channel_id=1, source_target_pairs={{0,8},{1,9},{2,10},{3,11},{4,12},{5,13},{6,14},{7,15},{8,0},{9,1},... | collective-permute-start | bytes 196616 | tf_op jit(solution)/shard_map/ppermute | solution.py:418
  46.3 1.8 %collective-permute-start.13 = (f32[64,256]{1,0:T(8,128)S(1)}, f32[64,256]{1,0:T(8,128)S(1)}, u32[]{:S(2)}, u32[]{:S(2)}) collective-permute-start(f32[64,256]{1,0:T(8,128)S(1)} %get-tuple-element.63), channel_id=1, source_target_pairs={{0,16},{1,17},{2,18},{3,19},{4,20},{5,21},{6,22},{7,23},{8,24},{9,... | collective-permute-start | bytes 196616 | tf_op jit(solution)/shard_map/ppermute | solution.py:418
  48.1 1.4 %collective-permute-start.14 = (f32[64,256]{1,0:T(8,128)S(1)}, f32[64,256]{1,0:T(8,128)S(1)}, u32[]{:S(2)}, u32[]{:S(2)}) collective-permute-start(f32[64,256]{1,0:T(8,128)S(1)} %get-tuple-element.64), channel_id=1, source_target_pairs={{0,24},{1,25},{2,26},{3,27},{4,28},{5,29},{6,30},{7,31},{8,16},{9,... | collective-permute-start | bytes 196616 | tf_op jit(solution)/shard_map/ppermute | solution.py:418
  49.5 2.3 %backward_part.5.refs_1_.refs_0_ = f32[1024,256]{1,0:T(8,128)S(1)} custom-call(bf16[16,1024,256]{2,1,0:T(8,128)(2,1)S(1)} %get-tuple-element.55.hi_ref, bf16[16,1024,256]{2,1,0:T(8,128)(2,1)S(1)} %get-tuple-element.56.lo_ref, bf16[128,1024]{1,0:T(8,128)(2,1)S(1)} %get-tuple-element.58.both_ref), custom_call_target="tpu_custom_call" | custom-call | flops 134217728 | bytes 262144 | tf_op jit(solution)/shard_map/backward_part/pallas_call | solution.py:308
  51.9 0.2 left_half.3
  52.0 2.4 %collective-permute-done.13.m2 = f32[64,256]{1,0:T(8,128)S(1)} collective-permute-done((f32[64,256]{1,0:T(8,128)S(1)}, f32[64,256]{1,0:T(8,128)S(1)}, u32[]{:S(2)}, u32[]{:S(2)}) %collective-permute-start.13) | collective-permute-done | bytes 65568 | tf_op jit(solution)/shard_map/ppermute | solution.py:418
  54.5 0.7 backward_part.9
  55.2 0.1 collective-permute-start.15
  55.3 0.7 backward_part.8.near
  56.1 0.8 collective-permute-done.15.far
  56.9 1.0 %collective-permute-start.16 = (f32[264,256]{1,0:T(8,128)S(1)}, f32[264,256]{1,0:T(8,128)S(1)}, u32[]{:S(2)}, u32[]{:S(2)}) collective-permute-start(f32[264,256]{1,0:T(8,128)S(1)} %get-tuple-element.65), channel_id=1, source_target_pairs={{0,4},{1,5},{2,6},{3,7},{4,0},{5,1},{6,2},{7,3},{8,12},{9,13},{10,... | collective-permute-start | bytes 811016 | tf_op jit(solution)/shard_map/ppermute | solution.py:418
  57.9 0.7 backward_part.7
  58.7 0.1 collective-permute-start.11
  58.8 1.6 %collective-permute-start.20 = (f32[4,64,256]{2,1,0:T(8,128)S(1)}, f32[4,64,256]{2,1,0:T(8,128)S(1)}, u32[]{:S(2)}, u32[]{:S(2)}) collective-permute-start(f32[4,64,256]{2,1,0:T(8,128)S(1)} %stack_left.1.refs_2_.own), channel_id=1, source_target_pairs={{0,1},{1,0},{2,3},{3,2},{4,5},{5,4},{6,7},{7,6},{8,9},{9,8},{10,11... | collective-permute-start | bytes 786440 | tf_op jit(solution)/shard_map/ppermute | solution.py:418
  60.3 0.7 backward_part.6.keep
  61.1 4.4 %collective-permute-done.16.got = f32[264,256]{1,0:T(8,128)S(1)} collective-permute-done((f32[264,256]{1,0:T(8,128)S(1)}, f32[264,256]{1,0:T(8,128)S(1)}, u32[]{:S(2)}, u32[]{:S(2)}) %collective-permute-start.16) | collective-permute-done | bytes 270368 | tf_op jit(solution)/shard_map/ppermute | solution.py:418
  65.5 0.3 right_norm.1
  65.8 1.4 %collective-permute-start.17 = (f32[64,256]{1,0:T(8,128)S(1)}, f32[64,256]{1,0:T(8,128)S(1)}, u32[]{:S(2)}, u32[]{:S(2)}) collective-permute-start(f32[64,256]{1,0:T(8,128)S(1)} %get-tuple-element.68), channel_id=1, source_target_pairs={{0,8},{1,9},{2,10},{3,11},{4,12},{5,13},{6,14},{7,15},{8,0},{9,1},... | collective-permute-start | bytes 196616 | tf_op jit(solution)/shard_map/ppermute | solution.py:418
  67.2 1.4 %collective-permute-start.18 = (f32[64,256]{1,0:T(8,128)S(1)}, f32[64,256]{1,0:T(8,128)S(1)}, u32[]{:S(2)}, u32[]{:S(2)}) collective-permute-start(f32[64,256]{1,0:T(8,128)S(1)} %get-tuple-element.69), channel_id=1, source_target_pairs={{0,16},{1,17},{2,18},{3,19},{4,20},{5,21},{6,22},{7,23},{8,24},{9,... | collective-permute-start | bytes 196616 | tf_op jit(solution)/shard_map/ppermute | solution.py:418
  68.6 1.6 %collective-permute-start.19 = (f32[64,256]{1,0:T(8,128)S(1)}, f32[64,256]{1,0:T(8,128)S(1)}, u32[]{:S(2)}, u32[]{:S(2)}) collective-permute-start(f32[64,256]{1,0:T(8,128)S(1)} %get-tuple-element.70), channel_id=1, source_target_pairs={{0,24},{1,25},{2,26},{3,27},{4,28},{5,29},{6,30},{7,31},{8,16},{9,... | collective-permute-start | bytes 196616 | tf_op jit(solution)/shard_map/ppermute | solution.py:418
  70.3 10.9 %all_to_all.5.squares = f32[32,1,128]{2,1,0:T(1,128)S(1)} all-to-all(f32[32,1,128]{2,1,0:T(1,128)S(1)} %bitcast.9), channel_id=1, replica_groups=mesh['doc'=16,'feat'=2] {'doc','feat'}, dimensions={0} | all-to-all | bytes 32768 | tf_op jit(solution)/shard_map/all_to_all | solution.py:471
  81.2 1.3 %finish.1 = (f32[512,256]{1,0:T(8,128)}, f32[256,256]{1,0:T(8,128)}, f32[256,256]{1,0:T(8,128)}, f32[256,256]{1,0:T(8,128)}, f32[1,256]{1,0:T(1,128)}, /*index=5*/f32[1,256]{1,0:T(1,128)}, f32[1,256]{1,0:T(1,128)}) custom-call(f32[64,256]{1,0:T(8,128)S(1)} %get-tuple-element.67.g0, f32[64,256]{1,0:T(8,128)S(1)} %collective-permute-done.17.g1, ...), custom_call_target="tpu_custom_call" | custom-call | flops 16384 | bytes 20480 | tf_op jit(solution)/shard_map/finish/pallas_call | solution.py:407
  (28 shorter events, 0.1 us)
Async XLA Ops:
  2.3 9.9 %collective-permute-start.1 = (f32[64,256]{1,0:T(8,128)S(1)}, f32[64,256]{1,0:T(8,128)S(1)}, u32[]{:S(2)}, u32[]{:S(2)}) collective-permute-start(f32[64,256]{1,0:T(8,128)S(1)} %get-tuple-element.44.e0), channel_id=1, source_target_pairs={{0,16},{1,17},{2,18},{3,19},{4,20},{5,21},{6,22},{7,23},{8,24},{9,... | collective-permute-start | bytes 196616 | tf_op jit(solution)/shard_map/ppermute | solution.py:418
  6.4 6.9 %collective-permute-start.2 = (f32[64,256]{1,0:T(8,128)S(1)}, f32[64,256]{1,0:T(8,128)S(1)}, u32[]{:S(2)}, u32[]{:S(2)}) collective-permute-start(f32[64,256]{1,0:T(8,128)S(1)} %get-tuple-element.44.e0), channel_id=1, source_target_pairs={{0,24},{1,25},{2,26},{3,27},{4,28},{5,29},{6,30},{7,31},{8,16},{9,... | collective-permute-start | bytes 196616 | tf_op jit(solution)/shard_map/ppermute | solution.py:418
  7.7 5.6 %collective-permute-start = (f32[64,256]{1,0:T(8,128)S(1)}, f32[64,256]{1,0:T(8,128)S(1)}, u32[]{:S(2)}, u32[]{:S(2)}) collective-permute-start(f32[64,256]{1,0:T(8,128)S(1)} %get-tuple-element.44.e0), channel_id=1, source_target_pairs={{0,8},{1,9},{2,10},{3,11},{4,12},{5,13},{6,14},{7,15},{8,0},{9,1},... | collective-permute-start | bytes 196616 | tf_op jit(solution)/shard_map/ppermute | solution.py:418
  8.0 13.7 %collective-permute-start.4 = (f32[128,256]{1,0:T(8,128)S(1)}, f32[128,256]{1,0:T(8,128)S(1)}, u32[]{:S(2)}, u32[]{:S(2)}) collective-permute-start(f32[128,256]{1,0:T(8,128)S(1)} %get-tuple-element.50), channel_id=1, source_target_pairs={{0,16},{1,17},{2,18},{3,19},{4,20},{5,21},{6,22},{7,23},{8,24},{9,... | collective-permute-start | bytes 393224 | tf_op jit(solution)/shard_map/ppermute | solution.py:418
  10.8 10.9 %collective-permute-start.5 = (f32[128,256]{1,0:T(8,128)S(1)}, f32[128,256]{1,0:T(8,128)S(1)}, u32[]{:S(2)}, u32[]{:S(2)}) collective-permute-start(f32[128,256]{1,0:T(8,128)S(1)} %get-tuple-element.51), channel_id=1, source_target_pairs={{0,24},{1,25},{2,26},{3,27},{4,28},{5,29},{6,30},{7,31},{8,16},{9,... | collective-permute-start | bytes 393224 | tf_op jit(solution)/shard_map/ppermute | solution.py:418
  12.1 9.6 %collective-permute-start.3 = (f32[128,256]{1,0:T(8,128)S(1)}, f32[128,256]{1,0:T(8,128)S(1)}, u32[]{:S(2)}, u32[]{:S(2)}) collective-permute-start(f32[128,256]{1,0:T(8,128)S(1)} %get-tuple-element.49), channel_id=1, source_target_pairs={{0,8},{1,9},{2,10},{3,11},{4,12},{5,13},{6,14},{7,15},{8,0},{9,1},... | collective-permute-start | bytes 393224 | tf_op jit(solution)/shard_map/ppermute | solution.py:418
  21.8 6.8 %collective-permute-start.7 = (f32[4,64,256]{2,1,0:T(8,128)S(1)}, f32[4,64,256]{2,1,0:T(8,128)S(1)}, u32[]{:S(2)}, u32[]{:S(2)}) collective-permute-start(f32[4,64,256]{2,1,0:T(8,128)S(1)} %stack_right.1.refs_0_.right), channel_id=1, source_target_pairs={{0,2},{1,3},{2,0},{3,1},{4,6},{5,7},{6,4},{7,5},{8,10},{9,11},{10,... | collective-permute-start | bytes 786440 | tf_op jit(solution)/shard_map/ppermute | solution.py:418
  21.9 9.5 %collective-permute-start.6 = (f32[4,64,256]{2,1,0:T(8,128)S(1)}, f32[4,64,256]{2,1,0:T(8,128)S(1)}, u32[]{:S(2)}, u32[]{:S(2)}) collective-permute-start(f32[4,64,256]{2,1,0:T(8,128)S(1)} %stack_right.1.refs_0_.right), channel_id=1, source_target_pairs={{0,4},{1,5},{2,6},{3,7},{4,0},{5,1},{6,2},{7,3},{8,12},{9,13},{10,... | collective-permute-start | bytes 786440 | tf_op jit(solution)/shard_map/ppermute | solution.py:418
  31.4 1.7 %collective-permute-start.8 = (f32[4,64,256]{2,1,0:T(8,128)S(1)}, f32[4,64,256]{2,1,0:T(8,128)S(1)}, u32[]{:S(2)}, u32[]{:S(2)}) collective-permute-start(f32[4,64,256]{2,1,0:T(8,128)S(1)} %collective-permute-done.6.refs_0_), channel_id=1, source_target_pairs={{0,2},{1,3},{2,0},{3,1},{4,6},{5,7},{6,4},{7,5},{8,10},{9,11},{10,... | collective-permute-start | bytes 786440 | tf_op jit(solution)/shard_map/ppermute | solution.py:418
  34.5 8.7 %collective-permute-start.10 = (f32[64,1024]{1,0:T(8,128)S(1)}, f32[64,1024]{1,0:T(8,128)S(1)}, u32[]{:S(2)}, u32[]{:S(2)}) collective-permute-start(f32[64,1024]{1,0:T(8,128)S(1)} %product_half.2.mine), channel_id=1, source_target_pairs={{0,1},{1,0},{2,3},{3,2},{4,5},{5,4},{6,7},{7,6},{8,9},{9,8},{10,11... | collective-permute-start | bytes 786440 | tf_op jit(solution)/shard_map/ppermute | solution.py:418
  38.9 1.5 %copy-start.3 = (f32[256]{0:T(256)S(1)}, f32[256]{0:T(256)}, u32[]{:S(2)}) copy-start(f32[256]{0:T(256)} %param.15) | copy-start | bytes 3076
  41.9 9.9 %collective-permute-start.9 = (f32[64,1024]{1,0:T(8,128)S(1)}, f32[64,1024]{1,0:T(8,128)S(1)}, u32[]{:S(2)}, u32[]{:S(2)}) collective-permute-start(f32[64,1024]{1,0:T(8,128)S(1)} %product_half.3.mine), channel_id=1, source_target_pairs={{0,1},{1,0},{2,3},{3,2},{4,5},{5,4},{6,7},{7,6},{8,9},{9,8},{10,11... | collective-permute-start | bytes 786440 | tf_op jit(solution)/shard_map/ppermute | solution.py:418
  43.3 8.7 %collective-permute-start.12 = (f32[64,256]{1,0:T(8,128)S(1)}, f32[64,256]{1,0:T(8,128)S(1)}, u32[]{:S(2)}, u32[]{:S(2)}) collective-permute-start(f32[64,256]{1,0:T(8,128)S(1)} %get-tuple-element.62), channel_id=1, source_target_pairs={{0,8},{1,9},{2,10},{3,11},{4,12},{5,13},{6,14},{7,15},{8,0},{9,1},... | collective-permute-start | bytes 196616 | tf_op jit(solution)/shard_map/ppermute | solution.py:418
  46.3 8.2 %collective-permute-start.13 = (f32[64,256]{1,0:T(8,128)S(1)}, f32[64,256]{1,0:T(8,128)S(1)}, u32[]{:S(2)}, u32[]{:S(2)}) collective-permute-start(f32[64,256]{1,0:T(8,128)S(1)} %get-tuple-element.63), channel_id=1, source_target_pairs={{0,16},{1,17},{2,18},{3,19},{4,20},{5,21},{6,22},{7,23},{8,24},{9,... | collective-permute-start | bytes 196616 | tf_op jit(solution)/shard_map/ppermute | solution.py:418
  48.1 6.4 %collective-permute-start.14 = (f32[64,256]{1,0:T(8,128)S(1)}, f32[64,256]{1,0:T(8,128)S(1)}, u32[]{:S(2)}, u32[]{:S(2)}) collective-permute-start(f32[64,256]{1,0:T(8,128)S(1)} %get-tuple-element.64), channel_id=1, source_target_pairs={{0,24},{1,25},{2,26},{3,27},{4,28},{5,29},{6,30},{7,31},{8,16},{9,... | collective-permute-start | bytes 196616 | tf_op jit(solution)/shard_map/ppermute | solution.py:418
  55.2 1.6 %collective-permute-start.15 = (f32[264,256]{1,0:T(8,128)S(1)}, f32[264,256]{1,0:T(8,128)S(1)}, u32[]{:S(2)}, u32[]{:S(2)}) collective-permute-start(f32[264,256]{1,0:T(8,128)S(1)} %backward_part.9), channel_id=1, source_target_pairs={{0,2},{1,3},{2,0},{3,1},{4,6},{5,7},{6,4},{7,5},{8,10},{9,11},{10,... | collective-permute-start | bytes 811016 | tf_op jit(solution)/shard_map/ppermute | solution.py:418
  56.9 8.6 %collective-permute-start.16 = (f32[264,256]{1,0:T(8,128)S(1)}, f32[264,256]{1,0:T(8,128)S(1)}, u32[]{:S(2)}, u32[]{:S(2)}) collective-permute-start(f32[264,256]{1,0:T(8,128)S(1)} %get-tuple-element.65), channel_id=1, source_target_pairs={{0,4},{1,5},{2,6},{3,7},{4,0},{5,1},{6,2},{7,3},{8,12},{9,13},{10,... | collective-permute-start | bytes 811016 | tf_op jit(solution)/shard_map/ppermute | solution.py:418
  58.6 22.5 %copy-start = (f32[256,256]{1,0:T(8,128)S(1)}, f32[256,256]{1,0:T(8,128)}, u32[]{:S(2)}) copy-start(f32[256,256]{1,0:T(8,128)} %right.1) | copy-start | bytes 786436
  58.6 22.5 %copy-start.1 = (f32[256,256]{1,0:T(8,128)S(1)}, f32[256,256]{1,0:T(8,128)}, u32[]{:S(2)}) copy-start(f32[256,256]{1,0:T(8,128)} %search.1) | copy-start | bytes 786436
  58.6 22.5 %copy-start.2 = (f32[256,256]{1,0:T(8,128)S(1)}, f32[256,256]{1,0:T(8,128)}, u32[]{:S(2)}) copy-start(f32[256,256]{1,0:T(8,128)} %solution.1) | copy-start | bytes 786436
  58.7 22.5 %copy-start.4 = (f32[256]{0:T(256)S(1)}, f32[256]{0:T(256)}, u32[]{:S(2)}) copy-start(f32[256]{0:T(256)} %param.16) | copy-start | bytes 3076
  58.7 22.5 %copy-start.5 = (f32[256]{0:T(256)S(1)}, f32[256]{0:T(256)}, u32[]{:S(2)}) copy-start(f32[256]{0:T(256)} %param.17) | copy-start | bytes 3076
  58.7 2.4 %collective-permute-start.11 = (f32[256,256]{1,0:T(8,128)S(1)}, f32[256,256]{1,0:T(8,128)S(1)}, u32[]{:S(2)}, u32[]{:S(2)}) collective-permute-start(f32[256,256]{1,0:T(8,128)S(1)} %backward_part.7), channel_id=1, source_target_pairs={{0,2},{1,3},{2,0},{3,1},{4,6},{5,7},{6,4},{7,5},{8,10},{9,11},{10,... | collective-permute-start | bytes 786440 | tf_op jit(solution)/shard_map/ppermute | solution.py:418
  58.8 11.5 %collective-permute-start.20 = (f32[4,64,256]{2,1,0:T(8,128)S(1)}, f32[4,64,256]{2,1,0:T(8,128)S(1)}, u32[]{:S(2)}, u32[]{:S(2)}) collective-permute-start(f32[4,64,256]{2,1,0:T(8,128)S(1)} %stack_left.1.refs_2_.own), channel_id=1, source_target_pairs={{0,1},{1,0},{2,3},{3,2},{4,5},{5,4},{6,7},{7,6},{8,9},{9,8},{10,11... | collective-permute-start | bytes 786440 | tf_op jit(solution)/shard_map/ppermute | solution.py:418
  65.8 15.3 %collective-permute-start.17 = (f32[64,256]{1,0:T(8,128)S(1)}, f32[64,256]{1,0:T(8,128)S(1)}, u32[]{:S(2)}, u32[]{:S(2)}) collective-permute-start(f32[64,256]{1,0:T(8,128)S(1)} %get-tuple-element.68), channel_id=1, source_target_pairs={{0,8},{1,9},{2,10},{3,11},{4,12},{5,13},{6,14},{7,15},{8,0},{9,1},... | collective-permute-start | bytes 196616 | tf_op jit(solution)/shard_map/ppermute | solution.py:418
  67.2 13.9 %collective-permute-start.18 = (f32[64,256]{1,0:T(8,128)S(1)}, f32[64,256]{1,0:T(8,128)S(1)}, u32[]{:S(2)}, u32[]{:S(2)}) collective-permute-start(f32[64,256]{1,0:T(8,128)S(1)} %get-tuple-element.69), channel_id=1, source_target_pairs={{0,16},{1,17},{2,18},{3,19},{4,20},{5,21},{6,22},{7,23},{8,24},{9,... | collective-permute-start | bytes 196616 | tf_op jit(solution)/shard_map/ppermute | solution.py:418
  68.6 12.5 %collective-permute-start.19 = (f32[64,256]{1,0:T(8,128)S(1)}, f32[64,256]{1,0:T(8,128)S(1)}, u32[]{:S(2)}, u32[]{:S(2)}) collective-permute-start(f32[64,256]{1,0:T(8,128)S(1)} %get-tuple-element.70), channel_id=1, source_target_pairs={{0,24},{1,25},{2,26},{3,27},{4,28},{5,29},{6,30},{7,31},{8,16},{9,... | collective-permute-start | bytes 196616 | tf_op jit(solution)/shard_map/ppermute | solution.py:418

commit v15 on v13

--- a/solution.py
+++ b/solution.py
@@ -27,7 +27,7 @@
 
 
 def cost(flops, nbytes, scale=64):
-    return pl.CostEstimate(flops=int(flops) // scale, bytes_accessed=int(nbytes) // scale, transcendentals=0)
+    return pl.CostEstimate(flops=int(flops / scale), bytes_accessed=int(nbytes / scale), transcendentals=0)
 
 
 def f32(*shape):
@@ -301,7 +301,7 @@
         out_ref[blocks * q :, :] = refs[parts.index("tail")][...]
 
 
-def backward_part(rows, both, first, blocks, before=None, tail=None, tokens=()):
+def backward_part(rows, both, first, blocks, before=None, tail=None, tokens=(), scale=64):
     q, docs = both.shape[0] // 2, both.shape[1]
     extra = {"before": before, "tail": tail, **{str(i): token for i, token in enumerate(tokens)}}
     extra = {name: value for name, value in extra.items() if value is not None}
@@ -312,41 +312,58 @@
         out_specs=whole(),
         out_shape=f32(height, 256),
         compiler_params=params(8),
-        cost_estimate=cost(8 * docs * 256 * 256 * blocks, 4 * docs * 256 * blocks),
+        cost_estimate=cost(8 * docs * 256 * 256 * blocks, 4 * docs * 256 * blocks, scale),
         name="backward_part",
     )(*rows, both, *extra.values())
 
 
-def far_sum_kernel(near, far, beta, send, beta_core):
-    n = near.shape[0]
-    beta_core[...] = beta[...] + far[n:, :]
-    send[0:n, :] = near[...] + far[0:n, :]
-    send[n:, :] = beta_core[...]
-
-
-def far_sums(near, far, beta):
-    rows = near.shape[0]
+def far_sum_kernel(near, far, beta, token, send_far, send_near, beta_core):
+    n = near.shape[0] // 2
+    beta_core[...] = beta[...] + far[2 * n :, :]
+    send_far[...] = near[n:, :] + far[n : 2 * n, :]
+    send_near[0:n, :] = near[0:n, :] + far[0:n, :]
+    send_near[n:, :] = beta_core[...]
+
+
+def far_sums(near, far, beta, token):
+    rows = near.shape[0] // 2
     return pl.pallas_call(
         far_sum_kernel,
-        out_shape=[f32(rows + 8, 256), f32(8, 256)],
+        out_shape=[f32(rows, 256), f32(rows + 8, 256), f32(8, 256)],
         compiler_params=params(8),
         cost_estimate=cost(near.size, near.size * 12),
         name="far_sums",
-    )(near, far, beta)
-
-
-def right_norm_kernel(docs_total, keep, peer, got, beta_core, right, g0, g1, g2, g3, sums, columns):
+    )(near, far, beta, token)
+
+
+def right_far_kernel(keep, peer, got, g2, g3):
+    q = g2.shape[0]
+    for k, g in ((2, g2), (3, g3)):
+        rows = slice(k * q, (k + 1) * q)
+        g[...] = (keep[rows, :] + peer[rows, :]) + got[(k - 2) * q : (k - 1) * q, :]
+
+
+def right_far(keep, peer, got):
+    q, rows = keep.shape[0] // 4, keep.shape[1]
+    return pl.pallas_call(
+        right_far_kernel,
+        out_shape=[f32(q, rows)] * 2,
+        compiler_params=params(8),
+        cost_estimate=cost(rows * q * 4, rows * q * 32),
+        name="right_far",
+    )(keep, peer, got)
+
+
+def right_norm_kernel(docs_total, keep, peer, got, beta_core, right, g2, g3, g0, g1, sums, columns):
     _, z, _ = coords()
     q = right.shape[1]
-    beta_sums = beta_core[0:1, :] + got[4 * q : 4 * q + 1, :]
+    beta_sums = beta_core[0:1, :] + got[2 * q : 2 * q + 1, :]
     columns[...] = row_to_column(jnp.sqrt(beta_sums / docs_total + epsilon))
     beta = columns[pl.ds(pl.multiple_of(z * q, q), q), :][:, 0:1]
-    raws = []
-    for k, g in enumerate((g0, g1, g2, g3)):
+    for k, g in enumerate((g0, g1)):
         rows = slice(k * q, (k + 1) * q)
-        total = (keep[rows, :] + peer[rows, :]) + got[rows, :]
-        g[...] = total
-        raws.append(total / beta - beta * right[k])
+        g[...] = (keep[rows, :] + peer[rows, :]) + got[rows, :]
+    raws = [g[...] / beta - beta * right[k] for k, g in enumerate((g0, g1, g2, g3))]
     line = square_sums(jnp.concatenate(raws, axis=1))
     folded = beta_sums[:, :128] + beta_sums[:, 128:]
     folded = folded + jnp.concatenate([folded[:, q:], folded[:, :q]], axis=1)
@@ -354,17 +371,17 @@
     sums[...] = jnp.broadcast_to(jnp.where(low, line, folded), sums.shape)
 
 
-def right_norm(docs_total, keep, peer, got, beta_core, right):
+def right_norm(docs_total, keep, peer, got, beta_core, right, far):
     q, rows = keep.shape[0] // 4, keep.shape[1]
-    *pieces, sums = pl.pallas_call(
+    g0, g1, sums = pl.pallas_call(
         functools.partial(right_norm_kernel, docs_total),
-        out_shape=[f32(q, rows)] * 4 + [f32(32, 128)],
+        out_shape=[f32(q, rows)] * 2 + [f32(32, 128)],
         scratch_shapes=[pltpu.VMEM((4 * q, 128), jnp.float32)],
         compiler_params=params(8),
-        cost_estimate=cost(rows * q * 64, rows * q * 100),
+        cost_estimate=cost(rows * q * 64, rows * q * 100, 64),
         name="right_norm",
-    )(keep, peer, got, beta_core, right)
-    return pieces, sums.reshape(32, 1, 128)
+    )(keep, peer, got, beta_core, right, *far)
+    return g0, g1, sums.reshape(32, 1, 128)
 
 
 def finish_kernel(docs_total, feat_total, g0, g1, g2, g3, squares, own, other, right, search, solution, phibar, rhobar,
@@ -461,15 +478,19 @@
     both1, beta1 = left_half(product1, swap(product0, Y_BIT), beta0, partial)
     far = swap(backward_part(rows1, both1, 12, 4, partial, beta1, [left_own]), CORE_BIT)
     near = backward_part(rows1, both1, 4, 4, partial)
-    send, beta_core = far_sums(near, far, beta1)
-    got = swap(send, X_BIT)
-    peer = backward_part(rows1, both1, 8, 4, partial)
-    left_other = swap(after(left_own, peer), Y_BIT)
-    keep = backward_part(rows1, both1, 0, 4, partial)
-
-    sent, sums = right_norm(docs_total, keep, swap(peer, CORE_BIT), got, beta_core, own)
-    pieces = along_z(sent)
-    squares = lax.all_to_all(after(sums, left_other), AXES, 0, 0, tiled=True)
+    peer = backward_part(rows1, both1, 8, 4, partial, None, [near])
+    send_far, send_near, beta_core = far_sums(near, far, beta1, peer)
+    got_far = swap(send_far, X_BIT)
+    got_near = swap(send_near, X_BIT)
+    keep = backward_part(rows1, both1, 0, 4, partial, None, [], 0.05)
+    peer = swap(peer, CORE_BIT)
+
+    g2, g3 = right_far(keep, peer, got_far)
+    p2, p3 = swap(g2, 2 << Z_SHIFT), swap(g3, 3 << Z_SHIFT)
+    g0, g1, sums = right_norm(docs_total, keep, peer, got_near, beta_core, own, (g2, g3))
+    pieces = [g0, swap(g1, 1 << Z_SHIFT), p2, p3]
+    left_other = swap(after(left_own, got_far), Y_BIT)
+    squares = lax.all_to_all(after(sums, left_own), AXES, 0, 0, tiled=True)
     left_next, right_next, search_next, solution_next, alpha_next, phibar_next, rhobar_next = finish(
         docs_total, feat_total, pieces, squares, left_own, left_other,
         right_vec, search_dir, solution_vec, phibar_row, rhobar_row,

time: 82.5 us -> 81.5 us (0.988)
    ppermute x21 -> x22, waiting for transfers between devices: 12.8 us -> 12.3 us  [swap(): return lax.ppermute(value, AXES, [(i, i ^ mask) for i in range(32)])]
    ppermute x21 -> x22, starting transfers between devices: 28.6 us -> 28.6 us  [swap(): return lax.ppermute(value, AXES, [(i, i ^ mask) for i in range(32)])]
  transfers between devices with their start and end apart: 21 -> 22, of which waited for: 8 -> 8; matrix products, arithmetic and copies ran while one was open for 0% -> 0% of each run, Pallas kernels for 28% -> 29%
where the time goes in v15:
time: 81.5 us; the launch traced here: 81.3 us
  starting transfers between devices  28.6 us (35%)
  Pallas kernels  28.3 us (35%)
  waiting for transfers between devices  12.3 us (15%)
  blocking collectives  11.1 us (14%)
  between operations  0.93 us (1%)
    ppermute x22, starting transfers between devices, swap(): return lax.ppermute(value, AXES, [(i, i ^ mask) for i in range(32)])  28.6 us
    ppermute x22, waiting for transfers between devices, swap(): return lax.ppermute(value, AXES, [(i, i ^ mask) for i in range(32)])  12.3 us
    all_to_all x1, blocking collectives, by_columns(): squares = lax.all_to_all(after(sums, left_own), AXES, 0, 0, tiled=True)  11.1 us
    pallas_call x2, Pallas kernels, build(): pl.pallas_call(functools.partial(build_kernel, rel), in_specs=[whole()] *...  9.67 us
    pallas_call x4, Pallas kernels, forward_part(): pl.pallas_call(functools.partial(forward_kernel, blocks, before is not No...  7.11 us
    pallas_call x5, Pallas kernels, backward_part(): pl.pallas_call(functools.partial(backward_kernel, first, blocks, tuple(ex...  5.23 us
    pallas_call x2, Pallas kernels, product_half(): pl.pallas_call(functools.partial(product_kernel, blocks), in_specs=[whole...  2.64 us
    pallas_call x1, Pallas kernels, prepare(): pl.pallas_call(prepare_kernel, in_specs=[pl.BlockSpec(memory_space=pltpu....  1.63 us
  transfers between devices with their start and end apart: 22, of which 8 were waited for; matrix products, arithmetic and copies ran while one was open for 0% of the time, Pallas kernels for 29%

profile of v15, /device:TPU:0, one launch (start us, length us, event | category | flops | bytes accessed | tf_op | source)
XLA Modules:
  0.0 81.3 jit_solution(1517226609853204579)
XLA Ops:
  0.6 1.6 %prepare.1 = (f32[64,256]{1,0:T(8,128)S(1)}, f32[128,256]{1,0:T(8,128)S(1)}, f32[128,256]{1,0:T(8,128)S(1)}, f32[128,256]{1,0:T(8,128)S(1)}, f32[128,256]{1,0:T(8,128)S(1)}) custom-call(s32[16,512]{1,0:T(8,128)} %bitcast.13, bf16[16,512]{1,0:T(8,128)(2,1)} %bitcast.14, f32[256,256]{1,0:T(8,128)} %right.1, f32[512,256]{1,0:T(8,128)} %left_hbm.1), custom_call_target="tpu_custom_call" | custom-call | bytes 16384 | tf_op jit(solution)/shard_map/prepare/pallas_call | solution.py:74
  2.3 4.1 %collective-permute-start.1 = (f32[64,256]{1,0:T(8,128)S(1)}, f32[64,256]{1,0:T(8,128)S(1)}, u32[]{:S(2)}, u32[]{:S(2)}) collective-permute-start(f32[64,256]{1,0:T(8,128)S(1)} %get-tuple-element.45.e0), channel_id=1, source_target_pairs={{0,16},{1,17},{2,18},{3,19},{4,20},{5,21},{6,22},{7,23},{8,24},{9,... | collective-permute-start | bytes 196616 | tf_op jit(solution)/shard_map/ppermute | solution.py:436
  6.4 1.4 %collective-permute-start.2 = (f32[64,256]{1,0:T(8,128)S(1)}, f32[64,256]{1,0:T(8,128)S(1)}, u32[]{:S(2)}, u32[]{:S(2)}) collective-permute-start(f32[64,256]{1,0:T(8,128)S(1)} %get-tuple-element.45.e0), channel_id=1, source_target_pairs={{0,24},{1,25},{2,26},{3,27},{4,28},{5,29},{6,30},{7,31},{8,16},{9,... | collective-permute-start | bytes 196616 | tf_op jit(solution)/shard_map/ppermute | solution.py:436
  7.7 0.2 collective-permute-start
  8.0 2.8 %collective-permute-start.4 = (f32[128,256]{1,0:T(8,128)S(1)}, f32[128,256]{1,0:T(8,128)S(1)}, u32[]{:S(2)}, u32[]{:S(2)}) collective-permute-start(f32[128,256]{1,0:T(8,128)S(1)} %get-tuple-element.51), channel_id=1, source_target_pairs={{0,16},{1,17},{2,18},{3,19},{4,20},{5,21},{6,22},{7,23},{8,24},{9,... | collective-permute-start | bytes 393224 | tf_op jit(solution)/shard_map/ppermute | solution.py:436
  10.8 1.4 %collective-permute-start.5 = (f32[128,256]{1,0:T(8,128)S(1)}, f32[128,256]{1,0:T(8,128)S(1)}, u32[]{:S(2)}, u32[]{:S(2)}) collective-permute-start(f32[128,256]{1,0:T(8,128)S(1)} %get-tuple-element.52), channel_id=1, source_target_pairs={{0,24},{1,25},{2,26},{3,27},{4,28},{5,29},{6,30},{7,31},{8,16},{9,... | collective-permute-start | bytes 393224 | tf_op jit(solution)/shard_map/ppermute | solution.py:436
  12.1 0.6 collective-permute-start.3
  12.7 0.5 collective-permute-done.2.e3
  13.3 4.7 %dense_rows.2 = (bf16[16,1024,256]{2,1,0:T(8,128)(2,1)S(1)}, bf16[16,1024,256]{2,1,0:T(8,128)(2,1)S(1)}, f32[8,128]{1,0:T(8,128)S(1)}) custom-call(f32[64,256]{1,0:T(8,128)S(1)} %get-tuple-element.45.e0, f32[64,256]{1,0:T(8,128)S(1)} %collective-permute-done.e1, f32[64,256]{1,0:T(8,128)S(1)} %collective-permute-done.1.e2, ...), custom_call_target="tpu_custom_call" | custom-call | flops 2147483648 | bytes 16777216 | tf_op jit(solution)/shard_map/dense_rows/pallas_call | solution.py:154
  18.0 3.6 %collective-permute-done.4.m2.refs_2_ = f32[128,256]{1,0:T(8,128)S(1)} collective-permute-done((f32[128,256]{1,0:T(8,128)S(1)}, f32[128,256]{1,0:T(8,128)S(1)}, u32[]{:S(2)}, u32[]{:S(2)}) %collective-permute-start.4) | collective-permute-done | bytes 131104 | tf_op jit(solution)/shard_map/ppermute | solution.py:436
  21.7 0.1 collective-permute-done.3.m1.refs_1_
  21.8 0.1 collective-permute-start.7
  21.9 1.8 %collective-permute-start.6 = (f32[4,64,256]{2,1,0:T(8,128)S(1)}, f32[4,64,256]{2,1,0:T(8,128)S(1)}, u32[]{:S(2)}, u32[]{:S(2)}) collective-permute-start(f32[4,64,256]{2,1,0:T(8,128)S(1)} %stack_right.1.refs_0_.right), channel_id=1, source_target_pairs={{0,4},{1,5},{2,6},{3,7},{4,0},{5,1},{6,2},{7,3},{8,12},{9,13},{10,... | collective-permute-start | bytes 786440 | tf_op jit(solution)/shard_map/ppermute | solution.py:436
  23.6 4.9 %dense_rows.3 = (bf16[16,1024,256]{2,1,0:T(8,128)(2,1)S(1)}, bf16[16,1024,256]{2,1,0:T(8,128)(2,1)S(1)}, f32[8,128]{1,0:T(8,128)S(1)}) custom-call(f32[64,256]{1,0:T(8,128)S(1)} %get-tuple-element.45.e0, f32[64,256]{1,0:T(8,128)S(1)} %collective-permute-done.e1, f32[64,256]{1,0:T(8,128)S(1)} %collective-permute-done.1.e2, ...), custom_call_target="tpu_custom_call" | custom-call | flops 33554432 | bytes 262144 | tf_op jit(solution)/shard_map/dense_rows/pallas_call | solution.py:154
  28.6 2.3 %forward_part.4.refs_1_ = f32[1024,128]{1,0:T(8,128)S(1)} custom-call(bf16[16,1024,256]{2,1,0:T(8,128)(2,1)S(1)} %get-tuple-element.46.hi_ref, bf16[16,1024,256]{2,1,0:T(8,128)(2,1)S(1)} %get-tuple-element.47.lo_ref, f32[4,64,256]{2,1,0:T(8,128)S(1)} %stack_right.1.refs_0_.right, f32[4,64,256]{2,1,0:T(8,128)S(1)} %collective-permute-done.7.refs_1_, ...), custom_call_target="tpu_custom_call" | custom-call | flops 67108864 | bytes 131072 | tf_op jit(solution)/shard_map/forward_part/pallas_call | solution.py:196
  30.9 0.2 collective-permute-start.8
  31.1 1.2 %forward_part.5.before = f32[1024,128]{1,0:T(8,128)S(1)} custom-call(bf16[16,1024,256]{2,1,0:T(8,128)(2,1)S(1)} %get-tuple-element.46.hi_ref, bf16[16,1024,256]{2,1,0:T(8,128)(2,1)S(1)} %get-tuple-element.47.lo_ref, f32[4,64,256]{2,1,0:T(8,128)S(1)} %collective-permute-done.6.refs_0_, f32[1024,128]{1,0:T(8,128)S(1)} %forward_part.4.refs_1_), custom_call_target="tpu_custom_call" | custom-call | flops 33554432 | bytes 65536 | tf_op jit(solution)/shard_map/forward_part/pallas_call | solution.py:196
  32.4 0.2 collective-permute-done.8.vec
  32.5 1.3 %product_half.2.mine = f32[64,1024]{1,0:T(8,128)S(1)} custom-call(bf16[16,1024,256]{2,1,0:T(8,128)(2,1)S(1)} %get-tuple-element.46.hi_ref, bf16[16,1024,256]{2,1,0:T(8,128)(2,1)S(1)} %get-tuple-element.47.lo_ref, f32[4,64,256]{2,1,0:T(8,128)S(1)} %collective-permute-done.8.vec, f32[1024,128]{1,0:T(8,128)S(1)} %forward_part.5.before), custom_call_target="tpu_custom_call" | custom-call | flops 33554432 | bytes 65536 | tf_op jit(solution)/shard_map/product_half/pallas_call | solution.py:228
  33.8 1.6 %collective-permute-start.10 = (f32[64,1024]{1,0:T(8,128)S(1)}, f32[64,1024]{1,0:T(8,128)S(1)}, u32[]{:S(2)}, u32[]{:S(2)}) collective-permute-start(f32[64,1024]{1,0:T(8,128)S(1)} %product_half.2.mine), channel_id=1, source_target_pairs={{0,1},{1,0},{2,3},{3,2},{4,5},{5,4},{6,7},{7,6},{8,9},{9,8},{10,11... | collective-permute-start | bytes 786440 | tf_op jit(solution)/shard_map/ppermute | solution.py:436
  35.4 2.3 %forward_part.6.refs_1_ = f32[1024,128]{1,0:T(8,128)S(1)} custom-call(bf16[16,1024,256]{2,1,0:T(8,128)(2,1)S(1)} %get-tuple-element.56.hi_ref, bf16[16,1024,256]{2,1,0:T(8,128)(2,1)S(1)} %get-tuple-element.57.lo_ref, f32[4,64,256]{2,1,0:T(8,128)S(1)} %stack_right.1.refs_0_.right, f32[4,64,256]{2,1,0:T(8,128)S(1)} %collective-permute-done.7.refs_1_), custom_call_target="tpu_custom_call" | custom-call | flops 67108864 | bytes 131072 | tf_op jit(solution)/shard_map/forward_part/pallas_call | solution.py:196
  37.7 1.2 %forward_part.7.before = f32[1024,128]{1,0:T(8,128)S(1)} custom-call(bf16[16,1024,256]{2,1,0:T(8,128)(2,1)S(1)} %get-tuple-element.56.hi_ref, bf16[16,1024,256]{2,1,0:T(8,128)(2,1)S(1)} %get-tuple-element.57.lo_ref, f32[4,64,256]{2,1,0:T(8,128)S(1)} %collective-permute-done.6.refs_0_, f32[1024,128]{1,0:T(8,128)S(1)} %forward_part.6.refs_1_), custom_call_target="tpu_custom_call" | custom-call | flops 33554432 | bytes 65536 | tf_op jit(solution)/shard_map/forward_part/pallas_call | solution.py:196
  39.0 1.3 %product_half.3.mine = f32[64,1024]{1,0:T(8,128)S(1)} custom-call(bf16[16,1024,256]{2,1,0:T(8,128)(2,1)S(1)} %get-tuple-element.56.hi_ref, bf16[16,1024,256]{2,1,0:T(8,128)(2,1)S(1)} %get-tuple-element.57.lo_ref, f32[4,64,256]{2,1,0:T(8,128)S(1)} %collective-permute-done.8.vec, f32[1024,128]{1,0:T(8,128)S(1)} %forward_part.7.before, ...), custom_call_target="tpu_custom_call" | custom-call | flops 33554432 | bytes 65536 | tf_op jit(solution)/shard_map/product_half/pallas_call | solution.py:228
  40.3 0.6 collective-permute-start.9
  40.9 1.4 %collective-permute-done.10.other = f32[64,1024]{1,0:T(8,128)S(1)} collective-permute-done((f32[64,1024]{1,0:T(8,128)S(1)}, f32[64,1024]{1,0:T(8,128)S(1)}, u32[]{:S(2)}, u32[]{:S(2)}) %collective-permute-start.10) | collective-permute-done | bytes 262176 | tf_op jit(solution)/shard_map/ppermute | solution.py:436
  42.3 0.2 left_half.2
  42.5 3.0 %collective-permute-start.12 = (f32[64,256]{1,0:T(8,128)S(1)}, f32[64,256]{1,0:T(8,128)S(1)}, u32[]{:S(2)}, u32[]{:S(2)}) collective-permute-start(f32[64,256]{1,0:T(8,128)S(1)} %get-tuple-element.63), channel_id=1, source_target_pairs={{0,8},{1,9},{2,10},{3,11},{4,12},{5,13},{6,14},{7,15},{8,0},{9,1},... | collective-permute-start | bytes 196616 | tf_op jit(solution)/shard_map/ppermute | solution.py:436
  45.5 1.8 %collective-permute-start.13 = (f32[64,256]{1,0:T(8,128)S(1)}, f32[64,256]{1,0:T(8,128)S(1)}, u32[]{:S(2)}, u32[]{:S(2)}) collective-permute-start(f32[64,256]{1,0:T(8,128)S(1)} %get-tuple-element.64), channel_id=1, source_target_pairs={{0,16},{1,17},{2,18},{3,19},{4,20},{5,21},{6,22},{7,23},{8,24},{9,... | collective-permute-start | bytes 196616 | tf_op jit(solution)/shard_map/ppermute | solution.py:436
  47.3 1.4 %collective-permute-start.14 = (f32[64,256]{1,0:T(8,128)S(1)}, f32[64,256]{1,0:T(8,128)S(1)}, u32[]{:S(2)}, u32[]{:S(2)}) collective-permute-start(f32[64,256]{1,0:T(8,128)S(1)} %get-tuple-element.65), channel_id=1, source_target_pairs={{0,24},{1,25},{2,26},{3,27},{4,28},{5,29},{6,30},{7,31},{8,16},{9,... | collective-permute-start | bytes 196616 | tf_op jit(solution)/shard_map/ppermute | solution.py:436
  48.7 2.3 %backward_part.5.refs_1_.refs_0_ = f32[1024,256]{1,0:T(8,128)S(1)} custom-call(bf16[16,1024,256]{2,1,0:T(8,128)(2,1)S(1)} %get-tuple-element.56.hi_ref, bf16[16,1024,256]{2,1,0:T(8,128)(2,1)S(1)} %get-tuple-element.57.lo_ref, bf16[128,1024]{1,0:T(8,128)(2,1)S(1)} %get-tuple-element.59.both_ref), custom_call_target="tpu_custom_call" | custom-call | flops 134217728 | bytes 262144 | tf_op jit(solution)/shard_map/backward_part/pallas_call | solution.py:309
  51.0 0.2 left_half.3
  51.2 2.3 %collective-permute-done.13.m2 = f32[64,256]{1,0:T(8,128)S(1)} collective-permute-done((f32[64,256]{1,0:T(8,128)S(1)}, f32[64,256]{1,0:T(8,128)S(1)}, u32[]{:S(2)}, u32[]{:S(2)}) %collective-permute-start.13) | collective-permute-done | bytes 65568 | tf_op jit(solution)/shard_map/ppermute | solution.py:436
  53.5 0.7 backward_part.9
  54.3 0.1 collective-permute-start.15
  54.3 0.7 backward_part.7.refs_1_.near
  55.1 0.7 backward_part.8.token
  55.9 1.4 %collective-permute-start.17 = (f32[128,256]{1,0:T(8,128)S(1)}, f32[128,256]{1,0:T(8,128)S(1)}, u32[]{:S(2)}, u32[]{:S(2)}) collective-permute-start(f32[128,256]{1,0:T(8,128)S(1)} %get-tuple-element.68), channel_id=1, source_target_pairs={{0,4},{1,5},{2,6},{3,7},{4,0},{5,1},{6,2},{7,3},{8,12},{9,13},{10,... | collective-permute-start | bytes 393224 | tf_op jit(solution)/shard_map/ppermute | solution.py:436
  57.3 0.2 collective-permute-start.11
  57.5 0.8 collective-permute-start.16
  58.2 4.0 %collective-permute-done.17.got = f32[128,256]{1,0:T(8,128)S(1)} collective-permute-done((f32[128,256]{1,0:T(8,128)S(1)}, f32[128,256]{1,0:T(8,128)S(1)}, u32[]{:S(2)}, u32[]{:S(2)}) %collective-permute-start.17) | collective-permute-done | bytes 131104 | tf_op jit(solution)/shard_map/ppermute | solution.py:436
  62.3 1.8 %collective-permute-start.21 = (f32[4,64,256]{2,1,0:T(8,128)S(1)}, f32[4,64,256]{2,1,0:T(8,128)S(1)}, u32[]{:S(2)}, u32[]{:S(2)}) collective-permute-start(f32[4,64,256]{2,1,0:T(8,128)S(1)} %stack_left.1.refs_2_.own), channel_id=1, source_target_pairs={{0,1},{1,0},{2,3},{3,2},{4,5},{5,4},{6,7},{7,6},{8,9},{9,8},{10,11... | collective-permute-start | bytes 786440 | tf_op jit(solution)/shard_map/ppermute | solution.py:436
  64.0 0.7 backward_part.6.keep
  64.8 2.1 %collective-permute-start.19 = (f32[64,256]{1,0:T(8,128)S(1)}, f32[64,256]{1,0:T(8,128)S(1)}, u32[]{:S(2)}, u32[]{:S(2)}) collective-permute-start(f32[64,256]{1,0:T(8,128)S(1)} %get-tuple-element.69.g2), channel_id=1, source_target_pairs={{0,16},{1,17},{2,18},{3,19},{4,20},{5,21},{6,22},{7,23},{8,24},{9,... | collective-permute-start | bytes 196616 | tf_op jit(solution)/shard_map/ppermute | solution.py:436
  67.0 1.4 %collective-permute-start.20 = (f32[64,256]{1,0:T(8,128)S(1)}, f32[64,256]{1,0:T(8,128)S(1)}, u32[]{:S(2)}, u32[]{:S(2)}) collective-permute-start(f32[64,256]{1,0:T(8,128)S(1)} %get-tuple-element.70.g3), channel_id=1, source_target_pairs={{0,24},{1,25},{2,26},{3,27},{4,28},{5,29},{6,30},{7,31},{8,16},{9,... | collective-permute-start | bytes 196616 | tf_op jit(solution)/shard_map/ppermute | solution.py:436
  68.4 0.3 right_norm.1
  68.7 0.1 collective-permute-start.18
  68.8 11.1 %all_to_all.5.squares = f32[32,1,128]{2,1,0:T(1,128)S(1)} all-to-all(f32[32,1,128]{2,1,0:T(1,128)S(1)} %bitcast.9), channel_id=1, replica_groups=mesh['doc'=16,'feat'=2] {'doc','feat'}, dimensions={0} | all-to-all | bytes 32768 | tf_op jit(solution)/shard_map/all_to_all | solution.py:493
  80.0 1.3 %finish.1 = (f32[512,256]{1,0:T(8,128)}, f32[256,256]{1,0:T(8,128)}, f32[256,256]{1,0:T(8,128)}, f32[256,256]{1,0:T(8,128)}, f32[1,256]{1,0:T(1,128)}, /*index=5*/f32[1,256]{1,0:T(1,128)}, f32[1,256]{1,0:T(1,128)}) custom-call(f32[64,256]{1,0:T(8,128)S(1)} %get-tuple-element.71.g0, f32[64,256]{1,0:T(8,128)S(1)} %collective-permute-done.18.g1, ...), custom_call_target="tpu_custom_call" | custom-call | flops 16384 | bytes 20480 | tf_op jit(solution)/shard_map/finish/pallas_call | solution.py:425
  (31 shorter events, 0.2 us)
Async XLA Ops:
  2.3 9.9 %collective-permute-start.1 = (f32[64,256]{1,0:T(8,128)S(1)}, f32[64,256]{1,0:T(8,128)S(1)}, u32[]{:S(2)}, u32[]{:S(2)}) collective-permute-start(f32[64,256]{1,0:T(8,128)S(1)} %get-tuple-element.45.e0), channel_id=1, source_target_pairs={{0,16},{1,17},{2,18},{3,19},{4,20},{5,21},{6,22},{7,23},{8,24},{9,... | collective-permute-start | bytes 196616 | tf_op jit(solution)/shard_map/ppermute | solution.py:436
  6.4 6.9 %collective-permute-start.2 = (f32[64,256]{1,0:T(8,128)S(1)}, f32[64,256]{1,0:T(8,128)S(1)}, u32[]{:S(2)}, u32[]{:S(2)}) collective-permute-start(f32[64,256]{1,0:T(8,128)S(1)} %get-tuple-element.45.e0), channel_id=1, source_target_pairs={{0,24},{1,25},{2,26},{3,27},{4,28},{5,29},{6,30},{7,31},{8,16},{9,... | collective-permute-start | bytes 196616 | tf_op jit(solution)/shard_map/ppermute | solution.py:436
  7.7 5.6 %collective-permute-start = (f32[64,256]{1,0:T(8,128)S(1)}, f32[64,256]{1,0:T(8,128)S(1)}, u32[]{:S(2)}, u32[]{:S(2)}) collective-permute-start(f32[64,256]{1,0:T(8,128)S(1)} %get-tuple-element.45.e0), channel_id=1, source_target_pairs={{0,8},{1,9},{2,10},{3,11},{4,12},{5,13},{6,14},{7,15},{8,0},{9,1},... | collective-permute-start | bytes 196616 | tf_op jit(solution)/shard_map/ppermute | solution.py:436
  8.0 13.7 %collective-permute-start.4 = (f32[128,256]{1,0:T(8,128)S(1)}, f32[128,256]{1,0:T(8,128)S(1)}, u32[]{:S(2)}, u32[]{:S(2)}) collective-permute-start(f32[128,256]{1,0:T(8,128)S(1)} %get-tuple-element.51), channel_id=1, source_target_pairs={{0,16},{1,17},{2,18},{3,19},{4,20},{5,21},{6,22},{7,23},{8,24},{9,... | collective-permute-start | bytes 393224 | tf_op jit(solution)/shard_map/ppermute | solution.py:436
  10.8 10.9 %collective-permute-start.5 = (f32[128,256]{1,0:T(8,128)S(1)}, f32[128,256]{1,0:T(8,128)S(1)}, u32[]{:S(2)}, u32[]{:S(2)}) collective-permute-start(f32[128,256]{1,0:T(8,128)S(1)} %get-tuple-element.52), channel_id=1, source_target_pairs={{0,24},{1,25},{2,26},{3,27},{4,28},{5,29},{6,30},{7,31},{8,16},{9,... | collective-permute-start | bytes 393224 | tf_op jit(solution)/shard_map/ppermute | solution.py:436
  12.1 9.6 %collective-permute-start.3 = (f32[128,256]{1,0:T(8,128)S(1)}, f32[128,256]{1,0:T(8,128)S(1)}, u32[]{:S(2)}, u32[]{:S(2)}) collective-permute-start(f32[128,256]{1,0:T(8,128)S(1)} %get-tuple-element.50), channel_id=1, source_target_pairs={{0,8},{1,9},{2,10},{3,11},{4,12},{5,13},{6,14},{7,15},{8,0},{9,1},... | collective-permute-start | bytes 393224 | tf_op jit(solution)/shard_map/ppermute | solution.py:436
  21.8 6.8 %collective-permute-start.7 = (f32[4,64,256]{2,1,0:T(8,128)S(1)}, f32[4,64,256]{2,1,0:T(8,128)S(1)}, u32[]{:S(2)}, u32[]{:S(2)}) collective-permute-start(f32[4,64,256]{2,1,0:T(8,128)S(1)} %stack_right.1.refs_0_.right), channel_id=1, source_target_pairs={{0,2},{1,3},{2,0},{3,1},{4,6},{5,7},{6,4},{7,5},{8,10},{9,11},{10,... | collective-permute-start | bytes 786440 | tf_op jit(solution)/shard_map/ppermute | solution.py:436
  21.9 9.0 %collective-permute-start.6 = (f32[4,64,256]{2,1,0:T(8,128)S(1)}, f32[4,64,256]{2,1,0:T(8,128)S(1)}, u32[]{:S(2)}, u32[]{:S(2)}) collective-permute-start(f32[4,64,256]{2,1,0:T(8,128)S(1)} %stack_right.1.refs_0_.right), channel_id=1, source_target_pairs={{0,4},{1,5},{2,6},{3,7},{4,0},{5,1},{6,2},{7,3},{8,12},{9,13},{10,... | collective-permute-start | bytes 786440 | tf_op jit(solution)/shard_map/ppermute | solution.py:436
  30.9 1.6 %collective-permute-start.8 = (f32[4,64,256]{2,1,0:T(8,128)S(1)}, f32[4,64,256]{2,1,0:T(8,128)S(1)}, u32[]{:S(2)}, u32[]{:S(2)}) collective-permute-start(f32[4,64,256]{2,1,0:T(8,128)S(1)} %collective-permute-done.6.refs_0_), channel_id=1, source_target_pairs={{0,2},{1,3},{2,0},{3,1},{4,6},{5,7},{6,4},{7,5},{8,10},{9,11},{10,... | collective-permute-start | bytes 786440 | tf_op jit(solution)/shard_map/ppermute | solution.py:436
  33.8 8.5 %collective-permute-start.10 = (f32[64,1024]{1,0:T(8,128)S(1)}, f32[64,1024]{1,0:T(8,128)S(1)}, u32[]{:S(2)}, u32[]{:S(2)}) collective-permute-start(f32[64,1024]{1,0:T(8,128)S(1)} %product_half.2.mine), channel_id=1, source_target_pairs={{0,1},{1,0},{2,3},{3,2},{4,5},{5,4},{6,7},{7,6},{8,9},{9,8},{10,11... | collective-permute-start | bytes 786440 | tf_op jit(solution)/shard_map/ppermute | solution.py:436
  37.7 1.3 %copy-start.3 = (f32[256]{0:T(256)S(1)}, f32[256]{0:T(256)}, u32[]{:S(2)}) copy-start(f32[256]{0:T(256)} %param.15) | copy-start | bytes 3076
  40.3 10.7 %collective-permute-start.9 = (f32[64,1024]{1,0:T(8,128)S(1)}, f32[64,1024]{1,0:T(8,128)S(1)}, u32[]{:S(2)}, u32[]{:S(2)}) collective-permute-start(f32[64,1024]{1,0:T(8,128)S(1)} %product_half.3.mine), channel_id=1, source_target_pairs={{0,1},{1,0},{2,3},{3,2},{4,5},{5,4},{6,7},{7,6},{8,9},{9,8},{10,11... | collective-permute-start | bytes 786440 | tf_op jit(solution)/shard_map/ppermute | solution.py:436
  42.5 8.7 %collective-permute-start.12 = (f32[64,256]{1,0:T(8,128)S(1)}, f32[64,256]{1,0:T(8,128)S(1)}, u32[]{:S(2)}, u32[]{:S(2)}) collective-permute-start(f32[64,256]{1,0:T(8,128)S(1)} %get-tuple-element.63), channel_id=1, source_target_pairs={{0,8},{1,9},{2,10},{3,11},{4,12},{5,13},{6,14},{7,15},{8,0},{9,1},... | collective-permute-start | bytes 196616 | tf_op jit(solution)/shard_map/ppermute | solution.py:436
  45.5 8.0 %collective-permute-start.13 = (f32[64,256]{1,0:T(8,128)S(1)}, f32[64,256]{1,0:T(8,128)S(1)}, u32[]{:S(2)}, u32[]{:S(2)}) collective-permute-start(f32[64,256]{1,0:T(8,128)S(1)} %get-tuple-element.64), channel_id=1, source_target_pairs={{0,16},{1,17},{2,18},{3,19},{4,20},{5,21},{6,22},{7,23},{8,24},{9,... | collective-permute-start | bytes 196616 | tf_op jit(solution)/shard_map/ppermute | solution.py:436
  47.3 6.2 %collective-permute-start.14 = (f32[64,256]{1,0:T(8,128)S(1)}, f32[64,256]{1,0:T(8,128)S(1)}, u32[]{:S(2)}, u32[]{:S(2)}) collective-permute-start(f32[64,256]{1,0:T(8,128)S(1)} %get-tuple-element.65), channel_id=1, source_target_pairs={{0,24},{1,25},{2,26},{3,27},{4,28},{5,29},{6,30},{7,31},{8,16},{9,... | collective-permute-start | bytes 196616 | tf_op jit(solution)/shard_map/ppermute | solution.py:436
  54.3 1.6 %collective-permute-start.15 = (f32[264,256]{1,0:T(8,128)S(1)}, f32[264,256]{1,0:T(8,128)S(1)}, u32[]{:S(2)}, u32[]{:S(2)}) collective-permute-start(f32[264,256]{1,0:T(8,128)S(1)} %backward_part.9), channel_id=1, source_target_pairs={{0,2},{1,3},{2,0},{3,1},{4,6},{5,7},{6,4},{7,5},{8,10},{9,11},{10,... | collective-permute-start | bytes 811016 | tf_op jit(solution)/shard_map/ppermute | solution.py:436
  55.9 6.4 %collective-permute-start.17 = (f32[128,256]{1,0:T(8,128)S(1)}, f32[128,256]{1,0:T(8,128)S(1)}, u32[]{:S(2)}, u32[]{:S(2)}) collective-permute-start(f32[128,256]{1,0:T(8,128)S(1)} %get-tuple-element.68), channel_id=1, source_target_pairs={{0,4},{1,5},{2,6},{3,7},{4,0},{5,1},{6,2},{7,3},{8,12},{9,13},{10,... | collective-permute-start | bytes 393224 | tf_op jit(solution)/shard_map/ppermute | solution.py:436
  57.3 7.5 %collective-permute-start.11 = (f32[256,256]{1,0:T(8,128)S(1)}, f32[256,256]{1,0:T(8,128)S(1)}, u32[]{:S(2)}, u32[]{:S(2)}) collective-permute-start(f32[256,256]{1,0:T(8,128)S(1)} %backward_part.8.token), channel_id=1, source_target_pairs={{0,2},{1,3},{2,0},{3,1},{4,6},{5,7},{6,4},{7,5},{8,10},{9,11},{10,... | collective-permute-start | bytes 786440 | tf_op jit(solution)/shard_map/ppermute | solution.py:436
  57.4 22.5 %copy-start = (f32[256,256]{1,0:T(8,128)S(1)}, f32[256,256]{1,0:T(8,128)}, u32[]{:S(2)}) copy-start(f32[256,256]{1,0:T(8,128)} %right.1) | copy-start | bytes 786436
  57.4 22.5 %copy-start.1 = (f32[256,256]{1,0:T(8,128)S(1)}, f32[256,256]{1,0:T(8,128)}, u32[]{:S(2)}) copy-start(f32[256,256]{1,0:T(8,128)} %search.1) | copy-start | bytes 786436
  57.4 22.5 %copy-start.2 = (f32[256,256]{1,0:T(8,128)S(1)}, f32[256,256]{1,0:T(8,128)}, u32[]{:S(2)}) copy-start(f32[256,256]{1,0:T(8,128)} %solution.1) | copy-start | bytes 786436
  57.4 22.5 %copy-start.4 = (f32[256]{0:T(256)S(1)}, f32[256]{0:T(256)}, u32[]{:S(2)}) copy-start(f32[256]{0:T(256)} %param.16) | copy-start | bytes 3076
  57.4 22.5 %copy-start.5 = (f32[256]{0:T(256)S(1)}, f32[256]{0:T(256)}, u32[]{:S(2)}) copy-start(f32[256]{0:T(256)} %param.17) | copy-start | bytes 3076
  57.5 10.9 %collective-permute-start.16 = (f32[136,256]{1,0:T(8,128)S(1)}, f32[136,256]{1,0:T(8,128)S(1)}, u32[]{:S(2)}, u32[]{:S(2)}) collective-permute-start(f32[136,256]{1,0:T(8,128)S(1)} %get-tuple-element.66), channel_id=1, source_target_pairs={{0,4},{1,5},{2,6},{3,7},{4,0},{5,1},{6,2},{7,3},{8,12},{9,13},{10,... | collective-permute-start | bytes 417800 | tf_op jit(solution)/shard_map/ppermute | solution.py:436
  62.3 17.6 %collective-permute-start.21 = (f32[4,64,256]{2,1,0:T(8,128)S(1)}, f32[4,64,256]{2,1,0:T(8,128)S(1)}, u32[]{:S(2)}, u32[]{:S(2)}) collective-permute-start(f32[4,64,256]{2,1,0:T(8,128)S(1)} %stack_left.1.refs_2_.own), channel_id=1, source_target_pairs={{0,1},{1,0},{2,3},{3,2},{4,5},{5,4},{6,7},{7,6},{8,9},{9,8},{10,11... | collective-permute-start | bytes 786440 | tf_op jit(solution)/shard_map/ppermute | solution.py:436
  64.8 15.1 %collective-permute-start.19 = (f32[64,256]{1,0:T(8,128)S(1)}, f32[64,256]{1,0:T(8,128)S(1)}, u32[]{:S(2)}, u32[]{:S(2)}) collective-permute-start(f32[64,256]{1,0:T(8,128)S(1)} %get-tuple-element.69.g2), channel_id=1, source_target_pairs={{0,16},{1,17},{2,18},{3,19},{4,20},{5,21},{6,22},{7,23},{8,24},{9,... | collective-permute-start | bytes 196616 | tf_op jit(solution)/shard_map/ppermute | solution.py:436
  67.0 12.9 %collective-permute-start.20 = (f32[64,256]{1,0:T(8,128)S(1)}, f32[64,256]{1,0:T(8,128)S(1)}, u32[]{:S(2)}, u32[]{:S(2)}) collective-permute-start(f32[64,256]{1,0:T(8,128)S(1)} %get-tuple-element.70.g3), channel_id=1, source_target_pairs={{0,24},{1,25},{2,26},{3,27},{4,28},{5,29},{6,30},{7,31},{8,16},{9,... | collective-permute-start | bytes 196616 | tf_op jit(solution)/shard_map/ppermute | solution.py:436
  68.7 11.2 %collective-permute-start.18 = (f32[64,256]{1,0:T(8,128)S(1)}, f32[64,256]{1,0:T(8,128)S(1)}, u32[]{:S(2)}, u32[]{:S(2)}) collective-permute-start(f32[64,256]{1,0:T(8,128)S(1)} %get-tuple-element.72), channel_id=1, source_target_pairs={{0,8},{1,9},{2,10},{3,11},{4,12},{5,13},{6,14},{7,15},{8,0},{9,1},... | collective-permute-start | bytes 196616 | tf_op jit(solution)/shard_map/ppermute | solution.py:436

commit v16 on v15

--- a/solution.py
+++ b/solution.py
@@ -476,9 +476,9 @@
     partial = backward_part(rows0, both0, 0, 16)
     left_own = stack(along_z(lefts), q, "stack_left")
     both1, beta1 = left_half(product1, swap(product0, Y_BIT), beta0, partial)
-    far = swap(backward_part(rows1, both1, 12, 4, partial, beta1, [left_own]), CORE_BIT)
-    near = backward_part(rows1, both1, 4, 4, partial)
-    peer = backward_part(rows1, both1, 8, 4, partial, None, [near])
+    far = swap(backward_part(rows1, both1, 12, 4, partial, beta1), CORE_BIT)
+    near = backward_part(rows1, both1, 4, 4, partial, None, [], 0.05)
+    peer = backward_part(rows1, both1, 8, 4, partial, None, [near], 0.05)
     send_far, send_near, beta_core = far_sums(near, far, beta1, peer)
     got_far = swap(send_far, X_BIT)
     got_near = swap(send_near, X_BIT)
@@ -489,7 +489,7 @@
     p2, p3 = swap(g2, 2 << Z_SHIFT), swap(g3, 3 << Z_SHIFT)
     g0, g1, sums = right_norm(docs_total, keep, peer, got_near, beta_core, own, (g2, g3))
     pieces = [g0, swap(g1, 1 << Z_SHIFT), p2, p3]
-    left_other = swap(after(left_own, got_far), Y_BIT)
+    left_other = swap(after(left_own, send_far), Y_BIT)
     squares = lax.all_to_all(after(sums, left_own), AXES, 0, 0, tiled=True)
     left_next, right_next, search_next, solution_next, alpha_next, phibar_next, rhobar_next = finish(
         docs_total, feat_total, pieces, squares, left_own, left_other,

time: 81.5 us -> 78.6 us (0.964)
  waiting for transfers between devices: 12.3 us -> 7.62 us
  blocking collectives: 11.1 us -> 12.3 us
    ppermute x22, waiting for transfers between devices: 12.3 us -> 7.62 us  [swap(): return lax.ppermute(value, AXES, [(i, i ^ mask) for i in range(32)])]
    all_to_all x1, blocking collectives: 11.1 us -> 12.3 us  [by_columns(): squares = lax.all_to_all(after(sums, left_own), AXES, 0, 0, tiled=True)]
  transfers between devices with their start and end apart: 22 -> 22, of which waited for: 8 -> 7; matrix products, arithmetic and copies ran while one was open for 0% -> 0% of each run, Pallas kernels for 29% -> 31%
where the time goes in v16:
time: 78.6 us; the launch traced here: 78.4 us
  starting transfers between devices  29.2 us (37%)
  Pallas kernels  28.3 us (36%)
  blocking collectives  12.3 us (16%)
  waiting for transfers between devices  7.62 us (10%)
  between operations  0.93 us (1%)
    ppermute x22, starting transfers between devices, swap(): return lax.ppermute(value, AXES, [(i, i ^ mask) for i in range(32)])  29.2 us
    all_to_all x1, blocking collectives, by_columns(): squares = lax.all_to_all(after(sums, left_own), AXES, 0, 0, tiled=True)  12.3 us
    pallas_call x2, Pallas kernels, build(): pl.pallas_call(functools.partial(build_kernel, rel), in_specs=[whole()] *...  9.66 us
    ppermute x22, waiting for transfers between devices, swap(): return lax.ppermute(value, AXES, [(i, i ^ mask) for i in range(32)])  7.62 us
    pallas_call x4, Pallas kernels, forward_part(): pl.pallas_call(functools.partial(forward_kernel, blocks, before is not No...  7.12 us
    pallas_call x5, Pallas kernels, backward_part(): pl.pallas_call(functools.partial(backward_kernel, first, blocks, tuple(ex...  5.19 us
    pallas_call x2, Pallas kernels, product_half(): pl.pallas_call(functools.partial(product_kernel, blocks), in_specs=[whole...  2.64 us
    pallas_call x1, Pallas kernels, prepare(): pl.pallas_call(prepare_kernel, in_specs=[pl.BlockSpec(memory_space=pltpu....  1.63 us
  transfers between devices with their start and end apart: 22, of which 7 were waited for; matrix products, arithmetic and copies ran while one was open for 0% of the time, Pallas kernels for 31%

profile of v16, /device:TPU:0, one launch (start us, length us, event | category | flops | bytes accessed | tf_op | source)
XLA Modules:
  0.0 78.4 jit_solution(5650894658960460186)
XLA Ops:
  0.6 1.6 %prepare.1 = (f32[64,256]{1,0:T(8,128)S(1)}, f32[128,256]{1,0:T(8,128)S(1)}, f32[128,256]{1,0:T(8,128)S(1)}, f32[128,256]{1,0:T(8,128)S(1)}, f32[128,256]{1,0:T(8,128)S(1)}) custom-call(s32[16,512]{1,0:T(8,128)} %bitcast.13, bf16[16,512]{1,0:T(8,128)(2,1)} %bitcast.14, f32[256,256]{1,0:T(8,128)} %right.1, f32[512,256]{1,0:T(8,128)} %left_hbm.1), custom_call_target="tpu_custom_call" | custom-call | bytes 16384 | tf_op jit(solution)/shard_map/prepare/pallas_call | solution.py:74
  2.3 4.1 %collective-permute-start.1 = (f32[64,256]{1,0:T(8,128)S(1)}, f32[64,256]{1,0:T(8,128)S(1)}, u32[]{:S(2)}, u32[]{:S(2)}) collective-permute-start(f32[64,256]{1,0:T(8,128)S(1)} %get-tuple-element.45.e0), channel_id=1, source_target_pairs={{0,16},{1,17},{2,18},{3,19},{4,20},{5,21},{6,22},{7,23},{8,24},{9,... | collective-permute-start | bytes 196616 | tf_op jit(solution)/shard_map/ppermute | solution.py:436
  6.4 1.4 %collective-permute-start.2 = (f32[64,256]{1,0:T(8,128)S(1)}, f32[64,256]{1,0:T(8,128)S(1)}, u32[]{:S(2)}, u32[]{:S(2)}) collective-permute-start(f32[64,256]{1,0:T(8,128)S(1)} %get-tuple-element.45.e0), channel_id=1, source_target_pairs={{0,24},{1,25},{2,26},{3,27},{4,28},{5,29},{6,30},{7,31},{8,16},{9,... | collective-permute-start | bytes 196616 | tf_op jit(solution)/shard_map/ppermute | solution.py:436
  7.7 0.2 collective-permute-start
  8.0 2.8 %collective-permute-start.4 = (f32[128,256]{1,0:T(8,128)S(1)}, f32[128,256]{1,0:T(8,128)S(1)}, u32[]{:S(2)}, u32[]{:S(2)}) collective-permute-start(f32[128,256]{1,0:T(8,128)S(1)} %get-tuple-element.51), channel_id=1, source_target_pairs={{0,16},{1,17},{2,18},{3,19},{4,20},{5,21},{6,22},{7,23},{8,24},{9,... | collective-permute-start | bytes 393224 | tf_op jit(solution)/shard_map/ppermute | solution.py:436
  10.8 1.4 %collective-permute-start.5 = (f32[128,256]{1,0:T(8,128)S(1)}, f32[128,256]{1,0:T(8,128)S(1)}, u32[]{:S(2)}, u32[]{:S(2)}) collective-permute-start(f32[128,256]{1,0:T(8,128)S(1)} %get-tuple-element.52), channel_id=1, source_target_pairs={{0,24},{1,25},{2,26},{3,27},{4,28},{5,29},{6,30},{7,31},{8,16},{9,... | collective-permute-start | bytes 393224 | tf_op jit(solution)/shard_map/ppermute | solution.py:436
  12.1 0.6 collective-permute-start.3
  12.7 0.5 collective-permute-done.2.e3
  13.3 4.7 %dense_rows.2 = (bf16[16,1024,256]{2,1,0:T(8,128)(2,1)S(1)}, bf16[16,1024,256]{2,1,0:T(8,128)(2,1)S(1)}, f32[8,128]{1,0:T(8,128)S(1)}) custom-call(f32[64,256]{1,0:T(8,128)S(1)} %get-tuple-element.45.e0, f32[64,256]{1,0:T(8,128)S(1)} %collective-permute-done.e1, f32[64,256]{1,0:T(8,128)S(1)} %collective-permute-done.1.e2, ...), custom_call_target="tpu_custom_call" | custom-call | flops 2147483648 | bytes 16777216 | tf_op jit(solution)/shard_map/dense_rows/pallas_call | solution.py:154
  18.1 3.6 %collective-permute-done.4.m2.refs_2_ = f32[128,256]{1,0:T(8,128)S(1)} collective-permute-done((f32[128,256]{1,0:T(8,128)S(1)}, f32[128,256]{1,0:T(8,128)S(1)}, u32[]{:S(2)}, u32[]{:S(2)}) %collective-permute-start.4) | collective-permute-done | bytes 131104 | tf_op jit(solution)/shard_map/ppermute | solution.py:436
  21.7 0.1 collective-permute-done.3.m1.refs_1_
  21.8 0.1 collective-permute-start.7
  21.9 1.8 %collective-permute-start.6 = (f32[4,64,256]{2,1,0:T(8,128)S(1)}, f32[4,64,256]{2,1,0:T(8,128)S(1)}, u32[]{:S(2)}, u32[]{:S(2)}) collective-permute-start(f32[4,64,256]{2,1,0:T(8,128)S(1)} %stack_right.1.refs_0_.right), channel_id=1, source_target_pairs={{0,4},{1,5},{2,6},{3,7},{4,0},{5,1},{6,2},{7,3},{8,12},{9,13},{10,... | collective-permute-start | bytes 786440 | tf_op jit(solution)/shard_map/ppermute | solution.py:436
  23.6 4.9 %dense_rows.3 = (bf16[16,1024,256]{2,1,0:T(8,128)(2,1)S(1)}, bf16[16,1024,256]{2,1,0:T(8,128)(2,1)S(1)}, f32[8,128]{1,0:T(8,128)S(1)}) custom-call(f32[64,256]{1,0:T(8,128)S(1)} %get-tuple-element.45.e0, f32[64,256]{1,0:T(8,128)S(1)} %collective-permute-done.e1, f32[64,256]{1,0:T(8,128)S(1)} %collective-permute-done.1.e2, ...), custom_call_target="tpu_custom_call" | custom-call | flops 33554432 | bytes 262144 | tf_op jit(solution)/shard_map/dense_rows/pallas_call | solution.py:154
  28.6 2.3 %forward_part.4.refs_1_ = f32[1024,128]{1,0:T(8,128)S(1)} custom-call(bf16[16,1024,256]{2,1,0:T(8,128)(2,1)S(1)} %get-tuple-element.46.hi_ref, bf16[16,1024,256]{2,1,0:T(8,128)(2,1)S(1)} %get-tuple-element.47.lo_ref, f32[4,64,256]{2,1,0:T(8,128)S(1)} %stack_right.1.refs_0_.right, f32[4,64,256]{2,1,0:T(8,128)S(1)} %collective-permute-done.7.refs_1_, ...), custom_call_target="tpu_custom_call" | custom-call | flops 67108864 | bytes 131072 | tf_op jit(solution)/shard_map/forward_part/pallas_call | solution.py:196
  30.9 0.3 collective-permute-start.8
  31.2 1.2 %forward_part.5.before = f32[1024,128]{1,0:T(8,128)S(1)} custom-call(bf16[16,1024,256]{2,1,0:T(8,128)(2,1)S(1)} %get-tuple-element.46.hi_ref, bf16[16,1024,256]{2,1,0:T(8,128)(2,1)S(1)} %get-tuple-element.47.lo_ref, f32[4,64,256]{2,1,0:T(8,128)S(1)} %collective-permute-done.6.refs_0_, f32[1024,128]{1,0:T(8,128)S(1)} %forward_part.4.refs_1_), custom_call_target="tpu_custom_call" | custom-call | flops 33554432 | bytes 65536 | tf_op jit(solution)/shard_map/forward_part/pallas_call | solution.py:196
  32.4 0.1 collective-permute-done.8.vec
  32.5 1.3 %product_half.2.mine = f32[64,1024]{1,0:T(8,128)S(1)} custom-call(bf16[16,1024,256]{2,1,0:T(8,128)(2,1)S(1)} %get-tuple-element.46.hi_ref, bf16[16,1024,256]{2,1,0:T(8,128)(2,1)S(1)} %get-tuple-element.47.lo_ref, f32[4,64,256]{2,1,0:T(8,128)S(1)} %collective-permute-done.8.vec, f32[1024,128]{1,0:T(8,128)S(1)} %forward_part.5.before), custom_call_target="tpu_custom_call" | custom-call | flops 33554432 | bytes 65536 | tf_op jit(solution)/shard_map/product_half/pallas_call | solution.py:228
  33.8 1.6 %collective-permute-start.10 = (f32[64,1024]{1,0:T(8,128)S(1)}, f32[64,1024]{1,0:T(8,128)S(1)}, u32[]{:S(2)}, u32[]{:S(2)}) collective-permute-start(f32[64,1024]{1,0:T(8,128)S(1)} %product_half.2.mine), channel_id=1, source_target_pairs={{0,1},{1,0},{2,3},{3,2},{4,5},{5,4},{6,7},{7,6},{8,9},{9,8},{10,11... | collective-permute-start | bytes 786440 | tf_op jit(solution)/shard_map/ppermute | solution.py:436
  35.4 2.3 %forward_part.6.refs_1_ = f32[1024,128]{1,0:T(8,128)S(1)} custom-call(bf16[16,1024,256]{2,1,0:T(8,128)(2,1)S(1)} %get-tuple-element.56.hi_ref, bf16[16,1024,256]{2,1,0:T(8,128)(2,1)S(1)} %get-tuple-element.57.lo_ref, f32[4,64,256]{2,1,0:T(8,128)S(1)} %stack_right.1.refs_0_.right, f32[4,64,256]{2,1,0:T(8,128)S(1)} %collective-permute-done.7.refs_1_), custom_call_target="tpu_custom_call" | custom-call | flops 67108864 | bytes 131072 | tf_op jit(solution)/shard_map/forward_part/pallas_call | solution.py:196
  37.8 1.2 %forward_part.7.before = f32[1024,128]{1,0:T(8,128)S(1)} custom-call(bf16[16,1024,256]{2,1,0:T(8,128)(2,1)S(1)} %get-tuple-element.56.hi_ref, bf16[16,1024,256]{2,1,0:T(8,128)(2,1)S(1)} %get-tuple-element.57.lo_ref, f32[4,64,256]{2,1,0:T(8,128)S(1)} %collective-permute-done.6.refs_0_, f32[1024,128]{1,0:T(8,128)S(1)} %forward_part.6.refs_1_), custom_call_target="tpu_custom_call" | custom-call | flops 33554432 | bytes 65536 | tf_op jit(solution)/shard_map/forward_part/pallas_call | solution.py:196
  39.0 1.3 %product_half.3.mine = f32[64,1024]{1,0:T(8,128)S(1)} custom-call(bf16[16,1024,256]{2,1,0:T(8,128)(2,1)S(1)} %get-tuple-element.56.hi_ref, bf16[16,1024,256]{2,1,0:T(8,128)(2,1)S(1)} %get-tuple-element.57.lo_ref, f32[4,64,256]{2,1,0:T(8,128)S(1)} %collective-permute-done.8.vec, f32[1024,128]{1,0:T(8,128)S(1)} %forward_part.7.before, ...), custom_call_target="tpu_custom_call" | custom-call | flops 33554432 | bytes 65536 | tf_op jit(solution)/shard_map/product_half/pallas_call | solution.py:228
  40.4 0.5 collective-permute-start.9
  40.9 1.4 %collective-permute-done.10.other = f32[64,1024]{1,0:T(8,128)S(1)} collective-permute-done((f32[64,1024]{1,0:T(8,128)S(1)}, f32[64,1024]{1,0:T(8,128)S(1)}, u32[]{:S(2)}, u32[]{:S(2)}) %collective-permute-start.10) | collective-permute-done | bytes 262176 | tf_op jit(solution)/shard_map/ppermute | solution.py:436
  42.3 0.2 left_half.2
  42.5 3.0 %collective-permute-start.18 = (f32[64,256]{1,0:T(8,128)S(1)}, f32[64,256]{1,0:T(8,128)S(1)}, u32[]{:S(2)}, u32[]{:S(2)}) collective-permute-start(f32[64,256]{1,0:T(8,128)S(1)} %get-tuple-element.71), channel_id=1, source_target_pairs={{0,8},{1,9},{2,10},{3,11},{4,12},{5,13},{6,14},{7,15},{8,0},{9,1},... | collective-permute-start | bytes 196616 | tf_op jit(solution)/shard_map/ppermute | solution.py:436
  45.5 1.8 %collective-permute-start.19 = (f32[64,256]{1,0:T(8,128)S(1)}, f32[64,256]{1,0:T(8,128)S(1)}, u32[]{:S(2)}, u32[]{:S(2)}) collective-permute-start(f32[64,256]{1,0:T(8,128)S(1)} %get-tuple-element.72), channel_id=1, source_target_pairs={{0,16},{1,17},{2,18},{3,19},{4,20},{5,21},{6,22},{7,23},{8,24},{9,... | collective-permute-start | bytes 196616 | tf_op jit(solution)/shard_map/ppermute | solution.py:436
  47.3 1.4 %collective-permute-start.20 = (f32[64,256]{1,0:T(8,128)S(1)}, f32[64,256]{1,0:T(8,128)S(1)}, u32[]{:S(2)}, u32[]{:S(2)}) collective-permute-start(f32[64,256]{1,0:T(8,128)S(1)} %get-tuple-element.73), channel_id=1, source_target_pairs={{0,24},{1,25},{2,26},{3,27},{4,28},{5,29},{6,30},{7,31},{8,16},{9,... | collective-permute-start | bytes 196616 | tf_op jit(solution)/shard_map/ppermute | solution.py:436
  48.7 2.3 %backward_part.5.refs_1_.refs_0_ = f32[1024,256]{1,0:T(8,128)S(1)} custom-call(bf16[16,1024,256]{2,1,0:T(8,128)(2,1)S(1)} %get-tuple-element.56.hi_ref, bf16[16,1024,256]{2,1,0:T(8,128)(2,1)S(1)} %get-tuple-element.57.lo_ref, bf16[128,1024]{1,0:T(8,128)(2,1)S(1)} %get-tuple-element.59.both_ref), custom_call_target="tpu_custom_call" | custom-call | flops 134217728 | bytes 262144 | tf_op jit(solution)/shard_map/backward_part/pallas_call | solution.py:309
  51.0 0.2 left_half.3
  51.2 0.7 backward_part.7.refs_1_.near
  51.9 0.7 backward_part.9
  52.6 0.1 collective-permute-start.12
  52.7 0.7 backward_part.8.token
  53.4 0.6 collective-permute-start.11
  54.0 0.2 collective-permute-done.12.far
  54.3 1.4 %collective-permute-start.14 = (f32[128,256]{1,0:T(8,128)S(1)}, f32[128,256]{1,0:T(8,128)S(1)}, u32[]{:S(2)}, u32[]{:S(2)}) collective-permute-start(f32[128,256]{1,0:T(8,128)S(1)} %get-tuple-element.64), channel_id=1, source_target_pairs={{0,4},{1,5},{2,6},{3,7},{4,0},{5,1},{6,2},{7,3},{8,12},{9,13},{10,... | collective-permute-start | bytes 393224 | tf_op jit(solution)/shard_map/ppermute | solution.py:436
  55.7 0.8 collective-permute-start.13
  56.5 1.9 %collective-permute-start.21 = (f32[4,64,256]{2,1,0:T(8,128)S(1)}, f32[4,64,256]{2,1,0:T(8,128)S(1)}, u32[]{:S(2)}, u32[]{:S(2)}) collective-permute-start(f32[4,64,256]{2,1,0:T(8,128)S(1)} %stack_left.1.own), channel_id=1, source_target_pairs={{0,1},{1,0},{2,3},{3,2},{4,5},{5,4},{6,7},{7,6},{8,9},{9,8},{10,11... | collective-permute-start | bytes 786440 | tf_op jit(solution)/shard_map/ppermute | solution.py:436
  58.4 0.7 backward_part.6.keep
  59.1 1.6 %collective-permute-done.14.got = f32[128,256]{1,0:T(8,128)S(1)} collective-permute-done((f32[128,256]{1,0:T(8,128)S(1)}, f32[128,256]{1,0:T(8,128)S(1)}, u32[]{:S(2)}, u32[]{:S(2)}) %collective-permute-start.14) | collective-permute-done | bytes 131104 | tf_op jit(solution)/shard_map/ppermute | solution.py:436
  60.7 2.3 %collective-permute-start.16 = (f32[64,256]{1,0:T(8,128)S(1)}, f32[64,256]{1,0:T(8,128)S(1)}, u32[]{:S(2)}, u32[]{:S(2)}) collective-permute-start(f32[64,256]{1,0:T(8,128)S(1)} %get-tuple-element.65.g2), channel_id=1, source_target_pairs={{0,16},{1,17},{2,18},{3,19},{4,20},{5,21},{6,22},{7,23},{8,24},{9,... | collective-permute-start | bytes 196616 | tf_op jit(solution)/shard_map/ppermute | solution.py:436
  63.0 0.8 %collective-permute-start.17 = (f32[64,256]{1,0:T(8,128)S(1)}, f32[64,256]{1,0:T(8,128)S(1)}, u32[]{:S(2)}, u32[]{:S(2)}) collective-permute-start(f32[64,256]{1,0:T(8,128)S(1)} %get-tuple-element.66.g3), channel_id=1, source_target_pairs={{0,24},{1,25},{2,26},{3,27},{4,28},{5,29},{6,30},{7,31},{8,16},{9,... | collective-permute-start | bytes 196616 | tf_op jit(solution)/shard_map/ppermute | solution.py:436
  63.8 0.3 right_norm.1
  64.1 0.5 collective-permute-start.15
  64.7 12.3 %all_to_all.5.squares = f32[32,1,128]{2,1,0:T(1,128)S(1)} all-to-all(f32[32,1,128]{2,1,0:T(1,128)S(1)} %bitcast.9), channel_id=1, replica_groups=mesh['doc'=16,'feat'=2] {'doc','feat'}, dimensions={0} | all-to-all | bytes 32768 | tf_op jit(solution)/shard_map/all_to_all | solution.py:493
  77.0 1.3 %finish.1 = (f32[512,256]{1,0:T(8,128)}, f32[256,256]{1,0:T(8,128)}, f32[256,256]{1,0:T(8,128)}, f32[256,256]{1,0:T(8,128)}, f32[1,256]{1,0:T(1,128)}, /*index=5*/f32[1,256]{1,0:T(1,128)}, f32[1,256]{1,0:T(1,128)}) custom-call(f32[64,256]{1,0:T(8,128)S(1)} %get-tuple-element.67.g0, f32[64,256]{1,0:T(8,128)S(1)} %collective-permute-done.15.g1, ...), custom_call_target="tpu_custom_call" | custom-call | flops 16384 | bytes 20480 | tf_op jit(solution)/shard_map/finish/pallas_call | solution.py:425
  (35 shorter events, 0.2 us)
Async XLA Ops:
  2.3 9.9 %collective-permute-start.1 = (f32[64,256]{1,0:T(8,128)S(1)}, f32[64,256]{1,0:T(8,128)S(1)}, u32[]{:S(2)}, u32[]{:S(2)}) collective-permute-start(f32[64,256]{1,0:T(8,128)S(1)} %get-tuple-element.45.e0), channel_id=1, source_target_pairs={{0,16},{1,17},{2,18},{3,19},{4,20},{5,21},{6,22},{7,23},{8,24},{9,... | collective-permute-start | bytes 196616 | tf_op jit(solution)/shard_map/ppermute | solution.py:436
  6.4 6.9 %collective-permute-start.2 = (f32[64,256]{1,0:T(8,128)S(1)}, f32[64,256]{1,0:T(8,128)S(1)}, u32[]{:S(2)}, u32[]{:S(2)}) collective-permute-start(f32[64,256]{1,0:T(8,128)S(1)} %get-tuple-element.45.e0), channel_id=1, source_target_pairs={{0,24},{1,25},{2,26},{3,27},{4,28},{5,29},{6,30},{7,31},{8,16},{9,... | collective-permute-start | bytes 196616 | tf_op jit(solution)/shard_map/ppermute | solution.py:436
  7.7 5.6 %collective-permute-start = (f32[64,256]{1,0:T(8,128)S(1)}, f32[64,256]{1,0:T(8,128)S(1)}, u32[]{:S(2)}, u32[]{:S(2)}) collective-permute-start(f32[64,256]{1,0:T(8,128)S(1)} %get-tuple-element.45.e0), channel_id=1, source_target_pairs={{0,8},{1,9},{2,10},{3,11},{4,12},{5,13},{6,14},{7,15},{8,0},{9,1},... | collective-permute-start | bytes 196616 | tf_op jit(solution)/shard_map/ppermute | solution.py:436
  8.0 13.7 %collective-permute-start.4 = (f32[128,256]{1,0:T(8,128)S(1)}, f32[128,256]{1,0:T(8,128)S(1)}, u32[]{:S(2)}, u32[]{:S(2)}) collective-permute-start(f32[128,256]{1,0:T(8,128)S(1)} %get-tuple-element.51), channel_id=1, source_target_pairs={{0,16},{1,17},{2,18},{3,19},{4,20},{5,21},{6,22},{7,23},{8,24},{9,... | collective-permute-start | bytes 393224 | tf_op jit(solution)/shard_map/ppermute | solution.py:436
  10.8 10.9 %collective-permute-start.5 = (f32[128,256]{1,0:T(8,128)S(1)}, f32[128,256]{1,0:T(8,128)S(1)}, u32[]{:S(2)}, u32[]{:S(2)}) collective-permute-start(f32[128,256]{1,0:T(8,128)S(1)} %get-tuple-element.52), channel_id=1, source_target_pairs={{0,24},{1,25},{2,26},{3,27},{4,28},{5,29},{6,30},{7,31},{8,16},{9,... | collective-permute-start | bytes 393224 | tf_op jit(solution)/shard_map/ppermute | solution.py:436
  12.1 9.6 %collective-permute-start.3 = (f32[128,256]{1,0:T(8,128)S(1)}, f32[128,256]{1,0:T(8,128)S(1)}, u32[]{:S(2)}, u32[]{:S(2)}) collective-permute-start(f32[128,256]{1,0:T(8,128)S(1)} %get-tuple-element.50), channel_id=1, source_target_pairs={{0,8},{1,9},{2,10},{3,11},{4,12},{5,13},{6,14},{7,15},{8,0},{9,1},... | collective-permute-start | bytes 393224 | tf_op jit(solution)/shard_map/ppermute | solution.py:436
  21.8 13.6 %copy-start = (f32[4,64,256]{2,1,0:T(8,128)}, f32[4,64,256]{2,1,0:T(8,128)S(1)}, u32[]{:S(2)}) copy-start(f32[4,64,256]{2,1,0:T(8,128)S(1)} %stack_right.1.refs_0_.right) | copy-start | bytes 786436
  21.8 6.8 %collective-permute-start.7 = (f32[4,64,256]{2,1,0:T(8,128)S(1)}, f32[4,64,256]{2,1,0:T(8,128)S(1)}, u32[]{:S(2)}, u32[]{:S(2)}) collective-permute-start(f32[4,64,256]{2,1,0:T(8,128)S(1)} %stack_right.1.refs_0_.right), channel_id=1, source_target_pairs={{0,2},{1,3},{2,0},{3,1},{4,6},{5,7},{6,4},{7,5},{8,10},{9,11},{10,... | collective-permute-start | bytes 786440 | tf_op jit(solution)/shard_map/ppermute | solution.py:436
  21.9 9.0 %collective-permute-start.6 = (f32[4,64,256]{2,1,0:T(8,128)S(1)}, f32[4,64,256]{2,1,0:T(8,128)S(1)}, u32[]{:S(2)}, u32[]{:S(2)}) collective-permute-start(f32[4,64,256]{2,1,0:T(8,128)S(1)} %stack_right.1.refs_0_.right), channel_id=1, source_target_pairs={{0,4},{1,5},{2,6},{3,7},{4,0},{5,1},{6,2},{7,3},{8,12},{9,13},{10,... | collective-permute-start | bytes 786440 | tf_op jit(solution)/shard_map/ppermute | solution.py:436
  30.9 1.6 %collective-permute-start.8 = (f32[4,64,256]{2,1,0:T(8,128)S(1)}, f32[4,64,256]{2,1,0:T(8,128)S(1)}, u32[]{:S(2)}, u32[]{:S(2)}) collective-permute-start(f32[4,64,256]{2,1,0:T(8,128)S(1)} %collective-permute-done.6.refs_0_), channel_id=1, source_target_pairs={{0,2},{1,3},{2,0},{3,1},{4,6},{5,7},{6,4},{7,5},{8,10},{9,11},{10,... | collective-permute-start | bytes 786440 | tf_op jit(solution)/shard_map/ppermute | solution.py:436
  33.8 8.5 %collective-permute-start.10 = (f32[64,1024]{1,0:T(8,128)S(1)}, f32[64,1024]{1,0:T(8,128)S(1)}, u32[]{:S(2)}, u32[]{:S(2)}) collective-permute-start(f32[64,1024]{1,0:T(8,128)S(1)} %product_half.2.mine), channel_id=1, source_target_pairs={{0,1},{1,0},{2,3},{3,2},{4,5},{5,4},{6,7},{7,6},{8,9},{9,8},{10,11... | collective-permute-start | bytes 786440 | tf_op jit(solution)/shard_map/ppermute | solution.py:436
  37.8 1.3 %copy-start.5 = (f32[256]{0:T(256)S(1)}, f32[256]{0:T(256)}, u32[]{:S(2)}) copy-start(f32[256]{0:T(256)} %param.15) | copy-start | bytes 3076
  40.4 10.7 %collective-permute-start.9 = (f32[64,1024]{1,0:T(8,128)S(1)}, f32[64,1024]{1,0:T(8,128)S(1)}, u32[]{:S(2)}, u32[]{:S(2)}) collective-permute-start(f32[64,1024]{1,0:T(8,128)S(1)} %product_half.3.mine), channel_id=1, source_target_pairs={{0,1},{1,0},{2,3},{3,2},{4,5},{5,4},{6,7},{7,6},{8,9},{9,8},{10,11... | collective-permute-start | bytes 786440 | tf_op jit(solution)/shard_map/ppermute | solution.py:436
  42.5 11.5 %collective-permute-start.18 = (f32[64,256]{1,0:T(8,128)S(1)}, f32[64,256]{1,0:T(8,128)S(1)}, u32[]{:S(2)}, u32[]{:S(2)}) collective-permute-start(f32[64,256]{1,0:T(8,128)S(1)} %get-tuple-element.71), channel_id=1, source_target_pairs={{0,8},{1,9},{2,10},{3,11},{4,12},{5,13},{6,14},{7,15},{8,0},{9,1},... | collective-permute-start | bytes 196616 | tf_op jit(solution)/shard_map/ppermute | solution.py:436
  45.5 8.5 %collective-permute-start.19 = (f32[64,256]{1,0:T(8,128)S(1)}, f32[64,256]{1,0:T(8,128)S(1)}, u32[]{:S(2)}, u32[]{:S(2)}) collective-permute-start(f32[64,256]{1,0:T(8,128)S(1)} %get-tuple-element.72), channel_id=1, source_target_pairs={{0,16},{1,17},{2,18},{3,19},{4,20},{5,21},{6,22},{7,23},{8,24},{9,... | collective-permute-start | bytes 196616 | tf_op jit(solution)/shard_map/ppermute | solution.py:436
  47.3 6.7 %collective-permute-start.20 = (f32[64,256]{1,0:T(8,128)S(1)}, f32[64,256]{1,0:T(8,128)S(1)}, u32[]{:S(2)}, u32[]{:S(2)}) collective-permute-start(f32[64,256]{1,0:T(8,128)S(1)} %get-tuple-element.73), channel_id=1, source_target_pairs={{0,24},{1,25},{2,26},{3,27},{4,28},{5,29},{6,30},{7,31},{8,16},{9,... | collective-permute-start | bytes 196616 | tf_op jit(solution)/shard_map/ppermute | solution.py:436
  52.6 1.6 %collective-permute-start.12 = (f32[264,256]{1,0:T(8,128)S(1)}, f32[264,256]{1,0:T(8,128)S(1)}, u32[]{:S(2)}, u32[]{:S(2)}) collective-permute-start(f32[264,256]{1,0:T(8,128)S(1)} %backward_part.9), channel_id=1, source_target_pairs={{0,2},{1,3},{2,0},{3,1},{4,6},{5,7},{6,4},{7,5},{8,10},{9,11},{10,... | collective-permute-start | bytes 811016 | tf_op jit(solution)/shard_map/ppermute | solution.py:436
  53.4 5.7 %collective-permute-start.11 = (f32[256,256]{1,0:T(8,128)S(1)}, f32[256,256]{1,0:T(8,128)S(1)}, u32[]{:S(2)}, u32[]{:S(2)}) collective-permute-start(f32[256,256]{1,0:T(8,128)S(1)} %backward_part.8.token), channel_id=1, source_target_pairs={{0,2},{1,3},{2,0},{3,1},{4,6},{5,7},{6,4},{7,5},{8,10},{9,11},{10,... | collective-permute-start | bytes 786440 | tf_op jit(solution)/shard_map/ppermute | solution.py:436
  54.3 6.4 %collective-permute-start.14 = (f32[128,256]{1,0:T(8,128)S(1)}, f32[128,256]{1,0:T(8,128)S(1)}, u32[]{:S(2)}, u32[]{:S(2)}) collective-permute-start(f32[128,256]{1,0:T(8,128)S(1)} %get-tuple-element.64), channel_id=1, source_target_pairs={{0,4},{1,5},{2,6},{3,7},{4,0},{5,1},{6,2},{7,3},{8,12},{9,13},{10,... | collective-permute-start | bytes 393224 | tf_op jit(solution)/shard_map/ppermute | solution.py:436
  55.7 8.1 %copy-start.1 = (f32[4,64,256]{2,1,0:T(8,128)S(1)}, f32[4,64,256]{2,1,0:T(8,128)}, u32[]{:S(2)}) copy-start(f32[4,64,256]{2,1,0:T(8,128)} %copy-done) | copy-start | bytes 786436
  55.7 21.3 %copy-start.2 = (f32[256,256]{1,0:T(8,128)S(1)}, f32[256,256]{1,0:T(8,128)}, u32[]{:S(2)}) copy-start(f32[256,256]{1,0:T(8,128)} %right.1) | copy-start | bytes 786436
  55.7 21.3 %copy-start.3 = (f32[256,256]{1,0:T(8,128)S(1)}, f32[256,256]{1,0:T(8,128)}, u32[]{:S(2)}) copy-start(f32[256,256]{1,0:T(8,128)} %search.1) | copy-start | bytes 786436
  55.7 21.4 %copy-start.4 = (f32[256,256]{1,0:T(8,128)S(1)}, f32[256,256]{1,0:T(8,128)}, u32[]{:S(2)}) copy-start(f32[256,256]{1,0:T(8,128)} %solution.1) | copy-start | bytes 786436
  55.7 21.4 %copy-start.6 = (f32[256]{0:T(256)S(1)}, f32[256]{0:T(256)}, u32[]{:S(2)}) copy-start(f32[256]{0:T(256)} %param.16) | copy-start | bytes 3076
  55.7 21.4 %copy-start.7 = (f32[256]{0:T(256)S(1)}, f32[256]{0:T(256)}, u32[]{:S(2)}) copy-start(f32[256]{0:T(256)} %param.17) | copy-start | bytes 3076
  55.7 8.1 %collective-permute-start.13 = (f32[136,256]{1,0:T(8,128)S(1)}, f32[136,256]{1,0:T(8,128)S(1)}, u32[]{:S(2)}, u32[]{:S(2)}) collective-permute-start(f32[136,256]{1,0:T(8,128)S(1)} %get-tuple-element.62), channel_id=1, source_target_pairs={{0,4},{1,5},{2,6},{3,7},{4,0},{5,1},{6,2},{7,3},{8,12},{9,13},{10,... | collective-permute-start | bytes 417800 | tf_op jit(solution)/shard_map/ppermute | solution.py:436
  56.5 20.5 %collective-permute-start.21 = (f32[4,64,256]{2,1,0:T(8,128)S(1)}, f32[4,64,256]{2,1,0:T(8,128)S(1)}, u32[]{:S(2)}, u32[]{:S(2)}) collective-permute-start(f32[4,64,256]{2,1,0:T(8,128)S(1)} %stack_left.1.own), channel_id=1, source_target_pairs={{0,1},{1,0},{2,3},{3,2},{4,5},{5,4},{6,7},{7,6},{8,9},{9,8},{10,11... | collective-permute-start | bytes 786440 | tf_op jit(solution)/shard_map/ppermute | solution.py:436
  60.7 16.3 %collective-permute-start.16 = (f32[64,256]{1,0:T(8,128)S(1)}, f32[64,256]{1,0:T(8,128)S(1)}, u32[]{:S(2)}, u32[]{:S(2)}) collective-permute-start(f32[64,256]{1,0:T(8,128)S(1)} %get-tuple-element.65.g2), channel_id=1, source_target_pairs={{0,16},{1,17},{2,18},{3,19},{4,20},{5,21},{6,22},{7,23},{8,24},{9,... | collective-permute-start | bytes 196616 | tf_op jit(solution)/shard_map/ppermute | solution.py:436
  63.0 14.0 %collective-permute-start.17 = (f32[64,256]{1,0:T(8,128)S(1)}, f32[64,256]{1,0:T(8,128)S(1)}, u32[]{:S(2)}, u32[]{:S(2)}) collective-permute-start(f32[64,256]{1,0:T(8,128)S(1)} %get-tuple-element.66.g3), channel_id=1, source_target_pairs={{0,24},{1,25},{2,26},{3,27},{4,28},{5,29},{6,30},{7,31},{8,16},{9,... | collective-permute-start | bytes 196616 | tf_op jit(solution)/shard_map/ppermute | solution.py:436
  64.1 12.9 %collective-permute-start.15 = (f32[64,256]{1,0:T(8,128)S(1)}, f32[64,256]{1,0:T(8,128)S(1)}, u32[]{:S(2)}, u32[]{:S(2)}) collective-permute-start(f32[64,256]{1,0:T(8,128)S(1)} %get-tuple-element.68), channel_id=1, source_target_pairs={{0,8},{1,9},{2,10},{3,11},{4,12},{5,13},{6,14},{7,15},{8,0},{9,1},... | collective-permute-start | bytes 196616 | tf_op jit(solution)/shard_map/ppermute | solution.py:436

commit v17 on v16

--- a/solution.py
+++ b/solution.py
@@ -38,8 +38,8 @@
     return jax.ShapeDtypeStruct(shape, jnp.bfloat16)
 
 
-def prepare_kernel(ids_hbm, vals_hbm, right_hbm, left_hbm, stored, m0, m1, m2, m3,
-                   ids, vals, wide, right, left, turned, arrived):
+def prepare_kernel(ids_hbm, vals_hbm, right_hbm, left_hbm, other, m0, m1, m2, m3,
+                   ids, vals, wide, lines, right, left, turned, arrived):
     _, z, y = coords()
     q, rows = turned.shape[1:]
     copies = [
@@ -53,33 +53,38 @@
     ]
     for copy in copies:
         copy.start()
-    lines, count = stored.shape[0] // 2, ids.shape[0]
+    count, n = ids.shape[0], lines.shape[0]
+    half = n // 2
     for part, ref in enumerate((ids, vals)):
         copies[part].wait()
         wide[...] = ref[...].astype(jnp.float32).T
         for r in range(256 // count):
-            stored[part * lines : (part + 1) * lines, r * count : (r + 1) * count] = wide[
-                pl.ds(r, lines, stride=256 // count), :
-            ]
-    for part, ref in enumerate((right, left)):
-        copies[2 + part].wait()
+            lines[:, r * count : (r + 1) * count] = wide[pl.ds(r, n, stride=256 // count), :]
+        at = slice(part * half, (part + 1) * half)
+        other[at, :] = lines[pl.ds(pl.multiple_of((1 - y) * half, half), half), :]
+        own = lines[pl.ds(pl.multiple_of(y * half, half), half), :]
+        for out in (m0, m1, m2, m3):
+            out[at, :] = own
+    for part, (copy, ref) in enumerate(zip(copies[2:], (right, left))):
+        copy.wait()
         turned[...] = ref[...].T.reshape(turned.shape)
         for k, out in enumerate((m0, m1, m2, m3)):
-            out[part * q : (part + 1) * q, :] = turned[z ^ k]
+            out[n + part * q : n + (part + 1) * q, :] = turned[z ^ k]
 
 
 def prepare(ids, vals, right, left):
     rows, cols = right.shape
-    q = cols // 4
+    n, q = ids.size // 256, cols // 4
     got = pl.pallas_call(
         prepare_kernel,
         in_specs=[pl.BlockSpec(memory_space=pltpu.HBM)] * 4,
         out_specs=[whole()] * 5,
-        out_shape=[pltpu.VMEM((ids.size // 128, 256), jnp.float32)] + [pltpu.VMEM((2 * q, rows), jnp.float32)] * 4,
+        out_shape=[pltpu.VMEM((n, 256), jnp.float32)] + [pltpu.VMEM((n + 2 * q, rows), jnp.float32)] * 4,
         scratch_shapes=[
             pltpu.VMEM(ids.shape, jnp.int32),
             pltpu.VMEM(vals.shape, jnp.bfloat16),
             pltpu.VMEM(ids.shape[::-1], jnp.float32),
+            pltpu.VMEM((n, 256), jnp.float32),
             pltpu.VMEM(right.shape, jnp.float32),
             pltpu.VMEM(right.shape, jnp.float32),
             pltpu.VMEM((4, q, rows), jnp.float32),
@@ -95,7 +100,8 @@
 def stack_kernel(m0, m1, m2, m3, *refs):
     out = refs[-1]
     for k, m in enumerate((m0, m1, m2, m3)):
-        out[k] = m[0 : out.shape[1], :]
+        at = m.shape[0] - 2 * out.shape[1] if m.shape[0] > out.shape[1] else 0
+        out[k] = m[at : at + out.shape[1], :]
 
 
 def stack(messages, q, name, *tokens):
@@ -109,11 +115,11 @@
     )(*messages, *tokens)
 
 
-def build_kernel(rel, e0, e1, e2, e3, *refs):
+def build_kernel(e0, e1, e2, e3, *refs):
     hi_ref, lo_ref, token = refs[-3:]
     token[...] = jnp.zeros_like(token)
-    d, _, y = coords()
-    n = e0.shape[0] // 2
+    d, _, _ = coords()
+    n = hi_ref.shape[1] // 64
     iota = lax.broadcasted_iota(jnp.int32, (256, 256), 0).astype(jnp.float32).astype(jnp.bfloat16)
     lane_doc = lax.broadcasted_iota(jnp.int32, (8, 256), 1) >> 4
     one = jnp.ones((256, 256), jnp.bfloat16)
@@ -125,9 +131,9 @@
 
     for k, entries in enumerate((e0, e1, e2, e3)):
 
-        @pl.loop(0, n // 16)
+        @pl.loop(0, n // 8)
         def _(step, k=k, entries=entries):
-            at = pl.multiple_of((y ^ rel) * (n // 2) + step * 8, 8)
+            at = pl.multiple_of(step * 8, 8)
             ids = entries[pl.ds(at, 8), :].astype(jnp.int32)
             vals = entries[pl.ds(n + at, 8), :]
             owner = (ids >> 8) ^ d
@@ -140,7 +146,7 @@
                 dense = lax.dot_general(pick, weigh, NT, preferred_element_type=jnp.float32)
                 high = dense.astype(jnp.bfloat16)
                 low = (dense - high.astype(jnp.float32)).astype(jnp.bfloat16)
-                docs = pl.ds(pl.multiple_of(k * 8 * n + step * 128 + 16 * t, 16), 16)
+                docs = pl.ds(pl.multiple_of(k * 16 * n + step * 128 + 16 * t, 16), 16)
                 hi_ref[:, docs, :] = high.reshape(16, 16, 256)
                 lo_ref[:, docs, :] = low.reshape(16, 16, 256)
 
@@ -149,15 +155,15 @@
     return pl.BlockSpec(memory_space=pltpu.VMEM)
 
 
-def build(entries, rel, *tokens):
-    docs = 4 * (entries[0].shape[0] // 4 * 16)
+def build(entries, lines, scale, *tokens):
+    docs = 4 * (lines // 2 * 16)
     *rows, token = pl.pallas_call(
-        functools.partial(build_kernel, rel),
+        build_kernel,
         in_specs=[whole()] * (4 + len(tokens)),
         out_specs=[whole()] * 3,
         out_shape=[pltpu.VMEM((16, docs, 256), jnp.bfloat16)] * 2 + [f32(8, 128)],
         compiler_params=params(8),
-        cost_estimate=cost(2 * docs * 16 * 256 * 256, docs * 4096 * 4, 1 if rel else 64),
+        cost_estimate=cost(2 * docs * 16 * 256 * 256, docs * 4096 * 4, scale),
         name="dense_rows",
     )(*entries, *tokens)
     return rows, token
@@ -220,7 +226,7 @@
     scale = columns[pl.ds(pl.multiple_of(z * q, q), q), :][:, 0:1]
     for k, m in enumerate(messages):
         at = slice(k * m.shape[1], (k + 1) * m.shape[1])
-        out[:, at] = product[:, at] - scale * m[q:, :]
+        out[:, at] = product[:, at] - scale * m[m.shape[0] - q :, :]
 
 
 def product_half(rows, vec, before, blocks, *left):
@@ -454,16 +460,17 @@
     feat_total = right_vec.shape[0] * 32
     alpha_row, phibar_row, rhobar_row = (v.reshape(1, -1) for v in (alpha_prev, phibar, rhobar))
 
-    stored, messages = prepare(col_ids.T, col_vals.T, right_vec, left_vec)
-    entries = along_z([stored] * 4)
-    messages = along_z([messages[0]] + [after(messages[1], entries[2]), messages[2], messages[3]])
+    other, messages = prepare(col_ids.T, col_vals.T, right_vec, left_vec)
+    others = along_z([other] * 4)
+    messages = along_z([messages[0], after(messages[1], others[2]), messages[2], messages[3]])
     q = right_vec.shape[1] // 4
-
-    rows1, token1 = build(entries, 1)
+    lines = other.shape[0]
+
+    rows1, token1 = build(others, lines, 1)
     own = stack(messages, q, "stack_right", token1)
     own_x = swap(own, X_BIT)
     own_peer = swap(own, CORE_BIT)
-    rows0, token0 = build(entries, 0, own)
+    rows0, token0 = build(messages, lines, 64, own)
     total1 = forward_part(rows1, [own, own_peer], (0, 8), None, [token0])
     x_peer = swap(after(own_x, total1), CORE_BIT)
     total1 = forward_part(rows1, [own_x], (4,), total1)

time: 78.6 us -> 78.6 us (level)
  waiting for transfers between devices: 7.62 us -> 9.42 us
  starting transfers between devices: 29.2 us -> 27.9 us
    ppermute x22, waiting for transfers between devices: 7.62 us -> 9.42 us  [swap(): return lax.ppermute(value, AXES, [(i, i ^ mask) for i in range(32)])]
    ppermute x22, starting transfers between devices: 29.2 us -> 27.9 us  [swap(): return lax.ppermute(value, AXES, [(i, i ^ mask) for i in range(32)])]
where the time goes in v17:
time: 78.6 us; the launch traced here: 78.5 us
  Pallas kernels  28.4 us (36%)
  starting transfers between devices  27.9 us (35%)
  blocking collectives  11.8 us (15%)
  waiting for transfers between devices  9.42 us (12%)
  between operations  0.94 us (1%)
    ppermute x22, starting transfers between devices, swap(): return lax.ppermute(value, AXES, [(i, i ^ mask) for i in range(32)])  27.9 us
    all_to_all x1, blocking collectives, by_columns(): squares = lax.all_to_all(after(sums, left_own), AXES, 0, 0, tiled=True)  11.8 us
    pallas_call x2, Pallas kernels, build(): pl.pallas_call(build_kernel, in_specs=[whole()] * (4 + len(tokens)), out_...  9.67 us
    ppermute x22, waiting for transfers between devices, swap(): return lax.ppermute(value, AXES, [(i, i ^ mask) for i in range(32)])  9.42 us
    pallas_call x4, Pallas kernels, forward_part(): pl.pallas_call(functools.partial(forward_kernel, blocks, before is not No...  7.12 us
    pallas_call x5, Pallas kernels, backward_part(): pl.pallas_call(functools.partial(backward_kernel, first, blocks, tuple(ex...  5.27 us
    pallas_call x2, Pallas kernels, product_half(): pl.pallas_call(functools.partial(product_kernel, blocks), in_specs=[whole...  2.64 us
    pallas_call x1, Pallas kernels, prepare(): pl.pallas_call(prepare_kernel, in_specs=[pl.BlockSpec(memory_space=pltpu....  1.66 us
  transfers between devices with their start and end apart: 22, of which 7 were waited for; matrix products, arithmetic and copies ran while one was open for 0% of the time, Pallas kernels for 31%

profile of v17, /device:TPU:0, one launch (start us, length us, event | category | flops | bytes accessed | tf_op | source)
XLA Modules:
  0.0 78.5 jit_solution(5882731884024416616)
XLA Ops:
  0.6 1.7 %prepare.1 = (f32[32,256]{1,0:T(8,128)S(1)}, f32[160,256]{1,0:T(8,128)S(1)}, f32[160,256]{1,0:T(8,128)S(1)}, f32[160,256]{1,0:T(8,128)S(1)}, f32[160,256]{1,0:T(8,128)S(1)}) custom-call(s32[16,512]{1,0:T(8,128)} %bitcast.13, bf16[16,512]{1,0:T(8,128)(2,1)} %bitcast.14, f32[256,256]{1,0:T(8,128)} %right.1, f32[512,256]{1,0:T(8,128)} %left_hbm.1), custom_call_target="tpu_custom_call" | custom-call | bytes 16384 | tf_op jit(solution)/shard_map/prepare/pallas_call | solution.py:78
  2.3 4.1 %collective-permute-start.1 = (f32[32,256]{1,0:T(8,128)S(1)}, f32[32,256]{1,0:T(8,128)S(1)}, u32[]{:S(2)}, u32[]{:S(2)}) collective-permute-start(f32[32,256]{1,0:T(8,128)S(1)} %get-tuple-element.45.e0), channel_id=1, source_target_pairs={{0,16},{1,17},{2,18},{3,19},{4,20},{5,21},{6,22},{7,23},{8,24},{9,... | collective-permute-start | bytes 98312 | tf_op jit(solution)/shard_map/ppermute | solution.py:442
  6.4 1.4 %collective-permute-start.2 = (f32[32,256]{1,0:T(8,128)S(1)}, f32[32,256]{1,0:T(8,128)S(1)}, u32[]{:S(2)}, u32[]{:S(2)}) collective-permute-start(f32[32,256]{1,0:T(8,128)S(1)} %get-tuple-element.45.e0), channel_id=1, source_target_pairs={{0,24},{1,25},{2,26},{3,27},{4,28},{5,29},{6,30},{7,31},{8,16},{9,... | collective-permute-start | bytes 98312 | tf_op jit(solution)/shard_map/ppermute | solution.py:442
  7.8 0.2 collective-permute-start
  8.0 2.8 %collective-permute-start.4 = (f32[160,256]{1,0:T(8,128)S(1)}, f32[160,256]{1,0:T(8,128)S(1)}, u32[]{:S(2)}, u32[]{:S(2)}) collective-permute-start(f32[160,256]{1,0:T(8,128)S(1)} %get-tuple-element.51), channel_id=1, source_target_pairs={{0,16},{1,17},{2,18},{3,19},{4,20},{5,21},{6,22},{7,23},{8,24},{9,... | collective-permute-start | bytes 491528 | tf_op jit(solution)/shard_map/ppermute | solution.py:442
  10.8 1.4 %collective-permute-start.5 = (f32[160,256]{1,0:T(8,128)S(1)}, f32[160,256]{1,0:T(8,128)S(1)}, u32[]{:S(2)}, u32[]{:S(2)}) collective-permute-start(f32[160,256]{1,0:T(8,128)S(1)} %get-tuple-element.52), channel_id=1, source_target_pairs={{0,24},{1,25},{2,26},{3,27},{4,28},{5,29},{6,30},{7,31},{8,16},{9,... | collective-permute-start | bytes 491528 | tf_op jit(solution)/shard_map/ppermute | solution.py:442
  12.2 0.4 collective-permute-done.2.e3
  12.6 4.8 %dense_rows.2 = (bf16[16,1024,256]{2,1,0:T(8,128)(2,1)S(1)}, bf16[16,1024,256]{2,1,0:T(8,128)(2,1)S(1)}, f32[8,128]{1,0:T(8,128)S(1)}) custom-call(f32[32,256]{1,0:T(8,128)S(1)} %get-tuple-element.45.e0, f32[32,256]{1,0:T(8,128)S(1)} %collective-permute-done.e1, f32[32,256]{1,0:T(8,128)S(1)} %collective-permute-done.1.e2, ...), custom_call_target="tpu_custom_call" | custom-call | flops 2147483648 | bytes 16777216 | tf_op jit(solution)/shard_map/dense_rows/pallas_call | solution.py:160
  17.3 5.5 %collective-permute-done.4.m2.e2.refs_2_ = f32[160,256]{1,0:T(8,128)S(1)} collective-permute-done((f32[160,256]{1,0:T(8,128)S(1)}, f32[160,256]{1,0:T(8,128)S(1)}, u32[]{:S(2)}, u32[]{:S(2)}) %collective-permute-start.4) | collective-permute-done | bytes 163872 | tf_op jit(solution)/shard_map/ppermute | solution.py:442
  22.8 0.1 collective-permute-done.3.m1.e1.refs_1_
  23.0 0.0 copy-start
  23.0 0.1 collective-permute-start.7
  23.1 1.6 %collective-permute-start.6 = (f32[4,64,256]{2,1,0:T(8,128)S(1)}, f32[4,64,256]{2,1,0:T(8,128)S(1)}, u32[]{:S(2)}, u32[]{:S(2)}) collective-permute-start(f32[4,64,256]{2,1,0:T(8,128)S(1)} %stack_right.1.refs_0_.right), channel_id=1, source_target_pairs={{0,4},{1,5},{2,6},{3,7},{4,0},{5,1},{6,2},{7,3},{8,12},{9,13},{10,... | collective-permute-start | bytes 786440 | tf_op jit(solution)/shard_map/ppermute | solution.py:442
  24.7 4.9 %dense_rows.3 = (bf16[16,1024,256]{2,1,0:T(8,128)(2,1)S(1)}, bf16[16,1024,256]{2,1,0:T(8,128)(2,1)S(1)}, f32[8,128]{1,0:T(8,128)S(1)}) custom-call(f32[160,256]{1,0:T(8,128)S(1)} %get-tuple-element.48.m0.e0.refs_0_, f32[160,256]{1,0:T(8,128)S(1)} %collective-permute-done.3.m1.e1.refs_1_, f32[160,256]{1,0:T(8,128)S(1)} %collective-permute-done.4.m2.e2.refs_2_, ...), custom_call_target="tpu_custom_call" | custom-call | flops 33554432 | bytes 262144 | tf_op jit(solution)/shard_map/dense_rows/pallas_call | solution.py:160
  29.6 2.3 %forward_part.4.refs_1_ = f32[1024,128]{1,0:T(8,128)S(1)} custom-call(bf16[16,1024,256]{2,1,0:T(8,128)(2,1)S(1)} %get-tuple-element.46.hi_ref, bf16[16,1024,256]{2,1,0:T(8,128)(2,1)S(1)} %get-tuple-element.47.lo_ref, f32[4,64,256]{2,1,0:T(8,128)S(1)} %stack_right.1.refs_0_.right, f32[4,64,256]{2,1,0:T(8,128)S(1)} %collective-permute-done.7.refs_1_, ...), custom_call_target="tpu_custom_call" | custom-call | flops 67108864 | bytes 131072 | tf_op jit(solution)/shard_map/forward_part/pallas_call | solution.py:202
  31.9 0.2 collective-permute-start.8
  32.2 1.2 %forward_part.5.before = f32[1024,128]{1,0:T(8,128)S(1)} custom-call(bf16[16,1024,256]{2,1,0:T(8,128)(2,1)S(1)} %get-tuple-element.46.hi_ref, bf16[16,1024,256]{2,1,0:T(8,128)(2,1)S(1)} %get-tuple-element.47.lo_ref, f32[4,64,256]{2,1,0:T(8,128)S(1)} %collective-permute-done.6.refs_0_, f32[1024,128]{1,0:T(8,128)S(1)} %forward_part.4.refs_1_), custom_call_target="tpu_custom_call" | custom-call | flops 33554432 | bytes 65536 | tf_op jit(solution)/shard_map/forward_part/pallas_call | solution.py:202
  33.4 0.1 collective-permute-done.8.vec
  33.5 1.3 %product_half.2.mine = f32[64,1024]{1,0:T(8,128)S(1)} custom-call(bf16[16,1024,256]{2,1,0:T(8,128)(2,1)S(1)} %get-tuple-element.46.hi_ref, bf16[16,1024,256]{2,1,0:T(8,128)(2,1)S(1)} %get-tuple-element.47.lo_ref, f32[4,64,256]{2,1,0:T(8,128)S(1)} %collective-permute-done.8.vec, f32[1024,128]{1,0:T(8,128)S(1)} %forward_part.5.before), custom_call_target="tpu_custom_call" | custom-call | flops 33554432 | bytes 65536 | tf_op jit(solution)/shard_map/product_half/pallas_call | solution.py:234
  34.8 1.6 %collective-permute-start.10 = (f32[64,1024]{1,0:T(8,128)S(1)}, f32[64,1024]{1,0:T(8,128)S(1)}, u32[]{:S(2)}, u32[]{:S(2)}) collective-permute-start(f32[64,1024]{1,0:T(8,128)S(1)} %product_half.2.mine), channel_id=1, source_target_pairs={{0,1},{1,0},{2,3},{3,2},{4,5},{5,4},{6,7},{7,6},{8,9},{9,8},{10,11... | collective-permute-start | bytes 786440 | tf_op jit(solution)/shard_map/ppermute | solution.py:442
  36.4 2.3 %forward_part.6.refs_1_ = f32[1024,128]{1,0:T(8,128)S(1)} custom-call(bf16[16,1024,256]{2,1,0:T(8,128)(2,1)S(1)} %get-tuple-element.56.hi_ref, bf16[16,1024,256]{2,1,0:T(8,128)(2,1)S(1)} %get-tuple-element.57.lo_ref, f32[4,64,256]{2,1,0:T(8,128)S(1)} %stack_right.1.refs_0_.right, f32[4,64,256]{2,1,0:T(8,128)S(1)} %collective-permute-done.7.refs_1_), custom_call_target="tpu_custom_call" | custom-call | flops 67108864 | bytes 131072 | tf_op jit(solution)/shard_map/forward_part/pallas_call | solution.py:202
  38.8 1.2 %forward_part.7.before = f32[1024,128]{1,0:T(8,128)S(1)} custom-call(bf16[16,1024,256]{2,1,0:T(8,128)(2,1)S(1)} %get-tuple-element.56.hi_ref, bf16[16,1024,256]{2,1,0:T(8,128)(2,1)S(1)} %get-tuple-element.57.lo_ref, f32[4,64,256]{2,1,0:T(8,128)S(1)} %collective-permute-done.6.refs_0_, f32[1024,128]{1,0:T(8,128)S(1)} %forward_part.6.refs_1_), custom_call_target="tpu_custom_call" | custom-call | flops 33554432 | bytes 65536 | tf_op jit(solution)/shard_map/forward_part/pallas_call | solution.py:202
  40.0 1.3 %product_half.3.mine = f32[64,1024]{1,0:T(8,128)S(1)} custom-call(bf16[16,1024,256]{2,1,0:T(8,128)(2,1)S(1)} %get-tuple-element.56.hi_ref, bf16[16,1024,256]{2,1,0:T(8,128)(2,1)S(1)} %get-tuple-element.57.lo_ref, f32[4,64,256]{2,1,0:T(8,128)S(1)} %collective-permute-done.8.vec, f32[1024,128]{1,0:T(8,128)S(1)} %forward_part.7.before, ...), custom_call_target="tpu_custom_call" | custom-call | flops 33554432 | bytes 65536 | tf_op jit(solution)/shard_map/product_half/pallas_call | solution.py:234
  41.4 0.5 collective-permute-start.9
  41.9 1.4 %collective-permute-done.10.other = f32[64,1024]{1,0:T(8,128)S(1)} collective-permute-done((f32[64,1024]{1,0:T(8,128)S(1)}, f32[64,1024]{1,0:T(8,128)S(1)}, u32[]{:S(2)}, u32[]{:S(2)}) %collective-permute-start.10) | collective-permute-done | bytes 262176 | tf_op jit(solution)/shard_map/ppermute | solution.py:442
  43.3 0.2 left_half.2
  43.5 3.2 %collective-permute-start.18 = (f32[64,256]{1,0:T(8,128)S(1)}, f32[64,256]{1,0:T(8,128)S(1)}, u32[]{:S(2)}, u32[]{:S(2)}) collective-permute-start(f32[64,256]{1,0:T(8,128)S(1)} %get-tuple-element.71), channel_id=1, source_target_pairs={{0,8},{1,9},{2,10},{3,11},{4,12},{5,13},{6,14},{7,15},{8,0},{9,1},... | collective-permute-start | bytes 196616 | tf_op jit(solution)/shard_map/ppermute | solution.py:442
  46.7 0.6 collective-permute-start.19
  47.3 1.8 %collective-permute-start.20 = (f32[64,256]{1,0:T(8,128)S(1)}, f32[64,256]{1,0:T(8,128)S(1)}, u32[]{:S(2)}, u32[]{:S(2)}) collective-permute-start(f32[64,256]{1,0:T(8,128)S(1)} %get-tuple-element.73), channel_id=1, source_target_pairs={{0,24},{1,25},{2,26},{3,27},{4,28},{5,29},{6,30},{7,31},{8,16},{9,... | collective-permute-start | bytes 196616 | tf_op jit(solution)/shard_map/ppermute | solution.py:442
  49.2 2.3 %backward_part.5.refs_1_.refs_0_ = f32[1024,256]{1,0:T(8,128)S(1)} custom-call(bf16[16,1024,256]{2,1,0:T(8,128)(2,1)S(1)} %get-tuple-element.56.hi_ref, bf16[16,1024,256]{2,1,0:T(8,128)(2,1)S(1)} %get-tuple-element.57.lo_ref, bf16[128,1024]{1,0:T(8,128)(2,1)S(1)} %get-tuple-element.59.both_ref), custom_call_target="tpu_custom_call" | custom-call | flops 134217728 | bytes 262144 | tf_op jit(solution)/shard_map/backward_part/pallas_call | solution.py:315
  51.5 0.2 left_half.3
  51.7 0.7 backward_part.7.refs_1_.near
  52.4 0.7 backward_part.9
  53.2 0.1 collective-permute-start.12
  53.3 0.7 backward_part.8.token
  54.0 0.6 collective-permute-start.11
  54.6 0.2 collective-permute-done.12.far
  54.8 1.4 %collective-permute-start.14 = (f32[128,256]{1,0:T(8,128)S(1)}, f32[128,256]{1,0:T(8,128)S(1)}, u32[]{:S(2)}, u32[]{:S(2)}) collective-permute-start(f32[128,256]{1,0:T(8,128)S(1)} %get-tuple-element.64), channel_id=1, source_target_pairs={{0,4},{1,5},{2,6},{3,7},{4,0},{5,1},{6,2},{7,3},{8,12},{9,13},{10,... | collective-permute-start | bytes 393224 | tf_op jit(solution)/shard_map/ppermute | solution.py:442
  56.2 0.8 collective-permute-start.13
  57.0 1.9 %collective-permute-start.21 = (f32[4,64,256]{2,1,0:T(8,128)S(1)}, f32[4,64,256]{2,1,0:T(8,128)S(1)}, u32[]{:S(2)}, u32[]{:S(2)}) collective-permute-start(f32[4,64,256]{2,1,0:T(8,128)S(1)} %stack_left.1.own), channel_id=1, source_target_pairs={{0,1},{1,0},{2,3},{3,2},{4,5},{5,4},{6,7},{7,6},{8,9},{9,8},{10,11... | collective-permute-start | bytes 786440 | tf_op jit(solution)/shard_map/ppermute | solution.py:442
  58.9 0.7 backward_part.6.keep
  59.6 1.6 %collective-permute-done.14.got = f32[128,256]{1,0:T(8,128)S(1)} collective-permute-done((f32[128,256]{1,0:T(8,128)S(1)}, f32[128,256]{1,0:T(8,128)S(1)}, u32[]{:S(2)}, u32[]{:S(2)}) %collective-permute-start.14) | collective-permute-done | bytes 131104 | tf_op jit(solution)/shard_map/ppermute | solution.py:442
  61.3 1.8 %collective-permute-start.16 = (f32[64,256]{1,0:T(8,128)S(1)}, f32[64,256]{1,0:T(8,128)S(1)}, u32[]{:S(2)}, u32[]{:S(2)}) collective-permute-start(f32[64,256]{1,0:T(8,128)S(1)} %get-tuple-element.65.g2), channel_id=1, source_target_pairs={{0,16},{1,17},{2,18},{3,19},{4,20},{5,21},{6,22},{7,23},{8,24},{9,... | collective-permute-start | bytes 196616 | tf_op jit(solution)/shard_map/ppermute | solution.py:442
  63.1 1.8 %collective-permute-start.17 = (f32[64,256]{1,0:T(8,128)S(1)}, f32[64,256]{1,0:T(8,128)S(1)}, u32[]{:S(2)}, u32[]{:S(2)}) collective-permute-start(f32[64,256]{1,0:T(8,128)S(1)} %get-tuple-element.66.g3), channel_id=1, source_target_pairs={{0,24},{1,25},{2,26},{3,27},{4,28},{5,29},{6,30},{7,31},{8,16},{9,... | collective-permute-start | bytes 196616 | tf_op jit(solution)/shard_map/ppermute | solution.py:442
  64.9 0.3 right_norm.1
  65.2 0.1 collective-permute-start.15
  65.3 11.8 %all_to_all.5.squares = f32[32,1,128]{2,1,0:T(1,128)S(1)} all-to-all(f32[32,1,128]{2,1,0:T(1,128)S(1)} %bitcast.9), channel_id=1, replica_groups=mesh['doc'=16,'feat'=2] {'doc','feat'}, dimensions={0} | all-to-all | bytes 32768 | tf_op jit(solution)/shard_map/all_to_all | solution.py:500
  77.1 1.3 %finish.1 = (f32[512,256]{1,0:T(8,128)}, f32[256,256]{1,0:T(8,128)}, f32[256,256]{1,0:T(8,128)}, f32[256,256]{1,0:T(8,128)}, f32[1,256]{1,0:T(1,128)}, /*index=5*/f32[1,256]{1,0:T(1,128)}, f32[1,256]{1,0:T(1,128)}) custom-call(f32[64,256]{1,0:T(8,128)S(1)} %get-tuple-element.67.g0, f32[64,256]{1,0:T(8,128)S(1)} %collective-permute-done.15.g1, ...), custom_call_target="tpu_custom_call" | custom-call | flops 16384 | bytes 20480 | tf_op jit(solution)/shard_map/finish/pallas_call | solution.py:431
  (35 shorter events, 0.2 us)
Async XLA Ops:
  2.3 9.9 %collective-permute-start.1 = (f32[32,256]{1,0:T(8,128)S(1)}, f32[32,256]{1,0:T(8,128)S(1)}, u32[]{:S(2)}, u32[]{:S(2)}) collective-permute-start(f32[32,256]{1,0:T(8,128)S(1)} %get-tuple-element.45.e0), channel_id=1, source_target_pairs={{0,16},{1,17},{2,18},{3,19},{4,20},{5,21},{6,22},{7,23},{8,24},{9,... | collective-permute-start | bytes 98312 | tf_op jit(solution)/shard_map/ppermute | solution.py:442
  6.4 6.2 %collective-permute-start.2 = (f32[32,256]{1,0:T(8,128)S(1)}, f32[32,256]{1,0:T(8,128)S(1)}, u32[]{:S(2)}, u32[]{:S(2)}) collective-permute-start(f32[32,256]{1,0:T(8,128)S(1)} %get-tuple-element.45.e0), channel_id=1, source_target_pairs={{0,24},{1,25},{2,26},{3,27},{4,28},{5,29},{6,30},{7,31},{8,16},{9,... | collective-permute-start | bytes 98312 | tf_op jit(solution)/shard_map/ppermute | solution.py:442
  7.8 4.8 %collective-permute-start = (f32[32,256]{1,0:T(8,128)S(1)}, f32[32,256]{1,0:T(8,128)S(1)}, u32[]{:S(2)}, u32[]{:S(2)}) collective-permute-start(f32[32,256]{1,0:T(8,128)S(1)} %get-tuple-element.45.e0), channel_id=1, source_target_pairs={{0,8},{1,9},{2,10},{3,11},{4,12},{5,13},{6,14},{7,15},{8,0},{9,1},... | collective-permute-start | bytes 98312 | tf_op jit(solution)/shard_map/ppermute | solution.py:442
  8.0 14.8 %collective-permute-start.4 = (f32[160,256]{1,0:T(8,128)S(1)}, f32[160,256]{1,0:T(8,128)S(1)}, u32[]{:S(2)}, u32[]{:S(2)}) collective-permute-start(f32[160,256]{1,0:T(8,128)S(1)} %get-tuple-element.51), channel_id=1, source_target_pairs={{0,16},{1,17},{2,18},{3,19},{4,20},{5,21},{6,22},{7,23},{8,24},{9,... | collective-permute-start | bytes 491528 | tf_op jit(solution)/shard_map/ppermute | solution.py:442
  10.8 12.0 %collective-permute-start.5 = (f32[160,256]{1,0:T(8,128)S(1)}, f32[160,256]{1,0:T(8,128)S(1)}, u32[]{:S(2)}, u32[]{:S(2)}) collective-permute-start(f32[160,256]{1,0:T(8,128)S(1)} %get-tuple-element.52), channel_id=1, source_target_pairs={{0,24},{1,25},{2,26},{3,27},{4,28},{5,29},{6,30},{7,31},{8,16},{9,... | collective-permute-start | bytes 491528 | tf_op jit(solution)/shard_map/ppermute | solution.py:442
  12.2 10.8 %collective-permute-start.3 = (f32[160,256]{1,0:T(8,128)S(1)}, f32[160,256]{1,0:T(8,128)S(1)}, u32[]{:S(2)}, u32[]{:S(2)}) collective-permute-start(f32[160,256]{1,0:T(8,128)S(1)} %get-tuple-element.50), channel_id=1, source_target_pairs={{0,8},{1,9},{2,10},{3,11},{4,12},{5,13},{6,14},{7,15},{8,0},{9,1},... | collective-permute-start | bytes 491528 | tf_op jit(solution)/shard_map/ppermute | solution.py:442
  23.0 13.4 %copy-start = (f32[4,64,256]{2,1,0:T(8,128)}, f32[4,64,256]{2,1,0:T(8,128)S(1)}, u32[]{:S(2)}) copy-start(f32[4,64,256]{2,1,0:T(8,128)S(1)} %stack_right.1.refs_0_.right) | copy-start | bytes 786436
  23.0 6.5 %collective-permute-start.7 = (f32[4,64,256]{2,1,0:T(8,128)S(1)}, f32[4,64,256]{2,1,0:T(8,128)S(1)}, u32[]{:S(2)}, u32[]{:S(2)}) collective-permute-start(f32[4,64,256]{2,1,0:T(8,128)S(1)} %stack_right.1.refs_0_.right), channel_id=1, source_target_pairs={{0,2},{1,3},{2,0},{3,1},{4,6},{5,7},{6,4},{7,5},{8,10},{9,11},{10,... | collective-permute-start | bytes 786440 | tf_op jit(solution)/shard_map/ppermute | solution.py:442
  23.1 8.8 %collective-permute-start.6 = (f32[4,64,256]{2,1,0:T(8,128)S(1)}, f32[4,64,256]{2,1,0:T(8,128)S(1)}, u32[]{:S(2)}, u32[]{:S(2)}) collective-permute-start(f32[4,64,256]{2,1,0:T(8,128)S(1)} %stack_right.1.refs_0_.right), channel_id=1, source_target_pairs={{0,4},{1,5},{2,6},{3,7},{4,0},{5,1},{6,2},{7,3},{8,12},{9,13},{10,... | collective-permute-start | bytes 786440 | tf_op jit(solution)/shard_map/ppermute | solution.py:442
  31.9 1.6 %collective-permute-start.8 = (f32[4,64,256]{2,1,0:T(8,128)S(1)}, f32[4,64,256]{2,1,0:T(8,128)S(1)}, u32[]{:S(2)}, u32[]{:S(2)}) collective-permute-start(f32[4,64,256]{2,1,0:T(8,128)S(1)} %collective-permute-done.6.refs_0_), channel_id=1, source_target_pairs={{0,2},{1,3},{2,0},{3,1},{4,6},{5,7},{6,4},{7,5},{8,10},{9,11},{10,... | collective-permute-start | bytes 786440 | tf_op jit(solution)/shard_map/ppermute | solution.py:442
  34.8 8.5 %collective-permute-start.10 = (f32[64,1024]{1,0:T(8,128)S(1)}, f32[64,1024]{1,0:T(8,128)S(1)}, u32[]{:S(2)}, u32[]{:S(2)}) collective-permute-start(f32[64,1024]{1,0:T(8,128)S(1)} %product_half.2.mine), channel_id=1, source_target_pairs={{0,1},{1,0},{2,3},{3,2},{4,5},{5,4},{6,7},{7,6},{8,9},{9,8},{10,11... | collective-permute-start | bytes 786440 | tf_op jit(solution)/shard_map/ppermute | solution.py:442
  38.8 1.3 %copy-start.5 = (f32[256]{0:T(256)S(1)}, f32[256]{0:T(256)}, u32[]{:S(2)}) copy-start(f32[256]{0:T(256)} %param.15) | copy-start | bytes 3076
  41.4 10.2 %collective-permute-start.9 = (f32[64,1024]{1,0:T(8,128)S(1)}, f32[64,1024]{1,0:T(8,128)S(1)}, u32[]{:S(2)}, u32[]{:S(2)}) collective-permute-start(f32[64,1024]{1,0:T(8,128)S(1)} %product_half.3.mine), channel_id=1, source_target_pairs={{0,1},{1,0},{2,3},{3,2},{4,5},{5,4},{6,7},{7,6},{8,9},{9,8},{10,11... | collective-permute-start | bytes 786440 | tf_op jit(solution)/shard_map/ppermute | solution.py:442
  43.5 11.0 %collective-permute-start.18 = (f32[64,256]{1,0:T(8,128)S(1)}, f32[64,256]{1,0:T(8,128)S(1)}, u32[]{:S(2)}, u32[]{:S(2)}) collective-permute-start(f32[64,256]{1,0:T(8,128)S(1)} %get-tuple-element.71), channel_id=1, source_target_pairs={{0,8},{1,9},{2,10},{3,11},{4,12},{5,13},{6,14},{7,15},{8,0},{9,1},... | collective-permute-start | bytes 196616 | tf_op jit(solution)/shard_map/ppermute | solution.py:442
  46.7 7.8 %collective-permute-start.19 = (f32[64,256]{1,0:T(8,128)S(1)}, f32[64,256]{1,0:T(8,128)S(1)}, u32[]{:S(2)}, u32[]{:S(2)}) collective-permute-start(f32[64,256]{1,0:T(8,128)S(1)} %get-tuple-element.72), channel_id=1, source_target_pairs={{0,16},{1,17},{2,18},{3,19},{4,20},{5,21},{6,22},{7,23},{8,24},{9,... | collective-permute-start | bytes 196616 | tf_op jit(solution)/shard_map/ppermute | solution.py:442
  47.3 7.2 %collective-permute-start.20 = (f32[64,256]{1,0:T(8,128)S(1)}, f32[64,256]{1,0:T(8,128)S(1)}, u32[]{:S(2)}, u32[]{:S(2)}) collective-permute-start(f32[64,256]{1,0:T(8,128)S(1)} %get-tuple-element.73), channel_id=1, source_target_pairs={{0,24},{1,25},{2,26},{3,27},{4,28},{5,29},{6,30},{7,31},{8,16},{9,... | collective-permute-start | bytes 196616 | tf_op jit(solution)/shard_map/ppermute | solution.py:442
  53.2 1.6 %collective-permute-start.12 = (f32[264,256]{1,0:T(8,128)S(1)}, f32[264,256]{1,0:T(8,128)S(1)}, u32[]{:S(2)}, u32[]{:S(2)}) collective-permute-start(f32[264,256]{1,0:T(8,128)S(1)} %backward_part.9), channel_id=1, source_target_pairs={{0,2},{1,3},{2,0},{3,1},{4,6},{5,7},{6,4},{7,5},{8,10},{9,11},{10,... | collective-permute-start | bytes 811016 | tf_op jit(solution)/shard_map/ppermute | solution.py:442
  54.0 5.6 %collective-permute-start.11 = (f32[256,256]{1,0:T(8,128)S(1)}, f32[256,256]{1,0:T(8,128)S(1)}, u32[]{:S(2)}, u32[]{:S(2)}) collective-permute-start(f32[256,256]{1,0:T(8,128)S(1)} %backward_part.8.token), channel_id=1, source_target_pairs={{0,2},{1,3},{2,0},{3,1},{4,6},{5,7},{6,4},{7,5},{8,10},{9,11},{10,... | collective-permute-start | bytes 786440 | tf_op jit(solution)/shard_map/ppermute | solution.py:442
  54.8 6.4 %collective-permute-start.14 = (f32[128,256]{1,0:T(8,128)S(1)}, f32[128,256]{1,0:T(8,128)S(1)}, u32[]{:S(2)}, u32[]{:S(2)}) collective-permute-start(f32[128,256]{1,0:T(8,128)S(1)} %get-tuple-element.64), channel_id=1, source_target_pairs={{0,4},{1,5},{2,6},{3,7},{4,0},{5,1},{6,2},{7,3},{8,12},{9,13},{10,... | collective-permute-start | bytes 393224 | tf_op jit(solution)/shard_map/ppermute | solution.py:442
  56.2 8.7 %copy-start.1 = (f32[4,64,256]{2,1,0:T(8,128)S(1)}, f32[4,64,256]{2,1,0:T(8,128)}, u32[]{:S(2)}) copy-start(f32[4,64,256]{2,1,0:T(8,128)} %copy-done) | copy-start | bytes 786436
  56.2 20.9 %copy-start.2 = (f32[256,256]{1,0:T(8,128)S(1)}, f32[256,256]{1,0:T(8,128)}, u32[]{:S(2)}) copy-start(f32[256,256]{1,0:T(8,128)} %right.1) | copy-start | bytes 786436
  56.2 20.9 %copy-start.3 = (f32[256,256]{1,0:T(8,128)S(1)}, f32[256,256]{1,0:T(8,128)}, u32[]{:S(2)}) copy-start(f32[256,256]{1,0:T(8,128)} %search.1) | copy-start | bytes 786436
  56.2 20.9 %copy-start.4 = (f32[256,256]{1,0:T(8,128)S(1)}, f32[256,256]{1,0:T(8,128)}, u32[]{:S(2)}) copy-start(f32[256,256]{1,0:T(8,128)} %solution.1) | copy-start | bytes 786436
  56.2 20.9 %copy-start.6 = (f32[256]{0:T(256)S(1)}, f32[256]{0:T(256)}, u32[]{:S(2)}) copy-start(f32[256]{0:T(256)} %param.16) | copy-start | bytes 3076
  56.2 20.9 %copy-start.7 = (f32[256]{0:T(256)S(1)}, f32[256]{0:T(256)}, u32[]{:S(2)}) copy-start(f32[256]{0:T(256)} %param.17) | copy-start | bytes 3076
  56.2 8.7 %collective-permute-start.13 = (f32[136,256]{1,0:T(8,128)S(1)}, f32[136,256]{1,0:T(8,128)S(1)}, u32[]{:S(2)}, u32[]{:S(2)}) collective-permute-start(f32[136,256]{1,0:T(8,128)S(1)} %get-tuple-element.62), channel_id=1, source_target_pairs={{0,4},{1,5},{2,6},{3,7},{4,0},{5,1},{6,2},{7,3},{8,12},{9,13},{10,... | collective-permute-start | bytes 417800 | tf_op jit(solution)/shard_map/ppermute | solution.py:442
  57.0 20.1 %collective-permute-start.21 = (f32[4,64,256]{2,1,0:T(8,128)S(1)}, f32[4,64,256]{2,1,0:T(8,128)S(1)}, u32[]{:S(2)}, u32[]{:S(2)}) collective-permute-start(f32[4,64,256]{2,1,0:T(8,128)S(1)} %stack_left.1.own), channel_id=1, source_target_pairs={{0,1},{1,0},{2,3},{3,2},{4,5},{5,4},{6,7},{7,6},{8,9},{9,8},{10,11... | collective-permute-start | bytes 786440 | tf_op jit(solution)/shard_map/ppermute | solution.py:442
  61.3 15.8 %collective-permute-start.16 = (f32[64,256]{1,0:T(8,128)S(1)}, f32[64,256]{1,0:T(8,128)S(1)}, u32[]{:S(2)}, u32[]{:S(2)}) collective-permute-start(f32[64,256]{1,0:T(8,128)S(1)} %get-tuple-element.65.g2), channel_id=1, source_target_pairs={{0,16},{1,17},{2,18},{3,19},{4,20},{5,21},{6,22},{7,23},{8,24},{9,... | collective-permute-start | bytes 196616 | tf_op jit(solution)/shard_map/ppermute | solution.py:442
  63.1 14.0 %collective-permute-start.17 = (f32[64,256]{1,0:T(8,128)S(1)}, f32[64,256]{1,0:T(8,128)S(1)}, u32[]{:S(2)}, u32[]{:S(2)}) collective-permute-start(f32[64,256]{1,0:T(8,128)S(1)} %get-tuple-element.66.g3), channel_id=1, source_target_pairs={{0,24},{1,25},{2,26},{3,27},{4,28},{5,29},{6,30},{7,31},{8,16},{9,... | collective-permute-start | bytes 196616 | tf_op jit(solution)/shard_map/ppermute | solution.py:442
  65.2 11.8 %collective-permute-start.15 = (f32[64,256]{1,0:T(8,128)S(1)}, f32[64,256]{1,0:T(8,128)S(1)}, u32[]{:S(2)}, u32[]{:S(2)}) collective-permute-start(f32[64,256]{1,0:T(8,128)S(1)} %get-tuple-element.68), channel_id=1, source_target_pairs={{0,8},{1,9},{2,10},{3,11},{4,12},{5,13},{6,14},{7,15},{8,0},{9,1},... | collective-permute-start | bytes 196616 | tf_op jit(solution)/shard_map/ppermute | solution.py:442

commit v18 on v17

--- a/solution.py
+++ b/solution.py
@@ -38,7 +38,7 @@
     return jax.ShapeDtypeStruct(shape, jnp.bfloat16)
 
 
-def prepare_kernel(ids_hbm, vals_hbm, right_hbm, left_hbm, other, m0, m1, m2, m3,
+def prepare_kernel(ids_hbm, vals_hbm, right_hbm, left_hbm, a0, a1, a2, a3, b0, b1, b2, b3,
                    ids, vals, wide, lines, right, left, turned, arrived):
     _, z, y = coords()
     q, rows = turned.shape[1:]
@@ -55,21 +55,22 @@
         copy.start()
     count, n = ids.shape[0], lines.shape[0]
     half = n // 2
+    groups = (b0, b1, b2, b3), (a0, a1, a2, a3)
     for part, ref in enumerate((ids, vals)):
         copies[part].wait()
         wide[...] = ref[...].astype(jnp.float32).T
         for r in range(256 // count):
             lines[:, r * count : (r + 1) * count] = wide[pl.ds(r, n, stride=256 // count), :]
         at = slice(part * half, (part + 1) * half)
-        other[at, :] = lines[pl.ds(pl.multiple_of((1 - y) * half, half), half), :]
-        own = lines[pl.ds(pl.multiple_of(y * half, half), half), :]
-        for out in (m0, m1, m2, m3):
-            out[at, :] = own
-    for part, (copy, ref) in enumerate(zip(copies[2:], (right, left))):
+        for rel, outs in enumerate(groups):
+            value = lines[pl.ds(pl.multiple_of((y ^ rel) * half, half), half), :]
+            for out in outs:
+                out[at, :] = value
+    for copy, ref, outs in zip(copies[2:], (right, left), groups[::-1]):
         copy.wait()
         turned[...] = ref[...].T.reshape(turned.shape)
-        for k, out in enumerate((m0, m1, m2, m3)):
-            out[n + part * q : n + (part + 1) * q, :] = turned[z ^ k]
+        for k, out in enumerate(outs):
+            out[n:, :] = turned[z ^ k]
 
 
 def prepare(ids, vals, right, left):
@@ -78,8 +79,8 @@
     got = pl.pallas_call(
         prepare_kernel,
         in_specs=[pl.BlockSpec(memory_space=pltpu.HBM)] * 4,
-        out_specs=[whole()] * 5,
-        out_shape=[pltpu.VMEM((n, 256), jnp.float32)] + [pltpu.VMEM((n + 2 * q, rows), jnp.float32)] * 4,
+        out_specs=[whole()] * 8,
+        out_shape=[pltpu.VMEM((n + q, rows), jnp.float32)] * 8,
         scratch_shapes=[
             pltpu.VMEM(ids.shape, jnp.int32),
             pltpu.VMEM(vals.shape, jnp.bfloat16),
@@ -94,14 +95,13 @@
         cost_estimate=cost(0, rows * cols * 16),
         name="prepare",
     )(ids, vals, right, left)
-    return got[0], got[1:]
+    return got[:4], got[4:]
 
 
 def stack_kernel(m0, m1, m2, m3, *refs):
     out = refs[-1]
     for k, m in enumerate((m0, m1, m2, m3)):
-        at = m.shape[0] - 2 * out.shape[1] if m.shape[0] > out.shape[1] else 0
-        out[k] = m[at : at + out.shape[1], :]
+        out[k] = m[m.shape[0] - out.shape[1] :, :]
 
 
 def stack(messages, q, name, *tokens):
@@ -460,24 +460,24 @@
     feat_total = right_vec.shape[0] * 32
     alpha_row, phibar_row, rhobar_row = (v.reshape(1, -1) for v in (alpha_prev, phibar, rhobar))
 
-    other, messages = prepare(col_ids.T, col_vals.T, right_vec, left_vec)
-    others = along_z([other] * 4)
-    messages = along_z([messages[0], after(messages[1], others[2]), messages[2], messages[3]])
+    first, second = prepare(col_ids.T, col_vals.T, right_vec, left_vec)
+    first = along_z(first)
+    second = along_z(second)
     q = right_vec.shape[1] // 4
-    lines = other.shape[0]
-
-    rows1, token1 = build(others, lines, 1)
-    own = stack(messages, q, "stack_right", token1)
+    lines = first[0].shape[0] - q
+
+    own = stack(first, q, "stack_right")
     own_x = swap(own, X_BIT)
     own_peer = swap(own, CORE_BIT)
-    rows0, token0 = build(messages, lines, 64, own)
+    rows1, token1 = build(first, lines, 0.05, own)
+    rows0, token0 = build(second, lines, 64, token1)
     total1 = forward_part(rows1, [own, own_peer], (0, 8), None, [token0])
     x_peer = swap(after(own_x, total1), CORE_BIT)
     total1 = forward_part(rows1, [own_x], (4,), total1)
     product1 = product_half(rows1, x_peer, total1, (12,))
     total0 = forward_part(rows0, [own, own_peer], (0, 8))
     total0 = forward_part(rows0, [own_x], (4,), total0)
-    product0 = product_half(rows0, x_peer, total0, (12,), *messages, alpha_row)
+    product0 = product_half(rows0, x_peer, total0, (12,), *second, alpha_row)
 
     *lefts, both0, beta0 = left_half(product0, swap(product1, Y_BIT))
     partial = backward_part(rows0, both0, 0, 16)

time: 78.6 us -> 79.8 us (1.015)
  starting transfers between devices: 27.9 us -> 30.4 us
  waiting for transfers between devices: 9.42 us -> 8.36 us
    ppermute x22, starting transfers between devices: 27.9 us -> 30.4 us  [swap(): return lax.ppermute(value, AXES, [(i, i ^ mask) for i in range(32)])]
    ppermute x22, waiting for transfers between devices: 9.42 us -> 8.36 us  [swap(): return lax.ppermute(value, AXES, [(i, i ^ mask) for i in range(32)])]
  transfers between devices with their start and end apart: 22 -> 22, of which waited for: 7 -> 6; matrix products, arithmetic and copies ran while one was open for 0% -> 0% of each run, Pallas kernels for 31% -> 30%
where the time goes in v18:
time: 79.8 us; the launch traced here: 79.7 us
  starting transfers between devices  30.4 us (38%)
  Pallas kernels  28.3 us (35%)
  blocking collectives  11.5 us (14%)
  waiting for transfers between devices  8.36 us (10%)
  between operations  0.95 us (1%)
    ppermute x22, starting transfers between devices, swap(): return lax.ppermute(value, AXES, [(i, i ^ mask) for i in range(32)])  30.4 us
    all_to_all x1, blocking collectives, by_columns(): squares = lax.all_to_all(after(sums, left_own), AXES, 0, 0, tiled=True)  11.5 us
    pallas_call x2, Pallas kernels, build(): pl.pallas_call(build_kernel, in_specs=[whole()] * (4 + len(tokens)), out_...  9.67 us
    ppermute x22, waiting for transfers between devices, swap(): return lax.ppermute(value, AXES, [(i, i ^ mask) for i in range(32)])  8.36 us
    pallas_call x4, Pallas kernels, forward_part(): pl.pallas_call(functools.partial(forward_kernel, blocks, before is not No...  7.12 us
    pallas_call x5, Pallas kernels, backward_part(): pl.pallas_call(functools.partial(backward_kernel, first, blocks, tuple(ex...  5.19 us
    pallas_call x2, Pallas kernels, product_half(): pl.pallas_call(functools.partial(product_kernel, blocks), in_specs=[whole...  2.64 us
    pallas_call x1, Pallas kernels, prepare(): pl.pallas_call(prepare_kernel, in_specs=[pl.BlockSpec(memory_space=pltpu....  1.66 us
  transfers between devices with their start and end apart: 22, of which 6 were waited for; matrix products, arithmetic and copies ran while one was open for 0% of the time, Pallas kernels for 30%

profile of v18, /device:TPU:0, one launch (start us, length us, event | category | flops | bytes accessed | tf_op | source)
XLA Modules:
  0.0 79.7 jit_solution(83869416295345577)
XLA Ops:
  0.6 1.7 %prepare.1 = (f32[96,256]{1,0:T(8,128)S(1)}, f32[96,256]{1,0:T(8,128)S(1)}, f32[96,256]{1,0:T(8,128)S(1)}, f32[96,256]{1,0:T(8,128)S(1)}, f32[96,256]{1,0:T(8,12...) custom-call(s32[16,512]{1,0:T(8,128)} %bitcast.13, bf16[16,512]{1,0:T(8,128)(2,1)} %bitcast.14, ...), custom_call_target="tpu_custom_call" | custom-call | bytes 16384 | tf_op jit(solution)/shard_map/prepare/pallas_call | solution.py:79
  2.3 3.1 %collective-permute-start = (f32[96,256]{1,0:T(8,128)S(1)}, f32[96,256]{1,0:T(8,128)S(1)}, u32[]{:S(2)}, u32[]{:S(2)}) collective-permute-start(f32[96,256]{1,0:T(8,128)S(1)} %get-tuple-element.48), channel_id=1, source_target_pairs={{0,8},{1,9},{2,10},{3,11},{4,12},{5,13},{6,14},{7,15},{8,0},{9,1},... | collective-permute-start | bytes 294920 | tf_op jit(solution)/shard_map/ppermute | solution.py:442
  5.4 2.6 %collective-permute-start.1 = (f32[96,256]{1,0:T(8,128)S(1)}, f32[96,256]{1,0:T(8,128)S(1)}, u32[]{:S(2)}, u32[]{:S(2)}) collective-permute-start(f32[96,256]{1,0:T(8,128)S(1)} %get-tuple-element.49), channel_id=1, source_target_pairs={{0,16},{1,17},{2,18},{3,19},{4,20},{5,21},{6,22},{7,23},{8,24},{9,... | collective-permute-start | bytes 294920 | tf_op jit(solution)/shard_map/ppermute | solution.py:442
  8.0 0.9 %collective-permute-start.5 = (f32[96,256]{1,0:T(8,128)S(1)}, f32[96,256]{1,0:T(8,128)S(1)}, u32[]{:S(2)}, u32[]{:S(2)}) collective-permute-start(f32[96,256]{1,0:T(8,128)S(1)} %get-tuple-element.54), channel_id=1, source_target_pairs={{0,8},{1,9},{2,10},{3,11},{4,12},{5,13},{6,14},{7,15},{8,0},{9,1},... | collective-permute-start | bytes 294920 | tf_op jit(solution)/shard_map/ppermute | solution.py:442
  8.9 3.5 %collective-permute-start.6 = (f32[96,256]{1,0:T(8,128)S(1)}, f32[96,256]{1,0:T(8,128)S(1)}, u32[]{:S(2)}, u32[]{:S(2)}) collective-permute-start(f32[96,256]{1,0:T(8,128)S(1)} %get-tuple-element.55), channel_id=1, source_target_pairs={{0,16},{1,17},{2,18},{3,19},{4,20},{5,21},{6,22},{7,23},{8,24},{9,... | collective-permute-start | bytes 294920 | tf_op jit(solution)/shard_map/ppermute | solution.py:442
  12.4 0.6 collective-permute-start.7
  13.0 3.1 %collective-permute-done.1.m2.e2 = f32[96,256]{1,0:T(8,128)S(1)} collective-permute-done((f32[96,256]{1,0:T(8,128)S(1)}, f32[96,256]{1,0:T(8,128)S(1)}, u32[]{:S(2)}, u32[]{:S(2)}) %collective-permute-start.1) | collective-permute-done | bytes 98336 | tf_op jit(solution)/shard_map/ppermute | solution.py:442
  16.1 0.0 copy-start
  16.1 0.1 collective-permute-start.4
  16.2 1.6 %collective-permute-start.3 = (f32[4,64,256]{2,1,0:T(8,128)S(1)}, f32[4,64,256]{2,1,0:T(8,128)S(1)}, u32[]{:S(2)}, u32[]{:S(2)}) collective-permute-start(f32[4,64,256]{2,1,0:T(8,128)S(1)} %stack_right.1.refs_0_.right), channel_id=1, source_target_pairs={{0,4},{1,5},{2,6},{3,7},{4,0},{5,1},{6,2},{7,3},{8,12},{9,13},{10,... | collective-permute-start | bytes 786440 | tf_op jit(solution)/shard_map/ppermute | solution.py:442
  17.8 4.7 %dense_rows.2 = (bf16[16,1024,256]{2,1,0:T(8,128)(2,1)S(1)}, bf16[16,1024,256]{2,1,0:T(8,128)(2,1)S(1)}, f32[8,128]{1,0:T(8,128)S(1)}) custom-call(f32[96,256]{1,0:T(8,128)S(1)} %get-tuple-element.47.m0.e0, f32[96,256]{1,0:T(8,128)S(1)} %collective-permute-done.m1.e1, f32[96,256]{1,0:T(8,128)S(1)} %collective-permute-done.1.m2.e2, ...), custom_call_target="tpu_custom_call" | custom-call | flops 42949672960 | bytes 335544320 | tf_op jit(solution)/shard_map/dense_rows/pallas_call | solution.py:160
  22.5 1.7 %collective-permute-done.6.e2.refs_2_ = f32[96,256]{1,0:T(8,128)S(1)} collective-permute-done((f32[96,256]{1,0:T(8,128)S(1)}, f32[96,256]{1,0:T(8,128)S(1)}, u32[]{:S(2)}, u32[]{:S(2)}) %collective-permute-start.6) | collective-permute-done | bytes 98336 | tf_op jit(solution)/shard_map/ppermute | solution.py:442
  24.3 4.9 %dense_rows.3 = (bf16[16,1024,256]{2,1,0:T(8,128)(2,1)S(1)}, bf16[16,1024,256]{2,1,0:T(8,128)(2,1)S(1)}, f32[8,128]{1,0:T(8,128)S(1)}) custom-call(f32[96,256]{1,0:T(8,128)S(1)} %get-tuple-element.53.e0.refs_0_, f32[96,256]{1,0:T(8,128)S(1)} %collective-permute-done.5.e1.refs_1_, f32[96,256]{1,0:T(8,128)S(1)} %collective-permute-done.6.e2.refs_2_, ...), custom_call_target="tpu_custom_call" | custom-call | flops 33554432 | bytes 262144 | tf_op jit(solution)/shard_map/dense_rows/pallas_call | solution.py:160
  29.2 2.3 %forward_part.4.refs_1_ = f32[1024,128]{1,0:T(8,128)S(1)} custom-call(bf16[16,1024,256]{2,1,0:T(8,128)(2,1)S(1)} %get-tuple-element.51.hi_ref, bf16[16,1024,256]{2,1,0:T(8,128)(2,1)S(1)} %get-tuple-element.52.lo_ref, f32[4,64,256]{2,1,0:T(8,128)S(1)} %stack_right.1.refs_0_.right, f32[4,64,256]{2,1,0:T(8,128)S(1)} %collective-permute-done.4.refs_1_, ...), custom_call_target="tpu_custom_call" | custom-call | flops 67108864 | bytes 131072 | tf_op jit(solution)/shard_map/forward_part/pallas_call | solution.py:202
  31.5 0.1 collective-permute-start.8
  31.6 1.2 %forward_part.5.before = f32[1024,128]{1,0:T(8,128)S(1)} custom-call(bf16[16,1024,256]{2,1,0:T(8,128)(2,1)S(1)} %get-tuple-element.51.hi_ref, bf16[16,1024,256]{2,1,0:T(8,128)(2,1)S(1)} %get-tuple-element.52.lo_ref, f32[4,64,256]{2,1,0:T(8,128)S(1)} %collective-permute-done.3.refs_0_, f32[1024,128]{1,0:T(8,128)S(1)} %forward_part.4.refs_1_), custom_call_target="tpu_custom_call" | custom-call | flops 33554432 | bytes 65536 | tf_op jit(solution)/shard_map/forward_part/pallas_call | solution.py:202
  32.9 0.3 collective-permute-done.8.vec
  33.1 1.3 %product_half.2.mine = f32[64,1024]{1,0:T(8,128)S(1)} custom-call(bf16[16,1024,256]{2,1,0:T(8,128)(2,1)S(1)} %get-tuple-element.51.hi_ref, bf16[16,1024,256]{2,1,0:T(8,128)(2,1)S(1)} %get-tuple-element.52.lo_ref, f32[4,64,256]{2,1,0:T(8,128)S(1)} %collective-permute-done.8.vec, f32[1024,128]{1,0:T(8,128)S(1)} %forward_part.5.before), custom_call_target="tpu_custom_call" | custom-call | flops 33554432 | bytes 65536 | tf_op jit(solution)/shard_map/product_half/pallas_call | solution.py:234
  34.5 1.6 %collective-permute-start.10 = (f32[64,1024]{1,0:T(8,128)S(1)}, f32[64,1024]{1,0:T(8,128)S(1)}, u32[]{:S(2)}, u32[]{:S(2)}) collective-permute-start(f32[64,1024]{1,0:T(8,128)S(1)} %product_half.2.mine), channel_id=1, source_target_pairs={{0,1},{1,0},{2,3},{3,2},{4,5},{5,4},{6,7},{7,6},{8,9},{9,8},{10,11... | collective-permute-start | bytes 786440 | tf_op jit(solution)/shard_map/ppermute | solution.py:442
  36.1 2.3 %forward_part.6.refs_1_ = f32[1024,128]{1,0:T(8,128)S(1)} custom-call(bf16[16,1024,256]{2,1,0:T(8,128)(2,1)S(1)} %get-tuple-element.60.hi_ref, bf16[16,1024,256]{2,1,0:T(8,128)(2,1)S(1)} %get-tuple-element.61.lo_ref, f32[4,64,256]{2,1,0:T(8,128)S(1)} %stack_right.1.refs_0_.right, f32[4,64,256]{2,1,0:T(8,128)S(1)} %collective-permute-done.4.refs_1_), custom_call_target="tpu_custom_call" | custom-call | flops 67108864 | bytes 131072 | tf_op jit(solution)/shard_map/forward_part/pallas_call | solution.py:202
  38.4 1.2 %forward_part.7.before = f32[1024,128]{1,0:T(8,128)S(1)} custom-call(bf16[16,1024,256]{2,1,0:T(8,128)(2,1)S(1)} %get-tuple-element.60.hi_ref, bf16[16,1024,256]{2,1,0:T(8,128)(2,1)S(1)} %get-tuple-element.61.lo_ref, f32[4,64,256]{2,1,0:T(8,128)S(1)} %collective-permute-done.3.refs_0_, f32[1024,128]{1,0:T(8,128)S(1)} %forward_part.6.refs_1_), custom_call_target="tpu_custom_call" | custom-call | flops 33554432 | bytes 65536 | tf_op jit(solution)/shard_map/forward_part/pallas_call | solution.py:202
  39.6 1.3 %product_half.3.mine = f32[64,1024]{1,0:T(8,128)S(1)} custom-call(bf16[16,1024,256]{2,1,0:T(8,128)(2,1)S(1)} %get-tuple-element.60.hi_ref, bf16[16,1024,256]{2,1,0:T(8,128)(2,1)S(1)} %get-tuple-element.61.lo_ref, f32[4,64,256]{2,1,0:T(8,128)S(1)} %collective-permute-done.8.vec, f32[1024,128]{1,0:T(8,128)S(1)} %forward_part.7.before, ...), custom_call_target="tpu_custom_call" | custom-call | flops 33554432 | bytes 65536 | tf_op jit(solution)/shard_map/product_half/pallas_call | solution.py:234
  41.0 0.6 collective-permute-start.9
  41.5 1.4 %collective-permute-done.10.other = f32[64,1024]{1,0:T(8,128)S(1)} collective-permute-done((f32[64,1024]{1,0:T(8,128)S(1)}, f32[64,1024]{1,0:T(8,128)S(1)}, u32[]{:S(2)}, u32[]{:S(2)}) %collective-permute-start.10) | collective-permute-done | bytes 262176 | tf_op jit(solution)/shard_map/ppermute | solution.py:442
  43.0 0.1 left_half.2
  43.1 5.1 %collective-permute-start.18 = (f32[64,256]{1,0:T(8,128)S(1)}, f32[64,256]{1,0:T(8,128)S(1)}, u32[]{:S(2)}, u32[]{:S(2)}) collective-permute-start(f32[64,256]{1,0:T(8,128)S(1)} %get-tuple-element.75), channel_id=1, source_target_pairs={{0,8},{1,9},{2,10},{3,11},{4,12},{5,13},{6,14},{7,15},{8,0},{9,1},... | collective-permute-start | bytes 196616 | tf_op jit(solution)/shard_map/ppermute | solution.py:442
  48.2 1.1 %collective-permute-start.19 = (f32[64,256]{1,0:T(8,128)S(1)}, f32[64,256]{1,0:T(8,128)S(1)}, u32[]{:S(2)}, u32[]{:S(2)}) collective-permute-start(f32[64,256]{1,0:T(8,128)S(1)} %get-tuple-element.76), channel_id=1, source_target_pairs={{0,16},{1,17},{2,18},{3,19},{4,20},{5,21},{6,22},{7,23},{8,24},{9,... | collective-permute-start | bytes 196616 | tf_op jit(solution)/shard_map/ppermute | solution.py:442
  49.3 1.4 %collective-permute-start.20 = (f32[64,256]{1,0:T(8,128)S(1)}, f32[64,256]{1,0:T(8,128)S(1)}, u32[]{:S(2)}, u32[]{:S(2)}) collective-permute-start(f32[64,256]{1,0:T(8,128)S(1)} %get-tuple-element.77), channel_id=1, source_target_pairs={{0,24},{1,25},{2,26},{3,27},{4,28},{5,29},{6,30},{7,31},{8,16},{9,... | collective-permute-start | bytes 196616 | tf_op jit(solution)/shard_map/ppermute | solution.py:442
  50.7 2.3 %backward_part.5.refs_1_.refs_0_ = f32[1024,256]{1,0:T(8,128)S(1)} custom-call(bf16[16,1024,256]{2,1,0:T(8,128)(2,1)S(1)} %get-tuple-element.60.hi_ref, bf16[16,1024,256]{2,1,0:T(8,128)(2,1)S(1)} %get-tuple-element.61.lo_ref, bf16[128,1024]{1,0:T(8,128)(2,1)S(1)} %get-tuple-element.63.both_ref), custom_call_target="tpu_custom_call" | custom-call | flops 134217728 | bytes 262144 | tf_op jit(solution)/shard_map/backward_part/pallas_call | solution.py:315
  53.0 0.2 left_half.3
  53.2 0.7 backward_part.7.refs_1_.near
  53.9 0.7 backward_part.9
  54.6 0.1 collective-permute-start.12
  54.7 0.7 backward_part.8.token
  55.4 0.6 collective-permute-start.11
  56.0 0.2 collective-permute-done.12.far
  56.3 0.6 collective-permute-start.14
  56.9 0.0 copy-start.6
  56.9 1.6 %collective-permute-start.13 = (f32[136,256]{1,0:T(8,128)S(1)}, f32[136,256]{1,0:T(8,128)S(1)}, u32[]{:S(2)}, u32[]{:S(2)}) collective-permute-start(f32[136,256]{1,0:T(8,128)S(1)} %get-tuple-element.66), channel_id=1, source_target_pairs={{0,4},{1,5},{2,6},{3,7},{4,0},{5,1},{6,2},{7,3},{8,12},{9,13},{10,... | collective-permute-start | bytes 417800 | tf_op jit(solution)/shard_map/ppermute | solution.py:442
  58.5 1.9 %collective-permute-start.21 = (f32[4,64,256]{2,1,0:T(8,128)S(1)}, f32[4,64,256]{2,1,0:T(8,128)S(1)}, u32[]{:S(2)}, u32[]{:S(2)}) collective-permute-start(f32[4,64,256]{2,1,0:T(8,128)S(1)} %stack_left.1.own), channel_id=1, source_target_pairs={{0,1},{1,0},{2,3},{3,2},{4,5},{5,4},{6,7},{7,6},{8,9},{9,8},{10,11... | collective-permute-start | bytes 786440 | tf_op jit(solution)/shard_map/ppermute | solution.py:442
  60.4 0.7 backward_part.6.keep
  61.1 1.6 %collective-permute-done.14.got = f32[128,256]{1,0:T(8,128)S(1)} collective-permute-done((f32[128,256]{1,0:T(8,128)S(1)}, f32[128,256]{1,0:T(8,128)S(1)}, u32[]{:S(2)}, u32[]{:S(2)}) %collective-permute-start.14) | collective-permute-done | bytes 131104 | tf_op jit(solution)/shard_map/ppermute | solution.py:442
  62.7 2.3 %collective-permute-start.16 = (f32[64,256]{1,0:T(8,128)S(1)}, f32[64,256]{1,0:T(8,128)S(1)}, u32[]{:S(2)}, u32[]{:S(2)}) collective-permute-start(f32[64,256]{1,0:T(8,128)S(1)} %get-tuple-element.69.g2), channel_id=1, source_target_pairs={{0,16},{1,17},{2,18},{3,19},{4,20},{5,21},{6,22},{7,23},{8,24},{9,... | collective-permute-start | bytes 196616 | tf_op jit(solution)/shard_map/ppermute | solution.py:442
  65.0 1.3 %collective-permute-start.17 = (f32[64,256]{1,0:T(8,128)S(1)}, f32[64,256]{1,0:T(8,128)S(1)}, u32[]{:S(2)}, u32[]{:S(2)}) collective-permute-start(f32[64,256]{1,0:T(8,128)S(1)} %get-tuple-element.70.g3), channel_id=1, source_target_pairs={{0,24},{1,25},{2,26},{3,27},{4,28},{5,29},{6,30},{7,31},{8,16},{9,... | collective-permute-start | bytes 196616 | tf_op jit(solution)/shard_map/ppermute | solution.py:442
  66.3 0.3 right_norm.1
  66.6 0.1 collective-permute-start.15
  66.7 11.5 %all_to_all.5.squares = f32[32,1,128]{2,1,0:T(1,128)S(1)} all-to-all(f32[32,1,128]{2,1,0:T(1,128)S(1)} %bitcast.9), channel_id=1, replica_groups=mesh['doc'=16,'feat'=2] {'doc','feat'}, dimensions={0} | all-to-all | bytes 32768 | tf_op jit(solution)/shard_map/all_to_all | solution.py:500
  78.3 1.3 %finish.1 = (f32[512,256]{1,0:T(8,128)}, f32[256,256]{1,0:T(8,128)}, f32[256,256]{1,0:T(8,128)}, f32[256,256]{1,0:T(8,128)}, f32[1,256]{1,0:T(1,128)}, /*index=5*/f32[1,256]{1,0:T(1,128)}, f32[1,256]{1,0:T(1,128)}) custom-call(f32[64,256]{1,0:T(8,128)S(1)} %get-tuple-element.71.g0, f32[64,256]{1,0:T(8,128)S(1)} %collective-permute-done.15.g1, ...), custom_call_target="tpu_custom_call" | custom-call | flops 16384 | bytes 20480 | tf_op jit(solution)/shard_map/finish/pallas_call | solution.py:431
  (35 shorter events, 0.2 us)
Async XLA Ops:
  2.3 10.1 %collective-permute-start = (f32[96,256]{1,0:T(8,128)S(1)}, f32[96,256]{1,0:T(8,128)S(1)}, u32[]{:S(2)}, u32[]{:S(2)}) collective-permute-start(f32[96,256]{1,0:T(8,128)S(1)} %get-tuple-element.48), channel_id=1, source_target_pairs={{0,8},{1,9},{2,10},{3,11},{4,12},{5,13},{6,14},{7,15},{8,0},{9,1},... | collective-permute-start | bytes 294920 | tf_op jit(solution)/shard_map/ppermute | solution.py:442
  5.4 10.7 %collective-permute-start.1 = (f32[96,256]{1,0:T(8,128)S(1)}, f32[96,256]{1,0:T(8,128)S(1)}, u32[]{:S(2)}, u32[]{:S(2)}) collective-permute-start(f32[96,256]{1,0:T(8,128)S(1)} %get-tuple-element.49), channel_id=1, source_target_pairs={{0,16},{1,17},{2,18},{3,19},{4,20},{5,21},{6,22},{7,23},{8,24},{9,... | collective-permute-start | bytes 294920 | tf_op jit(solution)/shard_map/ppermute | solution.py:442
  8.0 8.1 %collective-permute-start.2 = (f32[96,256]{1,0:T(8,128)S(1)}, f32[96,256]{1,0:T(8,128)S(1)}, u32[]{:S(2)}, u32[]{:S(2)}) collective-permute-start(f32[96,256]{1,0:T(8,128)S(1)} %get-tuple-element.50), channel_id=1, source_target_pairs={{0,24},{1,25},{2,26},{3,27},{4,28},{5,29},{6,30},{7,31},{8,16},{9,... | collective-permute-start | bytes 294920 | tf_op jit(solution)/shard_map/ppermute | solution.py:442
  8.0 14.5 %collective-permute-start.5 = (f32[96,256]{1,0:T(8,128)S(1)}, f32[96,256]{1,0:T(8,128)S(1)}, u32[]{:S(2)}, u32[]{:S(2)}) collective-permute-start(f32[96,256]{1,0:T(8,128)S(1)} %get-tuple-element.54), channel_id=1, source_target_pairs={{0,8},{1,9},{2,10},{3,11},{4,12},{5,13},{6,14},{7,15},{8,0},{9,1},... | collective-permute-start | bytes 294920 | tf_op jit(solution)/shard_map/ppermute | solution.py:442
  8.9 15.4 %collective-permute-start.6 = (f32[96,256]{1,0:T(8,128)S(1)}, f32[96,256]{1,0:T(8,128)S(1)}, u32[]{:S(2)}, u32[]{:S(2)}) collective-permute-start(f32[96,256]{1,0:T(8,128)S(1)} %get-tuple-element.55), channel_id=1, source_target_pairs={{0,16},{1,17},{2,18},{3,19},{4,20},{5,21},{6,22},{7,23},{8,24},{9,... | collective-permute-start | bytes 294920 | tf_op jit(solution)/shard_map/ppermute | solution.py:442
  12.4 11.9 %collective-permute-start.7 = (f32[96,256]{1,0:T(8,128)S(1)}, f32[96,256]{1,0:T(8,128)S(1)}, u32[]{:S(2)}, u32[]{:S(2)}) collective-permute-start(f32[96,256]{1,0:T(8,128)S(1)} %get-tuple-element.56), channel_id=1, source_target_pairs={{0,24},{1,25},{2,26},{3,27},{4,28},{5,29},{6,30},{7,31},{8,16},{9,... | collective-permute-start | bytes 294920 | tf_op jit(solution)/shard_map/ppermute | solution.py:442
  16.1 19.9 %copy-start = (f32[4,64,256]{2,1,0:T(8,128)}, f32[4,64,256]{2,1,0:T(8,128)S(1)}, u32[]{:S(2)}) copy-start(f32[4,64,256]{2,1,0:T(8,128)S(1)} %stack_right.1.refs_0_.right) | copy-start | bytes 786436
  16.1 13.1 %collective-permute-start.4 = (f32[4,64,256]{2,1,0:T(8,128)S(1)}, f32[4,64,256]{2,1,0:T(8,128)S(1)}, u32[]{:S(2)}, u32[]{:S(2)}) collective-permute-start(f32[4,64,256]{2,1,0:T(8,128)S(1)} %stack_right.1.refs_0_.right), channel_id=1, source_target_pairs={{0,2},{1,3},{2,0},{3,1},{4,6},{5,7},{6,4},{7,5},{8,10},{9,11},{10,... | collective-permute-start | bytes 786440 | tf_op jit(solution)/shard_map/ppermute | solution.py:442
  16.2 15.3 %collective-permute-start.3 = (f32[4,64,256]{2,1,0:T(8,128)S(1)}, f32[4,64,256]{2,1,0:T(8,128)S(1)}, u32[]{:S(2)}, u32[]{:S(2)}) collective-permute-start(f32[4,64,256]{2,1,0:T(8,128)S(1)} %stack_right.1.refs_0_.right), channel_id=1, source_target_pairs={{0,4},{1,5},{2,6},{3,7},{4,0},{5,1},{6,2},{7,3},{8,12},{9,13},{10,... | collective-permute-start | bytes 786440 | tf_op jit(solution)/shard_map/ppermute | solution.py:442
  31.5 1.6 %collective-permute-start.8 = (f32[4,64,256]{2,1,0:T(8,128)S(1)}, f32[4,64,256]{2,1,0:T(8,128)S(1)}, u32[]{:S(2)}, u32[]{:S(2)}) collective-permute-start(f32[4,64,256]{2,1,0:T(8,128)S(1)} %collective-permute-done.3.refs_0_), channel_id=1, source_target_pairs={{0,2},{1,3},{2,0},{3,1},{4,6},{5,7},{6,4},{7,5},{8,10},{9,11},{10,... | collective-permute-start | bytes 786440 | tf_op jit(solution)/shard_map/ppermute | solution.py:442
  34.5 8.5 %collective-permute-start.10 = (f32[64,1024]{1,0:T(8,128)S(1)}, f32[64,1024]{1,0:T(8,128)S(1)}, u32[]{:S(2)}, u32[]{:S(2)}) collective-permute-start(f32[64,1024]{1,0:T(8,128)S(1)} %product_half.2.mine), channel_id=1, source_target_pairs={{0,1},{1,0},{2,3},{3,2},{4,5},{5,4},{6,7},{7,6},{8,9},{9,8},{10,11... | collective-permute-start | bytes 786440 | tf_op jit(solution)/shard_map/ppermute | solution.py:442
  38.4 1.3 %copy-start.5 = (f32[256]{0:T(256)S(1)}, f32[256]{0:T(256)}, u32[]{:S(2)}) copy-start(f32[256]{0:T(256)} %param.15) | copy-start | bytes 3076
  41.0 12.0 %collective-permute-start.9 = (f32[64,1024]{1,0:T(8,128)S(1)}, f32[64,1024]{1,0:T(8,128)S(1)}, u32[]{:S(2)}, u32[]{:S(2)}) collective-permute-start(f32[64,1024]{1,0:T(8,128)S(1)} %product_half.3.mine), channel_id=1, source_target_pairs={{0,1},{1,0},{2,3},{3,2},{4,5},{5,4},{6,7},{7,6},{8,9},{9,8},{10,11... | collective-permute-start | bytes 786440 | tf_op jit(solution)/shard_map/ppermute | solution.py:442
  43.1 12.9 %collective-permute-start.18 = (f32[64,256]{1,0:T(8,128)S(1)}, f32[64,256]{1,0:T(8,128)S(1)}, u32[]{:S(2)}, u32[]{:S(2)}) collective-permute-start(f32[64,256]{1,0:T(8,128)S(1)} %get-tuple-element.75), channel_id=1, source_target_pairs={{0,8},{1,9},{2,10},{3,11},{4,12},{5,13},{6,14},{7,15},{8,0},{9,1},... | collective-permute-start | bytes 196616 | tf_op jit(solution)/shard_map/ppermute | solution.py:442
  48.2 7.8 %collective-permute-start.19 = (f32[64,256]{1,0:T(8,128)S(1)}, f32[64,256]{1,0:T(8,128)S(1)}, u32[]{:S(2)}, u32[]{:S(2)}) collective-permute-start(f32[64,256]{1,0:T(8,128)S(1)} %get-tuple-element.76), channel_id=1, source_target_pairs={{0,16},{1,17},{2,18},{3,19},{4,20},{5,21},{6,22},{7,23},{8,24},{9,... | collective-permute-start | bytes 196616 | tf_op jit(solution)/shard_map/ppermute | solution.py:442
  49.3 6.7 %collective-permute-start.20 = (f32[64,256]{1,0:T(8,128)S(1)}, f32[64,256]{1,0:T(8,128)S(1)}, u32[]{:S(2)}, u32[]{:S(2)}) collective-permute-start(f32[64,256]{1,0:T(8,128)S(1)} %get-tuple-element.77), channel_id=1, source_target_pairs={{0,24},{1,25},{2,26},{3,27},{4,28},{5,29},{6,30},{7,31},{8,16},{9,... | collective-permute-start | bytes 196616 | tf_op jit(solution)/shard_map/ppermute | solution.py:442
  54.6 1.6 %collective-permute-start.12 = (f32[264,256]{1,0:T(8,128)S(1)}, f32[264,256]{1,0:T(8,128)S(1)}, u32[]{:S(2)}, u32[]{:S(2)}) collective-permute-start(f32[264,256]{1,0:T(8,128)S(1)} %backward_part.9), channel_id=1, source_target_pairs={{0,2},{1,3},{2,0},{3,1},{4,6},{5,7},{6,4},{7,5},{8,10},{9,11},{10,... | collective-permute-start | bytes 811016 | tf_op jit(solution)/shard_map/ppermute | solution.py:442
  55.4 5.6 %collective-permute-start.11 = (f32[256,256]{1,0:T(8,128)S(1)}, f32[256,256]{1,0:T(8,128)S(1)}, u32[]{:S(2)}, u32[]{:S(2)}) collective-permute-start(f32[256,256]{1,0:T(8,128)S(1)} %backward_part.8.token), channel_id=1, source_target_pairs={{0,2},{1,3},{2,0},{3,1},{4,6},{5,7},{6,4},{7,5},{8,10},{9,11},{10,... | collective-permute-start | bytes 786440 | tf_op jit(solution)/shard_map/ppermute | solution.py:442
  56.3 6.4 %collective-permute-start.14 = (f32[128,256]{1,0:T(8,128)S(1)}, f32[128,256]{1,0:T(8,128)S(1)}, u32[]{:S(2)}, u32[]{:S(2)}) collective-permute-start(f32[128,256]{1,0:T(8,128)S(1)} %get-tuple-element.68), channel_id=1, source_target_pairs={{0,4},{1,5},{2,6},{3,7},{4,0},{5,1},{6,2},{7,3},{8,12},{9,13},{10,... | collective-permute-start | bytes 393224 | tf_op jit(solution)/shard_map/ppermute | solution.py:442
  56.9 9.4 %copy-start.1 = (f32[4,64,256]{2,1,0:T(8,128)S(1)}, f32[4,64,256]{2,1,0:T(8,128)}, u32[]{:S(2)}) copy-start(f32[4,64,256]{2,1,0:T(8,128)} %copy-done) | copy-start | bytes 786436
  56.9 21.4 %copy-start.2 = (f32[256,256]{1,0:T(8,128)S(1)}, f32[256,256]{1,0:T(8,128)}, u32[]{:S(2)}) copy-start(f32[256,256]{1,0:T(8,128)} %right.1) | copy-start | bytes 786436
  56.9 21.4 %copy-start.3 = (f32[256,256]{1,0:T(8,128)S(1)}, f32[256,256]{1,0:T(8,128)}, u32[]{:S(2)}) copy-start(f32[256,256]{1,0:T(8,128)} %search.1) | copy-start | bytes 786436
  56.9 21.4 %copy-start.4 = (f32[256,256]{1,0:T(8,128)S(1)}, f32[256,256]{1,0:T(8,128)}, u32[]{:S(2)}) copy-start(f32[256,256]{1,0:T(8,128)} %solution.1) | copy-start | bytes 786436
  56.9 21.4 %copy-start.6 = (f32[256]{0:T(256)S(1)}, f32[256]{0:T(256)}, u32[]{:S(2)}) copy-start(f32[256]{0:T(256)} %param.16) | copy-start | bytes 3076
  56.9 21.4 %copy-start.7 = (f32[256]{0:T(256)S(1)}, f32[256]{0:T(256)}, u32[]{:S(2)}) copy-start(f32[256]{0:T(256)} %param.17) | copy-start | bytes 3076
  56.9 9.4 %collective-permute-start.13 = (f32[136,256]{1,0:T(8,128)S(1)}, f32[136,256]{1,0:T(8,128)S(1)}, u32[]{:S(2)}, u32[]{:S(2)}) collective-permute-start(f32[136,256]{1,0:T(8,128)S(1)} %get-tuple-element.66), channel_id=1, source_target_pairs={{0,4},{1,5},{2,6},{3,7},{4,0},{5,1},{6,2},{7,3},{8,12},{9,13},{10,... | collective-permute-start | bytes 417800 | tf_op jit(solution)/shard_map/ppermute | solution.py:442
  58.5 19.8 %collective-permute-start.21 = (f32[4,64,256]{2,1,0:T(8,128)S(1)}, f32[4,64,256]{2,1,0:T(8,128)S(1)}, u32[]{:S(2)}, u32[]{:S(2)}) collective-permute-start(f32[4,64,256]{2,1,0:T(8,128)S(1)} %stack_left.1.own), channel_id=1, source_target_pairs={{0,1},{1,0},{2,3},{3,2},{4,5},{5,4},{6,7},{7,6},{8,9},{9,8},{10,11... | collective-permute-start | bytes 786440 | tf_op jit(solution)/shard_map/ppermute | solution.py:442
  62.7 15.5 %collective-permute-start.16 = (f32[64,256]{1,0:T(8,128)S(1)}, f32[64,256]{1,0:T(8,128)S(1)}, u32[]{:S(2)}, u32[]{:S(2)}) collective-permute-start(f32[64,256]{1,0:T(8,128)S(1)} %get-tuple-element.69.g2), channel_id=1, source_target_pairs={{0,16},{1,17},{2,18},{3,19},{4,20},{5,21},{6,22},{7,23},{8,24},{9,... | collective-permute-start | bytes 196616 | tf_op jit(solution)/shard_map/ppermute | solution.py:442
  65.0 13.3 %collective-permute-start.17 = (f32[64,256]{1,0:T(8,128)S(1)}, f32[64,256]{1,0:T(8,128)S(1)}, u32[]{:S(2)}, u32[]{:S(2)}) collective-permute-start(f32[64,256]{1,0:T(8,128)S(1)} %get-tuple-element.70.g3), channel_id=1, source_target_pairs={{0,24},{1,25},{2,26},{3,27},{4,28},{5,29},{6,30},{7,31},{8,16},{9,... | collective-permute-start | bytes 196616 | tf_op jit(solution)/shard_map/ppermute | solution.py:442
  66.6 11.6 %collective-permute-start.15 = (f32[64,256]{1,0:T(8,128)S(1)}, f32[64,256]{1,0:T(8,128)S(1)}, u32[]{:S(2)}, u32[]{:S(2)}) collective-permute-start(f32[64,256]{1,0:T(8,128)S(1)} %get-tuple-element.72), channel_id=1, source_target_pairs={{0,8},{1,9},{2,10},{3,11},{4,12},{5,13},{6,14},{7,15},{8,0},{9,1},... | collective-permute-start | bytes 196616 | tf_op jit(solution)/shard_map/ppermute | solution.py:442

commit v19 on v16

--- a/solution.py
+++ b/solution.py
@@ -38,7 +38,7 @@
     return jax.ShapeDtypeStruct(shape, jnp.bfloat16)
 
 
-def prepare_kernel(ids_hbm, vals_hbm, right_hbm, left_hbm, stored, m0, m1, m2, m3,
+def prepare_kernel(ids_hbm, vals_hbm, right_hbm, left_hbm, stored, m0, m1, m2, m3, u0, u1, u2, u3,
                    ids, vals, wide, right, left, turned, arrived):
     _, z, y = coords()
     q, rows = turned.shape[1:]
@@ -61,11 +61,11 @@
             stored[part * lines : (part + 1) * lines, r * count : (r + 1) * count] = wide[
                 pl.ds(r, lines, stride=256 // count), :
             ]
-    for part, ref in enumerate((right, left)):
-        copies[2 + part].wait()
+    for copy, ref, outs in zip(copies[2:], (right, left), ((m0, m1, m2, m3), (u0, u1, u2, u3))):
+        copy.wait()
         turned[...] = ref[...].T.reshape(turned.shape)
-        for k, out in enumerate((m0, m1, m2, m3)):
-            out[part * q : (part + 1) * q, :] = turned[z ^ k]
+        for k, out in enumerate(outs):
+            out[...] = turned[z ^ k]
 
 
 def prepare(ids, vals, right, left):
@@ -74,8 +74,8 @@
     got = pl.pallas_call(
         prepare_kernel,
         in_specs=[pl.BlockSpec(memory_space=pltpu.HBM)] * 4,
-        out_specs=[whole()] * 5,
-        out_shape=[pltpu.VMEM((ids.size // 128, 256), jnp.float32)] + [pltpu.VMEM((2 * q, rows), jnp.float32)] * 4,
+        out_specs=[whole()] * 9,
+        out_shape=[pltpu.VMEM((ids.size // 128, 256), jnp.float32)] + [pltpu.VMEM((q, rows), jnp.float32)] * 8,
         scratch_shapes=[
             pltpu.VMEM(ids.shape, jnp.int32),
             pltpu.VMEM(vals.shape, jnp.bfloat16),
@@ -89,7 +89,7 @@
         cost_estimate=cost(0, rows * cols * 16),
         name="prepare",
     )(ids, vals, right, left)
-    return got[0], got[1:]
+    return got[0], got[1:5], got[5:]
 
 
 def stack_kernel(m0, m1, m2, m3, *refs):
@@ -157,7 +157,7 @@
         out_specs=[whole()] * 3,
         out_shape=[pltpu.VMEM((16, docs, 256), jnp.bfloat16)] * 2 + [f32(8, 128)],
         compiler_params=params(8),
-        cost_estimate=cost(2 * docs * 16 * 256 * 256, docs * 4096 * 4, 1 if rel else 64),
+        cost_estimate=cost(2 * docs * 16 * 256 * 256, docs * 4096 * 4, 1 if rel else 0.05),
         name="dense_rows",
     )(*entries, *tokens)
     return rows, token
@@ -220,7 +220,7 @@
     scale = columns[pl.ds(pl.multiple_of(z * q, q), q), :][:, 0:1]
     for k, m in enumerate(messages):
         at = slice(k * m.shape[1], (k + 1) * m.shape[1])
-        out[:, at] = product[:, at] - scale * m[q:, :]
+        out[:, at] = product[:, at] - scale * m[...]
 
 
 def product_half(rows, vec, before, blocks, *left):
@@ -454,9 +454,10 @@
     feat_total = right_vec.shape[0] * 32
     alpha_row, phibar_row, rhobar_row = (v.reshape(1, -1) for v in (alpha_prev, phibar, rhobar))
 
-    stored, messages = prepare(col_ids.T, col_vals.T, right_vec, left_vec)
+    stored, messages, mine = prepare(col_ids.T, col_vals.T, right_vec, left_vec)
     entries = along_z([stored] * 4)
     messages = along_z([messages[0]] + [after(messages[1], entries[2]), messages[2], messages[3]])
+    mine = along_z(mine)
     q = right_vec.shape[1] // 4
 
     rows1, token1 = build(entries, 1)
@@ -464,13 +465,13 @@
     own_x = swap(own, X_BIT)
     own_peer = swap(own, CORE_BIT)
     rows0, token0 = build(entries, 0, own)
-    total1 = forward_part(rows1, [own, own_peer], (0, 8), None, [token0])
+    total1 = forward_part(rows1, [own, own_peer], (0, 8), None, [token0, *mine[1:]])
     x_peer = swap(after(own_x, total1), CORE_BIT)
     total1 = forward_part(rows1, [own_x], (4,), total1)
     product1 = product_half(rows1, x_peer, total1, (12,))
     total0 = forward_part(rows0, [own, own_peer], (0, 8))
     total0 = forward_part(rows0, [own_x], (4,), total0)
-    product0 = product_half(rows0, x_peer, total0, (12,), *messages, alpha_row)
+    product0 = product_half(rows0, x_peer, total0, (12,), *mine, alpha_row)
 
     *lefts, both0, beta0 = left_half(product0, swap(product1, Y_BIT))
     partial = backward_part(rows0, both0, 0, 16)

time: 78.6 us -> 79.2 us (level)
  starting transfers between devices: 29.2 us -> 34.1 us
  waiting for transfers between devices: 7.62 us -> 3.96 us
    ppermute x22 -> x25, starting transfers between devices: 29.2 us -> 34.1 us  [swap(): return lax.ppermute(value, AXES, [(i, i ^ mask) for i in range(32)])]
    ppermute x22 -> x25, waiting for transfers between devices: 7.62 us -> 3.96 us  [swap(): return lax.ppermute(value, AXES, [(i, i ^ mask) for i in range(32)])]
  transfers between devices with their start and end apart: 22 -> 25, of which waited for: 7 -> 5; matrix products, arithmetic and copies ran while one was open for 0% -> 0% of each run, Pallas kernels for 31% -> 30%
where the time goes in v19:
time: 79.2 us; the launch traced here: 79 us
  starting transfers between devices  34.1 us (43%)
  Pallas kernels  28.3 us (36%)
  blocking collectives  11.7 us (15%)
  waiting for transfers between devices  3.96 us (5%)
  between operations  0.96 us (1%)
    ppermute x25, starting transfers between devices, swap(): return lax.ppermute(value, AXES, [(i, i ^ mask) for i in range(32)])  34.1 us
    all_to_all x1, blocking collectives, by_columns(): squares = lax.all_to_all(after(sums, left_own), AXES, 0, 0, tiled=True)  11.7 us
    pallas_call x2, Pallas kernels, build(): pl.pallas_call(functools.partial(build_kernel, rel), in_specs=[whole()] *...  9.65 us
    pallas_call x4, Pallas kernels, forward_part(): pl.pallas_call(functools.partial(forward_kernel, blocks, before is not No...  7.12 us
    pallas_call x5, Pallas kernels, backward_part(): pl.pallas_call(functools.partial(backward_kernel, first, blocks, tuple(ex...  5.2 us
    ppermute x25, waiting for transfers between devices, swap(): return lax.ppermute(value, AXES, [(i, i ^ mask) for i in range(32)])  3.96 us
    pallas_call x2, Pallas kernels, product_half(): pl.pallas_call(functools.partial(product_kernel, blocks), in_specs=[whole...  2.64 us
    pallas_call x1, Pallas kernels, prepare(): pl.pallas_call(prepare_kernel, in_specs=[pl.BlockSpec(memory_space=pltpu....  1.63 us
  transfers between devices with their start and end apart: 25, of which 5 were waited for; matrix products, arithmetic and copies ran while one was open for 0% of the time, Pallas kernels for 30%

profile of v19, /device:TPU:0, one launch (start us, length us, event | category | flops | bytes accessed | tf_op | source)
XLA Modules:
  0.0 79.0 jit_solution(14620522891180055876)
XLA Ops:
  0.6 1.6 %prepare.1 = (f32[64,256]{1,0:T(8,128)S(1)}, f32[64,256]{1,0:T(8,128)S(1)}, f32[64,256]{1,0:T(8,128)S(1)}, f32[64,256]{1,0:T(8,128)S(1)}, f32[64,256]{1,0:T(8,12...) custom-call(s32[16,512]{1,0:T(8,128)} %bitcast.13, ...), custom_call_target="tpu_custom_call" | custom-call | bytes 16384 | tf_op jit(solution)/shard_map/prepare/pallas_call | solution.py:74
  2.3 4.1 %collective-permute-start.1 = (f32[64,256]{1,0:T(8,128)S(1)}, f32[64,256]{1,0:T(8,128)S(1)}, u32[]{:S(2)}, u32[]{:S(2)}) collective-permute-start(f32[64,256]{1,0:T(8,128)S(1)} %get-tuple-element.49.e0), channel_id=1, source_target_pairs={{0,16},{1,17},{2,18},{3,19},{4,20},{5,21},{6,22},{7,23},{8,24},{9,... | collective-permute-start | bytes 196616 | tf_op jit(solution)/shard_map/ppermute | solution.py:436
  6.4 1.4 %collective-permute-start.2 = (f32[64,256]{1,0:T(8,128)S(1)}, f32[64,256]{1,0:T(8,128)S(1)}, u32[]{:S(2)}, u32[]{:S(2)}) collective-permute-start(f32[64,256]{1,0:T(8,128)S(1)} %get-tuple-element.49.e0), channel_id=1, source_target_pairs={{0,24},{1,25},{2,26},{3,27},{4,28},{5,29},{6,30},{7,31},{8,16},{9,... | collective-permute-start | bytes 196616 | tf_op jit(solution)/shard_map/ppermute | solution.py:436
  7.7 0.2 collective-permute-start
  8.0 2.8 %collective-permute-start.4 = (f32[64,256]{1,0:T(8,128)S(1)}, f32[64,256]{1,0:T(8,128)S(1)}, u32[]{:S(2)}, u32[]{:S(2)}) collective-permute-start(f32[64,256]{1,0:T(8,128)S(1)} %get-tuple-element.55), channel_id=1, source_target_pairs={{0,16},{1,17},{2,18},{3,19},{4,20},{5,21},{6,22},{7,23},{8,24},{9,... | collective-permute-start | bytes 196616 | tf_op jit(solution)/shard_map/ppermute | solution.py:436
  10.8 1.4 %collective-permute-start.5 = (f32[64,256]{1,0:T(8,128)S(1)}, f32[64,256]{1,0:T(8,128)S(1)}, u32[]{:S(2)}, u32[]{:S(2)}) collective-permute-start(f32[64,256]{1,0:T(8,128)S(1)} %get-tuple-element.56), channel_id=1, source_target_pairs={{0,24},{1,25},{2,26},{3,27},{4,28},{5,29},{6,30},{7,31},{8,16},{9,... | collective-permute-start | bytes 196616 | tf_op jit(solution)/shard_map/ppermute | solution.py:436
  12.1 0.6 collective-permute-start.8
  12.7 0.5 collective-permute-done.2.e3
  13.2 5.4 %collective-permute-start.9 = (f32[64,256]{1,0:T(8,128)S(1)}, f32[64,256]{1,0:T(8,128)S(1)}, u32[]{:S(2)}, u32[]{:S(2)}) collective-permute-start(f32[64,256]{1,0:T(8,128)S(1)} %get-tuple-element.60), channel_id=1, source_target_pairs={{0,16},{1,17},{2,18},{3,19},{4,20},{5,21},{6,22},{7,23},{8,24},{9,... | collective-permute-start | bytes 196616 | tf_op jit(solution)/shard_map/ppermute | solution.py:436
  18.6 4.7 %dense_rows.2 = (bf16[16,1024,256]{2,1,0:T(8,128)(2,1)S(1)}, bf16[16,1024,256]{2,1,0:T(8,128)(2,1)S(1)}, f32[8,128]{1,0:T(8,128)S(1)}) custom-call(f32[64,256]{1,0:T(8,128)S(1)} %get-tuple-element.49.e0, f32[64,256]{1,0:T(8,128)S(1)} %collective-permute-done.e1, f32[64,256]{1,0:T(8,128)S(1)} %collective-permute-done.1.e2, ...), custom_call_target="tpu_custom_call" | custom-call | flops 2147483648 | bytes 16777216 | tf_op jit(solution)/shard_map/dense_rows/pallas_call | solution.py:154
  23.3 1.5 %collective-permute-start.10 = (f32[64,256]{1,0:T(8,128)S(1)}, f32[64,256]{1,0:T(8,128)S(1)}, u32[]{:S(2)}, u32[]{:S(2)}) collective-permute-start(f32[64,256]{1,0:T(8,128)S(1)} %get-tuple-element.61), channel_id=1, source_target_pairs={{0,24},{1,25},{2,26},{3,27},{4,28},{5,29},{6,30},{7,31},{8,16},{9,... | collective-permute-start | bytes 196616 | tf_op jit(solution)/shard_map/ppermute | solution.py:436
  24.9 0.1 collective-permute-start.7
  25.0 1.6 %collective-permute-start.6 = (f32[4,64,256]{2,1,0:T(8,128)S(1)}, f32[4,64,256]{2,1,0:T(8,128)S(1)}, u32[]{:S(2)}, u32[]{:S(2)}) collective-permute-start(f32[4,64,256]{2,1,0:T(8,128)S(1)} %stack_right.1.refs_0_.right), channel_id=1, source_target_pairs={{0,4},{1,5},{2,6},{3,7},{4,0},{5,1},{6,2},{7,3},{8,12},{9,13},{10,... | collective-permute-start | bytes 786440 | tf_op jit(solution)/shard_map/ppermute | solution.py:436
  26.6 4.9 %dense_rows.3 = (bf16[16,1024,256]{2,1,0:T(8,128)(2,1)S(1)}, bf16[16,1024,256]{2,1,0:T(8,128)(2,1)S(1)}, f32[8,128]{1,0:T(8,128)S(1)}) custom-call(f32[64,256]{1,0:T(8,128)S(1)} %get-tuple-element.49.e0, f32[64,256]{1,0:T(8,128)S(1)} %collective-permute-done.e1, f32[64,256]{1,0:T(8,128)S(1)} %collective-permute-done.1.e2, ...), custom_call_target="tpu_custom_call" | custom-call | flops 42949672960 | bytes 335544320 | tf_op jit(solution)/shard_map/dense_rows/pallas_call | solution.py:154
  31.5 2.3 %forward_part.4.refs_1_ = f32[1024,128]{1,0:T(8,128)S(1)} custom-call(bf16[16,1024,256]{2,1,0:T(8,128)(2,1)S(1)} %get-tuple-element.50.hi_ref, bf16[16,1024,256]{2,1,0:T(8,128)(2,1)S(1)} %get-tuple-element.51.lo_ref, f32[4,64,256]{2,1,0:T(8,128)S(1)} %stack_right.1.refs_0_.right, f32[4,64,256]{2,1,0:T(8,128)S(1)} %collective-permute-done.7.refs_1_, ...), custom_call_target="tpu_custom_call" | custom-call | flops 67108864 | bytes 131072 | tf_op jit(solution)/shard_map/forward_part/pallas_call | solution.py:196
  33.9 0.2 collective-permute-start.11
  34.1 1.2 %forward_part.5.before = f32[1024,128]{1,0:T(8,128)S(1)} custom-call(bf16[16,1024,256]{2,1,0:T(8,128)(2,1)S(1)} %get-tuple-element.50.hi_ref, bf16[16,1024,256]{2,1,0:T(8,128)(2,1)S(1)} %get-tuple-element.51.lo_ref, f32[4,64,256]{2,1,0:T(8,128)S(1)} %collective-permute-done.6.refs_0_, f32[1024,128]{1,0:T(8,128)S(1)} %forward_part.4.refs_1_), custom_call_target="tpu_custom_call" | custom-call | flops 33554432 | bytes 65536 | tf_op jit(solution)/shard_map/forward_part/pallas_call | solution.py:196
  35.4 0.1 collective-permute-done.11.vec
  35.5 1.3 %product_half.2.mine = f32[64,1024]{1,0:T(8,128)S(1)} custom-call(bf16[16,1024,256]{2,1,0:T(8,128)(2,1)S(1)} %get-tuple-element.50.hi_ref, bf16[16,1024,256]{2,1,0:T(8,128)(2,1)S(1)} %get-tuple-element.51.lo_ref, f32[4,64,256]{2,1,0:T(8,128)S(1)} %collective-permute-done.11.vec, f32[1024,128]{1,0:T(8,128)S(1)} %forward_part.5.before), custom_call_target="tpu_custom_call" | custom-call | flops 33554432 | bytes 65536 | tf_op jit(solution)/shard_map/product_half/pallas_call | solution.py:228
  36.8 1.6 %collective-permute-start.13 = (f32[64,1024]{1,0:T(8,128)S(1)}, f32[64,1024]{1,0:T(8,128)S(1)}, u32[]{:S(2)}, u32[]{:S(2)}) collective-permute-start(f32[64,1024]{1,0:T(8,128)S(1)} %product_half.2.mine), channel_id=1, source_target_pairs={{0,1},{1,0},{2,3},{3,2},{4,5},{5,4},{6,7},{7,6},{8,9},{9,8},{10,11... | collective-permute-start | bytes 786440 | tf_op jit(solution)/shard_map/ppermute | solution.py:436
  38.4 2.3 %forward_part.6.refs_1_ = f32[1024,128]{1,0:T(8,128)S(1)} custom-call(bf16[16,1024,256]{2,1,0:T(8,128)(2,1)S(1)} %get-tuple-element.63.hi_ref, bf16[16,1024,256]{2,1,0:T(8,128)(2,1)S(1)} %get-tuple-element.64.lo_ref, f32[4,64,256]{2,1,0:T(8,128)S(1)} %stack_right.1.refs_0_.right, f32[4,64,256]{2,1,0:T(8,128)S(1)} %collective-permute-done.7.refs_1_), custom_call_target="tpu_custom_call" | custom-call | flops 67108864 | bytes 131072 | tf_op jit(solution)/shard_map/forward_part/pallas_call | solution.py:196
  40.7 1.2 %forward_part.7.before = f32[1024,128]{1,0:T(8,128)S(1)} custom-call(bf16[16,1024,256]{2,1,0:T(8,128)(2,1)S(1)} %get-tuple-element.63.hi_ref, bf16[16,1024,256]{2,1,0:T(8,128)(2,1)S(1)} %get-tuple-element.64.lo_ref, f32[4,64,256]{2,1,0:T(8,128)S(1)} %collective-permute-done.6.refs_0_, f32[1024,128]{1,0:T(8,128)S(1)} %forward_part.6.refs_1_), custom_call_target="tpu_custom_call" | custom-call | flops 33554432 | bytes 65536 | tf_op jit(solution)/shard_map/forward_part/pallas_call | solution.py:196
  42.0 1.3 %product_half.3.mine = f32[64,1024]{1,0:T(8,128)S(1)} custom-call(bf16[16,1024,256]{2,1,0:T(8,128)(2,1)S(1)} %get-tuple-element.63.hi_ref, bf16[16,1024,256]{2,1,0:T(8,128)(2,1)S(1)} %get-tuple-element.64.lo_ref, f32[4,64,256]{2,1,0:T(8,128)S(1)} %collective-permute-done.11.vec, f32[1024,128]{1,0:T(8,128)S(1)} %forward_part.7.before, ...), custom_call_target="tpu_custom_call" | custom-call | flops 33554432 | bytes 65536 | tf_op jit(solution)/shard_map/product_half/pallas_call | solution.py:228
  43.3 0.6 collective-permute-start.12
  43.9 1.4 %collective-permute-done.13.other = f32[64,1024]{1,0:T(8,128)S(1)} collective-permute-done((f32[64,1024]{1,0:T(8,128)S(1)}, f32[64,1024]{1,0:T(8,128)S(1)}, u32[]{:S(2)}, u32[]{:S(2)}) %collective-permute-start.13) | collective-permute-done | bytes 262176 | tf_op jit(solution)/shard_map/ppermute | solution.py:436
  45.3 0.1 left_half.2
  45.5 0.6 collective-permute-start.21
  46.1 2.3 %collective-permute-start.22 = (f32[64,256]{1,0:T(8,128)S(1)}, f32[64,256]{1,0:T(8,128)S(1)}, u32[]{:S(2)}, u32[]{:S(2)}) collective-permute-start(f32[64,256]{1,0:T(8,128)S(1)} %get-tuple-element.80), channel_id=1, source_target_pairs={{0,16},{1,17},{2,18},{3,19},{4,20},{5,21},{6,22},{7,23},{8,24},{9,... | collective-permute-start | bytes 196616 | tf_op jit(solution)/shard_map/ppermute | solution.py:436
  48.5 1.5 %collective-permute-start.23 = (f32[64,256]{1,0:T(8,128)S(1)}, f32[64,256]{1,0:T(8,128)S(1)}, u32[]{:S(2)}, u32[]{:S(2)}) collective-permute-start(f32[64,256]{1,0:T(8,128)S(1)} %get-tuple-element.81), channel_id=1, source_target_pairs={{0,24},{1,25},{2,26},{3,27},{4,28},{5,29},{6,30},{7,31},{8,16},{9,... | collective-permute-start | bytes 196616 | tf_op jit(solution)/shard_map/ppermute | solution.py:436
  49.9 2.3 %backward_part.5.refs_1_.refs_0_ = f32[1024,256]{1,0:T(8,128)S(1)} custom-call(bf16[16,1024,256]{2,1,0:T(8,128)(2,1)S(1)} %get-tuple-element.63.hi_ref, bf16[16,1024,256]{2,1,0:T(8,128)(2,1)S(1)} %get-tuple-element.64.lo_ref, bf16[128,1024]{1,0:T(8,128)(2,1)S(1)} %get-tuple-element.67.both_ref), custom_call_target="tpu_custom_call" | custom-call | flops 134217728 | bytes 262144 | tf_op jit(solution)/shard_map/backward_part/pallas_call | solution.py:309
  52.3 0.2 left_half.3
  52.4 0.7 backward_part.7.refs_1_.near
  53.2 0.7 backward_part.9
  53.9 0.1 collective-permute-start.15
  54.0 0.7 backward_part.8.token
  54.7 0.6 collective-permute-start.14
  55.3 0.2 collective-permute-done.15.far
  55.5 1.3 %collective-permute-start.17 = (f32[128,256]{1,0:T(8,128)S(1)}, f32[128,256]{1,0:T(8,128)S(1)}, u32[]{:S(2)}, u32[]{:S(2)}) collective-permute-start(f32[128,256]{1,0:T(8,128)S(1)} %get-tuple-element.72), channel_id=1, source_target_pairs={{0,4},{1,5},{2,6},{3,7},{4,0},{5,1},{6,2},{7,3},{8,12},{9,13},{10,... | collective-permute-start | bytes 393224 | tf_op jit(solution)/shard_map/ppermute | solution.py:436
  56.9 0.8 %collective-permute-start.16 = (f32[136,256]{1,0:T(8,128)S(1)}, f32[136,256]{1,0:T(8,128)S(1)}, u32[]{:S(2)}, u32[]{:S(2)}) collective-permute-start(f32[136,256]{1,0:T(8,128)S(1)} %get-tuple-element.70), channel_id=1, source_target_pairs={{0,4},{1,5},{2,6},{3,7},{4,0},{5,1},{6,2},{7,3},{8,12},{9,13},{10,... | collective-permute-start | bytes 417800 | tf_op jit(solution)/shard_map/ppermute | solution.py:436
  57.7 1.8 %collective-permute-start.24 = (f32[4,64,256]{2,1,0:T(8,128)S(1)}, f32[4,64,256]{2,1,0:T(8,128)S(1)}, u32[]{:S(2)}, u32[]{:S(2)}) collective-permute-start(f32[4,64,256]{2,1,0:T(8,128)S(1)} %stack_left.1.own), channel_id=1, source_target_pairs={{0,1},{1,0},{2,3},{3,2},{4,5},{5,4},{6,7},{7,6},{8,9},{9,8},{10,11... | collective-permute-start | bytes 786440 | tf_op jit(solution)/shard_map/ppermute | solution.py:436
  59.6 0.7 backward_part.6.keep
  60.3 1.7 %collective-permute-done.17.got = f32[128,256]{1,0:T(8,128)S(1)} collective-permute-done((f32[128,256]{1,0:T(8,128)S(1)}, f32[128,256]{1,0:T(8,128)S(1)}, u32[]{:S(2)}, u32[]{:S(2)}) %collective-permute-start.17) | collective-permute-done | bytes 131104 | tf_op jit(solution)/shard_map/ppermute | solution.py:436
  62.0 1.3 %collective-permute-start.19 = (f32[64,256]{1,0:T(8,128)S(1)}, f32[64,256]{1,0:T(8,128)S(1)}, u32[]{:S(2)}, u32[]{:S(2)}) collective-permute-start(f32[64,256]{1,0:T(8,128)S(1)} %get-tuple-element.73.g2), channel_id=1, source_target_pairs={{0,16},{1,17},{2,18},{3,19},{4,20},{5,21},{6,22},{7,23},{8,24},{9,... | collective-permute-start | bytes 196616 | tf_op jit(solution)/shard_map/ppermute | solution.py:436
  63.3 1.2 %collective-permute-start.20 = (f32[64,256]{1,0:T(8,128)S(1)}, f32[64,256]{1,0:T(8,128)S(1)}, u32[]{:S(2)}, u32[]{:S(2)}) collective-permute-start(f32[64,256]{1,0:T(8,128)S(1)} %get-tuple-element.74.g3), channel_id=1, source_target_pairs={{0,24},{1,25},{2,26},{3,27},{4,28},{5,29},{6,30},{7,31},{8,16},{9,... | collective-permute-start | bytes 196616 | tf_op jit(solution)/shard_map/ppermute | solution.py:436
  64.5 0.3 right_norm.1
  64.8 1.1 %collective-permute-start.18 = (f32[64,256]{1,0:T(8,128)S(1)}, f32[64,256]{1,0:T(8,128)S(1)}, u32[]{:S(2)}, u32[]{:S(2)}) collective-permute-start(f32[64,256]{1,0:T(8,128)S(1)} %get-tuple-element.76), channel_id=1, source_target_pairs={{0,8},{1,9},{2,10},{3,11},{4,12},{5,13},{6,14},{7,15},{8,0},{9,1},... | collective-permute-start | bytes 196616 | tf_op jit(solution)/shard_map/ppermute | solution.py:436
  65.9 11.7 %all_to_all.5.squares = f32[32,1,128]{2,1,0:T(1,128)S(1)} all-to-all(f32[32,1,128]{2,1,0:T(1,128)S(1)} %bitcast.9), channel_id=1, replica_groups=mesh['doc'=16,'feat'=2] {'doc','feat'}, dimensions={0} | all-to-all | bytes 32768 | tf_op jit(solution)/shard_map/all_to_all | solution.py:494
  77.7 1.3 %finish.1 = (f32[512,256]{1,0:T(8,128)}, f32[256,256]{1,0:T(8,128)}, f32[256,256]{1,0:T(8,128)}, f32[256,256]{1,0:T(8,128)}, f32[1,256]{1,0:T(1,128)}, /*index=5*/f32[1,256]{1,0:T(1,128)}, f32[1,256]{1,0:T(1,128)}) custom-call(f32[64,256]{1,0:T(8,128)S(1)} %get-tuple-element.75.g0, f32[64,256]{1,0:T(8,128)S(1)} %collective-permute-done.18.g1, ...), custom_call_target="tpu_custom_call" | custom-call | flops 16384 | bytes 20480 | tf_op jit(solution)/shard_map/finish/pallas_call | solution.py:425
  (41 shorter events, 0.2 us)
Async XLA Ops:
  2.3 9.9 %collective-permute-start.1 = (f32[64,256]{1,0:T(8,128)S(1)}, f32[64,256]{1,0:T(8,128)S(1)}, u32[]{:S(2)}, u32[]{:S(2)}) collective-permute-start(f32[64,256]{1,0:T(8,128)S(1)} %get-tuple-element.49.e0), channel_id=1, source_target_pairs={{0,16},{1,17},{2,18},{3,19},{4,20},{5,21},{6,22},{7,23},{8,24},{9,... | collective-permute-start | bytes 196616 | tf_op jit(solution)/shard_map/ppermute | solution.py:436
  6.4 6.9 %collective-permute-start.2 = (f32[64,256]{1,0:T(8,128)S(1)}, f32[64,256]{1,0:T(8,128)S(1)}, u32[]{:S(2)}, u32[]{:S(2)}) collective-permute-start(f32[64,256]{1,0:T(8,128)S(1)} %get-tuple-element.49.e0), channel_id=1, source_target_pairs={{0,24},{1,25},{2,26},{3,27},{4,28},{5,29},{6,30},{7,31},{8,16},{9,... | collective-permute-start | bytes 196616 | tf_op jit(solution)/shard_map/ppermute | solution.py:436
  7.7 10.8 %collective-permute-start = (f32[64,256]{1,0:T(8,128)S(1)}, f32[64,256]{1,0:T(8,128)S(1)}, u32[]{:S(2)}, u32[]{:S(2)}) collective-permute-start(f32[64,256]{1,0:T(8,128)S(1)} %get-tuple-element.49.e0), channel_id=1, source_target_pairs={{0,8},{1,9},{2,10},{3,11},{4,12},{5,13},{6,14},{7,15},{8,0},{9,1},... | collective-permute-start | bytes 196616 | tf_op jit(solution)/shard_map/ppermute | solution.py:436
  8.0 15.4 %collective-permute-start.4 = (f32[64,256]{1,0:T(8,128)S(1)}, f32[64,256]{1,0:T(8,128)S(1)}, u32[]{:S(2)}, u32[]{:S(2)}) collective-permute-start(f32[64,256]{1,0:T(8,128)S(1)} %get-tuple-element.55), channel_id=1, source_target_pairs={{0,16},{1,17},{2,18},{3,19},{4,20},{5,21},{6,22},{7,23},{8,24},{9,... | collective-permute-start | bytes 196616 | tf_op jit(solution)/shard_map/ppermute | solution.py:436
  10.8 14.1 %collective-permute-start.5 = (f32[64,256]{1,0:T(8,128)S(1)}, f32[64,256]{1,0:T(8,128)S(1)}, u32[]{:S(2)}, u32[]{:S(2)}) collective-permute-start(f32[64,256]{1,0:T(8,128)S(1)} %get-tuple-element.56), channel_id=1, source_target_pairs={{0,24},{1,25},{2,26},{3,27},{4,28},{5,29},{6,30},{7,31},{8,16},{9,... | collective-permute-start | bytes 196616 | tf_op jit(solution)/shard_map/ppermute | solution.py:436
  12.1 19.4 %collective-permute-start.8 = (f32[64,256]{1,0:T(8,128)S(1)}, f32[64,256]{1,0:T(8,128)S(1)}, u32[]{:S(2)}, u32[]{:S(2)}) collective-permute-start(f32[64,256]{1,0:T(8,128)S(1)} %get-tuple-element.59), channel_id=1, source_target_pairs={{0,8},{1,9},{2,10},{3,11},{4,12},{5,13},{6,14},{7,15},{8,0},{9,1},... | collective-permute-start | bytes 196616 | tf_op jit(solution)/shard_map/ppermute | solution.py:436
  13.2 18.3 %collective-permute-start.9 = (f32[64,256]{1,0:T(8,128)S(1)}, f32[64,256]{1,0:T(8,128)S(1)}, u32[]{:S(2)}, u32[]{:S(2)}) collective-permute-start(f32[64,256]{1,0:T(8,128)S(1)} %get-tuple-element.60), channel_id=1, source_target_pairs={{0,16},{1,17},{2,18},{3,19},{4,20},{5,21},{6,22},{7,23},{8,24},{9,... | collective-permute-start | bytes 196616 | tf_op jit(solution)/shard_map/ppermute | solution.py:436
  18.6 6.3 %collective-permute-start.3 = (f32[64,256]{1,0:T(8,128)S(1)}, f32[64,256]{1,0:T(8,128)S(1)}, u32[]{:S(2)}, u32[]{:S(2)}) collective-permute-start(f32[64,256]{1,0:T(8,128)S(1)} %get-tuple-element.54), channel_id=1, source_target_pairs={{0,8},{1,9},{2,10},{3,11},{4,12},{5,13},{6,14},{7,15},{8,0},{9,1},... | collective-permute-start | bytes 196616 | tf_op jit(solution)/shard_map/ppermute | solution.py:436
  23.3 8.2 %collective-permute-start.10 = (f32[64,256]{1,0:T(8,128)S(1)}, f32[64,256]{1,0:T(8,128)S(1)}, u32[]{:S(2)}, u32[]{:S(2)}) collective-permute-start(f32[64,256]{1,0:T(8,128)S(1)} %get-tuple-element.61), channel_id=1, source_target_pairs={{0,24},{1,25},{2,26},{3,27},{4,28},{5,29},{6,30},{7,31},{8,16},{9,... | collective-permute-start | bytes 196616 | tf_op jit(solution)/shard_map/ppermute | solution.py:436
  24.9 13.5 %copy-start = (f32[4,64,256]{2,1,0:T(8,128)}, f32[4,64,256]{2,1,0:T(8,128)S(1)}, u32[]{:S(2)}) copy-start(f32[4,64,256]{2,1,0:T(8,128)S(1)} %stack_right.1.refs_0_.right) | copy-start | bytes 786436
  24.9 6.6 %collective-permute-start.7 = (f32[4,64,256]{2,1,0:T(8,128)S(1)}, f32[4,64,256]{2,1,0:T(8,128)S(1)}, u32[]{:S(2)}, u32[]{:S(2)}) collective-permute-start(f32[4,64,256]{2,1,0:T(8,128)S(1)} %stack_right.1.refs_0_.right), channel_id=1, source_target_pairs={{0,2},{1,3},{2,0},{3,1},{4,6},{5,7},{6,4},{7,5},{8,10},{9,11},{10,... | collective-permute-start | bytes 786440 | tf_op jit(solution)/shard_map/ppermute | solution.py:436
  25.0 8.9 %collective-permute-start.6 = (f32[4,64,256]{2,1,0:T(8,128)S(1)}, f32[4,64,256]{2,1,0:T(8,128)S(1)}, u32[]{:S(2)}, u32[]{:S(2)}) collective-permute-start(f32[4,64,256]{2,1,0:T(8,128)S(1)} %stack_right.1.refs_0_.right), channel_id=1, source_target_pairs={{0,4},{1,5},{2,6},{3,7},{4,0},{5,1},{6,2},{7,3},{8,12},{9,13},{10,... | collective-permute-start | bytes 786440 | tf_op jit(solution)/shard_map/ppermute | solution.py:436
  33.9 1.6 %collective-permute-start.11 = (f32[4,64,256]{2,1,0:T(8,128)S(1)}, f32[4,64,256]{2,1,0:T(8,128)S(1)}, u32[]{:S(2)}, u32[]{:S(2)}) collective-permute-start(f32[4,64,256]{2,1,0:T(8,128)S(1)} %collective-permute-done.6.refs_0_), channel_id=1, source_target_pairs={{0,2},{1,3},{2,0},{3,1},{4,6},{5,7},{6,4},{7,5},{8,10},{9,11},{10,... | collective-permute-start | bytes 786440 | tf_op jit(solution)/shard_map/ppermute | solution.py:436
  36.8 8.5 %collective-permute-start.13 = (f32[64,1024]{1,0:T(8,128)S(1)}, f32[64,1024]{1,0:T(8,128)S(1)}, u32[]{:S(2)}, u32[]{:S(2)}) collective-permute-start(f32[64,1024]{1,0:T(8,128)S(1)} %product_half.2.mine), channel_id=1, source_target_pairs={{0,1},{1,0},{2,3},{3,2},{4,5},{5,4},{6,7},{7,6},{8,9},{9,8},{10,11... | collective-permute-start | bytes 786440 | tf_op jit(solution)/shard_map/ppermute | solution.py:436
  40.7 1.3 %copy-start.5 = (f32[256]{0:T(256)S(1)}, f32[256]{0:T(256)}, u32[]{:S(2)}) copy-start(f32[256]{0:T(256)} %param.15) | copy-start | bytes 3076
  43.3 9.0 %collective-permute-start.12 = (f32[64,1024]{1,0:T(8,128)S(1)}, f32[64,1024]{1,0:T(8,128)S(1)}, u32[]{:S(2)}, u32[]{:S(2)}) collective-permute-start(f32[64,1024]{1,0:T(8,128)S(1)} %product_half.3.mine), channel_id=1, source_target_pairs={{0,1},{1,0},{2,3},{3,2},{4,5},{5,4},{6,7},{7,6},{8,9},{9,8},{10,11... | collective-permute-start | bytes 786440 | tf_op jit(solution)/shard_map/ppermute | solution.py:436
  45.5 9.8 %collective-permute-start.21 = (f32[64,256]{1,0:T(8,128)S(1)}, f32[64,256]{1,0:T(8,128)S(1)}, u32[]{:S(2)}, u32[]{:S(2)}) collective-permute-start(f32[64,256]{1,0:T(8,128)S(1)} %get-tuple-element.79), channel_id=1, source_target_pairs={{0,8},{1,9},{2,10},{3,11},{4,12},{5,13},{6,14},{7,15},{8,0},{9,1},... | collective-permute-start | bytes 196616 | tf_op jit(solution)/shard_map/ppermute | solution.py:436
  46.1 9.1 %collective-permute-start.22 = (f32[64,256]{1,0:T(8,128)S(1)}, f32[64,256]{1,0:T(8,128)S(1)}, u32[]{:S(2)}, u32[]{:S(2)}) collective-permute-start(f32[64,256]{1,0:T(8,128)S(1)} %get-tuple-element.80), channel_id=1, source_target_pairs={{0,16},{1,17},{2,18},{3,19},{4,20},{5,21},{6,22},{7,23},{8,24},{9,... | collective-permute-start | bytes 196616 | tf_op jit(solution)/shard_map/ppermute | solution.py:436
  48.5 6.8 %collective-permute-start.23 = (f32[64,256]{1,0:T(8,128)S(1)}, f32[64,256]{1,0:T(8,128)S(1)}, u32[]{:S(2)}, u32[]{:S(2)}) collective-permute-start(f32[64,256]{1,0:T(8,128)S(1)} %get-tuple-element.81), channel_id=1, source_target_pairs={{0,24},{1,25},{2,26},{3,27},{4,28},{5,29},{6,30},{7,31},{8,16},{9,... | collective-permute-start | bytes 196616 | tf_op jit(solution)/shard_map/ppermute | solution.py:436
  53.9 1.6 %collective-permute-start.15 = (f32[264,256]{1,0:T(8,128)S(1)}, f32[264,256]{1,0:T(8,128)S(1)}, u32[]{:S(2)}, u32[]{:S(2)}) collective-permute-start(f32[264,256]{1,0:T(8,128)S(1)} %backward_part.9), channel_id=1, source_target_pairs={{0,2},{1,3},{2,0},{3,1},{4,6},{5,7},{6,4},{7,5},{8,10},{9,11},{10,... | collective-permute-start | bytes 811016 | tf_op jit(solution)/shard_map/ppermute | solution.py:436
  54.7 5.6 %collective-permute-start.14 = (f32[256,256]{1,0:T(8,128)S(1)}, f32[256,256]{1,0:T(8,128)S(1)}, u32[]{:S(2)}, u32[]{:S(2)}) collective-permute-start(f32[256,256]{1,0:T(8,128)S(1)} %backward_part.8.token), channel_id=1, source_target_pairs={{0,2},{1,3},{2,0},{3,1},{4,6},{5,7},{6,4},{7,5},{8,10},{9,11},{10,... | collective-permute-start | bytes 786440 | tf_op jit(solution)/shard_map/ppermute | solution.py:436
  55.5 6.4 %collective-permute-start.17 = (f32[128,256]{1,0:T(8,128)S(1)}, f32[128,256]{1,0:T(8,128)S(1)}, u32[]{:S(2)}, u32[]{:S(2)}) collective-permute-start(f32[128,256]{1,0:T(8,128)S(1)} %get-tuple-element.72), channel_id=1, source_target_pairs={{0,4},{1,5},{2,6},{3,7},{4,0},{5,1},{6,2},{7,3},{8,12},{9,13},{10,... | collective-permute-start | bytes 393224 | tf_op jit(solution)/shard_map/ppermute | solution.py:436
  56.9 7.6 %copy-start.1 = (f32[4,64,256]{2,1,0:T(8,128)S(1)}, f32[4,64,256]{2,1,0:T(8,128)}, u32[]{:S(2)}) copy-start(f32[4,64,256]{2,1,0:T(8,128)} %copy-done) | copy-start | bytes 786436
  56.9 20.8 %copy-start.2 = (f32[256,256]{1,0:T(8,128)S(1)}, f32[256,256]{1,0:T(8,128)}, u32[]{:S(2)}) copy-start(f32[256,256]{1,0:T(8,128)} %right.1) | copy-start | bytes 786436
  56.9 20.8 %copy-start.3 = (f32[256,256]{1,0:T(8,128)S(1)}, f32[256,256]{1,0:T(8,128)}, u32[]{:S(2)}) copy-start(f32[256,256]{1,0:T(8,128)} %search.1) | copy-start | bytes 786436
  56.9 20.8 %copy-start.4 = (f32[256,256]{1,0:T(8,128)S(1)}, f32[256,256]{1,0:T(8,128)}, u32[]{:S(2)}) copy-start(f32[256,256]{1,0:T(8,128)} %solution.1) | copy-start | bytes 786436
  56.9 20.8 %copy-start.6 = (f32[256]{0:T(256)S(1)}, f32[256]{0:T(256)}, u32[]{:S(2)}) copy-start(f32[256]{0:T(256)} %param.16) | copy-start | bytes 3076
  56.9 20.8 %copy-start.7 = (f32[256]{0:T(256)S(1)}, f32[256]{0:T(256)}, u32[]{:S(2)}) copy-start(f32[256]{0:T(256)} %param.17) | copy-start | bytes 3076
  56.9 7.6 %collective-permute-start.16 = (f32[136,256]{1,0:T(8,128)S(1)}, f32[136,256]{1,0:T(8,128)S(1)}, u32[]{:S(2)}, u32[]{:S(2)}) collective-permute-start(f32[136,256]{1,0:T(8,128)S(1)} %get-tuple-element.70), channel_id=1, source_target_pairs={{0,4},{1,5},{2,6},{3,7},{4,0},{5,1},{6,2},{7,3},{8,12},{9,13},{10,... | collective-permute-start | bytes 417800 | tf_op jit(solution)/shard_map/ppermute | solution.py:436
  57.7 19.9 %collective-permute-start.24 = (f32[4,64,256]{2,1,0:T(8,128)S(1)}, f32[4,64,256]{2,1,0:T(8,128)S(1)}, u32[]{:S(2)}, u32[]{:S(2)}) collective-permute-start(f32[4,64,256]{2,1,0:T(8,128)S(1)} %stack_left.1.own), channel_id=1, source_target_pairs={{0,1},{1,0},{2,3},{3,2},{4,5},{5,4},{6,7},{7,6},{8,9},{9,8},{10,11... | collective-permute-start | bytes 786440 | tf_op jit(solution)/shard_map/ppermute | solution.py:436
  62.0 15.7 %collective-permute-start.19 = (f32[64,256]{1,0:T(8,128)S(1)}, f32[64,256]{1,0:T(8,128)S(1)}, u32[]{:S(2)}, u32[]{:S(2)}) collective-permute-start(f32[64,256]{1,0:T(8,128)S(1)} %get-tuple-element.73.g2), channel_id=1, source_target_pairs={{0,16},{1,17},{2,18},{3,19},{4,20},{5,21},{6,22},{7,23},{8,24},{9,... | collective-permute-start | bytes 196616 | tf_op jit(solution)/shard_map/ppermute | solution.py:436
  63.3 14.4 %collective-permute-start.20 = (f32[64,256]{1,0:T(8,128)S(1)}, f32[64,256]{1,0:T(8,128)S(1)}, u32[]{:S(2)}, u32[]{:S(2)}) collective-permute-start(f32[64,256]{1,0:T(8,128)S(1)} %get-tuple-element.74.g3), channel_id=1, source_target_pairs={{0,24},{1,25},{2,26},{3,27},{4,28},{5,29},{6,30},{7,31},{8,16},{9,... | collective-permute-start | bytes 196616 | tf_op jit(solution)/shard_map/ppermute | solution.py:436
  64.8 12.8 %collective-permute-start.18 = (f32[64,256]{1,0:T(8,128)S(1)}, f32[64,256]{1,0:T(8,128)S(1)}, u32[]{:S(2)}, u32[]{:S(2)}) collective-permute-start(f32[64,256]{1,0:T(8,128)S(1)} %get-tuple-element.76), channel_id=1, source_target_pairs={{0,8},{1,9},{2,10},{3,11},{4,12},{5,13},{6,14},{7,15},{8,0},{9,1},... | collective-permute-start | bytes 196616 | tf_op jit(solution)/shard_map/ppermute | solution.py:436

commit v20 on v16

--- a/solution.py
+++ b/solution.py
@@ -13,6 +13,7 @@
 
 
 Y_BIT, CORE_BIT, X_BIT, Z_SHIFT = 1, 2, 4, 3
+BACKWARDS = list(range(31, -1, -1))
 NT = (((1,), (1,)), ((), ()))
 
 
@@ -388,7 +389,7 @@
                   left_out, right_out, search_out, solution_out, alpha_out, phibar_out, rhobar_out, turned):
     _, z, y = coords()
     q, half = turned.shape[1:]
-    parts = [squares[i] for i in range(32)]
+    parts = [squares[i] for i in BACKWARDS]
     high = [jnp.concatenate([parts[8 * i][:, q:], parts[8 * i][:, :q]], axis=1) if i % 2 == 0 else parts[8 * i] for i in range(4)]
     while len(parts) > 4:
         parts = [a + b for a, b in zip(parts[::2], parts[1::2])]
@@ -490,7 +491,7 @@
     g0, g1, sums = right_norm(docs_total, keep, peer, got_near, beta_core, own, (g2, g3))
     pieces = [g0, swap(g1, 1 << Z_SHIFT), p2, p3]
     left_other = swap(after(left_own, send_far), Y_BIT)
-    squares = lax.all_to_all(after(sums, left_own), AXES, 0, 0, tiled=True)
+    squares = lax.all_to_all(after(sums, left_own), AXES, 0, 0, axis_index_groups=[BACKWARDS], tiled=True)
     left_next, right_next, search_next, solution_next, alpha_next, phibar_next, rhobar_next = finish(
         docs_total, feat_total, pieces, squares, left_own, left_other,
         right_vec, search_dir, solution_vec, phibar_row, rhobar_row,

time: 78.6 us -> 78.4 us (level)
  no operation moved by 1% of the time
where the time goes in v20:
time: 78.4 us; the launch traced here: 78.3 us
  starting transfers between devices  29.2 us (37%)
  Pallas kernels  28.3 us (36%)
  blocking collectives  12.2 us (16%)
  waiting for transfers between devices  7.62 us (10%)
  between operations  0.93 us (1%)
    ppermute x22, starting transfers between devices, swap(): return lax.ppermute(value, AXES, [(i, i ^ mask) for i in range(32)])  29.2 us
    all_to_all x1, blocking collectives, by_columns(): lax.all_to_all(after(sums, left_own), AXES, 0, 0, axis_index_groups=[BACK...  12.2 us
    pallas_call x2, Pallas kernels, build(): pl.pallas_call(functools.partial(build_kernel, rel), in_specs=[whole()] *...  9.66 us
    ppermute x22, waiting for transfers between devices, swap(): return lax.ppermute(value, AXES, [(i, i ^ mask) for i in range(32)])  7.62 us
    pallas_call x4, Pallas kernels, forward_part(): pl.pallas_call(functools.partial(forward_kernel, blocks, before is not No...  7.12 us
    pallas_call x5, Pallas kernels, backward_part(): pl.pallas_call(functools.partial(backward_kernel, first, blocks, tuple(ex...  5.19 us
    pallas_call x2, Pallas kernels, product_half(): pl.pallas_call(functools.partial(product_kernel, blocks), in_specs=[whole...  2.64 us
    pallas_call x1, Pallas kernels, prepare(): pl.pallas_call(prepare_kernel, in_specs=[pl.BlockSpec(memory_space=pltpu....  1.63 us
  transfers between devices with their start and end apart: 22, of which 7 were waited for; matrix products, arithmetic and copies ran while one was open for 0% of the time, Pallas kernels for 31%

profile of v20, /device:TPU:0, one launch (start us, length us, event | category | flops | bytes accessed | tf_op | source)
XLA Modules:
  0.0 78.3 jit_solution(1620233009523600774)
XLA Ops:
  0.6 1.6 %prepare.1 = (f32[64,256]{1,0:T(8,128)S(1)}, f32[128,256]{1,0:T(8,128)S(1)}, f32[128,256]{1,0:T(8,128)S(1)}, f32[128,256]{1,0:T(8,128)S(1)}, f32[128,256]{1,0:T(8,128)S(1)}) custom-call(s32[16,512]{1,0:T(8,128)} %bitcast.13, bf16[16,512]{1,0:T(8,128)(2,1)} %bitcast.14, f32[256,256]{1,0:T(8,128)} %right.1, f32[512,256]{1,0:T(8,128)} %left_hbm.1), custom_call_target="tpu_custom_call" | custom-call | bytes 16384 | tf_op jit(solution)/shard_map/prepare/pallas_call | solution.py:75
  2.3 4.1 %collective-permute-start.1 = (f32[64,256]{1,0:T(8,128)S(1)}, f32[64,256]{1,0:T(8,128)S(1)}, u32[]{:S(2)}, u32[]{:S(2)}) collective-permute-start(f32[64,256]{1,0:T(8,128)S(1)} %get-tuple-element.45.e0), channel_id=1, source_target_pairs={{0,16},{1,17},{2,18},{3,19},{4,20},{5,21},{6,22},{7,23},{8,24},{9,... | collective-permute-start | bytes 196616 | tf_op jit(solution)/shard_map/ppermute | solution.py:437
  6.4 1.4 %collective-permute-start.2 = (f32[64,256]{1,0:T(8,128)S(1)}, f32[64,256]{1,0:T(8,128)S(1)}, u32[]{:S(2)}, u32[]{:S(2)}) collective-permute-start(f32[64,256]{1,0:T(8,128)S(1)} %get-tuple-element.45.e0), channel_id=1, source_target_pairs={{0,24},{1,25},{2,26},{3,27},{4,28},{5,29},{6,30},{7,31},{8,16},{9,... | collective-permute-start | bytes 196616 | tf_op jit(solution)/shard_map/ppermute | solution.py:437
  7.7 0.2 collective-permute-start
  8.0 2.8 %collective-permute-start.4 = (f32[128,256]{1,0:T(8,128)S(1)}, f32[128,256]{1,0:T(8,128)S(1)}, u32[]{:S(2)}, u32[]{:S(2)}) collective-permute-start(f32[128,256]{1,0:T(8,128)S(1)} %get-tuple-element.51), channel_id=1, source_target_pairs={{0,16},{1,17},{2,18},{3,19},{4,20},{5,21},{6,22},{7,23},{8,24},{9,... | collective-permute-start | bytes 393224 | tf_op jit(solution)/shard_map/ppermute | solution.py:437
  10.8 1.4 %collective-permute-start.5 = (f32[128,256]{1,0:T(8,128)S(1)}, f32[128,256]{1,0:T(8,128)S(1)}, u32[]{:S(2)}, u32[]{:S(2)}) collective-permute-start(f32[128,256]{1,0:T(8,128)S(1)} %get-tuple-element.52), channel_id=1, source_target_pairs={{0,24},{1,25},{2,26},{3,27},{4,28},{5,29},{6,30},{7,31},{8,16},{9,... | collective-permute-start | bytes 393224 | tf_op jit(solution)/shard_map/ppermute | solution.py:437
  12.1 0.6 collective-permute-start.3
  12.7 0.5 collective-permute-done.2.e3
  13.3 4.7 %dense_rows.2 = (bf16[16,1024,256]{2,1,0:T(8,128)(2,1)S(1)}, bf16[16,1024,256]{2,1,0:T(8,128)(2,1)S(1)}, f32[8,128]{1,0:T(8,128)S(1)}) custom-call(f32[64,256]{1,0:T(8,128)S(1)} %get-tuple-element.45.e0, f32[64,256]{1,0:T(8,128)S(1)} %collective-permute-done.e1, f32[64,256]{1,0:T(8,128)S(1)} %collective-permute-done.1.e2, ...), custom_call_target="tpu_custom_call" | custom-call | flops 2147483648 | bytes 16777216 | tf_op jit(solution)/shard_map/dense_rows/pallas_call | solution.py:155
  18.1 3.6 %collective-permute-done.4.m2.refs_2_ = f32[128,256]{1,0:T(8,128)S(1)} collective-permute-done((f32[128,256]{1,0:T(8,128)S(1)}, f32[128,256]{1,0:T(8,128)S(1)}, u32[]{:S(2)}, u32[]{:S(2)}) %collective-permute-start.4) | collective-permute-done | bytes 131104 | tf_op jit(solution)/shard_map/ppermute | solution.py:437
  21.7 0.1 collective-permute-done.3.m1.refs_1_
  21.8 0.1 collective-permute-start.7
  21.9 1.8 %collective-permute-start.6 = (f32[4,64,256]{2,1,0:T(8,128)S(1)}, f32[4,64,256]{2,1,0:T(8,128)S(1)}, u32[]{:S(2)}, u32[]{:S(2)}) collective-permute-start(f32[4,64,256]{2,1,0:T(8,128)S(1)} %stack_right.1.refs_0_.right), channel_id=1, source_target_pairs={{0,4},{1,5},{2,6},{3,7},{4,0},{5,1},{6,2},{7,3},{8,12},{9,13},{10,... | collective-permute-start | bytes 786440 | tf_op jit(solution)/shard_map/ppermute | solution.py:437
  23.6 4.9 %dense_rows.3 = (bf16[16,1024,256]{2,1,0:T(8,128)(2,1)S(1)}, bf16[16,1024,256]{2,1,0:T(8,128)(2,1)S(1)}, f32[8,128]{1,0:T(8,128)S(1)}) custom-call(f32[64,256]{1,0:T(8,128)S(1)} %get-tuple-element.45.e0, f32[64,256]{1,0:T(8,128)S(1)} %collective-permute-done.e1, f32[64,256]{1,0:T(8,128)S(1)} %collective-permute-done.1.e2, ...), custom_call_target="tpu_custom_call" | custom-call | flops 33554432 | bytes 262144 | tf_op jit(solution)/shard_map/dense_rows/pallas_call | solution.py:155
  28.6 2.3 %forward_part.4.refs_1_ = f32[1024,128]{1,0:T(8,128)S(1)} custom-call(bf16[16,1024,256]{2,1,0:T(8,128)(2,1)S(1)} %get-tuple-element.46.hi_ref, bf16[16,1024,256]{2,1,0:T(8,128)(2,1)S(1)} %get-tuple-element.47.lo_ref, f32[4,64,256]{2,1,0:T(8,128)S(1)} %stack_right.1.refs_0_.right, f32[4,64,256]{2,1,0:T(8,128)S(1)} %collective-permute-done.7.refs_1_, ...), custom_call_target="tpu_custom_call" | custom-call | flops 67108864 | bytes 131072 | tf_op jit(solution)/shard_map/forward_part/pallas_call | solution.py:197
  30.9 0.3 collective-permute-start.8
  31.2 1.2 %forward_part.5.before = f32[1024,128]{1,0:T(8,128)S(1)} custom-call(bf16[16,1024,256]{2,1,0:T(8,128)(2,1)S(1)} %get-tuple-element.46.hi_ref, bf16[16,1024,256]{2,1,0:T(8,128)(2,1)S(1)} %get-tuple-element.47.lo_ref, f32[4,64,256]{2,1,0:T(8,128)S(1)} %collective-permute-done.6.refs_0_, f32[1024,128]{1,0:T(8,128)S(1)} %forward_part.4.refs_1_), custom_call_target="tpu_custom_call" | custom-call | flops 33554432 | bytes 65536 | tf_op jit(solution)/shard_map/forward_part/pallas_call | solution.py:197
  32.4 0.1 collective-permute-done.8.vec
  32.5 1.3 %product_half.2.mine = f32[64,1024]{1,0:T(8,128)S(1)} custom-call(bf16[16,1024,256]{2,1,0:T(8,128)(2,1)S(1)} %get-tuple-element.46.hi_ref, bf16[16,1024,256]{2,1,0:T(8,128)(2,1)S(1)} %get-tuple-element.47.lo_ref, f32[4,64,256]{2,1,0:T(8,128)S(1)} %collective-permute-done.8.vec, f32[1024,128]{1,0:T(8,128)S(1)} %forward_part.5.before), custom_call_target="tpu_custom_call" | custom-call | flops 33554432 | bytes 65536 | tf_op jit(solution)/shard_map/product_half/pallas_call | solution.py:229
  33.8 1.6 %collective-permute-start.10 = (f32[64,1024]{1,0:T(8,128)S(1)}, f32[64,1024]{1,0:T(8,128)S(1)}, u32[]{:S(2)}, u32[]{:S(2)}) collective-permute-start(f32[64,1024]{1,0:T(8,128)S(1)} %product_half.2.mine), channel_id=1, source_target_pairs={{0,1},{1,0},{2,3},{3,2},{4,5},{5,4},{6,7},{7,6},{8,9},{9,8},{10,11... | collective-permute-start | bytes 786440 | tf_op jit(solution)/shard_map/ppermute | solution.py:437
  35.4 2.3 %forward_part.6.refs_1_ = f32[1024,128]{1,0:T(8,128)S(1)} custom-call(bf16[16,1024,256]{2,1,0:T(8,128)(2,1)S(1)} %get-tuple-element.56.hi_ref, bf16[16,1024,256]{2,1,0:T(8,128)(2,1)S(1)} %get-tuple-element.57.lo_ref, f32[4,64,256]{2,1,0:T(8,128)S(1)} %stack_right.1.refs_0_.right, f32[4,64,256]{2,1,0:T(8,128)S(1)} %collective-permute-done.7.refs_1_), custom_call_target="tpu_custom_call" | custom-call | flops 67108864 | bytes 131072 | tf_op jit(solution)/shard_map/forward_part/pallas_call | solution.py:197
  37.8 1.2 %forward_part.7.before = f32[1024,128]{1,0:T(8,128)S(1)} custom-call(bf16[16,1024,256]{2,1,0:T(8,128)(2,1)S(1)} %get-tuple-element.56.hi_ref, bf16[16,1024,256]{2,1,0:T(8,128)(2,1)S(1)} %get-tuple-element.57.lo_ref, f32[4,64,256]{2,1,0:T(8,128)S(1)} %collective-permute-done.6.refs_0_, f32[1024,128]{1,0:T(8,128)S(1)} %forward_part.6.refs_1_), custom_call_target="tpu_custom_call" | custom-call | flops 33554432 | bytes 65536 | tf_op jit(solution)/shard_map/forward_part/pallas_call | solution.py:197
  39.0 1.3 %product_half.3.mine = f32[64,1024]{1,0:T(8,128)S(1)} custom-call(bf16[16,1024,256]{2,1,0:T(8,128)(2,1)S(1)} %get-tuple-element.56.hi_ref, bf16[16,1024,256]{2,1,0:T(8,128)(2,1)S(1)} %get-tuple-element.57.lo_ref, f32[4,64,256]{2,1,0:T(8,128)S(1)} %collective-permute-done.8.vec, f32[1024,128]{1,0:T(8,128)S(1)} %forward_part.7.before, ...), custom_call_target="tpu_custom_call" | custom-call | flops 33554432 | bytes 65536 | tf_op jit(solution)/shard_map/product_half/pallas_call | solution.py:229
  40.4 0.5 collective-permute-start.9
  40.9 1.4 %collective-permute-done.10.other = f32[64,1024]{1,0:T(8,128)S(1)} collective-permute-done((f32[64,1024]{1,0:T(8,128)S(1)}, f32[64,1024]{1,0:T(8,128)S(1)}, u32[]{:S(2)}, u32[]{:S(2)}) %collective-permute-start.10) | collective-permute-done | bytes 262176 | tf_op jit(solution)/shard_map/ppermute | solution.py:437
  42.3 0.2 left_half.2
  42.5 3.0 %collective-permute-start.18 = (f32[64,256]{1,0:T(8,128)S(1)}, f32[64,256]{1,0:T(8,128)S(1)}, u32[]{:S(2)}, u32[]{:S(2)}) collective-permute-start(f32[64,256]{1,0:T(8,128)S(1)} %get-tuple-element.71), channel_id=1, source_target_pairs={{0,8},{1,9},{2,10},{3,11},{4,12},{5,13},{6,14},{7,15},{8,0},{9,1},... | collective-permute-start | bytes 196616 | tf_op jit(solution)/shard_map/ppermute | solution.py:437
  45.5 1.8 %collective-permute-start.19 = (f32[64,256]{1,0:T(8,128)S(1)}, f32[64,256]{1,0:T(8,128)S(1)}, u32[]{:S(2)}, u32[]{:S(2)}) collective-permute-start(f32[64,256]{1,0:T(8,128)S(1)} %get-tuple-element.72), channel_id=1, source_target_pairs={{0,16},{1,17},{2,18},{3,19},{4,20},{5,21},{6,22},{7,23},{8,24},{9,... | collective-permute-start | bytes 196616 | tf_op jit(solution)/shard_map/ppermute | solution.py:437
  47.3 1.4 %collective-permute-start.20 = (f32[64,256]{1,0:T(8,128)S(1)}, f32[64,256]{1,0:T(8,128)S(1)}, u32[]{:S(2)}, u32[]{:S(2)}) collective-permute-start(f32[64,256]{1,0:T(8,128)S(1)} %get-tuple-element.73), channel_id=1, source_target_pairs={{0,24},{1,25},{2,26},{3,27},{4,28},{5,29},{6,30},{7,31},{8,16},{9,... | collective-permute-start | bytes 196616 | tf_op jit(solution)/shard_map/ppermute | solution.py:437
  48.7 2.3 %backward_part.5.refs_1_.refs_0_ = f32[1024,256]{1,0:T(8,128)S(1)} custom-call(bf16[16,1024,256]{2,1,0:T(8,128)(2,1)S(1)} %get-tuple-element.56.hi_ref, bf16[16,1024,256]{2,1,0:T(8,128)(2,1)S(1)} %get-tuple-element.57.lo_ref, bf16[128,1024]{1,0:T(8,128)(2,1)S(1)} %get-tuple-element.59.both_ref), custom_call_target="tpu_custom_call" | custom-call | flops 134217728 | bytes 262144 | tf_op jit(solution)/shard_map/backward_part/pallas_call | solution.py:310
  51.0 0.2 left_half.3
  51.2 0.7 backward_part.7.refs_1_.near
  51.9 0.7 backward_part.9
  52.6 0.1 collective-permute-start.12
  52.7 0.7 backward_part.8.token
  53.4 0.6 collective-permute-start.11
  54.0 0.2 collective-permute-done.12.far
  54.3 1.4 %collective-permute-start.14 = (f32[128,256]{1,0:T(8,128)S(1)}, f32[128,256]{1,0:T(8,128)S(1)}, u32[]{:S(2)}, u32[]{:S(2)}) collective-permute-start(f32[128,256]{1,0:T(8,128)S(1)} %get-tuple-element.64), channel_id=1, source_target_pairs={{0,4},{1,5},{2,6},{3,7},{4,0},{5,1},{6,2},{7,3},{8,12},{9,13},{10,... | collective-permute-start | bytes 393224 | tf_op jit(solution)/shard_map/ppermute | solution.py:437
  55.7 0.8 collective-permute-start.13
  56.5 1.9 %collective-permute-start.21 = (f32[4,64,256]{2,1,0:T(8,128)S(1)}, f32[4,64,256]{2,1,0:T(8,128)S(1)}, u32[]{:S(2)}, u32[]{:S(2)}) collective-permute-start(f32[4,64,256]{2,1,0:T(8,128)S(1)} %stack_left.1.own), channel_id=1, source_target_pairs={{0,1},{1,0},{2,3},{3,2},{4,5},{5,4},{6,7},{7,6},{8,9},{9,8},{10,11... | collective-permute-start | bytes 786440 | tf_op jit(solution)/shard_map/ppermute | solution.py:437
  58.4 0.7 backward_part.6.keep
  59.1 1.6 %collective-permute-done.14.got = f32[128,256]{1,0:T(8,128)S(1)} collective-permute-done((f32[128,256]{1,0:T(8,128)S(1)}, f32[128,256]{1,0:T(8,128)S(1)}, u32[]{:S(2)}, u32[]{:S(2)}) %collective-permute-start.14) | collective-permute-done | bytes 131104 | tf_op jit(solution)/shard_map/ppermute | solution.py:437
  60.7 2.3 %collective-permute-start.16 = (f32[64,256]{1,0:T(8,128)S(1)}, f32[64,256]{1,0:T(8,128)S(1)}, u32[]{:S(2)}, u32[]{:S(2)}) collective-permute-start(f32[64,256]{1,0:T(8,128)S(1)} %get-tuple-element.65.g2), channel_id=1, source_target_pairs={{0,16},{1,17},{2,18},{3,19},{4,20},{5,21},{6,22},{7,23},{8,24},{9,... | collective-permute-start | bytes 196616 | tf_op jit(solution)/shard_map/ppermute | solution.py:437
  63.0 0.8 %collective-permute-start.17 = (f32[64,256]{1,0:T(8,128)S(1)}, f32[64,256]{1,0:T(8,128)S(1)}, u32[]{:S(2)}, u32[]{:S(2)}) collective-permute-start(f32[64,256]{1,0:T(8,128)S(1)} %get-tuple-element.66.g3), channel_id=1, source_target_pairs={{0,24},{1,25},{2,26},{3,27},{4,28},{5,29},{6,30},{7,31},{8,16},{9,... | collective-permute-start | bytes 196616 | tf_op jit(solution)/shard_map/ppermute | solution.py:437
  63.8 0.3 right_norm.1
  64.1 0.5 collective-permute-start.15
  64.7 12.2 %all_to_all.5.squares = f32[32,1,128]{2,1,0:T(1,128)S(1)} all-to-all(f32[32,1,128]{2,1,0:T(1,128)S(1)} %bitcast.9), channel_id=1, replica_groups={{31,30,29,28,27,26,25,24,23,22,21,20,19,18,17,16,15,14,13,12,11,10,9,8,..., dimensions={0} | all-to-all | bytes 32768 | tf_op jit(solution)/shard_map/all_to_all | solution.py:494
  76.9 1.3 %finish.1 = (f32[512,256]{1,0:T(8,128)}, f32[256,256]{1,0:T(8,128)}, f32[256,256]{1,0:T(8,128)}, f32[256,256]{1,0:T(8,128)}, f32[1,256]{1,0:T(1,128)}, /*index=5*/f32[1,256]{1,0:T(1,128)}, f32[1,256]{1,0:T(1,128)}) custom-call(f32[64,256]{1,0:T(8,128)S(1)} %get-tuple-element.67.g0, f32[64,256]{1,0:T(8,128)S(1)} %collective-permute-done.15.g1, ...), custom_call_target="tpu_custom_call" | custom-call | flops 16384 | bytes 20480 | tf_op jit(solution)/shard_map/finish/pallas_call | solution.py:426
  (35 shorter events, 0.2 us)
Async XLA Ops:
  2.3 9.9 %collective-permute-start.1 = (f32[64,256]{1,0:T(8,128)S(1)}, f32[64,256]{1,0:T(8,128)S(1)}, u32[]{:S(2)}, u32[]{:S(2)}) collective-permute-start(f32[64,256]{1,0:T(8,128)S(1)} %get-tuple-element.45.e0), channel_id=1, source_target_pairs={{0,16},{1,17},{2,18},{3,19},{4,20},{5,21},{6,22},{7,23},{8,24},{9,... | collective-permute-start | bytes 196616 | tf_op jit(solution)/shard_map/ppermute | solution.py:437
  6.4 6.9 %collective-permute-start.2 = (f32[64,256]{1,0:T(8,128)S(1)}, f32[64,256]{1,0:T(8,128)S(1)}, u32[]{:S(2)}, u32[]{:S(2)}) collective-permute-start(f32[64,256]{1,0:T(8,128)S(1)} %get-tuple-element.45.e0), channel_id=1, source_target_pairs={{0,24},{1,25},{2,26},{3,27},{4,28},{5,29},{6,30},{7,31},{8,16},{9,... | collective-permute-start | bytes 196616 | tf_op jit(solution)/shard_map/ppermute | solution.py:437
  7.7 5.6 %collective-permute-start = (f32[64,256]{1,0:T(8,128)S(1)}, f32[64,256]{1,0:T(8,128)S(1)}, u32[]{:S(2)}, u32[]{:S(2)}) collective-permute-start(f32[64,256]{1,0:T(8,128)S(1)} %get-tuple-element.45.e0), channel_id=1, source_target_pairs={{0,8},{1,9},{2,10},{3,11},{4,12},{5,13},{6,14},{7,15},{8,0},{9,1},... | collective-permute-start | bytes 196616 | tf_op jit(solution)/shard_map/ppermute | solution.py:437
  8.0 13.7 %collective-permute-start.4 = (f32[128,256]{1,0:T(8,128)S(1)}, f32[128,256]{1,0:T(8,128)S(1)}, u32[]{:S(2)}, u32[]{:S(2)}) collective-permute-start(f32[128,256]{1,0:T(8,128)S(1)} %get-tuple-element.51), channel_id=1, source_target_pairs={{0,16},{1,17},{2,18},{3,19},{4,20},{5,21},{6,22},{7,23},{8,24},{9,... | collective-permute-start | bytes 393224 | tf_op jit(solution)/shard_map/ppermute | solution.py:437
  10.8 10.9 %collective-permute-start.5 = (f32[128,256]{1,0:T(8,128)S(1)}, f32[128,256]{1,0:T(8,128)S(1)}, u32[]{:S(2)}, u32[]{:S(2)}) collective-permute-start(f32[128,256]{1,0:T(8,128)S(1)} %get-tuple-element.52), channel_id=1, source_target_pairs={{0,24},{1,25},{2,26},{3,27},{4,28},{5,29},{6,30},{7,31},{8,16},{9,... | collective-permute-start | bytes 393224 | tf_op jit(solution)/shard_map/ppermute | solution.py:437
  12.1 9.6 %collective-permute-start.3 = (f32[128,256]{1,0:T(8,128)S(1)}, f32[128,256]{1,0:T(8,128)S(1)}, u32[]{:S(2)}, u32[]{:S(2)}) collective-permute-start(f32[128,256]{1,0:T(8,128)S(1)} %get-tuple-element.50), channel_id=1, source_target_pairs={{0,8},{1,9},{2,10},{3,11},{4,12},{5,13},{6,14},{7,15},{8,0},{9,1},... | collective-permute-start | bytes 393224 | tf_op jit(solution)/shard_map/ppermute | solution.py:437
  21.8 13.6 %copy-start = (f32[4,64,256]{2,1,0:T(8,128)}, f32[4,64,256]{2,1,0:T(8,128)S(1)}, u32[]{:S(2)}) copy-start(f32[4,64,256]{2,1,0:T(8,128)S(1)} %stack_right.1.refs_0_.right) | copy-start | bytes 786436
  21.8 6.8 %collective-permute-start.7 = (f32[4,64,256]{2,1,0:T(8,128)S(1)}, f32[4,64,256]{2,1,0:T(8,128)S(1)}, u32[]{:S(2)}, u32[]{:S(2)}) collective-permute-start(f32[4,64,256]{2,1,0:T(8,128)S(1)} %stack_right.1.refs_0_.right), channel_id=1, source_target_pairs={{0,2},{1,3},{2,0},{3,1},{4,6},{5,7},{6,4},{7,5},{8,10},{9,11},{10,... | collective-permute-start | bytes 786440 | tf_op jit(solution)/shard_map/ppermute | solution.py:437
  21.9 9.0 %collective-permute-start.6 = (f32[4,64,256]{2,1,0:T(8,128)S(1)}, f32[4,64,256]{2,1,0:T(8,128)S(1)}, u32[]{:S(2)}, u32[]{:S(2)}) collective-permute-start(f32[4,64,256]{2,1,0:T(8,128)S(1)} %stack_right.1.refs_0_.right), channel_id=1, source_target_pairs={{0,4},{1,5},{2,6},{3,7},{4,0},{5,1},{6,2},{7,3},{8,12},{9,13},{10,... | collective-permute-start | bytes 786440 | tf_op jit(solution)/shard_map/ppermute | solution.py:437
  30.9 1.6 %collective-permute-start.8 = (f32[4,64,256]{2,1,0:T(8,128)S(1)}, f32[4,64,256]{2,1,0:T(8,128)S(1)}, u32[]{:S(2)}, u32[]{:S(2)}) collective-permute-start(f32[4,64,256]{2,1,0:T(8,128)S(1)} %collective-permute-done.6.refs_0_), channel_id=1, source_target_pairs={{0,2},{1,3},{2,0},{3,1},{4,6},{5,7},{6,4},{7,5},{8,10},{9,11},{10,... | collective-permute-start | bytes 786440 | tf_op jit(solution)/shard_map/ppermute | solution.py:437
  33.8 8.5 %collective-permute-start.10 = (f32[64,1024]{1,0:T(8,128)S(1)}, f32[64,1024]{1,0:T(8,128)S(1)}, u32[]{:S(2)}, u32[]{:S(2)}) collective-permute-start(f32[64,1024]{1,0:T(8,128)S(1)} %product_half.2.mine), channel_id=1, source_target_pairs={{0,1},{1,0},{2,3},{3,2},{4,5},{5,4},{6,7},{7,6},{8,9},{9,8},{10,11... | collective-permute-start | bytes 786440 | tf_op jit(solution)/shard_map/ppermute | solution.py:437
  37.8 1.3 %copy-start.5 = (f32[256]{0:T(256)S(1)}, f32[256]{0:T(256)}, u32[]{:S(2)}) copy-start(f32[256]{0:T(256)} %param.15) | copy-start | bytes 3076
  40.4 10.7 %collective-permute-start.9 = (f32[64,1024]{1,0:T(8,128)S(1)}, f32[64,1024]{1,0:T(8,128)S(1)}, u32[]{:S(2)}, u32[]{:S(2)}) collective-permute-start(f32[64,1024]{1,0:T(8,128)S(1)} %product_half.3.mine), channel_id=1, source_target_pairs={{0,1},{1,0},{2,3},{3,2},{4,5},{5,4},{6,7},{7,6},{8,9},{9,8},{10,11... | collective-permute-start | bytes 786440 | tf_op jit(solution)/shard_map/ppermute | solution.py:437
  42.5 11.5 %collective-permute-start.18 = (f32[64,256]{1,0:T(8,128)S(1)}, f32[64,256]{1,0:T(8,128)S(1)}, u32[]{:S(2)}, u32[]{:S(2)}) collective-permute-start(f32[64,256]{1,0:T(8,128)S(1)} %get-tuple-element.71), channel_id=1, source_target_pairs={{0,8},{1,9},{2,10},{3,11},{4,12},{5,13},{6,14},{7,15},{8,0},{9,1},... | collective-permute-start | bytes 196616 | tf_op jit(solution)/shard_map/ppermute | solution.py:437
  45.5 8.5 %collective-permute-start.19 = (f32[64,256]{1,0:T(8,128)S(1)}, f32[64,256]{1,0:T(8,128)S(1)}, u32[]{:S(2)}, u32[]{:S(2)}) collective-permute-start(f32[64,256]{1,0:T(8,128)S(1)} %get-tuple-element.72), channel_id=1, source_target_pairs={{0,16},{1,17},{2,18},{3,19},{4,20},{5,21},{6,22},{7,23},{8,24},{9,... | collective-permute-start | bytes 196616 | tf_op jit(solution)/shard_map/ppermute | solution.py:437
  47.3 6.7 %collective-permute-start.20 = (f32[64,256]{1,0:T(8,128)S(1)}, f32[64,256]{1,0:T(8,128)S(1)}, u32[]{:S(2)}, u32[]{:S(2)}) collective-permute-start(f32[64,256]{1,0:T(8,128)S(1)} %get-tuple-element.73), channel_id=1, source_target_pairs={{0,24},{1,25},{2,26},{3,27},{4,28},{5,29},{6,30},{7,31},{8,16},{9,... | collective-permute-start | bytes 196616 | tf_op jit(solution)/shard_map/ppermute | solution.py:437
  52.6 1.6 %collective-permute-start.12 = (f32[264,256]{1,0:T(8,128)S(1)}, f32[264,256]{1,0:T(8,128)S(1)}, u32[]{:S(2)}, u32[]{:S(2)}) collective-permute-start(f32[264,256]{1,0:T(8,128)S(1)} %backward_part.9), channel_id=1, source_target_pairs={{0,2},{1,3},{2,0},{3,1},{4,6},{5,7},{6,4},{7,5},{8,10},{9,11},{10,... | collective-permute-start | bytes 811016 | tf_op jit(solution)/shard_map/ppermute | solution.py:437
  53.4 5.7 %collective-permute-start.11 = (f32[256,256]{1,0:T(8,128)S(1)}, f32[256,256]{1,0:T(8,128)S(1)}, u32[]{:S(2)}, u32[]{:S(2)}) collective-permute-start(f32[256,256]{1,0:T(8,128)S(1)} %backward_part.8.token), channel_id=1, source_target_pairs={{0,2},{1,3},{2,0},{3,1},{4,6},{5,7},{6,4},{7,5},{8,10},{9,11},{10,... | collective-permute-start | bytes 786440 | tf_op jit(solution)/shard_map/ppermute | solution.py:437
  54.3 6.4 %collective-permute-start.14 = (f32[128,256]{1,0:T(8,128)S(1)}, f32[128,256]{1,0:T(8,128)S(1)}, u32[]{:S(2)}, u32[]{:S(2)}) collective-permute-start(f32[128,256]{1,0:T(8,128)S(1)} %get-tuple-element.64), channel_id=1, source_target_pairs={{0,4},{1,5},{2,6},{3,7},{4,0},{5,1},{6,2},{7,3},{8,12},{9,13},{10,... | collective-permute-start | bytes 393224 | tf_op jit(solution)/shard_map/ppermute | solution.py:437
  55.7 8.1 %copy-start.1 = (f32[4,64,256]{2,1,0:T(8,128)S(1)}, f32[4,64,256]{2,1,0:T(8,128)}, u32[]{:S(2)}) copy-start(f32[4,64,256]{2,1,0:T(8,128)} %copy-done) | copy-start | bytes 786436
  55.7 21.2 %copy-start.2 = (f32[256,256]{1,0:T(8,128)S(1)}, f32[256,256]{1,0:T(8,128)}, u32[]{:S(2)}) copy-start(f32[256,256]{1,0:T(8,128)} %right.1) | copy-start | bytes 786436
  55.7 21.2 %copy-start.3 = (f32[256,256]{1,0:T(8,128)S(1)}, f32[256,256]{1,0:T(8,128)}, u32[]{:S(2)}) copy-start(f32[256,256]{1,0:T(8,128)} %search.1) | copy-start | bytes 786436
  55.7 21.2 %copy-start.4 = (f32[256,256]{1,0:T(8,128)S(1)}, f32[256,256]{1,0:T(8,128)}, u32[]{:S(2)}) copy-start(f32[256,256]{1,0:T(8,128)} %solution.1) | copy-start | bytes 786436
  55.7 21.2 %copy-start.6 = (f32[256]{0:T(256)S(1)}, f32[256]{0:T(256)}, u32[]{:S(2)}) copy-start(f32[256]{0:T(256)} %param.16) | copy-start | bytes 3076
  55.7 21.2 %copy-start.7 = (f32[256]{0:T(256)S(1)}, f32[256]{0:T(256)}, u32[]{:S(2)}) copy-start(f32[256]{0:T(256)} %param.17) | copy-start | bytes 3076
  55.7 8.1 %collective-permute-start.13 = (f32[136,256]{1,0:T(8,128)S(1)}, f32[136,256]{1,0:T(8,128)S(1)}, u32[]{:S(2)}, u32[]{:S(2)}) collective-permute-start(f32[136,256]{1,0:T(8,128)S(1)} %get-tuple-element.62), channel_id=1, source_target_pairs={{0,4},{1,5},{2,6},{3,7},{4,0},{5,1},{6,2},{7,3},{8,12},{9,13},{10,... | collective-permute-start | bytes 417800 | tf_op jit(solution)/shard_map/ppermute | solution.py:437
  56.5 20.4 %collective-permute-start.21 = (f32[4,64,256]{2,1,0:T(8,128)S(1)}, f32[4,64,256]{2,1,0:T(8,128)S(1)}, u32[]{:S(2)}, u32[]{:S(2)}) collective-permute-start(f32[4,64,256]{2,1,0:T(8,128)S(1)} %stack_left.1.own), channel_id=1, source_target_pairs={{0,1},{1,0},{2,3},{3,2},{4,5},{5,4},{6,7},{7,6},{8,9},{9,8},{10,11... | collective-permute-start | bytes 786440 | tf_op jit(solution)/shard_map/ppermute | solution.py:437
  60.7 16.1 %collective-permute-start.16 = (f32[64,256]{1,0:T(8,128)S(1)}, f32[64,256]{1,0:T(8,128)S(1)}, u32[]{:S(2)}, u32[]{:S(2)}) collective-permute-start(f32[64,256]{1,0:T(8,128)S(1)} %get-tuple-element.65.g2), channel_id=1, source_target_pairs={{0,16},{1,17},{2,18},{3,19},{4,20},{5,21},{6,22},{7,23},{8,24},{9,... | collective-permute-start | bytes 196616 | tf_op jit(solution)/shard_map/ppermute | solution.py:437
  63.0 13.9 %collective-permute-start.17 = (f32[64,256]{1,0:T(8,128)S(1)}, f32[64,256]{1,0:T(8,128)S(1)}, u32[]{:S(2)}, u32[]{:S(2)}) collective-permute-start(f32[64,256]{1,0:T(8,128)S(1)} %get-tuple-element.66.g3), channel_id=1, source_target_pairs={{0,24},{1,25},{2,26},{3,27},{4,28},{5,29},{6,30},{7,31},{8,16},{9,... | collective-permute-start | bytes 196616 | tf_op jit(solution)/shard_map/ppermute | solution.py:437
  64.1 12.8 %collective-permute-start.15 = (f32[64,256]{1,0:T(8,128)S(1)}, f32[64,256]{1,0:T(8,128)S(1)}, u32[]{:S(2)}, u32[]{:S(2)}) collective-permute-start(f32[64,256]{1,0:T(8,128)S(1)} %get-tuple-element.68), channel_id=1, source_target_pairs={{0,8},{1,9},{2,10},{3,11},{4,12},{5,13},{6,14},{7,15},{8,0},{9,1},... | collective-permute-start | bytes 196616 | tf_op jit(solution)/shard_map/ppermute | solution.py:437

commit v21 on v16

--- a/solution.py
+++ b/solution.py
@@ -42,15 +42,13 @@
                    ids, vals, wide, right, left, turned, arrived):
     _, z, y = coords()
     q, rows = turned.shape[1:]
-    copies = [
-        pltpu.make_async_copy(src, dst, arrived.at[i])
-        for i, (src, dst) in enumerate((
-            (ids_hbm, ids),
-            (vals_hbm, vals),
-            (right_hbm, right),
-            (left_hbm.at[pl.ds(pl.multiple_of(y * rows, rows), rows), :], left),
-        ))
-    ]
+    moves = [(ids_hbm, ids), (vals_hbm, vals)]
+    piece = rows // 4
+    for src, first, dst in ((right_hbm, 0, right), (left_hbm, y * rows, left)):
+        for i in range(4):
+            at = pl.multiple_of(first + i * piece, piece)
+            moves.append((src.at[pl.ds(at, piece), :], dst.at[i * piece : (i + 1) * piece, :]))
+    copies = [pltpu.make_async_copy(src, dst, arrived.at[i]) for i, (src, dst) in enumerate(moves)]
     for copy in copies:
         copy.start()
     lines, count = stored.shape[0] // 2, ids.shape[0]
@@ -62,7 +60,8 @@
                 pl.ds(r, lines, stride=256 // count), :
             ]
     for part, ref in enumerate((right, left)):
-        copies[2 + part].wait()
+        for copy in copies[2 + 4 * part : 6 + 4 * part]:
+            copy.wait()
         turned[...] = ref[...].T.reshape(turned.shape)
         for k, out in enumerate((m0, m1, m2, m3)):
             out[part * q : (part + 1) * q, :] = turned[z ^ k]
@@ -83,7 +82,7 @@
             pltpu.VMEM(right.shape, jnp.float32),
             pltpu.VMEM(right.shape, jnp.float32),
             pltpu.VMEM((4, q, rows), jnp.float32),
-            pltpu.SemaphoreType.DMA((4,)),
+            pltpu.SemaphoreType.DMA((10,)),
         ],
         compiler_params=params(60),
         cost_estimate=cost(0, rows * cols * 16),
@@ -385,7 +384,8 @@
 
 
 def finish_kernel(docs_total, feat_total, g0, g1, g2, g3, squares, own, other, right, search, solution, phibar, rhobar,
-                  left_out, right_out, search_out, solution_out, alpha_out, phibar_out, rhobar_out, turned):
+                  left_hbm, right_hbm, search_hbm, solution_hbm, alpha_out, phibar_out, rhobar_out,
+                  turned, left_out, right_out, search_out, solution_out, sent):
     _, z, y = coords()
     q, half = turned.shape[1:]
     parts = [squares[i] for i in range(32)]
@@ -399,10 +399,12 @@
     )
     alpha = jnp.sqrt(alpha_sums / feat_total + epsilon)
     beta = jnp.sqrt(beta_sums / docs_total + epsilon)
-    for part, ref in ((y, own), (1 - y, other)):
-        for k in range(4):
-            turned[z ^ k] = ref[k]
-        left_out[pl.ds(pl.multiple_of(part * half, half), half), :] = turned[...].reshape(-1, half).T / beta
+    copies = []
+
+    def send(src, dst):
+        copies.append(pltpu.make_async_copy(src, dst, sent.at[len(copies)]))
+        copies[-1].start()
+
     rho = jnp.sqrt(rhobar[...] * rhobar[...] + beta * beta)
     cosine = rhobar[...] / rho
     sine = beta / rho
@@ -411,21 +413,39 @@
     rhobar_out[...] = -cosine * alpha
     phibar_out[...] = sine * phibar[...]
     alpha_out[...] = alpha
+    solution_out[...] = solution[...] + (phi / rho) * search[...]
+    send(solution_out, solution_hbm)
+    for i, (part, ref) in enumerate(((y, own), (1 - y, other))):
+        for k in range(4):
+            turned[z ^ k] = ref[k]
+        left_out[i] = turned[...].reshape(-1, half).T / beta
+        send(left_out.at[i], left_hbm.at[pl.ds(pl.multiple_of(part * half, half), half), :])
     for k, g in enumerate((g0, g1, g2, g3)):
         turned[z ^ k] = g[...]
     got = turned[...].reshape(-1, half).T
-    following = (got / beta - beta * right[...]) / alpha
-    right_out[...] = following
-    search_out[...] = following - (theta / rho) * search[...]
-    solution_out[...] = solution[...] + (phi / rho) * search[...]
+    right_out[...] = (got / beta - beta * right[...]) / alpha
+    send(right_out, right_hbm)
+    search_out[...] = right_out[...] - (theta / rho) * search[...]
+    send(search_out, search_hbm)
+    for copy in copies:
+        copy.wait()
 
 
 def finish(docs_total, feat_total, pieces, squares, own, other, right, search, solution, phibar, rhobar):
     rows, cols = right.shape
     return pl.pallas_call(
         functools.partial(finish_kernel, docs_total, feat_total),
+        in_specs=[whole()] * 12,
+        out_specs=[pl.BlockSpec(memory_space=pltpu.HBM)] * 4 + [whole()] * 3,
         out_shape=[f32(2 * rows, cols)] + [f32(rows, cols)] * 3 + [f32(1, cols)] * 3,
-        scratch_shapes=[pltpu.VMEM((4, cols // 4, rows), jnp.float32)],
+        scratch_shapes=[
+            pltpu.VMEM((4, cols // 4, rows), jnp.float32),
+            pltpu.VMEM((2, rows, cols), jnp.float32),
+            pltpu.VMEM((rows, cols), jnp.float32),
+            pltpu.VMEM((rows, cols), jnp.float32),
+            pltpu.VMEM((rows, cols), jnp.float32),
+            pltpu.SemaphoreType.DMA((5,)),
+        ],
         compiler_params=params(12),
         cost_estimate=cost(rows * cols * 16, rows * cols * 20),
         name="finish",

time: 78.6 us -> 79.3 us (level)
  transfers between devices with their start and end apart: 22 -> 22, of which waited for: 7 -> 7; matrix products, arithmetic and copies ran while one was open for 0% -> 0% of each run, Pallas kernels for 31% -> 30%
where the time goes in v21:
time: 79.3 us; the launch traced here: 79.1 us
  starting transfers between devices  29.1 us (37%)
  Pallas kernels  28.8 us (36%)
  blocking collectives  12.3 us (16%)
  waiting for transfers between devices  7.75 us (10%)
  between operations  1.09 us (1%)
    ppermute x22, starting transfers between devices, swap(): return lax.ppermute(value, AXES, [(i, i ^ mask) for i in range(32)])  29.1 us
    all_to_all x1, blocking collectives, by_columns(): squares = lax.all_to_all(after(sums, left_own), AXES, 0, 0, tiled=True)  12.3 us
    pallas_call x2, Pallas kernels, build(): pl.pallas_call(functools.partial(build_kernel, rel), in_specs=[whole()] *...  9.63 us
    ppermute x22, waiting for transfers between devices, swap(): return lax.ppermute(value, AXES, [(i, i ^ mask) for i in range(32)])  7.75 us
    pallas_call x4, Pallas kernels, forward_part(): pl.pallas_call(functools.partial(forward_kernel, blocks, before is not No...  7.12 us
    pallas_call x5, Pallas kernels, backward_part(): pl.pallas_call(functools.partial(backward_kernel, first, blocks, tuple(ex...  5.19 us
    pallas_call x2, Pallas kernels, product_half(): pl.pallas_call(functools.partial(product_kernel, blocks), in_specs=[whole...  2.64 us
    pallas_call x1, Pallas kernels, finish(): pl.pallas_call(functools.partial(finish_kernel, docs_total, feat_total),...  1.85 us
  transfers between devices with their start and end apart: 22, of which 7 were waited for; matrix products, arithmetic and copies ran while one was open for 0% of the time, Pallas kernels for 30%

profile of v21, /device:TPU:0, one launch (start us, length us, event | category | flops | bytes accessed | tf_op | source)
XLA Modules:
  0.0 79.1 jit_solution(18298623293769815451)
XLA Ops:
  0.6 1.7 %prepare.1 = (f32[64,256]{1,0:T(8,128)S(1)}, f32[128,256]{1,0:T(8,128)S(1)}, f32[128,256]{1,0:T(8,128)S(1)}, f32[128,256]{1,0:T(8,128)S(1)}, f32[128,256]{1,0:T(8,128)S(1)}) custom-call(s32[16,512]{1,0:T(8,128)} %bitcast.13, bf16[16,512]{1,0:T(8,128)(2,1)} %bitcast.14, f32[256,256]{1,0:T(8,128)} %right.1, f32[512,256]{1,0:T(8,128)} %left_hbm.1), custom_call_target="tpu_custom_call" | custom-call | bytes 16384 | tf_op jit(solution)/shard_map/prepare/pallas_call | solution.py:73
  2.3 4.1 %collective-permute-start.1 = (f32[64,256]{1,0:T(8,128)S(1)}, f32[64,256]{1,0:T(8,128)S(1)}, u32[]{:S(2)}, u32[]{:S(2)}) collective-permute-start(f32[64,256]{1,0:T(8,128)S(1)} %get-tuple-element.45.e0), channel_id=1, source_target_pairs={{0,16},{1,17},{2,18},{3,19},{4,20},{5,21},{6,22},{7,23},{8,24},{9,... | collective-permute-start | bytes 196616 | tf_op jit(solution)/shard_map/ppermute | solution.py:456
  6.4 1.4 %collective-permute-start.2 = (f32[64,256]{1,0:T(8,128)S(1)}, f32[64,256]{1,0:T(8,128)S(1)}, u32[]{:S(2)}, u32[]{:S(2)}) collective-permute-start(f32[64,256]{1,0:T(8,128)S(1)} %get-tuple-element.45.e0), channel_id=1, source_target_pairs={{0,24},{1,25},{2,26},{3,27},{4,28},{5,29},{6,30},{7,31},{8,16},{9,... | collective-permute-start | bytes 196616 | tf_op jit(solution)/shard_map/ppermute | solution.py:456
  7.8 0.2 collective-permute-start
  8.0 2.8 %collective-permute-start.4 = (f32[128,256]{1,0:T(8,128)S(1)}, f32[128,256]{1,0:T(8,128)S(1)}, u32[]{:S(2)}, u32[]{:S(2)}) collective-permute-start(f32[128,256]{1,0:T(8,128)S(1)} %get-tuple-element.51), channel_id=1, source_target_pairs={{0,16},{1,17},{2,18},{3,19},{4,20},{5,21},{6,22},{7,23},{8,24},{9,... | collective-permute-start | bytes 393224 | tf_op jit(solution)/shard_map/ppermute | solution.py:456
  10.8 1.4 %collective-permute-start.5 = (f32[128,256]{1,0:T(8,128)S(1)}, f32[128,256]{1,0:T(8,128)S(1)}, u32[]{:S(2)}, u32[]{:S(2)}) collective-permute-start(f32[128,256]{1,0:T(8,128)S(1)} %get-tuple-element.52), channel_id=1, source_target_pairs={{0,24},{1,25},{2,26},{3,27},{4,28},{5,29},{6,30},{7,31},{8,16},{9,... | collective-permute-start | bytes 393224 | tf_op jit(solution)/shard_map/ppermute | solution.py:456
  12.2 0.6 collective-permute-start.3
  12.8 0.5 collective-permute-done.2.e3
  13.4 4.7 %dense_rows.2 = (bf16[16,1024,256]{2,1,0:T(8,128)(2,1)S(1)}, bf16[16,1024,256]{2,1,0:T(8,128)(2,1)S(1)}, f32[8,128]{1,0:T(8,128)S(1)}) custom-call(f32[64,256]{1,0:T(8,128)S(1)} %get-tuple-element.45.e0, f32[64,256]{1,0:T(8,128)S(1)} %collective-permute-done.e1, f32[64,256]{1,0:T(8,128)S(1)} %collective-permute-done.1.e2, ...), custom_call_target="tpu_custom_call" | custom-call | flops 2147483648 | bytes 16777216 | tf_op jit(solution)/shard_map/dense_rows/pallas_call | solution.py:153
  18.1 3.6 %collective-permute-done.4.m2.refs_2_ = f32[128,256]{1,0:T(8,128)S(1)} collective-permute-done((f32[128,256]{1,0:T(8,128)S(1)}, f32[128,256]{1,0:T(8,128)S(1)}, u32[]{:S(2)}, u32[]{:S(2)}) %collective-permute-start.4) | collective-permute-done | bytes 131104 | tf_op jit(solution)/shard_map/ppermute | solution.py:456
  21.7 0.1 collective-permute-done.3.m1.refs_1_
  21.9 0.1 collective-permute-start.7
  21.9 1.8 %collective-permute-start.6 = (f32[4,64,256]{2,1,0:T(8,128)S(1)}, f32[4,64,256]{2,1,0:T(8,128)S(1)}, u32[]{:S(2)}, u32[]{:S(2)}) collective-permute-start(f32[4,64,256]{2,1,0:T(8,128)S(1)} %stack_right.1.refs_0_.right), channel_id=1, source_target_pairs={{0,4},{1,5},{2,6},{3,7},{4,0},{5,1},{6,2},{7,3},{8,12},{9,13},{10,... | collective-permute-start | bytes 786440 | tf_op jit(solution)/shard_map/ppermute | solution.py:456
  23.7 4.9 %dense_rows.3 = (bf16[16,1024,256]{2,1,0:T(8,128)(2,1)S(1)}, bf16[16,1024,256]{2,1,0:T(8,128)(2,1)S(1)}, f32[8,128]{1,0:T(8,128)S(1)}) custom-call(f32[64,256]{1,0:T(8,128)S(1)} %get-tuple-element.45.e0, f32[64,256]{1,0:T(8,128)S(1)} %collective-permute-done.e1, f32[64,256]{1,0:T(8,128)S(1)} %collective-permute-done.1.e2, ...), custom_call_target="tpu_custom_call" | custom-call | flops 33554432 | bytes 262144 | tf_op jit(solution)/shard_map/dense_rows/pallas_call | solution.py:153
  28.6 2.3 %forward_part.4.refs_1_ = f32[1024,128]{1,0:T(8,128)S(1)} custom-call(bf16[16,1024,256]{2,1,0:T(8,128)(2,1)S(1)} %get-tuple-element.46.hi_ref, bf16[16,1024,256]{2,1,0:T(8,128)(2,1)S(1)} %get-tuple-element.47.lo_ref, f32[4,64,256]{2,1,0:T(8,128)S(1)} %stack_right.1.refs_0_.right, f32[4,64,256]{2,1,0:T(8,128)S(1)} %collective-permute-done.7.refs_1_, ...), custom_call_target="tpu_custom_call" | custom-call | flops 67108864 | bytes 131072 | tf_op jit(solution)/shard_map/forward_part/pallas_call | solution.py:195
  31.0 0.2 collective-permute-start.8
  31.2 1.2 %forward_part.5.before = f32[1024,128]{1,0:T(8,128)S(1)} custom-call(bf16[16,1024,256]{2,1,0:T(8,128)(2,1)S(1)} %get-tuple-element.46.hi_ref, bf16[16,1024,256]{2,1,0:T(8,128)(2,1)S(1)} %get-tuple-element.47.lo_ref, f32[4,64,256]{2,1,0:T(8,128)S(1)} %collective-permute-done.6.refs_0_, f32[1024,128]{1,0:T(8,128)S(1)} %forward_part.4.refs_1_), custom_call_target="tpu_custom_call" | custom-call | flops 33554432 | bytes 65536 | tf_op jit(solution)/shard_map/forward_part/pallas_call | solution.py:195
  32.4 0.1 collective-permute-done.8.vec
  32.6 1.3 %product_half.2.mine = f32[64,1024]{1,0:T(8,128)S(1)} custom-call(bf16[16,1024,256]{2,1,0:T(8,128)(2,1)S(1)} %get-tuple-element.46.hi_ref, bf16[16,1024,256]{2,1,0:T(8,128)(2,1)S(1)} %get-tuple-element.47.lo_ref, f32[4,64,256]{2,1,0:T(8,128)S(1)} %collective-permute-done.8.vec, f32[1024,128]{1,0:T(8,128)S(1)} %forward_part.5.before), custom_call_target="tpu_custom_call" | custom-call | flops 33554432 | bytes 65536 | tf_op jit(solution)/shard_map/product_half/pallas_call | solution.py:227
  33.9 1.6 %collective-permute-start.10 = (f32[64,1024]{1,0:T(8,128)S(1)}, f32[64,1024]{1,0:T(8,128)S(1)}, u32[]{:S(2)}, u32[]{:S(2)}) collective-permute-start(f32[64,1024]{1,0:T(8,128)S(1)} %product_half.2.mine), channel_id=1, source_target_pairs={{0,1},{1,0},{2,3},{3,2},{4,5},{5,4},{6,7},{7,6},{8,9},{9,8},{10,11... | collective-permute-start | bytes 786440 | tf_op jit(solution)/shard_map/ppermute | solution.py:456
  35.5 2.3 %forward_part.6.refs_1_ = f32[1024,128]{1,0:T(8,128)S(1)} custom-call(bf16[16,1024,256]{2,1,0:T(8,128)(2,1)S(1)} %get-tuple-element.56.hi_ref, bf16[16,1024,256]{2,1,0:T(8,128)(2,1)S(1)} %get-tuple-element.57.lo_ref, f32[4,64,256]{2,1,0:T(8,128)S(1)} %stack_right.1.refs_0_.right, f32[4,64,256]{2,1,0:T(8,128)S(1)} %collective-permute-done.7.refs_1_), custom_call_target="tpu_custom_call" | custom-call | flops 67108864 | bytes 131072 | tf_op jit(solution)/shard_map/forward_part/pallas_call | solution.py:195
  37.8 1.2 %forward_part.7.before = f32[1024,128]{1,0:T(8,128)S(1)} custom-call(bf16[16,1024,256]{2,1,0:T(8,128)(2,1)S(1)} %get-tuple-element.56.hi_ref, bf16[16,1024,256]{2,1,0:T(8,128)(2,1)S(1)} %get-tuple-element.57.lo_ref, f32[4,64,256]{2,1,0:T(8,128)S(1)} %collective-permute-done.6.refs_0_, f32[1024,128]{1,0:T(8,128)S(1)} %forward_part.6.refs_1_), custom_call_target="tpu_custom_call" | custom-call | flops 33554432 | bytes 65536 | tf_op jit(solution)/shard_map/forward_part/pallas_call | solution.py:195
  39.0 1.3 %product_half.3.mine = f32[64,1024]{1,0:T(8,128)S(1)} custom-call(bf16[16,1024,256]{2,1,0:T(8,128)(2,1)S(1)} %get-tuple-element.56.hi_ref, bf16[16,1024,256]{2,1,0:T(8,128)(2,1)S(1)} %get-tuple-element.57.lo_ref, f32[4,64,256]{2,1,0:T(8,128)S(1)} %collective-permute-done.8.vec, f32[1024,128]{1,0:T(8,128)S(1)} %forward_part.7.before, ...), custom_call_target="tpu_custom_call" | custom-call | flops 33554432 | bytes 65536 | tf_op jit(solution)/shard_map/product_half/pallas_call | solution.py:227
  40.4 0.6 collective-permute-start.9
  41.0 1.4 %collective-permute-done.10.other = f32[64,1024]{1,0:T(8,128)S(1)} collective-permute-done((f32[64,1024]{1,0:T(8,128)S(1)}, f32[64,1024]{1,0:T(8,128)S(1)}, u32[]{:S(2)}, u32[]{:S(2)}) %collective-permute-start.10) | collective-permute-done | bytes 262176 | tf_op jit(solution)/shard_map/ppermute | solution.py:456
  42.4 0.2 left_half.2
  42.6 3.0 %collective-permute-start.18 = (f32[64,256]{1,0:T(8,128)S(1)}, f32[64,256]{1,0:T(8,128)S(1)}, u32[]{:S(2)}, u32[]{:S(2)}) collective-permute-start(f32[64,256]{1,0:T(8,128)S(1)} %get-tuple-element.71), channel_id=1, source_target_pairs={{0,8},{1,9},{2,10},{3,11},{4,12},{5,13},{6,14},{7,15},{8,0},{9,1},... | collective-permute-start | bytes 196616 | tf_op jit(solution)/shard_map/ppermute | solution.py:456
  45.6 1.8 %collective-permute-start.19 = (f32[64,256]{1,0:T(8,128)S(1)}, f32[64,256]{1,0:T(8,128)S(1)}, u32[]{:S(2)}, u32[]{:S(2)}) collective-permute-start(f32[64,256]{1,0:T(8,128)S(1)} %get-tuple-element.72), channel_id=1, source_target_pairs={{0,16},{1,17},{2,18},{3,19},{4,20},{5,21},{6,22},{7,23},{8,24},{9,... | collective-permute-start | bytes 196616 | tf_op jit(solution)/shard_map/ppermute | solution.py:456
  47.3 1.4 %collective-permute-start.20 = (f32[64,256]{1,0:T(8,128)S(1)}, f32[64,256]{1,0:T(8,128)S(1)}, u32[]{:S(2)}, u32[]{:S(2)}) collective-permute-start(f32[64,256]{1,0:T(8,128)S(1)} %get-tuple-element.73), channel_id=1, source_target_pairs={{0,24},{1,25},{2,26},{3,27},{4,28},{5,29},{6,30},{7,31},{8,16},{9,... | collective-permute-start | bytes 196616 | tf_op jit(solution)/shard_map/ppermute | solution.py:456
  48.7 2.3 %backward_part.5.refs_1_.refs_0_ = f32[1024,256]{1,0:T(8,128)S(1)} custom-call(bf16[16,1024,256]{2,1,0:T(8,128)(2,1)S(1)} %get-tuple-element.56.hi_ref, bf16[16,1024,256]{2,1,0:T(8,128)(2,1)S(1)} %get-tuple-element.57.lo_ref, bf16[128,1024]{1,0:T(8,128)(2,1)S(1)} %get-tuple-element.59.both_ref), custom_call_target="tpu_custom_call" | custom-call | flops 134217728 | bytes 262144 | tf_op jit(solution)/shard_map/backward_part/pallas_call | solution.py:308
  51.1 0.2 left_half.3
  51.2 0.7 backward_part.7.refs_1_.near
  52.0 0.7 backward_part.9
  52.7 0.1 collective-permute-start.12
  52.8 0.7 backward_part.8.token
  53.5 0.6 collective-permute-start.11
  54.1 0.2 collective-permute-done.12.far
  54.3 1.4 %collective-permute-start.14 = (f32[128,256]{1,0:T(8,128)S(1)}, f32[128,256]{1,0:T(8,128)S(1)}, u32[]{:S(2)}, u32[]{:S(2)}) collective-permute-start(f32[128,256]{1,0:T(8,128)S(1)} %get-tuple-element.64), channel_id=1, source_target_pairs={{0,4},{1,5},{2,6},{3,7},{4,0},{5,1},{6,2},{7,3},{8,12},{9,13},{10,... | collective-permute-start | bytes 393224 | tf_op jit(solution)/shard_map/ppermute | solution.py:456
  55.8 0.8 collective-permute-start.13
  56.5 1.8 %collective-permute-start.21 = (f32[4,64,256]{2,1,0:T(8,128)S(1)}, f32[4,64,256]{2,1,0:T(8,128)S(1)}, u32[]{:S(2)}, u32[]{:S(2)}) collective-permute-start(f32[4,64,256]{2,1,0:T(8,128)S(1)} %stack_left.1.own), channel_id=1, source_target_pairs={{0,1},{1,0},{2,3},{3,2},{4,5},{5,4},{6,7},{7,6},{8,9},{9,8},{10,11... | collective-permute-start | bytes 786440 | tf_op jit(solution)/shard_map/ppermute | solution.py:456
  58.4 0.7 backward_part.6.keep
  59.1 1.7 %collective-permute-done.14.got = f32[128,256]{1,0:T(8,128)S(1)} collective-permute-done((f32[128,256]{1,0:T(8,128)S(1)}, f32[128,256]{1,0:T(8,128)S(1)}, u32[]{:S(2)}, u32[]{:S(2)}) %collective-permute-start.14) | collective-permute-done | bytes 131104 | tf_op jit(solution)/shard_map/ppermute | solution.py:456
  60.8 2.2 %collective-permute-start.16 = (f32[64,256]{1,0:T(8,128)S(1)}, f32[64,256]{1,0:T(8,128)S(1)}, u32[]{:S(2)}, u32[]{:S(2)}) collective-permute-start(f32[64,256]{1,0:T(8,128)S(1)} %get-tuple-element.65.g2), channel_id=1, source_target_pairs={{0,16},{1,17},{2,18},{3,19},{4,20},{5,21},{6,22},{7,23},{8,24},{9,... | collective-permute-start | bytes 196616 | tf_op jit(solution)/shard_map/ppermute | solution.py:456
  63.0 0.8 %collective-permute-start.17 = (f32[64,256]{1,0:T(8,128)S(1)}, f32[64,256]{1,0:T(8,128)S(1)}, u32[]{:S(2)}, u32[]{:S(2)}) collective-permute-start(f32[64,256]{1,0:T(8,128)S(1)} %get-tuple-element.66.g3), channel_id=1, source_target_pairs={{0,24},{1,25},{2,26},{3,27},{4,28},{5,29},{6,30},{7,31},{8,16},{9,... | collective-permute-start | bytes 196616 | tf_op jit(solution)/shard_map/ppermute | solution.py:456
  63.8 0.3 right_norm.1
  64.2 0.5 collective-permute-start.15
  64.7 12.3 %all_to_all.5.squares = f32[32,1,128]{2,1,0:T(1,128)S(1)} all-to-all(f32[32,1,128]{2,1,0:T(1,128)S(1)} %bitcast.9), channel_id=1, replica_groups=mesh['doc'=16,'feat'=2] {'doc','feat'}, dimensions={0} | all-to-all | bytes 32768 | tf_op jit(solution)/shard_map/all_to_all | solution.py:513
  77.1 1.9 %finish.1 = (f32[512,256]{1,0:T(8,128)}, f32[256,256]{1,0:T(8,128)}, f32[256,256]{1,0:T(8,128)}, f32[256,256]{1,0:T(8,128)}, f32[1,256]{1,0:T(1,128)}, /*index=5*/f32[1,256]{1,0:T(1,128)}, f32[1,256]{1,0:T(1,128)}) custom-call(f32[64,256]{1,0:T(8,128)S(1)} %get-tuple-element.67.g0, f32[64,256]{1,0:T(8,128)S(1)} %collective-permute-done.15.g1, ...), custom_call_target="tpu_custom_call" | custom-call | flops 16384 | bytes 20480 | tf_op jit(solution)/shard_map/finish/pallas_call | solution.py:436
  (35 shorter events, 0.2 us)
Async XLA Ops:
  2.3 9.9 %collective-permute-start.1 = (f32[64,256]{1,0:T(8,128)S(1)}, f32[64,256]{1,0:T(8,128)S(1)}, u32[]{:S(2)}, u32[]{:S(2)}) collective-permute-start(f32[64,256]{1,0:T(8,128)S(1)} %get-tuple-element.45.e0), channel_id=1, source_target_pairs={{0,16},{1,17},{2,18},{3,19},{4,20},{5,21},{6,22},{7,23},{8,24},{9,... | collective-permute-start | bytes 196616 | tf_op jit(solution)/shard_map/ppermute | solution.py:456
  6.4 6.9 %collective-permute-start.2 = (f32[64,256]{1,0:T(8,128)S(1)}, f32[64,256]{1,0:T(8,128)S(1)}, u32[]{:S(2)}, u32[]{:S(2)}) collective-permute-start(f32[64,256]{1,0:T(8,128)S(1)} %get-tuple-element.45.e0), channel_id=1, source_target_pairs={{0,24},{1,25},{2,26},{3,27},{4,28},{5,29},{6,30},{7,31},{8,16},{9,... | collective-permute-start | bytes 196616 | tf_op jit(solution)/shard_map/ppermute | solution.py:456
  7.8 5.6 %collective-permute-start = (f32[64,256]{1,0:T(8,128)S(1)}, f32[64,256]{1,0:T(8,128)S(1)}, u32[]{:S(2)}, u32[]{:S(2)}) collective-permute-start(f32[64,256]{1,0:T(8,128)S(1)} %get-tuple-element.45.e0), channel_id=1, source_target_pairs={{0,8},{1,9},{2,10},{3,11},{4,12},{5,13},{6,14},{7,15},{8,0},{9,1},... | collective-permute-start | bytes 196616 | tf_op jit(solution)/shard_map/ppermute | solution.py:456
  8.0 13.7 %collective-permute-start.4 = (f32[128,256]{1,0:T(8,128)S(1)}, f32[128,256]{1,0:T(8,128)S(1)}, u32[]{:S(2)}, u32[]{:S(2)}) collective-permute-start(f32[128,256]{1,0:T(8,128)S(1)} %get-tuple-element.51), channel_id=1, source_target_pairs={{0,16},{1,17},{2,18},{3,19},{4,20},{5,21},{6,22},{7,23},{8,24},{9,... | collective-permute-start | bytes 393224 | tf_op jit(solution)/shard_map/ppermute | solution.py:456
  10.8 10.9 %collective-permute-start.5 = (f32[128,256]{1,0:T(8,128)S(1)}, f32[128,256]{1,0:T(8,128)S(1)}, u32[]{:S(2)}, u32[]{:S(2)}) collective-permute-start(f32[128,256]{1,0:T(8,128)S(1)} %get-tuple-element.52), channel_id=1, source_target_pairs={{0,24},{1,25},{2,26},{3,27},{4,28},{5,29},{6,30},{7,31},{8,16},{9,... | collective-permute-start | bytes 393224 | tf_op jit(solution)/shard_map/ppermute | solution.py:456
  12.2 9.6 %collective-permute-start.3 = (f32[128,256]{1,0:T(8,128)S(1)}, f32[128,256]{1,0:T(8,128)S(1)}, u32[]{:S(2)}, u32[]{:S(2)}) collective-permute-start(f32[128,256]{1,0:T(8,128)S(1)} %get-tuple-element.50), channel_id=1, source_target_pairs={{0,8},{1,9},{2,10},{3,11},{4,12},{5,13},{6,14},{7,15},{8,0},{9,1},... | collective-permute-start | bytes 393224 | tf_op jit(solution)/shard_map/ppermute | solution.py:456
  21.8 13.6 %copy-start = (f32[4,64,256]{2,1,0:T(8,128)}, f32[4,64,256]{2,1,0:T(8,128)S(1)}, u32[]{:S(2)}) copy-start(f32[4,64,256]{2,1,0:T(8,128)S(1)} %stack_right.1.refs_0_.right) | copy-start | bytes 786436
  21.9 6.8 %collective-permute-start.7 = (f32[4,64,256]{2,1,0:T(8,128)S(1)}, f32[4,64,256]{2,1,0:T(8,128)S(1)}, u32[]{:S(2)}, u32[]{:S(2)}) collective-permute-start(f32[4,64,256]{2,1,0:T(8,128)S(1)} %stack_right.1.refs_0_.right), channel_id=1, source_target_pairs={{0,2},{1,3},{2,0},{3,1},{4,6},{5,7},{6,4},{7,5},{8,10},{9,11},{10,... | collective-permute-start | bytes 786440 | tf_op jit(solution)/shard_map/ppermute | solution.py:456
  21.9 9.0 %collective-permute-start.6 = (f32[4,64,256]{2,1,0:T(8,128)S(1)}, f32[4,64,256]{2,1,0:T(8,128)S(1)}, u32[]{:S(2)}, u32[]{:S(2)}) collective-permute-start(f32[4,64,256]{2,1,0:T(8,128)S(1)} %stack_right.1.refs_0_.right), channel_id=1, source_target_pairs={{0,4},{1,5},{2,6},{3,7},{4,0},{5,1},{6,2},{7,3},{8,12},{9,13},{10,... | collective-permute-start | bytes 786440 | tf_op jit(solution)/shard_map/ppermute | solution.py:456
  31.0 1.6 %collective-permute-start.8 = (f32[4,64,256]{2,1,0:T(8,128)S(1)}, f32[4,64,256]{2,1,0:T(8,128)S(1)}, u32[]{:S(2)}, u32[]{:S(2)}) collective-permute-start(f32[4,64,256]{2,1,0:T(8,128)S(1)} %collective-permute-done.6.refs_0_), channel_id=1, source_target_pairs={{0,2},{1,3},{2,0},{3,1},{4,6},{5,7},{6,4},{7,5},{8,10},{9,11},{10,... | collective-permute-start | bytes 786440 | tf_op jit(solution)/shard_map/ppermute | solution.py:456
  33.9 8.5 %collective-permute-start.10 = (f32[64,1024]{1,0:T(8,128)S(1)}, f32[64,1024]{1,0:T(8,128)S(1)}, u32[]{:S(2)}, u32[]{:S(2)}) collective-permute-start(f32[64,1024]{1,0:T(8,128)S(1)} %product_half.2.mine), channel_id=1, source_target_pairs={{0,1},{1,0},{2,3},{3,2},{4,5},{5,4},{6,7},{7,6},{8,9},{9,8},{10,11... | collective-permute-start | bytes 786440 | tf_op jit(solution)/shard_map/ppermute | solution.py:456
  37.8 1.3 %copy-start.5 = (f32[256]{0:T(256)S(1)}, f32[256]{0:T(256)}, u32[]{:S(2)}) copy-start(f32[256]{0:T(256)} %param.15) | copy-start | bytes 3076
  40.4 10.7 %collective-permute-start.9 = (f32[64,1024]{1,0:T(8,128)S(1)}, f32[64,1024]{1,0:T(8,128)S(1)}, u32[]{:S(2)}, u32[]{:S(2)}) collective-permute-start(f32[64,1024]{1,0:T(8,128)S(1)} %product_half.3.mine), channel_id=1, source_target_pairs={{0,1},{1,0},{2,3},{3,2},{4,5},{5,4},{6,7},{7,6},{8,9},{9,8},{10,11... | collective-permute-start | bytes 786440 | tf_op jit(solution)/shard_map/ppermute | solution.py:456
  42.6 11.5 %collective-permute-start.18 = (f32[64,256]{1,0:T(8,128)S(1)}, f32[64,256]{1,0:T(8,128)S(1)}, u32[]{:S(2)}, u32[]{:S(2)}) collective-permute-start(f32[64,256]{1,0:T(8,128)S(1)} %get-tuple-element.71), channel_id=1, source_target_pairs={{0,8},{1,9},{2,10},{3,11},{4,12},{5,13},{6,14},{7,15},{8,0},{9,1},... | collective-permute-start | bytes 196616 | tf_op jit(solution)/shard_map/ppermute | solution.py:456
  45.6 8.5 %collective-permute-start.19 = (f32[64,256]{1,0:T(8,128)S(1)}, f32[64,256]{1,0:T(8,128)S(1)}, u32[]{:S(2)}, u32[]{:S(2)}) collective-permute-start(f32[64,256]{1,0:T(8,128)S(1)} %get-tuple-element.72), channel_id=1, source_target_pairs={{0,16},{1,17},{2,18},{3,19},{4,20},{5,21},{6,22},{7,23},{8,24},{9,... | collective-permute-start | bytes 196616 | tf_op jit(solution)/shard_map/ppermute | solution.py:456
  47.3 6.7 %collective-permute-start.20 = (f32[64,256]{1,0:T(8,128)S(1)}, f32[64,256]{1,0:T(8,128)S(1)}, u32[]{:S(2)}, u32[]{:S(2)}) collective-permute-start(f32[64,256]{1,0:T(8,128)S(1)} %get-tuple-element.73), channel_id=1, source_target_pairs={{0,24},{1,25},{2,26},{3,27},{4,28},{5,29},{6,30},{7,31},{8,16},{9,... | collective-permute-start | bytes 196616 | tf_op jit(solution)/shard_map/ppermute | solution.py:456
  52.7 1.6 %collective-permute-start.12 = (f32[264,256]{1,0:T(8,128)S(1)}, f32[264,256]{1,0:T(8,128)S(1)}, u32[]{:S(2)}, u32[]{:S(2)}) collective-permute-start(f32[264,256]{1,0:T(8,128)S(1)} %backward_part.9), channel_id=1, source_target_pairs={{0,2},{1,3},{2,0},{3,1},{4,6},{5,7},{6,4},{7,5},{8,10},{9,11},{10,... | collective-permute-start | bytes 811016 | tf_op jit(solution)/shard_map/ppermute | solution.py:456
  53.5 5.6 %collective-permute-start.11 = (f32[256,256]{1,0:T(8,128)S(1)}, f32[256,256]{1,0:T(8,128)S(1)}, u32[]{:S(2)}, u32[]{:S(2)}) collective-permute-start(f32[256,256]{1,0:T(8,128)S(1)} %backward_part.8.token), channel_id=1, source_target_pairs={{0,2},{1,3},{2,0},{3,1},{4,6},{5,7},{6,4},{7,5},{8,10},{9,11},{10,... | collective-permute-start | bytes 786440 | tf_op jit(solution)/shard_map/ppermute | solution.py:456
  54.3 6.4 %collective-permute-start.14 = (f32[128,256]{1,0:T(8,128)S(1)}, f32[128,256]{1,0:T(8,128)S(1)}, u32[]{:S(2)}, u32[]{:S(2)}) collective-permute-start(f32[128,256]{1,0:T(8,128)S(1)} %get-tuple-element.64), channel_id=1, source_target_pairs={{0,4},{1,5},{2,6},{3,7},{4,0},{5,1},{6,2},{7,3},{8,12},{9,13},{10,... | collective-permute-start | bytes 393224 | tf_op jit(solution)/shard_map/ppermute | solution.py:456
  55.7 8.1 %copy-start.1 = (f32[4,64,256]{2,1,0:T(8,128)S(1)}, f32[4,64,256]{2,1,0:T(8,128)}, u32[]{:S(2)}) copy-start(f32[4,64,256]{2,1,0:T(8,128)} %copy-done) | copy-start | bytes 786436
  55.7 21.3 %copy-start.2 = (f32[256,256]{1,0:T(8,128)S(1)}, f32[256,256]{1,0:T(8,128)}, u32[]{:S(2)}) copy-start(f32[256,256]{1,0:T(8,128)} %right.1) | copy-start | bytes 786436
  55.7 21.3 %copy-start.3 = (f32[256,256]{1,0:T(8,128)S(1)}, f32[256,256]{1,0:T(8,128)}, u32[]{:S(2)}) copy-start(f32[256,256]{1,0:T(8,128)} %search.1) | copy-start | bytes 786436
  55.7 21.4 %copy-start.4 = (f32[256,256]{1,0:T(8,128)S(1)}, f32[256,256]{1,0:T(8,128)}, u32[]{:S(2)}) copy-start(f32[256,256]{1,0:T(8,128)} %solution.1) | copy-start | bytes 786436
  55.7 21.4 %copy-start.6 = (f32[256]{0:T(256)S(1)}, f32[256]{0:T(256)}, u32[]{:S(2)}) copy-start(f32[256]{0:T(256)} %param.16) | copy-start | bytes 3076
  55.7 21.4 %copy-start.7 = (f32[256]{0:T(256)S(1)}, f32[256]{0:T(256)}, u32[]{:S(2)}) copy-start(f32[256]{0:T(256)} %param.17) | copy-start | bytes 3076
  55.8 8.1 %collective-permute-start.13 = (f32[136,256]{1,0:T(8,128)S(1)}, f32[136,256]{1,0:T(8,128)S(1)}, u32[]{:S(2)}, u32[]{:S(2)}) collective-permute-start(f32[136,256]{1,0:T(8,128)S(1)} %get-tuple-element.62), channel_id=1, source_target_pairs={{0,4},{1,5},{2,6},{3,7},{4,0},{5,1},{6,2},{7,3},{8,12},{9,13},{10,... | collective-permute-start | bytes 417800 | tf_op jit(solution)/shard_map/ppermute | solution.py:456
  56.5 20.5 %collective-permute-start.21 = (f32[4,64,256]{2,1,0:T(8,128)S(1)}, f32[4,64,256]{2,1,0:T(8,128)S(1)}, u32[]{:S(2)}, u32[]{:S(2)}) collective-permute-start(f32[4,64,256]{2,1,0:T(8,128)S(1)} %stack_left.1.own), channel_id=1, source_target_pairs={{0,1},{1,0},{2,3},{3,2},{4,5},{5,4},{6,7},{7,6},{8,9},{9,8},{10,11... | collective-permute-start | bytes 786440 | tf_op jit(solution)/shard_map/ppermute | solution.py:456
  60.8 16.3 %collective-permute-start.16 = (f32[64,256]{1,0:T(8,128)S(1)}, f32[64,256]{1,0:T(8,128)S(1)}, u32[]{:S(2)}, u32[]{:S(2)}) collective-permute-start(f32[64,256]{1,0:T(8,128)S(1)} %get-tuple-element.65.g2), channel_id=1, source_target_pairs={{0,16},{1,17},{2,18},{3,19},{4,20},{5,21},{6,22},{7,23},{8,24},{9,... | collective-permute-start | bytes 196616 | tf_op jit(solution)/shard_map/ppermute | solution.py:456
  63.0 14.0 %collective-permute-start.17 = (f32[64,256]{1,0:T(8,128)S(1)}, f32[64,256]{1,0:T(8,128)S(1)}, u32[]{:S(2)}, u32[]{:S(2)}) collective-permute-start(f32[64,256]{1,0:T(8,128)S(1)} %get-tuple-element.66.g3), channel_id=1, source_target_pairs={{0,24},{1,25},{2,26},{3,27},{4,28},{5,29},{6,30},{7,31},{8,16},{9,... | collective-permute-start | bytes 196616 | tf_op jit(solution)/shard_map/ppermute | solution.py:456
  64.2 12.9 %collective-permute-start.15 = (f32[64,256]{1,0:T(8,128)S(1)}, f32[64,256]{1,0:T(8,128)S(1)}, u32[]{:S(2)}, u32[]{:S(2)}) collective-permute-start(f32[64,256]{1,0:T(8,128)S(1)} %get-tuple-element.68), channel_id=1, source_target_pairs={{0,8},{1,9},{2,10},{3,11},{4,12},{5,13},{6,14},{7,15},{8,0},{9,1},... | collective-permute-start | bytes 196616 | tf_op jit(solution)/shard_map/ppermute | solution.py:456

commit v22 on v16

--- a/solution.py
+++ b/solution.py
@@ -456,7 +456,7 @@
 
     stored, messages = prepare(col_ids.T, col_vals.T, right_vec, left_vec)
     entries = along_z([stored] * 4)
-    messages = along_z([messages[0]] + [after(messages[1], entries[2]), messages[2], messages[3]])
+    messages = along_z([messages[0]] + [after(messages[1], entries[1]), messages[2], messages[3]])
     q = right_vec.shape[1] // 4
 
     rows1, token1 = build(entries, 1)

time: 78.6 us -> 79.9 us (1.017)
  waiting for transfers between devices: 7.62 us -> 11.3 us
  starting transfers between devices: 29.2 us -> 26.7 us
    ppermute x22, waiting for transfers between devices: 7.62 us -> 11.3 us  [swap(): return lax.ppermute(value, AXES, [(i, i ^ mask) for i in range(32)])]
    ppermute x22, starting transfers between devices: 29.2 us -> 26.7 us  [swap(): return lax.ppermute(value, AXES, [(i, i ^ mask) for i in range(32)])]
  transfers between devices with their start and end apart: 22 -> 22, of which waited for: 7 -> 6; matrix products, arithmetic and copies ran while one was open for 0% -> 0% of each run, Pallas kernels for 31% -> 30%
where the time goes in v22:
time: 79.9 us; the launch traced here: 79.7 us
  Pallas kernels  28.3 us (35%)
  starting transfers between devices  26.7 us (33%)
  blocking collectives  12.3 us (15%)
  waiting for transfers between devices  11.3 us (14%)
  between operations  0.96 us (1%)
    ppermute x22, starting transfers between devices, swap(): return lax.ppermute(value, AXES, [(i, i ^ mask) for i in range(32)])  26.7 us
    all_to_all x1, blocking collectives, by_columns(): squares = lax.all_to_all(after(sums, left_own), AXES, 0, 0, tiled=True)  12.3 us
    ppermute x22, waiting for transfers between devices, swap(): return lax.ppermute(value, AXES, [(i, i ^ mask) for i in range(32)])  11.3 us
    pallas_call x2, Pallas kernels, build(): pl.pallas_call(functools.partial(build_kernel, rel), in_specs=[whole()] *...  9.63 us
    pallas_call x4, Pallas kernels, forward_part(): pl.pallas_call(functools.partial(forward_kernel, blocks, before is not No...  7.12 us
    pallas_call x5, Pallas kernels, backward_part(): pl.pallas_call(functools.partial(backward_kernel, first, blocks, tuple(ex...  5.19 us
    pallas_call x2, Pallas kernels, product_half(): pl.pallas_call(functools.partial(product_kernel, blocks), in_specs=[whole...  2.64 us
    pallas_call x1, Pallas kernels, prepare(): pl.pallas_call(prepare_kernel, in_specs=[pl.BlockSpec(memory_space=pltpu....  1.63 us
  transfers between devices with their start and end apart: 22, of which 6 were waited for; matrix products, arithmetic and copies ran while one was open for 0% of the time, Pallas kernels for 30%

profile of v22, /device:TPU:0, one launch (start us, length us, event | category | flops | bytes accessed | tf_op | source)
XLA Modules:
  0.0 79.7 jit_solution(2544574234507479126)
XLA Ops:
  0.6 1.6 %prepare.1 = (f32[64,256]{1,0:T(8,128)S(1)}, f32[128,256]{1,0:T(8,128)S(1)}, f32[128,256]{1,0:T(8,128)S(1)}, f32[128,256]{1,0:T(8,128)S(1)}, f32[128,256]{1,0:T(8,128)S(1)}) custom-call(s32[16,512]{1,0:T(8,128)} %bitcast.13, bf16[16,512]{1,0:T(8,128)(2,1)} %bitcast.14, f32[256,256]{1,0:T(8,128)} %right.1, f32[512,256]{1,0:T(8,128)} %left_hbm.1), custom_call_target="tpu_custom_call" | custom-call | bytes 16384 | tf_op jit(solution)/shard_map/prepare/pallas_call | solution.py:74
  2.3 3.1 %collective-permute-start = (f32[64,256]{1,0:T(8,128)S(1)}, f32[64,256]{1,0:T(8,128)S(1)}, u32[]{:S(2)}, u32[]{:S(2)}) collective-permute-start(f32[64,256]{1,0:T(8,128)S(1)} %get-tuple-element.45.e0), channel_id=1, source_target_pairs={{0,8},{1,9},{2,10},{3,11},{4,12},{5,13},{6,14},{7,15},{8,0},{9,1},... | collective-permute-start | bytes 196616 | tf_op jit(solution)/shard_map/ppermute | solution.py:436
  5.4 2.4 %collective-permute-start.2 = (f32[64,256]{1,0:T(8,128)S(1)}, f32[64,256]{1,0:T(8,128)S(1)}, u32[]{:S(2)}, u32[]{:S(2)}) collective-permute-start(f32[64,256]{1,0:T(8,128)S(1)} %get-tuple-element.45.e0), channel_id=1, source_target_pairs={{0,24},{1,25},{2,26},{3,27},{4,28},{5,29},{6,30},{7,31},{8,16},{9,... | collective-permute-start | bytes 196616 | tf_op jit(solution)/shard_map/ppermute | solution.py:436
  7.8 0.1 collective-permute-start.1
  8.0 2.8 %collective-permute-start.4 = (f32[128,256]{1,0:T(8,128)S(1)}, f32[128,256]{1,0:T(8,128)S(1)}, u32[]{:S(2)}, u32[]{:S(2)}) collective-permute-start(f32[128,256]{1,0:T(8,128)S(1)} %get-tuple-element.51), channel_id=1, source_target_pairs={{0,16},{1,17},{2,18},{3,19},{4,20},{5,21},{6,22},{7,23},{8,24},{9,... | collective-permute-start | bytes 393224 | tf_op jit(solution)/shard_map/ppermute | solution.py:436
  10.8 1.4 %collective-permute-start.5 = (f32[128,256]{1,0:T(8,128)S(1)}, f32[128,256]{1,0:T(8,128)S(1)}, u32[]{:S(2)}, u32[]{:S(2)}) collective-permute-start(f32[128,256]{1,0:T(8,128)S(1)} %get-tuple-element.52), channel_id=1, source_target_pairs={{0,24},{1,25},{2,26},{3,27},{4,28},{5,29},{6,30},{7,31},{8,16},{9,... | collective-permute-start | bytes 393224 | tf_op jit(solution)/shard_map/ppermute | solution.py:436
  12.1 0.1 collective-permute-done.2.e3
  12.2 7.9 %collective-permute-done.1.e2 = f32[64,256]{1,0:T(8,128)S(1)} collective-permute-done((f32[64,256]{1,0:T(8,128)S(1)}, f32[64,256]{1,0:T(8,128)S(1)}, u32[]{:S(2)}, u32[]{:S(2)}) %collective-permute-start.1) | collective-permute-done | bytes 65568 | tf_op jit(solution)/shard_map/ppermute | solution.py:436
  20.1 4.7 %dense_rows.2 = (bf16[16,1024,256]{2,1,0:T(8,128)(2,1)S(1)}, bf16[16,1024,256]{2,1,0:T(8,128)(2,1)S(1)}, f32[8,128]{1,0:T(8,128)S(1)}) custom-call(f32[64,256]{1,0:T(8,128)S(1)} %get-tuple-element.45.e0, f32[64,256]{1,0:T(8,128)S(1)} %collective-permute-done.e1, f32[64,256]{1,0:T(8,128)S(1)} %collective-permute-done.1.e2, ...), custom_call_target="tpu_custom_call" | custom-call | flops 2147483648 | bytes 16777216 | tf_op jit(solution)/shard_map/dense_rows/pallas_call | solution.py:154
  24.9 0.0 copy-start
  25.0 0.1 collective-permute-start.7
  25.0 1.5 %collective-permute-start.6 = (f32[4,64,256]{2,1,0:T(8,128)S(1)}, f32[4,64,256]{2,1,0:T(8,128)S(1)}, u32[]{:S(2)}, u32[]{:S(2)}) collective-permute-start(f32[4,64,256]{2,1,0:T(8,128)S(1)} %stack_right.1.refs_0_.right), channel_id=1, source_target_pairs={{0,4},{1,5},{2,6},{3,7},{4,0},{5,1},{6,2},{7,3},{8,12},{9,13},{10,... | collective-permute-start | bytes 786440 | tf_op jit(solution)/shard_map/ppermute | solution.py:436
  26.6 4.9 %dense_rows.3 = (bf16[16,1024,256]{2,1,0:T(8,128)(2,1)S(1)}, bf16[16,1024,256]{2,1,0:T(8,128)(2,1)S(1)}, f32[8,128]{1,0:T(8,128)S(1)}) custom-call(f32[64,256]{1,0:T(8,128)S(1)} %get-tuple-element.45.e0, f32[64,256]{1,0:T(8,128)S(1)} %collective-permute-done.e1, f32[64,256]{1,0:T(8,128)S(1)} %collective-permute-done.1.e2, ...), custom_call_target="tpu_custom_call" | custom-call | flops 33554432 | bytes 262144 | tf_op jit(solution)/shard_map/dense_rows/pallas_call | solution.py:154
  31.5 2.3 %forward_part.4.refs_1_ = f32[1024,128]{1,0:T(8,128)S(1)} custom-call(bf16[16,1024,256]{2,1,0:T(8,128)(2,1)S(1)} %get-tuple-element.46.hi_ref, bf16[16,1024,256]{2,1,0:T(8,128)(2,1)S(1)} %get-tuple-element.47.lo_ref, f32[4,64,256]{2,1,0:T(8,128)S(1)} %stack_right.1.refs_0_.right, f32[4,64,256]{2,1,0:T(8,128)S(1)} %collective-permute-done.7.refs_1_, ...), custom_call_target="tpu_custom_call" | custom-call | flops 67108864 | bytes 131072 | tf_op jit(solution)/shard_map/forward_part/pallas_call | solution.py:196
  33.8 0.2 collective-permute-start.8
  34.1 1.2 %forward_part.5.before = f32[1024,128]{1,0:T(8,128)S(1)} custom-call(bf16[16,1024,256]{2,1,0:T(8,128)(2,1)S(1)} %get-tuple-element.46.hi_ref, bf16[16,1024,256]{2,1,0:T(8,128)(2,1)S(1)} %get-tuple-element.47.lo_ref, f32[4,64,256]{2,1,0:T(8,128)S(1)} %collective-permute-done.6.refs_0_, f32[1024,128]{1,0:T(8,128)S(1)} %forward_part.4.refs_1_), custom_call_target="tpu_custom_call" | custom-call | flops 33554432 | bytes 65536 | tf_op jit(solution)/shard_map/forward_part/pallas_call | solution.py:196
  35.3 0.1 collective-permute-done.8.vec
  35.4 1.3 %product_half.2.mine = f32[64,1024]{1,0:T(8,128)S(1)} custom-call(bf16[16,1024,256]{2,1,0:T(8,128)(2,1)S(1)} %get-tuple-element.46.hi_ref, bf16[16,1024,256]{2,1,0:T(8,128)(2,1)S(1)} %get-tuple-element.47.lo_ref, f32[4,64,256]{2,1,0:T(8,128)S(1)} %collective-permute-done.8.vec, f32[1024,128]{1,0:T(8,128)S(1)} %forward_part.5.before), custom_call_target="tpu_custom_call" | custom-call | flops 33554432 | bytes 65536 | tf_op jit(solution)/shard_map/product_half/pallas_call | solution.py:228
  36.7 1.6 %collective-permute-start.10 = (f32[64,1024]{1,0:T(8,128)S(1)}, f32[64,1024]{1,0:T(8,128)S(1)}, u32[]{:S(2)}, u32[]{:S(2)}) collective-permute-start(f32[64,1024]{1,0:T(8,128)S(1)} %product_half.2.mine), channel_id=1, source_target_pairs={{0,1},{1,0},{2,3},{3,2},{4,5},{5,4},{6,7},{7,6},{8,9},{9,8},{10,11... | collective-permute-start | bytes 786440 | tf_op jit(solution)/shard_map/ppermute | solution.py:436
  38.3 2.3 %forward_part.6.refs_1_ = f32[1024,128]{1,0:T(8,128)S(1)} custom-call(bf16[16,1024,256]{2,1,0:T(8,128)(2,1)S(1)} %get-tuple-element.56.hi_ref, bf16[16,1024,256]{2,1,0:T(8,128)(2,1)S(1)} %get-tuple-element.57.lo_ref, f32[4,64,256]{2,1,0:T(8,128)S(1)} %stack_right.1.refs_0_.right, f32[4,64,256]{2,1,0:T(8,128)S(1)} %collective-permute-done.7.refs_1_), custom_call_target="tpu_custom_call" | custom-call | flops 67108864 | bytes 131072 | tf_op jit(solution)/shard_map/forward_part/pallas_call | solution.py:196
  40.7 0.0 copy-start.5
  40.7 1.2 %forward_part.7.before = f32[1024,128]{1,0:T(8,128)S(1)} custom-call(bf16[16,1024,256]{2,1,0:T(8,128)(2,1)S(1)} %get-tuple-element.56.hi_ref, bf16[16,1024,256]{2,1,0:T(8,128)(2,1)S(1)} %get-tuple-element.57.lo_ref, f32[4,64,256]{2,1,0:T(8,128)S(1)} %collective-permute-done.6.refs_0_, f32[1024,128]{1,0:T(8,128)S(1)} %forward_part.6.refs_1_), custom_call_target="tpu_custom_call" | custom-call | flops 33554432 | bytes 65536 | tf_op jit(solution)/shard_map/forward_part/pallas_call | solution.py:196
  41.9 1.3 %product_half.3.mine = f32[64,1024]{1,0:T(8,128)S(1)} custom-call(bf16[16,1024,256]{2,1,0:T(8,128)(2,1)S(1)} %get-tuple-element.56.hi_ref, bf16[16,1024,256]{2,1,0:T(8,128)(2,1)S(1)} %get-tuple-element.57.lo_ref, f32[4,64,256]{2,1,0:T(8,128)S(1)} %collective-permute-done.8.vec, f32[1024,128]{1,0:T(8,128)S(1)} %forward_part.7.before, ...), custom_call_target="tpu_custom_call" | custom-call | flops 33554432 | bytes 65536 | tf_op jit(solution)/shard_map/product_half/pallas_call | solution.py:228
  43.3 0.5 collective-permute-start.9
  43.8 1.4 %collective-permute-done.10.other = f32[64,1024]{1,0:T(8,128)S(1)} collective-permute-done((f32[64,1024]{1,0:T(8,128)S(1)}, f32[64,1024]{1,0:T(8,128)S(1)}, u32[]{:S(2)}, u32[]{:S(2)}) %collective-permute-start.10) | collective-permute-done | bytes 262176 | tf_op jit(solution)/shard_map/ppermute | solution.py:436
  45.2 0.2 left_half.2
  45.4 1.3 %collective-permute-start.18 = (f32[64,256]{1,0:T(8,128)S(1)}, f32[64,256]{1,0:T(8,128)S(1)}, u32[]{:S(2)}, u32[]{:S(2)}) collective-permute-start(f32[64,256]{1,0:T(8,128)S(1)} %get-tuple-element.71), channel_id=1, source_target_pairs={{0,8},{1,9},{2,10},{3,11},{4,12},{5,13},{6,14},{7,15},{8,0},{9,1},... | collective-permute-start | bytes 196616 | tf_op jit(solution)/shard_map/ppermute | solution.py:436
  46.7 2.3 %collective-permute-start.19 = (f32[64,256]{1,0:T(8,128)S(1)}, f32[64,256]{1,0:T(8,128)S(1)}, u32[]{:S(2)}, u32[]{:S(2)}) collective-permute-start(f32[64,256]{1,0:T(8,128)S(1)} %get-tuple-element.72), channel_id=1, source_target_pairs={{0,16},{1,17},{2,18},{3,19},{4,20},{5,21},{6,22},{7,23},{8,24},{9,... | collective-permute-start | bytes 196616 | tf_op jit(solution)/shard_map/ppermute | solution.py:436
  49.0 0.8 %collective-permute-start.20 = (f32[64,256]{1,0:T(8,128)S(1)}, f32[64,256]{1,0:T(8,128)S(1)}, u32[]{:S(2)}, u32[]{:S(2)}) collective-permute-start(f32[64,256]{1,0:T(8,128)S(1)} %get-tuple-element.73), channel_id=1, source_target_pairs={{0,24},{1,25},{2,26},{3,27},{4,28},{5,29},{6,30},{7,31},{8,16},{9,... | collective-permute-start | bytes 196616 | tf_op jit(solution)/shard_map/ppermute | solution.py:436
  49.9 2.3 %backward_part.5.refs_1_.refs_0_ = f32[1024,256]{1,0:T(8,128)S(1)} custom-call(bf16[16,1024,256]{2,1,0:T(8,128)(2,1)S(1)} %get-tuple-element.56.hi_ref, bf16[16,1024,256]{2,1,0:T(8,128)(2,1)S(1)} %get-tuple-element.57.lo_ref, bf16[128,1024]{1,0:T(8,128)(2,1)S(1)} %get-tuple-element.59.both_ref), custom_call_target="tpu_custom_call" | custom-call | flops 134217728 | bytes 262144 | tf_op jit(solution)/shard_map/backward_part/pallas_call | solution.py:309
  52.2 0.2 left_half.3
  52.4 0.7 backward_part.7.refs_1_.near
  53.1 0.7 backward_part.9
  53.8 0.1 collective-permute-start.12
  53.9 0.7 backward_part.8.token
  54.6 0.6 collective-permute-start.11
  55.2 0.2 collective-permute-done.12.far
  55.5 1.4 %collective-permute-start.14 = (f32[128,256]{1,0:T(8,128)S(1)}, f32[128,256]{1,0:T(8,128)S(1)}, u32[]{:S(2)}, u32[]{:S(2)}) collective-permute-start(f32[128,256]{1,0:T(8,128)S(1)} %get-tuple-element.64), channel_id=1, source_target_pairs={{0,4},{1,5},{2,6},{3,7},{4,0},{5,1},{6,2},{7,3},{8,12},{9,13},{10,... | collective-permute-start | bytes 393224 | tf_op jit(solution)/shard_map/ppermute | solution.py:436
  56.9 0.7 collective-permute-start.13
  57.7 1.9 %collective-permute-start.21 = (f32[4,64,256]{2,1,0:T(8,128)S(1)}, f32[4,64,256]{2,1,0:T(8,128)S(1)}, u32[]{:S(2)}, u32[]{:S(2)}) collective-permute-start(f32[4,64,256]{2,1,0:T(8,128)S(1)} %stack_left.1.own), channel_id=1, source_target_pairs={{0,1},{1,0},{2,3},{3,2},{4,5},{5,4},{6,7},{7,6},{8,9},{9,8},{10,11... | collective-permute-start | bytes 786440 | tf_op jit(solution)/shard_map/ppermute | solution.py:436
  59.6 0.7 backward_part.6.keep
  60.3 1.6 %collective-permute-done.14.got = f32[128,256]{1,0:T(8,128)S(1)} collective-permute-done((f32[128,256]{1,0:T(8,128)S(1)}, f32[128,256]{1,0:T(8,128)S(1)}, u32[]{:S(2)}, u32[]{:S(2)}) %collective-permute-start.14) | collective-permute-done | bytes 131104 | tf_op jit(solution)/shard_map/ppermute | solution.py:436
  61.9 1.5 %collective-permute-start.16 = (f32[64,256]{1,0:T(8,128)S(1)}, f32[64,256]{1,0:T(8,128)S(1)}, u32[]{:S(2)}, u32[]{:S(2)}) collective-permute-start(f32[64,256]{1,0:T(8,128)S(1)} %get-tuple-element.65.g2), channel_id=1, source_target_pairs={{0,16},{1,17},{2,18},{3,19},{4,20},{5,21},{6,22},{7,23},{8,24},{9,... | collective-permute-start | bytes 196616 | tf_op jit(solution)/shard_map/ppermute | solution.py:436
  63.4 1.6 %collective-permute-start.17 = (f32[64,256]{1,0:T(8,128)S(1)}, f32[64,256]{1,0:T(8,128)S(1)}, u32[]{:S(2)}, u32[]{:S(2)}) collective-permute-start(f32[64,256]{1,0:T(8,128)S(1)} %get-tuple-element.66.g3), channel_id=1, source_target_pairs={{0,24},{1,25},{2,26},{3,27},{4,28},{5,29},{6,30},{7,31},{8,16},{9,... | collective-permute-start | bytes 196616 | tf_op jit(solution)/shard_map/ppermute | solution.py:436
  65.1 0.3 right_norm.1
  65.4 0.6 collective-permute-start.15
  65.9 12.3 %all_to_all.5.squares = f32[32,1,128]{2,1,0:T(1,128)S(1)} all-to-all(f32[32,1,128]{2,1,0:T(1,128)S(1)} %bitcast.9), channel_id=1, replica_groups=mesh['doc'=16,'feat'=2] {'doc','feat'}, dimensions={0} | all-to-all | bytes 32768 | tf_op jit(solution)/shard_map/all_to_all | solution.py:493
  78.3 1.3 %finish.1 = (f32[512,256]{1,0:T(8,128)}, f32[256,256]{1,0:T(8,128)}, f32[256,256]{1,0:T(8,128)}, f32[256,256]{1,0:T(8,128)}, f32[1,256]{1,0:T(1,128)}, /*index=5*/f32[1,256]{1,0:T(1,128)}, f32[1,256]{1,0:T(1,128)}) custom-call(f32[64,256]{1,0:T(8,128)S(1)} %get-tuple-element.67.g0, f32[64,256]{1,0:T(8,128)S(1)} %collective-permute-done.15.g1, ...), custom_call_target="tpu_custom_call" | custom-call | flops 16384 | bytes 20480 | tf_op jit(solution)/shard_map/finish/pallas_call | solution.py:425
  (35 shorter events, 0.2 us)
Async XLA Ops:
  2.3 9.9 %collective-permute-start = (f32[64,256]{1,0:T(8,128)S(1)}, f32[64,256]{1,0:T(8,128)S(1)}, u32[]{:S(2)}, u32[]{:S(2)}) collective-permute-start(f32[64,256]{1,0:T(8,128)S(1)} %get-tuple-element.45.e0), channel_id=1, source_target_pairs={{0,8},{1,9},{2,10},{3,11},{4,12},{5,13},{6,14},{7,15},{8,0},{9,1},... | collective-permute-start | bytes 196616 | tf_op jit(solution)/shard_map/ppermute | solution.py:436
  5.4 6.9 %collective-permute-start.2 = (f32[64,256]{1,0:T(8,128)S(1)}, f32[64,256]{1,0:T(8,128)S(1)}, u32[]{:S(2)}, u32[]{:S(2)}) collective-permute-start(f32[64,256]{1,0:T(8,128)S(1)} %get-tuple-element.45.e0), channel_id=1, source_target_pairs={{0,24},{1,25},{2,26},{3,27},{4,28},{5,29},{6,30},{7,31},{8,16},{9,... | collective-permute-start | bytes 196616 | tf_op jit(solution)/shard_map/ppermute | solution.py:436
  7.8 12.3 %collective-permute-start.1 = (f32[64,256]{1,0:T(8,128)S(1)}, f32[64,256]{1,0:T(8,128)S(1)}, u32[]{:S(2)}, u32[]{:S(2)}) collective-permute-start(f32[64,256]{1,0:T(8,128)S(1)} %get-tuple-element.45.e0), channel_id=1, source_target_pairs={{0,16},{1,17},{2,18},{3,19},{4,20},{5,21},{6,22},{7,23},{8,24},{9,... | collective-permute-start | bytes 196616 | tf_op jit(solution)/shard_map/ppermute | solution.py:436
  8.0 16.9 %collective-permute-start.4 = (f32[128,256]{1,0:T(8,128)S(1)}, f32[128,256]{1,0:T(8,128)S(1)}, u32[]{:S(2)}, u32[]{:S(2)}) collective-permute-start(f32[128,256]{1,0:T(8,128)S(1)} %get-tuple-element.51), channel_id=1, source_target_pairs={{0,16},{1,17},{2,18},{3,19},{4,20},{5,21},{6,22},{7,23},{8,24},{9,... | collective-permute-start | bytes 393224 | tf_op jit(solution)/shard_map/ppermute | solution.py:436
  10.8 14.1 %collective-permute-start.5 = (f32[128,256]{1,0:T(8,128)S(1)}, f32[128,256]{1,0:T(8,128)S(1)}, u32[]{:S(2)}, u32[]{:S(2)}) collective-permute-start(f32[128,256]{1,0:T(8,128)S(1)} %get-tuple-element.52), channel_id=1, source_target_pairs={{0,24},{1,25},{2,26},{3,27},{4,28},{5,29},{6,30},{7,31},{8,16},{9,... | collective-permute-start | bytes 393224 | tf_op jit(solution)/shard_map/ppermute | solution.py:436
  12.1 12.8 %collective-permute-start.3 = (f32[128,256]{1,0:T(8,128)S(1)}, f32[128,256]{1,0:T(8,128)S(1)}, u32[]{:S(2)}, u32[]{:S(2)}) collective-permute-start(f32[128,256]{1,0:T(8,128)S(1)} %get-tuple-element.50), channel_id=1, source_target_pairs={{0,8},{1,9},{2,10},{3,11},{4,12},{5,13},{6,14},{7,15},{8,0},{9,1},... | collective-permute-start | bytes 393224 | tf_op jit(solution)/shard_map/ppermute | solution.py:436
  24.9 13.4 %copy-start = (f32[4,64,256]{2,1,0:T(8,128)}, f32[4,64,256]{2,1,0:T(8,128)S(1)}, u32[]{:S(2)}) copy-start(f32[4,64,256]{2,1,0:T(8,128)S(1)} %stack_right.1.refs_0_.right) | copy-start | bytes 786436
  25.0 6.5 %collective-permute-start.7 = (f32[4,64,256]{2,1,0:T(8,128)S(1)}, f32[4,64,256]{2,1,0:T(8,128)S(1)}, u32[]{:S(2)}, u32[]{:S(2)}) collective-permute-start(f32[4,64,256]{2,1,0:T(8,128)S(1)} %stack_right.1.refs_0_.right), channel_id=1, source_target_pairs={{0,2},{1,3},{2,0},{3,1},{4,6},{5,7},{6,4},{7,5},{8,10},{9,11},{10,... | collective-permute-start | bytes 786440 | tf_op jit(solution)/shard_map/ppermute | solution.py:436
  25.0 8.8 %collective-permute-start.6 = (f32[4,64,256]{2,1,0:T(8,128)S(1)}, f32[4,64,256]{2,1,0:T(8,128)S(1)}, u32[]{:S(2)}, u32[]{:S(2)}) collective-permute-start(f32[4,64,256]{2,1,0:T(8,128)S(1)} %stack_right.1.refs_0_.right), channel_id=1, source_target_pairs={{0,4},{1,5},{2,6},{3,7},{4,0},{5,1},{6,2},{7,3},{8,12},{9,13},{10,... | collective-permute-start | bytes 786440 | tf_op jit(solution)/shard_map/ppermute | solution.py:436
  33.8 1.6 %collective-permute-start.8 = (f32[4,64,256]{2,1,0:T(8,128)S(1)}, f32[4,64,256]{2,1,0:T(8,128)S(1)}, u32[]{:S(2)}, u32[]{:S(2)}) collective-permute-start(f32[4,64,256]{2,1,0:T(8,128)S(1)} %collective-permute-done.6.refs_0_), channel_id=1, source_target_pairs={{0,2},{1,3},{2,0},{3,1},{4,6},{5,7},{6,4},{7,5},{8,10},{9,11},{10,... | collective-permute-start | bytes 786440 | tf_op jit(solution)/shard_map/ppermute | solution.py:436
  36.7 8.5 %collective-permute-start.10 = (f32[64,1024]{1,0:T(8,128)S(1)}, f32[64,1024]{1,0:T(8,128)S(1)}, u32[]{:S(2)}, u32[]{:S(2)}) collective-permute-start(f32[64,1024]{1,0:T(8,128)S(1)} %product_half.2.mine), channel_id=1, source_target_pairs={{0,1},{1,0},{2,3},{3,2},{4,5},{5,4},{6,7},{7,6},{8,9},{9,8},{10,11... | collective-permute-start | bytes 786440 | tf_op jit(solution)/shard_map/ppermute | solution.py:436
  40.7 1.3 %copy-start.5 = (f32[256]{0:T(256)S(1)}, f32[256]{0:T(256)}, u32[]{:S(2)}) copy-start(f32[256]{0:T(256)} %param.15) | copy-start | bytes 3076
  43.3 8.9 %collective-permute-start.9 = (f32[64,1024]{1,0:T(8,128)S(1)}, f32[64,1024]{1,0:T(8,128)S(1)}, u32[]{:S(2)}, u32[]{:S(2)}) collective-permute-start(f32[64,1024]{1,0:T(8,128)S(1)} %product_half.3.mine), channel_id=1, source_target_pairs={{0,1},{1,0},{2,3},{3,2},{4,5},{5,4},{6,7},{7,6},{8,9},{9,8},{10,11... | collective-permute-start | bytes 786440 | tf_op jit(solution)/shard_map/ppermute | solution.py:436
  45.4 9.8 %collective-permute-start.18 = (f32[64,256]{1,0:T(8,128)S(1)}, f32[64,256]{1,0:T(8,128)S(1)}, u32[]{:S(2)}, u32[]{:S(2)}) collective-permute-start(f32[64,256]{1,0:T(8,128)S(1)} %get-tuple-element.71), channel_id=1, source_target_pairs={{0,8},{1,9},{2,10},{3,11},{4,12},{5,13},{6,14},{7,15},{8,0},{9,1},... | collective-permute-start | bytes 196616 | tf_op jit(solution)/shard_map/ppermute | solution.py:436
  46.7 8.4 %collective-permute-start.19 = (f32[64,256]{1,0:T(8,128)S(1)}, f32[64,256]{1,0:T(8,128)S(1)}, u32[]{:S(2)}, u32[]{:S(2)}) collective-permute-start(f32[64,256]{1,0:T(8,128)S(1)} %get-tuple-element.72), channel_id=1, source_target_pairs={{0,16},{1,17},{2,18},{3,19},{4,20},{5,21},{6,22},{7,23},{8,24},{9,... | collective-permute-start | bytes 196616 | tf_op jit(solution)/shard_map/ppermute | solution.py:436
  49.0 6.1 %collective-permute-start.20 = (f32[64,256]{1,0:T(8,128)S(1)}, f32[64,256]{1,0:T(8,128)S(1)}, u32[]{:S(2)}, u32[]{:S(2)}) collective-permute-start(f32[64,256]{1,0:T(8,128)S(1)} %get-tuple-element.73), channel_id=1, source_target_pairs={{0,24},{1,25},{2,26},{3,27},{4,28},{5,29},{6,30},{7,31},{8,16},{9,... | collective-permute-start | bytes 196616 | tf_op jit(solution)/shard_map/ppermute | solution.py:436
  53.8 1.6 %collective-permute-start.12 = (f32[264,256]{1,0:T(8,128)S(1)}, f32[264,256]{1,0:T(8,128)S(1)}, u32[]{:S(2)}, u32[]{:S(2)}) collective-permute-start(f32[264,256]{1,0:T(8,128)S(1)} %backward_part.9), channel_id=1, source_target_pairs={{0,2},{1,3},{2,0},{3,1},{4,6},{5,7},{6,4},{7,5},{8,10},{9,11},{10,... | collective-permute-start | bytes 811016 | tf_op jit(solution)/shard_map/ppermute | solution.py:436
  54.6 5.7 %collective-permute-start.11 = (f32[256,256]{1,0:T(8,128)S(1)}, f32[256,256]{1,0:T(8,128)S(1)}, u32[]{:S(2)}, u32[]{:S(2)}) collective-permute-start(f32[256,256]{1,0:T(8,128)S(1)} %backward_part.8.token), channel_id=1, source_target_pairs={{0,2},{1,3},{2,0},{3,1},{4,6},{5,7},{6,4},{7,5},{8,10},{9,11},{10,... | collective-permute-start | bytes 786440 | tf_op jit(solution)/shard_map/ppermute | solution.py:436
  55.5 6.4 %collective-permute-start.14 = (f32[128,256]{1,0:T(8,128)S(1)}, f32[128,256]{1,0:T(8,128)S(1)}, u32[]{:S(2)}, u32[]{:S(2)}) collective-permute-start(f32[128,256]{1,0:T(8,128)S(1)} %get-tuple-element.64), channel_id=1, source_target_pairs={{0,4},{1,5},{2,6},{3,7},{4,0},{5,1},{6,2},{7,3},{8,12},{9,13},{10,... | collective-permute-start | bytes 393224 | tf_op jit(solution)/shard_map/ppermute | solution.py:436
  56.9 8.2 %copy-start.1 = (f32[4,64,256]{2,1,0:T(8,128)S(1)}, f32[4,64,256]{2,1,0:T(8,128)}, u32[]{:S(2)}) copy-start(f32[4,64,256]{2,1,0:T(8,128)} %copy-done) | copy-start | bytes 786436
  56.9 21.4 %copy-start.2 = (f32[256,256]{1,0:T(8,128)S(1)}, f32[256,256]{1,0:T(8,128)}, u32[]{:S(2)}) copy-start(f32[256,256]{1,0:T(8,128)} %right.1) | copy-start | bytes 786436
  56.9 21.4 %copy-start.3 = (f32[256,256]{1,0:T(8,128)S(1)}, f32[256,256]{1,0:T(8,128)}, u32[]{:S(2)}) copy-start(f32[256,256]{1,0:T(8,128)} %search.1) | copy-start | bytes 786436
  56.9 21.4 %copy-start.4 = (f32[256,256]{1,0:T(8,128)S(1)}, f32[256,256]{1,0:T(8,128)}, u32[]{:S(2)}) copy-start(f32[256,256]{1,0:T(8,128)} %solution.1) | copy-start | bytes 786436
  56.9 21.4 %copy-start.6 = (f32[256]{0:T(256)S(1)}, f32[256]{0:T(256)}, u32[]{:S(2)}) copy-start(f32[256]{0:T(256)} %param.16) | copy-start | bytes 3076
  56.9 21.4 %copy-start.7 = (f32[256]{0:T(256)S(1)}, f32[256]{0:T(256)}, u32[]{:S(2)}) copy-start(f32[256]{0:T(256)} %param.17) | copy-start | bytes 3076
  56.9 8.1 %collective-permute-start.13 = (f32[136,256]{1,0:T(8,128)S(1)}, f32[136,256]{1,0:T(8,128)S(1)}, u32[]{:S(2)}, u32[]{:S(2)}) collective-permute-start(f32[136,256]{1,0:T(8,128)S(1)} %get-tuple-element.62), channel_id=1, source_target_pairs={{0,4},{1,5},{2,6},{3,7},{4,0},{5,1},{6,2},{7,3},{8,12},{9,13},{10,... | collective-permute-start | bytes 417800 | tf_op jit(solution)/shard_map/ppermute | solution.py:436
  57.7 20.6 %collective-permute-start.21 = (f32[4,64,256]{2,1,0:T(8,128)S(1)}, f32[4,64,256]{2,1,0:T(8,128)S(1)}, u32[]{:S(2)}, u32[]{:S(2)}) collective-permute-start(f32[4,64,256]{2,1,0:T(8,128)S(1)} %stack_left.1.own), channel_id=1, source_target_pairs={{0,1},{1,0},{2,3},{3,2},{4,5},{5,4},{6,7},{7,6},{8,9},{9,8},{10,11... | collective-permute-start | bytes 786440 | tf_op jit(solution)/shard_map/ppermute | solution.py:436
  61.9 16.4 %collective-permute-start.16 = (f32[64,256]{1,0:T(8,128)S(1)}, f32[64,256]{1,0:T(8,128)S(1)}, u32[]{:S(2)}, u32[]{:S(2)}) collective-permute-start(f32[64,256]{1,0:T(8,128)S(1)} %get-tuple-element.65.g2), channel_id=1, source_target_pairs={{0,16},{1,17},{2,18},{3,19},{4,20},{5,21},{6,22},{7,23},{8,24},{9,... | collective-permute-start | bytes 196616 | tf_op jit(solution)/shard_map/ppermute | solution.py:436
  63.4 14.9 %collective-permute-start.17 = (f32[64,256]{1,0:T(8,128)S(1)}, f32[64,256]{1,0:T(8,128)S(1)}, u32[]{:S(2)}, u32[]{:S(2)}) collective-permute-start(f32[64,256]{1,0:T(8,128)S(1)} %get-tuple-element.66.g3), channel_id=1, source_target_pairs={{0,24},{1,25},{2,26},{3,27},{4,28},{5,29},{6,30},{7,31},{8,16},{9,... | collective-permute-start | bytes 196616 | tf_op jit(solution)/shard_map/ppermute | solution.py:436
  65.4 12.9 %collective-permute-start.15 = (f32[64,256]{1,0:T(8,128)S(1)}, f32[64,256]{1,0:T(8,128)S(1)}, u32[]{:S(2)}, u32[]{:S(2)}) collective-permute-start(f32[64,256]{1,0:T(8,128)S(1)} %get-tuple-element.68), channel_id=1, source_target_pairs={{0,8},{1,9},{2,10},{3,11},{4,12},{5,13},{6,14},{7,15},{8,0},{9,1},... | collective-permute-start | bytes 196616 | tf_op jit(solution)/shard_map/ppermute | solution.py:436

commit v23 on v22

--- a/solution.py
+++ b/solution.py
@@ -456,7 +456,7 @@
 
     stored, messages = prepare(col_ids.T, col_vals.T, right_vec, left_vec)
     entries = along_z([stored] * 4)
-    messages = along_z([messages[0]] + [after(messages[1], entries[1]), messages[2], messages[3]])
+    messages = along_z([messages[0]] + [after(messages[1], entries[3]), messages[2], messages[3]])
     q = right_vec.shape[1] // 4
 
     rows1, token1 = build(entries, 1)

time: 79.9 us -> 78.4 us (0.981)
  waiting for transfers between devices: 11.3 us -> 9.11 us
  starting transfers between devices: 26.7 us -> 27.5 us
    ppermute x22, waiting for transfers between devices: 11.3 us -> 9.11 us  [swap(): return lax.ppermute(value, AXES, [(i, i ^ mask) for i in range(32)])]
    ppermute x22, starting transfers between devices: 26.7 us -> 27.5 us  [swap(): return lax.ppermute(value, AXES, [(i, i ^ mask) for i in range(32)])]
  transfers between devices with their start and end apart: 22 -> 22, of which waited for: 6 -> 6; matrix products, arithmetic and copies ran while one was open for 0% -> 0% of each run, Pallas kernels for 30% -> 31%
where the time goes in v23:
time: 78.4 us; the launch traced here: 78.2 us
  Pallas kernels  28.3 us (36%)
  starting transfers between devices  27.5 us (35%)
  blocking collectives  12.3 us (16%)
  waiting for transfers between devices  9.11 us (12%)
  between operations  0.95 us (1%)
    ppermute x22, starting transfers between devices, swap(): return lax.ppermute(value, AXES, [(i, i ^ mask) for i in range(32)])  27.5 us
    all_to_all x1, blocking collectives, by_columns(): squares = lax.all_to_all(after(sums, left_own), AXES, 0, 0, tiled=True)  12.3 us
    pallas_call x2, Pallas kernels, build(): pl.pallas_call(functools.partial(build_kernel, rel), in_specs=[whole()] *...  9.62 us
    ppermute x22, waiting for transfers between devices, swap(): return lax.ppermute(value, AXES, [(i, i ^ mask) for i in range(32)])  9.11 us
    pallas_call x4, Pallas kernels, forward_part(): pl.pallas_call(functools.partial(forward_kernel, blocks, before is not No...  7.12 us
    pallas_call x5, Pallas kernels, backward_part(): pl.pallas_call(functools.partial(backward_kernel, first, blocks, tuple(ex...  5.19 us
    pallas_call x2, Pallas kernels, product_half(): pl.pallas_call(functools.partial(product_kernel, blocks), in_specs=[whole...  2.64 us
    pallas_call x1, Pallas kernels, prepare(): pl.pallas_call(prepare_kernel, in_specs=[pl.BlockSpec(memory_space=pltpu....  1.63 us
  transfers between devices with their start and end apart: 22, of which 6 were waited for; matrix products, arithmetic and copies ran while one was open for 0% of the time, Pallas kernels for 31%

profile of v23, /device:TPU:0, one launch (start us, length us, event | category | flops | bytes accessed | tf_op | source)
XLA Modules:
  0.0 78.2 jit_solution(318819568990611945)
XLA Ops:
  0.6 1.6 %prepare.1 = (f32[64,256]{1,0:T(8,128)S(1)}, f32[128,256]{1,0:T(8,128)S(1)}, f32[128,256]{1,0:T(8,128)S(1)}, f32[128,256]{1,0:T(8,128)S(1)}, f32[128,256]{1,0:T(8,128)S(1)}) custom-call(s32[16,512]{1,0:T(8,128)} %bitcast.13, bf16[16,512]{1,0:T(8,128)(2,1)} %bitcast.14, f32[256,256]{1,0:T(8,128)} %right.1, f32[512,256]{1,0:T(8,128)} %left_hbm.1), custom_call_target="tpu_custom_call" | custom-call | bytes 16384 | tf_op jit(solution)/shard_map/prepare/pallas_call | solution.py:74
  2.3 5.1 %collective-permute-start.2 = (f32[64,256]{1,0:T(8,128)S(1)}, f32[64,256]{1,0:T(8,128)S(1)}, u32[]{:S(2)}, u32[]{:S(2)}) collective-permute-start(f32[64,256]{1,0:T(8,128)S(1)} %get-tuple-element.45.e0), channel_id=1, source_target_pairs={{0,24},{1,25},{2,26},{3,27},{4,28},{5,29},{6,30},{7,31},{8,16},{9,... | collective-permute-start | bytes 196616 | tf_op jit(solution)/shard_map/ppermute | solution.py:436
  7.4 0.6 collective-permute-start
  8.1 2.3 %collective-permute-start.4 = (f32[128,256]{1,0:T(8,128)S(1)}, f32[128,256]{1,0:T(8,128)S(1)}, u32[]{:S(2)}, u32[]{:S(2)}) collective-permute-start(f32[128,256]{1,0:T(8,128)S(1)} %get-tuple-element.51), channel_id=1, source_target_pairs={{0,16},{1,17},{2,18},{3,19},{4,20},{5,21},{6,22},{7,23},{8,24},{9,... | collective-permute-start | bytes 393224 | tf_op jit(solution)/shard_map/ppermute | solution.py:436
  10.3 1.5 %collective-permute-start.5 = (f32[128,256]{1,0:T(8,128)S(1)}, f32[128,256]{1,0:T(8,128)S(1)}, u32[]{:S(2)}, u32[]{:S(2)}) collective-permute-start(f32[128,256]{1,0:T(8,128)S(1)} %get-tuple-element.52), channel_id=1, source_target_pairs={{0,24},{1,25},{2,26},{3,27},{4,28},{5,29},{6,30},{7,31},{8,16},{9,... | collective-permute-start | bytes 393224 | tf_op jit(solution)/shard_map/ppermute | solution.py:436
  11.8 0.8 %collective-permute-start.3 = (f32[128,256]{1,0:T(8,128)S(1)}, f32[128,256]{1,0:T(8,128)S(1)}, u32[]{:S(2)}, u32[]{:S(2)}) collective-permute-start(f32[128,256]{1,0:T(8,128)S(1)} %get-tuple-element.50), channel_id=1, source_target_pairs={{0,8},{1,9},{2,10},{3,11},{4,12},{5,13},{6,14},{7,15},{8,0},{9,1},... | collective-permute-start | bytes 393224 | tf_op jit(solution)/shard_map/ppermute | solution.py:436
  12.6 5.1 %collective-permute-done.1.e2 = f32[64,256]{1,0:T(8,128)S(1)} collective-permute-done((f32[64,256]{1,0:T(8,128)S(1)}, f32[64,256]{1,0:T(8,128)S(1)}, u32[]{:S(2)}, u32[]{:S(2)}) %collective-permute-start.1) | collective-permute-done | bytes 65568 | tf_op jit(solution)/shard_map/ppermute | solution.py:436
  17.7 4.7 %dense_rows.2 = (bf16[16,1024,256]{2,1,0:T(8,128)(2,1)S(1)}, bf16[16,1024,256]{2,1,0:T(8,128)(2,1)S(1)}, f32[8,128]{1,0:T(8,128)S(1)}) custom-call(f32[64,256]{1,0:T(8,128)S(1)} %get-tuple-element.45.e0, f32[64,256]{1,0:T(8,128)S(1)} %collective-permute-done.e1, f32[64,256]{1,0:T(8,128)S(1)} %collective-permute-done.1.e2, ...), custom_call_target="tpu_custom_call" | custom-call | flops 2147483648 | bytes 16777216 | tf_op jit(solution)/shard_map/dense_rows/pallas_call | solution.py:154
  22.5 0.0 copy-start
  22.5 0.1 collective-permute-start.7
  22.6 1.2 %collective-permute-start.6 = (f32[4,64,256]{2,1,0:T(8,128)S(1)}, f32[4,64,256]{2,1,0:T(8,128)S(1)}, u32[]{:S(2)}, u32[]{:S(2)}) collective-permute-start(f32[4,64,256]{2,1,0:T(8,128)S(1)} %stack_right.1.refs_0_.right), channel_id=1, source_target_pairs={{0,4},{1,5},{2,6},{3,7},{4,0},{5,1},{6,2},{7,3},{8,12},{9,13},{10,... | collective-permute-start | bytes 786440 | tf_op jit(solution)/shard_map/ppermute | solution.py:436
  23.8 4.9 %dense_rows.3 = (bf16[16,1024,256]{2,1,0:T(8,128)(2,1)S(1)}, bf16[16,1024,256]{2,1,0:T(8,128)(2,1)S(1)}, f32[8,128]{1,0:T(8,128)S(1)}) custom-call(f32[64,256]{1,0:T(8,128)S(1)} %get-tuple-element.45.e0, f32[64,256]{1,0:T(8,128)S(1)} %collective-permute-done.e1, f32[64,256]{1,0:T(8,128)S(1)} %collective-permute-done.1.e2, ...), custom_call_target="tpu_custom_call" | custom-call | flops 33554432 | bytes 262144 | tf_op jit(solution)/shard_map/dense_rows/pallas_call | solution.py:154
  28.7 2.3 %forward_part.4.refs_1_ = f32[1024,128]{1,0:T(8,128)S(1)} custom-call(bf16[16,1024,256]{2,1,0:T(8,128)(2,1)S(1)} %get-tuple-element.46.hi_ref, bf16[16,1024,256]{2,1,0:T(8,128)(2,1)S(1)} %get-tuple-element.47.lo_ref, f32[4,64,256]{2,1,0:T(8,128)S(1)} %stack_right.1.refs_0_.right, f32[4,64,256]{2,1,0:T(8,128)S(1)} %collective-permute-done.7.refs_1_, ...), custom_call_target="tpu_custom_call" | custom-call | flops 67108864 | bytes 131072 | tf_op jit(solution)/shard_map/forward_part/pallas_call | solution.py:196
  31.1 0.3 collective-permute-done.6.refs_0_
  31.3 1.2 %forward_part.5.before = f32[1024,128]{1,0:T(8,128)S(1)} custom-call(bf16[16,1024,256]{2,1,0:T(8,128)(2,1)S(1)} %get-tuple-element.46.hi_ref, bf16[16,1024,256]{2,1,0:T(8,128)(2,1)S(1)} %get-tuple-element.47.lo_ref, f32[4,64,256]{2,1,0:T(8,128)S(1)} %collective-permute-done.6.refs_0_, f32[1024,128]{1,0:T(8,128)S(1)} %forward_part.4.refs_1_), custom_call_target="tpu_custom_call" | custom-call | flops 33554432 | bytes 65536 | tf_op jit(solution)/shard_map/forward_part/pallas_call | solution.py:196
  32.6 0.3 collective-permute-done.8.vec
  32.9 1.3 %product_half.2.mine = f32[64,1024]{1,0:T(8,128)S(1)} custom-call(bf16[16,1024,256]{2,1,0:T(8,128)(2,1)S(1)} %get-tuple-element.46.hi_ref, bf16[16,1024,256]{2,1,0:T(8,128)(2,1)S(1)} %get-tuple-element.47.lo_ref, f32[4,64,256]{2,1,0:T(8,128)S(1)} %collective-permute-done.8.vec, f32[1024,128]{1,0:T(8,128)S(1)} %forward_part.5.before), custom_call_target="tpu_custom_call" | custom-call | flops 33554432 | bytes 65536 | tf_op jit(solution)/shard_map/product_half/pallas_call | solution.py:228
  34.2 1.4 %collective-permute-start.10 = (f32[64,1024]{1,0:T(8,128)S(1)}, f32[64,1024]{1,0:T(8,128)S(1)}, u32[]{:S(2)}, u32[]{:S(2)}) collective-permute-start(f32[64,1024]{1,0:T(8,128)S(1)} %product_half.2.mine), channel_id=1, source_target_pairs={{0,1},{1,0},{2,3},{3,2},{4,5},{5,4},{6,7},{7,6},{8,9},{9,8},{10,11... | collective-permute-start | bytes 786440 | tf_op jit(solution)/shard_map/ppermute | solution.py:436
  35.6 2.3 %forward_part.6.refs_1_ = f32[1024,128]{1,0:T(8,128)S(1)} custom-call(bf16[16,1024,256]{2,1,0:T(8,128)(2,1)S(1)} %get-tuple-element.56.hi_ref, bf16[16,1024,256]{2,1,0:T(8,128)(2,1)S(1)} %get-tuple-element.57.lo_ref, f32[4,64,256]{2,1,0:T(8,128)S(1)} %stack_right.1.refs_0_.right, f32[4,64,256]{2,1,0:T(8,128)S(1)} %collective-permute-done.7.refs_1_), custom_call_target="tpu_custom_call" | custom-call | flops 67108864 | bytes 131072 | tf_op jit(solution)/shard_map/forward_part/pallas_call | solution.py:196
  37.9 0.0 copy-start.5
  37.9 1.2 %forward_part.7.before = f32[1024,128]{1,0:T(8,128)S(1)} custom-call(bf16[16,1024,256]{2,1,0:T(8,128)(2,1)S(1)} %get-tuple-element.56.hi_ref, bf16[16,1024,256]{2,1,0:T(8,128)(2,1)S(1)} %get-tuple-element.57.lo_ref, f32[4,64,256]{2,1,0:T(8,128)S(1)} %collective-permute-done.6.refs_0_, f32[1024,128]{1,0:T(8,128)S(1)} %forward_part.6.refs_1_), custom_call_target="tpu_custom_call" | custom-call | flops 33554432 | bytes 65536 | tf_op jit(solution)/shard_map/forward_part/pallas_call | solution.py:196
  39.2 1.3 %product_half.3.mine = f32[64,1024]{1,0:T(8,128)S(1)} custom-call(bf16[16,1024,256]{2,1,0:T(8,128)(2,1)S(1)} %get-tuple-element.56.hi_ref, bf16[16,1024,256]{2,1,0:T(8,128)(2,1)S(1)} %get-tuple-element.57.lo_ref, f32[4,64,256]{2,1,0:T(8,128)S(1)} %collective-permute-done.8.vec, f32[1024,128]{1,0:T(8,128)S(1)} %forward_part.7.before, ...), custom_call_target="tpu_custom_call" | custom-call | flops 33554432 | bytes 65536 | tf_op jit(solution)/shard_map/product_half/pallas_call | solution.py:228
  40.5 0.8 collective-permute-start.9
  41.3 1.4 %collective-permute-done.10.other = f32[64,1024]{1,0:T(8,128)S(1)} collective-permute-done((f32[64,1024]{1,0:T(8,128)S(1)}, f32[64,1024]{1,0:T(8,128)S(1)}, u32[]{:S(2)}, u32[]{:S(2)}) %collective-permute-start.10) | collective-permute-done | bytes 262176 | tf_op jit(solution)/shard_map/ppermute | solution.py:436
  42.7 0.2 left_half.2
  42.9 2.6 %collective-permute-start.18 = (f32[64,256]{1,0:T(8,128)S(1)}, f32[64,256]{1,0:T(8,128)S(1)}, u32[]{:S(2)}, u32[]{:S(2)}) collective-permute-start(f32[64,256]{1,0:T(8,128)S(1)} %get-tuple-element.71), channel_id=1, source_target_pairs={{0,8},{1,9},{2,10},{3,11},{4,12},{5,13},{6,14},{7,15},{8,0},{9,1},... | collective-permute-start | bytes 196616 | tf_op jit(solution)/shard_map/ppermute | solution.py:436
  45.4 2.2 %collective-permute-start.19 = (f32[64,256]{1,0:T(8,128)S(1)}, f32[64,256]{1,0:T(8,128)S(1)}, u32[]{:S(2)}, u32[]{:S(2)}) collective-permute-start(f32[64,256]{1,0:T(8,128)S(1)} %get-tuple-element.72), channel_id=1, source_target_pairs={{0,16},{1,17},{2,18},{3,19},{4,20},{5,21},{6,22},{7,23},{8,24},{9,... | collective-permute-start | bytes 196616 | tf_op jit(solution)/shard_map/ppermute | solution.py:436
  47.6 0.6 collective-permute-start.20
  48.2 2.3 %backward_part.5.refs_1_.refs_0_ = f32[1024,256]{1,0:T(8,128)S(1)} custom-call(bf16[16,1024,256]{2,1,0:T(8,128)(2,1)S(1)} %get-tuple-element.56.hi_ref, bf16[16,1024,256]{2,1,0:T(8,128)(2,1)S(1)} %get-tuple-element.57.lo_ref, bf16[128,1024]{1,0:T(8,128)(2,1)S(1)} %get-tuple-element.59.both_ref), custom_call_target="tpu_custom_call" | custom-call | flops 134217728 | bytes 262144 | tf_op jit(solution)/shard_map/backward_part/pallas_call | solution.py:309
  50.5 0.2 left_half.3
  50.7 0.7 backward_part.7.refs_1_.near
  51.4 0.7 backward_part.9
  52.1 0.1 collective-permute-start.12
  52.2 0.7 backward_part.8.token
  52.9 0.6 collective-permute-start.11
  53.5 0.3 collective-permute-done.20.m3
  53.8 1.4 %collective-permute-start.14 = (f32[128,256]{1,0:T(8,128)S(1)}, f32[128,256]{1,0:T(8,128)S(1)}, u32[]{:S(2)}, u32[]{:S(2)}) collective-permute-start(f32[128,256]{1,0:T(8,128)S(1)} %get-tuple-element.64), channel_id=1, source_target_pairs={{0,4},{1,5},{2,6},{3,7},{4,0},{5,1},{6,2},{7,3},{8,12},{9,13},{10,... | collective-permute-start | bytes 393224 | tf_op jit(solution)/shard_map/ppermute | solution.py:436
  55.3 0.0 copy-start.6
  55.3 0.8 collective-permute-start.13
  56.0 1.8 %collective-permute-start.21 = (f32[4,64,256]{2,1,0:T(8,128)S(1)}, f32[4,64,256]{2,1,0:T(8,128)S(1)}, u32[]{:S(2)}, u32[]{:S(2)}) collective-permute-start(f32[4,64,256]{2,1,0:T(8,128)S(1)} %stack_left.1.own), channel_id=1, source_target_pairs={{0,1},{1,0},{2,3},{3,2},{4,5},{5,4},{6,7},{7,6},{8,9},{9,8},{10,11... | collective-permute-start | bytes 786440 | tf_op jit(solution)/shard_map/ppermute | solution.py:436
  57.8 0.7 backward_part.6.keep
  58.5 1.7 %collective-permute-done.14.got = f32[128,256]{1,0:T(8,128)S(1)} collective-permute-done((f32[128,256]{1,0:T(8,128)S(1)}, f32[128,256]{1,0:T(8,128)S(1)}, u32[]{:S(2)}, u32[]{:S(2)}) %collective-permute-start.14) | collective-permute-done | bytes 131104 | tf_op jit(solution)/shard_map/ppermute | solution.py:436
  60.3 2.2 %collective-permute-start.16 = (f32[64,256]{1,0:T(8,128)S(1)}, f32[64,256]{1,0:T(8,128)S(1)}, u32[]{:S(2)}, u32[]{:S(2)}) collective-permute-start(f32[64,256]{1,0:T(8,128)S(1)} %get-tuple-element.65.g2), channel_id=1, source_target_pairs={{0,16},{1,17},{2,18},{3,19},{4,20},{5,21},{6,22},{7,23},{8,24},{9,... | collective-permute-start | bytes 196616 | tf_op jit(solution)/shard_map/ppermute | solution.py:436
  62.5 1.2 %collective-permute-start.17 = (f32[64,256]{1,0:T(8,128)S(1)}, f32[64,256]{1,0:T(8,128)S(1)}, u32[]{:S(2)}, u32[]{:S(2)}) collective-permute-start(f32[64,256]{1,0:T(8,128)S(1)} %get-tuple-element.66.g3), channel_id=1, source_target_pairs={{0,24},{1,25},{2,26},{3,27},{4,28},{5,29},{6,30},{7,31},{8,16},{9,... | collective-permute-start | bytes 196616 | tf_op jit(solution)/shard_map/ppermute | solution.py:436
  63.6 0.3 right_norm.1
  63.9 0.6 collective-permute-start.15
  64.5 12.3 %all_to_all.5.squares = f32[32,1,128]{2,1,0:T(1,128)S(1)} all-to-all(f32[32,1,128]{2,1,0:T(1,128)S(1)} %bitcast.9), channel_id=1, replica_groups=mesh['doc'=16,'feat'=2] {'doc','feat'}, dimensions={0} | all-to-all | bytes 32768 | tf_op jit(solution)/shard_map/all_to_all | solution.py:493
  76.9 1.3 %finish.1 = (f32[512,256]{1,0:T(8,128)}, f32[256,256]{1,0:T(8,128)}, f32[256,256]{1,0:T(8,128)}, f32[256,256]{1,0:T(8,128)}, f32[1,256]{1,0:T(1,128)}, /*index=5*/f32[1,256]{1,0:T(1,128)}, f32[1,256]{1,0:T(1,128)}) custom-call(f32[64,256]{1,0:T(8,128)S(1)} %get-tuple-element.67.g0, f32[64,256]{1,0:T(8,128)S(1)} %collective-permute-done.15.g1, ...), custom_call_target="tpu_custom_call" | custom-call | flops 16384 | bytes 20480 | tf_op jit(solution)/shard_map/finish/pallas_call | solution.py:425
  (35 shorter events, 0.2 us)
Async XLA Ops:
  2.3 9.5 %collective-permute-start.2 = (f32[64,256]{1,0:T(8,128)S(1)}, f32[64,256]{1,0:T(8,128)S(1)}, u32[]{:S(2)}, u32[]{:S(2)}) collective-permute-start(f32[64,256]{1,0:T(8,128)S(1)} %get-tuple-element.45.e0), channel_id=1, source_target_pairs={{0,24},{1,25},{2,26},{3,27},{4,28},{5,29},{6,30},{7,31},{8,16},{9,... | collective-permute-start | bytes 196616 | tf_op jit(solution)/shard_map/ppermute | solution.py:436
  7.4 10.3 %collective-permute-start.1 = (f32[64,256]{1,0:T(8,128)S(1)}, f32[64,256]{1,0:T(8,128)S(1)}, u32[]{:S(2)}, u32[]{:S(2)}) collective-permute-start(f32[64,256]{1,0:T(8,128)S(1)} %get-tuple-element.45.e0), channel_id=1, source_target_pairs={{0,16},{1,17},{2,18},{3,19},{4,20},{5,21},{6,22},{7,23},{8,24},{9,... | collective-permute-start | bytes 196616 | tf_op jit(solution)/shard_map/ppermute | solution.py:436
  7.4 10.3 %collective-permute-start = (f32[64,256]{1,0:T(8,128)S(1)}, f32[64,256]{1,0:T(8,128)S(1)}, u32[]{:S(2)}, u32[]{:S(2)}) collective-permute-start(f32[64,256]{1,0:T(8,128)S(1)} %get-tuple-element.45.e0), channel_id=1, source_target_pairs={{0,8},{1,9},{2,10},{3,11},{4,12},{5,13},{6,14},{7,15},{8,0},{9,1},... | collective-permute-start | bytes 196616 | tf_op jit(solution)/shard_map/ppermute | solution.py:436
  8.1 14.4 %collective-permute-start.4 = (f32[128,256]{1,0:T(8,128)S(1)}, f32[128,256]{1,0:T(8,128)S(1)}, u32[]{:S(2)}, u32[]{:S(2)}) collective-permute-start(f32[128,256]{1,0:T(8,128)S(1)} %get-tuple-element.51), channel_id=1, source_target_pairs={{0,16},{1,17},{2,18},{3,19},{4,20},{5,21},{6,22},{7,23},{8,24},{9,... | collective-permute-start | bytes 393224 | tf_op jit(solution)/shard_map/ppermute | solution.py:436
  10.3 12.1 %collective-permute-start.5 = (f32[128,256]{1,0:T(8,128)S(1)}, f32[128,256]{1,0:T(8,128)S(1)}, u32[]{:S(2)}, u32[]{:S(2)}) collective-permute-start(f32[128,256]{1,0:T(8,128)S(1)} %get-tuple-element.52), channel_id=1, source_target_pairs={{0,24},{1,25},{2,26},{3,27},{4,28},{5,29},{6,30},{7,31},{8,16},{9,... | collective-permute-start | bytes 393224 | tf_op jit(solution)/shard_map/ppermute | solution.py:436
  11.8 10.7 %collective-permute-start.3 = (f32[128,256]{1,0:T(8,128)S(1)}, f32[128,256]{1,0:T(8,128)S(1)}, u32[]{:S(2)}, u32[]{:S(2)}) collective-permute-start(f32[128,256]{1,0:T(8,128)S(1)} %get-tuple-element.50), channel_id=1, source_target_pairs={{0,8},{1,9},{2,10},{3,11},{4,12},{5,13},{6,14},{7,15},{8,0},{9,1},... | collective-permute-start | bytes 393224 | tf_op jit(solution)/shard_map/ppermute | solution.py:436
  22.5 13.0 %copy-start = (f32[4,64,256]{2,1,0:T(8,128)}, f32[4,64,256]{2,1,0:T(8,128)S(1)}, u32[]{:S(2)}) copy-start(f32[4,64,256]{2,1,0:T(8,128)S(1)} %stack_right.1.refs_0_.right) | copy-start | bytes 786436
  22.5 6.2 %collective-permute-start.7 = (f32[4,64,256]{2,1,0:T(8,128)S(1)}, f32[4,64,256]{2,1,0:T(8,128)S(1)}, u32[]{:S(2)}, u32[]{:S(2)}) collective-permute-start(f32[4,64,256]{2,1,0:T(8,128)S(1)} %stack_right.1.refs_0_.right), channel_id=1, source_target_pairs={{0,2},{1,3},{2,0},{3,1},{4,6},{5,7},{6,4},{7,5},{8,10},{9,11},{10,... | collective-permute-start | bytes 786440 | tf_op jit(solution)/shard_map/ppermute | solution.py:436
  22.6 8.7 %collective-permute-start.6 = (f32[4,64,256]{2,1,0:T(8,128)S(1)}, f32[4,64,256]{2,1,0:T(8,128)S(1)}, u32[]{:S(2)}, u32[]{:S(2)}) collective-permute-start(f32[4,64,256]{2,1,0:T(8,128)S(1)} %stack_right.1.refs_0_.right), channel_id=1, source_target_pairs={{0,4},{1,5},{2,6},{3,7},{4,0},{5,1},{6,2},{7,3},{8,12},{9,13},{10,... | collective-permute-start | bytes 786440 | tf_op jit(solution)/shard_map/ppermute | solution.py:436
  31.3 1.5 %collective-permute-start.8 = (f32[4,64,256]{2,1,0:T(8,128)S(1)}, f32[4,64,256]{2,1,0:T(8,128)S(1)}, u32[]{:S(2)}, u32[]{:S(2)}) collective-permute-start(f32[4,64,256]{2,1,0:T(8,128)S(1)} %collective-permute-done.6.refs_0_), channel_id=1, source_target_pairs={{0,2},{1,3},{2,0},{3,1},{4,6},{5,7},{6,4},{7,5},{8,10},{9,11},{10,... | collective-permute-start | bytes 786440 | tf_op jit(solution)/shard_map/ppermute | solution.py:436
  34.2 8.5 %collective-permute-start.10 = (f32[64,1024]{1,0:T(8,128)S(1)}, f32[64,1024]{1,0:T(8,128)S(1)}, u32[]{:S(2)}, u32[]{:S(2)}) collective-permute-start(f32[64,1024]{1,0:T(8,128)S(1)} %product_half.2.mine), channel_id=1, source_target_pairs={{0,1},{1,0},{2,3},{3,2},{4,5},{5,4},{6,7},{7,6},{8,9},{9,8},{10,11... | collective-permute-start | bytes 786440 | tf_op jit(solution)/shard_map/ppermute | solution.py:436
  37.9 1.3 %copy-start.5 = (f32[256]{0:T(256)S(1)}, f32[256]{0:T(256)}, u32[]{:S(2)}) copy-start(f32[256]{0:T(256)} %param.15) | copy-start | bytes 3076
  40.5 10.0 %collective-permute-start.9 = (f32[64,1024]{1,0:T(8,128)S(1)}, f32[64,1024]{1,0:T(8,128)S(1)}, u32[]{:S(2)}, u32[]{:S(2)}) collective-permute-start(f32[64,1024]{1,0:T(8,128)S(1)} %product_half.3.mine), channel_id=1, source_target_pairs={{0,1},{1,0},{2,3},{3,2},{4,5},{5,4},{6,7},{7,6},{8,9},{9,8},{10,11... | collective-permute-start | bytes 786440 | tf_op jit(solution)/shard_map/ppermute | solution.py:436
  42.9 10.7 %collective-permute-start.18 = (f32[64,256]{1,0:T(8,128)S(1)}, f32[64,256]{1,0:T(8,128)S(1)}, u32[]{:S(2)}, u32[]{:S(2)}) collective-permute-start(f32[64,256]{1,0:T(8,128)S(1)} %get-tuple-element.71), channel_id=1, source_target_pairs={{0,8},{1,9},{2,10},{3,11},{4,12},{5,13},{6,14},{7,15},{8,0},{9,1},... | collective-permute-start | bytes 196616 | tf_op jit(solution)/shard_map/ppermute | solution.py:436
  45.4 8.1 %collective-permute-start.19 = (f32[64,256]{1,0:T(8,128)S(1)}, f32[64,256]{1,0:T(8,128)S(1)}, u32[]{:S(2)}, u32[]{:S(2)}) collective-permute-start(f32[64,256]{1,0:T(8,128)S(1)} %get-tuple-element.72), channel_id=1, source_target_pairs={{0,16},{1,17},{2,18},{3,19},{4,20},{5,21},{6,22},{7,23},{8,24},{9,... | collective-permute-start | bytes 196616 | tf_op jit(solution)/shard_map/ppermute | solution.py:436
  47.6 6.2 %collective-permute-start.20 = (f32[64,256]{1,0:T(8,128)S(1)}, f32[64,256]{1,0:T(8,128)S(1)}, u32[]{:S(2)}, u32[]{:S(2)}) collective-permute-start(f32[64,256]{1,0:T(8,128)S(1)} %get-tuple-element.73), channel_id=1, source_target_pairs={{0,24},{1,25},{2,26},{3,27},{4,28},{5,29},{6,30},{7,31},{8,16},{9,... | collective-permute-start | bytes 196616 | tf_op jit(solution)/shard_map/ppermute | solution.py:436
  52.1 1.7 %collective-permute-start.12 = (f32[264,256]{1,0:T(8,128)S(1)}, f32[264,256]{1,0:T(8,128)S(1)}, u32[]{:S(2)}, u32[]{:S(2)}) collective-permute-start(f32[264,256]{1,0:T(8,128)S(1)} %backward_part.9), channel_id=1, source_target_pairs={{0,2},{1,3},{2,0},{3,1},{4,6},{5,7},{6,4},{7,5},{8,10},{9,11},{10,... | collective-permute-start | bytes 811016 | tf_op jit(solution)/shard_map/ppermute | solution.py:436
  52.9 5.6 %collective-permute-start.11 = (f32[256,256]{1,0:T(8,128)S(1)}, f32[256,256]{1,0:T(8,128)S(1)}, u32[]{:S(2)}, u32[]{:S(2)}) collective-permute-start(f32[256,256]{1,0:T(8,128)S(1)} %backward_part.8.token), channel_id=1, source_target_pairs={{0,2},{1,3},{2,0},{3,1},{4,6},{5,7},{6,4},{7,5},{8,10},{9,11},{10,... | collective-permute-start | bytes 786440 | tf_op jit(solution)/shard_map/ppermute | solution.py:436
  53.8 6.4 %collective-permute-start.14 = (f32[128,256]{1,0:T(8,128)S(1)}, f32[128,256]{1,0:T(8,128)S(1)}, u32[]{:S(2)}, u32[]{:S(2)}) collective-permute-start(f32[128,256]{1,0:T(8,128)S(1)} %get-tuple-element.64), channel_id=1, source_target_pairs={{0,4},{1,5},{2,6},{3,7},{4,0},{5,1},{6,2},{7,3},{8,12},{9,13},{10,... | collective-permute-start | bytes 393224 | tf_op jit(solution)/shard_map/ppermute | solution.py:436
  55.2 8.4 %copy-start.1 = (f32[4,64,256]{2,1,0:T(8,128)S(1)}, f32[4,64,256]{2,1,0:T(8,128)}, u32[]{:S(2)}) copy-start(f32[4,64,256]{2,1,0:T(8,128)} %copy-done) | copy-start | bytes 786436
  55.2 21.6 %copy-start.2 = (f32[256,256]{1,0:T(8,128)S(1)}, f32[256,256]{1,0:T(8,128)}, u32[]{:S(2)}) copy-start(f32[256,256]{1,0:T(8,128)} %right.1) | copy-start | bytes 786436
  55.2 21.6 %copy-start.3 = (f32[256,256]{1,0:T(8,128)S(1)}, f32[256,256]{1,0:T(8,128)}, u32[]{:S(2)}) copy-start(f32[256,256]{1,0:T(8,128)} %search.1) | copy-start | bytes 786436
  55.2 21.6 %copy-start.4 = (f32[256,256]{1,0:T(8,128)S(1)}, f32[256,256]{1,0:T(8,128)}, u32[]{:S(2)}) copy-start(f32[256,256]{1,0:T(8,128)} %solution.1) | copy-start | bytes 786436
  55.3 21.6 %copy-start.6 = (f32[256]{0:T(256)S(1)}, f32[256]{0:T(256)}, u32[]{:S(2)}) copy-start(f32[256]{0:T(256)} %param.16) | copy-start | bytes 3076
  55.3 21.6 %copy-start.7 = (f32[256]{0:T(256)S(1)}, f32[256]{0:T(256)}, u32[]{:S(2)}) copy-start(f32[256]{0:T(256)} %param.17) | copy-start | bytes 3076
  55.3 8.3 %collective-permute-start.13 = (f32[136,256]{1,0:T(8,128)S(1)}, f32[136,256]{1,0:T(8,128)S(1)}, u32[]{:S(2)}, u32[]{:S(2)}) collective-permute-start(f32[136,256]{1,0:T(8,128)S(1)} %get-tuple-element.62), channel_id=1, source_target_pairs={{0,4},{1,5},{2,6},{3,7},{4,0},{5,1},{6,2},{7,3},{8,12},{9,13},{10,... | collective-permute-start | bytes 417800 | tf_op jit(solution)/shard_map/ppermute | solution.py:436
  56.0 20.8 %collective-permute-start.21 = (f32[4,64,256]{2,1,0:T(8,128)S(1)}, f32[4,64,256]{2,1,0:T(8,128)S(1)}, u32[]{:S(2)}, u32[]{:S(2)}) collective-permute-start(f32[4,64,256]{2,1,0:T(8,128)S(1)} %stack_left.1.own), channel_id=1, source_target_pairs={{0,1},{1,0},{2,3},{3,2},{4,5},{5,4},{6,7},{7,6},{8,9},{9,8},{10,11... | collective-permute-start | bytes 786440 | tf_op jit(solution)/shard_map/ppermute | solution.py:436
  60.3 16.5 %collective-permute-start.16 = (f32[64,256]{1,0:T(8,128)S(1)}, f32[64,256]{1,0:T(8,128)S(1)}, u32[]{:S(2)}, u32[]{:S(2)}) collective-permute-start(f32[64,256]{1,0:T(8,128)S(1)} %get-tuple-element.65.g2), channel_id=1, source_target_pairs={{0,16},{1,17},{2,18},{3,19},{4,20},{5,21},{6,22},{7,23},{8,24},{9,... | collective-permute-start | bytes 196616 | tf_op jit(solution)/shard_map/ppermute | solution.py:436
  62.5 14.4 %collective-permute-start.17 = (f32[64,256]{1,0:T(8,128)S(1)}, f32[64,256]{1,0:T(8,128)S(1)}, u32[]{:S(2)}, u32[]{:S(2)}) collective-permute-start(f32[64,256]{1,0:T(8,128)S(1)} %get-tuple-element.66.g3), channel_id=1, source_target_pairs={{0,24},{1,25},{2,26},{3,27},{4,28},{5,29},{6,30},{7,31},{8,16},{9,... | collective-permute-start | bytes 196616 | tf_op jit(solution)/shard_map/ppermute | solution.py:436
  63.9 12.9 %collective-permute-start.15 = (f32[64,256]{1,0:T(8,128)S(1)}, f32[64,256]{1,0:T(8,128)S(1)}, u32[]{:S(2)}, u32[]{:S(2)}) collective-permute-start(f32[64,256]{1,0:T(8,128)S(1)} %get-tuple-element.68), channel_id=1, source_target_pairs={{0,8},{1,9},{2,10},{3,11},{4,12},{5,13},{6,14},{7,15},{8,0},{9,1},... | collective-permute-start | bytes 196616 | tf_op jit(solution)/shard_map/ppermute | solution.py:436

commit v24 on v23

--- a/solution.py
+++ b/solution.py
@@ -115,6 +115,7 @@
     d, _, y = coords()
     n = e0.shape[0] // 2
     iota = lax.broadcasted_iota(jnp.int32, (256, 256), 0).astype(jnp.float32).astype(jnp.bfloat16)
+    lanes = lax.broadcasted_iota(jnp.int32, (256, 256), 1).astype(jnp.float32)
     lane_doc = lax.broadcasted_iota(jnp.int32, (8, 256), 1) >> 4
     one = jnp.ones((256, 256), jnp.bfloat16)
     zero = jnp.zeros((256, 256), jnp.bfloat16)
@@ -134,10 +135,11 @@
             block = ((owner & 1) << 3) | ((owner & 2) << 1) | (owner >> 2)
             code = (block * 16 + lane_doc).astype(jnp.float32)
             inner = (ids & 255).astype(jnp.float32)
+            columns = jnp.concatenate([inner, vals] * 8, axis=0).T
             for t in range(8):
                 pick = jnp.where(iota == spread(code[t : t + 1]), one, zero)
-                weigh = jnp.where(iota == spread(inner[t : t + 1]), spread(vals[t : t + 1]), zero)
-                dense = lax.dot_general(pick, weigh, NT, preferred_element_type=jnp.float32)
+                weigh = jnp.where(lanes == columns[:, t : t + 1], columns[:, 8 + t : 9 + t], 0.0).astype(jnp.bfloat16)
+                dense = jnp.dot(pick, weigh, preferred_element_type=jnp.float32)
                 high = dense.astype(jnp.bfloat16)
                 low = (dense - high.astype(jnp.float32)).astype(jnp.bfloat16)
                 docs = pl.ds(pl.multiple_of(k * 8 * n + step * 128 + 16 * t, 16), 16)

time: 78.4 us -> 83 us (1.059)
  Pallas kernels: 28.3 us -> 33.6 us
    pallas_call x2, Pallas kernels: 9.62 us -> 15 us  [build(): pl.pallas_call(functools.partial(build_kernel, rel), in_specs=[whole()] *...]
  transfers between devices with their start and end apart: 22 -> 22, of which waited for: 6 -> 5; matrix products, arithmetic and copies ran while one was open for 0% -> 0% of each run, Pallas kernels for 31% -> 35%
where the time goes in v24:
time: 83 us; the launch traced here: 82.8 us
  Pallas kernels  33.6 us (40%)
  starting transfers between devices  27.5 us (33%)
  blocking collectives  11.6 us (14%)
  waiting for transfers between devices  9.14 us (11%)
  between operations  0.96 us (1%)
    ppermute x22, starting transfers between devices, swap(): return lax.ppermute(value, AXES, [(i, i ^ mask) for i in range(32)])  27.5 us
    pallas_call x2, Pallas kernels, build(): pl.pallas_call(functools.partial(build_kernel, rel), in_specs=[whole()] *...  15 us
    all_to_all x1, blocking collectives, by_columns(): squares = lax.all_to_all(after(sums, left_own), AXES, 0, 0, tiled=True)  11.6 us
    ppermute x22, waiting for transfers between devices, swap(): return lax.ppermute(value, AXES, [(i, i ^ mask) for i in range(32)])  9.14 us
    pallas_call x4, Pallas kernels, forward_part(): pl.pallas_call(functools.partial(forward_kernel, blocks, before is not No...  7.12 us
    pallas_call x5, Pallas kernels, backward_part(): pl.pallas_call(functools.partial(backward_kernel, first, blocks, tuple(ex...  5.19 us
    pallas_call x2, Pallas kernels, product_half(): pl.pallas_call(functools.partial(product_kernel, blocks), in_specs=[whole...  2.64 us
  transfers between devices with their start and end apart: 22, of which 5 were waited for; matrix products, arithmetic and copies ran while one was open for 0% of the time, Pallas kernels for 35%

profile of v24, /device:TPU:0, one launch (start us, length us, event | category | flops | bytes accessed | tf_op | source)
XLA Modules:
  0.0 82.8 jit_solution(12292907110778681756)
XLA Ops:
  0.6 1.6 %prepare.1 = (f32[64,256]{1,0:T(8,128)S(1)}, f32[128,256]{1,0:T(8,128)S(1)}, f32[128,256]{1,0:T(8,128)S(1)}, f32[128,256]{1,0:T(8,128)S(1)}, f32[128,256]{1,0:T(8,128)S(1)}) custom-call(s32[16,512]{1,0:T(8,128)} %bitcast.13, bf16[16,512]{1,0:T(8,128)(2,1)} %bitcast.14, f32[256,256]{1,0:T(8,128)} %right.1, f32[512,256]{1,0:T(8,128)} %left_hbm.1), custom_call_target="tpu_custom_call" | custom-call | bytes 16384 | tf_op jit(solution)/shard_map/prepare/pallas_call | solution.py:74
  2.3 5.1 %collective-permute-start.2 = (f32[64,256]{1,0:T(8,128)S(1)}, f32[64,256]{1,0:T(8,128)S(1)}, u32[]{:S(2)}, u32[]{:S(2)}) collective-permute-start(f32[64,256]{1,0:T(8,128)S(1)} %get-tuple-element.45.e0), channel_id=1, source_target_pairs={{0,24},{1,25},{2,26},{3,27},{4,28},{5,29},{6,30},{7,31},{8,16},{9,... | collective-permute-start | bytes 196616 | tf_op jit(solution)/shard_map/ppermute | solution.py:438
  7.4 0.6 collective-permute-start
  8.1 2.3 %collective-permute-start.4 = (f32[128,256]{1,0:T(8,128)S(1)}, f32[128,256]{1,0:T(8,128)S(1)}, u32[]{:S(2)}, u32[]{:S(2)}) collective-permute-start(f32[128,256]{1,0:T(8,128)S(1)} %get-tuple-element.51), channel_id=1, source_target_pairs={{0,16},{1,17},{2,18},{3,19},{4,20},{5,21},{6,22},{7,23},{8,24},{9,... | collective-permute-start | bytes 393224 | tf_op jit(solution)/shard_map/ppermute | solution.py:438
  10.3 1.5 %collective-permute-start.5 = (f32[128,256]{1,0:T(8,128)S(1)}, f32[128,256]{1,0:T(8,128)S(1)}, u32[]{:S(2)}, u32[]{:S(2)}) collective-permute-start(f32[128,256]{1,0:T(8,128)S(1)} %get-tuple-element.52), channel_id=1, source_target_pairs={{0,24},{1,25},{2,26},{3,27},{4,28},{5,29},{6,30},{7,31},{8,16},{9,... | collective-permute-start | bytes 393224 | tf_op jit(solution)/shard_map/ppermute | solution.py:438
  11.8 0.8 collective-permute-start.3
  12.6 5.1 %collective-permute-done.1.e2 = f32[64,256]{1,0:T(8,128)S(1)} collective-permute-done((f32[64,256]{1,0:T(8,128)S(1)}, f32[64,256]{1,0:T(8,128)S(1)}, u32[]{:S(2)}, u32[]{:S(2)}) %collective-permute-start.1) | collective-permute-done | bytes 65568 | tf_op jit(solution)/shard_map/ppermute | solution.py:438
  17.7 7.4 %dense_rows.2 = (bf16[16,1024,256]{2,1,0:T(8,128)(2,1)S(1)}, bf16[16,1024,256]{2,1,0:T(8,128)(2,1)S(1)}, f32[8,128]{1,0:T(8,128)S(1)}) custom-call(f32[64,256]{1,0:T(8,128)S(1)} %get-tuple-element.45.e0, f32[64,256]{1,0:T(8,128)S(1)} %collective-permute-done.e1, f32[64,256]{1,0:T(8,128)S(1)} %collective-permute-done.1.e2, ...), custom_call_target="tpu_custom_call" | custom-call | flops 2147483648 | bytes 16777216 | tf_op jit(solution)/shard_map/dense_rows/pallas_call | solution.py:156
  25.2 0.0 copy-start
  25.2 0.1 collective-permute-start.7
  25.3 1.2 %collective-permute-start.6 = (f32[4,64,256]{2,1,0:T(8,128)S(1)}, f32[4,64,256]{2,1,0:T(8,128)S(1)}, u32[]{:S(2)}, u32[]{:S(2)}) collective-permute-start(f32[4,64,256]{2,1,0:T(8,128)S(1)} %stack_right.1.refs_0_.right), channel_id=1, source_target_pairs={{0,4},{1,5},{2,6},{3,7},{4,0},{5,1},{6,2},{7,3},{8,12},{9,13},{10,... | collective-permute-start | bytes 786440 | tf_op jit(solution)/shard_map/ppermute | solution.py:438
  26.5 7.6 %dense_rows.3 = (bf16[16,1024,256]{2,1,0:T(8,128)(2,1)S(1)}, bf16[16,1024,256]{2,1,0:T(8,128)(2,1)S(1)}, f32[8,128]{1,0:T(8,128)S(1)}) custom-call(f32[64,256]{1,0:T(8,128)S(1)} %get-tuple-element.45.e0, f32[64,256]{1,0:T(8,128)S(1)} %collective-permute-done.e1, f32[64,256]{1,0:T(8,128)S(1)} %collective-permute-done.1.e2, ...), custom_call_target="tpu_custom_call" | custom-call | flops 33554432 | bytes 262144 | tf_op jit(solution)/shard_map/dense_rows/pallas_call | solution.py:156
  34.1 2.3 %forward_part.4.refs_1_ = f32[1024,128]{1,0:T(8,128)S(1)} custom-call(bf16[16,1024,256]{2,1,0:T(8,128)(2,1)S(1)} %get-tuple-element.46.hi_ref, bf16[16,1024,256]{2,1,0:T(8,128)(2,1)S(1)} %get-tuple-element.47.lo_ref, f32[4,64,256]{2,1,0:T(8,128)S(1)} %stack_right.1.refs_0_.right, f32[4,64,256]{2,1,0:T(8,128)S(1)} %collective-permute-done.7.refs_1_, ...), custom_call_target="tpu_custom_call" | custom-call | flops 67108864 | bytes 131072 | tf_op jit(solution)/shard_map/forward_part/pallas_call | solution.py:198
  36.4 0.2 collective-permute-start.8
  36.6 1.2 %forward_part.5.before = f32[1024,128]{1,0:T(8,128)S(1)} custom-call(bf16[16,1024,256]{2,1,0:T(8,128)(2,1)S(1)} %get-tuple-element.46.hi_ref, bf16[16,1024,256]{2,1,0:T(8,128)(2,1)S(1)} %get-tuple-element.47.lo_ref, f32[4,64,256]{2,1,0:T(8,128)S(1)} %collective-permute-done.6.refs_0_, f32[1024,128]{1,0:T(8,128)S(1)} %forward_part.4.refs_1_), custom_call_target="tpu_custom_call" | custom-call | flops 33554432 | bytes 65536 | tf_op jit(solution)/shard_map/forward_part/pallas_call | solution.py:198
  37.9 0.1 collective-permute-done.8.vec
  38.0 1.3 %product_half.2.mine = f32[64,1024]{1,0:T(8,128)S(1)} custom-call(bf16[16,1024,256]{2,1,0:T(8,128)(2,1)S(1)} %get-tuple-element.46.hi_ref, bf16[16,1024,256]{2,1,0:T(8,128)(2,1)S(1)} %get-tuple-element.47.lo_ref, f32[4,64,256]{2,1,0:T(8,128)S(1)} %collective-permute-done.8.vec, f32[1024,128]{1,0:T(8,128)S(1)} %forward_part.5.before), custom_call_target="tpu_custom_call" | custom-call | flops 33554432 | bytes 65536 | tf_op jit(solution)/shard_map/product_half/pallas_call | solution.py:230
  39.3 1.6 %collective-permute-start.10 = (f32[64,1024]{1,0:T(8,128)S(1)}, f32[64,1024]{1,0:T(8,128)S(1)}, u32[]{:S(2)}, u32[]{:S(2)}) collective-permute-start(f32[64,1024]{1,0:T(8,128)S(1)} %product_half.2.mine), channel_id=1, source_target_pairs={{0,1},{1,0},{2,3},{3,2},{4,5},{5,4},{6,7},{7,6},{8,9},{9,8},{10,11... | collective-permute-start | bytes 786440 | tf_op jit(solution)/shard_map/ppermute | solution.py:438
  40.9 2.3 %forward_part.6.refs_1_ = f32[1024,128]{1,0:T(8,128)S(1)} custom-call(bf16[16,1024,256]{2,1,0:T(8,128)(2,1)S(1)} %get-tuple-element.56.hi_ref, bf16[16,1024,256]{2,1,0:T(8,128)(2,1)S(1)} %get-tuple-element.57.lo_ref, f32[4,64,256]{2,1,0:T(8,128)S(1)} %stack_right.1.refs_0_.right, f32[4,64,256]{2,1,0:T(8,128)S(1)} %collective-permute-done.7.refs_1_), custom_call_target="tpu_custom_call" | custom-call | flops 67108864 | bytes 131072 | tf_op jit(solution)/shard_map/forward_part/pallas_call | solution.py:198
  43.2 0.0 copy-start.5
  43.3 1.2 %forward_part.7.before = f32[1024,128]{1,0:T(8,128)S(1)} custom-call(bf16[16,1024,256]{2,1,0:T(8,128)(2,1)S(1)} %get-tuple-element.56.hi_ref, bf16[16,1024,256]{2,1,0:T(8,128)(2,1)S(1)} %get-tuple-element.57.lo_ref, f32[4,64,256]{2,1,0:T(8,128)S(1)} %collective-permute-done.6.refs_0_, f32[1024,128]{1,0:T(8,128)S(1)} %forward_part.6.refs_1_), custom_call_target="tpu_custom_call" | custom-call | flops 33554432 | bytes 65536 | tf_op jit(solution)/shard_map/forward_part/pallas_call | solution.py:198
  44.5 1.3 %product_half.3.mine = f32[64,1024]{1,0:T(8,128)S(1)} custom-call(bf16[16,1024,256]{2,1,0:T(8,128)(2,1)S(1)} %get-tuple-element.56.hi_ref, bf16[16,1024,256]{2,1,0:T(8,128)(2,1)S(1)} %get-tuple-element.57.lo_ref, f32[4,64,256]{2,1,0:T(8,128)S(1)} %collective-permute-done.8.vec, f32[1024,128]{1,0:T(8,128)S(1)} %forward_part.7.before, ...), custom_call_target="tpu_custom_call" | custom-call | flops 33554432 | bytes 65536 | tf_op jit(solution)/shard_map/product_half/pallas_call | solution.py:230
  45.8 0.6 collective-permute-start.9
  46.4 1.4 %collective-permute-done.10.other = f32[64,1024]{1,0:T(8,128)S(1)} collective-permute-done((f32[64,1024]{1,0:T(8,128)S(1)}, f32[64,1024]{1,0:T(8,128)S(1)}, u32[]{:S(2)}, u32[]{:S(2)}) %collective-permute-start.10) | collective-permute-done | bytes 262176 | tf_op jit(solution)/shard_map/ppermute | solution.py:438
  47.8 0.2 left_half.2
  48.0 1.0 %collective-permute-start.18 = (f32[64,256]{1,0:T(8,128)S(1)}, f32[64,256]{1,0:T(8,128)S(1)}, u32[]{:S(2)}, u32[]{:S(2)}) collective-permute-start(f32[64,256]{1,0:T(8,128)S(1)} %get-tuple-element.71), channel_id=1, source_target_pairs={{0,8},{1,9},{2,10},{3,11},{4,12},{5,13},{6,14},{7,15},{8,0},{9,1},... | collective-permute-start | bytes 196616 | tf_op jit(solution)/shard_map/ppermute | solution.py:438
  49.0 3.9 %collective-permute-start.19 = (f32[64,256]{1,0:T(8,128)S(1)}, f32[64,256]{1,0:T(8,128)S(1)}, u32[]{:S(2)}, u32[]{:S(2)}) collective-permute-start(f32[64,256]{1,0:T(8,128)S(1)} %get-tuple-element.72), channel_id=1, source_target_pairs={{0,16},{1,17},{2,18},{3,19},{4,20},{5,21},{6,22},{7,23},{8,24},{9,... | collective-permute-start | bytes 196616 | tf_op jit(solution)/shard_map/ppermute | solution.py:438
  53.0 2.3 %backward_part.5.refs_1_.refs_0_ = f32[1024,256]{1,0:T(8,128)S(1)} custom-call(bf16[16,1024,256]{2,1,0:T(8,128)(2,1)S(1)} %get-tuple-element.56.hi_ref, bf16[16,1024,256]{2,1,0:T(8,128)(2,1)S(1)} %get-tuple-element.57.lo_ref, bf16[128,1024]{1,0:T(8,128)(2,1)S(1)} %get-tuple-element.59.both_ref), custom_call_target="tpu_custom_call" | custom-call | flops 134217728 | bytes 262144 | tf_op jit(solution)/shard_map/backward_part/pallas_call | solution.py:311
  55.3 0.2 left_half.3
  55.5 0.7 backward_part.7.refs_1_.near
  56.2 0.7 backward_part.9
  56.9 0.1 collective-permute-start.12
  57.0 0.7 backward_part.8.token
  57.7 0.6 collective-permute-start.11
  58.3 0.7 collective-permute-done.20.m3
  59.1 0.6 collective-permute-start.14
  59.7 0.0 copy-start.6
  59.7 0.0 copy-start.7
  59.7 1.6 %collective-permute-start.13 = (f32[136,256]{1,0:T(8,128)S(1)}, f32[136,256]{1,0:T(8,128)S(1)}, u32[]{:S(2)}, u32[]{:S(2)}) collective-permute-start(f32[136,256]{1,0:T(8,128)S(1)} %get-tuple-element.62), channel_id=1, source_target_pairs={{0,4},{1,5},{2,6},{3,7},{4,0},{5,1},{6,2},{7,3},{8,12},{9,13},{10,... | collective-permute-start | bytes 417800 | tf_op jit(solution)/shard_map/ppermute | solution.py:438
  61.3 1.8 %collective-permute-start.21 = (f32[4,64,256]{2,1,0:T(8,128)S(1)}, f32[4,64,256]{2,1,0:T(8,128)S(1)}, u32[]{:S(2)}, u32[]{:S(2)}) collective-permute-start(f32[4,64,256]{2,1,0:T(8,128)S(1)} %stack_left.1.own), channel_id=1, source_target_pairs={{0,1},{1,0},{2,3},{3,2},{4,5},{5,4},{6,7},{7,6},{8,9},{9,8},{10,11... | collective-permute-start | bytes 786440 | tf_op jit(solution)/shard_map/ppermute | solution.py:438
  63.1 0.7 backward_part.6.keep
  63.9 1.7 %collective-permute-done.14.got = f32[128,256]{1,0:T(8,128)S(1)} collective-permute-done((f32[128,256]{1,0:T(8,128)S(1)}, f32[128,256]{1,0:T(8,128)S(1)}, u32[]{:S(2)}, u32[]{:S(2)}) %collective-permute-start.14) | collective-permute-done | bytes 131104 | tf_op jit(solution)/shard_map/ppermute | solution.py:438
  65.6 1.1 %collective-permute-start.16 = (f32[64,256]{1,0:T(8,128)S(1)}, f32[64,256]{1,0:T(8,128)S(1)}, u32[]{:S(2)}, u32[]{:S(2)}) collective-permute-start(f32[64,256]{1,0:T(8,128)S(1)} %get-tuple-element.65.g2), channel_id=1, source_target_pairs={{0,16},{1,17},{2,18},{3,19},{4,20},{5,21},{6,22},{7,23},{8,24},{9,... | collective-permute-start | bytes 196616 | tf_op jit(solution)/shard_map/ppermute | solution.py:438
  66.7 2.3 %collective-permute-start.17 = (f32[64,256]{1,0:T(8,128)S(1)}, f32[64,256]{1,0:T(8,128)S(1)}, u32[]{:S(2)}, u32[]{:S(2)}) collective-permute-start(f32[64,256]{1,0:T(8,128)S(1)} %get-tuple-element.66.g3), channel_id=1, source_target_pairs={{0,24},{1,25},{2,26},{3,27},{4,28},{5,29},{6,30},{7,31},{8,16},{9,... | collective-permute-start | bytes 196616 | tf_op jit(solution)/shard_map/ppermute | solution.py:438
  69.0 0.3 right_norm.1
  69.3 0.6 collective-permute-start.15
  69.9 11.6 %all_to_all.5.squares = f32[32,1,128]{2,1,0:T(1,128)S(1)} all-to-all(f32[32,1,128]{2,1,0:T(1,128)S(1)} %bitcast.9), channel_id=1, replica_groups=mesh['doc'=16,'feat'=2] {'doc','feat'}, dimensions={0} | all-to-all | bytes 32768 | tf_op jit(solution)/shard_map/all_to_all | solution.py:495
  81.5 1.3 %finish.1 = (f32[512,256]{1,0:T(8,128)}, f32[256,256]{1,0:T(8,128)}, f32[256,256]{1,0:T(8,128)}, f32[256,256]{1,0:T(8,128)}, f32[1,256]{1,0:T(1,128)}, /*index=5*/f32[1,256]{1,0:T(1,128)}, f32[1,256]{1,0:T(1,128)}) custom-call(f32[64,256]{1,0:T(8,128)S(1)} %get-tuple-element.67.g0, f32[64,256]{1,0:T(8,128)S(1)} %collective-permute-done.15.g1, ...), custom_call_target="tpu_custom_call" | custom-call | flops 16384 | bytes 20480 | tf_op jit(solution)/shard_map/finish/pallas_call | solution.py:427
  (35 shorter events, 0.2 us)
Async XLA Ops:
  2.3 9.5 %collective-permute-start.2 = (f32[64,256]{1,0:T(8,128)S(1)}, f32[64,256]{1,0:T(8,128)S(1)}, u32[]{:S(2)}, u32[]{:S(2)}) collective-permute-start(f32[64,256]{1,0:T(8,128)S(1)} %get-tuple-element.45.e0), channel_id=1, source_target_pairs={{0,24},{1,25},{2,26},{3,27},{4,28},{5,29},{6,30},{7,31},{8,16},{9,... | collective-permute-start | bytes 196616 | tf_op jit(solution)/shard_map/ppermute | solution.py:438
  7.4 10.3 %collective-permute-start.1 = (f32[64,256]{1,0:T(8,128)S(1)}, f32[64,256]{1,0:T(8,128)S(1)}, u32[]{:S(2)}, u32[]{:S(2)}) collective-permute-start(f32[64,256]{1,0:T(8,128)S(1)} %get-tuple-element.45.e0), channel_id=1, source_target_pairs={{0,16},{1,17},{2,18},{3,19},{4,20},{5,21},{6,22},{7,23},{8,24},{9,... | collective-permute-start | bytes 196616 | tf_op jit(solution)/shard_map/ppermute | solution.py:438
  7.4 10.3 %collective-permute-start = (f32[64,256]{1,0:T(8,128)S(1)}, f32[64,256]{1,0:T(8,128)S(1)}, u32[]{:S(2)}, u32[]{:S(2)}) collective-permute-start(f32[64,256]{1,0:T(8,128)S(1)} %get-tuple-element.45.e0), channel_id=1, source_target_pairs={{0,8},{1,9},{2,10},{3,11},{4,12},{5,13},{6,14},{7,15},{8,0},{9,1},... | collective-permute-start | bytes 196616 | tf_op jit(solution)/shard_map/ppermute | solution.py:438
  8.1 17.1 %collective-permute-start.4 = (f32[128,256]{1,0:T(8,128)S(1)}, f32[128,256]{1,0:T(8,128)S(1)}, u32[]{:S(2)}, u32[]{:S(2)}) collective-permute-start(f32[128,256]{1,0:T(8,128)S(1)} %get-tuple-element.51), channel_id=1, source_target_pairs={{0,16},{1,17},{2,18},{3,19},{4,20},{5,21},{6,22},{7,23},{8,24},{9,... | collective-permute-start | bytes 393224 | tf_op jit(solution)/shard_map/ppermute | solution.py:438
  10.3 14.8 %collective-permute-start.5 = (f32[128,256]{1,0:T(8,128)S(1)}, f32[128,256]{1,0:T(8,128)S(1)}, u32[]{:S(2)}, u32[]{:S(2)}) collective-permute-start(f32[128,256]{1,0:T(8,128)S(1)} %get-tuple-element.52), channel_id=1, source_target_pairs={{0,24},{1,25},{2,26},{3,27},{4,28},{5,29},{6,30},{7,31},{8,16},{9,... | collective-permute-start | bytes 393224 | tf_op jit(solution)/shard_map/ppermute | solution.py:438
  11.8 13.4 %collective-permute-start.3 = (f32[128,256]{1,0:T(8,128)S(1)}, f32[128,256]{1,0:T(8,128)S(1)}, u32[]{:S(2)}, u32[]{:S(2)}) collective-permute-start(f32[128,256]{1,0:T(8,128)S(1)} %get-tuple-element.50), channel_id=1, source_target_pairs={{0,8},{1,9},{2,10},{3,11},{4,12},{5,13},{6,14},{7,15},{8,0},{9,1},... | collective-permute-start | bytes 393224 | tf_op jit(solution)/shard_map/ppermute | solution.py:438
  25.2 15.7 %copy-start = (f32[4,64,256]{2,1,0:T(8,128)}, f32[4,64,256]{2,1,0:T(8,128)S(1)}, u32[]{:S(2)}) copy-start(f32[4,64,256]{2,1,0:T(8,128)S(1)} %stack_right.1.refs_0_.right) | copy-start | bytes 786436
  25.2 8.9 %collective-permute-start.7 = (f32[4,64,256]{2,1,0:T(8,128)S(1)}, f32[4,64,256]{2,1,0:T(8,128)S(1)}, u32[]{:S(2)}, u32[]{:S(2)}) collective-permute-start(f32[4,64,256]{2,1,0:T(8,128)S(1)} %stack_right.1.refs_0_.right), channel_id=1, source_target_pairs={{0,2},{1,3},{2,0},{3,1},{4,6},{5,7},{6,4},{7,5},{8,10},{9,11},{10,... | collective-permute-start | bytes 786440 | tf_op jit(solution)/shard_map/ppermute | solution.py:438
  25.3 11.1 %collective-permute-start.6 = (f32[4,64,256]{2,1,0:T(8,128)S(1)}, f32[4,64,256]{2,1,0:T(8,128)S(1)}, u32[]{:S(2)}, u32[]{:S(2)}) collective-permute-start(f32[4,64,256]{2,1,0:T(8,128)S(1)} %stack_right.1.refs_0_.right), channel_id=1, source_target_pairs={{0,4},{1,5},{2,6},{3,7},{4,0},{5,1},{6,2},{7,3},{8,12},{9,13},{10,... | collective-permute-start | bytes 786440 | tf_op jit(solution)/shard_map/ppermute | solution.py:438
  36.4 1.6 %collective-permute-start.8 = (f32[4,64,256]{2,1,0:T(8,128)S(1)}, f32[4,64,256]{2,1,0:T(8,128)S(1)}, u32[]{:S(2)}, u32[]{:S(2)}) collective-permute-start(f32[4,64,256]{2,1,0:T(8,128)S(1)} %collective-permute-done.6.refs_0_), channel_id=1, source_target_pairs={{0,2},{1,3},{2,0},{3,1},{4,6},{5,7},{6,4},{7,5},{8,10},{9,11},{10,... | collective-permute-start | bytes 786440 | tf_op jit(solution)/shard_map/ppermute | solution.py:438
  39.3 8.5 %collective-permute-start.10 = (f32[64,1024]{1,0:T(8,128)S(1)}, f32[64,1024]{1,0:T(8,128)S(1)}, u32[]{:S(2)}, u32[]{:S(2)}) collective-permute-start(f32[64,1024]{1,0:T(8,128)S(1)} %product_half.2.mine), channel_id=1, source_target_pairs={{0,1},{1,0},{2,3},{3,2},{4,5},{5,4},{6,7},{7,6},{8,9},{9,8},{10,11... | collective-permute-start | bytes 786440 | tf_op jit(solution)/shard_map/ppermute | solution.py:438
  43.2 1.3 %copy-start.5 = (f32[256]{0:T(256)S(1)}, f32[256]{0:T(256)}, u32[]{:S(2)}) copy-start(f32[256]{0:T(256)} %param.15) | copy-start | bytes 3076
  45.8 9.5 %collective-permute-start.9 = (f32[64,1024]{1,0:T(8,128)S(1)}, f32[64,1024]{1,0:T(8,128)S(1)}, u32[]{:S(2)}, u32[]{:S(2)}) collective-permute-start(f32[64,1024]{1,0:T(8,128)S(1)} %product_half.3.mine), channel_id=1, source_target_pairs={{0,1},{1,0},{2,3},{3,2},{4,5},{5,4},{6,7},{7,6},{8,9},{9,8},{10,11... | collective-permute-start | bytes 786440 | tf_op jit(solution)/shard_map/ppermute | solution.py:438
  48.0 10.3 %collective-permute-start.18 = (f32[64,256]{1,0:T(8,128)S(1)}, f32[64,256]{1,0:T(8,128)S(1)}, u32[]{:S(2)}, u32[]{:S(2)}) collective-permute-start(f32[64,256]{1,0:T(8,128)S(1)} %get-tuple-element.71), channel_id=1, source_target_pairs={{0,8},{1,9},{2,10},{3,11},{4,12},{5,13},{6,14},{7,15},{8,0},{9,1},... | collective-permute-start | bytes 196616 | tf_op jit(solution)/shard_map/ppermute | solution.py:438
  49.0 9.3 %collective-permute-start.19 = (f32[64,256]{1,0:T(8,128)S(1)}, f32[64,256]{1,0:T(8,128)S(1)}, u32[]{:S(2)}, u32[]{:S(2)}) collective-permute-start(f32[64,256]{1,0:T(8,128)S(1)} %get-tuple-element.72), channel_id=1, source_target_pairs={{0,16},{1,17},{2,18},{3,19},{4,20},{5,21},{6,22},{7,23},{8,24},{9,... | collective-permute-start | bytes 196616 | tf_op jit(solution)/shard_map/ppermute | solution.py:438
  53.0 6.1 %collective-permute-start.20 = (f32[64,256]{1,0:T(8,128)S(1)}, f32[64,256]{1,0:T(8,128)S(1)}, u32[]{:S(2)}, u32[]{:S(2)}) collective-permute-start(f32[64,256]{1,0:T(8,128)S(1)} %get-tuple-element.73), channel_id=1, source_target_pairs={{0,24},{1,25},{2,26},{3,27},{4,28},{5,29},{6,30},{7,31},{8,16},{9,... | collective-permute-start | bytes 196616 | tf_op jit(solution)/shard_map/ppermute | solution.py:438
  56.9 2.1 %collective-permute-start.12 = (f32[264,256]{1,0:T(8,128)S(1)}, f32[264,256]{1,0:T(8,128)S(1)}, u32[]{:S(2)}, u32[]{:S(2)}) collective-permute-start(f32[264,256]{1,0:T(8,128)S(1)} %backward_part.9), channel_id=1, source_target_pairs={{0,2},{1,3},{2,0},{3,1},{4,6},{5,7},{6,4},{7,5},{8,10},{9,11},{10,... | collective-permute-start | bytes 811016 | tf_op jit(solution)/shard_map/ppermute | solution.py:438
  57.7 6.1 %collective-permute-start.11 = (f32[256,256]{1,0:T(8,128)S(1)}, f32[256,256]{1,0:T(8,128)S(1)}, u32[]{:S(2)}, u32[]{:S(2)}) collective-permute-start(f32[256,256]{1,0:T(8,128)S(1)} %backward_part.8.token), channel_id=1, source_target_pairs={{0,2},{1,3},{2,0},{3,1},{4,6},{5,7},{6,4},{7,5},{8,10},{9,11},{10,... | collective-permute-start | bytes 786440 | tf_op jit(solution)/shard_map/ppermute | solution.py:438
  59.1 6.5 %collective-permute-start.14 = (f32[128,256]{1,0:T(8,128)S(1)}, f32[128,256]{1,0:T(8,128)S(1)}, u32[]{:S(2)}, u32[]{:S(2)}) collective-permute-start(f32[128,256]{1,0:T(8,128)S(1)} %get-tuple-element.64), channel_id=1, source_target_pairs={{0,4},{1,5},{2,6},{3,7},{4,0},{5,1},{6,2},{7,3},{8,12},{9,13},{10,... | collective-permute-start | bytes 393224 | tf_op jit(solution)/shard_map/ppermute | solution.py:438
  59.7 9.3 %copy-start.1 = (f32[4,64,256]{2,1,0:T(8,128)S(1)}, f32[4,64,256]{2,1,0:T(8,128)}, u32[]{:S(2)}) copy-start(f32[4,64,256]{2,1,0:T(8,128)} %copy-done) | copy-start | bytes 786436
  59.7 21.7 %copy-start.2 = (f32[256,256]{1,0:T(8,128)S(1)}, f32[256,256]{1,0:T(8,128)}, u32[]{:S(2)}) copy-start(f32[256,256]{1,0:T(8,128)} %right.1) | copy-start | bytes 786436
  59.7 21.8 %copy-start.3 = (f32[256,256]{1,0:T(8,128)S(1)}, f32[256,256]{1,0:T(8,128)}, u32[]{:S(2)}) copy-start(f32[256,256]{1,0:T(8,128)} %search.1) | copy-start | bytes 786436
  59.7 21.8 %copy-start.4 = (f32[256,256]{1,0:T(8,128)S(1)}, f32[256,256]{1,0:T(8,128)}, u32[]{:S(2)}) copy-start(f32[256,256]{1,0:T(8,128)} %solution.1) | copy-start | bytes 786436
  59.7 21.8 %copy-start.6 = (f32[256]{0:T(256)S(1)}, f32[256]{0:T(256)}, u32[]{:S(2)}) copy-start(f32[256]{0:T(256)} %param.16) | copy-start | bytes 3076
  59.7 21.8 %copy-start.7 = (f32[256]{0:T(256)S(1)}, f32[256]{0:T(256)}, u32[]{:S(2)}) copy-start(f32[256]{0:T(256)} %param.17) | copy-start | bytes 3076
  59.7 9.2 %collective-permute-start.13 = (f32[136,256]{1,0:T(8,128)S(1)}, f32[136,256]{1,0:T(8,128)S(1)}, u32[]{:S(2)}, u32[]{:S(2)}) collective-permute-start(f32[136,256]{1,0:T(8,128)S(1)} %get-tuple-element.62), channel_id=1, source_target_pairs={{0,4},{1,5},{2,6},{3,7},{4,0},{5,1},{6,2},{7,3},{8,12},{9,13},{10,... | collective-permute-start | bytes 417800 | tf_op jit(solution)/shard_map/ppermute | solution.py:438
  61.3 20.1 %collective-permute-start.21 = (f32[4,64,256]{2,1,0:T(8,128)S(1)}, f32[4,64,256]{2,1,0:T(8,128)S(1)}, u32[]{:S(2)}, u32[]{:S(2)}) collective-permute-start(f32[4,64,256]{2,1,0:T(8,128)S(1)} %stack_left.1.own), channel_id=1, source_target_pairs={{0,1},{1,0},{2,3},{3,2},{4,5},{5,4},{6,7},{7,6},{8,9},{9,8},{10,11... | collective-permute-start | bytes 786440 | tf_op jit(solution)/shard_map/ppermute | solution.py:438
  65.6 15.8 %collective-permute-start.16 = (f32[64,256]{1,0:T(8,128)S(1)}, f32[64,256]{1,0:T(8,128)S(1)}, u32[]{:S(2)}, u32[]{:S(2)}) collective-permute-start(f32[64,256]{1,0:T(8,128)S(1)} %get-tuple-element.65.g2), channel_id=1, source_target_pairs={{0,16},{1,17},{2,18},{3,19},{4,20},{5,21},{6,22},{7,23},{8,24},{9,... | collective-permute-start | bytes 196616 | tf_op jit(solution)/shard_map/ppermute | solution.py:438
  66.7 14.7 %collective-permute-start.17 = (f32[64,256]{1,0:T(8,128)S(1)}, f32[64,256]{1,0:T(8,128)S(1)}, u32[]{:S(2)}, u32[]{:S(2)}) collective-permute-start(f32[64,256]{1,0:T(8,128)S(1)} %get-tuple-element.66.g3), channel_id=1, source_target_pairs={{0,24},{1,25},{2,26},{3,27},{4,28},{5,29},{6,30},{7,31},{8,16},{9,... | collective-permute-start | bytes 196616 | tf_op jit(solution)/shard_map/ppermute | solution.py:438
  69.3 12.1 %collective-permute-start.15 = (f32[64,256]{1,0:T(8,128)S(1)}, f32[64,256]{1,0:T(8,128)S(1)}, u32[]{:S(2)}, u32[]{:S(2)}) collective-permute-start(f32[64,256]{1,0:T(8,128)S(1)} %get-tuple-element.68), channel_id=1, source_target_pairs={{0,8},{1,9},{2,10},{3,11},{4,12},{5,13},{6,14},{7,15},{8,0},{9,1},... | collective-permute-start | bytes 196616 | tf_op jit(solution)/shard_map/ppermute | solution.py:438

commit v25 on v23

--- a/solution.py
+++ b/solution.py
@@ -337,17 +337,18 @@
 
 
 def right_far_kernel(keep, peer, got, g2, g3):
-    q = g2.shape[0]
+    q = g2.shape[0] - 8
     for k, g in ((2, g2), (3, g3)):
+        g[q:, :] = jnp.zeros_like(g[q:, :])
         rows = slice(k * q, (k + 1) * q)
-        g[...] = (keep[rows, :] + peer[rows, :]) + got[(k - 2) * q : (k - 1) * q, :]
+        g[0:q, :] = (keep[rows, :] + peer[rows, :]) + got[(k - 2) * q : (k - 1) * q, :]
 
 
 def right_far(keep, peer, got):
     q, rows = keep.shape[0] // 4, keep.shape[1]
     return pl.pallas_call(
         right_far_kernel,
-        out_shape=[f32(q, rows)] * 2,
+        out_shape=[f32(q + 8, rows)] * 2,
         compiler_params=params(8),
         cost_estimate=cost(rows * q * 4, rows * q * 32),
         name="right_far",
@@ -363,7 +364,7 @@
     for k, g in enumerate((g0, g1)):
         rows = slice(k * q, (k + 1) * q)
         g[...] = (keep[rows, :] + peer[rows, :]) + got[rows, :]
-    raws = [g[...] / beta - beta * right[k] for k, g in enumerate((g0, g1, g2, g3))]
+    raws = [g[0:q, :] / beta - beta * right[k] for k, g in enumerate((g0, g1, g2, g3))]
     line = square_sums(jnp.concatenate(raws, axis=1))
     folded = beta_sums[:, :128] + beta_sums[:, 128:]
     folded = folded + jnp.concatenate([folded[:, q:], folded[:, :q]], axis=1)
@@ -412,7 +413,7 @@
     phibar_out[...] = sine * phibar[...]
     alpha_out[...] = alpha
     for k, g in enumerate((g0, g1, g2, g3)):
-        turned[z ^ k] = g[...]
+        turned[z ^ k] = g[0:q, :]
     got = turned[...].reshape(-1, half).T
     following = (got / beta - beta * right[...]) / alpha
     right_out[...] = following
@@ -483,7 +484,7 @@
     got_far = swap(send_far, X_BIT)
     got_near = swap(send_near, X_BIT)
     keep = backward_part(rows1, both1, 0, 4, partial, None, [], 0.05)
-    peer = swap(peer, CORE_BIT)
+    peer = swap(after(peer, send_far), CORE_BIT)
 
     g2, g3 = right_far(keep, peer, got_far)
     p2, p3 = swap(g2, 2 << Z_SHIFT), swap(g3, 3 << Z_SHIFT)

time: 78.4 us -> 79.1 us (level)
  blocking collectives: 12.3 us -> 0 us
  waiting for transfers between devices: 9.11 us -> 16.8 us
  starting transfers between devices: 27.5 us -> 32.2 us
    all_to_all x1 -> x0, blocking collectives: 12.3 us -> none  [by_columns(): squares = lax.all_to_all(after(sums, left_own), AXES, 0, 0, tiled=True)]
    all_to_all x0 -> x1, waiting for transfers between devices: none -> 7.11 us  [by_columns(): squares = lax.all_to_all(after(sums, left_own), AXES, 0, 0, tiled=True)]
    all_to_all x0 -> x1, starting transfers between devices: none -> 5.32 us  [by_columns(): squares = lax.all_to_all(after(sums, left_own), AXES, 0, 0, tiled=True)]
  transfers between devices with their start and end apart: 22 -> 23, of which waited for: 6 -> 7; matrix products, arithmetic and copies ran while one was open for 0% -> 0% of each run, Pallas kernels for 31% -> 31%
where the time goes in v25:
time: 79.1 us; the launch traced here: 78.9 us
  starting transfers between devices  32.2 us (41%)
  Pallas kernels  28.9 us (37%)
  waiting for transfers between devices  16.8 us (21%)
  between operations  0.96 us (1%)
    ppermute x22, starting transfers between devices, swap(): return lax.ppermute(value, AXES, [(i, i ^ mask) for i in range(32)])  26.9 us
    ppermute x22, waiting for transfers between devices, swap(): return lax.ppermute(value, AXES, [(i, i ^ mask) for i in range(32)])  9.67 us
    pallas_call x2, Pallas kernels, build(): pl.pallas_call(functools.partial(build_kernel, rel), in_specs=[whole()] *...  9.62 us
    pallas_call x4, Pallas kernels, forward_part(): pl.pallas_call(functools.partial(forward_kernel, blocks, before is not No...  7.12 us
    all_to_all x1, waiting for transfers between devices, by_columns(): squares = lax.all_to_all(after(sums, left_own), AXES, 0, 0, tiled=True)  7.11 us
    all_to_all x1, starting transfers between devices, by_columns(): squares = lax.all_to_all(after(sums, left_own), AXES, 0, 0, tiled=True)  5.32 us
    pallas_call x5, Pallas kernels, backward_part(): pl.pallas_call(functools.partial(backward_kernel, first, blocks, tuple(ex...  5.19 us
    pallas_call x2, Pallas kernels, product_half(): pl.pallas_call(functools.partial(product_kernel, blocks), in_specs=[whole...  2.64 us
  transfers between devices with their start and end apart: 23, of which 7 were waited for; matrix products, arithmetic and copies ran while one was open for 0% of the time, Pallas kernels for 31%

profile of v25, /device:TPU:0, one launch (start us, length us, event | category | flops | bytes accessed | tf_op | source)
XLA Modules:
  0.0 78.9 jit_solution(8416923194005595936)
XLA Ops:
  0.6 1.6 %prepare.1 = (f32[64,256]{1,0:T(8,128)S(1)}, f32[128,256]{1,0:T(8,128)S(1)}, f32[128,256]{1,0:T(8,128)S(1)}, f32[128,256]{1,0:T(8,128)S(1)}, f32[128,256]{1,0:T(8,128)S(1)}) custom-call(s32[16,512]{1,0:T(8,128)} %bitcast.12, bf16[16,512]{1,0:T(8,128)(2,1)} %bitcast.13, f32[256,256]{1,0:T(8,128)} %right.1, f32[512,256]{1,0:T(8,128)} %left_hbm.1), custom_call_target="tpu_custom_call" | custom-call | bytes 16384 | tf_op jit(solution)/shard_map/prepare/pallas_call | solution.py:74
  2.3 5.1 %collective-permute-start.2 = (f32[64,256]{1,0:T(8,128)S(1)}, f32[64,256]{1,0:T(8,128)S(1)}, u32[]{:S(2)}, u32[]{:S(2)}) collective-permute-start(f32[64,256]{1,0:T(8,128)S(1)} %get-tuple-element.46.e0), channel_id=1, source_target_pairs={{0,24},{1,25},{2,26},{3,27},{4,28},{5,29},{6,30},{7,31},{8,16},{9,... | collective-permute-start | bytes 196616 | tf_op jit(solution)/shard_map/ppermute | solution.py:437
  7.4 0.6 collective-permute-start
  8.1 2.3 %collective-permute-start.4 = (f32[128,256]{1,0:T(8,128)S(1)}, f32[128,256]{1,0:T(8,128)S(1)}, u32[]{:S(2)}, u32[]{:S(2)}) collective-permute-start(f32[128,256]{1,0:T(8,128)S(1)} %get-tuple-element.52), channel_id=1, source_target_pairs={{0,16},{1,17},{2,18},{3,19},{4,20},{5,21},{6,22},{7,23},{8,24},{9,... | collective-permute-start | bytes 393224 | tf_op jit(solution)/shard_map/ppermute | solution.py:437
  10.3 1.5 %collective-permute-start.5 = (f32[128,256]{1,0:T(8,128)S(1)}, f32[128,256]{1,0:T(8,128)S(1)}, u32[]{:S(2)}, u32[]{:S(2)}) collective-permute-start(f32[128,256]{1,0:T(8,128)S(1)} %get-tuple-element.53), channel_id=1, source_target_pairs={{0,24},{1,25},{2,26},{3,27},{4,28},{5,29},{6,30},{7,31},{8,16},{9,... | collective-permute-start | bytes 393224 | tf_op jit(solution)/shard_map/ppermute | solution.py:437
  11.8 0.8 %collective-permute-start.3 = (f32[128,256]{1,0:T(8,128)S(1)}, f32[128,256]{1,0:T(8,128)S(1)}, u32[]{:S(2)}, u32[]{:S(2)}) collective-permute-start(f32[128,256]{1,0:T(8,128)S(1)} %get-tuple-element.51), channel_id=1, source_target_pairs={{0,8},{1,9},{2,10},{3,11},{4,12},{5,13},{6,14},{7,15},{8,0},{9,1},... | collective-permute-start | bytes 393224 | tf_op jit(solution)/shard_map/ppermute | solution.py:437
  12.6 5.1 %collective-permute-done.1.e2 = f32[64,256]{1,0:T(8,128)S(1)} collective-permute-done((f32[64,256]{1,0:T(8,128)S(1)}, f32[64,256]{1,0:T(8,128)S(1)}, u32[]{:S(2)}, u32[]{:S(2)}) %collective-permute-start.1) | collective-permute-done | bytes 65568 | tf_op jit(solution)/shard_map/ppermute | solution.py:437
  17.7 4.7 %dense_rows.2 = (bf16[16,1024,256]{2,1,0:T(8,128)(2,1)S(1)}, bf16[16,1024,256]{2,1,0:T(8,128)(2,1)S(1)}, f32[8,128]{1,0:T(8,128)S(1)}) custom-call(f32[64,256]{1,0:T(8,128)S(1)} %get-tuple-element.46.e0, f32[64,256]{1,0:T(8,128)S(1)} %collective-permute-done.e1, f32[64,256]{1,0:T(8,128)S(1)} %collective-permute-done.1.e2, ...), custom_call_target="tpu_custom_call" | custom-call | flops 2147483648 | bytes 16777216 | tf_op jit(solution)/shard_map/dense_rows/pallas_call | solution.py:154
  22.5 0.0 copy-start
  22.5 0.1 collective-permute-start.7
  22.6 1.2 %collective-permute-start.6 = (f32[4,64,256]{2,1,0:T(8,128)S(1)}, f32[4,64,256]{2,1,0:T(8,128)S(1)}, u32[]{:S(2)}, u32[]{:S(2)}) collective-permute-start(f32[4,64,256]{2,1,0:T(8,128)S(1)} %stack_right.1.refs_0_.right), channel_id=1, source_target_pairs={{0,4},{1,5},{2,6},{3,7},{4,0},{5,1},{6,2},{7,3},{8,12},{9,13},{10,... | collective-permute-start | bytes 786440 | tf_op jit(solution)/shard_map/ppermute | solution.py:437
  23.8 4.9 %dense_rows.3 = (bf16[16,1024,256]{2,1,0:T(8,128)(2,1)S(1)}, bf16[16,1024,256]{2,1,0:T(8,128)(2,1)S(1)}, f32[8,128]{1,0:T(8,128)S(1)}) custom-call(f32[64,256]{1,0:T(8,128)S(1)} %get-tuple-element.46.e0, f32[64,256]{1,0:T(8,128)S(1)} %collective-permute-done.e1, f32[64,256]{1,0:T(8,128)S(1)} %collective-permute-done.1.e2, ...), custom_call_target="tpu_custom_call" | custom-call | flops 33554432 | bytes 262144 | tf_op jit(solution)/shard_map/dense_rows/pallas_call | solution.py:154
  28.7 2.3 %forward_part.4.refs_1_ = f32[1024,128]{1,0:T(8,128)S(1)} custom-call(bf16[16,1024,256]{2,1,0:T(8,128)(2,1)S(1)} %get-tuple-element.47.hi_ref, bf16[16,1024,256]{2,1,0:T(8,128)(2,1)S(1)} %get-tuple-element.48.lo_ref, f32[4,64,256]{2,1,0:T(8,128)S(1)} %stack_right.1.refs_0_.right, f32[4,64,256]{2,1,0:T(8,128)S(1)} %collective-permute-done.7.refs_1_, ...), custom_call_target="tpu_custom_call" | custom-call | flops 67108864 | bytes 131072 | tf_op jit(solution)/shard_map/forward_part/pallas_call | solution.py:196
  31.1 0.3 collective-permute-done.6.refs_0_
  31.3 1.2 %forward_part.5.before = f32[1024,128]{1,0:T(8,128)S(1)} custom-call(bf16[16,1024,256]{2,1,0:T(8,128)(2,1)S(1)} %get-tuple-element.47.hi_ref, bf16[16,1024,256]{2,1,0:T(8,128)(2,1)S(1)} %get-tuple-element.48.lo_ref, f32[4,64,256]{2,1,0:T(8,128)S(1)} %collective-permute-done.6.refs_0_, f32[1024,128]{1,0:T(8,128)S(1)} %forward_part.4.refs_1_), custom_call_target="tpu_custom_call" | custom-call | flops 33554432 | bytes 65536 | tf_op jit(solution)/shard_map/forward_part/pallas_call | solution.py:196
  32.6 0.3 collective-permute-done.8.vec
  32.9 1.3 %product_half.2.mine = f32[64,1024]{1,0:T(8,128)S(1)} custom-call(bf16[16,1024,256]{2,1,0:T(8,128)(2,1)S(1)} %get-tuple-element.47.hi_ref, bf16[16,1024,256]{2,1,0:T(8,128)(2,1)S(1)} %get-tuple-element.48.lo_ref, f32[4,64,256]{2,1,0:T(8,128)S(1)} %collective-permute-done.8.vec, f32[1024,128]{1,0:T(8,128)S(1)} %forward_part.5.before), custom_call_target="tpu_custom_call" | custom-call | flops 33554432 | bytes 65536 | tf_op jit(solution)/shard_map/product_half/pallas_call | solution.py:228
  34.2 1.4 %collective-permute-start.10 = (f32[64,1024]{1,0:T(8,128)S(1)}, f32[64,1024]{1,0:T(8,128)S(1)}, u32[]{:S(2)}, u32[]{:S(2)}) collective-permute-start(f32[64,1024]{1,0:T(8,128)S(1)} %product_half.2.mine), channel_id=1, source_target_pairs={{0,1},{1,0},{2,3},{3,2},{4,5},{5,4},{6,7},{7,6},{8,9},{9,8},{10,11... | collective-permute-start | bytes 786440 | tf_op jit(solution)/shard_map/ppermute | solution.py:437
  35.6 2.3 %forward_part.6.refs_1_ = f32[1024,128]{1,0:T(8,128)S(1)} custom-call(bf16[16,1024,256]{2,1,0:T(8,128)(2,1)S(1)} %get-tuple-element.57.hi_ref, bf16[16,1024,256]{2,1,0:T(8,128)(2,1)S(1)} %get-tuple-element.58.lo_ref, f32[4,64,256]{2,1,0:T(8,128)S(1)} %stack_right.1.refs_0_.right, f32[4,64,256]{2,1,0:T(8,128)S(1)} %collective-permute-done.7.refs_1_), custom_call_target="tpu_custom_call" | custom-call | flops 67108864 | bytes 131072 | tf_op jit(solution)/shard_map/forward_part/pallas_call | solution.py:196
  37.9 0.0 copy-start.5
  37.9 1.2 %forward_part.7.before = f32[1024,128]{1,0:T(8,128)S(1)} custom-call(bf16[16,1024,256]{2,1,0:T(8,128)(2,1)S(1)} %get-tuple-element.57.hi_ref, bf16[16,1024,256]{2,1,0:T(8,128)(2,1)S(1)} %get-tuple-element.58.lo_ref, f32[4,64,256]{2,1,0:T(8,128)S(1)} %collective-permute-done.6.refs_0_, f32[1024,128]{1,0:T(8,128)S(1)} %forward_part.6.refs_1_), custom_call_target="tpu_custom_call" | custom-call | flops 33554432 | bytes 65536 | tf_op jit(solution)/shard_map/forward_part/pallas_call | solution.py:196
  39.2 1.3 %product_half.3.mine = f32[64,1024]{1,0:T(8,128)S(1)} custom-call(bf16[16,1024,256]{2,1,0:T(8,128)(2,1)S(1)} %get-tuple-element.57.hi_ref, bf16[16,1024,256]{2,1,0:T(8,128)(2,1)S(1)} %get-tuple-element.58.lo_ref, f32[4,64,256]{2,1,0:T(8,128)S(1)} %collective-permute-done.8.vec, f32[1024,128]{1,0:T(8,128)S(1)} %forward_part.7.before, ...), custom_call_target="tpu_custom_call" | custom-call | flops 33554432 | bytes 65536 | tf_op jit(solution)/shard_map/product_half/pallas_call | solution.py:228
  40.5 0.8 collective-permute-start.9
  41.3 1.4 %collective-permute-done.10.other = f32[64,1024]{1,0:T(8,128)S(1)} collective-permute-done((f32[64,1024]{1,0:T(8,128)S(1)}, f32[64,1024]{1,0:T(8,128)S(1)}, u32[]{:S(2)}, u32[]{:S(2)}) %collective-permute-start.10) | collective-permute-done | bytes 262176 | tf_op jit(solution)/shard_map/ppermute | solution.py:437
  42.7 0.2 left_half.2
  42.9 2.6 %collective-permute-start.18 = (f32[64,256]{1,0:T(8,128)S(1)}, f32[64,256]{1,0:T(8,128)S(1)}, u32[]{:S(2)}, u32[]{:S(2)}) collective-permute-start(f32[64,256]{1,0:T(8,128)S(1)} %get-tuple-element.73), channel_id=1, source_target_pairs={{0,8},{1,9},{2,10},{3,11},{4,12},{5,13},{6,14},{7,15},{8,0},{9,1},... | collective-permute-start | bytes 196616 | tf_op jit(solution)/shard_map/ppermute | solution.py:437
  45.4 2.2 %collective-permute-start.19 = (f32[64,256]{1,0:T(8,128)S(1)}, f32[64,256]{1,0:T(8,128)S(1)}, u32[]{:S(2)}, u32[]{:S(2)}) collective-permute-start(f32[64,256]{1,0:T(8,128)S(1)} %get-tuple-element.74), channel_id=1, source_target_pairs={{0,16},{1,17},{2,18},{3,19},{4,20},{5,21},{6,22},{7,23},{8,24},{9,... | collective-permute-start | bytes 196616 | tf_op jit(solution)/shard_map/ppermute | solution.py:437
  47.6 0.6 collective-permute-start.20
  48.2 2.3 %backward_part.5.refs_1_.refs_0_ = f32[1024,256]{1,0:T(8,128)S(1)} custom-call(bf16[16,1024,256]{2,1,0:T(8,128)(2,1)S(1)} %get-tuple-element.57.hi_ref, bf16[16,1024,256]{2,1,0:T(8,128)(2,1)S(1)} %get-tuple-element.58.lo_ref, bf16[128,1024]{1,0:T(8,128)(2,1)S(1)} %get-tuple-element.60.both_ref), custom_call_target="tpu_custom_call" | custom-call | flops 134217728 | bytes 262144 | tf_op jit(solution)/shard_map/backward_part/pallas_call | solution.py:309
  50.5 0.2 left_half.3
  50.7 0.7 backward_part.7.refs_1_.near
  51.4 0.7 backward_part.9
  52.1 0.1 collective-permute-start.11
  52.2 0.7 backward_part.8.token
  53.0 0.8 %collective-permute-done.20.m3 = f32[64,256]{1,0:T(8,128)S(1)} collective-permute-done((f32[64,256]{1,0:T(8,128)S(1)}, f32[64,256]{1,0:T(8,128)S(1)}, u32[]{:S(2)}, u32[]{:S(2)}) %collective-permute-start.20) | collective-permute-done | bytes 65568 | tf_op jit(solution)/shard_map/ppermute | solution.py:437
  53.8 1.4 %collective-permute-start.14 = (f32[128,256]{1,0:T(8,128)S(1)}, f32[128,256]{1,0:T(8,128)S(1)}, u32[]{:S(2)}, u32[]{:S(2)}) collective-permute-start(f32[128,256]{1,0:T(8,128)S(1)} %get-tuple-element.63), channel_id=1, source_target_pairs={{0,4},{1,5},{2,6},{3,7},{4,0},{5,1},{6,2},{7,3},{8,12},{9,13},{10,... | collective-permute-start | bytes 393224 | tf_op jit(solution)/shard_map/ppermute | solution.py:437
  55.3 0.0 copy-start.6
  55.3 0.8 collective-permute-start.13
  56.0 1.8 %collective-permute-start.21 = (f32[4,64,256]{2,1,0:T(8,128)S(1)}, f32[4,64,256]{2,1,0:T(8,128)S(1)}, u32[]{:S(2)}, u32[]{:S(2)}) collective-permute-start(f32[4,64,256]{2,1,0:T(8,128)S(1)} %stack_left.1.own), channel_id=1, source_target_pairs={{0,1},{1,0},{2,3},{3,2},{4,5},{5,4},{6,7},{7,6},{8,9},{9,8},{10,11... | collective-permute-start | bytes 786440 | tf_op jit(solution)/shard_map/ppermute | solution.py:437
  57.8 0.7 backward_part.6.keep
  58.5 1.7 %collective-permute-done.14.got = f32[128,256]{1,0:T(8,128)S(1)} collective-permute-done((f32[128,256]{1,0:T(8,128)S(1)}, f32[128,256]{1,0:T(8,128)S(1)}, u32[]{:S(2)}, u32[]{:S(2)}) %collective-permute-start.14) | collective-permute-done | bytes 131104 | tf_op jit(solution)/shard_map/ppermute | solution.py:437
  60.3 2.2 %collective-permute-start.16 = (f32[72,256]{1,0:T(8,128)S(1)}, f32[72,256]{1,0:T(8,128)S(1)}, u32[]{:S(2)}, u32[]{:S(2)}) collective-permute-start(f32[72,256]{1,0:T(8,128)S(1)} %get-tuple-element.67.g2), channel_id=1, source_target_pairs={{0,16},{1,17},{2,18},{3,19},{4,20},{5,21},{6,22},{7,23},{8,24},{9,... | collective-permute-start | bytes 221192 | tf_op jit(solution)/shard_map/ppermute | solution.py:437
  62.5 1.2 %collective-permute-start.17 = (f32[72,256]{1,0:T(8,128)S(1)}, f32[72,256]{1,0:T(8,128)S(1)}, u32[]{:S(2)}, u32[]{:S(2)}) collective-permute-start(f32[72,256]{1,0:T(8,128)S(1)} %get-tuple-element.68.g3), channel_id=1, source_target_pairs={{0,24},{1,25},{2,26},{3,27},{4,28},{5,29},{6,30},{7,31},{8,16},{9,... | collective-permute-start | bytes 221192 | tf_op jit(solution)/shard_map/ppermute | solution.py:437
  63.6 0.9 %right_norm.1 = (f32[64,256]{1,0:T(8,128)S(1)}, f32[64,256]{1,0:T(8,128)S(1)}, f32[32,128]{1,0:T(8,128)}) custom-call(f32[256,256]{1,0:T(8,128)S(1)} %backward_part.6.keep, f32[256,256]{1,0:T(8,128)S(1)} %collective-permute-done.12.peer, f32[136,256]{1,0:T(8,128)S(1)} %collective-permute-done.13.got, f32[8,256]{1,0:T(8,128)S(1)} %get-tuple-element.66.beta_core, ...), custom_call_target="tpu_custom_call" | custom-call | flops 16384 | bytes 25600 | tf_op jit(solution)/shard_map/right_norm/pallas_call | solution.py:377
  64.6 0.5 collective-permute-start.15
  65.1 5.3 %all-to-all-start = ((f32[32,1,128]{2,1,0:T(1,128)}), f32[32,1,128]{2,1,0:T(1,128)S(1)}, u32[]{:S(2)}, u32[]{:S(2)}) async-start(f32[32,1,128]{2,1,0:T(1,128)} %bitcast.3), calls=%async_computation | async-start | bytes 32768 | tf_op jit(solution)/shard_map/all_to_all | solution.py:494
  70.4 7.1 %all-to-all-done.squares = f32[32,1,128]{2,1,0:T(1,128)S(1)} async-done(((f32[32,1,128]{2,1,0:T(1,128)}), f32[32,1,128]{2,1,0:T(1,128)S(1)}, u32[]{:S(2)}, u32[]{:S(2)}) %all-to-all-start) | async-done | bytes 16416 | tf_op jit(solution)/shard_map/all_to_all | solution.py:494
  77.6 1.3 %finish.1 = (f32[512,256]{1,0:T(8,128)}, f32[256,256]{1,0:T(8,128)}, f32[256,256]{1,0:T(8,128)}, f32[256,256]{1,0:T(8,128)}, f32[1,256]{1,0:T(1,128)}, /*index=5*/f32[1,256]{1,0:T(1,128)}, f32[1,256]{1,0:T(1,128)}) custom-call(f32[64,256]{1,0:T(8,128)S(1)} %get-tuple-element.69.g0, f32[64,256]{1,0:T(8,128)S(1)} %collective-permute-done.15.g1, ...), custom_call_target="tpu_custom_call" | custom-call | flops 16384 | bytes 20480 | tf_op jit(solution)/shard_map/finish/pallas_call | solution.py:426
  (36 shorter events, 0.2 us)
Async XLA Ops:
  2.3 9.5 %collective-permute-start.2 = (f32[64,256]{1,0:T(8,128)S(1)}, f32[64,256]{1,0:T(8,128)S(1)}, u32[]{:S(2)}, u32[]{:S(2)}) collective-permute-start(f32[64,256]{1,0:T(8,128)S(1)} %get-tuple-element.46.e0), channel_id=1, source_target_pairs={{0,24},{1,25},{2,26},{3,27},{4,28},{5,29},{6,30},{7,31},{8,16},{9,... | collective-permute-start | bytes 196616 | tf_op jit(solution)/shard_map/ppermute | solution.py:437
  7.4 10.3 %collective-permute-start.1 = (f32[64,256]{1,0:T(8,128)S(1)}, f32[64,256]{1,0:T(8,128)S(1)}, u32[]{:S(2)}, u32[]{:S(2)}) collective-permute-start(f32[64,256]{1,0:T(8,128)S(1)} %get-tuple-element.46.e0), channel_id=1, source_target_pairs={{0,16},{1,17},{2,18},{3,19},{4,20},{5,21},{6,22},{7,23},{8,24},{9,... | collective-permute-start | bytes 196616 | tf_op jit(solution)/shard_map/ppermute | solution.py:437
  7.4 10.3 %collective-permute-start = (f32[64,256]{1,0:T(8,128)S(1)}, f32[64,256]{1,0:T(8,128)S(1)}, u32[]{:S(2)}, u32[]{:S(2)}) collective-permute-start(f32[64,256]{1,0:T(8,128)S(1)} %get-tuple-element.46.e0), channel_id=1, source_target_pairs={{0,8},{1,9},{2,10},{3,11},{4,12},{5,13},{6,14},{7,15},{8,0},{9,1},... | collective-permute-start | bytes 196616 | tf_op jit(solution)/shard_map/ppermute | solution.py:437
  8.1 14.4 %collective-permute-start.4 = (f32[128,256]{1,0:T(8,128)S(1)}, f32[128,256]{1,0:T(8,128)S(1)}, u32[]{:S(2)}, u32[]{:S(2)}) collective-permute-start(f32[128,256]{1,0:T(8,128)S(1)} %get-tuple-element.52), channel_id=1, source_target_pairs={{0,16},{1,17},{2,18},{3,19},{4,20},{5,21},{6,22},{7,23},{8,24},{9,... | collective-permute-start | bytes 393224 | tf_op jit(solution)/shard_map/ppermute | solution.py:437
  10.3 12.1 %collective-permute-start.5 = (f32[128,256]{1,0:T(8,128)S(1)}, f32[128,256]{1,0:T(8,128)S(1)}, u32[]{:S(2)}, u32[]{:S(2)}) collective-permute-start(f32[128,256]{1,0:T(8,128)S(1)} %get-tuple-element.53), channel_id=1, source_target_pairs={{0,24},{1,25},{2,26},{3,27},{4,28},{5,29},{6,30},{7,31},{8,16},{9,... | collective-permute-start | bytes 393224 | tf_op jit(solution)/shard_map/ppermute | solution.py:437
  11.8 10.7 %collective-permute-start.3 = (f32[128,256]{1,0:T(8,128)S(1)}, f32[128,256]{1,0:T(8,128)S(1)}, u32[]{:S(2)}, u32[]{:S(2)}) collective-permute-start(f32[128,256]{1,0:T(8,128)S(1)} %get-tuple-element.51), channel_id=1, source_target_pairs={{0,8},{1,9},{2,10},{3,11},{4,12},{5,13},{6,14},{7,15},{8,0},{9,1},... | collective-permute-start | bytes 393224 | tf_op jit(solution)/shard_map/ppermute | solution.py:437
  22.5 13.0 %copy-start = (f32[4,64,256]{2,1,0:T(8,128)}, f32[4,64,256]{2,1,0:T(8,128)S(1)}, u32[]{:S(2)}) copy-start(f32[4,64,256]{2,1,0:T(8,128)S(1)} %stack_right.1.refs_0_.right) | copy-start | bytes 786436
  22.5 6.2 %collective-permute-start.7 = (f32[4,64,256]{2,1,0:T(8,128)S(1)}, f32[4,64,256]{2,1,0:T(8,128)S(1)}, u32[]{:S(2)}, u32[]{:S(2)}) collective-permute-start(f32[4,64,256]{2,1,0:T(8,128)S(1)} %stack_right.1.refs_0_.right), channel_id=1, source_target_pairs={{0,2},{1,3},{2,0},{3,1},{4,6},{5,7},{6,4},{7,5},{8,10},{9,11},{10,... | collective-permute-start | bytes 786440 | tf_op jit(solution)/shard_map/ppermute | solution.py:437
  22.6 8.7 %collective-permute-start.6 = (f32[4,64,256]{2,1,0:T(8,128)S(1)}, f32[4,64,256]{2,1,0:T(8,128)S(1)}, u32[]{:S(2)}, u32[]{:S(2)}) collective-permute-start(f32[4,64,256]{2,1,0:T(8,128)S(1)} %stack_right.1.refs_0_.right), channel_id=1, source_target_pairs={{0,4},{1,5},{2,6},{3,7},{4,0},{5,1},{6,2},{7,3},{8,12},{9,13},{10,... | collective-permute-start | bytes 786440 | tf_op jit(solution)/shard_map/ppermute | solution.py:437
  31.3 1.5 %collective-permute-start.8 = (f32[4,64,256]{2,1,0:T(8,128)S(1)}, f32[4,64,256]{2,1,0:T(8,128)S(1)}, u32[]{:S(2)}, u32[]{:S(2)}) collective-permute-start(f32[4,64,256]{2,1,0:T(8,128)S(1)} %collective-permute-done.6.refs_0_), channel_id=1, source_target_pairs={{0,2},{1,3},{2,0},{3,1},{4,6},{5,7},{6,4},{7,5},{8,10},{9,11},{10,... | collective-permute-start | bytes 786440 | tf_op jit(solution)/shard_map/ppermute | solution.py:437
  34.2 8.5 %collective-permute-start.10 = (f32[64,1024]{1,0:T(8,128)S(1)}, f32[64,1024]{1,0:T(8,128)S(1)}, u32[]{:S(2)}, u32[]{:S(2)}) collective-permute-start(f32[64,1024]{1,0:T(8,128)S(1)} %product_half.2.mine), channel_id=1, source_target_pairs={{0,1},{1,0},{2,3},{3,2},{4,5},{5,4},{6,7},{7,6},{8,9},{9,8},{10,11... | collective-permute-start | bytes 786440 | tf_op jit(solution)/shard_map/ppermute | solution.py:437
  37.9 1.3 %copy-start.5 = (f32[256]{0:T(256)S(1)}, f32[256]{0:T(256)}, u32[]{:S(2)}) copy-start(f32[256]{0:T(256)} %param.15) | copy-start | bytes 3076
  40.5 10.0 %collective-permute-start.9 = (f32[64,1024]{1,0:T(8,128)S(1)}, f32[64,1024]{1,0:T(8,128)S(1)}, u32[]{:S(2)}, u32[]{:S(2)}) collective-permute-start(f32[64,1024]{1,0:T(8,128)S(1)} %product_half.3.mine), channel_id=1, source_target_pairs={{0,1},{1,0},{2,3},{3,2},{4,5},{5,4},{6,7},{7,6},{8,9},{9,8},{10,11... | collective-permute-start | bytes 786440 | tf_op jit(solution)/shard_map/ppermute | solution.py:437
  42.9 10.1 %collective-permute-start.18 = (f32[64,256]{1,0:T(8,128)S(1)}, f32[64,256]{1,0:T(8,128)S(1)}, u32[]{:S(2)}, u32[]{:S(2)}) collective-permute-start(f32[64,256]{1,0:T(8,128)S(1)} %get-tuple-element.73), channel_id=1, source_target_pairs={{0,8},{1,9},{2,10},{3,11},{4,12},{5,13},{6,14},{7,15},{8,0},{9,1},... | collective-permute-start | bytes 196616 | tf_op jit(solution)/shard_map/ppermute | solution.py:437
  45.4 7.5 %collective-permute-start.19 = (f32[64,256]{1,0:T(8,128)S(1)}, f32[64,256]{1,0:T(8,128)S(1)}, u32[]{:S(2)}, u32[]{:S(2)}) collective-permute-start(f32[64,256]{1,0:T(8,128)S(1)} %get-tuple-element.74), channel_id=1, source_target_pairs={{0,16},{1,17},{2,18},{3,19},{4,20},{5,21},{6,22},{7,23},{8,24},{9,... | collective-permute-start | bytes 196616 | tf_op jit(solution)/shard_map/ppermute | solution.py:437
  47.6 6.2 %collective-permute-start.20 = (f32[64,256]{1,0:T(8,128)S(1)}, f32[64,256]{1,0:T(8,128)S(1)}, u32[]{:S(2)}, u32[]{:S(2)}) collective-permute-start(f32[64,256]{1,0:T(8,128)S(1)} %get-tuple-element.75), channel_id=1, source_target_pairs={{0,24},{1,25},{2,26},{3,27},{4,28},{5,29},{6,30},{7,31},{8,16},{9,... | collective-permute-start | bytes 196616 | tf_op jit(solution)/shard_map/ppermute | solution.py:437
  52.1 1.7 %collective-permute-start.11 = (f32[264,256]{1,0:T(8,128)S(1)}, f32[264,256]{1,0:T(8,128)S(1)}, u32[]{:S(2)}, u32[]{:S(2)}) collective-permute-start(f32[264,256]{1,0:T(8,128)S(1)} %backward_part.9), channel_id=1, source_target_pairs={{0,2},{1,3},{2,0},{3,1},{4,6},{5,7},{6,4},{7,5},{8,10},{9,11},{10,... | collective-permute-start | bytes 811016 | tf_op jit(solution)/shard_map/ppermute | solution.py:437
  53.8 6.4 %collective-permute-start.14 = (f32[128,256]{1,0:T(8,128)S(1)}, f32[128,256]{1,0:T(8,128)S(1)}, u32[]{:S(2)}, u32[]{:S(2)}) collective-permute-start(f32[128,256]{1,0:T(8,128)S(1)} %get-tuple-element.63), channel_id=1, source_target_pairs={{0,4},{1,5},{2,6},{3,7},{4,0},{5,1},{6,2},{7,3},{8,12},{9,13},{10,... | collective-permute-start | bytes 393224 | tf_op jit(solution)/shard_map/ppermute | solution.py:437
  55.2 8.4 %copy-start.1 = (f32[4,64,256]{2,1,0:T(8,128)S(1)}, f32[4,64,256]{2,1,0:T(8,128)}, u32[]{:S(2)}) copy-start(f32[4,64,256]{2,1,0:T(8,128)} %copy-done) | copy-start | bytes 786436
  55.2 22.3 %copy-start.2 = (f32[256,256]{1,0:T(8,128)S(1)}, f32[256,256]{1,0:T(8,128)}, u32[]{:S(2)}) copy-start(f32[256,256]{1,0:T(8,128)} %right.1) | copy-start | bytes 786436
  55.2 22.3 %copy-start.3 = (f32[256,256]{1,0:T(8,128)S(1)}, f32[256,256]{1,0:T(8,128)}, u32[]{:S(2)}) copy-start(f32[256,256]{1,0:T(8,128)} %search.1) | copy-start | bytes 786436
  55.2 22.3 %copy-start.4 = (f32[256,256]{1,0:T(8,128)S(1)}, f32[256,256]{1,0:T(8,128)}, u32[]{:S(2)}) copy-start(f32[256,256]{1,0:T(8,128)} %solution.1) | copy-start | bytes 786436
  55.3 22.3 %copy-start.6 = (f32[256]{0:T(256)S(1)}, f32[256]{0:T(256)}, u32[]{:S(2)}) copy-start(f32[256]{0:T(256)} %param.16) | copy-start | bytes 3076
  55.3 22.3 %copy-start.7 = (f32[256]{0:T(256)S(1)}, f32[256]{0:T(256)}, u32[]{:S(2)}) copy-start(f32[256]{0:T(256)} %param.17) | copy-start | bytes 3076
  55.3 8.3 %collective-permute-start.13 = (f32[136,256]{1,0:T(8,128)S(1)}, f32[136,256]{1,0:T(8,128)S(1)}, u32[]{:S(2)}, u32[]{:S(2)}) collective-permute-start(f32[136,256]{1,0:T(8,128)S(1)} %get-tuple-element.65), channel_id=1, source_target_pairs={{0,4},{1,5},{2,6},{3,7},{4,0},{5,1},{6,2},{7,3},{8,12},{9,13},{10,... | collective-permute-start | bytes 417800 | tf_op jit(solution)/shard_map/ppermute | solution.py:437
  56.0 4.2 %collective-permute-start.12 = (f32[256,256]{1,0:T(8,128)S(1)}, f32[256,256]{1,0:T(8,128)S(1)}, u32[]{:S(2)}, u32[]{:S(2)}) collective-permute-start(f32[256,256]{1,0:T(8,128)S(1)} %backward_part.8.token), channel_id=1, source_target_pairs={{0,2},{1,3},{2,0},{3,1},{4,6},{5,7},{6,4},{7,5},{8,10},{9,11},{10,... | collective-permute-start | bytes 786440 | tf_op jit(solution)/shard_map/ppermute | solution.py:437
  56.0 14.3 %collective-permute-start.21 = (f32[4,64,256]{2,1,0:T(8,128)S(1)}, f32[4,64,256]{2,1,0:T(8,128)S(1)}, u32[]{:S(2)}, u32[]{:S(2)}) collective-permute-start(f32[4,64,256]{2,1,0:T(8,128)S(1)} %stack_left.1.own), channel_id=1, source_target_pairs={{0,1},{1,0},{2,3},{3,2},{4,5},{5,4},{6,7},{7,6},{8,9},{9,8},{10,11... | collective-permute-start | bytes 786440 | tf_op jit(solution)/shard_map/ppermute | solution.py:437
  60.3 17.2 %collective-permute-start.16 = (f32[72,256]{1,0:T(8,128)S(1)}, f32[72,256]{1,0:T(8,128)S(1)}, u32[]{:S(2)}, u32[]{:S(2)}) collective-permute-start(f32[72,256]{1,0:T(8,128)S(1)} %get-tuple-element.67.g2), channel_id=1, source_target_pairs={{0,16},{1,17},{2,18},{3,19},{4,20},{5,21},{6,22},{7,23},{8,24},{9,... | collective-permute-start | bytes 221192 | tf_op jit(solution)/shard_map/ppermute | solution.py:437
  62.5 15.0 %collective-permute-start.17 = (f32[72,256]{1,0:T(8,128)S(1)}, f32[72,256]{1,0:T(8,128)S(1)}, u32[]{:S(2)}, u32[]{:S(2)}) collective-permute-start(f32[72,256]{1,0:T(8,128)S(1)} %get-tuple-element.68.g3), channel_id=1, source_target_pairs={{0,24},{1,25},{2,26},{3,27},{4,28},{5,29},{6,30},{7,31},{8,16},{9,... | collective-permute-start | bytes 221192 | tf_op jit(solution)/shard_map/ppermute | solution.py:437
  64.6 12.9 %collective-permute-start.15 = (f32[64,256]{1,0:T(8,128)S(1)}, f32[64,256]{1,0:T(8,128)S(1)}, u32[]{:S(2)}, u32[]{:S(2)}) collective-permute-start(f32[64,256]{1,0:T(8,128)S(1)} %get-tuple-element.70), channel_id=1, source_target_pairs={{0,8},{1,9},{2,10},{3,11},{4,12},{5,13},{6,14},{7,15},{8,0},{9,1},... | collective-permute-start | bytes 196616 | tf_op jit(solution)/shard_map/ppermute | solution.py:437
  65.1 12.5 %all-to-all-start = ((f32[32,1,128]{2,1,0:T(1,128)}), f32[32,1,128]{2,1,0:T(1,128)S(1)}, u32[]{:S(2)}, u32[]{:S(2)}) async-start(f32[32,1,128]{2,1,0:T(1,128)} %bitcast.3), calls=%async_computation | async-start | bytes 32768 | tf_op jit(solution)/shard_map/all_to_all | solution.py:494
